TPU v7x, 32 devices: a whole 2x2x4 slice. The times are simulated.
32 devices in a mesh: groups: 1, blk: 8 (over z, y), inner: 4 (over x, core).
Axes of the slice: x: 2, y: 2, z: 4, core: 2. Of those that a mesh axis runs over, the one named last changes fastest.
Arguments:
- alignment_left: float32 [128, 4096], P(('groups', 'blk')), may hold values from -6 to 6
- alignment_right: float32 [512, 4096], P(('groups', 'blk', 'inner')), may hold values from -6 to 6
- projection_matrix: float32 [1024, 128], replicated, may hold values from -0.1875 to 0.1875
- cotangent: float32 [128, 8, 64, 128], P(('groups', 'blk'), None, 'inner'), may hold values from -6 to 6
Outputs:
- pair_update: float32 [128, 8, 64, 128], P(('groups', 'blk'), None, 'inner')
- grad_left: float32 [128, 4096], P(('groups', 'blk'), 'inner')
- grad_right: float32 [512, 4096], P(('groups', 'blk', 'inner'))
- grad_weight: float32 [1024, 128], P('groups')
All inputs are finite; a program needn't handle non-finite values.
Results may differ from a plain program's by a relative error of at most 0.0001.
Values sent between devices are 32-bit elements; how exact they have to be, the bound alone decides.
No kernel may reach another device: no remote copies, remote signals or barrier semaphores. Data moves between devices by JAX's collectives and lax.ppermute only.
A program may use at most 128 MiB of HBM per device.

v0:
```python
import jax
import jax.numpy as jnp
from jax import lax
from jax.sharding import PartitionSpec as P

ENTRY_CHANNELS = 32


highest = lax.Precision.HIGHEST


def tile_terms(left_sequence, right_block, grad_block, projection_matrix):
    window_row_count, sequence_count, channel_count = left_sequence.shape
    column_count = right_block.shape[0]
    right_sequence = right_block.reshape(column_count, sequence_count, channel_count)
    outer = (
        jnp.einsum("isx,jsy->ijxy", left_sequence, right_sequence, precision=highest)
        / sequence_count
    )
    outer_flat = outer.reshape(window_row_count, column_count, channel_count * channel_count)
    pair_block = jnp.einsum("ijk,kp->ijp", outer_flat, projection_matrix, precision=highest)
    outer_grad = jnp.einsum("ijp,kp->ijk", grad_block, projection_matrix, precision=highest)
    outer_grad = outer_grad.reshape(window_row_count, column_count, channel_count, channel_count)
    weight_part = jnp.einsum("ijk,ijp->kp", outer_flat, grad_block, precision=highest)
    left_part = (
        jnp.einsum("ijxy,jsy->isx", outer_grad, right_sequence, precision=highest) / sequence_count
    )
    found_terms = (pair_block, weight_part, left_part)
    right_part = (
        jnp.einsum("ijxy,isx->jsy", outer_grad, left_sequence, precision=highest) / sequence_count
    )
    found_terms = found_terms + (right_part.reshape(column_count, sequence_count * channel_count),)
    return found_terms


def absorb(running, right_block, grads_flat, left_sequence, projection_matrix, offset):
    column_count = right_block.shape[0]
    grad_block = lax.dynamic_slice_in_dim(grads_flat, offset, column_count, 1)
    found_terms = tile_terms(left_sequence, right_block, grad_block, projection_matrix)
    pair_all = lax.dynamic_update_slice_in_dim(running[0], found_terms[0], offset, 1)
    result = (pair_all, running[1] + found_terms[1], running[2] + found_terms[2])
    result = result + (lax.dynamic_update_slice_in_dim(running[3], found_terms[3], offset, 0),)
    return result


def local(alignment_left, alignment_right, projection_matrix, cotangent):
    window_row_count, feature_count = alignment_left.shape
    column_count = alignment_right.shape[0]
    block_count = lax.axis_size("blk")
    channel_count = projection_matrix.shape[0] // ENTRY_CHANNELS * 0 + ENTRY_CHANNELS
    sequence_count = feature_count // channel_count
    pair_count = projection_matrix.shape[1]
    left_sequence = alignment_left.reshape(window_row_count, sequence_count, channel_count)
    grads_flat = cotangent.reshape(window_row_count, block_count * column_count, pair_count)
    initial = (
        jnp.zeros((window_row_count, block_count * column_count, pair_count), jnp.float32),
        jnp.zeros(projection_matrix.shape, jnp.float32),
        jnp.zeros((window_row_count, sequence_count, channel_count), jnp.float32),
    )
    initial = initial + (jnp.zeros((block_count * column_count, feature_count), jnp.float32),)
    collected_rows = lax.all_gather(alignment_right, "blk", axis=0, tiled=True)

    def visit_block(block_index, running):
        offset = block_index * column_count
        right_block = lax.dynamic_slice_in_dim(collected_rows, offset, column_count, 0)
        return absorb(running, right_block, grads_flat, left_sequence, projection_matrix, offset)

    state = lax.fori_loop(0, block_count, visit_block, initial)
    pair_update = state[0].reshape(cotangent.shape)
    grad_weight = lax.psum(state[1], ("blk", "inner"))
    grad_left = lax.psum_scatter(
        state[2].reshape(window_row_count, feature_count), "inner", scatter_dimension=1, tiled=True
    )
    grad_right = lax.psum_scatter(state[3], "blk", scatter_dimension=0, tiled=True)
    return (pair_update, grad_left, grad_right, grad_weight)


def solution(mesh):
    placed = (
        P(("groups", "blk"), None),
        P(("groups", "blk", "inner"), None),
        P(),
        P(("groups", "blk"), None, "inner", None),
    )
    return jax.shard_map(
        local,
        mesh=mesh,
        in_specs=placed,
        out_specs=(
            P(("groups", "blk"), None, "inner", None),
            P(("groups", "blk"), "inner"),
            P(("groups", "blk", "inner"), None),
            P("groups", None),
        ),
        check_vma=False,
    )
```

profile of v0, /device:TPU:0, one launch (start us, length us, event | category | flops | bytes accessed | tf_op | source)
XLA Modules:
  0.0 697.4 jit_solution(4504615217928859609)
XLA Ops:
  9.6 52.6 %all-gather.2.cloned.1.call-done = f32[128,4096]{1,0:T(8,128)} async-done(((f32[16,4096]{1,0:T(8,128)}), f32[128,4096]{1,0:T(8,128)}) %all-gather.2.cloned.1.call-update) | async-done | bytes 2097168 | tf_op jit(solution)/shard_map/all_gather | solution.py:61
  63.8 404.8 %while.20 = (s32[]{:T(128)}, f32[16,128,128]{2,1,0:T(8,128)S(1)}, f32[1024,128]{1,0:T(8,128)}, f32[16,128,32]{1,2,0:T(8,128)S(1)}, f32[128,4096]{1,0:T(8,128)}, ...) while((s32[]{:T(128)}, f32[16,128,128]{2,1,0:T(8,128)S(1)}, ...), condition=%wide.region_1.0_spmd.clone, body=%wide.region_0.0_spmd.clone.sunk | while | flops 2416705536 | bytes 19529932 | solution.py:68
  63.8 1.9 fusion.49
  65.7 2.7 reshape.67
  68.4 9.0 %fusion.50 = f32[16,128,32]{1,2,0:T(8,128)S(1)} fusion(f32[16,16,32,32]{3,2,1,0:T(8,128)} %reshape.67, f32[16,128,32]{1,2,0:T(8,128)S(1)} %get-tuple-element.315), kind=kOutput, calls=%fused_computation.5.clone.1 | convolution fusion | flops 402718720 | bytes 1572864 | tf_op jit(solution)/shard_map/while/body/eval_jaxpr/ijxy,isx->jsy/dot_general | solution.py:30
  80.3 5.3 fusion.52
  85.6 15.0 %multiply_bitcast_fusion.2 = f32[16,16,32,32]{2,3,0,1:T(8,128)} fusion(f32[16,128,32]{2,1,0:T(8,128)S(1)} %reshape.69, f32[16,128,32]{1,2,0:T(8,128)S(1)} %get-tuple-element.315), kind=kOutput, calls=%fused_computation.clone.1 | convolution fusion | flops 402915328 | bytes 1572864 | tf_op jit(solution)/shard_map/while/body/eval_jaxpr/isx,jsy->ijxy/dot_general | solution.py:17
  100.6 5.4 copy.28
  105.9 3.7 reshape.70
  109.7 3.5 fusion.51
  116.1 2.7 reshape.67
  118.9 9.0 %fusion.50 = f32[16,128,32]{1,2,0:T(8,128)S(1)} fusion(f32[16,16,32,32]{3,2,1,0:T(8,128)} %reshape.67, f32[16,128,32]{1,2,0:T(8,128)S(1)} %get-tuple-element.315), kind=kOutput, calls=%fused_computation.5.clone.1 | convolution fusion | flops 402718720 | bytes 1572864 | tf_op jit(solution)/shard_map/while/body/eval_jaxpr/ijxy,isx->jsy/dot_general | solution.py:30
  130.7 5.3 fusion.52
  136.0 15.0 %multiply_bitcast_fusion.2 = f32[16,16,32,32]{2,3,0,1:T(8,128)} fusion(f32[16,128,32]{2,1,0:T(8,128)S(1)} %reshape.69, f32[16,128,32]{1,2,0:T(8,128)S(1)} %get-tuple-element.315), kind=kOutput, calls=%fused_computation.clone.1 | convolution fusion | flops 402915328 | bytes 1572864 | tf_op jit(solution)/shard_map/while/body/eval_jaxpr/isx,jsy->ijxy/dot_general | solution.py:17
  151.0 5.4 copy.28
  156.3 3.7 reshape.70
  160.1 3.7 fusion.51
  166.8 2.7 reshape.67
  169.5 9.0 %fusion.50 = f32[16,128,32]{1,2,0:T(8,128)S(1)} fusion(f32[16,16,32,32]{3,2,1,0:T(8,128)} %reshape.67, f32[16,128,32]{1,2,0:T(8,128)S(1)} %get-tuple-element.315), kind=kOutput, calls=%fused_computation.5.clone.1 | convolution fusion | flops 402718720 | bytes 1572864 | tf_op jit(solution)/shard_map/while/body/eval_jaxpr/ijxy,isx->jsy/dot_general | solution.py:30
  181.3 5.3 fusion.52
  186.6 15.0 %multiply_bitcast_fusion.2 = f32[16,16,32,32]{2,3,0,1:T(8,128)} fusion(f32[16,128,32]{2,1,0:T(8,128)S(1)} %reshape.69, f32[16,128,32]{1,2,0:T(8,128)S(1)} %get-tuple-element.315), kind=kOutput, calls=%fused_computation.clone.1 | convolution fusion | flops 402915328 | bytes 1572864 | tf_op jit(solution)/shard_map/while/body/eval_jaxpr/isx,jsy->ijxy/dot_general | solution.py:17
  201.6 5.4 copy.28
  207.0 3.7 reshape.70
  210.7 3.7 fusion.51
  215.5 1.9 fusion.49
  217.4 2.7 reshape.67
  220.1 9.0 %fusion.50 = f32[16,128,32]{1,2,0:T(8,128)S(1)} fusion(f32[16,16,32,32]{3,2,1,0:T(8,128)} %reshape.67, f32[16,128,32]{1,2,0:T(8,128)S(1)} %get-tuple-element.315), kind=kOutput, calls=%fused_computation.5.clone.1 | convolution fusion | flops 402718720 | bytes 1572864 | tf_op jit(solution)/shard_map/while/body/eval_jaxpr/ijxy,isx->jsy/dot_general | solution.py:30
  232.0 5.3 fusion.52
  237.3 15.0 %multiply_bitcast_fusion.2 = f32[16,16,32,32]{2,3,0,1:T(8,128)} fusion(f32[16,128,32]{2,1,0:T(8,128)S(1)} %reshape.69, f32[16,128,32]{1,2,0:T(8,128)S(1)} %get-tuple-element.315), kind=kOutput, calls=%fused_computation.clone.1 | convolution fusion | flops 402915328 | bytes 1572864 | tf_op jit(solution)/shard_map/while/body/eval_jaxpr/isx,jsy->ijxy/dot_general | solution.py:17
  252.2 5.4 copy.28
  257.6 3.7 reshape.70
  261.4 3.7 fusion.51
  268.0 2.7 reshape.67
  270.7 9.0 %fusion.50 = f32[16,128,32]{1,2,0:T(8,128)S(1)} fusion(f32[16,16,32,32]{3,2,1,0:T(8,128)} %reshape.67, f32[16,128,32]{1,2,0:T(8,128)S(1)} %get-tuple-element.315), kind=kOutput, calls=%fused_computation.5.clone.1 | convolution fusion | flops 402718720 | bytes 1572864 | tf_op jit(solution)/shard_map/while/body/eval_jaxpr/ijxy,isx->jsy/dot_general | solution.py:30
  282.6 5.3 fusion.52
  287.9 15.0 %multiply_bitcast_fusion.2 = f32[16,16,32,32]{2,3,0,1:T(8,128)} fusion(f32[16,128,32]{2,1,0:T(8,128)S(1)} %reshape.69, f32[16,128,32]{1,2,0:T(8,128)S(1)} %get-tuple-element.315), kind=kOutput, calls=%fused_computation.clone.1 | convolution fusion | flops 402915328 | bytes 1572864 | tf_op jit(solution)/shard_map/while/body/eval_jaxpr/isx,jsy->ijxy/dot_general | solution.py:17
  302.9 5.4 copy.28
  308.2 3.7 reshape.70
  312.0 3.7 fusion.51
  316.8 1.9 fusion.49
  318.7 2.7 reshape.67
  321.4 9.0 %fusion.50 = f32[16,128,32]{1,2,0:T(8,128)S(1)} fusion(f32[16,16,32,32]{3,2,1,0:T(8,128)} %reshape.67, f32[16,128,32]{1,2,0:T(8,128)S(1)} %get-tuple-element.315), kind=kOutput, calls=%fused_computation.5.clone.1 | convolution fusion | flops 402718720 | bytes 1572864 | tf_op jit(solution)/shard_map/while/body/eval_jaxpr/ijxy,isx->jsy/dot_general | solution.py:30
  333.2 5.3 fusion.52
  338.5 15.0 %multiply_bitcast_fusion.2 = f32[16,16,32,32]{2,3,0,1:T(8,128)} fusion(f32[16,128,32]{2,1,0:T(8,128)S(1)} %reshape.69, f32[16,128,32]{1,2,0:T(8,128)S(1)} %get-tuple-element.315), kind=kOutput, calls=%fused_computation.clone.1 | convolution fusion | flops 402915328 | bytes 1572864 | tf_op jit(solution)/shard_map/while/body/eval_jaxpr/isx,jsy->ijxy/dot_general | solution.py:17
  353.5 5.4 copy.28
  358.9 3.7 reshape.70
  362.6 3.7 fusion.51
  369.3 2.7 reshape.67
  372.0 9.0 %fusion.50 = f32[16,128,32]{1,2,0:T(8,128)S(1)} fusion(f32[16,16,32,32]{3,2,1,0:T(8,128)} %reshape.67, f32[16,128,32]{1,2,0:T(8,128)S(1)} %get-tuple-element.315), kind=kOutput, calls=%fused_computation.5.clone.1 | convolution fusion | flops 402718720 | bytes 1572864 | tf_op jit(solution)/shard_map/while/body/eval_jaxpr/ijxy,isx->jsy/dot_general | solution.py:30
  383.8 5.3 fusion.52
  389.1 15.0 %multiply_bitcast_fusion.2 = f32[16,16,32,32]{2,3,0,1:T(8,128)} fusion(f32[16,128,32]{2,1,0:T(8,128)S(1)} %reshape.69, f32[16,128,32]{1,2,0:T(8,128)S(1)} %get-tuple-element.315), kind=kOutput, calls=%fused_computation.clone.1 | convolution fusion | flops 402915328 | bytes 1572864 | tf_op jit(solution)/shard_map/while/body/eval_jaxpr/isx,jsy->ijxy/dot_general | solution.py:17
  404.1 5.4 copy.28
  409.5 3.7 reshape.70
  413.2 3.7 fusion.51
  419.9 2.7 reshape.67
  422.6 9.0 %fusion.50 = f32[16,128,32]{1,2,0:T(8,128)S(1)} fusion(f32[16,16,32,32]{3,2,1,0:T(8,128)} %reshape.67, f32[16,128,32]{1,2,0:T(8,128)S(1)} %get-tuple-element.315), kind=kOutput, calls=%fused_computation.5.clone.1 | convolution fusion | flops 402718720 | bytes 1572864 | tf_op jit(solution)/shard_map/while/body/eval_jaxpr/ijxy,isx->jsy/dot_general | solution.py:30
  434.5 5.3 fusion.52
  439.7 15.0 %multiply_bitcast_fusion.2 = f32[16,16,32,32]{2,3,0,1:T(8,128)} fusion(f32[16,128,32]{2,1,0:T(8,128)S(1)} %reshape.69, f32[16,128,32]{1,2,0:T(8,128)S(1)} %get-tuple-element.315), kind=kOutput, calls=%fused_computation.clone.1 | convolution fusion | flops 402915328 | bytes 1572864 | tf_op jit(solution)/shard_map/while/body/eval_jaxpr/isx,jsy->ijxy/dot_general | solution.py:17
  454.7 5.4 copy.28
  460.1 3.7 reshape.70
  463.9 3.7 fusion.51
  470.8 124.3 %all-reduce.2.cloned.1.call-done = f32[1024,128]{1,0:T(8,128)} async-done(((f32[1024,128]{1,0:T(8,128)}), f32[1024,128]{1,0:T(8,128)}) %all-reduce.2.cloned.1.call-update) | async-done | bytes 524304 | tf_op jit(solution)/shard_map/psum | solution.py:70
  595.1 22.3 %reduce-scatter.3.cloned.1.call-done = f32[16,1024]{1,0:T(8,128)} async-done(((f32[16,4096]{1,0:T(8,128)}), f32[16,1024]{1,0:T(8,128)}) %reduce-scatter.3.cloned.1.call-update) | async-done | bytes 65552 | tf_op jit(solution)/shard_map/reduce_scatter | solution.py:71
  617.4 71.6 %reduce-scatter.5.cloned.1.call-done = f32[16,4096]{1,0:T(8,128)} async-done(((f32[128,4096]{1,0:T(8,128)}), f32[16,4096]{1,0:T(8,128)}) %reduce-scatter.5.cloned.1.call-update) | async-done | bytes 262160 | tf_op jit(solution)/shard_map/reduce_scatter | solution.py:74
  (66 shorter events, 48.3 us)
Async XLA Ops:
  7.2 56.6 %copy-start = (f32[1024,128]{1,0:T(8,128)S(1)}, f32[1024,128]{1,0:T(8,128)}, u32[]{:S(2)}) copy-start(f32[1024,128]{1,0:T(8,128)} %param.8) | copy-start | bytes 1572868
  7.2 55.0 %all-gather.2.cloned.1.call-start = ((), (), s32[]{:S(2)}) async-start(), calls=%async_computation.2 | async-start | bytes 2359296 | tf_op jit(solution)/shard_map/all_gather | solution.py:61
  7.9 587.2 %all-reduce.2.cloned.1.call-start = ((), (), s32[]{:S(2)}) async-start(), calls=%async_computation.5 | async-start | bytes 1048576 | tf_op jit(solution)/shard_map/psum | solution.py:70
  468.6 222.3 %copy-start.1 = (f32[16,128,128]{2,1,0:T(8,128)}, f32[16,128,128]{2,1,0:T(8,128)S(1)}, u32[]{:S(2)}) copy-start(f32[16,128,128]{2,1,0:T(8,128)S(1)} %get-tuple-element.161) | copy-start | bytes 3145732
  468.6 148.8 %reduce-scatter.3.cloned.1.call-start = ((), (), s32[]{:S(2)}) async-start(), calls=%async_computation.3 | async-start | bytes 327680 | tf_op jit(solution)/shard_map/reduce_scatter | solution.py:71
  470.2 218.8 %reduce-scatter.5.cloned.1.call-start = ((), (), s32[]{:S(2)}) async-start(), calls=%async_computation.4 | async-start | bytes 2359296 | tf_op jit(solution)/shard_map/reduce_scatter | solution.py:74
Sparse Core Ops, SparseCore 0:
  10.1 51.9 all-gather.1
  468.8 126.3 all-reduce.1
  598.3 19.0 reduce-scatter.2
  621.4 67.5 reduce-scatter.4
where the time goes:
time: 699 us; the launch traced here: 697 us
  matrix products  287 us (41%)
  waiting for transfers between devices  272 us (39%)
  local copies, waits for them, and re-layouts  124 us (18%)
  between operations  13.8 us (2%)
    psum x1, waiting for transfers between devices, local(): grad_weight = lax.psum(state[1], ('blk', 'inner'))  124 us
    dot_general x8, matrix products, tile_terms(): jnp.einsum('isx,jsy->ijxy', left_sequence, right_sequence, precision=high...  120 us
    dot_general x8, matrix products, tile_terms(): jnp.einsum('ijxy,isx->jsy', outer_grad, left_sequence, precision=highest)  71.8 us
    reduce_scatter x1, waiting for transfers between devices, local(): lax.psum_scatter(state[3], 'blk', scatter_dimension=0, tiled=True)  71.6 us
    all_gather x1, waiting for transfers between devices, local(): collected_rows = lax.all_gather(alignment_right, 'blk', axis=0, tiled=True)  52.6 us
    div x8, local copies, waits for them, and re-layouts, tile_terms(): jnp.einsum('isx,jsy->ijxy', left_sequence, right_sequence, precision=high...  43 us
    dot_general x8, matrix products, tile_terms(): jnp.einsum('ijxy,jsy->isx', outer_grad, right_sequence, precision=highest)  42.3 us
    reshape x8, local copies, waits for them, and re-layouts, tile_terms(): outer.reshape(window_row_count, column_count, channel_count * channel_count)  30 us
  transfers between devices with their start and end apart: 4, of which 4 were waited for; matrix products, arithmetic and copies ran while one was open for 0% of the time, Pallas kernels for 0%

commit v1 on v0

v1 whole, which is shorter than its diff:
```python
import functools

import jax
import jax.numpy as jnp
from jax import lax
from jax.experimental import pallas as pl
from jax.experimental.pallas import tpu as pltpu
from jax.sharding import PartitionSpec as P

ENTRY_CHANNELS = 32
F32 = jnp.float32
BF16 = jnp.bfloat16
VMEM_LIMIT = 48 * 1024 * 1024


def halves(values):
    high = values.astype(BF16)
    low = (values - high.astype(F32)).astype(BF16)
    return high, low


def dot(left, right):
    return jnp.dot(left, right, preferred_element_type=F32)


def dot_rows(left, right):
    return lax.dot_general(left, right, (((1,), (1,)), ((), ())), preferred_element_type=F32)


def ring_position(block, count):
    return jnp.where(lax.rem(block, 2) == 0, block // 2, count - 1 - block // 2)


def ring_block(position, count):
    return jnp.where(position < count // 2, 2 * position, 2 * count - 1 - 2 * position)


def slot_blocks(count):
    position = ring_position(lax.axis_index("blk"), count)
    return [ring_block(lax.rem(position + slot, count), count) for slot in range(count)]


def pair_rows(block_refs, index):
    return jnp.concatenate([ref[index] for ref in block_refs], axis=0)


def cotangent_rows(cotangent_ref, row, blocks):
    return jnp.concatenate([cotangent_ref[row, block] for block in blocks], axis=0)


def weight_by_y(weight_ref, y, channels):
    return weight_ref[pl.ds(y, channels, stride=channels), :]


def gradient_kernel(count, weight_ref, cotangent_ref, left_ref, *refs):
    right_refs = refs[:count]
    high_ref, low_ref, weight_cat, left_flip = refs[count:]
    rows = cotangent_ref.shape[0]
    channels = ENTRY_CHANNELS
    sequences = left_ref.shape[1]
    blocks = slot_blocks(count)
    columns = count * cotangent_ref.shape[2]
    for y in range(channels):
        high, low = halves(weight_by_y(weight_ref, y, channels))
        weight_cat[y * channels : (y + 1) * channels, :] = jnp.concatenate([high, low, high], 1)
    flip_high, flip_low = halves(left_ref[...].T)
    left_flip[:sequences, :] = flip_high
    left_flip[sequences:, :] = flip_low

    def grad_step(pair, carry):
        grads = [cotangent_rows(cotangent_ref, 2 * pair + part, blocks) for part in range(2)]
        high, low = halves(jnp.concatenate(grads, 0))
        found = dot_rows(weight_cat[...], jnp.concatenate([high, high, low], 1))
        high, low = halves(found)
        high_ref[pair] = high
        low_ref[pair] = low
        return carry

    lax.fori_loop(0, rows // 2, grad_step, 0)

    def right_step(step, carry):
        def stacked(ref):
            return jnp.concatenate(
                [rows_of_y(ref, 2 * step + part, rows, columns) for part in range(2)], 1
            )

        first = dot(left_flip[...], stacked(high_ref))
        second = dot(left_flip[:sequences, :], stacked(low_ref))
        found = first[:sequences] + first[sequences:] + second
        for part in range(2):
            turned = found[:, part * columns : (part + 1) * columns].T
            depth = columns // count
            for slot in range(count):
                right_refs[slot][2 * step + part] = turned[slot * depth : (slot + 1) * depth]
        return carry

    lax.fori_loop(0, channels // 2, right_step, 0)


def rows_of_y(ref, y, rows, columns):
    channels = ENTRY_CHANNELS
    start = pl.multiple_of(y * channels, channels)
    return jnp.concatenate(
        [
            ref[row // 2, pl.ds(start, channels), (row % 2) * columns : (row % 2 + 1) * columns]
            for row in range(rows)
        ],
        0,
    )


def outer_phase(left_ref, block_refs, high_ref, low_ref, rows):
    channels = ENTRY_CHANNELS
    count = len(block_refs)
    columns = count * block_refs[0].shape[1]
    high, low = halves(left_ref[...])
    left_cat = jnp.concatenate([high, low, high], 1)

    def step_of(step, carry):
        right = [pair_rows(block_refs, 2 * step + part) for part in range(2)]
        high, low = halves(jnp.concatenate(right, 0))
        found = dot_rows(left_cat, jnp.concatenate([high, high, low], 1))
        high, low = halves(found)
        for ref, values in ((high_ref, high), (low_ref, low)):
            for part in range(2):
                start = pl.multiple_of((2 * step + part) * channels, channels)
                for row in range(rows):
                    ref[
                        row // 2,
                        pl.ds(start, channels),
                        (row % 2) * columns : (row % 2 + 1) * columns,
                    ] = values[
                        row * channels : (row + 1) * channels,
                        part * columns : (part + 1) * columns,
                    ]
        return carry

    lax.fori_loop(0, channels // 2, step_of, 0)


def weight_kernel(count, inner, left_ref, cotangent_ref, *refs):
    block_refs = refs[:count]
    out_refs = refs[count : count + inner]
    high_ref, low_ref, total = refs[count + inner :]
    rows = cotangent_ref.shape[0]
    pairs = cotangent_ref.shape[3]
    blocks = slot_blocks(count)
    outer_phase(left_ref, block_refs, high_ref, low_ref, rows)
    total[...] = jnp.zeros_like(total)

    def step_of(pair, carry):
        grads = [cotangent_rows(cotangent_ref, 2 * pair + part, blocks) for part in range(2)]
        high, low = halves(jnp.concatenate(grads, 0))
        both = dot(high_ref[pair], jnp.concatenate([high, low], 1))
        total[...] += both[:, :pairs] + both[:, pairs:] + dot(low_ref[pair], high)
        return carry

    lax.fori_loop(0, rows // 2, step_of, 0)
    mine = lax.axis_index("inner")
    here = lax.axis_index("blk")
    size = total.shape[0] // (inner * count)
    for other in range(inner):
        for part in range(count):
            chunk = lax.bitwise_xor(mine, other) * count + lax.bitwise_xor(here, part)
            out_refs[other][part] = total[pl.ds(pl.multiple_of(chunk * size, size), size), :]


def left_kernel(count, inner, high_ref, low_ref, *refs):
    block_refs = refs[:count]
    out_refs = refs[count : count + inner]
    total, flipped = refs[count + inner :]
    rows = 2 * high_ref.shape[0]
    channels = ENTRY_CHANNELS
    columns = high_ref.shape[2] // 2
    sequences = block_refs[0].shape[2]
    total[...] = jnp.zeros_like(total)
    group = 4

    def step_of(step, carry):
        ys = [group * step + part for part in range(group)]
        high, low = halves(jnp.concatenate([pair_rows(block_refs, y) for y in ys], 0))
        grads_high = jnp.concatenate([rows_of_y(high_ref, y, rows, columns) for y in ys], 1)
        grads_low = jnp.concatenate([rows_of_y(low_ref, y, rows, columns) for y in ys], 1)
        both = dot(grads_high, jnp.concatenate([high, low], 1))
        total[...] += both[:, :sequences] + both[:, sequences:] + dot(grads_low, high)
        return carry

    lax.fori_loop(0, channels // group, step_of, 0)
    flipped[...] = total[...].T * (1.0 / sequences)
    mine = lax.axis_index("inner")
    size = sequences // inner
    for other in range(inner):
        start = pl.multiple_of(lax.bitwise_xor(mine, other) * size, size)
        out_refs[other][...] = flipped[pl.ds(start, size), :]


def pair_kernel(count, left_ref, weight_ref, *refs):
    block_refs = refs[:count]
    out_ref, high_ref, low_ref, weight_flip, weight_rows = refs[count:]
    rows = out_ref.shape[0]
    channels = ENTRY_CHANNELS
    depth = out_ref.shape[2]
    pairs = out_ref.shape[3]
    columns = count * depth
    blocks = slot_blocks(count)
    for y in range(channels):
        weight_rows[y * channels : (y + 1) * channels, :] = weight_by_y(weight_ref, y, channels)
    flip_high, flip_low = halves(weight_rows[...].T)
    weight_flip[:pairs, :] = flip_high
    weight_flip[pairs:, :] = flip_low
    outer_phase(left_ref, block_refs, high_ref, low_ref, rows)

    def step_of(pair, carry):
        first = dot(weight_flip[...], high_ref[pair])
        found = first[:pairs] + first[pairs:] + dot(weight_flip[:pairs, :], low_ref[pair])
        for part in range(2):
            turned = found[:, part * columns : (part + 1) * columns].T
            for slot in range(count):
                out_ref[2 * pair + part, blocks[slot]] = turned[slot * depth : (slot + 1) * depth]
        return carry

    lax.fori_loop(0, rows // 2, step_of, 0)


def place_kernel(count, inner, *refs):
    own_refs = refs[:count]
    other_refs = refs[count : count + inner - 1]
    out_ref = refs[-1]
    channels = ENTRY_CHANNELS
    mine = lax.axis_index("inner")
    here = lax.axis_index("blk")
    size = own_refs[0].shape[0]
    for other in range(inner):
        for part in range(count):
            chunk = lax.bitwise_xor(mine, other) * count + lax.bitwise_xor(here, part)
            first = chunk * size
            y = first // channels
            x = lax.rem(first, channels)
            piece = own_refs[part][...] if other == 0 else other_refs[other - 1][part]
            out_ref[pl.ds(x * channels + y, size, stride=channels), :] = piece


def call(kernel, out_shape, scratch, flops):
    return pl.pallas_call(
        kernel,
        out_shape=out_shape,
        scratch_shapes=scratch,
        compiler_params=pltpu.CompilerParams(vmem_limit_bytes=VMEM_LIMIT),
        cost_estimate=pl.CostEstimate(flops=flops, bytes_accessed=8 << 20, transcendentals=0),
    )


def ring_moves(count, inner):
    order = [2 * r if r < count // 2 else 2 * count - 1 - 2 * r for r in range(count)]
    upward = [(order[r], order[(r + 1) % count]) for r in range(count)]
    downward = [(there, here) for here, there in upward]
    across = []
    for q in range(inner):
        for here, there in upward if q % 2 == 0 else downward:
            across.append((here * inner + q, there * inner + q))
    return upward, downward, across


def ring_gather(block, count, inner):
    upward, downward, across = ring_moves(count, inner)
    even = lax.rem(lax.axis_index("inner"), 2) == 0
    slots = [block] * count
    up = down = block
    for step in range(1, count // 2):
        up = lax.ppermute(up, "blk", upward)
        down = lax.ppermute(down, "blk", downward)
        slots[count - step] = up
        slots[step] = down
    slots[count // 2] = lax.ppermute(jnp.where(even, up, down), ("blk", "inner"), across)
    return slots


def ring_scatter(parts, count, inner):
    upward, downward, across = ring_moves(count, inner)
    even = lax.rem(lax.axis_index("inner"), 2) == 0
    half = count // 2
    first = lax.ppermute(parts[half], ("blk", "inner"), across)
    up = parts[half - 1] + jnp.where(even, first, 0.0)
    down = parts[half + 1] + jnp.where(even, 0.0, first)
    for step in range(half - 1, 0, -1):
        up = lax.ppermute(up, "blk", upward)
        down = lax.ppermute(down, "blk", downward)
        if step > 1:
            up = parts[step - 1] + up
            down = parts[count - step + 1] + down
    return parts[0] + up + down


def swap(value, axis, size, distance):
    return lax.ppermute(value, axis, [(here, here ^ distance) for here in range(size)])


def local(alignment_left, alignment_right, projection_matrix, cotangent):
    rows, features = alignment_left.shape
    depth = alignment_right.shape[0]
    count = lax.axis_size("blk")
    inner = lax.axis_size("inner")
    channels = ENTRY_CHANNELS
    sequences = features // channels
    outer, pairs = projection_matrix.shape
    columns = count * depth
    flops = 2 * rows * columns * outer * pairs * 3

    right = alignment_right.reshape(depth, sequences, channels).transpose(2, 0, 1)
    slots = ring_gather(right, count, inner)

    left = alignment_left.reshape(rows, sequences, channels).transpose(0, 2, 1)
    left = left.reshape(rows * channels, sequences) * (1.0 / sequences)

    wide = (rows // 2, outer, 2 * columns)
    block_shape = jax.ShapeDtypeStruct((channels, depth, sequences), F32)
    found = call(
        functools.partial(gradient_kernel, count),
        [block_shape] * count + [jax.ShapeDtypeStruct(wide, BF16)] * 2,
        [pltpu.VMEM((outer, 3 * pairs), BF16), pltpu.VMEM((2 * sequences, rows * channels), BF16)],
        2 * flops,
    )(projection_matrix, cotangent, left)
    grads_high, grads_low = found[count:]
    right_grad = ring_scatter(found[:count], count, inner)
    grad_right = right_grad.transpose(1, 2, 0).reshape(depth, features)

    size = outer // (count * inner)
    wide_scratch = [pltpu.VMEM(wide, BF16), pltpu.VMEM(wide, BF16)]
    weight_parts = call(
        functools.partial(weight_kernel, count, inner),
        [jax.ShapeDtypeStruct((count, size, pairs), F32)] * inner,
        wide_scratch + [pltpu.VMEM((outer, pairs), F32)],
        2 * flops,
    )(left, cotangent, *slots)

    weight_own = weight_parts[0]
    for other in range(1, inner):
        weight_own = weight_own + swap(weight_parts[other], "inner", inner, other)
    weight_sum = weight_own[0]
    for other in range(1, count):
        weight_sum = weight_sum + swap(weight_own[other], "blk", count, other)
    gathered = [weight_sum]
    for other in range(1, count):
        gathered.append(swap(weight_sum, "blk", count, other))
    stacked = jnp.stack(gathered)
    spread = [swap(stacked, "inner", inner, other) for other in range(1, inner)]

    left_parts = call(
        functools.partial(left_kernel, count, inner),
        [jax.ShapeDtypeStruct((sequences // inner, rows * channels), F32)] * inner,
        [
            pltpu.VMEM((rows * channels, sequences), F32),
            pltpu.VMEM((sequences, rows * channels), F32),
        ],
        flops,
    )(grads_high, grads_low, *slots)
    left_sum = left_parts[0]
    for other in range(1, inner):
        left_sum = left_sum + swap(left_parts[other], "inner", inner, other)
    grad_left = left_sum.reshape(sequences // inner, rows, channels).transpose(1, 0, 2)
    grad_left = grad_left.reshape(rows, features // inner)

    pair_update = call(
        functools.partial(pair_kernel, count),
        jax.ShapeDtypeStruct(cotangent.shape, F32),
        wide_scratch
        + [pltpu.VMEM((2 * pairs, outer), BF16), pltpu.VMEM((outer, pairs), F32)],
        2 * flops,
    )(left, projection_matrix, *slots)

    grad_weight = call(
        functools.partial(place_kernel, count, inner),
        jax.ShapeDtypeStruct(projection_matrix.shape, F32),
        [],
        0,
    )(*gathered, *spread)
    return (pair_update, grad_left, grad_right, grad_weight)


def solution(mesh):
    placed = (
        P(("groups", "blk"), None),
        P(("groups", "blk", "inner"), None),
        P(),
        P(("groups", "blk"), None, "inner", None),
    )
    return jax.shard_map(
        local,
        mesh=mesh,
        in_specs=placed,
        out_specs=(
            P(("groups", "blk"), None, "inner", None),
            P(("groups", "blk"), "inner"),
            P(("groups", "blk", "inner"), None),
            P("groups", None),
        ),
        check_vma=False,
    )
```

time: 699 us -> 136 us (0.19)
  matrix products: 287 us -> 0 us
  waiting for transfers between devices: 272 us -> 36.6 us
  local copies, waits for them, and re-layouts: 124 us -> 8.75 us
  starting transfers between devices: 0.16 us -> 45.9 us
  Pallas kernels: 0 us -> 41.6 us
  between operations: 13.8 us -> 0.83 us
    dot_general x48 -> x0, matrix products: 287 us -> none  [the longest x8 120 us: tile_terms(): jnp.einsum('isx,jsy->ijxy', left_sequence, right_sequence, precision=high...]
    psum x1 -> x0, waiting for transfers between devices: 124 us -> none  [local(): grad_weight = lax.psum(state[1], ('blk', 'inner'))]
    reduce_scatter x2 -> x0, waiting for transfers between devices: 93.9 us -> none  [the longest x1 71.6 us: local(): lax.psum_scatter(state[3], 'blk', scatter_dimension=0, tiled=True)]
    reshape x34 -> x5, local copies, waits for them, and re-layouts: 60.8 us -> 3.77 us  [the longest x2 1.68 us: local(): alignment_right.reshape(depth, sequences, channels).transpose(2, 0, 1)]
    all_gather x1 -> x0, waiting for transfers between devices: 52.6 us -> none  [local(): collected_rows = lax.all_gather(alignment_right, 'blk', axis=0, tiled=True)]
    ppermute x0 -> x37, starting transfers between devices: none -> 45.9 us  [the longest x23 30.5 us: swap(): lax.ppermute(value, axis, [(here, here ^ distance) for here in range(size)])]
    div x16 -> x0, local copies, waits for them, and re-layouts: 45.7 us -> none  [the longest x8 43 us: tile_terms(): jnp.einsum('isx,jsy->ijxy', left_sequence, right_sequence, precision=high...]
    pallas_call x0 -> x5, Pallas kernels: none -> 41.6 us  [the longest x1 13.1 us: local(): call(functools.partial(gradient_kernel, count), [block_shape] * count + [...]
  transfers between devices with their start and end apart: 4 -> 37, of which waited for: 4 -> 15; matrix products, arithmetic and copies ran while one was open for 0% -> 4% of each run, Pallas kernels for 0% -> 30%
where the time goes in v1:
time: 136 us
  starting transfers between devices  45.9 us (34%)
  Pallas kernels  41.6 us (31%)
  waiting for transfers between devices  36.6 us (27%)
  local copies, waits for them, and re-layouts  8.75 us (6%)
  other arithmetic  2.33 us (2%)
    ppermute x23, starting transfers between devices, swap(): lax.ppermute(value, axis, [(here, here ^ distance) for here in range(size)])  30.5 us
    ppermute x23, waiting for transfers between devices, swap(): lax.ppermute(value, axis, [(here, here ^ distance) for here in range(size)])  17.9 us
    pallas_call x1, Pallas kernels, local(): call(functools.partial(gradient_kernel, count), [block_shape] * count + [...  13.1 us
    pallas_call x1, Pallas kernels, local(): call(functools.partial(pair_kernel, count), jax.ShapeDtypeStruct(cotangen...  10.6 us
    pallas_call x1, Pallas kernels, local(): call(functools.partial(weight_kernel, count, inner), [jax.ShapeDtypeStruc...  9.36 us
    pallas_call x1, Pallas kernels, local(): call(functools.partial(left_kernel, count, inner), [jax.ShapeDtypeStruct(...  7.19 us
    ppermute x1, waiting for transfers between devices, ring_scatter(): first = lax.ppermute(parts[half], ('blk', 'inner'), across)  5.72 us
    ppermute x3, starting transfers between devices, ring_gather(): down = lax.ppermute(down, 'blk', downward)  4.99 us
  transfers between devices with their start and end apart: 37, of which 15 were waited for; matrix products, arithmetic and copies ran while one was open for 4% of the time, Pallas kernels for 30%

profile of v1, /device:TPU:0, one launch (start us, length us, event | category | flops | bytes accessed | tf_op | source)
XLA Modules:
  0.0 136.0 jit_solution(4311578411041575611)
XLA Ops:
  0.6 1.3 reshape.26
  2.0 0.3 copy.11
  2.3 3.0 %collective-permute-start = (f32[32,16,128]{2,1,0:T(8,128)S(1)}, f32[32,16,128]{2,1,0:T(8,128)S(1)}, u32[]{:S(2)}, u32[]{:S(2)}) collective-permute-start(f32[32,16,128]{2,1,0:T(8,128)S(1)} %bitcast.53), channel_id=1, source_target_pairs={{8,0},{16,8},{24,16},{28,24},{20,28},{12,20},{4,12},{0,4},{9,1},{1... | collective-permute-start | bytes 786440 | tf_op jit(solution)/shard_map/ppermute | solution.py:271
  5.5 1.0 broadcast_multiply_fusion
  6.5 0.3 mul.14
  6.8 0.3 copy.10
  7.1 4.6 %collective-permute-done.refs_1_ = f32[32,16,128]{2,1,0:T(8,128)S(1)} collective-permute-done((f32[32,16,128]{2,1,0:T(8,128)S(1)}, f32[32,16,128]{2,1,0:T(8,128)S(1)}, u32[]{:S(2)}, u32[]{:S(2)}) %collective-permute-start) | collective-permute-done | bytes 262176 | tf_op jit(solution)/shard_map/ppermute | solution.py:271
  11.7 1.7 %collective-permute-start.1 = (f32[32,16,128]{2,1,0:T(8,128)S(1)}, f32[32,16,128]{2,1,0:T(8,128)S(1)}, u32[]{:S(2)}, u32[]{:S(2)}) collective-permute-start(f32[32,16,128]{2,1,0:T(8,128)S(1)} %collective-permute-done.refs_1_), channel_id=1, source_target_pairs={{8,0},{16,8},{24,16},{28,24},{20,28},{12,20},{4,12},{0,4},{9,1},{1... | collective-permute-start | bytes 786440 | tf_op jit(solution)/shard_map/ppermute | solution.py:271
  13.4 0.3 collective-permute-start.4
  13.8 1.2 copy-done.3
  15.0 13.1 %shard_map.76 = (f32[32,16,128]{2,1,0:T(8,128)S(1)}, f32[32,16,128]{2,1,0:T(8,128)S(1)}, f32[32,16,128]{2,1,0:T(8,128)S(1)}, f32[32,16,128]{2,1,0:T(8,128)S(1)},...) custom-call(f32[1024,128]{1,0:T(8,128)S(1)} %copy-done.5, ...), custom_call_target="tpu_custom_call" | custom-call | flops 3221225472 | bytes 8388608 | tf_op jit(solution)/shard_map/pallas_call | solution.py:317
  28.1 0.7 copy-done
  28.8 0.7 copy-done.1
  29.5 1.7 %collective-permute-start.10 = (f32[32,16,128]{2,1,0:T(8,128)}, f32[32,16,128]{2,1,0:T(8,128)}, u32[]{:S(2)}, u32[]{:S(2)}) collective-permute-start(f32[32,16,128]{2,1,0:T(8,128)} %get-tuple-element.32), channel_id=1, source_target_pairs={{0,8},{8,16},{16,24},{24,28},{28,20},{20,12},{12,4},{4,0},{9,1},{1... | collective-permute-start | bytes 786440 | tf_op jit(solution)/shard_map/ppermute | solution.py:282
  31.5 1.7 %collective-permute-start.5 = (f32[32,16,128]{2,1,0:T(8,128)S(1)}, f32[32,16,128]{2,1,0:T(8,128)S(1)}, u32[]{:S(2)}, u32[]{:S(2)}) collective-permute-start(f32[32,16,128]{2,1,0:T(8,128)S(1)} %collective-permute-done.4.refs_6_), channel_id=1, source_target_pairs={{0,8},{8,16},{16,24},{24,28},{28,20},{20,12},{12,4},{4,0},{1,9},{9... | collective-permute-start | bytes 786440 | tf_op jit(solution)/shard_map/ppermute | solution.py:270
  33.3 5.7 %collective-permute-done.10 = f32[32,16,128]{2,1,0:T(8,128)} collective-permute-done((f32[32,16,128]{2,1,0:T(8,128)}, f32[32,16,128]{2,1,0:T(8,128)}, u32[]{:S(2)}, u32[]{:S(2)}) %collective-permute-start.10) | collective-permute-done | bytes 262176 | tf_op jit(solution)/shard_map/ppermute | solution.py:282
  39.0 1.1 select_add_fusion.1
  40.1 0.4 collective-permute-start.11
  40.5 1.6 %collective-permute-start.14 = (f32[32,16,128]{2,1,0:T(8,128)S(1)}, f32[32,16,128]{2,1,0:T(8,128)S(1)}, u32[]{:S(2)}, u32[]{:S(2)}) collective-permute-start(f32[32,16,128]{2,1,0:T(8,128)S(1)} %get-tuple-element.43), channel_id=1, source_target_pairs={{8,0},{16,8},{24,16},{28,24},{20,28},{12,20},{4,12},{0,4},{9,1},{1... | collective-permute-start | bytes 786440 | tf_op jit(solution)/shard_map/ppermute | solution.py:287
  42.2 2.3 %collective-permute-done.5.refs_5_ = f32[32,16,128]{2,1,0:T(8,128)S(1)} collective-permute-done((f32[32,16,128]{2,1,0:T(8,128)S(1)}, f32[32,16,128]{2,1,0:T(8,128)S(1)}, u32[]{:S(2)}, u32[]{:S(2)}) %collective-permute-start.5) | collective-permute-done | bytes 262176 | tf_op jit(solution)/shard_map/ppermute | solution.py:270
  44.5 0.5 collective-permute-start.6
  45.0 2.3 %collective-permute-done.11 = f32[32,16,128]{2,1,0:T(8,128)S(1)} collective-permute-done((f32[32,16,128]{2,1,0:T(8,128)S(1)}, f32[32,16,128]{2,1,0:T(8,128)S(1)}, u32[]{:S(2)}, u32[]{:S(2)}) %collective-permute-start.11) | collective-permute-done | bytes 262176 | tf_op jit(solution)/shard_map/ppermute | solution.py:286
  47.3 0.5 collective-permute-start.12
  47.8 0.4 collective-permute-done.14
  48.2 1.3 collective-permute-start.15
  49.5 3.4 %collective-permute-done.6.refs_4_ = f32[32,16,128]{2,1,0:T(8,128)S(1)} collective-permute-done((f32[32,16,128]{2,1,0:T(8,128)S(1)}, f32[32,16,128]{2,1,0:T(8,128)S(1)}, u32[]{:S(2)}, u32[]{:S(2)}) %collective-permute-start.6) | collective-permute-done | bytes 262176 | tf_op jit(solution)/shard_map/ppermute | solution.py:274
  52.9 1.2 copy-done.4
  54.1 9.4 %shard_map.78 = (f32[8,32,128]{2,1,0:T(8,128)S(1)}, f32[8,32,128]{2,1,0:T(8,128)S(1)}, f32[8,32,128]{2,1,0:T(8,128)S(1)}, f32[8,32,128]{2,1,0:T(8,128)S(1)}) custom-call(f32[512,128]{1,0:T(8,128)S(1)} %bitcast.59, f32[16,8,16,128]{3,2,1,0:T(8,128)S(1)} %copy-done.4, f32[32,16,128]{2,1,0:T(8,128)S(1)} %bitcast.55, ...), custom_call_target="tpu_custom_call" | custom-call | flops 3221225472 | bytes 8388608 | tf_op jit(solution)/shard_map/pallas_call | solution.py:329
  63.5 1.6 %collective-permute-start.18 = (f32[8,32,128]{2,1,0:T(8,128)S(1)}, f32[8,32,128]{2,1,0:T(8,128)S(1)}, u32[]{:S(2)}, u32[]{:S(2)}) collective-permute-start(f32[8,32,128]{2,1,0:T(8,128)S(1)} %get-tuple-element.38), channel_id=1, source_target_pairs={{0,2},{1,3},{2,0},{3,1},{4,6},{5,7},{6,4},{7,5},{8,10},{9,11},{10,... | collective-permute-start | bytes 393224 | tf_op jit(solution)/shard_map/ppermute | solution.py:295
  65.1 0.3 collective-permute-start.19
  65.4 0.5 collective-permute-start.13
  66.0 1.6 %collective-permute-start.16 = (f32[32,16,128]{2,1,0:T(8,128)S(1)}, f32[32,16,128]{2,1,0:T(8,128)S(1)}, u32[]{:S(2)}, u32[]{:S(2)}) collective-permute-start(f32[32,16,128]{2,1,0:T(8,128)S(1)} %add.72), channel_id=1, source_target_pairs={{8,0},{16,8},{24,16},{28,24},{20,28},{12,20},{4,12},{0,4},{9,1},{1... | collective-permute-start | bytes 786440 | tf_op jit(solution)/shard_map/ppermute | solution.py:287
  67.6 2.3 %collective-permute-done.18 = f32[8,32,128]{2,1,0:T(8,128)S(1)} collective-permute-done((f32[8,32,128]{2,1,0:T(8,128)S(1)}, f32[8,32,128]{2,1,0:T(8,128)S(1)}, u32[]{:S(2)}, u32[]{:S(2)}) %collective-permute-start.18) | collective-permute-done | bytes 131104 | tf_op jit(solution)/shard_map/ppermute | solution.py:295
  69.9 1.9 %collective-permute-done.19 = f32[8,32,128]{2,1,0:T(8,128)S(1)} collective-permute-done((f32[8,32,128]{2,1,0:T(8,128)S(1)}, f32[8,32,128]{2,1,0:T(8,128)S(1)}, u32[]{:S(2)}, u32[]{:S(2)}) %collective-permute-start.19) | collective-permute-done | bytes 131104 | tf_op jit(solution)/shard_map/ppermute | solution.py:295
  71.9 1.6 %collective-permute-start.20 = (f32[32,128]{1,0:T(8,128)S(1)}, f32[32,128]{1,0:T(8,128)S(1)}, u32[]{:S(2)}, u32[]{:S(2)}) collective-permute-start(f32[32,128]{1,0:T(8,128)S(1)} %get-tuple-element.44), channel_id=1, source_target_pairs={{0,4},{4,0},{8,12},{12,8},{16,20},{20,16},{24,28},{28,24},{1,5},{5... | collective-permute-start | bytes 49160 | tf_op jit(solution)/shard_map/ppermute | solution.py:295
  73.5 1.6 %collective-permute-start.21 = (f32[32,128]{1,0:T(8,128)S(1)}, f32[32,128]{1,0:T(8,128)S(1)}, u32[]{:S(2)}, u32[]{:S(2)}) collective-permute-start(f32[32,128]{1,0:T(8,128)S(1)} %get-tuple-element.50), channel_id=1, source_target_pairs={{0,8},{4,12},{8,0},{12,4},{16,24},{20,28},{24,16},{28,20},{1,9},{5... | collective-permute-start | bytes 49160 | tf_op jit(solution)/shard_map/ppermute | solution.py:295
  75.1 10.6 %shard_map.75 = f32[16,8,16,128]{3,2,1,0:T(8,128)} custom-call(f32[512,128]{1,0:T(8,128)S(1)} %bitcast.60, f32[1024,128]{1,0:T(8,128)S(1)} %copy-done.6, f32[32,16,128]{2,1,0:T(8,128)S(1)} %bitcast.56, f32[32,16,128]{2,1,0:T(8,128)S(1)} %collective-permute-done.refs_1_, f32[32,16,128]{2,1,0:T(8,128)S(1)} %collective-permute-done.1.refs_2_, ...), custom_call_target="tpu_custom_call" | custom-call | flops 3221225472 | bytes 8388608 | tf_op jit(solution)/shard_map/pallas_call | solution.py:363
  85.7 0.3 collective-permute-start.22
  86.0 1.2 collective-permute-start.23
  87.3 2.7 %collective-permute-start.24 = (f32[32,128]{1,0:T(8,128)S(1)}, f32[32,128]{1,0:T(8,128)S(1)}, u32[]{:S(2)}, u32[]{:S(2)}) collective-permute-start(f32[32,128]{1,0:T(8,128)S(1)} %get-tuple-element.47), channel_id=1, source_target_pairs={{0,20},{4,16},{8,28},{12,24},{16,4},{20,0},{24,12},{28,8},{1,21},{... | collective-permute-start | bytes 49160 | tf_op jit(solution)/shard_map/ppermute | solution.py:295
  90.0 1.1 collective-permute-start.25
  91.1 2.6 %collective-permute-start.26 = (f32[32,128]{1,0:T(8,128)S(1)}, f32[32,128]{1,0:T(8,128)S(1)}, u32[]{:S(2)}, u32[]{:S(2)}) collective-permute-start(f32[32,128]{1,0:T(8,128)S(1)} %get-tuple-element.45), channel_id=1, source_target_pairs={{0,28},{4,24},{8,20},{12,16},{16,12},{20,8},{24,4},{28,0},{1,29},{... | collective-permute-start | bytes 49160 | tf_op jit(solution)/shard_map/ppermute | solution.py:295
  93.8 1.7 %collective-permute-done.25 = f32[32,128]{1,0:T(8,128)S(1)} collective-permute-done((f32[32,128]{1,0:T(8,128)S(1)}, f32[32,128]{1,0:T(8,128)S(1)}, u32[]{:S(2)}, u32[]{:S(2)}) %collective-permute-start.25) | collective-permute-done | bytes 16416 | tf_op jit(solution)/shard_map/ppermute | solution.py:295
  95.5 2.0 %collective-permute-done.26 = f32[32,128]{1,0:T(8,128)S(1)} collective-permute-done((f32[32,128]{1,0:T(8,128)S(1)}, f32[32,128]{1,0:T(8,128)S(1)}, u32[]{:S(2)}, u32[]{:S(2)}) %collective-permute-start.26) | collective-permute-done | bytes 16416 | tf_op jit(solution)/shard_map/ppermute | solution.py:295
  97.5 0.6 collective-permute-start.27
  98.1 7.2 %shard_map.77 = (f32[32,512]{1,0:T(8,128)S(1)}, f32[32,512]{1,0:T(8,128)S(1)}, f32[32,512]{1,0:T(8,128)S(1)}, f32[32,512]{1,0:T(8,128)S(1)}) custom-call(bf16[8,1024,256]{2,1,0:T(8,128)(2,1)} %get-tuple-element.22.high_ref, bf16[8,1024,256]{2,1,0:T(8,128)(2,1)} %get-tuple-element.23.low_ref, f32[32,16,128]{2,1,0:T(8,128)S(1)} %bitcast.57, ...), custom_call_target="tpu_custom_call" | custom-call | flops 1610612736 | bytes 8388608 | tf_op jit(solution)/shard_map/pallas_call | solution.py:348
  105.3 0.3 copy.13
  105.7 1.2 reshape.29
  106.9 1.5 %collective-permute-start.8 = (f32[32,512]{1,0:T(8,128)S(1)}, f32[32,512]{1,0:T(8,128)S(1)}, u32[]{:S(2)}, u32[]{:S(2)}) collective-permute-start(f32[32,512]{1,0:T(8,128)S(1)} %get-tuple-element.26), channel_id=1, source_target_pairs={{0,2},{1,3},{2,0},{3,1},{4,6},{5,7},{6,4},{7,5},{8,10},{9,11},{10,... | collective-permute-start | bytes 196616 | tf_op jit(solution)/shard_map/ppermute | solution.py:295
  108.4 0.4 collective-permute-start.9
  108.8 2.9 %collective-permute-start.29 = (f32[32,128]{1,0:T(8,128)S(1)}, f32[32,128]{1,0:T(8,128)S(1)}, u32[]{:S(2)}, u32[]{:S(2)}) collective-permute-start(f32[32,128]{1,0:T(8,128)S(1)} %get-tuple-element.41.refs_0_), channel_id=1, source_target_pairs={{0,12},{4,8},{8,4},{12,0},{16,28},{20,24},{24,20},{28,16},{1,13},{... | collective-permute-start | bytes 49160 | tf_op jit(solution)/shard_map/ppermute | solution.py:295
  111.7 0.8 collective-permute-done.28.refs_2_
  112.5 1.2 collective-permute-start.30
  113.7 3.9 %collective-permute-start.31 = (f32[32,128]{1,0:T(8,128)S(1)}, f32[32,128]{1,0:T(8,128)S(1)}, u32[]{:S(2)}, u32[]{:S(2)}) collective-permute-start(f32[32,128]{1,0:T(8,128)S(1)} %get-tuple-element.41.refs_0_), channel_id=1, source_target_pairs={{0,20},{4,16},{8,28},{12,24},{16,4},{20,0},{24,12},{28,8},{1,21},{... | collective-permute-start | bytes 49160 | tf_op jit(solution)/shard_map/ppermute | solution.py:295
  117.6 2.2 %collective-permute-start.32 = (f32[32,128]{1,0:T(8,128)S(1)}, f32[32,128]{1,0:T(8,128)S(1)}, u32[]{:S(2)}, u32[]{:S(2)}) collective-permute-start(f32[32,128]{1,0:T(8,128)S(1)} %get-tuple-element.41.refs_0_), channel_id=1, source_target_pairs={{0,24},{4,28},{8,16},{12,20},{16,8},{20,12},{24,0},{28,4},{1,25},{... | collective-permute-start | bytes 49160 | tf_op jit(solution)/shard_map/ppermute | solution.py:295
  119.9 2.7 %collective-permute-start.33 = (f32[32,128]{1,0:T(8,128)S(1)}, f32[32,128]{1,0:T(8,128)S(1)}, u32[]{:S(2)}, u32[]{:S(2)}) collective-permute-start(f32[32,128]{1,0:T(8,128)S(1)} %get-tuple-element.41.refs_0_), channel_id=1, source_target_pairs={{0,28},{4,24},{8,20},{12,16},{16,12},{20,8},{24,4},{28,0},{1,29},{... | collective-permute-start | bytes 49160 | tf_op jit(solution)/shard_map/ppermute | solution.py:295
  122.6 0.6 collective-permute-done.32.refs_6_
  123.2 3.1 %collective-permute-done.33.refs_7_ = f32[32,128]{1,0:T(8,128)S(1)} collective-permute-done((f32[32,128]{1,0:T(8,128)S(1)}, f32[32,128]{1,0:T(8,128)S(1)}, u32[]{:S(2)}, u32[]{:S(2)}) %collective-permute-start.33) | collective-permute-done | bytes 16416 | tf_op jit(solution)/shard_map/ppermute | solution.py:295
  126.3 1.5 %collective-permute-start.35 = (f32[8,32,128]{2,1,0:T(8,128)S(1)}, f32[8,32,128]{2,1,0:T(8,128)S(1)}, u32[]{:S(2)}, u32[]{:S(2)}) collective-permute-start(f32[8,32,128]{2,1,0:T(8,128)S(1)} %constant_dynamic-update-slice_fusion), channel_id=1, source_target_pairs={{0,2},{1,3},{2,0},{3,1},{4,6},{5,7},{6,4},{7,5},{8,10},{9,11},{10,... | collective-permute-start | bytes 393224 | tf_op jit(solution)/shard_map/ppermute | solution.py:295
  127.8 0.4 collective-permute-start.36
  128.4 0.8 reshape.28
  129.2 3.4 %collective-permute-done.35.refs_9_ = f32[8,32,128]{2,1,0:T(8,128)S(1)} collective-permute-done((f32[8,32,128]{2,1,0:T(8,128)S(1)}, f32[8,32,128]{2,1,0:T(8,128)S(1)}, u32[]{:S(2)}, u32[]{:S(2)}) %collective-permute-start.35) | collective-permute-done | bytes 131104 | tf_op jit(solution)/shard_map/ppermute | solution.py:295
  132.6 2.0 %collective-permute-done.36.refs_10_ = f32[8,32,128]{2,1,0:T(8,128)S(1)} collective-permute-done((f32[8,32,128]{2,1,0:T(8,128)S(1)}, f32[8,32,128]{2,1,0:T(8,128)S(1)}, u32[]{:S(2)}, u32[]{:S(2)}) %collective-permute-start.36) | collective-permute-done | bytes 131104 | tf_op jit(solution)/shard_map/ppermute | solution.py:295
  134.6 1.3 shard_map.79
  (57 shorter events, 1.1 us)
Async XLA Ops:
  0.6 13.1 %copy-start.5 = (f32[1024,128]{1,0:T(8,128)S(1)}, f32[1024,128]{1,0:T(8,128)}, u32[]{:S(2)}) copy-start(f32[1024,128]{1,0:T(8,128)} %weight_ref.3) | copy-start | bytes 1572868
  2.3 9.4 %collective-permute-start = (f32[32,16,128]{2,1,0:T(8,128)S(1)}, f32[32,16,128]{2,1,0:T(8,128)S(1)}, u32[]{:S(2)}, u32[]{:S(2)}) collective-permute-start(f32[32,16,128]{2,1,0:T(8,128)S(1)} %bitcast.53), channel_id=1, source_target_pairs={{8,0},{16,8},{24,16},{28,24},{20,28},{12,20},{4,12},{0,4},{9,1},{1... | collective-permute-start | bytes 786440 | tf_op jit(solution)/shard_map/ppermute | solution.py:271
  5.4 8.0 %collective-permute-start.3 = (f32[32,16,128]{2,1,0:T(8,128)S(1)}, f32[32,16,128]{2,1,0:T(8,128)S(1)}, u32[]{:S(2)}, u32[]{:S(2)}) collective-permute-start(f32[32,16,128]{2,1,0:T(8,128)S(1)} %bitcast.54), channel_id=1, source_target_pairs={{0,8},{8,16},{16,24},{24,28},{28,20},{20,12},{12,4},{4,0},{1,9},{9... | collective-permute-start | bytes 786440 | tf_op jit(solution)/shard_map/ppermute | solution.py:270
  11.7 19.5 %collective-permute-start.1 = (f32[32,16,128]{2,1,0:T(8,128)S(1)}, f32[32,16,128]{2,1,0:T(8,128)S(1)}, u32[]{:S(2)}, u32[]{:S(2)}) collective-permute-start(f32[32,16,128]{2,1,0:T(8,128)S(1)} %collective-permute-done.refs_1_), channel_id=1, source_target_pairs={{8,0},{16,8},{24,16},{28,24},{20,28},{12,20},{4,12},{0,4},{9,1},{1... | collective-permute-start | bytes 786440 | tf_op jit(solution)/shard_map/ppermute | solution.py:271
  13.4 18.1 %collective-permute-start.4 = (f32[32,16,128]{2,1,0:T(8,128)S(1)}, f32[32,16,128]{2,1,0:T(8,128)S(1)}, u32[]{:S(2)}, u32[]{:S(2)}) collective-permute-start(f32[32,16,128]{2,1,0:T(8,128)S(1)} %collective-permute-done.3.refs_7_), channel_id=1, source_target_pairs={{0,8},{8,16},{16,24},{24,28},{28,20},{20,12},{12,4},{4,0},{1,9},{9... | collective-permute-start | bytes 786440 | tf_op jit(solution)/shard_map/ppermute | solution.py:270
  13.8 1.2 copy-start.3
  28.1 0.7 copy-start
  28.8 0.7 copy-start.1
  29.5 9.5 %collective-permute-start.10 = (f32[32,16,128]{2,1,0:T(8,128)}, f32[32,16,128]{2,1,0:T(8,128)}, u32[]{:S(2)}, u32[]{:S(2)}) collective-permute-start(f32[32,16,128]{2,1,0:T(8,128)} %get-tuple-element.32), channel_id=1, source_target_pairs={{0,8},{8,16},{16,24},{24,28},{28,20},{20,12},{12,4},{4,0},{9,1},{1... | collective-permute-start | bytes 786440 | tf_op jit(solution)/shard_map/ppermute | solution.py:282
  31.2 10.9 %collective-permute-start.2 = (f32[32,16,128]{2,1,0:T(8,128)S(1)}, f32[32,16,128]{2,1,0:T(8,128)S(1)}, u32[]{:S(2)}, u32[]{:S(2)}) collective-permute-start(f32[32,16,128]{2,1,0:T(8,128)S(1)} %collective-permute-done.1.refs_2_), channel_id=1, source_target_pairs={{8,0},{16,8},{24,16},{28,24},{20,28},{12,20},{4,12},{0,4},{9,1},{1... | collective-permute-start | bytes 786440 | tf_op jit(solution)/shard_map/ppermute | solution.py:271
  31.5 12.9 %collective-permute-start.5 = (f32[32,16,128]{2,1,0:T(8,128)S(1)}, f32[32,16,128]{2,1,0:T(8,128)S(1)}, u32[]{:S(2)}, u32[]{:S(2)}) collective-permute-start(f32[32,16,128]{2,1,0:T(8,128)S(1)} %collective-permute-done.4.refs_6_), channel_id=1, source_target_pairs={{0,8},{8,16},{16,24},{24,28},{28,20},{20,12},{12,4},{4,0},{1,9},{9... | collective-permute-start | bytes 786440 | tf_op jit(solution)/shard_map/ppermute | solution.py:270
  40.1 7.2 %collective-permute-start.11 = (f32[32,16,128]{2,1,0:T(8,128)S(1)}, f32[32,16,128]{2,1,0:T(8,128)S(1)}, u32[]{:S(2)}, u32[]{:S(2)}) collective-permute-start(f32[32,16,128]{2,1,0:T(8,128)S(1)} %get-tuple-element.42), channel_id=1, source_target_pairs={{0,8},{8,16},{16,24},{24,28},{28,20},{20,12},{12,4},{4,0},{1,9},{9... | collective-permute-start | bytes 786440 | tf_op jit(solution)/shard_map/ppermute | solution.py:286
  40.5 7.7 %collective-permute-start.14 = (f32[32,16,128]{2,1,0:T(8,128)S(1)}, f32[32,16,128]{2,1,0:T(8,128)S(1)}, u32[]{:S(2)}, u32[]{:S(2)}) collective-permute-start(f32[32,16,128]{2,1,0:T(8,128)S(1)} %get-tuple-element.43), channel_id=1, source_target_pairs={{8,0},{16,8},{24,16},{28,24},{20,28},{12,20},{4,12},{0,4},{9,1},{1... | collective-permute-start | bytes 786440 | tf_op jit(solution)/shard_map/ppermute | solution.py:287
  44.5 8.4 %collective-permute-start.6 = (f32[32,16,128]{2,1,0:T(8,128)S(1)}, f32[32,16,128]{2,1,0:T(8,128)S(1)}, u32[]{:S(2)}, u32[]{:S(2)}) collective-permute-start(f32[32,16,128]{2,1,0:T(8,128)S(1)} %broadcast_select_fusion), channel_id=1, source_target_pairs={{0,8},{8,16},{16,24},{24,28},{28,20},{20,12},{12,4},{4,0},{9,1},{1... | collective-permute-start | bytes 786440 | tf_op jit(solution)/shard_map/ppermute | solution.py:274
  47.3 18.1 %collective-permute-start.12 = (f32[32,16,128]{2,1,0:T(8,128)S(1)}, f32[32,16,128]{2,1,0:T(8,128)S(1)}, u32[]{:S(2)}, u32[]{:S(2)}) collective-permute-start(f32[32,16,128]{2,1,0:T(8,128)S(1)} %add.67), channel_id=1, source_target_pairs={{0,8},{8,16},{16,24},{24,28},{28,20},{20,12},{12,4},{4,0},{1,9},{9... | collective-permute-start | bytes 786440 | tf_op jit(solution)/shard_map/ppermute | solution.py:286
  48.2 26.9 %copy-start.6 = (f32[1024,128]{1,0:T(8,128)S(1)}, f32[1024,128]{1,0:T(8,128)}, u32[]{:S(2)}) copy-start(f32[1024,128]{1,0:T(8,128)} %weight_ref.3) | copy-start | bytes 1572868
  48.2 17.7 %collective-permute-start.15 = (f32[32,16,128]{2,1,0:T(8,128)S(1)}, f32[32,16,128]{2,1,0:T(8,128)S(1)}, u32[]{:S(2)}, u32[]{:S(2)}) collective-permute-start(f32[32,16,128]{2,1,0:T(8,128)S(1)} %add.71), channel_id=1, source_target_pairs={{8,0},{16,8},{24,16},{28,24},{20,28},{12,20},{4,12},{0,4},{9,1},{1... | collective-permute-start | bytes 786440 | tf_op jit(solution)/shard_map/ppermute | solution.py:287
  52.9 1.2 copy-start.4
  63.5 4.2 %collective-permute-start.17 = (f32[8,32,128]{2,1,0:T(8,128)S(1)}, f32[8,32,128]{2,1,0:T(8,128)S(1)}, u32[]{:S(2)}, u32[]{:S(2)}) collective-permute-start(f32[8,32,128]{2,1,0:T(8,128)S(1)} %get-tuple-element.37), channel_id=1, source_target_pairs={{0,1},{1,0},{2,3},{3,2},{4,5},{5,4},{6,7},{7,6},{8,9},{9,8},{10,11... | collective-permute-start | bytes 393224 | tf_op jit(solution)/shard_map/ppermute | solution.py:295
  63.5 6.4 %collective-permute-start.18 = (f32[8,32,128]{2,1,0:T(8,128)S(1)}, f32[8,32,128]{2,1,0:T(8,128)S(1)}, u32[]{:S(2)}, u32[]{:S(2)}) collective-permute-start(f32[8,32,128]{2,1,0:T(8,128)S(1)} %get-tuple-element.38), channel_id=1, source_target_pairs={{0,2},{1,3},{2,0},{3,1},{4,6},{5,7},{6,4},{7,5},{8,10},{9,11},{10,... | collective-permute-start | bytes 393224 | tf_op jit(solution)/shard_map/ppermute | solution.py:295
  65.1 6.7 %collective-permute-start.19 = (f32[8,32,128]{2,1,0:T(8,128)S(1)}, f32[8,32,128]{2,1,0:T(8,128)S(1)}, u32[]{:S(2)}, u32[]{:S(2)}) collective-permute-start(f32[8,32,128]{2,1,0:T(8,128)S(1)} %get-tuple-element.39), channel_id=1, source_target_pairs={{0,3},{1,2},{2,1},{3,0},{4,7},{5,6},{6,5},{7,4},{8,11},{9,10},{10,... | collective-permute-start | bytes 393224 | tf_op jit(solution)/shard_map/ppermute | solution.py:295
  65.4 20.6 %collective-permute-start.13 = (f32[32,16,128]{2,1,0:T(8,128)S(1)}, f32[32,16,128]{2,1,0:T(8,128)S(1)}, u32[]{:S(2)}, u32[]{:S(2)}) collective-permute-start(f32[32,16,128]{2,1,0:T(8,128)S(1)} %add.68), channel_id=1, source_target_pairs={{0,8},{8,16},{16,24},{24,28},{28,20},{20,12},{12,4},{4,0},{1,9},{9... | collective-permute-start | bytes 786440 | tf_op jit(solution)/shard_map/ppermute | solution.py:286
  66.0 21.3 %collective-permute-start.16 = (f32[32,16,128]{2,1,0:T(8,128)S(1)}, f32[32,16,128]{2,1,0:T(8,128)S(1)}, u32[]{:S(2)}, u32[]{:S(2)}) collective-permute-start(f32[32,16,128]{2,1,0:T(8,128)S(1)} %add.72), channel_id=1, source_target_pairs={{8,0},{16,8},{24,16},{28,24},{20,28},{12,20},{4,12},{0,4},{9,1},{1... | collective-permute-start | bytes 786440 | tf_op jit(solution)/shard_map/ppermute | solution.py:287
  71.9 18.1 %collective-permute-start.20 = (f32[32,128]{1,0:T(8,128)S(1)}, f32[32,128]{1,0:T(8,128)S(1)}, u32[]{:S(2)}, u32[]{:S(2)}) collective-permute-start(f32[32,128]{1,0:T(8,128)S(1)} %get-tuple-element.44), channel_id=1, source_target_pairs={{0,4},{4,0},{8,12},{12,8},{16,20},{20,16},{24,28},{28,24},{1,5},{5... | collective-permute-start | bytes 49160 | tf_op jit(solution)/shard_map/ppermute | solution.py:295
  73.5 20.2 %copy-start.2 = (f32[32,16,128]{2,1,0:T(8,128)S(1)}, f32[32,16,128]{2,1,0:T(8,128)}, u32[]{:S(2)}) copy-start(f32[32,16,128]{2,1,0:T(8,128)} %copy-done.1) | copy-start | bytes 786436
  73.5 17.6 %collective-permute-start.21 = (f32[32,128]{1,0:T(8,128)S(1)}, f32[32,128]{1,0:T(8,128)S(1)}, u32[]{:S(2)}, u32[]{:S(2)}) collective-permute-start(f32[32,128]{1,0:T(8,128)S(1)} %get-tuple-element.50), channel_id=1, source_target_pairs={{0,8},{4,12},{8,0},{12,4},{16,24},{20,28},{24,16},{28,20},{1,9},{5... | collective-permute-start | bytes 49160 | tf_op jit(solution)/shard_map/ppermute | solution.py:295
  85.7 8.1 %collective-permute-start.22 = (f32[32,128]{1,0:T(8,128)S(1)}, f32[32,128]{1,0:T(8,128)S(1)}, u32[]{:S(2)}, u32[]{:S(2)}) collective-permute-start(f32[32,128]{1,0:T(8,128)S(1)} %get-tuple-element.49), channel_id=1, source_target_pairs={{0,12},{4,8},{8,4},{12,0},{16,28},{20,24},{24,20},{28,16},{1,13},{... | collective-permute-start | bytes 49160 | tf_op jit(solution)/shard_map/ppermute | solution.py:295
  86.0 7.7 %collective-permute-start.23 = (f32[32,128]{1,0:T(8,128)S(1)}, f32[32,128]{1,0:T(8,128)S(1)}, u32[]{:S(2)}, u32[]{:S(2)}) collective-permute-start(f32[32,128]{1,0:T(8,128)S(1)} %get-tuple-element.48), channel_id=1, source_target_pairs={{0,16},{4,20},{8,24},{12,28},{16,0},{20,4},{24,8},{28,12},{1,17},{... | collective-permute-start | bytes 49160 | tf_op jit(solution)/shard_map/ppermute | solution.py:295
  87.3 6.5 %collective-permute-start.24 = (f32[32,128]{1,0:T(8,128)S(1)}, f32[32,128]{1,0:T(8,128)S(1)}, u32[]{:S(2)}, u32[]{:S(2)}) collective-permute-start(f32[32,128]{1,0:T(8,128)S(1)} %get-tuple-element.47), channel_id=1, source_target_pairs={{0,20},{4,16},{8,28},{12,24},{16,4},{20,0},{24,12},{28,8},{1,21},{... | collective-permute-start | bytes 49160 | tf_op jit(solution)/shard_map/ppermute | solution.py:295
  90.0 5.5 %collective-permute-start.25 = (f32[32,128]{1,0:T(8,128)S(1)}, f32[32,128]{1,0:T(8,128)S(1)}, u32[]{:S(2)}, u32[]{:S(2)}) collective-permute-start(f32[32,128]{1,0:T(8,128)S(1)} %get-tuple-element.46), channel_id=1, source_target_pairs={{0,24},{4,28},{8,16},{12,20},{16,8},{20,12},{24,0},{28,4},{1,25},{... | collective-permute-start | bytes 49160 | tf_op jit(solution)/shard_map/ppermute | solution.py:295
  91.1 6.4 %collective-permute-start.26 = (f32[32,128]{1,0:T(8,128)S(1)}, f32[32,128]{1,0:T(8,128)S(1)}, u32[]{:S(2)}, u32[]{:S(2)}) collective-permute-start(f32[32,128]{1,0:T(8,128)S(1)} %get-tuple-element.45), channel_id=1, source_target_pairs={{0,28},{4,24},{8,20},{12,16},{16,12},{20,8},{24,4},{28,0},{1,29},{... | collective-permute-start | bytes 49160 | tf_op jit(solution)/shard_map/ppermute | solution.py:295
  97.5 11.2 %collective-permute-start.27 = (f32[32,128]{1,0:T(8,128)S(1)}, f32[32,128]{1,0:T(8,128)S(1)}, u32[]{:S(2)}, u32[]{:S(2)}) collective-permute-start(f32[32,128]{1,0:T(8,128)S(1)} %get-tuple-element.41.refs_0_), channel_id=1, source_target_pairs={{0,4},{4,0},{8,12},{12,8},{16,20},{20,16},{24,28},{28,24},{1,5},{5... | collective-permute-start | bytes 49160 | tf_op jit(solution)/shard_map/ppermute | solution.py:295
  106.9 20.9 %collective-permute-start.7 = (f32[32,512]{1,0:T(8,128)S(1)}, f32[32,512]{1,0:T(8,128)S(1)}, u32[]{:S(2)}, u32[]{:S(2)}) collective-permute-start(f32[32,512]{1,0:T(8,128)S(1)} %get-tuple-element.25), channel_id=1, source_target_pairs={{0,1},{1,0},{2,3},{3,2},{4,5},{5,4},{6,7},{7,6},{8,9},{9,8},{10,11... | collective-permute-start | bytes 196616 | tf_op jit(solution)/shard_map/ppermute | solution.py:295
  106.9 21.3 %collective-permute-start.8 = (f32[32,512]{1,0:T(8,128)S(1)}, f32[32,512]{1,0:T(8,128)S(1)}, u32[]{:S(2)}, u32[]{:S(2)}) collective-permute-start(f32[32,512]{1,0:T(8,128)S(1)} %get-tuple-element.26), channel_id=1, source_target_pairs={{0,2},{1,3},{2,0},{3,1},{4,6},{5,7},{6,4},{7,5},{8,10},{9,11},{10,... | collective-permute-start | bytes 196616 | tf_op jit(solution)/shard_map/ppermute | solution.py:295
  108.4 19.8 %collective-permute-start.9 = (f32[32,512]{1,0:T(8,128)S(1)}, f32[32,512]{1,0:T(8,128)S(1)}, u32[]{:S(2)}, u32[]{:S(2)}) collective-permute-start(f32[32,512]{1,0:T(8,128)S(1)} %get-tuple-element.27), channel_id=1, source_target_pairs={{0,3},{1,2},{2,1},{3,0},{4,7},{5,6},{6,5},{7,4},{8,11},{9,10},{10,... | collective-permute-start | bytes 196616 | tf_op jit(solution)/shard_map/ppermute | solution.py:295
  108.8 3.7 %collective-permute-start.28 = (f32[32,128]{1,0:T(8,128)S(1)}, f32[32,128]{1,0:T(8,128)S(1)}, u32[]{:S(2)}, u32[]{:S(2)}) collective-permute-start(f32[32,128]{1,0:T(8,128)S(1)} %get-tuple-element.41.refs_0_), channel_id=1, source_target_pairs={{0,8},{4,12},{8,0},{12,4},{16,24},{20,28},{24,16},{28,20},{1,9},{5... | collective-permute-start | bytes 49160 | tf_op jit(solution)/shard_map/ppermute | solution.py:295
  108.8 4.9 %collective-permute-start.29 = (f32[32,128]{1,0:T(8,128)S(1)}, f32[32,128]{1,0:T(8,128)S(1)}, u32[]{:S(2)}, u32[]{:S(2)}) collective-permute-start(f32[32,128]{1,0:T(8,128)S(1)} %get-tuple-element.41.refs_0_), channel_id=1, source_target_pairs={{0,12},{4,8},{8,4},{12,0},{16,28},{20,24},{24,20},{28,16},{1,13},{... | collective-permute-start | bytes 49160 | tf_op jit(solution)/shard_map/ppermute | solution.py:295
  112.5 5.1 %collective-permute-start.30 = (f32[32,128]{1,0:T(8,128)S(1)}, f32[32,128]{1,0:T(8,128)S(1)}, u32[]{:S(2)}, u32[]{:S(2)}) collective-permute-start(f32[32,128]{1,0:T(8,128)S(1)} %get-tuple-element.41.refs_0_), channel_id=1, source_target_pairs={{0,16},{4,20},{8,24},{12,28},{16,0},{20,4},{24,8},{28,12},{1,17},{... | collective-permute-start | bytes 49160 | tf_op jit(solution)/shard_map/ppermute | solution.py:295
  113.7 6.2 %collective-permute-start.31 = (f32[32,128]{1,0:T(8,128)S(1)}, f32[32,128]{1,0:T(8,128)S(1)}, u32[]{:S(2)}, u32[]{:S(2)}) collective-permute-start(f32[32,128]{1,0:T(8,128)S(1)} %get-tuple-element.41.refs_0_), channel_id=1, source_target_pairs={{0,20},{4,16},{8,28},{12,24},{16,4},{20,0},{24,12},{28,8},{1,21},{... | collective-permute-start | bytes 49160 | tf_op jit(solution)/shard_map/ppermute | solution.py:295
  117.6 5.5 %collective-permute-start.32 = (f32[32,128]{1,0:T(8,128)S(1)}, f32[32,128]{1,0:T(8,128)S(1)}, u32[]{:S(2)}, u32[]{:S(2)}) collective-permute-start(f32[32,128]{1,0:T(8,128)S(1)} %get-tuple-element.41.refs_0_), channel_id=1, source_target_pairs={{0,24},{4,28},{8,16},{12,20},{16,8},{20,12},{24,0},{28,4},{1,25},{... | collective-permute-start | bytes 49160 | tf_op jit(solution)/shard_map/ppermute | solution.py:295
  119.9 6.4 %collective-permute-start.33 = (f32[32,128]{1,0:T(8,128)S(1)}, f32[32,128]{1,0:T(8,128)S(1)}, u32[]{:S(2)}, u32[]{:S(2)}) collective-permute-start(f32[32,128]{1,0:T(8,128)S(1)} %get-tuple-element.41.refs_0_), channel_id=1, source_target_pairs={{0,28},{4,24},{8,20},{12,16},{16,12},{20,8},{24,4},{28,0},{1,29},{... | collective-permute-start | bytes 49160 | tf_op jit(solution)/shard_map/ppermute | solution.py:295
  126.3 2.9 %collective-permute-start.34 = (f32[8,32,128]{2,1,0:T(8,128)S(1)}, f32[8,32,128]{2,1,0:T(8,128)S(1)}, u32[]{:S(2)}, u32[]{:S(2)}) collective-permute-start(f32[8,32,128]{2,1,0:T(8,128)S(1)} %constant_dynamic-update-slice_fusion), channel_id=1, source_target_pairs={{0,1},{1,0},{2,3},{3,2},{4,5},{5,4},{6,7},{7,6},{8,9},{9,8},{10,11... | collective-permute-start | bytes 393224 | tf_op jit(solution)/shard_map/ppermute | solution.py:295
  126.3 6.3 %collective-permute-start.35 = (f32[8,32,128]{2,1,0:T(8,128)S(1)}, f32[8,32,128]{2,1,0:T(8,128)S(1)}, u32[]{:S(2)}, u32[]{:S(2)}) collective-permute-start(f32[8,32,128]{2,1,0:T(8,128)S(1)} %constant_dynamic-update-slice_fusion), channel_id=1, source_target_pairs={{0,2},{1,3},{2,0},{3,1},{4,6},{5,7},{6,4},{7,5},{8,10},{9,11},{10,... | collective-permute-start | bytes 393224 | tf_op jit(solution)/shard_map/ppermute | solution.py:295
  127.8 6.8 %collective-permute-start.36 = (f32[8,32,128]{2,1,0:T(8,128)S(1)}, f32[8,32,128]{2,1,0:T(8,128)S(1)}, u32[]{:S(2)}, u32[]{:S(2)}) collective-permute-start(f32[8,32,128]{2,1,0:T(8,128)S(1)} %constant_dynamic-update-slice_fusion), channel_id=1, source_target_pairs={{0,3},{1,2},{2,1},{3,0},{4,7},{5,6},{6,5},{7,4},{8,11},{9,10},{10,... | collective-permute-start | bytes 393224 | tf_op jit(solution)/shard_map/ppermute | solution.py:295

commit v2 on v1

--- a/solution.py
+++ b/solution.py
@@ -52,20 +52,13 @@
     return weight_ref[pl.ds(y, channels, stride=channels), :]
 
 
-def gradient_kernel(count, weight_ref, cotangent_ref, left_ref, *refs):
-    right_refs = refs[:count]
-    high_ref, low_ref, weight_cat, left_flip = refs[count:]
+def gradient_kernel(count, weight_ref, cotangent_ref, high_ref, low_ref, weight_cat):
     rows = cotangent_ref.shape[0]
     channels = ENTRY_CHANNELS
-    sequences = left_ref.shape[1]
     blocks = slot_blocks(count)
-    columns = count * cotangent_ref.shape[2]
     for y in range(channels):
         high, low = halves(weight_by_y(weight_ref, y, channels))
         weight_cat[y * channels : (y + 1) * channels, :] = jnp.concatenate([high, low, high], 1)
-    flip_high, flip_low = halves(left_ref[...].T)
-    left_flip[:sequences, :] = flip_high
-    left_flip[sequences:, :] = flip_low
 
     def grad_step(pair, carry):
         grads = [cotangent_rows(cotangent_ref, 2 * pair + part, blocks) for part in range(2)]
@@ -77,6 +70,18 @@
         return carry
 
     lax.fori_loop(0, rows // 2, grad_step, 0)
+
+
+def right_kernel(count, high_ref, low_ref, left_ref, *refs):
+    right_refs = refs[:count]
+    left_flip = refs[count]
+    rows = 2 * high_ref.shape[0]
+    columns = high_ref.shape[2] // 2
+    channels = ENTRY_CHANNELS
+    sequences = left_ref.shape[1]
+    flip_high, flip_low = halves(left_ref[...].T)
+    left_flip[:sequences, :] = flip_high
+    left_flip[sequences:, :] = flip_low
 
     def right_step(step, carry):
         def stacked(ref):
@@ -138,10 +143,9 @@
     lax.fori_loop(0, channels // 2, step_of, 0)
 
 
-def weight_kernel(count, inner, left_ref, cotangent_ref, *refs):
+def weight_kernel(count, left_ref, cotangent_ref, *refs):
     block_refs = refs[:count]
-    out_refs = refs[count : count + inner]
-    high_ref, low_ref, total = refs[count + inner :]
+    out_ref, high_ref, low_ref, total = refs[count:]
     rows = cotangent_ref.shape[0]
     pairs = cotangent_ref.shape[3]
     blocks = slot_blocks(count)
@@ -156,13 +160,7 @@
         return carry
 
     lax.fori_loop(0, rows // 2, step_of, 0)
-    mine = lax.axis_index("inner")
-    here = lax.axis_index("blk")
-    size = total.shape[0] // (inner * count)
-    for other in range(inner):
-        for part in range(count):
-            chunk = lax.bitwise_xor(mine, other) * count + lax.bitwise_xor(here, part)
-            out_refs[other][part] = total[pl.ds(pl.multiple_of(chunk * size, size), size), :]
+    out_ref[...] = total[...]
 
 
 def left_kernel(count, inner, high_ref, low_ref, *refs):
@@ -194,9 +192,7 @@
         out_refs[other][...] = flipped[pl.ds(start, size), :]
 
 
-def pair_kernel(count, left_ref, weight_ref, *refs):
-    block_refs = refs[:count]
-    out_ref, high_ref, low_ref, weight_flip, weight_rows = refs[count:]
+def pair_kernel(count, high_ref, low_ref, weight_ref, out_ref, weight_flip, weight_rows):
     rows = out_ref.shape[0]
     channels = ENTRY_CHANNELS
     depth = out_ref.shape[2]
@@ -208,7 +204,6 @@
     flip_high, flip_low = halves(weight_rows[...].T)
     weight_flip[:pairs, :] = flip_high
     weight_flip[pairs:, :] = flip_low
-    outer_phase(left_ref, block_refs, high_ref, low_ref, rows)
 
     def step_of(pair, carry):
         first = dot(weight_flip[...], high_ref[pair])
@@ -222,22 +217,11 @@
     lax.fori_loop(0, rows // 2, step_of, 0)
 
 
-def place_kernel(count, inner, *refs):
-    own_refs = refs[:count]
-    other_refs = refs[count : count + inner - 1]
-    out_ref = refs[-1]
-    channels = ENTRY_CHANNELS
-    mine = lax.axis_index("inner")
-    here = lax.axis_index("blk")
-    size = own_refs[0].shape[0]
-    for other in range(inner):
-        for part in range(count):
-            chunk = lax.bitwise_xor(mine, other) * count + lax.bitwise_xor(here, part)
-            first = chunk * size
-            y = first // channels
-            x = lax.rem(first, channels)
-            piece = own_refs[part][...] if other == 0 else other_refs[other - 1][part]
-            out_ref[pl.ds(x * channels + y, size, stride=channels), :] = piece
+def place_kernel(in_ref, out_ref):
+    channels = ENTRY_CHANNELS
+    for y in range(channels):
+        rows = in_ref[y * channels : (y + 1) * channels, :]
+        out_ref[pl.ds(y, channels, stride=channels), :] = rows
 
 
 def call(kernel, out_shape, scratch, flops):
@@ -312,38 +296,37 @@
     left = alignment_left.reshape(rows, sequences, channels).transpose(0, 2, 1)
     left = left.reshape(rows * channels, sequences) * (1.0 / sequences)
 
-    wide = (rows // 2, outer, 2 * columns)
+    wide = jax.ShapeDtypeStruct((rows // 2, outer, 2 * columns), BF16)
     block_shape = jax.ShapeDtypeStruct((channels, depth, sequences), F32)
-    found = call(
+    grads_high, grads_low = call(
         functools.partial(gradient_kernel, count),
-        [block_shape] * count + [jax.ShapeDtypeStruct(wide, BF16)] * 2,
-        [pltpu.VMEM((outer, 3 * pairs), BF16), pltpu.VMEM((2 * sequences, rows * channels), BF16)],
-        2 * flops,
-    )(projection_matrix, cotangent, left)
-    grads_high, grads_low = found[count:]
-    right_grad = ring_scatter(found[:count], count, inner)
+        [wide] * 2,
+        [pltpu.VMEM((outer, 3 * pairs), BF16)],
+        flops,
+    )(projection_matrix, cotangent)
+    right_parts = call(
+        functools.partial(right_kernel, count),
+        [block_shape] * count,
+        [pltpu.VMEM((2 * sequences, rows * channels), BF16)],
+        flops,
+    )(grads_high, grads_low, left)
+    right_grad = ring_scatter(right_parts, count, inner)
     grad_right = right_grad.transpose(1, 2, 0).reshape(depth, features)
 
     size = outer // (count * inner)
-    wide_scratch = [pltpu.VMEM(wide, BF16), pltpu.VMEM(wide, BF16)]
-    weight_parts = call(
-        functools.partial(weight_kernel, count, inner),
-        [jax.ShapeDtypeStruct((count, size, pairs), F32)] * inner,
-        wide_scratch + [pltpu.VMEM((outer, pairs), F32)],
+    weight_part, outer_high, outer_low = call(
+        functools.partial(weight_kernel, count),
+        [jax.ShapeDtypeStruct((outer, pairs), F32)] + [wide] * 2,
+        [pltpu.VMEM((outer, pairs), F32)],
         2 * flops,
     )(left, cotangent, *slots)
-
-    weight_own = weight_parts[0]
-    for other in range(1, inner):
-        weight_own = weight_own + swap(weight_parts[other], "inner", inner, other)
-    weight_sum = weight_own[0]
-    for other in range(1, count):
-        weight_sum = weight_sum + swap(weight_own[other], "blk", count, other)
-    gathered = [weight_sum]
-    for other in range(1, count):
-        gathered.append(swap(weight_sum, "blk", count, other))
-    stacked = jnp.stack(gathered)
-    spread = [swap(stacked, "inner", inner, other) for other in range(1, inner)]
+    everyone = ("blk", "inner")
+    pieces = lax.all_to_all(weight_part.reshape(count * inner, size, pairs), everyone, 0, 0)
+    weight_sum = jnp.sum(pieces, axis=0)
+    weight_full = lax.all_gather(weight_sum, everyone, axis=0, tiled=True)
+    grad_weight = call(
+        place_kernel, jax.ShapeDtypeStruct(projection_matrix.shape, F32), [], 0
+    )(weight_full)
 
     left_parts = call(
         functools.partial(left_kernel, count, inner),
@@ -363,17 +346,9 @@
     pair_update = call(
         functools.partial(pair_kernel, count),
         jax.ShapeDtypeStruct(cotangent.shape, F32),
-        wide_scratch
-        + [pltpu.VMEM((2 * pairs, outer), BF16), pltpu.VMEM((outer, pairs), F32)],
-        2 * flops,
-    )(left, projection_matrix, *slots)
-
-    grad_weight = call(
-        functools.partial(place_kernel, count, inner),
-        jax.ShapeDtypeStruct(projection_matrix.shape, F32),
-        [],
-        0,
-    )(*gathered, *spread)
+        [pltpu.VMEM((2 * pairs, outer), BF16), pltpu.VMEM((outer, pairs), F32)],
+        flops,
+    )(outer_high, outer_low, projection_matrix)
     return (pair_update, grad_left, grad_right, grad_weight)
 
 

time: 136 us -> 145 us (1.066)
  blocking collectives: 0 us -> 41.9 us
  waiting for transfers between devices: 36.6 us -> 12.4 us
  starting transfers between devices: 45.9 us -> 23.7 us
  local copies, waits for them, and re-layouts: 8.75 us -> 15.5 us
  other arithmetic: 2.33 us -> 6.78 us
  Pallas kernels: 41.6 us -> 43.7 us
    all_gather x0 -> x1, blocking collectives: none -> 41.9 us  [local(): weight_full = lax.all_gather(weight_sum, everyone, axis=0, tiled=True)]
    ppermute x23 -> x3, starting transfers between devices: 30.5 us -> 2.01 us  [swap(): lax.ppermute(value, axis, [(here, here ^ distance) for here in range(size)])]
    ppermute x23 -> x3, waiting for transfers between devices: 17.9 us -> 0.01 us  [swap(): lax.ppermute(value, axis, [(here, here ^ distance) for here in range(size)])]
    pallas_call x3 -> x4, Pallas kernels: 23.8 us -> 29.4 us  [the longest x1 12.3 us: local(): call(functools.partial(weight_kernel, count), [jax.ShapeDtypeStruct((oute...]
    all_to_all x0 -> x1, starting transfers between devices: none -> 4.85 us  [local(): lax.all_to_all(weight_part.reshape(count * inner, size, pairs), everyone,...]
    ppermute x3, waiting for transfers between devices: 4.62 us -> 0.01 us  [ring_gather(): down = lax.ppermute(down, 'blk', downward)]
    unnamed x20 -> x24, local copies, waits for them, and re-layouts: 3.89 us -> 8.48 us
    pallas_call x1, Pallas kernels: 10.6 us -> 7.09 us  [local(): call(functools.partial(pair_kernel, count), jax.ShapeDtypeStruct(cotangen...]
  transfers between devices with their start and end apart: 37 -> 18, of which waited for: 15 -> 6; matrix products, arithmetic and copies ran while one was open for 4% -> 8% of each run, Pallas kernels for 30% -> 29%
where the time goes in v2:
time: 145 us
  Pallas kernels  43.7 us (30%)
  blocking collectives  41.9 us (29%)
  starting transfers between devices  23.7 us (16%)
  local copies, waits for them, and re-layouts  15.5 us (11%)
  waiting for transfers between devices  12.4 us (9%)
  other arithmetic  6.78 us (5%)
    all_gather x1, blocking collectives, local(): weight_full = lax.all_gather(weight_sum, everyone, axis=0, tiled=True)  41.9 us
    pallas_call x1, Pallas kernels, local(): call(functools.partial(weight_kernel, count), [jax.ShapeDtypeStruct((oute...  12.3 us
    pallas_call x1, Pallas kernels, local(): call(functools.partial(right_kernel, count), [block_shape] * count, [pltp...  9.82 us
    unnamed x24, local copies, waits for them, and re-layouts  8.48 us
    pallas_call x1, Pallas kernels, local(): call(functools.partial(left_kernel, count, inner), [jax.ShapeDtypeStruct(...  7.22 us
    pallas_call x1, Pallas kernels, local(): call(functools.partial(pair_kernel, count), jax.ShapeDtypeStruct(cotangen...  7.09 us
    pallas_call x1, Pallas kernels, local(): call(functools.partial(gradient_kernel, count), [wide] * 2, [pltpu.VMEM((...  6.01 us
    ppermute x1, waiting for transfers between devices, ring_scatter(): first = lax.ppermute(parts[half], ('blk', 'inner'), across)  5.11 us
  transfers between devices with their start and end apart: 18, of which 6 were waited for; matrix products, arithmetic and copies ran while one was open for 8% of the time, Pallas kernels for 29%

profile of v2, /device:TPU:0, one launch (start us, length us, event | category | flops | bytes accessed | tf_op | source)
XLA Modules:
  0.0 144.8 jit_solution(6935720994291346118)
XLA Ops:
  0.6 1.3 reshape.29
  2.0 0.3 copy.11
  2.3 3.0 %collective-permute-start = (f32[32,16,128]{2,1,0:T(8,128)S(1)}, f32[32,16,128]{2,1,0:T(8,128)S(1)}, u32[]{:S(2)}, u32[]{:S(2)}) collective-permute-start(f32[32,16,128]{2,1,0:T(8,128)S(1)} %bitcast.7), channel_id=1, source_target_pairs={{8,0},{16,8},{24,16},{28,24},{20,28},{12,20},{4,12},{0,4},{9,1},{1... | collective-permute-start | bytes 786440 | tf_op jit(solution)/shard_map/ppermute | solution.py:255
  5.4 0.1 collective-permute-start.3
  5.5 1.0 broadcast_multiply_fusion
  6.5 1.3 mul.14
  7.8 1.5 %copy.10 = f32[16,32,128]{2,1,0:T(8,128)S(1)} copy(f32[16,32,128]{1,2,0:T(8,128)} %bitcast.13) | data formatting | bytes 524288 | tf_op jit(solution)/shard_map/mul | solution.py:297
  9.3 0.0 copy-start.10
  9.3 1.2 copy-done.10
  10.5 6.0 %shard_map.77 = (bf16[8,1024,256]{2,1,0:T(8,128)(2,1)S(1)}, bf16[8,1024,256]{2,1,0:T(8,128)(2,1)}) custom-call(f32[1024,128]{1,0:T(8,128)S(1)} %copy-done.2, f32[16,8,16,128]{3,2,1,0:T(8,128)S(1)} %copy-done.10), custom_call_target="tpu_custom_call" | custom-call | flops 1610612736 | bytes 8388608 | tf_op jit(solution)/shard_map/pallas_call | solution.py:301
  16.6 2.0 %copy-done = bf16[8,1024,256]{2,1,0:T(8,128)(2,1)} copy-done((bf16[8,1024,256]{2,1,0:T(8,128)(2,1)}, bf16[8,1024,256]{2,1,0:T(8,128)(2,1)S(1)}, u32[]{:S(2)}) %copy-start) | copy-done | bytes 4194328
  18.6 0.0 collective-permute-done.refs_1_
  18.6 1.9 %collective-permute-start.1 = (f32[32,16,128]{2,1,0:T(8,128)S(1)}, f32[32,16,128]{2,1,0:T(8,128)S(1)}, u32[]{:S(2)}, u32[]{:S(2)}) collective-permute-start(f32[32,16,128]{2,1,0:T(8,128)S(1)} %collective-permute-done.refs_1_), channel_id=1, source_target_pairs={{8,0},{16,8},{24,16},{28,24},{20,28},{12,20},{4,12},{0,4},{9,1},{1... | collective-permute-start | bytes 786440 | tf_op jit(solution)/shard_map/ppermute | solution.py:255
  20.5 0.0 collective-permute-done.3.refs_7_
  20.5 0.1 collective-permute-start.4
  20.6 9.8 %shard_map.79 = (f32[32,16,128]{2,1,0:T(8,128)S(1)}, f32[32,16,128]{2,1,0:T(8,128)S(1)}, f32[32,16,128]{2,1,0:T(8,128)S(1)}, f32[32,16,128]{2,1,0:T(8,128)S(1)},...) custom-call(bf16[8,1024,256]{2,1,0:T(8,128)(2,1)} %copy-done, ...), custom_call_target="tpu_custom_call" | custom-call | flops 1610612736 | bytes 8388608 | tf_op jit(solution)/shard_map/pallas_call | solution.py:307
  30.4 0.7 copy-done.3
  31.1 0.7 copy-done.6
  31.9 0.7 copy-done.7
  32.6 0.7 copy-done.8
  33.3 2.0 %collective-permute-start.10 = (f32[32,16,128]{2,1,0:T(8,128)}, f32[32,16,128]{2,1,0:T(8,128)}, u32[]{:S(2)}, u32[]{:S(2)}) collective-permute-start(f32[32,16,128]{2,1,0:T(8,128)} %get-tuple-element.33), channel_id=1, source_target_pairs={{0,8},{8,16},{16,24},{24,28},{28,20},{20,12},{12,4},{4,0},{9,1},{1... | collective-permute-start | bytes 786440 | tf_op jit(solution)/shard_map/ppermute | solution.py:266
  35.2 0.0 collective-permute-done.1.refs_2_
  35.2 0.1 collective-permute-start.2
  35.3 0.0 collective-permute-done.4.refs_6_
  35.3 2.0 %collective-permute-start.5 = (f32[32,16,128]{2,1,0:T(8,128)S(1)}, f32[32,16,128]{2,1,0:T(8,128)S(1)}, u32[]{:S(2)}, u32[]{:S(2)}) collective-permute-start(f32[32,16,128]{2,1,0:T(8,128)S(1)} %collective-permute-done.4.refs_6_), channel_id=1, source_target_pairs={{0,8},{8,16},{16,24},{24,28},{28,20},{20,12},{12,4},{4,0},{1,9},{9... | collective-permute-start | bytes 786440 | tf_op jit(solution)/shard_map/ppermute | solution.py:254
  37.3 5.1 %collective-permute-done.10 = f32[32,16,128]{2,1,0:T(8,128)} collective-permute-done((f32[32,16,128]{2,1,0:T(8,128)}, f32[32,16,128]{2,1,0:T(8,128)}, u32[]{:S(2)}, u32[]{:S(2)}) %collective-permute-start.10) | collective-permute-done | bytes 262176 | tf_op jit(solution)/shard_map/ppermute | solution.py:266
  42.4 1.2 select_add_fusion.1
  43.5 1.4 collective-permute-start.11
  44.9 0.9 collective-permute-start.14
  45.8 2.1 %collective-permute-done.5.refs_5_ = f32[32,16,128]{2,1,0:T(8,128)S(1)} collective-permute-done((f32[32,16,128]{2,1,0:T(8,128)S(1)}, f32[32,16,128]{2,1,0:T(8,128)S(1)}, u32[]{:S(2)}, u32[]{:S(2)}) %collective-permute-start.5) | collective-permute-done | bytes 262176 | tf_op jit(solution)/shard_map/ppermute | solution.py:254
  47.9 1.3 collective-permute-start.6
  49.2 1.9 %collective-permute-done.11 = f32[32,16,128]{2,1,0:T(8,128)S(1)} collective-permute-done((f32[32,16,128]{2,1,0:T(8,128)S(1)}, f32[32,16,128]{2,1,0:T(8,128)S(1)}, u32[]{:S(2)}, u32[]{:S(2)}) %collective-permute-start.11) | collective-permute-done | bytes 262176 | tf_op jit(solution)/shard_map/ppermute | solution.py:270
  51.1 1.7 %add.37 = f32[32,16,128]{2,1,0:T(8,128)} add(f32[32,16,128]{2,1,0:T(8,128)} %copy-done.3, f32[32,16,128]{2,1,0:T(8,128)S(1)} %collective-permute-done.11) | non-fusion elementwise | flops 65536 | bytes 786432 | tf_op jit(solution)/shard_map/add | solution.py:273
  52.8 0.9 collective-permute-start.12
  53.7 0.0 collective-permute-done.14
  53.7 0.7 add.41
  54.4 1.1 collective-permute-start.15
  55.6 0.1 collective-permute-done.6.refs_4_
  55.6 1.2 copy-done.11
  56.9 12.3 %shard_map.75 = (f32[1024,128]{1,0:T(8,128)}, bf16[8,1024,256]{2,1,0:T(8,128)(2,1)}, bf16[8,1024,256]{2,1,0:T(8,128)(2,1)}) custom-call(f32[512,128]{1,0:T(8,128)S(1)} %bitcast.12, f32[16,8,16,128]{3,2,1,0:T(8,128)S(1)} %copy-done.11, f32[32,16,128]{2,1,0:T(8,128)S(1)} %bitcast.9, f32[32,16,128]{2,1,0:T(8,128)S(1)} %collective-permute-done.refs_1_, ...), custom_call_target="tpu_custom_call" | custom-call | flops 3221225472 | bytes 8388608 | tf_op jit(solution)/shard_map/pallas_call | solution.py:317
  69.2 4.9 %all-to-all-start = ((f32[32,32,128]{2,1,0:T(8,128)}), f32[32,32,128]{2,1,0:T(8,128)}, u32[]{:S(2)}, u32[]{:S(2)}) async-start(f32[32,32,128]{2,1,0:T(8,128)} %bitcast.5), calls=%async_computation | async-start | bytes 1048576 | tf_op jit(solution)/shard_map/all_to_all | solution.py:324
  74.1 0.0 collective-permute-done.12
  74.1 1.0 add.38
  75.1 1.7 %collective-permute-start.13 = (f32[32,16,128]{2,1,0:T(8,128)S(1)}, f32[32,16,128]{2,1,0:T(8,128)S(1)}, u32[]{:S(2)}, u32[]{:S(2)}) collective-permute-start(f32[32,16,128]{2,1,0:T(8,128)S(1)} %add.38), channel_id=1, source_target_pairs={{0,8},{8,16},{16,24},{24,28},{28,20},{20,12},{12,4},{4,0},{1,9},{9... | collective-permute-start | bytes 786440 | tf_op jit(solution)/shard_map/ppermute | solution.py:270
  76.9 0.4 collective-permute-start.16
  77.2 1.1 copy-done.5
  78.4 7.2 %shard_map.78 = (f32[32,512]{1,0:T(8,128)S(1)}, f32[32,512]{1,0:T(8,128)S(1)}, f32[32,512]{1,0:T(8,128)S(1)}, f32[32,512]{1,0:T(8,128)S(1)}) custom-call(bf16[8,1024,256]{2,1,0:T(8,128)(2,1)} %copy-done, bf16[8,1024,256]{2,1,0:T(8,128)(2,1)} %get-tuple-element.24.low_ref, f32[32,16,128]{2,1,0:T(8,128)S(1)} %bitcast.10, ...), custom_call_target="tpu_custom_call" | custom-call | flops 1610612736 | bytes 8388608 | tf_op jit(solution)/shard_map/pallas_call | solution.py:331
  85.6 0.1 collective-permute-start.7
  85.7 1.9 %collective-permute-start.8 = (f32[32,512]{1,0:T(8,128)S(1)}, f32[32,512]{1,0:T(8,128)S(1)}, u32[]{:S(2)}, u32[]{:S(2)}) collective-permute-start(f32[32,512]{1,0:T(8,128)S(1)} %get-tuple-element.27), channel_id=1, source_target_pairs={{0,2},{1,3},{2,0},{3,1},{4,6},{5,7},{6,4},{7,5},{8,10},{9,11},{10,... | collective-permute-start | bytes 196616 | tf_op jit(solution)/shard_map/ppermute | solution.py:279
  87.6 0.1 collective-permute-start.9
  87.6 1.1 collective-permute-done.13
  88.7 2.1 %collective-permute-done.16 = f32[32,16,128]{2,1,0:T(8,128)S(1)} collective-permute-done((f32[32,16,128]{2,1,0:T(8,128)S(1)}, f32[32,16,128]{2,1,0:T(8,128)S(1)}, u32[]{:S(2)}, u32[]{:S(2)}) %collective-permute-start.16) | collective-permute-done | bytes 262176 | tf_op jit(solution)/shard_map/ppermute | solution.py:271
  90.8 0.1 add_bitcast_fusion
  90.9 7.1 %shard_map.76 = f32[16,8,16,128]{3,2,1,0:T(8,128)} custom-call(bf16[8,1024,256]{2,1,0:T(8,128)(2,1)S(1)} %copy-done.1, bf16[8,1024,256]{2,1,0:T(8,128)(2,1)} %get-tuple-element.22.low_ref, f32[1024,128]{1,0:T(8,128)S(1)} %copy-done.2), custom_call_target="tpu_custom_call" | custom-call | flops 1610612736 | bytes 8388608 | tf_op jit(solution)/shard_map/pallas_call | solution.py:346
  98.0 0.3 copy.13
  98.3 1.2 reshape.32
  99.5 0.0 collective-permute-done.7
  99.5 0.0 collective-permute-done.8
  99.6 0.1 reshape.30
  99.7 0.1 copy.12
  99.8 0.8 reshape.31
  100.6 1.1 reduce_sum.9
  101.7 41.9 %all_gather.3.in_ref = f32[1024,128]{1,0:T(8,128)S(1)} all-gather(f32[32,128]{1,0:T(8,128)S(1)} %reduce_sum.9), channel_id=1, replica_groups=mesh['groups'=1,'blk'=8,'inner'=4] {'blk','inner'}, dimensions={0}, use_global_device_ids=true | all-gather | bytes 540672 | tf_op jit(solution)/shard_map/all_gather | solution.py:326
  143.6 1.3 shard_map.80
  (22 shorter events, 0.1 us)
Async XLA Ops:
  0.6 8.7 %copy-start.2 = (f32[1024,128]{1,0:T(8,128)S(1)}, f32[1024,128]{1,0:T(8,128)}, u32[]{:S(2)}) copy-start(f32[1024,128]{1,0:T(8,128)} %weight_ref.3) | copy-start | bytes 1572868
  2.3 16.2 %collective-permute-start = (f32[32,16,128]{2,1,0:T(8,128)S(1)}, f32[32,16,128]{2,1,0:T(8,128)S(1)}, u32[]{:S(2)}, u32[]{:S(2)}) collective-permute-start(f32[32,16,128]{2,1,0:T(8,128)S(1)} %bitcast.7), channel_id=1, source_target_pairs={{8,0},{16,8},{24,16},{28,24},{20,28},{12,20},{4,12},{0,4},{9,1},{1... | collective-permute-start | bytes 786440 | tf_op jit(solution)/shard_map/ppermute | solution.py:255
  5.4 15.1 %collective-permute-start.3 = (f32[32,16,128]{2,1,0:T(8,128)S(1)}, f32[32,16,128]{2,1,0:T(8,128)S(1)}, u32[]{:S(2)}, u32[]{:S(2)}) collective-permute-start(f32[32,16,128]{2,1,0:T(8,128)S(1)} %bitcast.8), channel_id=1, source_target_pairs={{0,8},{8,16},{16,24},{24,28},{28,20},{20,12},{12,4},{4,0},{1,9},{9... | collective-permute-start | bytes 786440 | tf_op jit(solution)/shard_map/ppermute | solution.py:254
  9.3 1.2 copy-start.10
  16.5 2.0 %copy-start = (bf16[8,1024,256]{2,1,0:T(8,128)(2,1)}, bf16[8,1024,256]{2,1,0:T(8,128)(2,1)S(1)}, u32[]{:S(2)}) copy-start(bf16[8,1024,256]{2,1,0:T(8,128)(2,1)S(1)} %get-tuple-element.23.high_ref) | copy-start | bytes 12582916
  18.6 16.7 %collective-permute-start.1 = (f32[32,16,128]{2,1,0:T(8,128)S(1)}, f32[32,16,128]{2,1,0:T(8,128)S(1)}, u32[]{:S(2)}, u32[]{:S(2)}) collective-permute-start(f32[32,16,128]{2,1,0:T(8,128)S(1)} %collective-permute-done.refs_1_), channel_id=1, source_target_pairs={{8,0},{16,8},{24,16},{28,24},{20,28},{12,20},{4,12},{0,4},{9,1},{1... | collective-permute-start | bytes 786440 | tf_op jit(solution)/shard_map/ppermute | solution.py:255
  20.5 14.8 %collective-permute-start.4 = (f32[32,16,128]{2,1,0:T(8,128)S(1)}, f32[32,16,128]{2,1,0:T(8,128)S(1)}, u32[]{:S(2)}, u32[]{:S(2)}) collective-permute-start(f32[32,16,128]{2,1,0:T(8,128)S(1)} %collective-permute-done.3.refs_7_), channel_id=1, source_target_pairs={{0,8},{8,16},{16,24},{24,28},{28,20},{20,12},{12,4},{4,0},{1,9},{9... | collective-permute-start | bytes 786440 | tf_op jit(solution)/shard_map/ppermute | solution.py:254
  30.4 0.7 copy-start.3
  31.1 0.7 copy-start.6
  31.8 0.7 copy-start.7
  32.6 0.7 copy-start.8
  33.3 9.1 %collective-permute-start.10 = (f32[32,16,128]{2,1,0:T(8,128)}, f32[32,16,128]{2,1,0:T(8,128)}, u32[]{:S(2)}, u32[]{:S(2)}) collective-permute-start(f32[32,16,128]{2,1,0:T(8,128)} %get-tuple-element.33), channel_id=1, source_target_pairs={{0,8},{8,16},{16,24},{24,28},{28,20},{20,12},{12,4},{4,0},{9,1},{1... | collective-permute-start | bytes 786440 | tf_op jit(solution)/shard_map/ppermute | solution.py:266
  35.2 10.6 %collective-permute-start.2 = (f32[32,16,128]{2,1,0:T(8,128)S(1)}, f32[32,16,128]{2,1,0:T(8,128)S(1)}, u32[]{:S(2)}, u32[]{:S(2)}) collective-permute-start(f32[32,16,128]{2,1,0:T(8,128)S(1)} %collective-permute-done.1.refs_2_), channel_id=1, source_target_pairs={{8,0},{16,8},{24,16},{28,24},{20,28},{12,20},{4,12},{0,4},{9,1},{1... | collective-permute-start | bytes 786440 | tf_op jit(solution)/shard_map/ppermute | solution.py:255
  35.3 12.6 %collective-permute-start.5 = (f32[32,16,128]{2,1,0:T(8,128)S(1)}, f32[32,16,128]{2,1,0:T(8,128)S(1)}, u32[]{:S(2)}, u32[]{:S(2)}) collective-permute-start(f32[32,16,128]{2,1,0:T(8,128)S(1)} %collective-permute-done.4.refs_6_), channel_id=1, source_target_pairs={{0,8},{8,16},{16,24},{24,28},{28,20},{20,12},{12,4},{4,0},{1,9},{9... | collective-permute-start | bytes 786440 | tf_op jit(solution)/shard_map/ppermute | solution.py:254
  43.5 7.5 %collective-permute-start.11 = (f32[32,16,128]{2,1,0:T(8,128)S(1)}, f32[32,16,128]{2,1,0:T(8,128)S(1)}, u32[]{:S(2)}, u32[]{:S(2)}) collective-permute-start(f32[32,16,128]{2,1,0:T(8,128)S(1)} %get-tuple-element.38), channel_id=1, source_target_pairs={{0,8},{8,16},{16,24},{24,28},{28,20},{20,12},{12,4},{4,0},{1,9},{9... | collective-permute-start | bytes 786440 | tf_op jit(solution)/shard_map/ppermute | solution.py:270
  44.9 8.8 %collective-permute-start.14 = (f32[32,16,128]{2,1,0:T(8,128)S(1)}, f32[32,16,128]{2,1,0:T(8,128)S(1)}, u32[]{:S(2)}, u32[]{:S(2)}) collective-permute-start(f32[32,16,128]{2,1,0:T(8,128)S(1)} %get-tuple-element.39), channel_id=1, source_target_pairs={{8,0},{16,8},{24,16},{28,24},{20,28},{12,20},{4,12},{0,4},{9,1},{1... | collective-permute-start | bytes 786440 | tf_op jit(solution)/shard_map/ppermute | solution.py:271
  47.9 7.7 %collective-permute-start.6 = (f32[32,16,128]{2,1,0:T(8,128)S(1)}, f32[32,16,128]{2,1,0:T(8,128)S(1)}, u32[]{:S(2)}, u32[]{:S(2)}) collective-permute-start(f32[32,16,128]{2,1,0:T(8,128)S(1)} %broadcast_select_fusion), channel_id=1, source_target_pairs={{0,8},{8,16},{16,24},{24,28},{28,20},{20,12},{12,4},{4,0},{9,1},{1... | collective-permute-start | bytes 786440 | tf_op jit(solution)/shard_map/ppermute | solution.py:258
  52.8 21.3 %collective-permute-start.12 = (f32[32,16,128]{2,1,0:T(8,128)}, f32[32,16,128]{2,1,0:T(8,128)}, u32[]{:S(2)}, u32[]{:S(2)}) collective-permute-start(f32[32,16,128]{2,1,0:T(8,128)} %add.37), channel_id=1, source_target_pairs={{0,8},{8,16},{16,24},{24,28},{28,20},{20,12},{12,4},{4,0},{1,9},{9... | collective-permute-start | bytes 786440 | tf_op jit(solution)/shard_map/ppermute | solution.py:270
  54.4 22.4 %collective-permute-start.15 = (f32[32,16,128]{2,1,0:T(8,128)}, f32[32,16,128]{2,1,0:T(8,128)S(1)}, u32[]{:S(2)}, u32[]{:S(2)}) collective-permute-start(f32[32,16,128]{2,1,0:T(8,128)} %add.41), channel_id=1, source_target_pairs={{8,0},{16,8},{24,16},{28,24},{20,28},{12,20},{4,12},{0,4},{9,1},{1... | collective-permute-start | bytes 786440 | tf_op jit(solution)/shard_map/ppermute | solution.py:271
  55.6 1.2 copy-start.11
  56.9 12.3 %copy-start.4 = (f32[32,16,128]{2,1,0:T(8,128)}, f32[32,16,128]{2,1,0:T(8,128)S(1)}, u32[]{:S(2)}) copy-start(f32[32,16,128]{2,1,0:T(8,128)S(1)} %collective-permute-done.6.refs_4_) | copy-start | bytes 786436
  69.2 31.4 %all-to-all-start = ((f32[32,32,128]{2,1,0:T(8,128)}), f32[32,32,128]{2,1,0:T(8,128)}, u32[]{:S(2)}, u32[]{:S(2)}) async-start(f32[32,32,128]{2,1,0:T(8,128)} %bitcast.5), calls=%async_computation | async-start | bytes 1048576 | tf_op jit(solution)/shard_map/all_to_all | solution.py:324
  75.1 13.7 %collective-permute-start.13 = (f32[32,16,128]{2,1,0:T(8,128)S(1)}, f32[32,16,128]{2,1,0:T(8,128)S(1)}, u32[]{:S(2)}, u32[]{:S(2)}) collective-permute-start(f32[32,16,128]{2,1,0:T(8,128)S(1)} %add.38), channel_id=1, source_target_pairs={{0,8},{8,16},{16,24},{24,28},{28,20},{20,12},{12,4},{4,0},{1,9},{9... | collective-permute-start | bytes 786440 | tf_op jit(solution)/shard_map/ppermute | solution.py:270
  76.8 14.1 %copy-start.1 = (bf16[8,1024,256]{2,1,0:T(8,128)(2,1)S(1)}, bf16[8,1024,256]{2,1,0:T(8,128)(2,1)}, u32[]{:S(2)}) copy-start(bf16[8,1024,256]{2,1,0:T(8,128)(2,1)} %get-tuple-element.21.high_ref) | copy-start | bytes 12582916
  76.9 14.0 %collective-permute-start.16 = (f32[32,16,128]{2,1,0:T(8,128)S(1)}, f32[32,16,128]{2,1,0:T(8,128)S(1)}, u32[]{:S(2)}, u32[]{:S(2)}) collective-permute-start(f32[32,16,128]{2,1,0:T(8,128)S(1)} %add.42), channel_id=1, source_target_pairs={{8,0},{16,8},{24,16},{28,24},{20,28},{12,20},{4,12},{0,4},{9,1},{1... | collective-permute-start | bytes 786440 | tf_op jit(solution)/shard_map/ppermute | solution.py:271
  77.2 1.1 copy-start.5
  78.4 12.5 %copy-start.9 = (f32[32,16,128]{2,1,0:T(8,128)S(1)}, f32[32,16,128]{2,1,0:T(8,128)}, u32[]{:S(2)}) copy-start(f32[32,16,128]{2,1,0:T(8,128)} %copy-done.8) | copy-start | bytes 786436
  85.6 13.9 %collective-permute-start.7 = (f32[32,512]{1,0:T(8,128)S(1)}, f32[32,512]{1,0:T(8,128)S(1)}, u32[]{:S(2)}, u32[]{:S(2)}) collective-permute-start(f32[32,512]{1,0:T(8,128)S(1)} %get-tuple-element.26), channel_id=1, source_target_pairs={{0,1},{1,0},{2,3},{3,2},{4,5},{5,4},{6,7},{7,6},{8,9},{9,8},{10,11... | collective-permute-start | bytes 196616 | tf_op jit(solution)/shard_map/ppermute | solution.py:279
  85.7 13.9 %collective-permute-start.8 = (f32[32,512]{1,0:T(8,128)S(1)}, f32[32,512]{1,0:T(8,128)S(1)}, u32[]{:S(2)}, u32[]{:S(2)}) collective-permute-start(f32[32,512]{1,0:T(8,128)S(1)} %get-tuple-element.27), channel_id=1, source_target_pairs={{0,2},{1,3},{2,0},{3,1},{4,6},{5,7},{6,4},{7,5},{8,10},{9,11},{10,... | collective-permute-start | bytes 196616 | tf_op jit(solution)/shard_map/ppermute | solution.py:279
  87.6 12.0 %collective-permute-start.9 = (f32[32,512]{1,0:T(8,128)S(1)}, f32[32,512]{1,0:T(8,128)S(1)}, u32[]{:S(2)}, u32[]{:S(2)}) collective-permute-start(f32[32,512]{1,0:T(8,128)S(1)} %get-tuple-element.28), channel_id=1, source_target_pairs={{0,3},{1,2},{2,1},{3,0},{4,7},{5,6},{6,5},{7,4},{8,11},{9,10},{10,... | collective-permute-start | bytes 196616 | tf_op jit(solution)/shard_map/ppermute | solution.py:279

commit v3 on v0

v3 whole, which is shorter than its diff:
```python
import functools

import jax
import jax.numpy as jnp
from jax import lax
from jax.experimental import pallas as pl
from jax.experimental.pallas import tpu as pltpu
from jax.sharding import PartitionSpec as P

ENTRY_CHANNELS = 32
LANES = 128
F32 = jnp.float32
BF16 = jnp.bfloat16
MIB = 1024 * 1024


def halves(values):
    high = values.astype(BF16)
    low = (values - high.astype(F32)).astype(BF16)
    return high, low


def dot(left, right):
    return jnp.dot(left, right, preferred_element_type=F32)


def dot_rows(left, right):
    return lax.dot_general(left, right, (((1,), (1,)), ((), ())), preferred_element_type=F32)


def fold_of(columns):
    return max(1, LANES // columns)


def strided_rows(ref, first):
    return ref[pl.ds(first, ENTRY_CHANNELS, stride=ENTRY_CHANNELS), :]


def folded_weight(weight_ref, step, fold):
    return jnp.concatenate(
        [strided_rows(weight_ref, step * fold + part) for part in range(fold)], 1
    )


def gradient_kernel(
    by_parity, weight_ref, cotangent_ref, high_ref, low_ref, spread_high, spread_low, weight_cat
):
    channels = ENTRY_CHANNELS
    depth, pairs = cotangent_ref.shape[2:]
    block_count = cotangent_ref.shape[1]
    blocks = list(range(block_count))
    if by_parity:
        parity = lax.rem(lax.axis_index("blk"), 2)
        blocks = [2 * block + parity for block in range(block_count // 2)]
    fold = fold_of(len(blocks) * depth)
    columns = len(blocks) * depth
    for step in range(channels // fold):
        high, low = halves(folded_weight(weight_ref, step, fold))
        weight_cat[step * channels : (step + 1) * channels, :] = jnp.concatenate(
            [high, low, high], 1
        )
    empty = jnp.zeros((columns, pairs), BF16)

    def step_of(pair, carry):
        spread = ([], [])
        for part in range(2):
            rows = jnp.concatenate([cotangent_ref[2 * pair + part, block] for block in blocks], 0)
            for found, values in zip(spread, halves(rows)):
                for place in range(fold):
                    found.append(
                        jnp.concatenate(
                            [values if place == other else empty for other in range(fold)], 1
                        )
                    )
        high, low = (jnp.concatenate(found, 0) for found in spread)
        spread_high[pair] = high
        spread_low[pair] = low
        found = dot_rows(weight_cat[...], jnp.concatenate([high, high, low], 1))
        high, low = halves(found)
        high_ref[pair] = high
        low_ref[pair] = low
        return carry

    lax.fori_loop(0, high_ref.shape[0], step_of, 0)


def rows_of_step(refs, step, lanes):
    start = pl.multiple_of(step * ENTRY_CHANNELS, ENTRY_CHANNELS)
    return jnp.concatenate(
        [
            ref[pair, pl.ds(start, ENTRY_CHANNELS), part * lanes : (part + 1) * lanes]
            for ref in refs
            for pair in range(ref.shape[0])
            for part in range(2)
        ],
        0,
    )


def right_rows(right_ref, step, fold):
    return jnp.concatenate(
        [
            right_ref[block, step * fold + part]
            for part in range(fold)
            for block in range(right_ref.shape[0])
        ],
        0,
    )


def both_left(left_refs):
    sequences = left_refs[0].shape[1]
    return jnp.concatenate([ref[...] for ref in left_refs], 0) * (1.0 / sequences)


def right_kernel(own_high, own_low, peer_high, peer_low, own_left, peer_left, out_ref, left_flip):
    sequences = own_left.shape[1]
    blocks, channels, depth = out_ref.shape[:3]
    lanes = own_high.shape[2] // 2
    fold = lanes // (blocks * depth)
    flip_high, flip_low = halves(both_left([own_left, peer_left]).T)
    left_flip[:sequences, :] = flip_high
    left_flip[sequences:, :] = flip_low

    def step_of(step, carry):
        def stacked(refs):
            return jnp.concatenate(
                [rows_of_step(refs, 2 * step + part, lanes) for part in range(2)], 1
            )

        first = dot(left_flip[...], stacked([own_high, peer_high]))
        second = dot(left_flip[:sequences, :], stacked([own_low, peer_low]))
        found = first[:sequences] + first[sequences:] + second
        for part in range(2):
            turned = found[:, part * lanes : (part + 1) * lanes].T
            for place in range(fold):
                for block in range(blocks):
                    start = (place * blocks + block) * depth
                    y = (2 * step + part) * fold + place
                    out_ref[block, y] = turned[start : start + depth]
        return carry

    lax.fori_loop(0, channels // (2 * fold), step_of, 0)


def weight_kernel(
    own_left,
    peer_left,
    right_ref,
    own_spread_high,
    own_spread_low,
    peer_spread_high,
    peer_spread_low,
    keep_ref,
    send_ref,
    own_high,
    own_low,
    peer_high,
    peer_low,
    total,
):
    channels = ENTRY_CHANNELS
    blocks, _, depth, _ = right_ref.shape
    fold = fold_of(blocks * depth)
    lanes = fold * blocks * depth
    pairs = total.shape[1] // fold
    high, low = halves(both_left([own_left, peer_left]))
    left_cat = jnp.concatenate([high, low, high], 1)

    def outer_step(step, carry):
        right = [right_rows(right_ref, 2 * step + part, fold) for part in range(2)]
        high, low = halves(jnp.concatenate(right, 0))
        found = dot_rows(left_cat, jnp.concatenate([high, high, low], 1))
        high, low = halves(found)
        for part in range(2):
            start = pl.multiple_of((2 * step + part) * channels, channels)
            row = 0
            for high_ref, low_ref in ((own_high, own_low), (peer_high, peer_low)):
                for index in range(2 * high_ref.shape[0]):
                    place = (
                        index // 2,
                        pl.ds(start, channels),
                        slice((index % 2) * lanes, (index % 2 + 1) * lanes),
                    )
                    source = (
                        slice(row, row + channels),
                        slice(part * lanes, (part + 1) * lanes),
                    )
                    high_ref[place] = high[source]
                    low_ref[place] = low[source]
                    row += channels
        return carry

    lax.fori_loop(0, channels // (2 * fold), outer_step, 0)
    total[...] = jnp.zeros_like(total)

    def weight_step(pair, carry):
        found = None
        for high_ref, low_ref, spread_high, spread_low in (
            (own_high, own_low, own_spread_high, own_spread_low),
            (peer_high, peer_low, peer_spread_high, peer_spread_low),
        ):
            left = jnp.concatenate([high_ref[pair], low_ref[pair], high_ref[pair]], 1)
            high = spread_high[pair]
            term = dot(left, jnp.concatenate([high, high, spread_low[pair]], 0))
            found = term if found is None else found + term
        total[...] += found
        return carry

    lax.fori_loop(0, own_high.shape[0], weight_step, 0)
    core = lax.rem(lax.axis_index("inner"), 2)
    steps = channels // (2 * fold)
    for out_ref, half in ((keep_ref, core), (send_ref, 1 - core)):
        for step in range(steps):
            start = pl.multiple_of((half * steps + step) * channels, channels)
            found = total[pl.ds(start, channels), :]
            for part in range(fold):
                y = step * fold + part
                out_ref[y * channels : (y + 1) * channels, :] = found[
                    :, part * pairs : (part + 1) * pairs
                ]


def left_kernel(own_high, own_low, peer_high, peer_low, right_ref, out_ref, total, flipped):
    lanes = own_high.shape[2] // 2
    blocks, channels, depth, sequences = right_ref.shape
    fold = lanes // (blocks * depth)
    group = 4
    total[...] = jnp.zeros_like(total)

    def step_of(step, carry):
        steps = [group * step + part for part in range(group)]
        high, low = halves(jnp.concatenate([right_rows(right_ref, s, fold) for s in steps], 0))
        grads_high = jnp.concatenate(
            [rows_of_step([own_high, peer_high], s, lanes) for s in steps], 1
        )
        grads_low = jnp.concatenate(
            [rows_of_step([own_low, peer_low], s, lanes) for s in steps], 1
        )
        both = dot(grads_high, jnp.concatenate([high, low], 1))
        total[...] += both[:, :sequences] + both[:, sequences:] + dot(grads_low, high)
        return carry

    lax.fori_loop(0, channels // (fold * group), step_of, 0)
    flipped[...] = total[...].T * (1.0 / sequences)
    parity = lax.rem(lax.axis_index("blk"), 2)
    inner, size, width = out_ref.shape[1:]
    for side, start in ((parity, 0), (1 - parity, width)):
        for part in range(inner):
            out_ref[side, part] = flipped[part * size : (part + 1) * size, start : start + width]


def pair_kernel(final, high_ref, low_ref, weight_ref, *refs):
    if final:
        other_ref, out_ref, weight_flip, weight_rows = refs
    else:
        out_ref, weight_flip, weight_rows = refs
    channels = ENTRY_CHANNELS
    depth, pairs = out_ref.shape[2:]
    blocks = out_ref.shape[1] // 2 if final else out_ref.shape[1]
    lanes = high_ref.shape[2] // 2
    columns = blocks * depth
    fold = lanes // columns
    parity = lax.rem(lax.axis_index("blk"), 2)
    for step in range(channels // fold):
        weight_rows[step * channels : (step + 1) * channels, :] = folded_weight(
            weight_ref, step, fold
        )
    flip_high, flip_low = halves(weight_rows[...].T)
    wide = fold * pairs
    weight_flip[:wide, :] = flip_high
    weight_flip[wide:, :] = flip_low

    def step_of(pair, carry):
        first = dot(weight_flip[...], high_ref[pair])
        found = first[:wide] + first[wide:] + dot(weight_flip[:wide, :], low_ref[pair])
        for part in range(2):
            turned = None
            for place in range(fold):
                start = part * lanes
                piece = found[place * pairs : (place + 1) * pairs, start : start + lanes].T
                piece = piece[place * columns : (place + 1) * columns]
                turned = piece if turned is None else turned + piece
            row = 2 * pair + part
            for block in range(blocks):
                where = 2 * block + parity if final else block
                out_ref[row, where] = turned[block * depth : (block + 1) * depth]
                if final:
                    out_ref[row, 2 * block + 1 - parity] = other_ref[row, block]
        return carry

    lax.fori_loop(0, high_ref.shape[0], step_of, 0)


def place_kernel(mine_ref, other_ref, out_ref):
    channels = ENTRY_CHANNELS
    core = lax.rem(lax.axis_index("inner"), 2)
    steps = mine_ref.shape[0] // channels
    for ref, half in ((mine_ref, core), (other_ref, 1 - core)):
        for step in range(steps):
            rows = ref[step * channels : (step + 1) * channels, :]
            out_ref[pl.ds(half * steps + step, channels, stride=channels), :] = rows


def local(alignment_left, alignment_right, projection_matrix, cotangent):
    rows, features = alignment_left.shape
    depth = alignment_right.shape[0]
    count = lax.axis_size("blk")
    inner = lax.axis_size("inner")
    channels = ENTRY_CHANNELS
    sequences = features // channels
    outer, pairs = projection_matrix.shape
    blocks = count // 2
    columns = blocks * depth
    fold = fold_of(columns)
    lanes = fold * columns
    flops = 2 * rows * 2 * columns * outer * pairs * 3
    limit = (8 + 14 * columns * 2 // LANES) * MIB
    everyone = ("blk", "inner")
    parity = lax.rem(lax.axis_index("blk"), 2)

    def call(kernel, out_shape, scratch, cost):
        return pl.pallas_call(
            kernel,
            out_shape=out_shape,
            scratch_shapes=scratch,
            compiler_params=pltpu.CompilerParams(vmem_limit_bytes=limit),
            cost_estimate=pl.CostEstimate(
                flops=int(cost), bytes_accessed=4 * MIB, transcendentals=0
            ),
        )

    def shape(*sizes, kind=F32):
        return jax.ShapeDtypeStruct(sizes, kind)

    partner = [(here, here ^ 1) for here in range(count)]
    same_parity = [[2 * step + side for step in range(blocks)] for side in range(2)]
    row_groups = [
        [(2 * step + side) * inner + part for side in range(2) for part in range(inner)]
        for step in range(blocks)
    ]
    core_groups = [list(range(core, count * inner, 2)) for core in range(2)]
    cores = [(here, here ^ 1) for here in range(inner)]

    right = alignment_right.reshape(depth, sequences, channels).transpose(2, 0, 1)
    right = jnp.broadcast_to(right[None], (blocks,) + right.shape)
    right = lax.all_to_all(right, "blk", 0, 0, axis_index_groups=same_parity)

    left = alignment_left.reshape(rows, sequences, channels).transpose(0, 2, 1)
    left = left.reshape(rows * channels, sequences)
    left_peer = lax.ppermute(left, "blk", partner)
    by_side = cotangent.reshape(rows, blocks, 2, depth, pairs)
    cotangent_peer = lax.ppermute(
        jnp.where(parity == 0, by_side[:, :, 1], by_side[:, :, 0]), "blk", partner
    )

    tall = shape(rows // 2, outer // fold, 2 * lanes, kind=BF16)
    spread = shape(rows // 2, 2 * lanes, fold * pairs, kind=BF16)
    weight_scratch = [pltpu.VMEM((outer // fold, 3 * fold * pairs), BF16)]
    own = call(
        functools.partial(gradient_kernel, True), [tall] * 2 + [spread] * 2, weight_scratch, flops / 2
    )(projection_matrix, cotangent)
    peer = call(
        functools.partial(gradient_kernel, False),
        [tall] * 2 + [spread] * 2,
        weight_scratch,
        flops / 2,
    )(projection_matrix, cotangent_peer)

    right_parts = call(
        right_kernel,
        shape(blocks, channels, depth, sequences),
        [pltpu.VMEM((2 * sequences, 2 * rows * channels), BF16)],
        flops,
    )(*own[:2], *peer[:2], left, left_peer)
    right_parts = lax.all_to_all(right_parts, "blk", 0, 0, axis_index_groups=same_parity)
    grad_right = jnp.sum(right_parts, 0).transpose(1, 2, 0).reshape(depth, features)

    half = shape(outer // 2, pairs)
    keep, send, *outers = call(
        weight_kernel,
        [half] * 2 + [tall] * 4,
        [pltpu.VMEM((outer // fold, fold * pairs), F32)],
        2 * flops,
    )(left, left_peer, right, *own[2:], *peer[2:])
    keep = keep + lax.ppermute(send, "inner", cores)
    members = count * inner // 2
    pieces = keep.reshape(members, outer // 2 // members, pairs)
    pieces = lax.all_to_all(pieces, everyone, 0, 0, axis_index_groups=core_groups)
    piece = jnp.sum(pieces, 0)
    pieces = jnp.broadcast_to(piece[None], (members,) + piece.shape)
    pieces = lax.all_to_all(pieces, everyone, 0, 0, axis_index_groups=core_groups)
    mine = pieces.reshape(outer // 2, pairs)
    other = lax.ppermute(mine, "inner", cores)
    grad_weight = call(place_kernel, shape(outer, pairs), [], 0)(mine, other)

    pair_scratch = [
        pltpu.VMEM((2 * fold * pairs, outer // fold), BF16),
        pltpu.VMEM((outer // fold, fold * pairs), F32),
    ]
    pair_peer = call(
        functools.partial(pair_kernel, False),
        shape(rows, blocks, depth, pairs),
        pair_scratch,
        flops / 2,
    )(*outers[2:], projection_matrix)
    pair_peer = lax.ppermute(pair_peer, "blk", partner)

    left_parts = call(
        left_kernel,
        shape(2, inner, sequences // inner, rows * channels),
        [
            pltpu.VMEM((2 * rows * channels, sequences), F32),
            pltpu.VMEM((sequences, 2 * rows * channels), F32),
        ],
        flops,
    )(*own[:2], *peer[:2], right)
    left_parts = left_parts.reshape(2 * inner, sequences // inner, rows * channels)
    left_parts = lax.all_to_all(left_parts, everyone, 0, 0, axis_index_groups=row_groups)
    grad_left = jnp.sum(left_parts, 0).reshape(sequences // inner, rows, channels)
    grad_left = grad_left.transpose(1, 0, 2).reshape(rows, features // inner)

    pair_update = call(
        functools.partial(pair_kernel, True), shape(*cotangent.shape), pair_scratch, flops / 2
    )(*outers[:2], projection_matrix, pair_peer)
    return (pair_update, grad_left, grad_right, grad_weight)


def solution(mesh):
    placed = (
        P(("groups", "blk"), None),
        P(("groups", "blk", "inner"), None),
        P(),
        P(("groups", "blk"), None, "inner", None),
    )
    return jax.shard_map(
        local,
        mesh=mesh,
        in_specs=placed,
        out_specs=(
            P(("groups", "blk"), None, "inner", None),
            P(("groups", "blk"), "inner"),
            P(("groups", "blk", "inner"), None),
            P("groups", None),
        ),
        check_vma=False,
    )
```

time: 699 us -> 150 us (0.21)
  matrix products: 287 us -> 0 us
  waiting for transfers between devices: 272 us -> 28.3 us
  local copies, waits for them, and re-layouts: 124 us -> 48.9 us
  Pallas kernels: 0 us -> 36.9 us
  starting transfers between devices: 0.16 us -> 29.5 us
  between operations: 13.8 us -> 0.85 us
    dot_general x48 -> x0, matrix products: 287 us -> none  [the longest x8 120 us: tile_terms(): jnp.einsum('isx,jsy->ijxy', left_sequence, right_sequence, precision=high...]
    psum x1 -> x0, waiting for transfers between devices: 124 us -> none  [local(): grad_weight = lax.psum(state[1], ('blk', 'inner'))]
    reduce_scatter x2 -> x0, waiting for transfers between devices: 93.9 us -> none  [the longest x1 71.6 us: local(): lax.psum_scatter(state[3], 'blk', scatter_dimension=0, tiled=True)]
    reshape x34 -> x5, local copies, waits for them, and re-layouts: 60.8 us -> 6.02 us  [the longest x1 2.42 us: local(): jnp.sum(right_parts, 0).transpose(1, 2, 0).reshape(depth, features)]
    all_gather x1 -> x0, waiting for transfers between devices: 52.6 us -> none  [local(): collected_rows = lax.all_gather(alignment_right, 'blk', axis=0, tiled=True)]
    div x16 -> x0, local copies, waits for them, and re-layouts: 45.7 us -> none  [the longest x8 43 us: tile_terms(): jnp.einsum('isx,jsy->ijxy', left_sequence, right_sequence, precision=high...]
    pallas_call x0 -> x8, Pallas kernels: none -> 36.9 us  [the longest x1 8.96 us: local(): call(weight_kernel, [half] * 2 + [tall] * 4, [pltpu.VMEM((outer // fold,...]
    unnamed x6 -> x72, local copies, waits for them, and re-layouts: 2.19 us -> 37.4 us
  transfers between devices with their start and end apart: 4 -> 10, of which waited for: 4 -> 6; matrix products, arithmetic and copies ran while one was open for 0% -> 8% of each run, Pallas kernels for 0% -> 17%
where the time goes in v3:
time: 150 us; the launch traced here: 149 us
  local copies, waits for them, and re-layouts  48.9 us (33%)
  Pallas kernels  36.9 us (25%)
  starting transfers between devices  29.5 us (20%)
  waiting for transfers between devices  28.3 us (19%)
  other arithmetic  4.65 us (3%)
    unnamed x72, local copies, waits for them, and re-layouts  37.4 us
    all_to_all x1, waiting for transfers between devices, local(): lax.all_to_all(right_parts, 'blk', 0, 0, axis_index_groups=same_parity)  12.9 us
    all_to_all x2, starting transfers between devices, local(): lax.all_to_all(pieces, everyone, 0, 0, axis_index_groups=core_groups)  11.4 us
    pallas_call x1, Pallas kernels, local(): call(weight_kernel, [half] * 2 + [tall] * 4, [pltpu.VMEM((outer // fold,...  8.96 us
    all_to_all x1, waiting for transfers between devices, local(): lax.all_to_all(left_parts, everyone, 0, 0, axis_index_groups=row_groups)  8.7 us
    all_to_all x1, starting transfers between devices, local(): right = lax.all_to_all(right, 'blk', 0, 0, axis_index_groups=same_parity)  6.45 us
    pallas_call x1, Pallas kernels, local(): call(functools.partial(pair_kernel, True), shape(*cotangent.shape), pair_...  5.02 us
    pallas_call x1, Pallas kernels, local(): call(functools.partial(pair_kernel, False), shape(rows, blocks, depth, pa...  4.84 us
  transfers between devices with their start and end apart: 10, of which 6 were waited for; matrix products, arithmetic and copies ran while one was open for 8% of the time, Pallas kernels for 17%

profile of v3, /device:TPU:0, one launch (start us, length us, event | category | flops | bytes accessed | tf_op | source)
XLA Modules:
  0.0 149.1 jit_solution(15826543797413751131)
XLA Ops:
  0.6 1.3 reshape.44
  1.9 0.3 copy.20
  2.3 1.1 broadcast_in_dim.4
  3.3 6.4 %all-to-all-start = ((f32[4,32,16,128]{3,2,1,0:T(8,128)}), f32[4,32,16,128]{3,2,1,0:T(8,128)S(1)}, u32[]{:S(2)}, u32[]{:S(2)}) async-start(f32[4,32,16,128]{3,2,1,0:T(8,128)} %broadcast_in_dim.4), calls=%async_computation | async-start | bytes 2097152 | tf_op jit(solution)/shard_map/all_to_all | solution.py:347
  9.8 0.9 fusion.1
  10.7 1.5 %collective-permute-start.1 = (f32[16,4,16,128]{3,2,1,0:T(8,128)}, f32[16,4,16,128]{3,2,1,0:T(8,128)}, u32[]{:S(2)}, u32[]{:S(2)}) collective-permute-start(f32[16,4,16,128]{3,2,1,0:T(8,128)} %fusion.1), channel_id=1, source_target_pairs={{0,4},{4,0},{8,12},{12,8},{16,20},{20,16},{24,28},{28,24},{1,5},{5... | collective-permute-start | bytes 1572872 | tf_op jit(solution)/shard_map/ppermute | solution.py:353
  12.2 0.3 reshape.42
  12.8 0.6 collective-permute-start
  13.4 1.0 copy-done.13
  14.4 1.2 copy-done.21
  15.7 3.6 %shard_map.75 = (bf16[8,512,256]{2,1,0:T(8,128)(2,1)S(1)}, bf16[8,512,256]{2,1,0:T(8,128)(2,1)S(1)}, bf16[8,256,256]{2,1,0:T(8,128)(2,1)S(1)}, bf16[8,256,256]{2,1,0:T(8,128)(2,1)S(1)}) custom-call(f32[1024,128]{1,0:T(8,128)S(1)} %copy-done.13, f32[16,8,16,128]{3,2,1,0:T(8,128)S(1)} %copy-done.21), custom_call_target="tpu_custom_call" | custom-call | flops 805306368 | bytes 4194304 | tf_op jit(solution)/shard_map/pallas_call | solution.py:360
  19.3 1.3 copy-done
  20.6 1.0 copy-done.25
  21.6 1.1 copy-done.27
  22.6 3.2 %collective-permute-done.1.cotangent_ref = f32[16,4,16,128]{3,2,1,0:T(8,128)} collective-permute-done((f32[16,4,16,128]{3,2,1,0:T(8,128)}, f32[16,4,16,128]{3,2,1,0:T(8,128)}, u32[]{:S(2)}, u32[]{:S(2)}) %collective-permute-start.1) | collective-permute-done | bytes 524320 | tf_op jit(solution)/shard_map/ppermute | solution.py:353
  25.8 4.6 %shard_map.76 = (bf16[8,512,256]{2,1,0:T(8,128)(2,1)S(1)}, bf16[8,512,256]{2,1,0:T(8,128)(2,1)S(1)}, bf16[8,256,256]{2,1,0:T(8,128)(2,1)S(1)}, bf16[8,256,256]{2,1,0:T(8,128)(2,1)S(1)}) custom-call(f32[1024,128]{1,0:T(8,128)S(1)} %copy-done.13, f32[16,4,16,128]{3,2,1,0:T(8,128)} %collective-permute-done.1.cotangent_ref), custom_call_target="tpu_custom_call" | custom-call | flops 805306368 | bytes 4194304 | tf_op jit(solution)/shard_map/pallas_call | solution.py:363
  30.4 1.3 copy-done.3
  31.8 1.4 copy-done.6
  33.2 1.0 copy-done.29
  34.1 1.0 copy-done.31
  35.1 0.7 copy-done.22
  35.8 0.9 copy-done.23
  36.8 1.2 copy-done.26
  38.0 1.2 copy-done.28
  39.2 1.2 copy-done.30
  40.4 1.2 copy-done.32
  41.7 9.0 %shard_map.77 = (f32[512,128]{1,0:T(8,128)S(1)}, f32[512,128]{1,0:T(8,128)S(1)}, bf16[8,512,256]{2,1,0:T(8,128)(2,1)S(1)}, bf16[8,512,256]{2,1,0:T(8,128)(2,1)S(...) custom-call(f32[512,128]{1,0:T(8,128)S(1)} %bitcast.23, f32[512,128]{1,0:T(8,128)S(1)} %copy-done.23, ...), custom_call_target="tpu_custom_call" | custom-call | flops 3221225472 | bytes 4194304 | tf_op jit(solution)/shard_map/pallas_call | solution.py:380
  50.6 1.4 copy-done.9
  52.0 1.3 copy-done.11
  53.4 1.4 copy-done.16
  54.8 1.3 copy-done.18
  56.1 1.5 %collective-permute-done.3 = f32[512,128]{1,0:T(8,128)S(1)} collective-permute-done((f32[512,128]{1,0:T(8,128)S(1)}, f32[512,128]{1,0:T(8,128)S(1)}, u32[]{:S(2)}, u32[]{:S(2)}) %collective-permute-start.3) | collective-permute-done | bytes 262176 | tf_op jit(solution)/shard_map/ppermute | solution.py:386
  57.6 0.7 add.3
  58.3 7.2 %all-to-all-start.3 = ((f32[16,32,128]{2,1,0:T(8,128)}), f32[16,32,128]{2,1,0:T(8,128)}, u32[]{:S(2)}, u32[]{:S(2)}) async-start(f32[16,32,128]{2,1,0:T(8,128)} %bitcast.29), calls=%async_computation.3 | async-start | bytes 524288 | tf_op jit(solution)/shard_map/all_to_all | solution.py:389
  65.5 1.6 %copy-done.1 = bf16[8,512,256]{2,1,0:T(8,128)(2,1)S(1)} copy-done((bf16[8,512,256]{2,1,0:T(8,128)(2,1)S(1)}, bf16[8,512,256]{2,1,0:T(8,128)(2,1)}, u32[]{:S(2)}) %copy-start.1) | copy-done | bytes 2097176
  67.1 1.6 %copy-done.4 = bf16[8,512,256]{2,1,0:T(8,128)(2,1)S(1)} copy-done((bf16[8,512,256]{2,1,0:T(8,128)(2,1)S(1)}, bf16[8,512,256]{2,1,0:T(8,128)(2,1)}, u32[]{:S(2)}) %copy-start.4) | copy-done | bytes 2097176
  68.7 1.6 %copy-done.7 = bf16[8,512,256]{2,1,0:T(8,128)(2,1)S(1)} copy-done((bf16[8,512,256]{2,1,0:T(8,128)(2,1)S(1)}, bf16[8,512,256]{2,1,0:T(8,128)(2,1)}, u32[]{:S(2)}) %copy-start.7) | copy-done | bytes 2097176
  70.3 3.1 %shard_map.80 = f32[2,4,32,512]{3,2,1,0:T(8,128)S(1)} custom-call(bf16[8,512,256]{2,1,0:T(8,128)(2,1)S(1)} %get-tuple-element.26.own_high, bf16[8,512,256]{2,1,0:T(8,128)(2,1)S(1)} %copy-done.1, bf16[8,512,256]{2,1,0:T(8,128)(2,1)S(1)} %copy-done.4, bf16[8,512,256]{2,1,0:T(8,128)(2,1)S(1)} %copy-done.7, f32[4,32,16,128]{3,2,1,0:T(8,128)S(1)} %all-to-all-done.right_ref), custom_call_target="tpu_custom_call" | custom-call | flops 1610612736 | bytes 4194304 | tf_op jit(solution)/shard_map/pallas_call | solution.py:409
  73.4 0.8 copy-done.15
  74.2 1.5 %all-to-all-done.3 = f32[16,32,128]{2,1,0:T(8,128)} async-done(((f32[16,32,128]{2,1,0:T(8,128)}), f32[16,32,128]{2,1,0:T(8,128)}, u32[]{:S(2)}, u32[]{:S(2)}) %all-to-all-start.3) | async-done | bytes 262176 | tf_op jit(solution)/shard_map/all_to_all | solution.py:389
  75.7 3.5 %all-to-all-start.1 = ((f32[8,32,512]{2,1,0:T(8,128)}), f32[8,32,512]{2,1,0:T(8,128)S(1)}, u32[]{:S(2)}, u32[]{:S(2)}) async-start(f32[8,32,512]{2,1,0:T(8,128)} %bitcast.21), calls=%async_computation.1 | async-start | bytes 1048576 | tf_op jit(solution)/shard_map/all_to_all | solution.py:419
  79.2 1.0 reduce_sum.29
  80.2 8.7 %all-to-all-done.1 = f32[8,32,512]{2,1,0:T(8,128)S(1)} async-done(((f32[8,32,512]{2,1,0:T(8,128)}), f32[8,32,512]{2,1,0:T(8,128)S(1)}, u32[]{:S(2)}, u32[]{:S(2)}) %all-to-all-start.1) | async-done | bytes 524320 | tf_op jit(solution)/shard_map/all_to_all | solution.py:419
  88.9 0.8 broadcast_in_dim.5
  89.7 4.2 %all-to-all-start.4 = ((f32[16,32,128]{2,1,0:T(8,128)}), f32[16,32,128]{2,1,0:T(8,128)}, u32[]{:S(2)}, u32[]{:S(2)}) async-start(f32[16,32,128]{2,1,0:T(8,128)} %broadcast_in_dim.5), calls=%async_computation.4 | async-start | bytes 524288 | tf_op jit(solution)/shard_map/all_to_all | solution.py:392
  93.9 1.6 %copy-done.2 = bf16[8,512,256]{2,1,0:T(8,128)(2,1)S(1)} copy-done((bf16[8,512,256]{2,1,0:T(8,128)(2,1)S(1)}, bf16[8,512,256]{2,1,0:T(8,128)(2,1)}, u32[]{:S(2)}) %copy-start.2) | copy-done | bytes 2097176
  95.5 1.6 %copy-done.5 = bf16[8,512,256]{2,1,0:T(8,128)(2,1)S(1)} copy-done((bf16[8,512,256]{2,1,0:T(8,128)(2,1)S(1)}, bf16[8,512,256]{2,1,0:T(8,128)(2,1)}, u32[]{:S(2)}) %copy-start.5) | copy-done | bytes 2097176
  97.1 1.6 %copy-done.8 = bf16[8,512,256]{2,1,0:T(8,128)(2,1)S(1)} copy-done((bf16[8,512,256]{2,1,0:T(8,128)(2,1)S(1)}, bf16[8,512,256]{2,1,0:T(8,128)(2,1)}, u32[]{:S(2)}) %copy-start.8) | copy-done | bytes 2097176
  98.7 4.7 %shard_map.81 = f32[4,32,16,128]{3,2,1,0:T(8,128)} custom-call(bf16[8,512,256]{2,1,0:T(8,128)(2,1)S(1)} %get-tuple-element.26.own_high, bf16[8,512,256]{2,1,0:T(8,128)(2,1)S(1)} %copy-done.2, bf16[8,512,256]{2,1,0:T(8,128)(2,1)S(1)} %copy-done.5, bf16[8,512,256]{2,1,0:T(8,128)(2,1)S(1)} %copy-done.8, f32[512,128]{1,0:T(8,128)S(1)} %bitcast.24, ...), custom_call_target="tpu_custom_call" | custom-call | flops 1610612736 | bytes 4194304 | tf_op jit(solution)/shard_map/pallas_call | solution.py:370
  103.4 0.3 all-to-all-done.4
  103.8 4.7 %all-to-all-start.2 = ((f32[4,32,16,128]{3,2,1,0:T(8,128)}), f32[4,32,16,128]{3,2,1,0:T(8,128)}, u32[]{:S(2)}, u32[]{:S(2)}) async-start(f32[4,32,16,128]{3,2,1,0:T(8,128)} %shard_map.81), calls=%async_computation.2 | async-start | bytes 2097152 | tf_op jit(solution)/shard_map/all_to_all | solution.py:376
  108.4 1.6 %copy-done.17 = bf16[8,512,256]{2,1,0:T(8,128)(2,1)S(1)} copy-done((bf16[8,512,256]{2,1,0:T(8,128)(2,1)S(1)}, bf16[8,512,256]{2,1,0:T(8,128)(2,1)}, u32[]{:S(2)}) %copy-start.17) | copy-done | bytes 2097176
  110.0 1.6 %copy-done.19 = bf16[8,512,256]{2,1,0:T(8,128)(2,1)S(1)} copy-done((bf16[8,512,256]{2,1,0:T(8,128)(2,1)S(1)}, bf16[8,512,256]{2,1,0:T(8,128)(2,1)}, u32[]{:S(2)}) %copy-start.19) | copy-done | bytes 2097176
  111.6 4.8 %shard_map.78 = f32[16,4,16,128]{3,2,1,0:T(8,128)} custom-call(bf16[8,512,256]{2,1,0:T(8,128)(2,1)S(1)} %copy-done.17, bf16[8,512,256]{2,1,0:T(8,128)(2,1)S(1)} %copy-done.19, f32[1024,128]{1,0:T(8,128)S(1)} %copy-done.14), custom_call_target="tpu_custom_call" | custom-call | flops 805306368 | bytes 4194304 | tf_op jit(solution)/shard_map/pallas_call | solution.py:401
  116.5 1.5 collective-permute-start.2
  118.1 0.8 copy.23
  118.9 1.9 %reshape.48 = f32[16,1024]{1,0:T(8,128)} reshape(f32[16,32,32]{2,1,0:T(8,128)} %copy.23) | data formatting | bytes 131072 | tf_op jit(solution)/shard_map/reshape | solution.py:421
  120.8 12.9 %all-to-all-done.2 = f32[4,32,16,128]{3,2,1,0:T(8,128)} async-done(((f32[4,32,16,128]{3,2,1,0:T(8,128)}), f32[4,32,16,128]{3,2,1,0:T(8,128)}, u32[]{:S(2)}, u32[]{:S(2)}) %all-to-all-start.2) | async-done | bytes 1048608 | tf_op jit(solution)/shard_map/all_to_all | solution.py:376
  133.7 2.0 %reduce_sum.28 = f32[32,16,128]{2,1,0:T(8,128)} reduce(f32[4,32,16,128]{3,2,1,0:T(8,128)} %all-to-all-done.2, f32[]{:T(128)} %constant.13.clone.1), dimensions={0}, to_apply=%region_1.2 | reduce | flops 196608 | bytes 1310724 | tf_op jit(solution)/shard_map/reduce_sum | solution.py:377
  135.7 2.3 %copy.24 = f32[16,128,32]{2,1,0:T(8,128)} copy(f32[16,128,32]{1,0,2:T(8,128)} %bitcast.28) | data formatting | bytes 524288 | tf_op jit(solution)/shard_map/transpose | solution.py:377
  138.0 2.4 %reshape.49 = f32[16,4096]{1,0:T(8,128)} reshape(f32[16,128,32]{2,1,0:T(8,128)} %copy.24) | data formatting | bytes 524288 | tf_op jit(solution)/shard_map/reshape | solution.py:377
  140.4 1.6 %copy-done.12 = bf16[8,512,256]{2,1,0:T(8,128)(2,1)S(1)} copy-done((bf16[8,512,256]{2,1,0:T(8,128)(2,1)S(1)}, bf16[8,512,256]{2,1,0:T(8,128)(2,1)}, u32[]{:S(2)}) %copy-start.12) | copy-done | bytes 2097176
  142.0 5.0 %shard_map.79 = f32[16,8,16,128]{3,2,1,0:T(8,128)} custom-call(bf16[8,512,256]{2,1,0:T(8,128)(2,1)S(1)} %copy-done.10, bf16[8,512,256]{2,1,0:T(8,128)(2,1)S(1)} %copy-done.12, f32[1024,128]{1,0:T(8,128)S(1)} %copy-done.14, f32[16,4,16,128]{3,2,1,0:T(8,128)S(1)} %collective-permute-done.2.refs_0_), custom_call_target="tpu_custom_call" | custom-call | flops 805306368 | bytes 4194304 | tf_op jit(solution)/shard_map/pallas_call | solution.py:423
  147.0 2.1 %shard_map.82 = f32[1024,128]{1,0:T(8,128)} custom-call(f32[512,128]{1,0:T(8,128)} %bitcast.9.mine_ref, f32[512,128]{1,0:T(8,128)S(1)} %collective-permute-done.4.other_ref), custom_call_target="tpu_custom_call" | custom-call | bytes 4194304 | tf_op jit(solution)/shard_map/pallas_call | solution.py:395
  (52 shorter events, 0.6 us)
Async XLA Ops:
  1.9 7.9 %copy-start.20 = (f32[16,8,16,128]{3,2,1,0:T(8,128)S(1)}, f32[16,8,16,128]{3,2,1,0:T(8,128)}, u32[]{:S(2)}) copy-start(f32[16,8,16,128]{3,2,1,0:T(8,128)} %cotangent_ref.1) | copy-start | bytes 3145732
  3.3 8.8 %copy-start.35 = (f32[16,4096]{1,0:T(8,128)S(1)}, f32[16,4096]{1,0:T(8,128)}, u32[]{:S(2)}) copy-start(f32[16,4096]{1,0:T(8,128)} %param.4) | copy-start | bytes 786436
  3.3 32.5 %all-to-all-start = ((f32[4,32,16,128]{3,2,1,0:T(8,128)}), f32[4,32,16,128]{3,2,1,0:T(8,128)S(1)}, u32[]{:S(2)}, u32[]{:S(2)}) async-start(f32[4,32,16,128]{3,2,1,0:T(8,128)} %broadcast_in_dim.4), calls=%async_computation | async-start | bytes 2097152 | tf_op jit(solution)/shard_map/all_to_all | solution.py:347
  10.7 15.2 %collective-permute-start.1 = (f32[16,4,16,128]{3,2,1,0:T(8,128)}, f32[16,4,16,128]{3,2,1,0:T(8,128)}, u32[]{:S(2)}, u32[]{:S(2)}) collective-permute-start(f32[16,4,16,128]{3,2,1,0:T(8,128)} %fusion.1), channel_id=1, source_target_pairs={{0,4},{4,0},{8,12},{12,8},{16,20},{20,16},{24,28},{28,24},{1,5},{5... | collective-permute-start | bytes 1572872 | tf_op jit(solution)/shard_map/ppermute | solution.py:353
  12.8 22.3 %collective-permute-start = (f32[512,128]{1,0:T(8,128)S(1)}, f32[512,128]{1,0:T(8,128)S(1)}, u32[]{:S(2)}, u32[]{:S(2)}) collective-permute-start(f32[512,128]{1,0:T(8,128)S(1)} %bitcast.22), channel_id=1, source_target_pairs={{0,4},{4,0},{8,12},{12,8},{16,20},{20,16},{24,28},{28,24},{1,5},{5... | collective-permute-start | bytes 786440 | tf_op jit(solution)/shard_map/ppermute | solution.py:351
  13.4 1.0 copy-start.13
  14.4 1.2 copy-start.21
  19.2 1.4 copy-start
  20.6 1.0 copy-start.25
  21.6 1.1 copy-start.27
  30.4 1.3 copy-start.3
  31.8 1.4 copy-start.6
  33.1 1.0 copy-start.29
  34.1 1.0 copy-start.31
  35.1 0.7 copy-start.22
  35.8 1.0 copy-start.23
  36.8 1.2 copy-start.26
  38.0 1.2 copy-start.28
  39.2 1.2 copy-start.30
  40.4 1.2 copy-start.32
  50.6 1.4 copy-start.9
  52.0 1.3 copy-start.11
  53.4 1.4 copy-start.16
  54.8 1.3 copy-start.18
  56.1 1.5 %collective-permute-start.3 = (f32[512,128]{1,0:T(8,128)S(1)}, f32[512,128]{1,0:T(8,128)S(1)}, u32[]{:S(2)}, u32[]{:S(2)}) collective-permute-start(f32[512,128]{1,0:T(8,128)S(1)} %get-tuple-element.31), channel_id=1, source_target_pairs={{0,1},{1,0},{2,3},{3,2},{4,5},{5,4},{6,7},{7,6},{8,9},{9,8},{10,11... | collective-permute-start | bytes 786440 | tf_op jit(solution)/shard_map/ppermute | solution.py:386
  58.3 17.4 %all-to-all-start.3 = ((f32[16,32,128]{2,1,0:T(8,128)}), f32[16,32,128]{2,1,0:T(8,128)}, u32[]{:S(2)}, u32[]{:S(2)}) async-start(f32[16,32,128]{2,1,0:T(8,128)} %bitcast.29), calls=%async_computation.3 | async-start | bytes 524288 | tf_op jit(solution)/shard_map/all_to_all | solution.py:389
  65.5 1.6 %copy-start.1 = (bf16[8,512,256]{2,1,0:T(8,128)(2,1)S(1)}, bf16[8,512,256]{2,1,0:T(8,128)(2,1)}, u32[]{:S(2)}) copy-start(bf16[8,512,256]{2,1,0:T(8,128)(2,1)} %copy-done) | copy-start | bytes 6291460
  67.1 1.6 %copy-start.4 = (bf16[8,512,256]{2,1,0:T(8,128)(2,1)S(1)}, bf16[8,512,256]{2,1,0:T(8,128)(2,1)}, u32[]{:S(2)}) copy-start(bf16[8,512,256]{2,1,0:T(8,128)(2,1)} %copy-done.3) | copy-start | bytes 6291460
  68.7 1.6 %copy-start.7 = (bf16[8,512,256]{2,1,0:T(8,128)(2,1)S(1)}, bf16[8,512,256]{2,1,0:T(8,128)(2,1)}, u32[]{:S(2)}) copy-start(bf16[8,512,256]{2,1,0:T(8,128)(2,1)} %copy-done.6) | copy-start | bytes 6291460
  73.4 0.8 copy-start.15
  74.2 19.7 %copy-start.24 = (f32[512,128]{1,0:T(8,128)S(1)}, f32[512,128]{1,0:T(8,128)}, u32[]{:S(2)}) copy-start(f32[512,128]{1,0:T(8,128)} %copy-done.22) | copy-start | bytes 786436
  75.7 13.2 %all-to-all-start.1 = ((f32[8,32,512]{2,1,0:T(8,128)}), f32[8,32,512]{2,1,0:T(8,128)S(1)}, u32[]{:S(2)}, u32[]{:S(2)}) async-start(f32[8,32,512]{2,1,0:T(8,128)} %bitcast.21), calls=%async_computation.1 | async-start | bytes 1048576 | tf_op jit(solution)/shard_map/all_to_all | solution.py:419
  88.9 5.0 %copy-start.33 = (f32[8,32,512]{2,1,0:T(8,128)}, f32[8,32,512]{2,1,0:T(8,128)S(1)}, u32[]{:S(2)}) copy-start(f32[8,32,512]{2,1,0:T(8,128)S(1)} %all-to-all-done.1) | copy-start | bytes 1572868
  89.7 14.1 %all-to-all-start.4 = ((f32[16,32,128]{2,1,0:T(8,128)}), f32[16,32,128]{2,1,0:T(8,128)}, u32[]{:S(2)}, u32[]{:S(2)}) async-start(f32[16,32,128]{2,1,0:T(8,128)} %broadcast_in_dim.5), calls=%async_computation.4 | async-start | bytes 524288 | tf_op jit(solution)/shard_map/all_to_all | solution.py:392
  93.9 1.6 %copy-start.2 = (bf16[8,512,256]{2,1,0:T(8,128)(2,1)S(1)}, bf16[8,512,256]{2,1,0:T(8,128)(2,1)}, u32[]{:S(2)}) copy-start(bf16[8,512,256]{2,1,0:T(8,128)(2,1)} %copy-done) | copy-start | bytes 6291460
  95.5 1.6 %copy-start.5 = (bf16[8,512,256]{2,1,0:T(8,128)(2,1)S(1)}, bf16[8,512,256]{2,1,0:T(8,128)(2,1)}, u32[]{:S(2)}) copy-start(bf16[8,512,256]{2,1,0:T(8,128)(2,1)} %copy-done.3) | copy-start | bytes 6291460
  97.1 1.6 %copy-start.8 = (bf16[8,512,256]{2,1,0:T(8,128)(2,1)S(1)}, bf16[8,512,256]{2,1,0:T(8,128)(2,1)}, u32[]{:S(2)}) copy-start(bf16[8,512,256]{2,1,0:T(8,128)(2,1)} %copy-done.6) | copy-start | bytes 6291460
  103.4 5.0 %copy-start.14 = (f32[1024,128]{1,0:T(8,128)S(1)}, f32[1024,128]{1,0:T(8,128)}, u32[]{:S(2)}) copy-start(f32[1024,128]{1,0:T(8,128)} %weight_ref.7) | copy-start | bytes 1572868
  103.8 29.9 %all-to-all-start.2 = ((f32[4,32,16,128]{3,2,1,0:T(8,128)}), f32[4,32,16,128]{3,2,1,0:T(8,128)}, u32[]{:S(2)}, u32[]{:S(2)}) async-start(f32[4,32,16,128]{3,2,1,0:T(8,128)} %shard_map.81), calls=%async_computation.2 | async-start | bytes 2097152 | tf_op jit(solution)/shard_map/all_to_all | solution.py:376
  108.4 1.6 %copy-start.17 = (bf16[8,512,256]{2,1,0:T(8,128)(2,1)S(1)}, bf16[8,512,256]{2,1,0:T(8,128)(2,1)}, u32[]{:S(2)}) copy-start(bf16[8,512,256]{2,1,0:T(8,128)(2,1)} %copy-done.16) | copy-start | bytes 6291460
  110.0 1.6 %copy-start.19 = (bf16[8,512,256]{2,1,0:T(8,128)(2,1)S(1)}, bf16[8,512,256]{2,1,0:T(8,128)(2,1)}, u32[]{:S(2)}) copy-start(bf16[8,512,256]{2,1,0:T(8,128)(2,1)} %copy-done.18) | copy-start | bytes 6291460
  111.6 6.3 %copy-start.34 = (f32[8,32,512]{2,1,0:T(8,128)S(1)}, f32[8,32,512]{2,1,0:T(8,128)}, u32[]{:S(2)}) copy-start(f32[8,32,512]{2,1,0:T(8,128)} %copy-done.33) | copy-start | bytes 1572868
  116.5 23.9 %collective-permute-start.2 = (f32[16,4,16,128]{3,2,1,0:T(8,128)}, f32[16,4,16,128]{3,2,1,0:T(8,128)S(1)}, u32[]{:S(2)}, u32[]{:S(2)}) collective-permute-start(f32[16,4,16,128]{3,2,1,0:T(8,128)} %shard_map.78), channel_id=1, source_target_pairs={{0,4},{4,0},{8,12},{12,8},{16,20},{20,16},{24,28},{28,24},{1,5},{5... | collective-permute-start | bytes 1572872 | tf_op jit(solution)/shard_map/ppermute | solution.py:407
  117.9 29.1 %collective-permute-start.4 = (f32[512,128]{1,0:T(8,128)}, f32[512,128]{1,0:T(8,128)S(1)}, u32[]{:S(2)}, u32[]{:S(2)}) collective-permute-start(f32[512,128]{1,0:T(8,128)} %bitcast.9.mine_ref), channel_id=1, source_target_pairs={{0,1},{1,0},{2,3},{3,2},{4,5},{5,4},{6,7},{7,6},{8,9},{9,8},{10,11... | collective-permute-start | bytes 786440 | tf_op jit(solution)/shard_map/ppermute | solution.py:394
  118.9 21.5 %copy-start.10 = (bf16[8,512,256]{2,1,0:T(8,128)(2,1)S(1)}, bf16[8,512,256]{2,1,0:T(8,128)(2,1)}, u32[]{:S(2)}) copy-start(bf16[8,512,256]{2,1,0:T(8,128)(2,1)} %copy-done.9) | copy-start | bytes 6291460
  140.4 1.6 %copy-start.12 = (bf16[8,512,256]{2,1,0:T(8,128)(2,1)S(1)}, bf16[8,512,256]{2,1,0:T(8,128)(2,1)}, u32[]{:S(2)}) copy-start(bf16[8,512,256]{2,1,0:T(8,128)(2,1)} %copy-done.11) | copy-start | bytes 6291460

commit v4 on v0

v4 whole, which is shorter than its diff:
```python
import functools

import jax
import jax.numpy as jnp
from jax import lax
from jax.experimental import pallas as pl
from jax.experimental.pallas import tpu as pltpu
from jax.sharding import PartitionSpec as P

ENTRY_CHANNELS = 32
LANES = 128
PACK = LANES // ENTRY_CHANNELS
F32 = jnp.float32
BF16 = jnp.bfloat16
MIB = 1024 * 1024
VMEM_LIMIT = 60 * MIB


def halves(values):
    high = values.astype(BF16)
    low = (values - high.astype(F32)).astype(BF16)
    return high, low


def dot(left, right):
    return jnp.dot(left, right, preferred_element_type=F32)


def dot_rows(left, right):
    return lax.dot_general(left, right, (((1,), (1,)), ((), ())), preferred_element_type=F32)


def fold_of(columns):
    return max(1, LANES // columns)


def strided(start, size, stride):
    return pl.ds(start, size, stride=stride)


def folded_weight(weight_ref, step, fold):
    channels = ENTRY_CHANNELS
    return jnp.concatenate(
        [weight_ref[strided(step * fold + part, channels, channels), :] for part in range(fold)], 1
    )


def own_slots(blocks):
    here = lax.axis_index("blk")
    return [lax.bitwise_xor(here, 2 * slot) for slot in range(blocks)]


def peer_slots(blocks):
    here = lax.axis_index("blk") // 2
    return [lax.bitwise_xor(here, slot) for slot in range(blocks)]


def spread_of(cotangent_ref, pair, slots, fold):
    columns = len(slots) * cotangent_ref.shape[2]
    empty = jnp.zeros((columns, cotangent_ref.shape[3]), BF16)
    spread = ([], [])
    for part in range(2):
        rows = jnp.concatenate([cotangent_ref[2 * pair + part, slot] for slot in slots], 0)
        for found, values in zip(spread, halves(rows)):
            for place in range(fold):
                found.append(
                    jnp.concatenate(
                        [values if place == other else empty for other in range(fold)], 1
                    )
                )
    return [jnp.concatenate(found, 0) for found in spread]


def turn_in_kernel(rows_minor, in_ref, out_ref, tiles, square):
    channels = ENTRY_CHANNELS
    rows, features = in_ref.shape
    count = features // LANES
    for tile in range(count):
        tiles[tile * rows : (tile + 1) * rows, :] = in_ref[:, tile * LANES : (tile + 1) * LANES]
    for group in range(rows // PACK):
        found = [tiles[strided(group * PACK + k, count, rows), :] for k in range(PACK)]
        for part in range(PACK):
            lanes = slice(part * channels, (part + 1) * channels)
            square[strided(part, count, PACK), :] = jnp.concatenate([v[:, lanes] for v in found], 1)
        turned = square[...].T
        if rows_minor:
            for k in range(PACK):
                out_ref[strided(group * PACK + k, channels, rows), :] = turned[
                    k * channels : (k + 1) * channels
                ]
        else:
            out_ref[group * LANES : (group + 1) * LANES, :] = turned


def turn_out_kernel(parts, *refs):
    part_refs, (out_ref, total, square, tiles) = refs[:parts], refs[parts:]
    channels = ENTRY_CHANNELS
    rows, features = out_ref.shape
    count = features // LANES
    found = part_refs[0][...]
    for ref in part_refs[1:]:
        found = found + ref[...]
    total[...] = found
    for group in range(rows // PACK):
        stacked = [total[strided(group * PACK + k, channels, rows), :] for k in range(PACK)]
        square[...] = jnp.concatenate(stacked, 0).T
        pieces = [square[strided(part, count, PACK), :] for part in range(PACK)]
        for k in range(PACK):
            lanes = slice(k * channels, (k + 1) * channels)
            tiles[strided(group * PACK + k, count, rows), :] = jnp.concatenate(
                [piece[:, lanes] for piece in pieces], 1
            )
    for tile in range(count):
        out_ref[:, tile * LANES : (tile + 1) * LANES] = tiles[tile * rows : (tile + 1) * rows, :]


def left_sum_kernel(parts_ref, out_ref, total, tiles):
    channels = ENTRY_CHANNELS
    parts, size, width = parts_ref.shape
    rows, features = out_ref.shape
    count = features // LANES
    found = parts_ref[0]
    for part in range(1, parts):
        found = found + parts_ref[part]
    for tile in range(width // LANES):
        total[tile * size : (tile + 1) * size, :] = found[:, tile * LANES : (tile + 1) * LANES]
    for tile in range(width // LANES):
        pieces = [total[strided(tile * size + part, count, PACK), :] for part in range(PACK)]
        for k in range(PACK):
            lanes = slice(k * channels, (k + 1) * channels)
            tiles[strided(tile * PACK + k, count, rows), :] = jnp.concatenate(
                [piece[:, lanes] for piece in pieces], 1
            )
    for tile in range(count):
        out_ref[:, tile * LANES : (tile + 1) * LANES] = tiles[tile * rows : (tile + 1) * rows, :]


def gradient_kernel(own, blocks, weight_ref, cotangent_ref, out_ref, weight_cat):
    channels = ENTRY_CHANNELS
    depth, pairs = cotangent_ref.shape[2:]
    fold = fold_of(blocks * depth)

    @pl.when(pl.program_id(0) == 0)
    def prepare():
        for step in range(channels // fold):
            high, low = halves(folded_weight(weight_ref, step, fold))
            weight_cat[step * channels : (step + 1) * channels, :] = jnp.concatenate(
                [high, low, high], 1
            )

    slots = own_slots(blocks) if own else peer_slots(blocks)
    high, low = spread_of(cotangent_ref, 0, slots, fold)
    found = dot_rows(weight_cat[...], jnp.concatenate([high, high, low], 1))
    out_ref[0] = jnp.concatenate(halves(found), 1)


def rows_of_step(refs, step, half, lanes):
    channels = ENTRY_CHANNELS
    start = 2 * half * lanes
    return jnp.concatenate(
        [
            ref[
                pair,
                step * channels : (step + 1) * channels,
                start + part * lanes : start + (part + 1) * lanes,
            ]
            for ref in refs
            for pair in range(ref.shape[0])
            for part in range(2)
        ],
        0,
    )


def both_left(left_refs):
    sequences = left_refs[0].shape[1]
    return jnp.concatenate([ref[...] for ref in left_refs], 0) * (1.0 / sequences)


def right_kernel(fold, depth, own_ref, peer_ref, own_left, peer_left, *refs):
    out_refs, left_flip = refs[:-1], refs[-1]
    blocks = len(out_refs)
    sequences = own_left.shape[1]
    lanes = fold * blocks * depth

    @pl.when(pl.program_id(0) == 0)
    def prepare():
        flip_high, flip_low = halves(both_left([own_left, peer_left]).T)
        left_flip[:sequences, :] = flip_high
        left_flip[sequences:, :] = flip_low

    def stacked(half):
        return jnp.concatenate(
            [rows_of_step([own_ref, peer_ref], part, half, lanes) for part in range(2)], 1
        )

    first = dot(left_flip[...], stacked(0))
    second = dot(left_flip[:sequences, :], stacked(1))
    found = first[:sequences] + first[sequences:] + second
    for part in range(2):
        turned = found[:, part * lanes : (part + 1) * lanes].T
        for place in range(fold):
            for slot in range(blocks):
                start = (place * blocks + slot) * depth
                y = part * fold + place
                out_refs[slot][y * depth : (y + 1) * depth, :] = turned[start : start + depth]


def right_rows(right_refs, step, fold, depth):
    return jnp.concatenate(
        [
            ref[pl.ds(pl.multiple_of((step * fold + part) * depth, depth), depth), :]
            for part in range(fold)
            for ref in right_refs
        ],
        0,
    )


def weight_kernel(blocks, own_left, peer_left, own_cotangent, peer_cotangent, *refs):
    right_refs = refs[:blocks]
    keep_ref, send_ref, own_out, peer_out, own_ref, peer_ref, total, semaphores = refs[blocks:]
    channels = ENTRY_CHANNELS
    depth, pairs = own_cotangent.shape[2:]
    fold = fold_of(blocks * depth)
    lanes = fold * blocks * depth
    high, low = halves(both_left([own_left, peer_left]))
    left_cat = jnp.concatenate([high, low, high], 1)

    def outer_step(step, carry):
        right = [right_rows(right_refs, 2 * step + part, fold, depth) for part in range(2)]
        high, low = halves(jnp.concatenate(right, 0))
        found = dot_rows(left_cat, jnp.concatenate([high, high, low], 1))
        both = halves(found)
        for part in range(2):
            start = pl.multiple_of((2 * step + part) * channels, channels)
            row = 0
            for ref in (own_ref, peer_ref):
                for index in range(2 * ref.shape[0]):
                    for half in range(2):
                        lane = (2 * half + index % 2) * lanes
                        ref[index // 2, pl.ds(start, channels), lane : lane + lanes] = both[half][
                            row : row + channels, part * lanes : (part + 1) * lanes
                        ]
                    row += channels
        return carry

    lax.fori_loop(0, channels // (2 * fold), outer_step, 0)
    copies = [
        pltpu.make_async_copy(own_ref, own_out, semaphores.at[0]),
        pltpu.make_async_copy(peer_ref, peer_out, semaphores.at[1]),
    ]
    for copy in copies:
        copy.start()
    total[...] = jnp.zeros_like(total)

    def weight_step(pair, carry):
        found = None
        for ref, cotangent_ref, slots in (
            (own_ref, own_cotangent, own_slots(blocks)),
            (peer_ref, peer_cotangent, peer_slots(blocks)),
        ):
            high, low = spread_of(cotangent_ref, pair, slots, fold)
            left = ref[pair]
            left = jnp.concatenate([left, left[:, : 2 * lanes]], 1)
            term = dot(left, jnp.concatenate([high, high, low], 0))
            found = term if found is None else found + term
        total[...] += found
        return carry

    lax.fori_loop(0, own_ref.shape[0], weight_step, 0)
    core = lax.rem(lax.axis_index("inner"), 2)
    steps = channels // (2 * fold)
    for out_ref, half in ((keep_ref, core), (send_ref, 1 - core)):
        for step in range(steps):
            start = pl.multiple_of((half * steps + step) * channels, channels)
            found = total[pl.ds(start, channels), :]
            for part in range(fold):
                y = step * fold + part
                out_ref[y * channels : (y + 1) * channels, :] = found[
                    :, part * pairs : (part + 1) * pairs
                ]
    for copy in copies:
        copy.wait()


def left_kernel(blocks, depth, steps, own_ref, peer_ref, *refs):
    right_refs = refs[:blocks]
    out_ref, total, flipped = refs[blocks:]
    lanes = own_ref.shape[2] // 4
    fold = lanes // (blocks * depth)
    sequences = right_refs[0].shape[1]
    at = pl.program_id(0)

    @pl.when(at == 0)
    def prepare():
        total[...] = jnp.zeros_like(total)

    right = [right_rows(right_refs, at * steps + part, fold, depth) for part in range(steps)]
    high, low = halves(jnp.concatenate(right, 0))
    grads = [
        jnp.concatenate(
            [rows_of_step([own_ref, peer_ref], part, half, lanes) for part in range(steps)], 1
        )
        for half in range(2)
    ]
    both = dot(grads[0], jnp.concatenate([high, low], 1))
    total[...] += both[:, :sequences] + both[:, sequences:] + dot(grads[1], high)

    @pl.when(at == pl.num_programs(0) - 1)
    def finish():
        flipped[...] = total[...].T * (1.0 / sequences)
        parity = lax.rem(lax.axis_index("blk"), 2)
        inner, size, width = out_ref.shape[1:]
        for side, start in ((parity, 0), (1 - parity, width)):
            for part in range(inner):
                out_ref[side, part] = flipped[
                    part * size : (part + 1) * size, start : start + width
                ]


def pair_kernel(final, blocks, outer_ref, weight_ref, *refs):
    if final:
        other_ref, out_ref, weight_flip, weight_rows = refs
    else:
        out_ref, weight_flip, weight_rows = refs
    channels = ENTRY_CHANNELS
    depth, pairs = out_ref.shape[2:]
    lanes = outer_ref.shape[2] // 4
    columns = blocks * depth
    fold = lanes // columns
    wide = fold * pairs

    @pl.when(pl.program_id(0) == 0)
    def prepare():
        for step in range(channels // fold):
            weight_rows[step * channels : (step + 1) * channels, :] = folded_weight(
                weight_ref, step, fold
            )
        flip_high, flip_low = halves(weight_rows[...].T)
        weight_flip[:wide, :] = flip_high
        weight_flip[wide:, :] = flip_low

    first = dot(weight_flip[...], outer_ref[0, :, : 2 * lanes])
    second = dot(weight_flip[:wide, :], outer_ref[0, :, 2 * lanes :])
    found = first[:wide] + first[wide:] + second
    slots = own_slots(blocks) if final else peer_slots(blocks)
    for part in range(2):
        turned = []
        for place in range(fold):
            start = part * lanes
            piece = found[place * pairs : (place + 1) * pairs, start : start + lanes].T
            turned.append(piece[place * columns : (place + 1) * columns])
        turned = functools.reduce(jnp.add, turned)
        for slot in range(blocks):
            out_ref[part, slots[slot]] = turned[slot * depth : (slot + 1) * depth]
            if final:
                other = 2 * slot + 1 - lax.rem(lax.axis_index("blk"), 2)
                out_ref[part, other] = other_ref[part, slot]


def spread_sum_kernel(in_ref, out_ref):
    found = in_ref[0]
    for part in range(1, in_ref.shape[0]):
        found = found + in_ref[part]
    for part in range(in_ref.shape[0]):
        out_ref[part] = found


def place_kernel(mine_ref, other_ref, out_ref):
    channels = ENTRY_CHANNELS
    core = lax.rem(lax.axis_index("inner"), 2)
    steps = mine_ref.shape[0] // channels
    for ref, half in ((mine_ref, core), (other_ref, 1 - core)):
        for step in range(steps):
            rows = ref[step * channels : (step + 1) * channels, :]
            out_ref[strided(half * steps + step, channels, channels), :] = rows


def shape(*sizes, kind=F32):
    return jax.ShapeDtypeStruct(sizes, kind)


def call(kernel, out_shape, scratch=(), cost=0, name=None, **grid):
    return pl.pallas_call(
        kernel,
        out_shape=out_shape,
        scratch_shapes=list(scratch),
        compiler_params=pltpu.CompilerParams(vmem_limit_bytes=VMEM_LIMIT),
        cost_estimate=pl.CostEstimate(flops=int(cost), bytes_accessed=2 * MIB, transcendentals=0),
        name=name,
        **grid,
    )


def whole(*sizes):
    return pl.BlockSpec(sizes, lambda step: (0,) * len(sizes))


def along(axis, *sizes):
    return pl.BlockSpec(
        sizes, lambda step: tuple(step if at == axis else 0 for at in range(len(sizes)))
    )


def local(alignment_left, alignment_right, projection_matrix, cotangent):
    rows, features = alignment_left.shape
    depth = alignment_right.shape[0]
    count = lax.axis_size("blk")
    inner = lax.axis_size("inner")
    channels = ENTRY_CHANNELS
    sequences = features // channels
    outer, pairs = projection_matrix.shape
    blocks = count // 2
    fold = fold_of(blocks * depth)
    lanes = fold * blocks * depth
    tall = outer // fold
    steps = channels // fold
    row_pairs = rows // 2
    flops = 2 * rows * 2 * blocks * depth * outer * pairs * 3
    everyone = ("blk", "inner")

    partner = [(here, here ^ 1) for here in range(count)]
    slot_moves = [[(here, here ^ (2 * slot)) for here in range(count)] for slot in range(blocks)]
    cores = [(here, here ^ 1) for here in range(inner)]
    row_groups = [
        [(2 * step + side) * inner + part for side in range(2) for part in range(inner)]
        for step in range(blocks)
    ]
    core_groups = [list(range(core, count * inner, 2)) for core in range(2)]

    def turn(values, rows_minor, name):
        size = values.shape[0]
        return call(
            functools.partial(turn_in_kernel, rows_minor),
            shape(size * channels, sequences),
            [pltpu.VMEM((size * features // LANES, LANES), F32), pltpu.VMEM((LANES, LANES), F32)],
            name=name,
        )(values)

    right = turn(alignment_right, True, "turn_right")
    rights = [right]
    for slot in range(1, blocks):
        rights.append(lax.ppermute(right, "blk", slot_moves[slot]))

    by_side = cotangent.reshape(rows, blocks, 2, depth, pairs)
    parity = lax.rem(lax.axis_index("blk"), 2)
    cotangent_peer = lax.ppermute(
        jnp.where(parity == 0, by_side[:, :, 1], by_side[:, :, 0]), "blk", partner
    )
    left = turn(alignment_left, False, "turn_left")
    left_peer = lax.ppermute(left, "blk", partner)

    def gradient(values, own, name):
        return call(
            functools.partial(gradient_kernel, own, blocks),
            shape(row_pairs, tall, 4 * lanes, kind=BF16),
            [pltpu.VMEM((tall, 3 * fold * pairs), BF16)],
            flops / 2,
            name,
            grid=(row_pairs,),
            in_specs=[whole(outer, pairs), along(0, 2, values.shape[1], depth, pairs)],
            out_specs=along(0, 1, tall, 4 * lanes),
        )(projection_matrix, values)

    grad_own = gradient(cotangent, True, "gradient_own")
    grad_peer = gradient(cotangent_peer, False, "gradient_peer")

    half_steps = steps // 2
    right_parts = call(
        functools.partial(right_kernel, fold, depth),
        [shape(channels * depth, sequences)] * blocks,
        [pltpu.VMEM((2 * sequences, 2 * rows * channels), BF16)],
        flops,
        "right_parts",
        grid=(half_steps,),
        in_specs=[along(1, row_pairs, 2 * channels, 4 * lanes)] * 2
        + [whole(rows * channels, sequences)] * 2,
        out_specs=[along(0, 2 * fold * depth, sequences)] * blocks,
    )(grad_own, grad_peer, left, left_peer)
    right_found = [right_parts[0]]
    for slot in range(1, blocks):
        right_found.append(lax.ppermute(right_parts[slot], "blk", slot_moves[slot]))

    vmem = pl.BlockSpec(memory_space=pltpu.VMEM)
    hbm = pl.BlockSpec(memory_space=pl.ANY)
    factor = shape(row_pairs, tall, 4 * lanes, kind=BF16)
    factor_scratch = pltpu.VMEM(factor.shape, BF16)
    keep, send, outer_own, outer_peer = call(
        functools.partial(weight_kernel, blocks),
        [shape(outer // 2, pairs)] * 2 + [factor] * 2,
        [
            factor_scratch,
            factor_scratch,
            pltpu.VMEM((tall, fold * pairs), F32),
            pltpu.SemaphoreType.DMA((2,)),
        ],
        2 * flops,
        "weight",
        in_specs=[vmem] * (4 + blocks),
        out_specs=[vmem, vmem, hbm, hbm],
    )(left, left_peer, cotangent, cotangent_peer, *rights)
    keep = keep + lax.ppermute(send, "inner", cores)
    members = count * inner // 2
    pieces = keep.reshape(members, outer // 2 // members, pairs)
    pieces = lax.all_to_all(pieces, everyone, 0, 0, axis_index_groups=core_groups)
    pieces = call(spread_sum_kernel, shape(*pieces.shape), name="weight_sum")(pieces)
    pieces = lax.all_to_all(pieces, everyone, 0, 0, axis_index_groups=core_groups)
    mine = pieces.reshape(outer // 2, pairs)
    other = lax.ppermute(mine, "inner", cores)
    grad_weight = call(place_kernel, shape(outer, pairs), name="place")(mine, other)

    def pair(values, others, name):
        final = bool(others)
        width = count if final else blocks
        return call(
            functools.partial(pair_kernel, final, blocks),
            shape(rows, width, depth, pairs),
            [
                pltpu.VMEM((2 * fold * pairs, tall), BF16),
                pltpu.VMEM((tall, fold * pairs), F32),
            ],
            flops / 2,
            name,
            grid=(row_pairs,),
            in_specs=[along(0, 1, tall, 4 * lanes), whole(outer, pairs)]
            + [along(0, 2, blocks, depth, pairs)] * len(others),
            out_specs=along(0, 2, width, depth, pairs),
        )(values, projection_matrix, *others)

    pair_peer = lax.ppermute(pair(outer_peer, [], "pair_peer"), "blk", partner)

    group = 4
    left_parts = call(
        functools.partial(left_kernel, blocks, depth, group),
        shape(2, inner, sequences // inner, rows * channels),
        [
            pltpu.VMEM((2 * rows * channels, sequences), F32),
            pltpu.VMEM((sequences, 2 * rows * channels), F32),
        ],
        flops,
        "left_parts",
        grid=(steps // group,),
        in_specs=[along(1, row_pairs, group * channels, 4 * lanes)] * 2
        + [whole(channels * depth, sequences)] * blocks,
        out_specs=whole(2, inner, sequences // inner, rows * channels),
    )(grad_own, grad_peer, *rights)
    left_parts = left_parts.reshape(2 * inner, sequences // inner, rows * channels)
    left_parts = lax.all_to_all(left_parts, everyone, 0, 0, axis_index_groups=row_groups)
    size = sequences // inner
    grad_left = call(
        left_sum_kernel,
        shape(rows, features // inner),
        [
            pltpu.VMEM((size * rows * channels // LANES, LANES), F32),
            pltpu.VMEM((rows * features // inner // LANES, LANES), F32),
        ],
        name="left_sum",
    )(left_parts)

    grad_right = call(
        functools.partial(turn_out_kernel, blocks),
        shape(depth, features),
        [
            pltpu.VMEM((channels * depth, sequences), F32),
            pltpu.VMEM((LANES, LANES), F32),
            pltpu.VMEM((depth * features // LANES, LANES), F32),
        ],
        name="turn_right_sum",
    )(*right_found)

    pair_update = pair(outer_own, [pair_peer], "pair_own")
    return (pair_update, grad_left, grad_right, grad_weight)


def solution(mesh):
    placed = (
        P(("groups", "blk"), None),
        P(("groups", "blk", "inner"), None),
        P(),
        P(("groups", "blk"), None, "inner", None),
    )
    return jax.shard_map(
        local,
        mesh=mesh,
        in_specs=placed,
        out_specs=(
            P(("groups", "blk"), None, "inner", None),
            P(("groups", "blk"), "inner"),
            P(("groups", "blk", "inner"), None),
            P("groups", None),
        ),
        check_vma=False,
    )
```

time: 699 us -> 161 us (0.23)
  the two profiles are of different devices: /device:TPU:0 before, /device:TPU:10 now
where the time goes in v4:
time: 161 us; the launch traced here: 160 us
  Pallas kernels  70.9 us (44%)
  waiting for transfers between devices  44.6 us (28%)
  starting transfers between devices  20.5 us (13%)
  blocking collectives  16.2 us (10%)
  local copies, waits for them, and re-layouts  4.56 us (3%)
  other arithmetic  2.28 us (1%)
    ppermute x3, waiting for transfers between devices, local(): right_found.append(lax.ppermute(right_parts[slot], 'blk', slot_moves[slot]))  23.2 us
    all_to_all x1, blocking collectives, local(): lax.all_to_all(pieces, everyone, 0, 0, axis_index_groups=core_groups)  16.2 us
    pallas_call x2, Pallas kernels, pair(): call(functools.partial(pair_kernel, final, blocks), shape(rows, width, de...  16.1 us
    pallas_call x2, Pallas kernels, gradient(): call(functools.partial(gradient_kernel, own, blocks), shape(row_pairs, ta...  15.4 us
    pallas_call x1, Pallas kernels, local(): call(functools.partial(weight_kernel, blocks), [shape(outer // 2, pairs)]...  11.7 us
    ppermute x3, waiting for transfers between devices, local(): rights.append(lax.ppermute(right, 'blk', slot_moves[slot]))  10.8 us
    ppermute x1, waiting for transfers between devices, local(): left_peer = lax.ppermute(left, 'blk', partner)  8.91 us
    pallas_call x1, Pallas kernels, local(): call(functools.partial(right_kernel, fold, depth), [shape(channels * dept...  8.61 us
  transfers between devices with their start and end apart: 13, of which 7 were waited for; matrix products, arithmetic and copies ran while one was open for 0% of the time, Pallas kernels for 35%

profile of v4, /device:TPU:10, one launch (start us, length us, event | category | flops | bytes accessed | tf_op | source)
XLA Modules:
  0.0 159.7 jit_solution(12707521133973212340)
XLA Ops:
  0.6 1.3 fusion.1
  1.9 1.6 collective-permute-start.1
  3.5 2.1 %turn_left.1.own_left = f32[512,128]{1,0:T(8,128)} custom-call(f32[16,4096]{1,0:T(8,128)} %in_ref.2), custom_call_target="tpu_custom_call" | custom-call | bytes 2097152 | tf_op jit(solution)/shard_map/turn_left/pallas_call | solution.py:434
  5.7 0.5 collective-permute-start
  6.2 2.2 %turn_right.1.refs_0_ = f32[512,128]{1,0:T(8,128)} custom-call(f32[16,4096]{1,0:T(8,128)} %in_ref.3), custom_call_target="tpu_custom_call" | custom-call | bytes 2097152 | tf_op jit(solution)/shard_map/turn_right/pallas_call | solution.py:434
  8.3 1.6 collective-permute-start.4
  9.9 1.2 collective-permute-start.3
  11.1 1.2 collective-permute-start.2
  12.4 8.9 %collective-permute-done.peer_left = f32[512,128]{1,0:T(8,128)S(1)} collective-permute-done((f32[512,128]{1,0:T(8,128)}, f32[512,128]{1,0:T(8,128)S(1)}, u32[]{:S(2)}, u32[]{:S(2)}) %collective-permute-start) | collective-permute-done | bytes 262176 | tf_op jit(solution)/shard_map/ppermute | solution.py:452
  21.3 0.0 copy-start.4
  21.3 7.0 %collective-permute-done.4.refs_3_ = f32[512,128]{1,0:T(8,128)S(1)} collective-permute-done((f32[512,128]{1,0:T(8,128)}, f32[512,128]{1,0:T(8,128)S(1)}, u32[]{:S(2)}, u32[]{:S(2)}) %collective-permute-start.4) | collective-permute-done | bytes 262176 | tf_op jit(solution)/shard_map/ppermute | solution.py:444
  28.3 0.0 copy-start.5
  28.3 3.8 %collective-permute-done.3.refs_2_ = f32[512,128]{1,0:T(8,128)S(1)} collective-permute-done((f32[512,128]{1,0:T(8,128)}, f32[512,128]{1,0:T(8,128)S(1)}, u32[]{:S(2)}, u32[]{:S(2)}) %collective-permute-start.3) | collective-permute-done | bytes 262176 | tf_op jit(solution)/shard_map/ppermute | solution.py:444
  32.1 0.0 copy-start.6
  32.1 0.0 collective-permute-done.2.refs_1_
  32.1 0.0 copy-start.7
  32.1 0.0 collective-permute-done.1.peer_cotangent.cotangent_ref
  32.1 0.0 copy-done.4
  32.1 0.0 copy-done.5
  32.1 0.7 copy-done.6
  32.8 0.1 copy-done.7
  32.9 0.0 copy-start.3
  32.9 0.8 copy-done.3
  33.7 11.7 %weight.1 = (f32[512,128]{1,0:T(8,128)}, f32[512,128]{1,0:T(8,128)}, bf16[8,512,512]{2,1,0:T(8,128)(2,1)}, bf16[8,512,512]{2,1,0:T(8,128)(2,1)}) custom-call(f32[512,128]{1,0:T(8,128)} %turn_left.1.own_left, f32[512,128]{1,0:T(8,128)} %copy-done.4, f32[16,8,16,128]{3,2,1,0:T(8,128)} %cotangent_ref.1, f32[16,4,16,128]{3,2,1,0:T(8,128)} %copy-done.3, ...), custom_call_target="tpu_custom_call" | custom-call | flops 3221225472 | bytes 2097152 | tf_op jit(solution)/shard_map/weight/pallas_call | solution.py:489
  45.4 0.1 collective-permute-start.9
  45.5 1.7 %collective-permute-done.9 = f32[512,128]{1,0:T(8,128)S(1)} collective-permute-done((f32[512,128]{1,0:T(8,128)}, f32[512,128]{1,0:T(8,128)S(1)}, u32[]{:S(2)}, u32[]{:S(2)}) %collective-permute-start.9) | collective-permute-done | bytes 262176 | tf_op jit(solution)/shard_map/ppermute | solution.py:503
  47.2 1.0 add.3
  48.2 16.2 %all_to_all.15.in_ref = f32[16,32,128]{2,1,0:T(8,128)} all-to-all(f32[16,32,128]{2,1,0:T(8,128)S(1)} %bitcast.18), channel_id=1, replica_groups={{0,2,4,6,8,10,12,14,16,18,20,22,24,26,28,30},{1,3,5,7,9,11,13,15,17,19,..., dimensions={0} | all-to-all | bytes 524288 | tf_op jit(solution)/shard_map/all_to_all | solution.py:506
  64.4 1.7 %weight_sum.1 = f32[16,32,128]{2,1,0:T(8,128)} custom-call(f32[16,32,128]{2,1,0:T(8,128)} %all_to_all.15.in_ref), custom_call_target="tpu_custom_call" | custom-call | bytes 2097152 | tf_op jit(solution)/shard_map/weight_sum/pallas_call | solution.py:507
  66.1 5.3 %all-to-all-start.2 = ((f32[16,32,128]{2,1,0:T(8,128)}), f32[16,32,128]{2,1,0:T(8,128)S(1)}, u32[]{:S(2)}, u32[]{:S(2)}) async-start(f32[16,32,128]{2,1,0:T(8,128)} %weight_sum.1), calls=%async_computation.2 | async-start | bytes 524288 | tf_op jit(solution)/shard_map/all_to_all | solution.py:508
  71.4 7.9 %gradient_own.1.own_ref = bf16[8,512,512]{2,1,0:T(8,128)(2,1)} custom-call(f32[1024,128]{1,0:T(8,128)} %weight_ref.7, f32[16,8,16,128]{3,2,1,0:T(8,128)} %cotangent_ref.1), custom_call_target="tpu_custom_call" | custom-call | flops 805306368 | bytes 2097152 | tf_op jit(solution)/shard_map/gradient_own/pallas_call | solution.py:455
  79.3 8.0 %pair_peer.1 = f32[16,4,16,128]{3,2,1,0:T(8,128)} custom-call(bf16[8,512,512]{2,1,0:T(8,128)(2,1)} %get-tuple-element.13.outer_ref, f32[1024,128]{1,0:T(8,128)} %weight_ref.7), custom_call_target="tpu_custom_call" | custom-call | flops 805306368 | bytes 2097152 | tf_op jit(solution)/shard_map/pair_peer/pallas_call | solution.py:516
  87.3 1.5 collective-permute-start.5
  88.8 7.4 %gradient_peer.1.peer_ref = bf16[8,512,512]{2,1,0:T(8,128)(2,1)} custom-call(f32[1024,128]{1,0:T(8,128)} %weight_ref.7, f32[16,4,16,128]{3,2,1,0:T(8,128)} %copy-done.3), custom_call_target="tpu_custom_call" | custom-call | flops 805306368 | bytes 2097152 | tf_op jit(solution)/shard_map/gradient_peer/pallas_call | solution.py:455
  96.2 6.7 %left_parts.1 = f32[2,4,32,512]{3,2,1,0:T(8,128)} custom-call(bf16[8,512,512]{2,1,0:T(8,128)(2,1)} %gradient_own.1.own_ref, bf16[8,512,512]{2,1,0:T(8,128)(2,1)} %gradient_peer.1.peer_ref, f32[512,128]{1,0:T(8,128)} %turn_right.1.refs_0_, f32[512,128]{1,0:T(8,128)} %copy-done.7, f32[512,128]{1,0:T(8,128)} %copy-done.6, f32[512,128]{1,0:T(8,128)} %copy-done.5), custom_call_target="tpu_custom_call" | custom-call | flops 1610612736 | bytes 2097152 | tf_op jit(solution)/shard_map/left_parts/pallas_call | solution.py:534
  103.0 0.0 all-to-all-done.2
  103.0 0.0 copy-start.1
  103.0 4.0 %all-to-all-start = ((f32[8,32,512]{2,1,0:T(8,128)}), f32[8,32,512]{2,1,0:T(8,128)S(1)}, u32[]{:S(2)}, u32[]{:S(2)}) async-start(f32[8,32,512]{2,1,0:T(8,128)} %bitcast.17), calls=%async_computation | async-start | bytes 1048576 | tf_op jit(solution)/shard_map/all_to_all | solution.py:549
  106.9 8.6 %right_parts.1 = (f32[512,128]{1,0:T(8,128)}, f32[512,128]{1,0:T(8,128)}, f32[512,128]{1,0:T(8,128)}, f32[512,128]{1,0:T(8,128)}) custom-call(bf16[8,512,512]{2,1,0:T(8,128)(2,1)} %gradient_own.1.own_ref, bf16[8,512,512]{2,1,0:T(8,128)(2,1)} %gradient_peer.1.peer_ref, f32[512,128]{1,0:T(8,128)} %turn_left.1.own_left, f32[512,128]{1,0:T(8,128)} %copy-done.4), custom_call_target="tpu_custom_call" | custom-call | flops 1610612736 | bytes 2097152 | tf_op jit(solution)/shard_map/right_parts/pallas_call | solution.py:470
  115.6 0.6 collective-permute-start.6
  116.1 2.4 %collective-permute-start.7 = (f32[512,128]{1,0:T(8,128)}, f32[512,128]{1,0:T(8,128)S(1)}, u32[]{:S(2)}, u32[]{:S(2)}) collective-permute-start(f32[512,128]{1,0:T(8,128)} %get-tuple-element.16), channel_id=1, source_target_pairs={{0,16},{4,20},{8,24},{12,28},{16,0},{20,4},{24,8},{28,12},{1,17},{... | collective-permute-start | bytes 786440 | tf_op jit(solution)/shard_map/ppermute | solution.py:483
  118.5 0.6 collective-permute-start.8
  119.1 0.0 copy-done.1
  119.1 0.0 collective-permute-start.10
  119.1 8.2 %collective-permute-done.6.refs_1_ = f32[512,128]{1,0:T(8,128)S(1)} collective-permute-done((f32[512,128]{1,0:T(8,128)}, f32[512,128]{1,0:T(8,128)S(1)}, u32[]{:S(2)}, u32[]{:S(2)}) %collective-permute-start.6) | collective-permute-done | bytes 262176 | tf_op jit(solution)/shard_map/ppermute | solution.py:483
  127.3 0.0 copy-start.8
  127.3 9.5 %collective-permute-done.7.refs_2_ = f32[512,128]{1,0:T(8,128)S(1)} collective-permute-done((f32[512,128]{1,0:T(8,128)}, f32[512,128]{1,0:T(8,128)S(1)}, u32[]{:S(2)}, u32[]{:S(2)}) %collective-permute-start.7) | collective-permute-done | bytes 262176 | tf_op jit(solution)/shard_map/ppermute | solution.py:483
  136.8 0.0 copy-start.9
  136.8 5.5 %collective-permute-done.8.refs_3_ = f32[512,128]{1,0:T(8,128)S(1)} collective-permute-done((f32[512,128]{1,0:T(8,128)}, f32[512,128]{1,0:T(8,128)S(1)}, u32[]{:S(2)}, u32[]{:S(2)}) %collective-permute-start.8) | collective-permute-done | bytes 262176 | tf_op jit(solution)/shard_map/ppermute | solution.py:483
  142.2 0.0 copy-start.10
  142.2 0.0 copy-done.8
  142.2 0.0 copy-done.9
  142.2 0.7 copy-done.10
  142.9 2.4 %turn_right_sum.1 = f32[16,4096]{1,0:T(8,128)} custom-call(f32[512,128]{1,0:T(8,128)} %get-tuple-element.14.refs_0_, f32[512,128]{1,0:T(8,128)} %copy-done.8, f32[512,128]{1,0:T(8,128)} %copy-done.9, f32[512,128]{1,0:T(8,128)} %copy-done.10), custom_call_target="tpu_custom_call" | custom-call | bytes 2097152 | tf_op jit(solution)/shard_map/turn_right_sum/pallas_call | solution.py:561
  145.3 0.0 all-to-all-done.parts_ref
  145.3 0.0 copy-start
  145.3 0.8 copy-done
  146.1 1.8 %left_sum.1 = f32[16,1024]{1,0:T(8,128)} custom-call(f32[8,32,512]{2,1,0:T(8,128)} %copy-done), custom_call_target="tpu_custom_call" | custom-call | bytes 2097152 | tf_op jit(solution)/shard_map/left_sum/pallas_call | solution.py:551
  147.9 0.0 collective-permute-done.5.refs_0_
  148.0 0.8 copy-done.2
  148.7 8.1 %pair_own.1 = f32[16,8,16,128]{3,2,1,0:T(8,128)} custom-call(bf16[8,512,512]{2,1,0:T(8,128)(2,1)} %get-tuple-element.12.outer_ref, f32[1024,128]{1,0:T(8,128)} %weight_ref.7, f32[16,4,16,128]{3,2,1,0:T(8,128)} %copy-done.2), custom_call_target="tpu_custom_call" | custom-call | flops 805306368 | bytes 2097152 | tf_op jit(solution)/shard_map/pair_own/pallas_call | solution.py:516
  156.9 0.0 collective-permute-done.10.other_ref
  156.9 0.7 copy-done.11
  157.6 2.1 %place.1 = f32[1024,128]{1,0:T(8,128)} custom-call(f32[512,128]{1,0:T(8,128)} %bitcast.20, f32[512,128]{1,0:T(8,128)} %copy-done.11), custom_call_target="tpu_custom_call" | custom-call | bytes 2097152 | tf_op jit(solution)/shard_map/place/pallas_call | solution.py:511
  (2 shorter events, 0.0 us)
Async XLA Ops:
  1.9 30.1 %collective-permute-start.1 = (f32[16,4,16,128]{3,2,1,0:T(8,128)S(1)}, f32[16,4,16,128]{3,2,1,0:T(8,128)S(1)}, u32[]{:S(2)}, u32[]{:S(2)}) collective-permute-start(f32[16,4,16,128]{3,2,1,0:T(8,128)S(1)} %fusion.1), channel_id=1, source_target_pairs={{0,4},{4,0},{8,12},{12,8},{16,20},{20,16},{24,28},{28,24},{1,5},{5... | collective-permute-start | bytes 1572872 | tf_op jit(solution)/shard_map/ppermute | solution.py:448
  5.7 15.6 %collective-permute-start = (f32[512,128]{1,0:T(8,128)}, f32[512,128]{1,0:T(8,128)S(1)}, u32[]{:S(2)}, u32[]{:S(2)}) collective-permute-start(f32[512,128]{1,0:T(8,128)} %turn_left.1.own_left), channel_id=1, source_target_pairs={{0,4},{4,0},{8,12},{12,8},{16,20},{20,16},{24,28},{28,24},{1,5},{5... | collective-permute-start | bytes 786440 | tf_op jit(solution)/shard_map/ppermute | solution.py:452
  8.3 19.9 %collective-permute-start.4 = (f32[512,128]{1,0:T(8,128)}, f32[512,128]{1,0:T(8,128)S(1)}, u32[]{:S(2)}, u32[]{:S(2)}) collective-permute-start(f32[512,128]{1,0:T(8,128)} %turn_right.1.refs_0_), channel_id=1, source_target_pairs={{0,24},{4,28},{8,16},{12,20},{16,8},{20,12},{24,0},{28,4},{1,25},{... | collective-permute-start | bytes 786440 | tf_op jit(solution)/shard_map/ppermute | solution.py:444
  9.9 22.2 %collective-permute-start.3 = (f32[512,128]{1,0:T(8,128)}, f32[512,128]{1,0:T(8,128)S(1)}, u32[]{:S(2)}, u32[]{:S(2)}) collective-permute-start(f32[512,128]{1,0:T(8,128)} %turn_right.1.refs_0_), channel_id=1, source_target_pairs={{0,16},{4,20},{8,24},{12,28},{16,0},{20,4},{24,8},{28,12},{1,17},{... | collective-permute-start | bytes 786440 | tf_op jit(solution)/shard_map/ppermute | solution.py:444
  11.1 20.9 %collective-permute-start.2 = (f32[512,128]{1,0:T(8,128)}, f32[512,128]{1,0:T(8,128)S(1)}, u32[]{:S(2)}, u32[]{:S(2)}) collective-permute-start(f32[512,128]{1,0:T(8,128)} %turn_right.1.refs_0_), channel_id=1, source_target_pairs={{0,8},{4,12},{8,0},{12,4},{16,24},{20,28},{24,16},{28,20},{1,9},{5... | collective-permute-start | bytes 786440 | tf_op jit(solution)/shard_map/ppermute | solution.py:444
  21.3 10.8 %copy-start.4 = (f32[512,128]{1,0:T(8,128)}, f32[512,128]{1,0:T(8,128)S(1)}, u32[]{:S(2)}) copy-start(f32[512,128]{1,0:T(8,128)S(1)} %collective-permute-done.peer_left) | copy-start | bytes 786436
  28.3 3.8 %copy-start.5 = (f32[512,128]{1,0:T(8,128)}, f32[512,128]{1,0:T(8,128)S(1)}, u32[]{:S(2)}) copy-start(f32[512,128]{1,0:T(8,128)S(1)} %collective-permute-done.4.refs_3_) | copy-start | bytes 786436
  32.1 0.7 copy-start.6
  32.1 0.8 copy-start.7
  32.9 0.8 copy-start.3
  45.4 1.8 %collective-permute-start.9 = (f32[512,128]{1,0:T(8,128)}, f32[512,128]{1,0:T(8,128)S(1)}, u32[]{:S(2)}, u32[]{:S(2)}) collective-permute-start(f32[512,128]{1,0:T(8,128)} %get-tuple-element.19), channel_id=1, source_target_pairs={{0,1},{1,0},{2,3},{3,2},{4,5},{5,4},{6,7},{7,6},{8,9},{9,8},{10,11... | collective-permute-start | bytes 786440 | tf_op jit(solution)/shard_map/ppermute | solution.py:503
  66.1 36.8 %all-to-all-start.2 = ((f32[16,32,128]{2,1,0:T(8,128)}), f32[16,32,128]{2,1,0:T(8,128)S(1)}, u32[]{:S(2)}, u32[]{:S(2)}) async-start(f32[16,32,128]{2,1,0:T(8,128)} %weight_sum.1), calls=%async_computation.2 | async-start | bytes 524288 | tf_op jit(solution)/shard_map/all_to_all | solution.py:508
  87.3 60.7 %collective-permute-start.5 = (f32[16,4,16,128]{3,2,1,0:T(8,128)}, f32[16,4,16,128]{3,2,1,0:T(8,128)S(1)}, u32[]{:S(2)}, u32[]{:S(2)}) collective-permute-start(f32[16,4,16,128]{3,2,1,0:T(8,128)} %pair_peer.1), channel_id=1, source_target_pairs={{0,4},{4,0},{8,12},{12,8},{16,20},{20,16},{24,28},{28,24},{1,5},{5... | collective-permute-start | bytes 1572872 | tf_op jit(solution)/shard_map/ppermute | solution.py:531
  103.0 16.1 %copy-start.1 = (f32[16,32,128]{2,1,0:T(8,128)}, f32[16,32,128]{2,1,0:T(8,128)S(1)}, u32[]{:S(2)}) copy-start(f32[16,32,128]{2,1,0:T(8,128)S(1)} %all-to-all-done.2) | copy-start | bytes 786436
  103.0 42.4 %all-to-all-start = ((f32[8,32,512]{2,1,0:T(8,128)}), f32[8,32,512]{2,1,0:T(8,128)S(1)}, u32[]{:S(2)}, u32[]{:S(2)}) async-start(f32[8,32,512]{2,1,0:T(8,128)} %bitcast.17), calls=%async_computation | async-start | bytes 1048576 | tf_op jit(solution)/shard_map/all_to_all | solution.py:549
  115.6 11.7 %collective-permute-start.6 = (f32[512,128]{1,0:T(8,128)}, f32[512,128]{1,0:T(8,128)S(1)}, u32[]{:S(2)}, u32[]{:S(2)}) collective-permute-start(f32[512,128]{1,0:T(8,128)} %get-tuple-element.15), channel_id=1, source_target_pairs={{0,8},{4,12},{8,0},{12,4},{16,24},{20,28},{24,16},{28,20},{1,9},{5... | collective-permute-start | bytes 786440 | tf_op jit(solution)/shard_map/ppermute | solution.py:483
  116.1 20.6 %collective-permute-start.7 = (f32[512,128]{1,0:T(8,128)}, f32[512,128]{1,0:T(8,128)S(1)}, u32[]{:S(2)}, u32[]{:S(2)}) collective-permute-start(f32[512,128]{1,0:T(8,128)} %get-tuple-element.16), channel_id=1, source_target_pairs={{0,16},{4,20},{8,24},{12,28},{16,0},{20,4},{24,8},{28,12},{1,17},{... | collective-permute-start | bytes 786440 | tf_op jit(solution)/shard_map/ppermute | solution.py:483
  118.5 23.7 %collective-permute-start.8 = (f32[512,128]{1,0:T(8,128)}, f32[512,128]{1,0:T(8,128)S(1)}, u32[]{:S(2)}, u32[]{:S(2)}) collective-permute-start(f32[512,128]{1,0:T(8,128)} %get-tuple-element.17), channel_id=1, source_target_pairs={{0,24},{4,28},{8,16},{12,20},{16,8},{20,12},{24,0},{28,4},{1,25},{... | collective-permute-start | bytes 786440 | tf_op jit(solution)/shard_map/ppermute | solution.py:483
  119.1 37.8 %collective-permute-start.10 = (f32[512,128]{1,0:T(8,128)S(1)}, f32[512,128]{1,0:T(8,128)S(1)}, u32[]{:S(2)}, u32[]{:S(2)}) collective-permute-start(f32[512,128]{1,0:T(8,128)S(1)} %bitcast.19), channel_id=1, source_target_pairs={{0,1},{1,0},{2,3},{3,2},{4,5},{5,4},{6,7},{7,6},{8,9},{9,8},{10,11... | collective-permute-start | bytes 786440 | tf_op jit(solution)/shard_map/ppermute | solution.py:510
  127.3 15.0 %copy-start.8 = (f32[512,128]{1,0:T(8,128)}, f32[512,128]{1,0:T(8,128)S(1)}, u32[]{:S(2)}) copy-start(f32[512,128]{1,0:T(8,128)S(1)} %collective-permute-done.6.refs_1_) | copy-start | bytes 786436
  136.8 5.5 %copy-start.9 = (f32[512,128]{1,0:T(8,128)}, f32[512,128]{1,0:T(8,128)S(1)}, u32[]{:S(2)}) copy-start(f32[512,128]{1,0:T(8,128)S(1)} %collective-permute-done.7.refs_2_) | copy-start | bytes 786436
  142.2 0.7 copy-start.10
  145.3 0.8 copy-start
  148.0 0.8 copy-start.2
  156.9 0.7 copy-start.11

commit v5 on v4

v5 whole, which is shorter than its diff:
```python
import functools

import jax
import jax.numpy as jnp
from jax import lax
from jax.experimental import pallas as pl
from jax.experimental.pallas import tpu as pltpu
from jax.sharding import PartitionSpec as P

ENTRY_CHANNELS = 32
LANES = 128
PACK = LANES // ENTRY_CHANNELS
F32 = jnp.float32
BF16 = jnp.bfloat16
MIB = 1024 * 1024


def halves(values):
    high = values.astype(BF16)
    low = (values - high.astype(F32)).astype(BF16)
    return high, low


def dot(left, right):
    return jnp.dot(left, right, preferred_element_type=F32)


def dot_rows(left, right):
    return lax.dot_general(left, right, (((1,), (1,)), ((), ())), preferred_element_type=F32)


def fold_of(columns):
    return max(1, LANES // columns)


def strided(start, size, stride):
    return pl.ds(start, size, stride=stride)


def folded_weight(weight_ref, step, fold):
    channels = ENTRY_CHANNELS
    return jnp.concatenate(
        [weight_ref[strided(step * fold + part, channels, channels), :] for part in range(fold)], 1
    )


def own_slots(blocks):
    here = lax.axis_index("blk")
    return [lax.bitwise_xor(here, 2 * slot) for slot in range(blocks)]


def peer_slots(blocks):
    here = lax.axis_index("blk") // 2
    return [lax.bitwise_xor(here, slot) for slot in range(blocks)]


def spread_of(cotangent_ref, pair, slots, fold):
    columns = len(slots) * cotangent_ref.shape[2]
    empty = jnp.zeros((columns, cotangent_ref.shape[3]), BF16)
    spread = ([], [])
    for part in range(2):
        rows = jnp.concatenate([cotangent_ref[2 * pair + part, slot] for slot in slots], 0)
        for found, values in zip(spread, halves(rows)):
            for place in range(fold):
                found.append(
                    jnp.concatenate(
                        [values if place == other else empty for other in range(fold)], 1
                    )
                )
    return [jnp.concatenate(found, 0) for found in spread]


def turn_out_kernel(parts, *refs):
    part_refs, (out_ref, total, square, tiles) = refs[:parts], refs[parts:]
    channels = ENTRY_CHANNELS
    rows, features = out_ref.shape
    count = features // LANES
    found = part_refs[0][...]
    for ref in part_refs[1:]:
        found = found + ref[...]
    total[...] = found
    for group in range(rows // PACK):
        stacked = [total[strided(group * PACK + k, channels, rows), :] for k in range(PACK)]
        square[...] = jnp.concatenate(stacked, 0).T
        pieces = [square[strided(part, count, PACK), :] for part in range(PACK)]
        for k in range(PACK):
            lanes = slice(k * channels, (k + 1) * channels)
            tiles[strided(group * PACK + k, count, rows), :] = jnp.concatenate(
                [piece[:, lanes] for piece in pieces], 1
            )
    for tile in range(count):
        out_ref[:, tile * LANES : (tile + 1) * LANES] = tiles[tile * rows : (tile + 1) * rows, :]


def left_sum_kernel(parts_ref, out_ref, total, tiles):
    channels = ENTRY_CHANNELS
    parts, size, width = parts_ref.shape
    rows, features = out_ref.shape
    count = features // LANES
    found = parts_ref[0]
    for part in range(1, parts):
        found = found + parts_ref[part]
    for tile in range(width // LANES):
        total[tile * size : (tile + 1) * size, :] = found[:, tile * LANES : (tile + 1) * LANES]
    for tile in range(width // LANES):
        pieces = [total[strided(tile * size + part, count, PACK), :] for part in range(PACK)]
        for k in range(PACK):
            lanes = slice(k * channels, (k + 1) * channels)
            tiles[strided(tile * PACK + k, count, rows), :] = jnp.concatenate(
                [piece[:, lanes] for piece in pieces], 1
            )
    for tile in range(count):
        out_ref[:, tile * LANES : (tile + 1) * LANES] = tiles[tile * rows : (tile + 1) * rows, :]


def prepare_weight(weight_ref, weight_cat, fold):
    channels = ENTRY_CHANNELS
    for step in range(channels // fold):
        high, low = halves(folded_weight(weight_ref, step, fold))
        weight_cat[step * channels : (step + 1) * channels, :] = jnp.concatenate(
            [high, low, high], 1
        )


def gradient_phase(slots, fold, cotangent_ref, out_ref, weight_cat):
    def step_of(pair, carry):
        high, low = spread_of(cotangent_ref, pair, slots, fold)
        found = dot_rows(weight_cat[...], jnp.concatenate([high, high, low], 1))
        out_ref[pair] = jnp.concatenate(halves(found), 1)
        return carry

    lax.fori_loop(0, out_ref.shape[0], step_of, 0)


def gradient_kernel(blocks, weight_ref, cotangent_ref, out_ref, weight_cat):
    fold = fold_of(blocks * cotangent_ref.shape[2])
    prepare_weight(weight_ref, weight_cat, fold)
    gradient_phase(own_slots(blocks), fold, cotangent_ref, out_ref, weight_cat)


def rows_of_step(refs, step, half, lanes):
    channels = ENTRY_CHANNELS
    rows = pl.ds(pl.multiple_of(step * channels, channels), channels)
    start = 2 * half * lanes
    return jnp.concatenate(
        [
            ref[pair, rows, start + part * lanes : start + (part + 1) * lanes]
            for ref in refs
            for pair in range(ref.shape[0])
            for part in range(2)
        ],
        0,
    )


def both_left(left_refs):
    sequences = left_refs[0].shape[1]
    return jnp.concatenate([ref[...] for ref in left_refs], 0) * (1.0 / sequences)


def right_kernel(
    blocks, weight_ref, cotangent_ref, own_ref, own_left, peer_left, peer_ref, *refs
):
    out_refs, (weight_cat, left_flip) = refs[:blocks], refs[blocks:]
    sequences = own_left.shape[1]
    depth = cotangent_ref.shape[2]
    fold = fold_of(blocks * depth)
    lanes = fold * blocks * depth
    prepare_weight(weight_ref, weight_cat, fold)
    gradient_phase(peer_slots(blocks), fold, cotangent_ref, peer_ref, weight_cat)
    flip_high, flip_low = halves(both_left([own_left, peer_left]).T)
    left_flip[:sequences, :] = flip_high
    left_flip[sequences:, :] = flip_low

    def step_of(step, carry):
        def stacked(half):
            return jnp.concatenate(
                [
                    rows_of_step([own_ref, peer_ref], 2 * step + part, half, lanes)
                    for part in range(2)
                ],
                1,
            )

        first = dot(left_flip[...], stacked(0))
        second = dot(left_flip[:sequences, :], stacked(1))
        found = first[:sequences] + first[sequences:] + second
        for part in range(2):
            turned = found[:, part * lanes : (part + 1) * lanes].T
            for place in range(fold):
                for slot in range(blocks):
                    start = (place * blocks + slot) * depth
                    row = pl.multiple_of(((2 * step + part) * fold + place) * depth, depth)
                    out_refs[slot][pl.ds(row, depth), :] = turned[start : start + depth]
        return carry

    lax.fori_loop(0, ENTRY_CHANNELS // (2 * fold), step_of, 0)


def right_rows(right_refs, step, fold, depth):
    return jnp.concatenate(
        [
            ref[pl.ds(pl.multiple_of((step * fold + part) * depth, depth), depth), :]
            for part in range(fold)
            for ref in right_refs
        ],
        0,
    )


def weight_kernel(blocks, own_left, peer_left, own_cotangent, peer_cotangent, *refs):
    right_refs, refs = refs[:blocks], refs[blocks + 1 :]
    keep_ref, send_ref, own_out, peer_out, own_ref, peer_ref, total, semaphores = refs
    channels = ENTRY_CHANNELS
    depth, pairs = own_cotangent.shape[2:]
    fold = fold_of(blocks * depth)
    lanes = fold * blocks * depth
    high, low = halves(both_left([own_left, peer_left]))
    left_cat = jnp.concatenate([high, low, high], 1)

    def copies(step):
        size = 2 * channels
        rows = pl.ds(pl.multiple_of(step * size, size), size)
        return [
            pltpu.make_async_copy(ref.at[:, rows], out.at[:, rows], semaphores.at[step, side])
            for side, (ref, out) in enumerate(((own_ref, own_out), (peer_ref, peer_out)))
        ]

    def outer_step(step, carry):
        right = [right_rows(right_refs, 2 * step + part, fold, depth) for part in range(2)]
        high, low = halves(jnp.concatenate(right, 0))
        found = dot_rows(left_cat, jnp.concatenate([high, high, low], 1))
        both = halves(found)
        for part in range(2):
            start = pl.multiple_of((2 * step + part) * channels, channels)
            row = 0
            for ref in (own_ref, peer_ref):
                for index in range(2 * ref.shape[0]):
                    for half in range(2):
                        lane = (2 * half + index % 2) * lanes
                        ref[index // 2, pl.ds(start, channels), lane : lane + lanes] = both[half][
                            row : row + channels, part * lanes : (part + 1) * lanes
                        ]
                    row += channels
        for copy in copies(step):
            copy.start()
        return carry

    lax.fori_loop(0, channels // (2 * fold), outer_step, 0)
    total[...] = jnp.zeros_like(total)

    def weight_step(pair, carry):
        found = None
        for ref, cotangent_ref, slots in (
            (own_ref, own_cotangent, own_slots(blocks)),
            (peer_ref, peer_cotangent, peer_slots(blocks)),
        ):
            high, low = spread_of(cotangent_ref, pair, slots, fold)
            left = ref[pair]
            left = jnp.concatenate([left, left[:, : 2 * lanes]], 1)
            term = dot(left, jnp.concatenate([high, high, low], 0))
            found = term if found is None else found + term
        total[...] += found
        return carry

    lax.fori_loop(0, own_ref.shape[0], weight_step, 0)
    core = lax.rem(lax.axis_index("inner"), 2)
    steps = channels // (2 * fold)
    for out_ref, half in ((keep_ref, core), (send_ref, 1 - core)):
        for step in range(steps):
            start = pl.multiple_of((half * steps + step) * channels, channels)
            found = total[pl.ds(start, channels), :]
            for part in range(fold):
                y = step * fold + part
                out_ref[y * channels : (y + 1) * channels, :] = found[
                    :, part * pairs : (part + 1) * pairs
                ]

    def finish(step, carry):
        for copy in copies(step):
            copy.wait()
        return carry

    lax.fori_loop(0, channels // (2 * fold), finish, 0)


def left_kernel(blocks, depth, own_ref, peer_ref, *refs):
    right_refs = refs[:blocks]
    out_ref, total, flipped = refs[blocks:]
    lanes = own_ref.shape[2] // 4
    fold = lanes // (blocks * depth)
    sequences = right_refs[0].shape[1]
    group = 4
    total[...] = jnp.zeros_like(total)

    def step_of(step, carry):
        steps = [group * step + part for part in range(group)]
        right = [right_rows(right_refs, at, fold, depth) for at in steps]
        high, low = halves(jnp.concatenate(right, 0))
        grads = [
            jnp.concatenate([rows_of_step([own_ref, peer_ref], at, half, lanes) for at in steps], 1)
            for half in range(2)
        ]
        both = dot(grads[0], jnp.concatenate([high, low], 1))
        total[...] += both[:, :sequences] + both[:, sequences:] + dot(grads[1], high)
        return carry

    lax.fori_loop(0, ENTRY_CHANNELS // (fold * group), step_of, 0)
    flipped[...] = total[...].T * (1.0 / sequences)
    parity = lax.rem(lax.axis_index("blk"), 2)
    inner, size, width = out_ref.shape[1:]
    for side, start in ((parity, 0), (1 - parity, width)):
        for part in range(inner):
            out_ref[side, part] = flipped[part * size : (part + 1) * size, start : start + width]


def pair_kernel(final, blocks, outer_hbm, weight_ref, *refs):
    if final:
        other_ref, out_ref, outer_ref, weight_flip, weight_rows, semaphores = refs
    else:
        out_ref, outer_ref, weight_flip, weight_rows, semaphores = refs
    channels = ENTRY_CHANNELS
    depth, pairs = out_ref.shape[2:]
    count = outer_ref.shape[0]
    lanes = outer_ref.shape[2] // 4
    columns = blocks * depth
    fold = lanes // columns
    wide = fold * pairs

    def copy_of(pair):
        return pltpu.make_async_copy(outer_hbm.at[pair], outer_ref.at[pair], semaphores.at[pair])

    for pair in range(count):
        copy_of(pair).start()
    for step in range(channels // fold):
        weight_rows[step * channels : (step + 1) * channels, :] = folded_weight(
            weight_ref, step, fold
        )
    flip_high, flip_low = halves(weight_rows[...].T)
    weight_flip[:wide, :] = flip_high
    weight_flip[wide:, :] = flip_low
    slots = own_slots(blocks) if final else peer_slots(blocks)

    def step_of(pair, carry):
        copy_of(pair).wait()
        first = dot(weight_flip[...], outer_ref[pair, :, : 2 * lanes])
        second = dot(weight_flip[:wide, :], outer_ref[pair, :, 2 * lanes :])
        found = first[:wide] + first[wide:] + second
        for part in range(2):
            turned = []
            for place in range(fold):
                start = part * lanes
                piece = found[place * pairs : (place + 1) * pairs, start : start + lanes].T
                turned.append(piece[place * columns : (place + 1) * columns])
            turned = functools.reduce(jnp.add, turned)
            row = 2 * pair + part
            for slot in range(blocks):
                out_ref[row, slots[slot]] = turned[slot * depth : (slot + 1) * depth]
                if final:
                    other = 2 * slot + 1 - lax.rem(lax.axis_index("blk"), 2)
                    out_ref[row, other] = other_ref[row, slot]
        return carry

    lax.fori_loop(0, count, step_of, 0)


def spread_sum_kernel(in_ref, out_ref):
    found = in_ref[0]
    for part in range(1, in_ref.shape[0]):
        found = found + in_ref[part]
    for part in range(in_ref.shape[0]):
        out_ref[part] = found


def place_kernel(mine_ref, other_ref, out_ref):
    channels = ENTRY_CHANNELS
    core = lax.rem(lax.axis_index("inner"), 2)
    steps = mine_ref.shape[0] // channels
    for ref, half in ((mine_ref, core), (other_ref, 1 - core)):
        for step in range(steps):
            rows = ref[step * channels : (step + 1) * channels, :]
            out_ref[strided(half * steps + step, channels, channels), :] = rows


def shape(*sizes, kind=F32):
    return jax.ShapeDtypeStruct(sizes, kind)


def call(kernel, out_shape, scratch=(), cost=0, name=None, limit=16 * MIB, **specs):
    return pl.pallas_call(
        kernel,
        out_shape=out_shape,
        scratch_shapes=list(scratch),
        compiler_params=pltpu.CompilerParams(vmem_limit_bytes=limit),
        cost_estimate=pl.CostEstimate(flops=int(cost), bytes_accessed=2 * MIB, transcendentals=0),
        name=name,
        **specs,
    )


def local(alignment_left, alignment_right, projection_matrix, cotangent):
    rows, features = alignment_left.shape
    depth = alignment_right.shape[0]
    count = lax.axis_size("blk")
    inner = lax.axis_size("inner")
    channels = ENTRY_CHANNELS
    sequences = features // channels
    outer, pairs = projection_matrix.shape
    blocks = count // 2
    fold = fold_of(blocks * depth)
    lanes = fold * blocks * depth
    tall = outer // fold
    steps = channels // fold
    row_pairs = rows // 2
    flops = 2 * rows * 2 * blocks * depth * outer * pairs * 3
    everyone = ("blk", "inner")

    partner = [(here, here ^ 1) for here in range(count)]
    slot_moves = [[(here, here ^ (2 * slot)) for here in range(count)] for slot in range(blocks)]
    cores = [(here, here ^ 1) for here in range(inner)]
    row_groups = [
        [(2 * step + side) * inner + part for side in range(2) for part in range(inner)]
        for step in range(blocks)
    ]
    core_groups = [list(range(core, count * inner, 2)) for core in range(2)]

    limit = 20 * MIB * max(1, blocks * depth * fold // LANES * 2 // fold)
    large = functools.partial(call, limit=limit)

    right = alignment_right.reshape(depth, sequences, channels).transpose(2, 0, 1)
    right = right.reshape(channels * depth, sequences)
    rights = [right]
    for slot in range(1, blocks):
        rights.append(lax.ppermute(right, "blk", slot_moves[slot]))

    cotangent, alignment_left, _ = lax.optimization_barrier((cotangent, alignment_left, right))
    by_side = cotangent.reshape(rows, blocks, 2, depth, pairs)
    parity = lax.rem(lax.axis_index("blk"), 2)
    cotangent_peer = lax.ppermute(
        jnp.where(parity == 0, by_side[:, :, 1], by_side[:, :, 0]), "blk", partner
    )
    left = alignment_left.reshape(rows, sequences, channels).transpose(0, 2, 1)
    left = left.reshape(rows * channels, sequences)
    left_peer = lax.ppermute(left, "blk", partner)

    factor = shape(row_pairs, tall, 4 * lanes, kind=BF16)
    factor_scratch = pltpu.VMEM(factor.shape, BF16)
    weight_scratch = pltpu.VMEM((tall, 3 * fold * pairs), BF16)
    grad_own = large(
        functools.partial(gradient_kernel, blocks), factor, [weight_scratch], flops, "gradient_own"
    )(projection_matrix, cotangent)
    grad_peer, *right_parts = large(
        functools.partial(right_kernel, blocks),
        [factor] + [shape(channels * depth, sequences)] * blocks,
        [weight_scratch, pltpu.VMEM((2 * sequences, 2 * rows * channels), BF16)],
        2 * flops,
        "right_parts",
    )(projection_matrix, cotangent_peer, grad_own, left, left_peer)

    vmem = pl.BlockSpec(memory_space=pltpu.VMEM)
    hbm = pl.BlockSpec(memory_space=pl.ANY)
    keep, send, outer_own, outer_peer = large(
        functools.partial(weight_kernel, blocks),
        [shape(outer // 2, pairs)] * 2 + [factor] * 2,
        [
            factor_scratch,
            factor_scratch,
            pltpu.VMEM((tall, fold * pairs), F32),
            pltpu.SemaphoreType.DMA((steps // 2, 2)),
        ],
        2 * flops,
        "weight",
        in_specs=[vmem] * (4 + blocks) + [hbm],
        out_specs=[vmem, vmem, hbm, hbm],
    )(left, left_peer, cotangent, cotangent_peer, *rights, right_parts[0])
    sent = lax.ppermute(send, "inner", cores)

    left_parts = large(
        functools.partial(left_kernel, blocks, depth),
        shape(2, inner, sequences // inner, rows * channels),
        [
            pltpu.VMEM((2 * rows * channels, sequences), F32),
            pltpu.VMEM((sequences, 2 * rows * channels), F32),
        ],
        flops,
        "left_parts",
    )(grad_own, grad_peer, *rights)

    keep, left_parts = lax.optimization_barrier((keep, left_parts))
    members = count * inner // 2
    pieces = (keep + sent).reshape(members, outer // 2 // members, pairs)
    pieces, left_parts, outer_own, outer_peer, *right_parts = lax.optimization_barrier(
        (pieces, left_parts, outer_own, outer_peer, *right_parts)
    )
    pieces = lax.all_to_all(pieces, everyone, 0, 0, axis_index_groups=core_groups)
    pieces = call(spread_sum_kernel, shape(*pieces.shape), name="weight_sum")(pieces)
    pieces = lax.all_to_all(pieces, everyone, 0, 0, axis_index_groups=core_groups)
    mine = pieces.reshape(outer // 2, pairs)
    other = lax.ppermute(mine, "inner", cores)
    grad_weight = call(place_kernel, shape(outer, pairs), name="place")(mine, other)

    right_found = [right_parts[0]]
    for slot in range(1, blocks):
        right_found.append(lax.ppermute(right_parts[slot], "blk", slot_moves[slot]))

    def pair(values, others, name):
        final = bool(others)
        return large(
            functools.partial(pair_kernel, final, blocks),
            shape(rows, count if final else blocks, depth, pairs),
            [
                factor_scratch,
                pltpu.VMEM((2 * fold * pairs, tall), BF16),
                pltpu.VMEM((tall, fold * pairs), F32),
                pltpu.SemaphoreType.DMA((row_pairs,)),
            ],
            flops,
            name,
            in_specs=[hbm] + [vmem] * (1 + len(others)),
        )(values, projection_matrix, *others)

    pair_peer = lax.ppermute(pair(outer_peer, [], "pair_peer"), "blk", partner)

    left_parts = left_parts.reshape(2 * inner, sequences // inner, rows * channels)
    left_parts = lax.all_to_all(left_parts, everyone, 0, 0, axis_index_groups=row_groups)
    size = sequences // inner
    grad_left = call(
        left_sum_kernel,
        shape(rows, features // inner),
        [
            pltpu.VMEM((size * rows * channels // LANES, LANES), F32),
            pltpu.VMEM((rows * features // inner // LANES, LANES), F32),
        ],
        name="left_sum",
    )(left_parts)

    grad_right = call(
        functools.partial(turn_out_kernel, blocks),
        shape(depth, features),
        [
            pltpu.VMEM((channels * depth, sequences), F32),
            pltpu.VMEM((LANES, LANES), F32),
            pltpu.VMEM((depth * features // LANES, LANES), F32),
        ],
        name="turn_right_sum",
    )(*right_found)

    pair_update = pair(outer_own, [pair_peer], "pair_own")
    return (pair_update, grad_left, grad_right, grad_weight)


def solution(mesh):
    placed = (
        P(("groups", "blk"), None),
        P(("groups", "blk", "inner"), None),
        P(),
        P(("groups", "blk"), None, "inner", None),
    )
    return jax.shard_map(
        local,
        mesh=mesh,
        in_specs=placed,
        out_specs=(
            P(("groups", "blk"), None, "inner", None),
            P(("groups", "blk"), "inner"),
            P(("groups", "blk", "inner"), None),
            P("groups", None),
        ),
        check_vma=False,
    )
```

time: 161 us -> 124 us (0.77)
  Pallas kernels: 70.9 us -> 39 us
  waiting for transfers between devices: 44.6 us -> 30.7 us
  local copies, waits for them, and re-layouts: 4.56 us -> 13.8 us
    pallas_call x9 -> x6, Pallas kernels: 62.8 us -> 35.1 us  [the longest x1 9.9 us: local(): large(functools.partial(weight_kernel, blocks), [shape(outer // 2, pairs)...]
    ppermute x3, waiting for transfers between devices: 10.8 us -> 2.01 us  [local(): rights.append(lax.ppermute(right, 'blk', slot_moves[slot]))]
    unnamed x24 -> x12, local copies, waits for them, and re-layouts: 4.56 us -> 8.32 us
    reshape x0 -> x2, local copies, waits for them, and re-layouts: none -> 3.67 us  [the longest x1 2.27 us: local(): left = alignment_left.reshape(rows, sequences, channels).transpose(0, 2, 1)]
    ppermute x1, waiting for transfers between devices: 8.91 us -> 5.78 us  [local(): left_peer = lax.ppermute(left, 'blk', partner)]
    transpose x0 -> x2, local copies, waits for them, and re-layouts: none -> 1.86 us  [the longest x1 1.53 us: local(): left = alignment_left.reshape(rows, sequences, channels).transpose(0, 2, 1)]
    ppermute x1, waiting for transfers between devices: 1.73 us -> 0.01 us  [local(): sent = lax.ppermute(send, 'inner', cores)]
  transfers between devices with their start and end apart: 13 -> 13, of which waited for: 7 -> 5; matrix products, arithmetic and copies ran while one was open for 0% -> 3% of each run, Pallas kernels for 35% -> 22%
where the time goes in v5:
time: 124 us; the launch traced here: 123 us
  Pallas kernels  39 us (31%)
  waiting for transfers between devices  30.7 us (25%)
  starting transfers between devices  21.1 us (17%)
  blocking collectives  16.6 us (13%)
  local copies, waits for them, and re-layouts  13.8 us (11%)
  other arithmetic  1.32 us (1%)
    ppermute x3, waiting for transfers between devices, local(): right_found.append(lax.ppermute(right_parts[slot], 'blk', slot_moves[slot]))  22.9 us
    all_to_all x1, blocking collectives, local(): lax.all_to_all(pieces, everyone, 0, 0, axis_index_groups=core_groups)  16.6 us
    pallas_call x1, Pallas kernels, local(): large(functools.partial(weight_kernel, blocks), [shape(outer // 2, pairs)...  9.9 us
    pallas_call x2, Pallas kernels, pair(): large(functools.partial(pair_kernel, final, blocks), shape(rows, count if...  9.76 us
    unnamed x12, local copies, waits for them, and re-layouts  8.32 us
    pallas_call x1, Pallas kernels, local(): large(functools.partial(right_kernel, blocks), [factor] + [shape(channels...  8.02 us
    ppermute x1, waiting for transfers between devices, local(): left_peer = lax.ppermute(left, 'blk', partner)  5.78 us
    all_to_all x1, starting transfers between devices, local(): lax.all_to_all(pieces, everyone, 0, 0, axis_index_groups=core_groups)  5.29 us
  transfers between devices with their start and end apart: 13, of which 5 were waited for; matrix products, arithmetic and copies ran while one was open for 3% of the time, Pallas kernels for 22%

profile of v5, /device:TPU:10, one launch (start us, length us, event | category | flops | bytes accessed | tf_op | source)
XLA Modules:
  0.0 123.3 jit_solution(10614977577888658872)
XLA Ops:
  0.6 0.0 copy-start.2
  0.6 0.0 copy-start.3
  0.7 1.4 %reshape.34 = f32[16,128,32]{2,1,0:T(8,128)S(1)} reshape(f32[16,4096]{1,0:T(8,128)} %param.5) | data formatting | bytes 524288 | tf_op jit(solution)/shard_map/reshape | solution.py:430
  2.1 0.3 copy.10
  2.4 1.3 %fusion.1 = f32[16,4,16,128]{3,2,1,0:T(8,128)S(1)} fusion(f32[16,4,2,16,128]{4,3,2,1,0:T(8,128)} %bitcast.25, pred[]{:T(512)S(6)} %eq.3), kind=kLoop, calls=%fused_computation.2 | loop fusion | flops 131072 | bytes 1572865 | tf_op jit(solution)/shard_map/jit(_where)/select_n | solution.py:440
  3.7 1.6 %collective-permute-start.1 = (f32[16,4,16,128]{3,2,1,0:T(8,128)S(1)}, f32[16,4,16,128]{3,2,1,0:T(8,128)S(1)}, u32[]{:S(2)}, u32[]{:S(2)}) collective-permute-start(f32[16,4,16,128]{3,2,1,0:T(8,128)S(1)} %fusion.1), channel_id=1, source_target_pairs={{0,4},{4,0},{8,12},{12,8},{16,20},{20,16},{24,28},{28,24},{1,5},{5... | collective-permute-start | bytes 1572872 | tf_op jit(solution)/shard_map/ppermute | solution.py:439
  5.3 2.3 %reshape.36 = f32[16,128,32]{2,1,0:T(8,128)} reshape(f32[16,4096]{1,0:T(8,128)} %param.4) | data formatting | bytes 524288 | tf_op jit(solution)/shard_map/reshape | solution.py:442
  7.6 1.5 %copy.11 = f32[16,32,128]{2,1,0:T(8,128)S(1)} copy(f32[16,32,128]{1,2,0:T(8,128)} %bitcast.32) | data formatting | bytes 524288 | tf_op jit(solution)/shard_map/transpose | solution.py:442
  9.1 0.6 collective-permute-start
  9.6 1.6 %collective-permute-start.4 = (f32[512,128]{1,0:T(8,128)S(1)}, f32[512,128]{1,0:T(8,128)S(1)}, u32[]{:S(2)}, u32[]{:S(2)}) collective-permute-start(f32[512,128]{1,0:T(8,128)S(1)} %bitcast.20), channel_id=1, source_target_pairs={{0,24},{4,28},{8,16},{12,20},{16,8},{20,12},{24,0},{28,4},{1,25},{... | collective-permute-start | bytes 786440 | tf_op jit(solution)/shard_map/ppermute | solution.py:434
  11.2 1.2 %collective-permute-start.3 = (f32[512,128]{1,0:T(8,128)S(1)}, f32[512,128]{1,0:T(8,128)S(1)}, u32[]{:S(2)}, u32[]{:S(2)}) collective-permute-start(f32[512,128]{1,0:T(8,128)S(1)} %bitcast.21), channel_id=1, source_target_pairs={{0,16},{4,20},{8,24},{12,28},{16,0},{20,4},{24,8},{28,12},{1,17},{... | collective-permute-start | bytes 786440 | tf_op jit(solution)/shard_map/ppermute | solution.py:434
  12.5 1.2 %collective-permute-start.2 = (f32[512,128]{1,0:T(8,128)S(1)}, f32[512,128]{1,0:T(8,128)S(1)}, u32[]{:S(2)}, u32[]{:S(2)}) collective-permute-start(f32[512,128]{1,0:T(8,128)S(1)} %bitcast.22), channel_id=1, source_target_pairs={{0,8},{4,12},{8,0},{12,4},{16,24},{20,28},{24,16},{28,20},{1,9},{5... | collective-permute-start | bytes 786440 | tf_op jit(solution)/shard_map/ppermute | solution.py:434
  13.7 0.0 copy-done.2
  13.7 0.0 copy-done.3
  13.7 3.6 %gradient_own.1.own_ref = bf16[8,512,512]{2,1,0:T(8,128)(2,1)S(1)} custom-call(f32[1024,128]{1,0:T(8,128)S(1)} %copy-done.3, f32[16,8,16,128]{3,2,1,0:T(8,128)S(1)} %copy-done.2), custom_call_target="tpu_custom_call" | custom-call | flops 1610612736 | bytes 2097152 | tf_op jit(solution)/shard_map/gradient_own/pallas_call | solution.py:449
  17.3 5.8 %collective-permute-done.peer_left = f32[512,128]{1,0:T(8,128)S(1)} collective-permute-done((f32[512,128]{1,0:T(8,128)S(1)}, f32[512,128]{1,0:T(8,128)S(1)}, u32[]{:S(2)}, u32[]{:S(2)}) %collective-permute-start) | collective-permute-done | bytes 262176 | tf_op jit(solution)/shard_map/ppermute | solution.py:444
  23.1 0.0 collective-permute-done.1.cotangent_ref.peer_cotangent
  23.1 8.0 %right_parts.1 = (bf16[8,512,512]{2,1,0:T(8,128)(2,1)S(1)}, f32[512,128]{1,0:T(8,128)S(1)}, f32[512,128]{1,0:T(8,128)}, f32[512,128]{1,0:T(8,128)S(1)}, f32[512,128]{1,0:T(8,128)S(1)}) custom-call(f32[1024,128]{1,0:T(8,128)S(1)} %copy-done.3, f32[16,4,16,128]{3,2,1,0:T(8,128)S(1)} %collective-permute-done.1.cotangent_ref.peer_cotangent, ...), custom_call_target="tpu_custom_call" | custom-call | flops 3221225472 | bytes 2097152 | tf_op jit(solution)/shard_map/right_parts/pallas_call | solution.py:452
  31.1 0.0 collective-permute-done.4.refs_3_
  31.1 2.0 %collective-permute-done.3.refs_2_ = f32[512,128]{1,0:T(8,128)S(1)} collective-permute-done((f32[512,128]{1,0:T(8,128)S(1)}, f32[512,128]{1,0:T(8,128)S(1)}, u32[]{:S(2)}, u32[]{:S(2)}) %collective-permute-start.3) | collective-permute-done | bytes 262176 | tf_op jit(solution)/shard_map/ppermute | solution.py:434
  33.1 0.0 collective-permute-done.2.refs_1_
  33.1 9.9 %weight.1 = (f32[512,128]{1,0:T(8,128)S(1)}, f32[512,128]{1,0:T(8,128)S(1)}, bf16[8,512,512]{2,1,0:T(8,128)(2,1)S(1)}, bf16[8,512,512]{2,1,0:T(8,128)(2,1)S(1)}) custom-call(f32[512,128]{1,0:T(8,128)S(1)} %bitcast.30, f32[512,128]{1,0:T(8,128)S(1)} %collective-permute-done.peer_left, f32[16,8,16,128]{3,2,1,0:T(8,128)S(1)} %copy-done.2, ...), custom_call_target="tpu_custom_call" | custom-call | flops 3221225472 | bytes 2097152 | tf_op jit(solution)/shard_map/weight/pallas_call | solution.py:462
  43.0 0.0 copy-start
  43.0 1.9 %copy-done = bf16[8,512,512]{2,1,0:T(8,128)(2,1)} copy-done((bf16[8,512,512]{2,1,0:T(8,128)(2,1)}, bf16[8,512,512]{2,1,0:T(8,128)(2,1)S(1)}, u32[]{:S(2)}) %copy-start) | copy-done | bytes 4194328
  44.9 0.0 copy-start.4
  44.9 2.0 %copy-done.4 = bf16[8,512,512]{2,1,0:T(8,128)(2,1)} copy-done((bf16[8,512,512]{2,1,0:T(8,128)(2,1)}, bf16[8,512,512]{2,1,0:T(8,128)(2,1)S(1)}, u32[]{:S(2)}) %copy-start.4) | copy-done | bytes 4194328
  46.9 0.0 collective-permute-start.5
  46.9 3.9 %left_parts.1 = f32[2,4,32,512]{3,2,1,0:T(8,128)} custom-call(bf16[8,512,512]{2,1,0:T(8,128)(2,1)S(1)} %gradient_own.1.own_ref, bf16[8,512,512]{2,1,0:T(8,128)(2,1)S(1)} %get-tuple-element.29.peer_ref, f32[512,128]{1,0:T(8,128)S(1)} %bitcast.24, f32[512,128]{1,0:T(8,128)S(1)} %collective-permute-done.2.refs_1_, ...), custom_call_target="tpu_custom_call" | custom-call | flops 1610612736 | bytes 2097152 | tf_op jit(solution)/shard_map/left_parts/pallas_call | solution.py:478
  50.8 0.0 collective-permute-done.5
  50.9 16.6 %all_to_all.15.in_ref = f32[16,32,128]{2,1,0:T(8,128)S(1)} all-to-all(f32[16,32,128]{2,1,0:T(8,128)S(1)} %bitcast.33), channel_id=1, replica_groups={{0,2,4,6,8,10,12,14,16,18,20,22,24,26,28,30},{1,3,5,7,9,11,13,15,17,19,..., dimensions={0} | all-to-all | bytes 524288 | tf_op jit(solution)/shard_map/all_to_all | solution.py:495
  67.5 0.7 weight_sum.1
  68.2 5.3 %all-to-all-start.2 = ((f32[16,32,128]{2,1,0:T(8,128)}), f32[16,32,128]{2,1,0:T(8,128)S(1)}, u32[]{:S(2)}, u32[]{:S(2)}) async-start(f32[16,32,128]{2,1,0:T(8,128)} %weight_sum.1), calls=%async_computation.2 | async-start | bytes 524288 | tf_op jit(solution)/shard_map/all_to_all | solution.py:497
  73.5 0.0 copy-start.5
  73.5 2.2 %copy-done.5 = bf16[8,512,512]{2,1,0:T(8,128)(2,1)S(1)} copy-done((bf16[8,512,512]{2,1,0:T(8,128)(2,1)S(1)}, bf16[8,512,512]{2,1,0:T(8,128)(2,1)}, u32[]{:S(2)}) %copy-start.5) | copy-done | bytes 4194328
  75.7 4.4 %pair_peer.1 = f32[16,4,16,128]{3,2,1,0:T(8,128)S(1)} custom-call(bf16[8,512,512]{2,1,0:T(8,128)(2,1)S(1)} %copy-done.5, f32[1024,128]{1,0:T(8,128)S(1)} %copy-done.3), custom_call_target="tpu_custom_call" | custom-call | flops 1610612736 | bytes 2097152 | tf_op jit(solution)/shard_map/pair_peer/pallas_call | solution.py:508
  80.1 1.5 %collective-permute-start.6 = (f32[16,4,16,128]{3,2,1,0:T(8,128)S(1)}, f32[16,4,16,128]{3,2,1,0:T(8,128)S(1)}, u32[]{:S(2)}, u32[]{:S(2)}) collective-permute-start(f32[16,4,16,128]{3,2,1,0:T(8,128)S(1)} %pair_peer.1), channel_id=1, source_target_pairs={{0,4},{4,0},{8,12},{12,8},{16,20},{20,16},{24,28},{28,24},{1,5},{5... | collective-permute-start | bytes 1572872 | tf_op jit(solution)/shard_map/ppermute | solution.py:522
  81.6 0.0 all-to-all-done.2
  81.6 4.6 %all-to-all-start = ((f32[8,32,512]{2,1,0:T(8,128)}), f32[8,32,512]{2,1,0:T(8,128)S(1)}, u32[]{:S(2)}, u32[]{:S(2)}) async-start(f32[8,32,512]{2,1,0:T(8,128)} %bitcast.7), calls=%async_computation | async-start | bytes 1048576 | tf_op jit(solution)/shard_map/all_to_all | solution.py:525
  86.2 0.8 collective-permute-start.7
  87.1 1.4 %collective-permute-start.8 = (f32[512,128]{1,0:T(8,128)S(1)}, f32[512,128]{1,0:T(8,128)S(1)}, u32[]{:S(2)}, u32[]{:S(2)}) collective-permute-start(f32[512,128]{1,0:T(8,128)S(1)} %get-tuple-element.43), channel_id=1, source_target_pairs={{0,16},{4,20},{8,24},{12,28},{16,0},{20,4},{24,8},{28,12},{1,17},{... | collective-permute-start | bytes 786440 | tf_op jit(solution)/shard_map/ppermute | solution.py:504
  88.5 1.2 collective-permute-start.9
  89.7 0.0 collective-permute-start.10
  89.7 8.3 %collective-permute-done.7.refs_1_ = f32[512,128]{1,0:T(8,128)S(1)} collective-permute-done((f32[512,128]{1,0:T(8,128)}, f32[512,128]{1,0:T(8,128)S(1)}, u32[]{:S(2)}, u32[]{:S(2)}) %collective-permute-start.7) | collective-permute-done | bytes 262176 | tf_op jit(solution)/shard_map/ppermute | solution.py:504
  98.0 8.4 %collective-permute-done.8.refs_2_ = f32[512,128]{1,0:T(8,128)S(1)} collective-permute-done((f32[512,128]{1,0:T(8,128)S(1)}, f32[512,128]{1,0:T(8,128)S(1)}, u32[]{:S(2)}, u32[]{:S(2)}) %collective-permute-start.8) | collective-permute-done | bytes 262176 | tf_op jit(solution)/shard_map/ppermute | solution.py:504
  106.5 6.2 %collective-permute-done.9.refs_3_ = f32[512,128]{1,0:T(8,128)S(1)} collective-permute-done((f32[512,128]{1,0:T(8,128)S(1)}, f32[512,128]{1,0:T(8,128)S(1)}, u32[]{:S(2)}, u32[]{:S(2)}) %collective-permute-start.9) | collective-permute-done | bytes 262176 | tf_op jit(solution)/shard_map/ppermute | solution.py:504
  112.7 1.2 turn_right_sum.1
  113.9 0.0 all-to-all-done.parts_ref
  113.9 0.8 left_sum.1
  114.7 0.0 collective-permute-done.6.refs_0_
  114.7 0.0 copy-start.1
  114.7 2.2 %copy-done.1 = bf16[8,512,512]{2,1,0:T(8,128)(2,1)S(1)} copy-done((bf16[8,512,512]{2,1,0:T(8,128)(2,1)S(1)}, bf16[8,512,512]{2,1,0:T(8,128)(2,1)}, u32[]{:S(2)}) %copy-start.1) | copy-done | bytes 4194328
  116.8 5.4 %pair_own.1 = f32[16,8,16,128]{3,2,1,0:T(8,128)} custom-call(bf16[8,512,512]{2,1,0:T(8,128)(2,1)S(1)} %copy-done.1, f32[1024,128]{1,0:T(8,128)S(1)} %copy-done.3, f32[16,4,16,128]{3,2,1,0:T(8,128)S(1)} %collective-permute-done.6.refs_0_), custom_call_target="tpu_custom_call" | custom-call | flops 1610612736 | bytes 2097152 | tf_op jit(solution)/shard_map/pair_own/pallas_call | solution.py:508
  122.2 0.0 collective-permute-done.10.other_ref
  122.2 1.1 place.1
  (1 shorter events, 0.0 us)
Async XLA Ops:
  0.6 13.1 %copy-start.2 = (f32[16,8,16,128]{3,2,1,0:T(8,128)S(1)}, f32[16,8,16,128]{3,2,1,0:T(8,128)}, u32[]{:S(2)}) copy-start(f32[16,8,16,128]{3,2,1,0:T(8,128)} %own_cotangent) | copy-start | bytes 3145732
  0.6 13.1 %copy-start.3 = (f32[1024,128]{1,0:T(8,128)S(1)}, f32[1024,128]{1,0:T(8,128)}, u32[]{:S(2)}) copy-start(f32[1024,128]{1,0:T(8,128)} %weight_ref.7) | copy-start | bytes 1572868
  3.7 19.3 %collective-permute-start.1 = (f32[16,4,16,128]{3,2,1,0:T(8,128)S(1)}, f32[16,4,16,128]{3,2,1,0:T(8,128)S(1)}, u32[]{:S(2)}, u32[]{:S(2)}) collective-permute-start(f32[16,4,16,128]{3,2,1,0:T(8,128)S(1)} %fusion.1), channel_id=1, source_target_pairs={{0,4},{4,0},{8,12},{12,8},{16,20},{20,16},{24,28},{28,24},{1,5},{5... | collective-permute-start | bytes 1572872 | tf_op jit(solution)/shard_map/ppermute | solution.py:439
  9.1 14.0 %collective-permute-start = (f32[512,128]{1,0:T(8,128)S(1)}, f32[512,128]{1,0:T(8,128)S(1)}, u32[]{:S(2)}, u32[]{:S(2)}) collective-permute-start(f32[512,128]{1,0:T(8,128)S(1)} %bitcast.28), channel_id=1, source_target_pairs={{0,4},{4,0},{8,12},{12,8},{16,20},{20,16},{24,28},{28,24},{1,5},{5... | collective-permute-start | bytes 786440 | tf_op jit(solution)/shard_map/ppermute | solution.py:444
  9.6 21.4 %collective-permute-start.4 = (f32[512,128]{1,0:T(8,128)S(1)}, f32[512,128]{1,0:T(8,128)S(1)}, u32[]{:S(2)}, u32[]{:S(2)}) collective-permute-start(f32[512,128]{1,0:T(8,128)S(1)} %bitcast.20), channel_id=1, source_target_pairs={{0,24},{4,28},{8,16},{12,20},{16,8},{20,12},{24,0},{28,4},{1,25},{... | collective-permute-start | bytes 786440 | tf_op jit(solution)/shard_map/ppermute | solution.py:434
  11.2 21.9 %collective-permute-start.3 = (f32[512,128]{1,0:T(8,128)S(1)}, f32[512,128]{1,0:T(8,128)S(1)}, u32[]{:S(2)}, u32[]{:S(2)}) collective-permute-start(f32[512,128]{1,0:T(8,128)S(1)} %bitcast.21), channel_id=1, source_target_pairs={{0,16},{4,20},{8,24},{12,28},{16,0},{20,4},{24,8},{28,12},{1,17},{... | collective-permute-start | bytes 786440 | tf_op jit(solution)/shard_map/ppermute | solution.py:434
  12.5 20.6 %collective-permute-start.2 = (f32[512,128]{1,0:T(8,128)S(1)}, f32[512,128]{1,0:T(8,128)S(1)}, u32[]{:S(2)}, u32[]{:S(2)}) collective-permute-start(f32[512,128]{1,0:T(8,128)S(1)} %bitcast.22), channel_id=1, source_target_pairs={{0,8},{4,12},{8,0},{12,4},{16,24},{20,28},{24,16},{28,20},{1,9},{5... | collective-permute-start | bytes 786440 | tf_op jit(solution)/shard_map/ppermute | solution.py:434
  43.0 1.9 %copy-start = (bf16[8,512,512]{2,1,0:T(8,128)(2,1)}, bf16[8,512,512]{2,1,0:T(8,128)(2,1)S(1)}, u32[]{:S(2)}) copy-start(bf16[8,512,512]{2,1,0:T(8,128)(2,1)S(1)} %get-tuple-element.38.outer_hbm) | copy-start | bytes 12582916
  44.9 2.0 %copy-start.4 = (bf16[8,512,512]{2,1,0:T(8,128)(2,1)}, bf16[8,512,512]{2,1,0:T(8,128)(2,1)S(1)}, u32[]{:S(2)}) copy-start(bf16[8,512,512]{2,1,0:T(8,128)(2,1)S(1)} %get-tuple-element.39.outer_hbm) | copy-start | bytes 12582916
  46.9 3.9 %collective-permute-start.5 = (f32[512,128]{1,0:T(8,128)S(1)}, f32[512,128]{1,0:T(8,128)S(1)}, u32[]{:S(2)}, u32[]{:S(2)}) collective-permute-start(f32[512,128]{1,0:T(8,128)S(1)} %get-tuple-element.31), channel_id=1, source_target_pairs={{0,1},{1,0},{2,3},{3,2},{4,5},{5,4},{6,7},{7,6},{8,9},{9,8},{10,11... | collective-permute-start | bytes 786440 | tf_op jit(solution)/shard_map/ppermute | solution.py:476
  68.2 13.4 %all-to-all-start.2 = ((f32[16,32,128]{2,1,0:T(8,128)}), f32[16,32,128]{2,1,0:T(8,128)S(1)}, u32[]{:S(2)}, u32[]{:S(2)}) async-start(f32[16,32,128]{2,1,0:T(8,128)} %weight_sum.1), calls=%async_computation.2 | async-start | bytes 524288 | tf_op jit(solution)/shard_map/all_to_all | solution.py:497
  73.5 2.2 %copy-start.5 = (bf16[8,512,512]{2,1,0:T(8,128)(2,1)S(1)}, bf16[8,512,512]{2,1,0:T(8,128)(2,1)}, u32[]{:S(2)}) copy-start(bf16[8,512,512]{2,1,0:T(8,128)(2,1)} %copy-done.4) | copy-start | bytes 12582916
  80.1 34.6 %collective-permute-start.6 = (f32[16,4,16,128]{3,2,1,0:T(8,128)S(1)}, f32[16,4,16,128]{3,2,1,0:T(8,128)S(1)}, u32[]{:S(2)}, u32[]{:S(2)}) collective-permute-start(f32[16,4,16,128]{3,2,1,0:T(8,128)S(1)} %pair_peer.1), channel_id=1, source_target_pairs={{0,4},{4,0},{8,12},{12,8},{16,20},{20,16},{24,28},{28,24},{1,5},{5... | collective-permute-start | bytes 1572872 | tf_op jit(solution)/shard_map/ppermute | solution.py:522
  81.6 32.3 %all-to-all-start = ((f32[8,32,512]{2,1,0:T(8,128)}), f32[8,32,512]{2,1,0:T(8,128)S(1)}, u32[]{:S(2)}, u32[]{:S(2)}) async-start(f32[8,32,512]{2,1,0:T(8,128)} %bitcast.7), calls=%async_computation | async-start | bytes 1048576 | tf_op jit(solution)/shard_map/all_to_all | solution.py:525
  86.2 11.8 %collective-permute-start.7 = (f32[512,128]{1,0:T(8,128)}, f32[512,128]{1,0:T(8,128)S(1)}, u32[]{:S(2)}, u32[]{:S(2)}) collective-permute-start(f32[512,128]{1,0:T(8,128)} %get-tuple-element.42), channel_id=1, source_target_pairs={{0,8},{4,12},{8,0},{12,4},{16,24},{20,28},{24,16},{28,20},{1,9},{5... | collective-permute-start | bytes 786440 | tf_op jit(solution)/shard_map/ppermute | solution.py:504
  87.1 19.4 %collective-permute-start.8 = (f32[512,128]{1,0:T(8,128)S(1)}, f32[512,128]{1,0:T(8,128)S(1)}, u32[]{:S(2)}, u32[]{:S(2)}) collective-permute-start(f32[512,128]{1,0:T(8,128)S(1)} %get-tuple-element.43), channel_id=1, source_target_pairs={{0,16},{4,20},{8,24},{12,28},{16,0},{20,4},{24,8},{28,12},{1,17},{... | collective-permute-start | bytes 786440 | tf_op jit(solution)/shard_map/ppermute | solution.py:504
  88.5 24.2 %collective-permute-start.9 = (f32[512,128]{1,0:T(8,128)S(1)}, f32[512,128]{1,0:T(8,128)S(1)}, u32[]{:S(2)}, u32[]{:S(2)}) collective-permute-start(f32[512,128]{1,0:T(8,128)S(1)} %get-tuple-element.44), channel_id=1, source_target_pairs={{0,24},{4,28},{8,16},{12,20},{16,8},{20,12},{24,0},{28,4},{1,25},{... | collective-permute-start | bytes 786440 | tf_op jit(solution)/shard_map/ppermute | solution.py:504
  89.7 32.5 %collective-permute-start.10 = (f32[512,128]{1,0:T(8,128)S(1)}, f32[512,128]{1,0:T(8,128)S(1)}, u32[]{:S(2)}, u32[]{:S(2)}) collective-permute-start(f32[512,128]{1,0:T(8,128)S(1)} %bitcast.26), channel_id=1, source_target_pairs={{0,1},{1,0},{2,3},{3,2},{4,5},{5,4},{6,7},{7,6},{8,9},{9,8},{10,11... | collective-permute-start | bytes 786440 | tf_op jit(solution)/shard_map/ppermute | solution.py:499
  114.7 2.2 %copy-start.1 = (bf16[8,512,512]{2,1,0:T(8,128)(2,1)S(1)}, bf16[8,512,512]{2,1,0:T(8,128)(2,1)}, u32[]{:S(2)}) copy-start(bf16[8,512,512]{2,1,0:T(8,128)(2,1)} %copy-done) | copy-start | bytes 12582916

commit v6 on v5

--- a/solution.py
+++ b/solution.py
@@ -209,8 +209,8 @@
 
 
 def weight_kernel(blocks, own_left, peer_left, own_cotangent, peer_cotangent, *refs):
-    right_refs, refs = refs[:blocks], refs[blocks + 1 :]
-    keep_ref, send_ref, own_out, peer_out, own_ref, peer_ref, total, semaphores = refs
+    right_refs = refs[:blocks]
+    keep_ref, send_ref, own_out, peer_out, own_ref, peer_ref, total, semaphores = refs[blocks:]
     channels = ENTRY_CHANNELS
     depth, pairs = own_cotangent.shape[2:]
     fold = fold_of(blocks * depth)
@@ -386,16 +386,29 @@
     return jax.ShapeDtypeStruct(sizes, kind)
 
 
-def call(kernel, out_shape, scratch=(), cost=0, name=None, limit=16 * MIB, **specs):
-    return pl.pallas_call(
-        kernel,
-        out_shape=out_shape,
-        scratch_shapes=list(scratch),
-        compiler_params=pltpu.CompilerParams(vmem_limit_bytes=limit),
-        cost_estimate=pl.CostEstimate(flops=int(cost), bytes_accessed=2 * MIB, transcendentals=0),
-        name=name,
-        **specs,
-    )
+def call(kernel, out_shape, scratch=(), name=None, limit=16 * MIB, far=(), after=(), out_specs=None):
+    def run(*operands):
+        vmem = pl.BlockSpec(memory_space=pltpu.VMEM)
+        hbm = pl.BlockSpec(memory_space=pltpu.HBM)
+        in_specs = [pl.BlockSpec(memory_space=pl.ANY)] * len(after)
+        in_specs += [hbm if at in far else vmem for at in range(len(operands))]
+        operands = [
+            pltpu.with_memory_space_constraint(operand, pltpu.HBM) if at in far else operand
+            for at, operand in enumerate(operands)
+        ]
+        extra = {} if out_specs is None else {"out_specs": out_specs}
+        return pl.pallas_call(
+            lambda *refs: kernel(*refs[len(after) :]),
+            out_shape=out_shape,
+            in_specs=in_specs,
+            scratch_shapes=list(scratch),
+            compiler_params=pltpu.CompilerParams(vmem_limit_bytes=limit),
+            cost_estimate=pl.CostEstimate(flops=1, bytes_accessed=1, transcendentals=0),
+            name=name,
+            **extra,
+        )(*after, *operands)
+
+    return run
 
 
 def local(alignment_left, alignment_right, projection_matrix, cotangent):
@@ -412,7 +425,6 @@
     tall = outer // fold
     steps = channels // fold
     row_pairs = rows // 2
-    flops = 2 * rows * 2 * blocks * depth * outer * pairs * 3
     everyone = ("blk", "inner")
 
     partner = [(here, here ^ 1) for here in range(count)]
@@ -433,7 +445,7 @@
     for slot in range(1, blocks):
         rights.append(lax.ppermute(right, "blk", slot_moves[slot]))
 
-    cotangent, alignment_left, _ = lax.optimization_barrier((cotangent, alignment_left, right))
+    cotangent, _ = lax.optimization_barrier((cotangent, right))
     by_side = cotangent.reshape(rows, blocks, 2, depth, pairs)
     parity = lax.rem(lax.axis_index("blk"), 2)
     cotangent_peer = lax.ppermute(
@@ -447,32 +459,33 @@
     factor_scratch = pltpu.VMEM(factor.shape, BF16)
     weight_scratch = pltpu.VMEM((tall, 3 * fold * pairs), BF16)
     grad_own = large(
-        functools.partial(gradient_kernel, blocks), factor, [weight_scratch], flops, "gradient_own"
+        functools.partial(gradient_kernel, blocks), factor, [weight_scratch], "gradient_own"
     )(projection_matrix, cotangent)
     grad_peer, *right_parts = large(
         functools.partial(right_kernel, blocks),
         [factor] + [shape(channels * depth, sequences)] * blocks,
         [weight_scratch, pltpu.VMEM((2 * sequences, 2 * rows * channels), BF16)],
-        2 * flops,
         "right_parts",
     )(projection_matrix, cotangent_peer, grad_own, left, left_peer)
+    right_found = [right_parts[0]]
+    for slot in range(1, blocks):
+        right_found.append(lax.ppermute(right_parts[slot], "blk", slot_moves[slot]))
 
     vmem = pl.BlockSpec(memory_space=pltpu.VMEM)
-    hbm = pl.BlockSpec(memory_space=pl.ANY)
+    hbm = pl.BlockSpec(memory_space=pltpu.HBM)
     keep, send, outer_own, outer_peer = large(
         functools.partial(weight_kernel, blocks),
-        [shape(outer // 2, pairs)] * 2 + [factor] * 2,
+        [shape(outer // 2, pairs)] * 2 + [pltpu.HBM(factor.shape, BF16)] * 2,
         [
             factor_scratch,
             factor_scratch,
             pltpu.VMEM((tall, fold * pairs), F32),
             pltpu.SemaphoreType.DMA((steps // 2, 2)),
         ],
-        2 * flops,
         "weight",
-        in_specs=[vmem] * (4 + blocks) + [hbm],
+        after=[right_parts[0]],
         out_specs=[vmem, vmem, hbm, hbm],
-    )(left, left_peer, cotangent, cotangent_peer, *rights, right_parts[0])
+    )(left, left_peer, cotangent, cotangent_peer, *rights)
     sent = lax.ppermute(send, "inner", cores)
 
     left_parts = large(
@@ -482,28 +495,16 @@
             pltpu.VMEM((2 * rows * channels, sequences), F32),
             pltpu.VMEM((sequences, 2 * rows * channels), F32),
         ],
-        flops,
         "left_parts",
+        after=[keep],
     )(grad_own, grad_peer, *rights)
 
+    members = count * inner // 2
     keep, left_parts = lax.optimization_barrier((keep, left_parts))
-    members = count * inner // 2
     pieces = (keep + sent).reshape(members, outer // 2 // members, pairs)
-    pieces, left_parts, outer_own, outer_peer, *right_parts = lax.optimization_barrier(
-        (pieces, left_parts, outer_own, outer_peer, *right_parts)
-    )
-    pieces = lax.all_to_all(pieces, everyone, 0, 0, axis_index_groups=core_groups)
-    pieces = call(spread_sum_kernel, shape(*pieces.shape), name="weight_sum")(pieces)
-    pieces = lax.all_to_all(pieces, everyone, 0, 0, axis_index_groups=core_groups)
-    mine = pieces.reshape(outer // 2, pairs)
-    other = lax.ppermute(mine, "inner", cores)
-    grad_weight = call(place_kernel, shape(outer, pairs), name="place")(mine, other)
-
-    right_found = [right_parts[0]]
-    for slot in range(1, blocks):
-        right_found.append(lax.ppermute(right_parts[slot], "blk", slot_moves[slot]))
-
-    def pair(values, others, name):
+    pieces, left_parts = lax.optimization_barrier((pieces, left_parts))
+
+    def pair(values, others, after, name):
         final = bool(others)
         return large(
             functools.partial(pair_kernel, final, blocks),
@@ -514,12 +515,19 @@
                 pltpu.VMEM((tall, fold * pairs), F32),
                 pltpu.SemaphoreType.DMA((row_pairs,)),
             ],
-            flops,
             name,
-            in_specs=[hbm] + [vmem] * (1 + len(others)),
+            far=[0],
+            after=after,
         )(values, projection_matrix, *others)
 
-    pair_peer = lax.ppermute(pair(outer_peer, [], "pair_peer"), "blk", partner)
+    pair_own_rows = pair(outer_peer, [], [pieces, *right_found[1:]], "pair_peer")
+    pair_peer = lax.ppermute(pair_own_rows, "blk", partner)
+
+    pieces = lax.all_to_all(pieces, everyone, 0, 0, axis_index_groups=core_groups)
+    pieces = call(
+        spread_sum_kernel, shape(*pieces.shape), name="weight_sum", after=[pair_own_rows]
+    )(pieces)
+    pieces = lax.all_to_all(pieces, everyone, 0, 0, axis_index_groups=core_groups)
 
     left_parts = left_parts.reshape(2 * inner, sequences // inner, rows * channels)
     left_parts = lax.all_to_all(left_parts, everyone, 0, 0, axis_index_groups=row_groups)
@@ -545,7 +553,14 @@
         name="turn_right_sum",
     )(*right_found)
 
-    pair_update = pair(outer_own, [pair_peer], "pair_own")
+    pair_update = pair(outer_own, [pair_peer], [], "pair_own")
+
+    pieces, pair_update, grad_left, grad_right = lax.optimization_barrier(
+        (pieces, pair_update, grad_left, grad_right)
+    )
+    mine = pieces.reshape(outer // 2, pairs)
+    other = lax.ppermute(mine, "inner", cores)
+    grad_weight = call(place_kernel, shape(outer, pairs), name="place")(mine, other)
     return (pair_update, grad_left, grad_right, grad_weight)
 
 

time: 124 us -> 125 us (level)
  the two profiles are of different devices: /device:TPU:10 before, /device:TPU:11 now
where the time goes in v6:
time: 125 us; the launch traced here: 124 us
  waiting for transfers between devices  40.8 us (33%)
  Pallas kernels  39.9 us (32%)
  starting transfers between devices  23.9 us (19%)
  blocking collectives  12.5 us (10%)
  local copies, waits for them, and re-layouts  5.32 us (4%)
  other arithmetic  1.32 us (1%)
    pallas_call x10, Pallas kernels, run(): pl.pallas_call(lambda *refs: kernel(*refs[len(after):]), out_shape=out_sh...  39.9 us
    ppermute x3, waiting for transfers between devices, local(): right_found.append(lax.ppermute(right_parts[slot], 'blk', slot_moves[slot]))  22.7 us
    all_to_all x1, blocking collectives, local(): lax.all_to_all(pieces, everyone, 0, 0, axis_index_groups=core_groups)  12.5 us
    ppermute x1, waiting for transfers between devices, local(): left_peer = lax.ppermute(left, 'blk', partner)  7.82 us
    all_to_all x1, starting transfers between devices, local(): lax.all_to_all(left_parts, everyone, 0, 0, axis_index_groups=row_groups)  6.8 us
    ppermute x1, waiting for transfers between devices, local(): pair_peer = lax.ppermute(pair_own_rows, 'blk', partner)  6.73 us
    all_to_all x1, starting transfers between devices, local(): lax.all_to_all(pieces, everyone, 0, 0, axis_index_groups=core_groups)  3.66 us
    ppermute x1, starting transfers between devices, local(): other = lax.ppermute(mine, 'inner', cores)  2.8 us
  transfers between devices with their start and end apart: 13, of which 7 were waited for; matrix products, arithmetic and copies ran while one was open for 2% of the time, Pallas kernels for 24%

profile of v6, /device:TPU:11, one launch (start us, length us, event | category | flops | bytes accessed | tf_op | source)
XLA Modules:
  0.0 124.5 jit_solution(16098785978710186884)
XLA Ops:
  0.6 0.0 copy-start
  0.6 0.0 copy-start.5
  0.7 0.0 copy-start.1
  0.7 1.4 %reshape.34 = f32[16,128,32]{2,1,0:T(8,128)S(1)} reshape(f32[16,4096]{1,0:T(8,128)} %param.5) | data formatting | bytes 524288 | tf_op jit(solution)/shard_map/reshape | solution.py:442
  2.1 0.3 copy.10
  2.4 1.3 %fusion.1 = f32[16,4,16,128]{3,2,1,0:T(8,128)S(1)} fusion(f32[16,4,2,16,128]{4,3,2,1,0:T(8,128)} %bitcast.20, pred[]{:T(512)S(6)} %eq.3), kind=kLoop, calls=%fused_computation.2 | loop fusion | flops 131072 | bytes 1572865 | tf_op jit(solution)/shard_map/jit(_where)/select_n | solution.py:452
  3.7 1.3 %collective-permute-start = (f32[16,4,16,128]{3,2,1,0:T(8,128)S(1)}, f32[16,4,16,128]{3,2,1,0:T(8,128)S(1)}, u32[]{:S(2)}, u32[]{:S(2)}) collective-permute-start(f32[16,4,16,128]{3,2,1,0:T(8,128)S(1)} %fusion.1), channel_id=1, source_target_pairs={{0,4},{4,0},{8,12},{12,8},{16,20},{20,16},{24,28},{28,24},{1,5},{5... | collective-permute-start | bytes 1572872 | tf_op jit(solution)/shard_map/ppermute | solution.py:451
  5.0 0.0 copy-done.5
  5.0 1.3 %reshape.37 = f32[16,128,32]{2,1,0:T(8,128)} reshape(f32[16,4096]{1,0:T(8,128)S(1)} %copy-done.5) | data formatting | bytes 524288 | tf_op jit(solution)/shard_map/reshape | solution.py:454
  6.4 1.5 %copy.13 = f32[16,32,128]{2,1,0:T(8,128)S(1)} copy(f32[16,32,128]{1,2,0:T(8,128)} %bitcast.34) | data formatting | bytes 524288 | tf_op jit(solution)/shard_map/transpose | solution.py:454
  7.9 0.3 collective-permute-start.1
  8.2 0.2 collective-permute-start.2
  8.3 2.3 %collective-permute-start.3 = (f32[512,128]{1,0:T(8,128)S(1)}, f32[512,128]{1,0:T(8,128)S(1)}, u32[]{:S(2)}, u32[]{:S(2)}) collective-permute-start(f32[512,128]{1,0:T(8,128)S(1)} %bitcast.24), channel_id=1, source_target_pairs={{0,16},{4,20},{8,24},{12,28},{16,0},{20,4},{24,8},{28,12},{1,17},{... | collective-permute-start | bytes 786440 | tf_op jit(solution)/shard_map/ppermute | solution.py:446
  10.6 0.2 collective-permute-start.4
  10.8 0.0 copy-done
  10.8 0.0 copy-done.1
  10.8 3.6 %gradient_own.1.refs_2_.refs_1_ = bf16[8,512,512]{2,1,0:T(8,128)(2,1)S(1)} custom-call(f32[1024,128]{1,0:T(8,128)S(1)} %copy-done.1, f32[16,8,16,128]{3,2,1,0:T(8,128)S(1)} %copy-done), custom_call_target="tpu_custom_call" | custom-call | flops 1 | bytes 1 | tf_op jit(solution)/shard_map/gradient_own/pallas_call | solution.py:400
  14.4 7.8 %collective-permute-done.1.refs_4_.refs_2_ = f32[512,128]{1,0:T(8,128)S(1)} collective-permute-done((f32[512,128]{1,0:T(8,128)S(1)}, f32[512,128]{1,0:T(8,128)S(1)}, u32[]{:S(2)}, u32[]{:S(2)}) %collective-permute-start.1) | collective-permute-done | bytes 262176 | tf_op jit(solution)/shard_map/ppermute | solution.py:456
  22.2 0.0 collective-permute-done.refs_1_.refs_4_
  22.2 7.3 %right_parts.1 = (bf16[8,512,512]{2,1,0:T(8,128)(2,1)S(1)}, f32[512,128]{1,0:T(8,128)S(1)}, f32[512,128]{1,0:T(8,128)S(1)}, f32[512,128]{1,0:T(8,128)S(1)}, f32[512,128]{1,0:T(8,128)S(1)}) custom-call(f32[1024,128]{1,0:T(8,128)S(1)} %copy-done.1, f32[16,4,16,128]{3,2,1,0:T(8,128)S(1)} %collective-permute-done.refs_1_.refs_4_, ...), custom_call_target="tpu_custom_call" | custom-call | flops 1 | bytes 1 | tf_op jit(solution)/shard_map/right_parts/pallas_call | solution.py:400
  29.5 0.0 copy-start.2
  29.5 0.7 copy-done.2
  30.2 0.0 copy-start.4
  30.2 0.0 collective-permute-done.2.refs_6_.refs_4_
  30.2 0.0 collective-permute-done.3.refs_7_.refs_5_
  30.2 2.4 %collective-permute-done.4.refs_8_.refs_6_ = f32[512,128]{1,0:T(8,128)S(1)} collective-permute-done((f32[512,128]{1,0:T(8,128)S(1)}, f32[512,128]{1,0:T(8,128)S(1)}, u32[]{:S(2)}, u32[]{:S(2)}) %collective-permute-start.4) | collective-permute-done | bytes 262176 | tf_op jit(solution)/shard_map/ppermute | solution.py:446
  32.6 9.3 %weight.1 = (f32[512,128]{1,0:T(8,128)S(1)}, f32[512,128]{1,0:T(8,128)S(1)}, bf16[8,512,512]{2,1,0:T(8,128)(2,1)}, bf16[8,512,512]{2,1,0:T(8,128)(2,1)}) custom-call(f32[512,128]{1,0:T(8,128)S(1)} %get-tuple-element.23.refs_0_, f32[512,128]{1,0:T(8,128)S(1)} %bitcast.30, f32[512,128]{1,0:T(8,128)S(1)} %collective-permute-done.1.refs_4_.refs_2_, ...), custom_call_target="tpu_custom_call" | custom-call | flops 1 | bytes 1 | tf_op jit(solution)/shard_map/weight/pallas_call | solution.py:400
  41.9 2.5 %collective-permute-start.5 = (f32[512,128]{1,0:T(8,128)S(1)}, f32[512,128]{1,0:T(8,128)S(1)}, u32[]{:S(2)}, u32[]{:S(2)}) collective-permute-start(f32[512,128]{1,0:T(8,128)S(1)} %get-tuple-element.27), channel_id=1, source_target_pairs={{0,1},{1,0},{2,3},{3,2},{4,5},{5,4},{6,7},{7,6},{8,9},{9,8},{10,11... | collective-permute-start | bytes 786440 | tf_op jit(solution)/shard_map/ppermute | solution.py:489
  44.4 0.0 copy-start.3
  44.4 3.9 %left_parts.1 = f32[2,4,32,512]{3,2,1,0:T(8,128)} custom-call(f32[512,128]{1,0:T(8,128)S(1)} %get-tuple-element.26.refs_0_, bf16[8,512,512]{2,1,0:T(8,128)(2,1)S(1)} %gradient_own.1.refs_2_.refs_1_, bf16[8,512,512]{2,1,0:T(8,128)(2,1)S(1)} %get-tuple-element.25.refs_2_, f32[512,128]{1,0:T(8,128)S(1)} %bitcast.27, ...), custom_call_target="tpu_custom_call" | custom-call | flops 1 | bytes 1 | tf_op jit(solution)/shard_map/left_parts/pallas_call | solution.py:400
  48.2 0.0 copy-done.4
  48.2 0.0 collective-permute-done.5
  48.3 12.5 %all_to_all.15.refs_1_ = f32[16,32,128]{2,1,0:T(8,128)S(1)} all-to-all(f32[16,32,128]{2,1,0:T(8,128)S(1)} %bitcast.21), channel_id=1, replica_groups={{0,2,4,6,8,10,12,14,16,18,20,22,24,26,28,30},{1,3,5,7,9,11,13,15,17,19,..., dimensions={0} | all-to-all | bytes 524288 | tf_op jit(solution)/shard_map/all_to_all | solution.py:526
  60.8 6.8 %all-to-all-start.2 = ((f32[8,32,512]{2,1,0:T(8,128)}), f32[8,32,512]{2,1,0:T(8,128)S(1)}, u32[]{:S(2)}, u32[]{:S(2)}) async-start(f32[8,32,512]{2,1,0:T(8,128)} %bitcast.7), calls=%async_computation.2 | async-start | bytes 1048576 | tf_op jit(solution)/shard_map/all_to_all | solution.py:533
  67.6 0.7 collective-permute-start.6
  68.2 0.0 copy-done.3
  68.3 0.3 collective-permute-start.7
  68.6 1.7 %collective-permute-start.8 = (f32[512,128]{1,0:T(8,128)S(1)}, f32[512,128]{1,0:T(8,128)S(1)}, u32[]{:S(2)}, u32[]{:S(2)}) collective-permute-start(f32[512,128]{1,0:T(8,128)S(1)} %get-tuple-element.32), channel_id=1, source_target_pairs={{0,24},{4,28},{8,16},{12,20},{16,8},{20,12},{24,0},{28,4},{1,25},{... | collective-permute-start | bytes 786440 | tf_op jit(solution)/shard_map/ppermute | solution.py:472
  70.2 7.8 %collective-permute-done.6.refs_1_ = f32[512,128]{1,0:T(8,128)S(1)} collective-permute-done((f32[512,128]{1,0:T(8,128)}, f32[512,128]{1,0:T(8,128)S(1)}, u32[]{:S(2)}, u32[]{:S(2)}) %collective-permute-start.6) | collective-permute-done | bytes 262176 | tf_op jit(solution)/shard_map/ppermute | solution.py:472
  78.1 2.4 %collective-permute-done.7.refs_2_ = f32[512,128]{1,0:T(8,128)S(1)} collective-permute-done((f32[512,128]{1,0:T(8,128)S(1)}, f32[512,128]{1,0:T(8,128)S(1)}, u32[]{:S(2)}, u32[]{:S(2)}) %collective-permute-start.7) | collective-permute-done | bytes 262176 | tf_op jit(solution)/shard_map/ppermute | solution.py:472
  80.5 12.5 %collective-permute-done.8.refs_3_ = f32[512,128]{1,0:T(8,128)S(1)} collective-permute-done((f32[512,128]{1,0:T(8,128)S(1)}, f32[512,128]{1,0:T(8,128)S(1)}, u32[]{:S(2)}, u32[]{:S(2)}) %collective-permute-start.8) | collective-permute-done | bytes 262176 | tf_op jit(solution)/shard_map/ppermute | solution.py:472
  92.9 5.1 %pair_peer.1.refs_0_ = f32[16,4,16,128]{3,2,1,0:T(8,128)S(1)} custom-call(f32[16,32,128]{2,1,0:T(8,128)S(1)} %bitcast.22, f32[512,128]{1,0:T(8,128)S(1)} %collective-permute-done.6.refs_1_, f32[512,128]{1,0:T(8,128)S(1)} %collective-permute-done.7.refs_2_, f32[512,128]{1,0:T(8,128)S(1)} %collective-permute-done.8.refs_3_, ...), custom_call_target="tpu_custom_call" | custom-call | flops 1 | bytes 1 | tf_op jit(solution)/shard_map/pair_peer/pallas_call | solution.py:400
  98.0 1.3 %collective-permute-start.9 = (f32[16,4,16,128]{3,2,1,0:T(8,128)S(1)}, f32[16,4,16,128]{3,2,1,0:T(8,128)}, u32[]{:S(2)}, u32[]{:S(2)}) collective-permute-start(f32[16,4,16,128]{3,2,1,0:T(8,128)S(1)} %pair_peer.1.refs_0_), channel_id=1, source_target_pairs={{0,4},{4,0},{8,12},{12,8},{16,20},{20,16},{24,28},{28,24},{1,5},{5... | collective-permute-start | bytes 1572872 | tf_op jit(solution)/shard_map/ppermute | solution.py:524
  99.3 0.8 weight_sum.1
  100.1 0.0 all-to-all-done.2.refs_0_
  100.1 3.7 %all-to-all-start.1 = ((f32[16,32,128]{2,1,0:T(8,128)}), f32[16,32,128]{2,1,0:T(8,128)S(1)}, u32[]{:S(2)}, u32[]{:S(2)}) async-start(f32[16,32,128]{2,1,0:T(8,128)} %weight_sum.1), calls=%async_computation.1 | async-start | bytes 524288 | tf_op jit(solution)/shard_map/all_to_all | solution.py:530
  103.7 1.2 turn_right_sum.1
  104.9 0.8 left_sum.1
  105.7 6.7 %collective-permute-done.9.refs_2_ = f32[16,4,16,128]{3,2,1,0:T(8,128)} collective-permute-done((f32[16,4,16,128]{3,2,1,0:T(8,128)S(1)}, f32[16,4,16,128]{3,2,1,0:T(8,128)}, u32[]{:S(2)}, u32[]{:S(2)}) %collective-permute-start.9) | collective-permute-done | bytes 524320 | tf_op jit(solution)/shard_map/ppermute | solution.py:524
  112.4 7.0 %pair_own.1 = f32[16,8,16,128]{3,2,1,0:T(8,128)} custom-call(bf16[8,512,512]{2,1,0:T(8,128)(2,1)} %get-tuple-element.34.refs_0_, f32[1024,128]{1,0:T(8,128)S(1)} %copy-done.1, f32[16,4,16,128]{3,2,1,0:T(8,128)} %collective-permute-done.9.refs_2_), custom_call_target="tpu_custom_call" | custom-call | flops 1 | bytes 1 | tf_op jit(solution)/shard_map/pair_own/pallas_call | solution.py:400
  119.4 0.0 all-to-all-done.1
  119.4 2.8 %collective-permute-start.10 = (f32[512,128]{1,0:T(8,128)S(1)}, f32[512,128]{1,0:T(8,128)S(1)}, u32[]{:S(2)}, u32[]{:S(2)}) collective-permute-start(f32[512,128]{1,0:T(8,128)S(1)} %bitcast.31), channel_id=1, source_target_pairs={{0,1},{1,0},{2,3},{3,2},{4,5},{5,4},{6,7},{7,6},{8,9},{9,8},{10,11... | collective-permute-start | bytes 786440 | tf_op jit(solution)/shard_map/ppermute | solution.py:562
  122.2 1.2 collective-permute-done.10.refs_1_
  123.4 1.1 place.1
  (1 shorter events, 0.0 us)
Async XLA Ops:
  0.6 10.2 %copy-start = (f32[16,8,16,128]{3,2,1,0:T(8,128)S(1)}, f32[16,8,16,128]{3,2,1,0:T(8,128)}, u32[]{:S(2)}) copy-start(f32[16,8,16,128]{3,2,1,0:T(8,128)} %refs_3_) | copy-start | bytes 3145732
  0.6 4.4 %copy-start.5 = (f32[16,4096]{1,0:T(8,128)S(1)}, f32[16,4096]{1,0:T(8,128)}, u32[]{:S(2)}) copy-start(f32[16,4096]{1,0:T(8,128)} %param.4) | copy-start | bytes 786436
  0.7 10.2 %copy-start.1 = (f32[1024,128]{1,0:T(8,128)S(1)}, f32[1024,128]{1,0:T(8,128)}, u32[]{:S(2)}) copy-start(f32[1024,128]{1,0:T(8,128)} %refs_1_.2) | copy-start | bytes 1572868
  3.7 18.5 %collective-permute-start = (f32[16,4,16,128]{3,2,1,0:T(8,128)S(1)}, f32[16,4,16,128]{3,2,1,0:T(8,128)S(1)}, u32[]{:S(2)}, u32[]{:S(2)}) collective-permute-start(f32[16,4,16,128]{3,2,1,0:T(8,128)S(1)} %fusion.1), channel_id=1, source_target_pairs={{0,4},{4,0},{8,12},{12,8},{16,20},{20,16},{24,28},{28,24},{1,5},{5... | collective-permute-start | bytes 1572872 | tf_op jit(solution)/shard_map/ppermute | solution.py:451
  7.9 14.3 %collective-permute-start.1 = (f32[512,128]{1,0:T(8,128)S(1)}, f32[512,128]{1,0:T(8,128)S(1)}, u32[]{:S(2)}, u32[]{:S(2)}) collective-permute-start(f32[512,128]{1,0:T(8,128)S(1)} %bitcast.28), channel_id=1, source_target_pairs={{0,4},{4,0},{8,12},{12,8},{16,20},{20,16},{24,28},{28,24},{1,5},{5... | collective-permute-start | bytes 786440 | tf_op jit(solution)/shard_map/ppermute | solution.py:456
  8.2 22.0 %collective-permute-start.2 = (f32[512,128]{1,0:T(8,128)S(1)}, f32[512,128]{1,0:T(8,128)S(1)}, u32[]{:S(2)}, u32[]{:S(2)}) collective-permute-start(f32[512,128]{1,0:T(8,128)S(1)} %bitcast.23), channel_id=1, source_target_pairs={{0,8},{4,12},{8,0},{12,4},{16,24},{20,28},{24,16},{28,20},{1,9},{5... | collective-permute-start | bytes 786440 | tf_op jit(solution)/shard_map/ppermute | solution.py:446
  8.3 21.9 %collective-permute-start.3 = (f32[512,128]{1,0:T(8,128)S(1)}, f32[512,128]{1,0:T(8,128)S(1)}, u32[]{:S(2)}, u32[]{:S(2)}) collective-permute-start(f32[512,128]{1,0:T(8,128)S(1)} %bitcast.24), channel_id=1, source_target_pairs={{0,16},{4,20},{8,24},{12,28},{16,0},{20,4},{24,8},{28,12},{1,17},{... | collective-permute-start | bytes 786440 | tf_op jit(solution)/shard_map/ppermute | solution.py:446
  10.6 21.9 %collective-permute-start.4 = (f32[512,128]{1,0:T(8,128)S(1)}, f32[512,128]{1,0:T(8,128)S(1)}, u32[]{:S(2)}, u32[]{:S(2)}) collective-permute-start(f32[512,128]{1,0:T(8,128)S(1)} %bitcast.25), channel_id=1, source_target_pairs={{0,24},{4,28},{8,16},{12,20},{16,8},{20,12},{24,0},{28,4},{1,25},{... | collective-permute-start | bytes 786440 | tf_op jit(solution)/shard_map/ppermute | solution.py:446
  29.5 0.7 copy-start.2
  30.2 18.0 %copy-start.4 = (f32[512,128]{1,0:T(8,128)}, f32[512,128]{1,0:T(8,128)S(1)}, u32[]{:S(2)}) copy-start(f32[512,128]{1,0:T(8,128)S(1)} %get-tuple-element.30) | copy-start | bytes 786436
  41.9 6.4 %collective-permute-start.5 = (f32[512,128]{1,0:T(8,128)S(1)}, f32[512,128]{1,0:T(8,128)S(1)}, u32[]{:S(2)}, u32[]{:S(2)}) collective-permute-start(f32[512,128]{1,0:T(8,128)S(1)} %get-tuple-element.27), channel_id=1, source_target_pairs={{0,1},{1,0},{2,3},{3,2},{4,5},{5,4},{6,7},{7,6},{8,9},{9,8},{10,11... | collective-permute-start | bytes 786440 | tf_op jit(solution)/shard_map/ppermute | solution.py:489
  44.4 23.9 %copy-start.3 = (f32[512,128]{1,0:T(8,128)S(1)}, f32[512,128]{1,0:T(8,128)}, u32[]{:S(2)}) copy-start(f32[512,128]{1,0:T(8,128)} %copy-done.2) | copy-start | bytes 786436
  60.8 39.3 %all-to-all-start.2 = ((f32[8,32,512]{2,1,0:T(8,128)}), f32[8,32,512]{2,1,0:T(8,128)S(1)}, u32[]{:S(2)}, u32[]{:S(2)}) async-start(f32[8,32,512]{2,1,0:T(8,128)} %bitcast.7), calls=%async_computation.2 | async-start | bytes 1048576 | tf_op jit(solution)/shard_map/all_to_all | solution.py:533
  67.6 10.5 %collective-permute-start.6 = (f32[512,128]{1,0:T(8,128)}, f32[512,128]{1,0:T(8,128)S(1)}, u32[]{:S(2)}, u32[]{:S(2)}) collective-permute-start(f32[512,128]{1,0:T(8,128)} %copy-done.4), channel_id=1, source_target_pairs={{0,8},{4,12},{8,0},{12,4},{16,24},{20,28},{24,16},{28,20},{1,9},{5... | collective-permute-start | bytes 786440 | tf_op jit(solution)/shard_map/ppermute | solution.py:472
  68.3 12.2 %collective-permute-start.7 = (f32[512,128]{1,0:T(8,128)S(1)}, f32[512,128]{1,0:T(8,128)S(1)}, u32[]{:S(2)}, u32[]{:S(2)}) collective-permute-start(f32[512,128]{1,0:T(8,128)S(1)} %copy-done.3), channel_id=1, source_target_pairs={{0,16},{4,20},{8,24},{12,28},{16,0},{20,4},{24,8},{28,12},{1,17},{... | collective-permute-start | bytes 786440 | tf_op jit(solution)/shard_map/ppermute | solution.py:472
  68.6 24.3 %collective-permute-start.8 = (f32[512,128]{1,0:T(8,128)S(1)}, f32[512,128]{1,0:T(8,128)S(1)}, u32[]{:S(2)}, u32[]{:S(2)}) collective-permute-start(f32[512,128]{1,0:T(8,128)S(1)} %get-tuple-element.32), channel_id=1, source_target_pairs={{0,24},{4,28},{8,16},{12,20},{16,8},{20,12},{24,0},{28,4},{1,25},{... | collective-permute-start | bytes 786440 | tf_op jit(solution)/shard_map/ppermute | solution.py:472
  98.0 14.4 %collective-permute-start.9 = (f32[16,4,16,128]{3,2,1,0:T(8,128)S(1)}, f32[16,4,16,128]{3,2,1,0:T(8,128)}, u32[]{:S(2)}, u32[]{:S(2)}) collective-permute-start(f32[16,4,16,128]{3,2,1,0:T(8,128)S(1)} %pair_peer.1.refs_0_), channel_id=1, source_target_pairs={{0,4},{4,0},{8,12},{12,8},{16,20},{20,16},{24,28},{28,24},{1,5},{5... | collective-permute-start | bytes 1572872 | tf_op jit(solution)/shard_map/ppermute | solution.py:524
  100.1 19.4 %all-to-all-start.1 = ((f32[16,32,128]{2,1,0:T(8,128)}), f32[16,32,128]{2,1,0:T(8,128)S(1)}, u32[]{:S(2)}, u32[]{:S(2)}) async-start(f32[16,32,128]{2,1,0:T(8,128)} %weight_sum.1), calls=%async_computation.1 | async-start | bytes 524288 | tf_op jit(solution)/shard_map/all_to_all | solution.py:530
  119.4 4.0 %collective-permute-start.10 = (f32[512,128]{1,0:T(8,128)S(1)}, f32[512,128]{1,0:T(8,128)S(1)}, u32[]{:S(2)}, u32[]{:S(2)}) collective-permute-start(f32[512,128]{1,0:T(8,128)S(1)} %bitcast.31), channel_id=1, source_target_pairs={{0,1},{1,0},{2,3},{3,2},{4,5},{5,4},{6,7},{7,6},{8,9},{9,8},{10,11... | collective-permute-start | bytes 786440 | tf_op jit(solution)/shard_map/ppermute | solution.py:562

commit v7 on v6

--- a/solution.py
+++ b/solution.py
@@ -45,13 +45,12 @@
 
 
 def own_slots(blocks):
-    here = lax.axis_index("blk")
-    return [lax.bitwise_xor(here, 2 * slot) for slot in range(blocks)]
+    parity = lax.rem(lax.axis_index("blk"), 2)
+    return [2 * block + parity for block in range(blocks)]
 
 
 def peer_slots(blocks):
-    here = lax.axis_index("blk") // 2
-    return [lax.bitwise_xor(here, slot) for slot in range(blocks)]
+    return list(range(blocks))
 
 
 def spread_of(cotangent_ref, pair, slots, fold):
@@ -70,17 +69,12 @@
     return [jnp.concatenate(found, 0) for found in spread]
 
 
-def turn_out_kernel(parts, *refs):
-    part_refs, (out_ref, total, square, tiles) = refs[:parts], refs[parts:]
+def turn_out_kernel(in_ref, out_ref, square, tiles):
     channels = ENTRY_CHANNELS
     rows, features = out_ref.shape
     count = features // LANES
-    found = part_refs[0][...]
-    for ref in part_refs[1:]:
-        found = found + ref[...]
-    total[...] = found
     for group in range(rows // PACK):
-        stacked = [total[strided(group * PACK + k, channels, rows), :] for k in range(PACK)]
+        stacked = [in_ref[strided(group * PACK + k, channels, rows), :] for k in range(PACK)]
         square[...] = jnp.concatenate(stacked, 0).T
         pieces = [square[strided(part, count, PACK), :] for part in range(PACK)]
         for k in range(PACK):
@@ -92,14 +86,12 @@
         out_ref[:, tile * LANES : (tile + 1) * LANES] = tiles[tile * rows : (tile + 1) * rows, :]
 
 
-def left_sum_kernel(parts_ref, out_ref, total, tiles):
-    channels = ENTRY_CHANNELS
-    parts, size, width = parts_ref.shape
+def turn_left_kernel(in_ref, out_ref, total, tiles):
+    channels = ENTRY_CHANNELS
+    size, width = in_ref.shape
     rows, features = out_ref.shape
     count = features // LANES
-    found = parts_ref[0]
-    for part in range(1, parts):
-        found = found + parts_ref[part]
+    found = in_ref[...]
     for tile in range(width // LANES):
         total[tile * size : (tile + 1) * size, :] = found[:, tile * LANES : (tile + 1) * LANES]
     for tile in range(width // LANES):
@@ -161,7 +153,7 @@
 def right_kernel(
     blocks, weight_ref, cotangent_ref, own_ref, own_left, peer_left, peer_ref, *refs
 ):
-    out_refs, (weight_cat, left_flip) = refs[:blocks], refs[blocks:]
+    out_ref, weight_cat, left_flip = refs
     sequences = own_left.shape[1]
     depth = cotangent_ref.shape[2]
     fold = fold_of(blocks * depth)
@@ -191,26 +183,25 @@
                 for slot in range(blocks):
                     start = (place * blocks + slot) * depth
                     row = pl.multiple_of(((2 * step + part) * fold + place) * depth, depth)
-                    out_refs[slot][pl.ds(row, depth), :] = turned[start : start + depth]
+                    out_ref[slot, pl.ds(row, depth), :] = turned[start : start + depth]
         return carry
 
     lax.fori_loop(0, ENTRY_CHANNELS // (2 * fold), step_of, 0)
 
 
-def right_rows(right_refs, step, fold, depth):
+def right_rows(right_ref, step, fold, depth):
     return jnp.concatenate(
         [
-            ref[pl.ds(pl.multiple_of((step * fold + part) * depth, depth), depth), :]
+            right_ref[block, pl.ds(pl.multiple_of((step * fold + part) * depth, depth), depth), :]
             for part in range(fold)
-            for ref in right_refs
+            for block in range(right_ref.shape[0])
         ],
         0,
     )
 
 
 def weight_kernel(blocks, own_left, peer_left, own_cotangent, peer_cotangent, *refs):
-    right_refs = refs[:blocks]
-    keep_ref, send_ref, own_out, peer_out, own_ref, peer_ref, total, semaphores = refs[blocks:]
+    right_ref, keep_ref, send_ref, own_out, peer_out, own_ref, peer_ref, total, semaphores = refs
     channels = ENTRY_CHANNELS
     depth, pairs = own_cotangent.shape[2:]
     fold = fold_of(blocks * depth)
@@ -227,7 +218,7 @@
         ]
 
     def outer_step(step, carry):
-        right = [right_rows(right_refs, 2 * step + part, fold, depth) for part in range(2)]
+        right = [right_rows(right_ref, 2 * step + part, fold, depth) for part in range(2)]
         high, low = halves(jnp.concatenate(right, 0))
         found = dot_rows(left_cat, jnp.concatenate([high, high, low], 1))
         both = halves(found)
@@ -284,18 +275,17 @@
     lax.fori_loop(0, channels // (2 * fold), finish, 0)
 
 
-def left_kernel(blocks, depth, own_ref, peer_ref, *refs):
-    right_refs = refs[:blocks]
-    out_ref, total, flipped = refs[blocks:]
+def left_kernel(own_ref, peer_ref, right_ref, own_out, peer_out, total):
+    blocks, rows, sequences = right_ref.shape
     lanes = own_ref.shape[2] // 4
+    depth = rows // ENTRY_CHANNELS
     fold = lanes // (blocks * depth)
-    sequences = right_refs[0].shape[1]
     group = 4
     total[...] = jnp.zeros_like(total)
 
     def step_of(step, carry):
         steps = [group * step + part for part in range(group)]
-        right = [right_rows(right_refs, at, fold, depth) for at in steps]
+        right = [right_rows(right_ref, at, fold, depth) for at in steps]
         high, low = halves(jnp.concatenate(right, 0))
         grads = [
             jnp.concatenate([rows_of_step([own_ref, peer_ref], at, half, lanes) for at in steps], 1)
@@ -306,12 +296,10 @@
         return carry
 
     lax.fori_loop(0, ENTRY_CHANNELS // (fold * group), step_of, 0)
-    flipped[...] = total[...].T * (1.0 / sequences)
-    parity = lax.rem(lax.axis_index("blk"), 2)
-    inner, size, width = out_ref.shape[1:]
-    for side, start in ((parity, 0), (1 - parity, width)):
-        for part in range(inner):
-            out_ref[side, part] = flipped[part * size : (part + 1) * size, start : start + width]
+    flipped = total[...].T * (1.0 / sequences)
+    width = own_out.shape[1]
+    own_out[...] = flipped[:, :width]
+    peer_out[...] = flipped[:, width:]
 
 
 def pair_kernel(final, blocks, outer_hbm, weight_ref, *refs):
@@ -428,12 +416,8 @@
     everyone = ("blk", "inner")
 
     partner = [(here, here ^ 1) for here in range(count)]
-    slot_moves = [[(here, here ^ (2 * slot)) for here in range(count)] for slot in range(blocks)]
+    same_parity = [[2 * block + side for block in range(blocks)] for side in range(2)]
     cores = [(here, here ^ 1) for here in range(inner)]
-    row_groups = [
-        [(2 * step + side) * inner + part for side in range(2) for part in range(inner)]
-        for step in range(blocks)
-    ]
     core_groups = [list(range(core, count * inner, 2)) for core in range(2)]
 
     limit = 20 * MIB * max(1, blocks * depth * fold // LANES * 2 // fold)
@@ -441,11 +425,8 @@
 
     right = alignment_right.reshape(depth, sequences, channels).transpose(2, 0, 1)
     right = right.reshape(channels * depth, sequences)
-    rights = [right]
-    for slot in range(1, blocks):
-        rights.append(lax.ppermute(right, "blk", slot_moves[slot]))
-
-    cotangent, _ = lax.optimization_barrier((cotangent, right))
+    right = lax.all_gather(right, "blk", axis_index_groups=same_parity)
+
     by_side = cotangent.reshape(rows, blocks, 2, depth, pairs)
     parity = lax.rem(lax.axis_index("blk"), 2)
     cotangent_peer = lax.ppermute(
@@ -461,15 +442,15 @@
     grad_own = large(
         functools.partial(gradient_kernel, blocks), factor, [weight_scratch], "gradient_own"
     )(projection_matrix, cotangent)
-    grad_peer, *right_parts = large(
+    grad_peer, right_parts = large(
         functools.partial(right_kernel, blocks),
-        [factor] + [shape(channels * depth, sequences)] * blocks,
+        [factor, shape(blocks, channels * depth, sequences)],
         [weight_scratch, pltpu.VMEM((2 * sequences, 2 * rows * channels), BF16)],
         "right_parts",
     )(projection_matrix, cotangent_peer, grad_own, left, left_peer)
-    right_found = [right_parts[0]]
-    for slot in range(1, blocks):
-        right_found.append(lax.ppermute(right_parts[slot], "blk", slot_moves[slot]))
+    right_sum = lax.psum_scatter(
+        right_parts, "blk", scatter_dimension=0, axis_index_groups=same_parity
+    )
 
     vmem = pl.BlockSpec(memory_space=pltpu.VMEM)
     hbm = pl.BlockSpec(memory_space=pltpu.HBM)
@@ -483,26 +464,22 @@
             pltpu.SemaphoreType.DMA((steps // 2, 2)),
         ],
         "weight",
-        after=[right_parts[0]],
+        after=[right_parts],
         out_specs=[vmem, vmem, hbm, hbm],
-    )(left, left_peer, cotangent, cotangent_peer, *rights)
+    )(left, left_peer, cotangent, cotangent_peer, right)
     sent = lax.ppermute(send, "inner", cores)
 
-    left_parts = large(
-        functools.partial(left_kernel, blocks, depth),
-        shape(2, inner, sequences // inner, rows * channels),
-        [
-            pltpu.VMEM((2 * rows * channels, sequences), F32),
-            pltpu.VMEM((sequences, 2 * rows * channels), F32),
-        ],
+    left_own, left_other = large(
+        left_kernel,
+        [shape(sequences, rows * channels)] * 2,
+        [pltpu.VMEM((2 * rows * channels, sequences), F32)],
         "left_parts",
         after=[keep],
-    )(grad_own, grad_peer, *rights)
-
+    )(grad_own, grad_peer, right)
+    left_other = lax.ppermute(left_other, "blk", partner)
+    keep, left_own = lax.optimization_barrier((keep, left_own))
     members = count * inner // 2
-    keep, left_parts = lax.optimization_barrier((keep, left_parts))
     pieces = (keep + sent).reshape(members, outer // 2 // members, pairs)
-    pieces, left_parts = lax.optimization_barrier((pieces, left_parts))
 
     def pair(values, others, after, name):
         final = bool(others)
@@ -520,7 +497,7 @@
             after=after,
         )(values, projection_matrix, *others)
 
-    pair_own_rows = pair(outer_peer, [], [pieces, *right_found[1:]], "pair_peer")
+    pair_own_rows = pair(outer_peer, [], [pieces], "pair_peer")
     pair_peer = lax.ppermute(pair_own_rows, "blk", partner)
 
     pieces = lax.all_to_all(pieces, everyone, 0, 0, axis_index_groups=core_groups)
@@ -529,35 +506,30 @@
     )(pieces)
     pieces = lax.all_to_all(pieces, everyone, 0, 0, axis_index_groups=core_groups)
 
-    left_parts = left_parts.reshape(2 * inner, sequences // inner, rows * channels)
-    left_parts = lax.all_to_all(left_parts, everyone, 0, 0, axis_index_groups=row_groups)
+    left_sum = lax.psum_scatter(
+        left_own + left_other, "inner", scatter_dimension=0, tiled=True
+    )
     size = sequences // inner
     grad_left = call(
-        left_sum_kernel,
+        turn_left_kernel,
         shape(rows, features // inner),
         [
             pltpu.VMEM((size * rows * channels // LANES, LANES), F32),
             pltpu.VMEM((rows * features // inner // LANES, LANES), F32),
         ],
-        name="left_sum",
-    )(left_parts)
+        name="turn_left",
+    )(left_sum)
 
     grad_right = call(
-        functools.partial(turn_out_kernel, blocks),
+        turn_out_kernel,
         shape(depth, features),
-        [
-            pltpu.VMEM((channels * depth, sequences), F32),
-            pltpu.VMEM((LANES, LANES), F32),
-            pltpu.VMEM((depth * features // LANES, LANES), F32),
-        ],
-        name="turn_right_sum",
-    )(*right_found)
+        [pltpu.VMEM((LANES, LANES), F32), pltpu.VMEM((depth * features // LANES, LANES), F32)],
+        name="turn_right",
+    )(right_sum)
 
     pair_update = pair(outer_own, [pair_peer], [], "pair_own")
 
-    pieces, pair_update, grad_left, grad_right = lax.optimization_barrier(
-        (pieces, pair_update, grad_left, grad_right)
-    )
+    pieces, pair_update, grad_right = lax.optimization_barrier((pieces, pair_update, grad_right))
     mine = pieces.reshape(outer // 2, pairs)
     other = lax.ppermute(mine, "inner", cores)
     grad_weight = call(place_kernel, shape(outer, pairs), name="place")(mine, other)

time: 125 us -> 129 us (1.032)
  the two profiles are of different devices: /device:TPU:11 before, /device:TPU:0 now
where the time goes in v7:
time: 129 us; the launch traced here: 128 us
  waiting for transfers between devices  41.5 us (32%)
  Pallas kernels  39.1 us (30%)
  starting transfers between devices  16 us (12%)
  local copies, waits for them, and re-layouts  14.4 us (11%)
  between operations  13.9 us (11%)
  other arithmetic  3.56 us (3%)
    pallas_call x10, Pallas kernels, run(): pl.pallas_call(lambda *refs: kernel(*refs[len(after):]), out_shape=out_sh...  39.1 us
    ppermute x1, waiting for transfers between devices, local(): left_other = lax.ppermute(left_other, 'blk', partner)  13.1 us
    ppermute x1, waiting for transfers between devices, local(): left_peer = lax.ppermute(left, 'blk', partner)  12.4 us
    reduce_scatter x1, waiting for transfers between devices, local(): lax.psum_scatter(left_own + left_other, 'inner', scatter_dimension=0, til...  12.3 us
    all_to_all x2, starting transfers between devices, local(): lax.all_to_all(pieces, everyone, 0, 0, axis_index_groups=core_groups)  10.7 us
    unnamed x20, local copies, waits for them, and re-layouts  10.3 us
    all_to_all x2, waiting for transfers between devices, local(): lax.all_to_all(pieces, everyone, 0, 0, axis_index_groups=core_groups)  3.55 us
    ppermute x1, starting transfers between devices, local(): lax.ppermute(jnp.where(parity == 0, by_side[:, :, 1], by_side[:, :, 0]),...  2.97 us
  transfers between devices with their start and end apart: 11, of which 4 were waited for; matrix products, arithmetic and copies ran while one was open for 4% of the time, Pallas kernels for 30%

profile of v7, /device:TPU:0, one launch (start us, length us, event | category | flops | bytes accessed | tf_op | source)
XLA Modules:
  0.0 128.3 jit_solution(163289609298798143)
XLA Ops:
  7.2 0.0 copy-start.2
  7.2 0.0 copy-start.3
  7.2 0.0 all-gather.2.cloned.1.call-start
  7.2 1.4 %reshape.31 = f32[16,128,32]{2,1,0:T(8,128)S(1)} reshape(f32[16,4096]{1,0:T(8,128)} %param.5) | data formatting | bytes 524288 | tf_op jit(solution)/shard_map/reshape | solution.py:426
  8.6 1.0 copy.20
  9.7 0.0 all-gather.2.cloned.1.call-update
  9.7 0.0 reduce-scatter.3.cloned.1.call-start
  9.7 2.1 %fusion.1 = f32[16,4,16,128]{3,2,1,0:T(8,128)} fusion(f32[16,4,2,16,128]{4,3,2,1,0:T(8,128)} %bitcast.20, pred[]{:T(512)S(6)} %eq.3), kind=kLoop, calls=%fused_computation.2 | loop fusion | flops 131072 | bytes 1572865 | tf_op jit(solution)/shard_map/jit(_where)/select_n | solution.py:433
  11.8 3.0 %collective-permute-start = (f32[16,4,16,128]{3,2,1,0:T(8,128)}, f32[16,4,16,128]{3,2,1,0:T(8,128)S(1)}, u32[]{:S(2)}, u32[]{:S(2)}) collective-permute-start(f32[16,4,16,128]{3,2,1,0:T(8,128)} %fusion.1), channel_id=1, source_target_pairs={{0,4},{4,0},{8,12},{12,8},{16,20},{20,16},{24,28},{28,24},{1,5},{5... | collective-permute-start | bytes 1572872 | tf_op jit(solution)/shard_map/ppermute | solution.py:432
  14.8 1.3 %reshape.29 = f32[16,128,32]{2,1,0:T(8,128)S(1)} reshape(f32[16,4096]{1,0:T(8,128)} %param.4) | data formatting | bytes 524288 | tf_op jit(solution)/shard_map/reshape | solution.py:435
  16.1 0.3 copy.19
  16.4 0.1 collective-permute-start.1
  16.5 0.0 copy-done.2
  16.5 0.0 copy-done.3
  16.5 3.6 %gradient_own.1.refs_2_.refs_1_ = bf16[8,512,512]{2,1,0:T(8,128)(2,1)S(1)} custom-call(f32[1024,128]{1,0:T(8,128)S(1)} %copy-done.3, f32[16,8,16,128]{3,2,1,0:T(8,128)S(1)} %copy-done.2), custom_call_target="tpu_custom_call" | custom-call | flops 1 | bytes 1 | tf_op jit(solution)/shard_map/gradient_own/pallas_call | solution.py:388
  20.1 12.4 %collective-permute-done.1.refs_4_.refs_2_ = f32[512,128]{1,0:T(8,128)S(1)} collective-permute-done((f32[512,128]{1,0:T(8,128)S(1)}, f32[512,128]{1,0:T(8,128)S(1)}, u32[]{:S(2)}, u32[]{:S(2)}) %collective-permute-start.1) | collective-permute-done | bytes 262176 | tf_op jit(solution)/shard_map/ppermute | solution.py:437
  32.5 0.0 collective-permute-done.refs_1_.refs_4_
  32.6 8.3 %right_parts.1 = (bf16[8,512,512]{2,1,0:T(8,128)(2,1)S(1)}, f32[4,512,128]{2,1,0:T(8,128)}) custom-call(f32[1024,128]{1,0:T(8,128)S(1)} %copy-done.3, f32[16,4,16,128]{3,2,1,0:T(8,128)S(1)} %collective-permute-done.refs_1_.refs_4_, bf16[8,512,512]{2,1,0:T(8,128)(2,1)S(1)} %gradient_own.1.refs_2_.refs_1_, f32[512,128]{1,0:T(8,128)S(1)} %bitcast.22, ...), custom_call_target="tpu_custom_call" | custom-call | flops 1 | bytes 1 | tf_op jit(solution)/shard_map/right_parts/pallas_call | solution.py:388
  40.9 0.0 copy-start
  40.9 2.0 %copy-done = bf16[8,512,512]{2,1,0:T(8,128)(2,1)} copy-done((bf16[8,512,512]{2,1,0:T(8,128)(2,1)}, bf16[8,512,512]{2,1,0:T(8,128)(2,1)S(1)}, u32[]{:S(2)}) %copy-start) | copy-done | bytes 4194328
  42.9 0.0 copy-start.4
  42.9 1.9 %copy-done.4 = bf16[8,512,512]{2,1,0:T(8,128)(2,1)} copy-done((bf16[8,512,512]{2,1,0:T(8,128)(2,1)}, bf16[8,512,512]{2,1,0:T(8,128)(2,1)S(1)}, u32[]{:S(2)}) %copy-start.4) | copy-done | bytes 4194328
  44.8 0.0 reduce-scatter.3.cloned.1.call-update
  44.8 0.0 all-gather.2.cloned.1.call-done.refs_5_.refs_3_
  44.8 0.0 copy-start.6
  44.8 1.2 copy-done.6
  46.1 0.0 copy-start.1
  46.1 9.2 %weight.1 = (f32[512,128]{1,0:T(8,128)S(1)}, f32[512,128]{1,0:T(8,128)S(1)}, bf16[8,512,512]{2,1,0:T(8,128)(2,1)}, bf16[8,512,512]{2,1,0:T(8,128)(2,1)}) custom-call(f32[4,512,128]{2,1,0:T(8,128)} %get-tuple-element.17.refs_0_, f32[512,128]{1,0:T(8,128)S(1)} %bitcast.23, f32[512,128]{1,0:T(8,128)S(1)} %collective-permute-done.1.refs_4_.refs_2_, ...), custom_call_target="tpu_custom_call" | custom-call | flops 1 | bytes 1 | tf_op jit(solution)/shard_map/weight/pallas_call | solution.py:388
  55.3 0.1 collective-permute-start.2
  55.4 0.0 copy-done.1
  55.4 0.0 copy-start.5
  55.4 2.2 %copy-done.5 = bf16[8,512,512]{2,1,0:T(8,128)(2,1)S(1)} copy-done((bf16[8,512,512]{2,1,0:T(8,128)(2,1)S(1)}, bf16[8,512,512]{2,1,0:T(8,128)(2,1)}, u32[]{:S(2)}) %copy-start.5) | copy-done | bytes 4194328
  57.6 0.0 copy-start.7
  57.6 1.2 copy-done.7
  58.8 3.1 %left_parts.1 = (f32[128,512]{1,0:T(8,128)S(1)}, f32[128,512]{1,0:T(8,128)S(1)}) custom-call(f32[512,128]{1,0:T(8,128)S(1)} %get-tuple-element.21.refs_0_, bf16[8,512,512]{2,1,0:T(8,128)(2,1)S(1)} %copy-done.1, bf16[8,512,512]{2,1,0:T(8,128)(2,1)S(1)} %copy-done.5, f32[4,512,128]{2,1,0:T(8,128)S(1)} %copy-done.7), custom_call_target="tpu_custom_call" | custom-call | flops 1 | bytes 1 | tf_op jit(solution)/shard_map/left_parts/pallas_call | solution.py:388
  61.9 0.0 collective-permute-done.2
  61.9 0.7 add.10
  62.7 7.1 %all-to-all-start = ((f32[16,32,128]{2,1,0:T(8,128)}), f32[16,32,128]{2,1,0:T(8,128)S(1)}, u32[]{:S(2)}, u32[]{:S(2)}) async-start(f32[16,32,128]{2,1,0:T(8,128)} %bitcast.6.refs_0_), calls=%async_computation | async-start | bytes 524288 | tf_op jit(solution)/shard_map/all_to_all | solution.py:503
  69.8 5.0 %pair_peer.1.refs_0_ = f32[16,4,16,128]{3,2,1,0:T(8,128)S(1)} custom-call(f32[16,32,128]{2,1,0:T(8,128)} %bitcast.6.refs_0_, bf16[8,512,512]{2,1,0:T(8,128)(2,1)} %get-tuple-element.23.refs_1_, f32[1024,128]{1,0:T(8,128)S(1)} %copy-done.3), custom_call_target="tpu_custom_call" | custom-call | flops 1 | bytes 1 | tf_op jit(solution)/shard_map/pair_peer/pallas_call | solution.py:388
  74.8 2.0 %collective-permute-start.3 = (f32[16,4,16,128]{3,2,1,0:T(8,128)S(1)}, f32[16,4,16,128]{3,2,1,0:T(8,128)S(1)}, u32[]{:S(2)}, u32[]{:S(2)}) collective-permute-start(f32[16,4,16,128]{3,2,1,0:T(8,128)S(1)} %pair_peer.1.refs_0_), channel_id=1, source_target_pairs={{0,4},{4,0},{8,12},{12,8},{16,20},{20,16},{24,28},{28,24},{1,5},{5... | collective-permute-start | bytes 1572872 | tf_op jit(solution)/shard_map/ppermute | solution.py:501
  76.8 0.1 collective-permute-start.4
  76.9 3.5 %all-to-all-done.refs_1_ = f32[16,32,128]{2,1,0:T(8,128)S(1)} async-done(((f32[16,32,128]{2,1,0:T(8,128)}), f32[16,32,128]{2,1,0:T(8,128)S(1)}, u32[]{:S(2)}, u32[]{:S(2)}) %all-to-all-start) | async-done | bytes 262176 | tf_op jit(solution)/shard_map/all_to_all | solution.py:503
  80.4 0.8 weight_sum.1
  81.2 3.5 %all-to-all-start.1 = ((f32[16,32,128]{2,1,0:T(8,128)}), f32[16,32,128]{2,1,0:T(8,128)S(1)}, u32[]{:S(2)}, u32[]{:S(2)}) async-start(f32[16,32,128]{2,1,0:T(8,128)} %weight_sum.1), calls=%async_computation.1 | async-start | bytes 524288 | tf_op jit(solution)/shard_map/all_to_all | solution.py:507
  84.7 0.0 reduce-scatter.5.cloned.1.call-start
  84.8 13.1 %collective-permute-done.4 = f32[128,512]{1,0:T(8,128)S(1)} collective-permute-done((f32[128,512]{1,0:T(8,128)S(1)}, f32[128,512]{1,0:T(8,128)S(1)}, u32[]{:S(2)}, u32[]{:S(2)}) %collective-permute-start.4) | collective-permute-done | bytes 262176 | tf_op jit(solution)/shard_map/ppermute | solution.py:479
  97.8 0.7 add.11
  98.6 0.0 reduce-scatter.5.cloned.1.call-update
  98.6 0.0 collective-permute-done.3.refs_2_
  98.6 6.1 %pair_own.1 = f32[16,8,16,128]{3,2,1,0:T(8,128)} custom-call(bf16[8,512,512]{2,1,0:T(8,128)(2,1)} %get-tuple-element.24.refs_0_, f32[1024,128]{1,0:T(8,128)S(1)} %copy-done.3, f32[16,4,16,128]{3,2,1,0:T(8,128)S(1)} %collective-permute-done.3.refs_2_), custom_call_target="tpu_custom_call" | custom-call | flops 1 | bytes 1 | tf_op jit(solution)/shard_map/pair_own/pallas_call | solution.py:388
  104.7 0.0 reduce-scatter.3.cloned.1.call-done
  104.7 0.0 copy-start.8
  104.7 0.9 copy-done.8
  105.7 1.1 turn_right.1
  106.8 0.0 all-to-all-done.1
  106.8 0.0 collective-permute-start.5
  106.8 12.3 %reduce-scatter.5.cloned.1.call-done.refs_0_ = f32[32,512]{1,0:T(8,128)} async-done(((f32[128,512]{1,0:T(8,128)}), f32[32,512]{1,0:T(8,128)}) %reduce-scatter.5.cloned.1.call-update) | async-done | bytes 65552 | tf_op jit(solution)/shard_map/reduce_scatter | solution.py:509
  119.1 0.0 copy-start.9
  119.1 0.8 copy-done.9
  119.9 0.8 turn_left.1
  120.7 0.0 collective-permute-done.5.refs_1_
  120.7 1.1 place.1
Async XLA Ops:
  7.2 9.3 %copy-start.2 = (f32[16,8,16,128]{3,2,1,0:T(8,128)S(1)}, f32[16,8,16,128]{3,2,1,0:T(8,128)}, u32[]{:S(2)}) copy-start(f32[16,8,16,128]{3,2,1,0:T(8,128)} %refs_3_.1) | copy-start | bytes 3145732
  7.2 9.3 %copy-start.3 = (f32[1024,128]{1,0:T(8,128)S(1)}, f32[1024,128]{1,0:T(8,128)}, u32[]{:S(2)}) copy-start(f32[1024,128]{1,0:T(8,128)} %refs_1_.3) | copy-start | bytes 1572868
  7.2 37.6 %all-gather.2.cloned.1.call-start = ((), (), s32[]{:S(2)}) async-start(), calls=%async_computation.4 | async-start | bytes 1310720 | tf_op jit(solution)/shard_map/all_gather | solution.py:428
  9.7 95.0 %reduce-scatter.3.cloned.1.call-start = ((), (), s32[]{:S(2)}) async-start(), calls=%async_computation.5 | async-start | bytes 1310720 | tf_op jit(solution)/shard_map/reduce_scatter | solution.py:451
  11.8 20.7 %collective-permute-start = (f32[16,4,16,128]{3,2,1,0:T(8,128)}, f32[16,4,16,128]{3,2,1,0:T(8,128)S(1)}, u32[]{:S(2)}, u32[]{:S(2)}) collective-permute-start(f32[16,4,16,128]{3,2,1,0:T(8,128)} %fusion.1), channel_id=1, source_target_pairs={{0,4},{4,0},{8,12},{12,8},{16,20},{20,16},{24,28},{28,24},{1,5},{5... | collective-permute-start | bytes 1572872 | tf_op jit(solution)/shard_map/ppermute | solution.py:432
  16.4 16.1 %collective-permute-start.1 = (f32[512,128]{1,0:T(8,128)S(1)}, f32[512,128]{1,0:T(8,128)S(1)}, u32[]{:S(2)}, u32[]{:S(2)}) collective-permute-start(f32[512,128]{1,0:T(8,128)S(1)} %bitcast.21), channel_id=1, source_target_pairs={{0,4},{4,0},{8,12},{12,8},{16,20},{20,16},{24,28},{28,24},{1,5},{5... | collective-permute-start | bytes 786440 | tf_op jit(solution)/shard_map/ppermute | solution.py:437
  40.9 2.0 %copy-start = (bf16[8,512,512]{2,1,0:T(8,128)(2,1)}, bf16[8,512,512]{2,1,0:T(8,128)(2,1)S(1)}, u32[]{:S(2)}) copy-start(bf16[8,512,512]{2,1,0:T(8,128)(2,1)S(1)} %gradient_own.1.refs_2_.refs_1_) | copy-start | bytes 12582916
  42.9 1.9 %copy-start.4 = (bf16[8,512,512]{2,1,0:T(8,128)(2,1)}, bf16[8,512,512]{2,1,0:T(8,128)(2,1)S(1)}, u32[]{:S(2)}) copy-start(bf16[8,512,512]{2,1,0:T(8,128)(2,1)S(1)} %get-tuple-element.19.refs_2_) | copy-start | bytes 12582916
  44.8 1.2 copy-start.6
  46.1 9.3 %copy-start.1 = (bf16[8,512,512]{2,1,0:T(8,128)(2,1)S(1)}, bf16[8,512,512]{2,1,0:T(8,128)(2,1)}, u32[]{:S(2)}) copy-start(bf16[8,512,512]{2,1,0:T(8,128)(2,1)} %copy-done) | copy-start | bytes 12582916
  55.3 6.6 %collective-permute-start.2 = (f32[512,128]{1,0:T(8,128)S(1)}, f32[512,128]{1,0:T(8,128)S(1)}, u32[]{:S(2)}, u32[]{:S(2)}) collective-permute-start(f32[512,128]{1,0:T(8,128)S(1)} %get-tuple-element.22), channel_id=1, source_target_pairs={{0,1},{1,0},{2,3},{3,2},{4,5},{5,4},{6,7},{7,6},{8,9},{9,8},{10,11... | collective-permute-start | bytes 786440 | tf_op jit(solution)/shard_map/ppermute | solution.py:470
  55.4 2.2 %copy-start.5 = (bf16[8,512,512]{2,1,0:T(8,128)(2,1)S(1)}, bf16[8,512,512]{2,1,0:T(8,128)(2,1)}, u32[]{:S(2)}) copy-start(bf16[8,512,512]{2,1,0:T(8,128)(2,1)} %copy-done.4) | copy-start | bytes 12582916
  57.6 1.2 copy-start.7
  62.7 17.7 %all-to-all-start = ((f32[16,32,128]{2,1,0:T(8,128)}), f32[16,32,128]{2,1,0:T(8,128)S(1)}, u32[]{:S(2)}, u32[]{:S(2)}) async-start(f32[16,32,128]{2,1,0:T(8,128)} %bitcast.6.refs_0_), calls=%async_computation | async-start | bytes 524288 | tf_op jit(solution)/shard_map/all_to_all | solution.py:503
  74.8 23.8 %collective-permute-start.3 = (f32[16,4,16,128]{3,2,1,0:T(8,128)S(1)}, f32[16,4,16,128]{3,2,1,0:T(8,128)S(1)}, u32[]{:S(2)}, u32[]{:S(2)}) collective-permute-start(f32[16,4,16,128]{3,2,1,0:T(8,128)S(1)} %pair_peer.1.refs_0_), channel_id=1, source_target_pairs={{0,4},{4,0},{8,12},{12,8},{16,20},{20,16},{24,28},{28,24},{1,5},{5... | collective-permute-start | bytes 1572872 | tf_op jit(solution)/shard_map/ppermute | solution.py:501
  76.8 21.1 %collective-permute-start.4 = (f32[128,512]{1,0:T(8,128)S(1)}, f32[128,512]{1,0:T(8,128)S(1)}, u32[]{:S(2)}, u32[]{:S(2)}) collective-permute-start(f32[128,512]{1,0:T(8,128)S(1)} %get-tuple-element.27), channel_id=1, source_target_pairs={{0,4},{4,0},{8,12},{12,8},{16,20},{20,16},{24,28},{28,24},{1,5},{5... | collective-permute-start | bytes 786440 | tf_op jit(solution)/shard_map/ppermute | solution.py:479
  81.2 25.6 %all-to-all-start.1 = ((f32[16,32,128]{2,1,0:T(8,128)}), f32[16,32,128]{2,1,0:T(8,128)S(1)}, u32[]{:S(2)}, u32[]{:S(2)}) async-start(f32[16,32,128]{2,1,0:T(8,128)} %weight_sum.1), calls=%async_computation.1 | async-start | bytes 524288 | tf_op jit(solution)/shard_map/all_to_all | solution.py:507
  84.7 34.4 %reduce-scatter.5.cloned.1.call-start = ((), (), s32[]{:S(2)}) async-start(), calls=%async_computation.6 | async-start | bytes 327680 | tf_op jit(solution)/shard_map/reduce_scatter | solution.py:509
  104.7 1.0 copy-start.8
  106.8 13.9 %collective-permute-start.5 = (f32[512,128]{1,0:T(8,128)S(1)}, f32[512,128]{1,0:T(8,128)S(1)}, u32[]{:S(2)}, u32[]{:S(2)}) collective-permute-start(f32[512,128]{1,0:T(8,128)S(1)} %bitcast.24), channel_id=1, source_target_pairs={{0,1},{1,0},{2,3},{3,2},{4,5},{5,4},{6,7},{7,6},{8,9},{9,8},{10,11... | collective-permute-start | bytes 786440 | tf_op jit(solution)/shard_map/ppermute | solution.py:534
  119.1 0.8 copy-start.9
Sparse Core Ops, SparseCore 0:
  10.2 30.6 all-gather.1
  44.9 28.6 reduce-scatter.2
  98.7 20.3 reduce-scatter.4

commit v8 on v6

--- a/solution.py
+++ b/solution.py
@@ -70,15 +70,12 @@
     return [jnp.concatenate(found, 0) for found in spread]
 
 
-def turn_out_kernel(parts, *refs):
+def turn_right_kernel(parts, *refs):
     part_refs, (out_ref, total, square, tiles) = refs[:parts], refs[parts:]
     channels = ENTRY_CHANNELS
     rows, features = out_ref.shape
     count = features // LANES
-    found = part_refs[0][...]
-    for ref in part_refs[1:]:
-        found = found + ref[...]
-    total[...] = found
+    total[...] = functools.reduce(jnp.add, [ref[...] for ref in part_refs])
     for group in range(rows // PACK):
         stacked = [total[strided(group * PACK + k, channels, rows), :] for k in range(PACK)]
         square[...] = jnp.concatenate(stacked, 0).T
@@ -92,14 +89,13 @@
         out_ref[:, tile * LANES : (tile + 1) * LANES] = tiles[tile * rows : (tile + 1) * rows, :]
 
 
-def left_sum_kernel(parts_ref, out_ref, total, tiles):
-    channels = ENTRY_CHANNELS
-    parts, size, width = parts_ref.shape
+def turn_left_kernel(parts, *refs):
+    part_refs, (out_ref, total, tiles) = refs[:parts], refs[parts:]
+    channels = ENTRY_CHANNELS
+    size, width = part_refs[0].shape
     rows, features = out_ref.shape
     count = features // LANES
-    found = parts_ref[0]
-    for part in range(1, parts):
-        found = found + parts_ref[part]
+    found = functools.reduce(jnp.add, [ref[...] for ref in part_refs])
     for tile in range(width // LANES):
         total[tile * size : (tile + 1) * size, :] = found[:, tile * LANES : (tile + 1) * LANES]
     for tile in range(width // LANES):
@@ -132,10 +128,37 @@
     lax.fori_loop(0, out_ref.shape[0], step_of, 0)
 
 
-def gradient_kernel(blocks, weight_ref, cotangent_ref, out_ref, weight_cat):
+def gradient_kernel(blocks, weight_ref, cotangent_ref, left_ref, out_ref, partial_ref, weight_cat, left_flip):
     fold = fold_of(blocks * cotangent_ref.shape[2])
     prepare_weight(weight_ref, weight_cat, fold)
     gradient_phase(own_slots(blocks), fold, cotangent_ref, out_ref, weight_cat)
+
+    def store(step, found):
+        partial_ref[step] = found
+
+    right_phase(left_ref, out_ref, left_flip, store)
+
+
+def right_phase(left_ref, factor_ref, left_flip, store):
+    sequences = left_ref.shape[1]
+    lanes = factor_ref.shape[2] // 4
+    flip_high, flip_low = halves((left_ref[...] * (1.0 / sequences)).T)
+    left_flip[:sequences, :] = flip_high
+    left_flip[sequences:, :] = flip_low
+
+    def step_of(step, carry):
+        high, low = (
+            jnp.concatenate(
+                [rows_of_step([factor_ref], 2 * step + part, half, lanes) for part in range(2)], 1
+            )
+            for half in range(2)
+        )
+        first = dot(left_flip[...], high)
+        second = dot(left_flip[:sequences, :], low)
+        store(step, first[:sequences] + first[sequences:] + second)
+        return carry
+
+    lax.fori_loop(0, factor_ref.shape[1] // (2 * ENTRY_CHANNELS), step_of, 0)
 
 
 def rows_of_step(refs, step, half, lanes):
@@ -158,33 +181,16 @@
     return jnp.concatenate([ref[...] for ref in left_refs], 0) * (1.0 / sequences)
 
 
-def right_kernel(
-    blocks, weight_ref, cotangent_ref, own_ref, own_left, peer_left, peer_ref, *refs
-):
+def right_kernel(blocks, weight_ref, cotangent_ref, left_ref, partial_ref, peer_ref, *refs):
     out_refs, (weight_cat, left_flip) = refs[:blocks], refs[blocks:]
-    sequences = own_left.shape[1]
     depth = cotangent_ref.shape[2]
     fold = fold_of(blocks * depth)
     lanes = fold * blocks * depth
     prepare_weight(weight_ref, weight_cat, fold)
     gradient_phase(peer_slots(blocks), fold, cotangent_ref, peer_ref, weight_cat)
-    flip_high, flip_low = halves(both_left([own_left, peer_left]).T)
-    left_flip[:sequences, :] = flip_high
-    left_flip[sequences:, :] = flip_low
-
-    def step_of(step, carry):
-        def stacked(half):
-            return jnp.concatenate(
-                [
-                    rows_of_step([own_ref, peer_ref], 2 * step + part, half, lanes)
-                    for part in range(2)
-                ],
-                1,
-            )
-
-        first = dot(left_flip[...], stacked(0))
-        second = dot(left_flip[:sequences, :], stacked(1))
-        found = first[:sequences] + first[sequences:] + second
+
+    def store(step, found):
+        found = found + partial_ref[step]
         for part in range(2):
             turned = found[:, part * lanes : (part + 1) * lanes].T
             for place in range(fold):
@@ -192,9 +198,8 @@
                     start = (place * blocks + slot) * depth
                     row = pl.multiple_of(((2 * step + part) * fold + place) * depth, depth)
                     out_refs[slot][pl.ds(row, depth), :] = turned[start : start + depth]
-        return carry
-
-    lax.fori_loop(0, ENTRY_CHANNELS // (2 * fold), step_of, 0)
+
+    right_phase(left_ref, peer_ref, left_flip, store)
 
 
 def right_rows(right_refs, step, fold, depth):
@@ -250,17 +255,15 @@
     total[...] = jnp.zeros_like(total)
 
     def weight_step(pair, carry):
-        found = None
+        lefts, rights = [], []
         for ref, cotangent_ref, slots in (
             (own_ref, own_cotangent, own_slots(blocks)),
             (peer_ref, peer_cotangent, peer_slots(blocks)),
         ):
             high, low = spread_of(cotangent_ref, pair, slots, fold)
-            left = ref[pair]
-            left = jnp.concatenate([left, left[:, : 2 * lanes]], 1)
-            term = dot(left, jnp.concatenate([high, high, low], 0))
-            found = term if found is None else found + term
-        total[...] += found
+            lefts += [ref[pair], ref[pair, :, : 2 * lanes]]
+            rights += [high, high, low]
+        total[...] += dot(jnp.concatenate(lefts, 1), jnp.concatenate(rights, 0))
         return carry
 
     lax.fori_loop(0, own_ref.shape[0], weight_step, 0)
@@ -285,8 +288,7 @@
 
 
 def left_kernel(blocks, depth, own_ref, peer_ref, *refs):
-    right_refs = refs[:blocks]
-    out_ref, total, flipped = refs[blocks:]
+    right_refs, (own_out, peer_out, total, flipped) = refs[:blocks], refs[blocks:]
     lanes = own_ref.shape[2] // 4
     fold = lanes // (blocks * depth)
     sequences = right_refs[0].shape[1]
@@ -307,11 +309,17 @@
 
     lax.fori_loop(0, ENTRY_CHANNELS // (fold * group), step_of, 0)
     flipped[...] = total[...].T * (1.0 / sequences)
-    parity = lax.rem(lax.axis_index("blk"), 2)
-    inner, size, width = out_ref.shape[1:]
-    for side, start in ((parity, 0), (1 - parity, width)):
-        for part in range(inner):
-            out_ref[side, part] = flipped[part * size : (part + 1) * size, start : start + width]
+    inner, size, width = own_out.shape
+    here = lax.axis_index("inner")
+    for slot in range(inner):
+        start = pl.multiple_of(lax.bitwise_xor(here, slot) * size, size)
+        own_out[slot] = flipped[pl.ds(start, size), :width]
+        peer_out[slot] = flipped[pl.ds(start, size), width:]
+
+
+def left_add_kernel(own_ref, other_ref, *out_refs):
+    for slot, ref in enumerate(out_refs):
+        ref[...] = own_ref[slot] + other_ref[slot]
 
 
 def pair_kernel(final, blocks, outer_hbm, weight_ref, *refs):
@@ -429,11 +437,8 @@
 
     partner = [(here, here ^ 1) for here in range(count)]
     slot_moves = [[(here, here ^ (2 * slot)) for here in range(count)] for slot in range(blocks)]
+    inner_moves = [[(here, here ^ slot) for here in range(inner)] for slot in range(inner)]
     cores = [(here, here ^ 1) for here in range(inner)]
-    row_groups = [
-        [(2 * step + side) * inner + part for side in range(2) for part in range(inner)]
-        for step in range(blocks)
-    ]
     core_groups = [list(range(core, count * inner, 2)) for core in range(2)]
 
     limit = 20 * MIB * max(1, blocks * depth * fold // LANES * 2 // fold)
@@ -445,7 +450,6 @@
     for slot in range(1, blocks):
         rights.append(lax.ppermute(right, "blk", slot_moves[slot]))
 
-    cotangent, _ = lax.optimization_barrier((cotangent, right))
     by_side = cotangent.reshape(rows, blocks, 2, depth, pairs)
     parity = lax.rem(lax.axis_index("blk"), 2)
     cotangent_peer = lax.ppermute(
@@ -458,15 +462,19 @@
     factor = shape(row_pairs, tall, 4 * lanes, kind=BF16)
     factor_scratch = pltpu.VMEM(factor.shape, BF16)
     weight_scratch = pltpu.VMEM((tall, 3 * fold * pairs), BF16)
-    grad_own = large(
-        functools.partial(gradient_kernel, blocks), factor, [weight_scratch], "gradient_own"
-    )(projection_matrix, cotangent)
+    flip_scratch = pltpu.VMEM((2 * sequences, rows * channels), BF16)
+    grad_own, partial = large(
+        functools.partial(gradient_kernel, blocks),
+        [factor, shape(steps // 2, sequences, 2 * lanes)],
+        [weight_scratch, flip_scratch],
+        "gradient_own",
+    )(projection_matrix, cotangent, left)
     grad_peer, *right_parts = large(
         functools.partial(right_kernel, blocks),
         [factor] + [shape(channels * depth, sequences)] * blocks,
-        [weight_scratch, pltpu.VMEM((2 * sequences, 2 * rows * channels), BF16)],
+        [weight_scratch, flip_scratch],
         "right_parts",
-    )(projection_matrix, cotangent_peer, grad_own, left, left_peer)
+    )(projection_matrix, cotangent_peer, left_peer, partial)
     right_found = [right_parts[0]]
     for slot in range(1, blocks):
         right_found.append(lax.ppermute(right_parts[slot], "blk", slot_moves[slot]))
@@ -488,9 +496,10 @@
     )(left, left_peer, cotangent, cotangent_peer, *rights)
     sent = lax.ppermute(send, "inner", cores)
 
-    left_parts = large(
+    size = sequences // inner
+    left_own, left_other = large(
         functools.partial(left_kernel, blocks, depth),
-        shape(2, inner, sequences // inner, rows * channels),
+        [shape(inner, size, rows * channels)] * 2,
         [
             pltpu.VMEM((2 * rows * channels, sequences), F32),
             pltpu.VMEM((sequences, 2 * rows * channels), F32),
@@ -498,11 +507,10 @@
         "left_parts",
         after=[keep],
     )(grad_own, grad_peer, *rights)
-
+    left_other = lax.ppermute(left_other, "blk", partner)
+    keep, left_own = lax.optimization_barrier((keep, left_own))
     members = count * inner // 2
-    keep, left_parts = lax.optimization_barrier((keep, left_parts))
     pieces = (keep + sent).reshape(members, outer // 2 // members, pairs)
-    pieces, left_parts = lax.optimization_barrier((pieces, left_parts))
 
     def pair(values, others, after, name):
         final = bool(others)
@@ -520,7 +528,7 @@
             after=after,
         )(values, projection_matrix, *others)
 
-    pair_own_rows = pair(outer_peer, [], [pieces, *right_found[1:]], "pair_peer")
+    pair_own_rows = pair(outer_peer, [], [pieces], "pair_peer")
     pair_peer = lax.ppermute(pair_own_rows, "blk", partner)
 
     pieces = lax.all_to_all(pieces, everyone, 0, 0, axis_index_groups=core_groups)
@@ -529,28 +537,32 @@
     )(pieces)
     pieces = lax.all_to_all(pieces, everyone, 0, 0, axis_index_groups=core_groups)
 
-    left_parts = left_parts.reshape(2 * inner, sequences // inner, rows * channels)
-    left_parts = lax.all_to_all(left_parts, everyone, 0, 0, axis_index_groups=row_groups)
-    size = sequences // inner
+    left_found = call(
+        left_add_kernel, [shape(size, rows * channels)] * inner, name="left_add"
+    )(left_own, left_other)
+    left_found = [
+        lax.ppermute(part, "inner", inner_moves[slot]) if slot else part
+        for slot, part in enumerate(left_found)
+    ]
     grad_left = call(
-        left_sum_kernel,
+        functools.partial(turn_left_kernel, inner),
         shape(rows, features // inner),
         [
             pltpu.VMEM((size * rows * channels // LANES, LANES), F32),
             pltpu.VMEM((rows * features // inner // LANES, LANES), F32),
         ],
-        name="left_sum",
-    )(left_parts)
+        name="turn_left",
+    )(*left_found)
 
     grad_right = call(
-        functools.partial(turn_out_kernel, blocks),
+        functools.partial(turn_right_kernel, blocks),
         shape(depth, features),
         [
             pltpu.VMEM((channels * depth, sequences), F32),
             pltpu.VMEM((LANES, LANES), F32),
             pltpu.VMEM((depth * features // LANES, LANES), F32),
         ],
-        name="turn_right_sum",
+        name="turn_right",
     )(*right_found)
 
     pair_update = pair(outer_own, [pair_peer], [], "pair_own")

time: 125 us -> 113 us (0.904)
  the two profiles are of different devices: /device:TPU:11 before, /device:TPU:0 now
where the time goes in v8:
time: 113 us
  Pallas kernels  41.3 us (37%)
  waiting for transfers between devices  34.6 us (31%)
  starting transfers between devices  27.3 us (24%)
  local copies, waits for them, and re-layouts  6.68 us (6%)
  other arithmetic  2.15 us (2%)
    pallas_call x11, Pallas kernels, run(): pl.pallas_call(lambda *refs: kernel(*refs[len(after):]), out_shape=out_sh...  41.3 us
    ppermute x3, waiting for transfers between devices, local(): right_found.append(lax.ppermute(right_parts[slot], 'blk', slot_moves[slot]))  11.4 us
    all_to_all x2, starting transfers between devices, local(): lax.all_to_all(pieces, everyone, 0, 0, axis_index_groups=core_groups)  9.28 us
    ppermute x3, waiting for transfers between devices, local(): rights.append(lax.ppermute(right, 'blk', slot_moves[slot]))  7.85 us
    ppermute x1, waiting for transfers between devices, local(): left_other = lax.ppermute(left_other, 'blk', partner)  7.07 us
    ppermute x3, starting transfers between devices, local(): rights.append(lax.ppermute(right, 'blk', slot_moves[slot]))  4.79 us
    ppermute x3, starting transfers between devices, local(): right_found.append(lax.ppermute(right_parts[slot], 'blk', slot_moves[slot]))  4.39 us
    all_to_all x2, waiting for transfers between devices, local(): lax.all_to_all(pieces, everyone, 0, 0, axis_index_groups=core_groups)  3.57 us
  transfers between devices with their start and end apart: 17, of which 7 were waited for; matrix products, arithmetic and copies ran while one was open for 6% of the time, Pallas kernels for 27%

profile of v8, /device:TPU:0, one launch (start us, length us, event | category | flops | bytes accessed | tf_op | source)
XLA Modules:
  0.0 112.8 jit_solution(7152277854679458606)
XLA Ops:
  0.6 0.0 copy-start
  0.6 0.0 copy-start.2
  0.7 0.0 copy-start.1
  0.7 1.4 %fusion.1 = f32[16,4,16,128]{3,2,1,0:T(8,128)S(1)} fusion(f32[16,4,2,16,128]{4,3,2,1,0:T(8,128)} %bitcast.19, pred[]{:T(512)S(6)} %eq.3), kind=kLoop, calls=%fused_computation.2 | loop fusion | flops 131072 | bytes 1572865 | tf_op jit(solution)/shard_map/jit(_where)/select_n | solution.py:456
  2.1 3.0 %collective-permute-start = (f32[16,4,16,128]{3,2,1,0:T(8,128)S(1)}, f32[16,4,16,128]{3,2,1,0:T(8,128)S(1)}, u32[]{:S(2)}, u32[]{:S(2)}) collective-permute-start(f32[16,4,16,128]{3,2,1,0:T(8,128)S(1)} %fusion.1), channel_id=1, source_target_pairs={{0,4},{4,0},{8,12},{12,8},{16,20},{20,16},{24,28},{28,24},{1,5},{5... | collective-permute-start | bytes 1572872 | tf_op jit(solution)/shard_map/ppermute | solution.py:455
  5.1 2.3 %reshape.32 = f32[16,128,32]{2,1,0:T(8,128)} reshape(f32[16,4096]{1,0:T(8,128)} %param.4) | data formatting | bytes 524288 | tf_op jit(solution)/shard_map/reshape | solution.py:458
  7.4 1.5 %copy.12 = f32[16,32,128]{2,1,0:T(8,128)S(1)} copy(f32[16,32,128]{1,2,0:T(8,128)} %bitcast.30) | data formatting | bytes 524288 | tf_op jit(solution)/shard_map/transpose | solution.py:458
  8.9 0.1 collective-permute-start.1
  9.0 0.0 copy-done.2
  9.0 1.3 %reshape.34 = f32[16,128,32]{2,1,0:T(8,128)} reshape(f32[16,4096]{1,0:T(8,128)S(1)} %copy-done.2) | data formatting | bytes 524288 | tf_op jit(solution)/shard_map/reshape | solution.py:447
  10.3 1.6 %copy.13 = f32[32,16,128]{2,1,0:T(8,128)S(1)} copy(f32[32,16,128]{0,2,1:T(8,128)} %bitcast.31) | data formatting | bytes 524288 | tf_op jit(solution)/shard_map/transpose | solution.py:447
  11.9 4.2 %collective-permute-start.4 = (f32[512,128]{1,0:T(8,128)S(1)}, f32[512,128]{1,0:T(8,128)S(1)}, u32[]{:S(2)}, u32[]{:S(2)}) collective-permute-start(f32[512,128]{1,0:T(8,128)S(1)} %bitcast.20), channel_id=1, source_target_pairs={{0,24},{4,28},{8,16},{12,20},{16,8},{20,12},{24,0},{28,4},{1,25},{... | collective-permute-start | bytes 786440 | tf_op jit(solution)/shard_map/ppermute | solution.py:451
  16.0 0.0 collective-permute-start.3
  16.0 0.6 collective-permute-start.2
  16.7 0.0 copy-done
  16.7 0.0 copy-done.1
  16.7 5.9 %gradient_own.1 = (bf16[8,512,512]{2,1,0:T(8,128)(2,1)S(1)}, f32[8,128,256]{2,1,0:T(8,128)S(1)}) custom-call(f32[1024,128]{1,0:T(8,128)S(1)} %copy-done.1, f32[16,8,16,128]{3,2,1,0:T(8,128)S(1)} %copy-done, f32[512,128]{1,0:T(8,128)S(1)} %bitcast.26), custom_call_target="tpu_custom_call" | custom-call | flops 1 | bytes 1 | tf_op jit(solution)/shard_map/gradient_own/pallas_call | solution.py:408
  22.6 0.0 collective-permute-done.1.refs_2_
  22.7 0.0 collective-permute-done.refs_1_.refs_4_
  22.7 7.3 %right_parts.1 = (bf16[8,512,512]{2,1,0:T(8,128)(2,1)S(1)}, f32[512,128]{1,0:T(8,128)S(1)}, f32[512,128]{1,0:T(8,128)}, f32[512,128]{1,0:T(8,128)}, f32[512,128]{1,0:T(8,128)S(1)}) custom-call(f32[1024,128]{1,0:T(8,128)S(1)} %copy-done.1, f32[16,4,16,128]{3,2,1,0:T(8,128)S(1)} %collective-permute-done.refs_1_.refs_4_, ...), custom_call_target="tpu_custom_call" | custom-call | flops 1 | bytes 1 | tf_op jit(solution)/shard_map/right_parts/pallas_call | solution.py:408
  29.9 0.0 collective-permute-done.4.refs_8_.refs_6_
  29.9 7.8 %collective-permute-done.3.refs_7_.refs_5_ = f32[512,128]{1,0:T(8,128)S(1)} collective-permute-done((f32[512,128]{1,0:T(8,128)S(1)}, f32[512,128]{1,0:T(8,128)S(1)}, u32[]{:S(2)}, u32[]{:S(2)}) %collective-permute-start.3) | collective-permute-done | bytes 262176 | tf_op jit(solution)/shard_map/ppermute | solution.py:451
  37.8 0.0 collective-permute-done.2.refs_6_.refs_4_
  37.8 9.3 %weight.1 = (f32[512,128]{1,0:T(8,128)S(1)}, f32[512,128]{1,0:T(8,128)S(1)}, bf16[8,512,512]{2,1,0:T(8,128)(2,1)}, bf16[8,512,512]{2,1,0:T(8,128)(2,1)}) custom-call(f32[512,128]{1,0:T(8,128)S(1)} %get-tuple-element.28.refs_0_, f32[512,128]{1,0:T(8,128)S(1)} %bitcast.27, f32[512,128]{1,0:T(8,128)S(1)} %collective-permute-done.1.refs_2_, ...), custom_call_target="tpu_custom_call" | custom-call | flops 1 | bytes 1 | tf_op jit(solution)/shard_map/weight/pallas_call | solution.py:408
  47.1 0.1 collective-permute-start.5
  47.2 3.8 %left_parts.1 = (f32[4,32,512]{2,1,0:T(8,128)S(1)}, f32[4,32,512]{2,1,0:T(8,128)}) custom-call(f32[512,128]{1,0:T(8,128)S(1)} %get-tuple-element.33.refs_0_, bf16[8,512,512]{2,1,0:T(8,128)(2,1)S(1)} %get-tuple-element.30.refs_1_, bf16[8,512,512]{2,1,0:T(8,128)(2,1)S(1)} %get-tuple-element.31.refs_2_, f32[512,128]{1,0:T(8,128)S(1)} %bitcast.24, ...), custom_call_target="tpu_custom_call" | custom-call | flops 1 | bytes 1 | tf_op jit(solution)/shard_map/left_parts/pallas_call | solution.py:408
  51.0 0.0 collective-permute-done.5
  51.0 0.7 add.3
  51.7 5.7 %all-to-all-start = ((f32[16,32,128]{2,1,0:T(8,128)}), f32[16,32,128]{2,1,0:T(8,128)S(1)}, u32[]{:S(2)}, u32[]{:S(2)}) async-start(f32[16,32,128]{2,1,0:T(8,128)} %bitcast.6.refs_0_), calls=%async_computation | async-start | bytes 524288 | tf_op jit(solution)/shard_map/all_to_all | solution.py:534
  57.5 5.1 %pair_peer.1.refs_0_ = f32[16,4,16,128]{3,2,1,0:T(8,128)S(1)} custom-call(f32[16,32,128]{2,1,0:T(8,128)} %bitcast.6.refs_0_, bf16[8,512,512]{2,1,0:T(8,128)(2,1)} %get-tuple-element.35.refs_1_, f32[1024,128]{1,0:T(8,128)S(1)} %copy-done.1), custom_call_target="tpu_custom_call" | custom-call | flops 1 | bytes 1 | tf_op jit(solution)/shard_map/pair_peer/pallas_call | solution.py:408
  62.6 2.0 %collective-permute-start.6 = (f32[16,4,16,128]{3,2,1,0:T(8,128)S(1)}, f32[16,4,16,128]{3,2,1,0:T(8,128)S(1)}, u32[]{:S(2)}, u32[]{:S(2)}) collective-permute-start(f32[16,4,16,128]{3,2,1,0:T(8,128)S(1)} %pair_peer.1.refs_0_), channel_id=1, source_target_pairs={{0,4},{4,0},{8,12},{12,8},{16,20},{20,16},{24,28},{28,24},{1,5},{5... | collective-permute-start | bytes 1572872 | tf_op jit(solution)/shard_map/ppermute | solution.py:532
  64.6 3.6 %all-to-all-done.refs_1_ = f32[16,32,128]{2,1,0:T(8,128)S(1)} async-done(((f32[16,32,128]{2,1,0:T(8,128)}), f32[16,32,128]{2,1,0:T(8,128)S(1)}, u32[]{:S(2)}, u32[]{:S(2)}) %all-to-all-start) | async-done | bytes 262176 | tf_op jit(solution)/shard_map/all_to_all | solution.py:534
  68.1 0.8 weight_sum.1
  68.9 3.5 %all-to-all-start.1 = ((f32[16,32,128]{2,1,0:T(8,128)}), f32[16,32,128]{2,1,0:T(8,128)S(1)}, u32[]{:S(2)}, u32[]{:S(2)}) async-start(f32[16,32,128]{2,1,0:T(8,128)} %weight_sum.1), calls=%async_computation.1 | async-start | bytes 524288 | tf_op jit(solution)/shard_map/all_to_all | solution.py:538
  72.4 1.9 %collective-permute-start.7 = (f32[4,32,512]{2,1,0:T(8,128)}, f32[4,32,512]{2,1,0:T(8,128)S(1)}, u32[]{:S(2)}, u32[]{:S(2)}) collective-permute-start(f32[4,32,512]{2,1,0:T(8,128)} %get-tuple-element.38), channel_id=1, source_target_pairs={{0,4},{4,0},{8,12},{12,8},{16,20},{20,16},{24,28},{28,24},{1,5},{5... | collective-permute-start | bytes 786440 | tf_op jit(solution)/shard_map/ppermute | solution.py:510
  74.4 1.5 %collective-permute-start.11 = (f32[512,128]{1,0:T(8,128)}, f32[512,128]{1,0:T(8,128)S(1)}, u32[]{:S(2)}, u32[]{:S(2)}) collective-permute-start(f32[512,128]{1,0:T(8,128)} %get-tuple-element.43), channel_id=1, source_target_pairs={{0,8},{4,12},{8,0},{12,4},{16,24},{20,28},{24,16},{28,20},{1,9},{5... | collective-permute-start | bytes 786440 | tf_op jit(solution)/shard_map/ppermute | solution.py:480
  75.8 2.4 %collective-permute-start.12 = (f32[512,128]{1,0:T(8,128)}, f32[512,128]{1,0:T(8,128)S(1)}, u32[]{:S(2)}, u32[]{:S(2)}) collective-permute-start(f32[512,128]{1,0:T(8,128)} %get-tuple-element.44), channel_id=1, source_target_pairs={{0,16},{4,20},{8,24},{12,28},{16,0},{20,4},{24,8},{28,12},{1,17},{... | collective-permute-start | bytes 786440 | tf_op jit(solution)/shard_map/ppermute | solution.py:480
  78.2 0.6 collective-permute-start.13
  78.7 7.1 %collective-permute-done.7.refs_1_ = f32[4,32,512]{2,1,0:T(8,128)S(1)} collective-permute-done((f32[4,32,512]{2,1,0:T(8,128)}, f32[4,32,512]{2,1,0:T(8,128)S(1)}, u32[]{:S(2)}, u32[]{:S(2)}) %collective-permute-start.7) | collective-permute-done | bytes 262176 | tf_op jit(solution)/shard_map/ppermute | solution.py:510
  85.8 0.1 collective-permute-start.8
  85.9 3.3 %collective-permute-done.11.refs_1_ = f32[512,128]{1,0:T(8,128)S(1)} collective-permute-done((f32[512,128]{1,0:T(8,128)}, f32[512,128]{1,0:T(8,128)S(1)}, u32[]{:S(2)}, u32[]{:S(2)}) %collective-permute-start.11) | collective-permute-done | bytes 262176 | tf_op jit(solution)/shard_map/ppermute | solution.py:480
  89.2 1.5 %collective-permute-start.9 = (f32[32,512]{1,0:T(8,128)S(1)}, f32[32,512]{1,0:T(8,128)S(1)}, u32[]{:S(2)}, u32[]{:S(2)}) collective-permute-start(f32[32,512]{1,0:T(8,128)S(1)} %get-tuple-element.41), channel_id=1, source_target_pairs={{0,2},{1,3},{2,0},{3,1},{4,6},{5,7},{6,4},{7,5},{8,10},{9,11},{10,... | collective-permute-start | bytes 196616 | tf_op jit(solution)/shard_map/ppermute | solution.py:544
  90.7 8.1 %collective-permute-done.12.refs_2_ = f32[512,128]{1,0:T(8,128)S(1)} collective-permute-done((f32[512,128]{1,0:T(8,128)}, f32[512,128]{1,0:T(8,128)S(1)}, u32[]{:S(2)}, u32[]{:S(2)}) %collective-permute-start.12) | collective-permute-done | bytes 262176 | tf_op jit(solution)/shard_map/ppermute | solution.py:480
  98.8 0.0 collective-permute-start.10
  98.8 0.0 collective-permute-done.13.refs_3_
  98.8 1.2 %turn_right.1 = f32[16,4096]{1,0:T(8,128)} custom-call(f32[512,128]{1,0:T(8,128)S(1)} %get-tuple-element.28.refs_0_, f32[512,128]{1,0:T(8,128)S(1)} %collective-permute-done.11.refs_1_, f32[512,128]{1,0:T(8,128)S(1)} %collective-permute-done.12.refs_2_, f32[512,128]{1,0:T(8,128)S(1)} %collective-permute-done.13.refs_3_), custom_call_target="tpu_custom_call" | custom-call | flops 1 | bytes 1 | tf_op jit(solution)/shard_map/turn_right/pallas_call | solution.py:408
  100.0 0.0 collective-permute-done.8.refs_1_
  100.0 0.0 collective-permute-done.9.refs_2_
  100.1 3.2 %collective-permute-done.10.refs_3_ = f32[32,512]{1,0:T(8,128)S(1)} collective-permute-done((f32[32,512]{1,0:T(8,128)S(1)}, f32[32,512]{1,0:T(8,128)S(1)}, u32[]{:S(2)}, u32[]{:S(2)}) %collective-permute-start.10) | collective-permute-done | bytes 65568 | tf_op jit(solution)/shard_map/ppermute | solution.py:544
  103.2 0.8 turn_left.1
  104.0 0.0 collective-permute-done.6.refs_2_
  104.0 6.1 %pair_own.1 = f32[16,8,16,128]{3,2,1,0:T(8,128)} custom-call(bf16[8,512,512]{2,1,0:T(8,128)(2,1)} %get-tuple-element.36.refs_0_, f32[1024,128]{1,0:T(8,128)S(1)} %copy-done.1, f32[16,4,16,128]{3,2,1,0:T(8,128)S(1)} %collective-permute-done.6.refs_2_), custom_call_target="tpu_custom_call" | custom-call | flops 1 | bytes 1 | tf_op jit(solution)/shard_map/pair_own/pallas_call | solution.py:408
  110.1 0.0 all-to-all-done.1
  110.1 0.2 collective-permute-start.14
  110.2 1.4 %collective-permute-done.14.refs_1_ = f32[512,128]{1,0:T(8,128)S(1)} collective-permute-done((f32[512,128]{1,0:T(8,128)S(1)}, f32[512,128]{1,0:T(8,128)S(1)}, u32[]{:S(2)}, u32[]{:S(2)}) %collective-permute-start.14) | collective-permute-done | bytes 262176 | tf_op jit(solution)/shard_map/ppermute | solution.py:574
  111.7 1.1 place.1
  (1 shorter events, 0.0 us)
Async XLA Ops:
  0.6 16.0 %copy-start = (f32[16,8,16,128]{3,2,1,0:T(8,128)S(1)}, f32[16,8,16,128]{3,2,1,0:T(8,128)}, u32[]{:S(2)}) copy-start(f32[16,8,16,128]{3,2,1,0:T(8,128)} %refs_3_.1) | copy-start | bytes 3145732
  0.6 8.3 %copy-start.2 = (f32[16,4096]{1,0:T(8,128)S(1)}, f32[16,4096]{1,0:T(8,128)}, u32[]{:S(2)}) copy-start(f32[16,4096]{1,0:T(8,128)} %param.5) | copy-start | bytes 786436
  0.7 16.0 %copy-start.1 = (f32[1024,128]{1,0:T(8,128)S(1)}, f32[1024,128]{1,0:T(8,128)}, u32[]{:S(2)}) copy-start(f32[1024,128]{1,0:T(8,128)} %refs_1_.3) | copy-start | bytes 1572868
  2.1 20.6 %collective-permute-start = (f32[16,4,16,128]{3,2,1,0:T(8,128)S(1)}, f32[16,4,16,128]{3,2,1,0:T(8,128)S(1)}, u32[]{:S(2)}, u32[]{:S(2)}) collective-permute-start(f32[16,4,16,128]{3,2,1,0:T(8,128)S(1)} %fusion.1), channel_id=1, source_target_pairs={{0,4},{4,0},{8,12},{12,8},{16,20},{20,16},{24,28},{28,24},{1,5},{5... | collective-permute-start | bytes 1572872 | tf_op jit(solution)/shard_map/ppermute | solution.py:455
  8.9 13.7 %collective-permute-start.1 = (f32[512,128]{1,0:T(8,128)S(1)}, f32[512,128]{1,0:T(8,128)S(1)}, u32[]{:S(2)}, u32[]{:S(2)}) collective-permute-start(f32[512,128]{1,0:T(8,128)S(1)} %bitcast.25), channel_id=1, source_target_pairs={{0,4},{4,0},{8,12},{12,8},{16,20},{20,16},{24,28},{28,24},{1,5},{5... | collective-permute-start | bytes 786440 | tf_op jit(solution)/shard_map/ppermute | solution.py:460
  11.9 18.1 %collective-permute-start.4 = (f32[512,128]{1,0:T(8,128)S(1)}, f32[512,128]{1,0:T(8,128)S(1)}, u32[]{:S(2)}, u32[]{:S(2)}) collective-permute-start(f32[512,128]{1,0:T(8,128)S(1)} %bitcast.20), channel_id=1, source_target_pairs={{0,24},{4,28},{8,16},{12,20},{16,8},{20,12},{24,0},{28,4},{1,25},{... | collective-permute-start | bytes 786440 | tf_op jit(solution)/shard_map/ppermute | solution.py:451
  16.0 21.7 %collective-permute-start.3 = (f32[512,128]{1,0:T(8,128)S(1)}, f32[512,128]{1,0:T(8,128)S(1)}, u32[]{:S(2)}, u32[]{:S(2)}) collective-permute-start(f32[512,128]{1,0:T(8,128)S(1)} %bitcast.21), channel_id=1, source_target_pairs={{0,16},{4,20},{8,24},{12,28},{16,0},{20,4},{24,8},{28,12},{1,17},{... | collective-permute-start | bytes 786440 | tf_op jit(solution)/shard_map/ppermute | solution.py:451
  16.0 21.7 %collective-permute-start.2 = (f32[512,128]{1,0:T(8,128)S(1)}, f32[512,128]{1,0:T(8,128)S(1)}, u32[]{:S(2)}, u32[]{:S(2)}) collective-permute-start(f32[512,128]{1,0:T(8,128)S(1)} %bitcast.22), channel_id=1, source_target_pairs={{0,8},{4,12},{8,0},{12,4},{16,24},{20,28},{24,16},{28,20},{1,9},{5... | collective-permute-start | bytes 786440 | tf_op jit(solution)/shard_map/ppermute | solution.py:451
  47.1 3.9 %collective-permute-start.5 = (f32[512,128]{1,0:T(8,128)S(1)}, f32[512,128]{1,0:T(8,128)S(1)}, u32[]{:S(2)}, u32[]{:S(2)}) collective-permute-start(f32[512,128]{1,0:T(8,128)S(1)} %get-tuple-element.34), channel_id=1, source_target_pairs={{0,1},{1,0},{2,3},{3,2},{4,5},{5,4},{6,7},{7,6},{8,9},{9,8},{10,11... | collective-permute-start | bytes 786440 | tf_op jit(solution)/shard_map/ppermute | solution.py:497
  51.7 16.4 %all-to-all-start = ((f32[16,32,128]{2,1,0:T(8,128)}), f32[16,32,128]{2,1,0:T(8,128)S(1)}, u32[]{:S(2)}, u32[]{:S(2)}) async-start(f32[16,32,128]{2,1,0:T(8,128)} %bitcast.6.refs_0_), calls=%async_computation | async-start | bytes 524288 | tf_op jit(solution)/shard_map/all_to_all | solution.py:534
  62.6 41.4 %collective-permute-start.6 = (f32[16,4,16,128]{3,2,1,0:T(8,128)S(1)}, f32[16,4,16,128]{3,2,1,0:T(8,128)S(1)}, u32[]{:S(2)}, u32[]{:S(2)}) collective-permute-start(f32[16,4,16,128]{3,2,1,0:T(8,128)S(1)} %pair_peer.1.refs_0_), channel_id=1, source_target_pairs={{0,4},{4,0},{8,12},{12,8},{16,20},{20,16},{24,28},{28,24},{1,5},{5... | collective-permute-start | bytes 1572872 | tf_op jit(solution)/shard_map/ppermute | solution.py:532
  68.9 41.2 %all-to-all-start.1 = ((f32[16,32,128]{2,1,0:T(8,128)}), f32[16,32,128]{2,1,0:T(8,128)S(1)}, u32[]{:S(2)}, u32[]{:S(2)}) async-start(f32[16,32,128]{2,1,0:T(8,128)} %weight_sum.1), calls=%async_computation.1 | async-start | bytes 524288 | tf_op jit(solution)/shard_map/all_to_all | solution.py:538
  72.4 13.4 %collective-permute-start.7 = (f32[4,32,512]{2,1,0:T(8,128)}, f32[4,32,512]{2,1,0:T(8,128)S(1)}, u32[]{:S(2)}, u32[]{:S(2)}) collective-permute-start(f32[4,32,512]{2,1,0:T(8,128)} %get-tuple-element.38), channel_id=1, source_target_pairs={{0,4},{4,0},{8,12},{12,8},{16,20},{20,16},{24,28},{28,24},{1,5},{5... | collective-permute-start | bytes 786440 | tf_op jit(solution)/shard_map/ppermute | solution.py:510
  74.4 14.9 %collective-permute-start.11 = (f32[512,128]{1,0:T(8,128)}, f32[512,128]{1,0:T(8,128)S(1)}, u32[]{:S(2)}, u32[]{:S(2)}) collective-permute-start(f32[512,128]{1,0:T(8,128)} %get-tuple-element.43), channel_id=1, source_target_pairs={{0,8},{4,12},{8,0},{12,4},{16,24},{20,28},{24,16},{28,20},{1,9},{5... | collective-permute-start | bytes 786440 | tf_op jit(solution)/shard_map/ppermute | solution.py:480
  75.8 23.0 %collective-permute-start.12 = (f32[512,128]{1,0:T(8,128)}, f32[512,128]{1,0:T(8,128)S(1)}, u32[]{:S(2)}, u32[]{:S(2)}) collective-permute-start(f32[512,128]{1,0:T(8,128)} %get-tuple-element.44), channel_id=1, source_target_pairs={{0,16},{4,20},{8,24},{12,28},{16,0},{20,4},{24,8},{28,12},{1,17},{... | collective-permute-start | bytes 786440 | tf_op jit(solution)/shard_map/ppermute | solution.py:480
  78.2 20.7 %collective-permute-start.13 = (f32[512,128]{1,0:T(8,128)S(1)}, f32[512,128]{1,0:T(8,128)S(1)}, u32[]{:S(2)}, u32[]{:S(2)}) collective-permute-start(f32[512,128]{1,0:T(8,128)S(1)} %get-tuple-element.45), channel_id=1, source_target_pairs={{0,24},{4,28},{8,16},{12,20},{16,8},{20,12},{24,0},{28,4},{1,25},{... | collective-permute-start | bytes 786440 | tf_op jit(solution)/shard_map/ppermute | solution.py:480
  85.8 14.2 %collective-permute-start.8 = (f32[32,512]{1,0:T(8,128)S(1)}, f32[32,512]{1,0:T(8,128)S(1)}, u32[]{:S(2)}, u32[]{:S(2)}) collective-permute-start(f32[32,512]{1,0:T(8,128)S(1)} %get-tuple-element.40), channel_id=1, source_target_pairs={{0,1},{1,0},{2,3},{3,2},{4,5},{5,4},{6,7},{7,6},{8,9},{9,8},{10,11... | collective-permute-start | bytes 196616 | tf_op jit(solution)/shard_map/ppermute | solution.py:544
  89.2 10.8 %collective-permute-start.9 = (f32[32,512]{1,0:T(8,128)S(1)}, f32[32,512]{1,0:T(8,128)S(1)}, u32[]{:S(2)}, u32[]{:S(2)}) collective-permute-start(f32[32,512]{1,0:T(8,128)S(1)} %get-tuple-element.41), channel_id=1, source_target_pairs={{0,2},{1,3},{2,0},{3,1},{4,6},{5,7},{6,4},{7,5},{8,10},{9,11},{10,... | collective-permute-start | bytes 196616 | tf_op jit(solution)/shard_map/ppermute | solution.py:544
  98.8 4.4 %collective-permute-start.10 = (f32[32,512]{1,0:T(8,128)S(1)}, f32[32,512]{1,0:T(8,128)S(1)}, u32[]{:S(2)}, u32[]{:S(2)}) collective-permute-start(f32[32,512]{1,0:T(8,128)S(1)} %get-tuple-element.42), channel_id=1, source_target_pairs={{0,3},{1,2},{2,1},{3,0},{4,7},{5,6},{6,5},{7,4},{8,11},{9,10},{10,... | collective-permute-start | bytes 196616 | tf_op jit(solution)/shard_map/ppermute | solution.py:544
  110.1 1.6 %collective-permute-start.14 = (f32[512,128]{1,0:T(8,128)S(1)}, f32[512,128]{1,0:T(8,128)S(1)}, u32[]{:S(2)}, u32[]{:S(2)}) collective-permute-start(f32[512,128]{1,0:T(8,128)S(1)} %bitcast.28), channel_id=1, source_target_pairs={{0,1},{1,0},{2,3},{3,2},{4,5},{5,4},{6,7},{7,6},{8,9},{9,8},{10,11... | collective-permute-start | bytes 786440 | tf_op jit(solution)/shard_map/ppermute | solution.py:574

commit v9 on v8

--- a/solution.py
+++ b/solution.py
@@ -70,12 +70,46 @@
     return [jnp.concatenate(found, 0) for found in spread]
 
 
+def turn_in(rows_minor, in_ref, out_ref, tiles, square):
+    channels = ENTRY_CHANNELS
+    rows, features = in_ref.shape
+    count = features // LANES
+    for tile in range(count):
+        tiles[tile * rows : (tile + 1) * rows, :] = in_ref[:, tile * LANES : (tile + 1) * LANES]
+    for group in range(rows // PACK):
+        found = [tiles[strided(group * PACK + k, count, rows), :] for k in range(PACK)]
+        for part in range(PACK):
+            lanes = slice(part * channels, (part + 1) * channels)
+            square[group, strided(part, count, PACK), :] = jnp.concatenate(
+                [values[:, lanes] for values in found], 1
+            )
+        turned = square[group].T
+        if rows_minor:
+            for k in range(PACK):
+                out_ref[strided(group * PACK + k, channels, rows), :] = turned[
+                    k * channels : (k + 1) * channels
+                ]
+        else:
+            out_ref[group * LANES : (group + 1) * LANES, :] = turned
+
+
+def prepare_kernel(
+    cotangent_hbm, right_ref, left_ref, right_out, left_out, send_ref, tiles, square, semaphore
+):
+    other = 1 - lax.rem(lax.axis_index("blk"), 2)
+    copy = pltpu.make_async_copy(cotangent_hbm.at[:, :, other], send_ref, semaphore)
+    copy.start()
+    turn_in(True, right_ref, right_out, tiles.at[0], square.at[0])
+    turn_in(False, left_ref, left_out, tiles.at[1], square.at[1])
+    copy.wait()
+
+
 def turn_right_kernel(parts, *refs):
     part_refs, (out_ref, total, square, tiles) = refs[:parts], refs[parts:]
     channels = ENTRY_CHANNELS
     rows, features = out_ref.shape
     count = features // LANES
-    total[...] = functools.reduce(jnp.add, [ref[...] for ref in part_refs])
+    total[...] = functools.reduce(jnp.add, [ref[0] for ref in part_refs])
     for group in range(rows // PACK):
         stacked = [total[strided(group * PACK + k, channels, rows), :] for k in range(PACK)]
         square[...] = jnp.concatenate(stacked, 0).T
@@ -182,7 +216,7 @@
 
 
 def right_kernel(blocks, weight_ref, cotangent_ref, left_ref, partial_ref, peer_ref, *refs):
-    out_refs, (weight_cat, left_flip) = refs[:blocks], refs[blocks:]
+    keep_ref, send_ref, weight_cat, left_flip = refs
     depth = cotangent_ref.shape[2]
     fold = fold_of(blocks * depth)
     lanes = fold * blocks * depth
@@ -197,9 +231,16 @@
                 for slot in range(blocks):
                     start = (place * blocks + slot) * depth
                     row = pl.multiple_of(((2 * step + part) * fold + place) * depth, depth)
-                    out_refs[slot][pl.ds(row, depth), :] = turned[start : start + depth]
+                    out_ref = send_ref if slot % 2 else keep_ref
+                    out_ref[slot // 2, pl.ds(row, depth), :] = turned[start : start + depth]
 
     right_phase(left_ref, peer_ref, left_flip, store)
+
+
+def halve_kernel(keep_ref, found_ref, keep_out, send_out):
+    for slot in range(keep_ref.shape[0]):
+        out_ref = send_out if slot % 2 else keep_out
+        out_ref[slot // 2] = keep_ref[slot] + found_ref[slot]
 
 
 def right_rows(right_refs, step, fold, depth):
@@ -322,11 +363,9 @@
         ref[...] = own_ref[slot] + other_ref[slot]
 
 
-def pair_kernel(final, blocks, outer_hbm, weight_ref, *refs):
-    if final:
-        other_ref, out_ref, outer_ref, weight_flip, weight_rows, semaphores = refs
-    else:
-        out_ref, outer_ref, weight_flip, weight_rows, semaphores = refs
+def pair_kernel(
+    blocks, outer_hbm, weight_ref, out_ref, outer_ref, weight_flip, weight_rows, semaphores
+):
     channels = ENTRY_CHANNELS
     depth, pairs = out_ref.shape[2:]
     count = outer_ref.shape[0]
@@ -347,7 +386,7 @@
     flip_high, flip_low = halves(weight_rows[...].T)
     weight_flip[:wide, :] = flip_high
     weight_flip[wide:, :] = flip_low
-    slots = own_slots(blocks) if final else peer_slots(blocks)
+    slots = peer_slots(blocks)
 
     def step_of(pair, carry):
         copy_of(pair).wait()
@@ -364,12 +403,21 @@
             row = 2 * pair + part
             for slot in range(blocks):
                 out_ref[row, slots[slot]] = turned[slot * depth : (slot + 1) * depth]
-                if final:
-                    other = 2 * slot + 1 - lax.rem(lax.axis_index("blk"), 2)
-                    out_ref[row, other] = other_ref[row, slot]
         return carry
 
     lax.fori_loop(0, count, step_of, 0)
+
+
+def merge_kernel(own_ref, other_ref, out_ref, semaphores):
+    parity = lax.rem(lax.axis_index("blk"), 2)
+    copies = [
+        pltpu.make_async_copy(ref, out_ref.at[:, :, side], semaphores.at[at])
+        for at, (ref, side) in enumerate(((own_ref, parity), (other_ref, 1 - parity)))
+    ]
+    for copy in copies:
+        copy.start()
+    for copy in copies:
+        copy.wait()
 
 
 def spread_sum_kernel(in_ref, out_ref):
@@ -444,19 +492,26 @@
     limit = 20 * MIB * max(1, blocks * depth * fold // LANES * 2 // fold)
     large = functools.partial(call, limit=limit)
 
-    right = alignment_right.reshape(depth, sequences, channels).transpose(2, 0, 1)
-    right = right.reshape(channels * depth, sequences)
+    by_side = cotangent.reshape(rows, blocks, 2, depth, pairs)
+    right, left, cotangent_send = call(
+        prepare_kernel,
+        [
+            shape(channels * depth, sequences),
+            shape(rows * channels, sequences),
+            shape(rows, blocks, depth, pairs),
+        ],
+        [
+            pltpu.VMEM((2, rows * features // LANES, LANES), F32),
+            pltpu.VMEM((2, rows // PACK, LANES, LANES), F32),
+            pltpu.SemaphoreType.DMA,
+        ],
+        name="prepare",
+        far=[0],
+    )(by_side, alignment_right, alignment_left)
     rights = [right]
     for slot in range(1, blocks):
         rights.append(lax.ppermute(right, "blk", slot_moves[slot]))
-
-    by_side = cotangent.reshape(rows, blocks, 2, depth, pairs)
-    parity = lax.rem(lax.axis_index("blk"), 2)
-    cotangent_peer = lax.ppermute(
-        jnp.where(parity == 0, by_side[:, :, 1], by_side[:, :, 0]), "blk", partner
-    )
-    left = alignment_left.reshape(rows, sequences, channels).transpose(0, 2, 1)
-    left = left.reshape(rows * channels, sequences)
+    cotangent_peer = lax.ppermute(cotangent_send, "blk", partner)
     left_peer = lax.ppermute(left, "blk", partner)
 
     factor = shape(row_pairs, tall, 4 * lanes, kind=BF16)
@@ -469,15 +524,14 @@
         [weight_scratch, flip_scratch],
         "gradient_own",
     )(projection_matrix, cotangent, left)
-    grad_peer, *right_parts = large(
+    right_half = shape(blocks // 2, channels * depth, sequences)
+    grad_peer, right_keep, right_send = large(
         functools.partial(right_kernel, blocks),
-        [factor] + [shape(channels * depth, sequences)] * blocks,
+        [factor, right_half, right_half],
         [weight_scratch, flip_scratch],
         "right_parts",
     )(projection_matrix, cotangent_peer, left_peer, partial)
-    right_found = [right_parts[0]]
-    for slot in range(1, blocks):
-        right_found.append(lax.ppermute(right_parts[slot], "blk", slot_moves[slot]))
+    right_send = lax.ppermute(right_send, "blk", slot_moves[1])
 
     vmem = pl.BlockSpec(memory_space=pltpu.VMEM)
     hbm = pl.BlockSpec(memory_space=pltpu.HBM)
@@ -491,7 +545,7 @@
             pltpu.SemaphoreType.DMA((steps // 2, 2)),
         ],
         "weight",
-        after=[right_parts[0]],
+        after=[right_keep],
         out_specs=[vmem, vmem, hbm, hbm],
     )(left, left_peer, cotangent, cotangent_peer, *rights)
     sent = lax.ppermute(send, "inner", cores)
@@ -508,15 +562,22 @@
         after=[keep],
     )(grad_own, grad_peer, *rights)
     left_other = lax.ppermute(left_other, "blk", partner)
-    keep, left_own = lax.optimization_barrier((keep, left_own))
+    slot = 2
+    while slot < blocks:
+        part = shape(blocks // (2 * slot), channels * depth, sequences)
+        right_keep, right_send = call(
+            halve_kernel, [part, part], name="right_halve", after=[left_own]
+        )(right_keep, right_send)
+        right_send = lax.ppermute(right_send, "blk", slot_moves[slot])
+        slot = 2 * slot
+    keep, left_own, right_keep = lax.optimization_barrier((keep, left_own, right_keep))
     members = count * inner // 2
     pieces = (keep + sent).reshape(members, outer // 2 // members, pairs)
 
-    def pair(values, others, after, name):
-        final = bool(others)
+    def pair(values, after, name):
         return large(
-            functools.partial(pair_kernel, final, blocks),
-            shape(rows, count if final else blocks, depth, pairs),
+            functools.partial(pair_kernel, blocks),
+            shape(rows, blocks, depth, pairs),
             [
                 factor_scratch,
                 pltpu.VMEM((2 * fold * pairs, tall), BF16),
@@ -526,20 +587,24 @@
             name,
             far=[0],
             after=after,
-        )(values, projection_matrix, *others)
-
-    pair_own_rows = pair(outer_peer, [], [pieces], "pair_peer")
-    pair_peer = lax.ppermute(pair_own_rows, "blk", partner)
+        )(values, projection_matrix)
+
+    pair_other = pair(outer_peer, [pieces], "pair_peer")
+    pair_found = lax.ppermute(pair_other, "blk", partner)
+    pair_own = pair(outer_own, [pair_other], "pair_own")
 
     pieces = lax.all_to_all(pieces, everyone, 0, 0, axis_index_groups=core_groups)
-    pieces = call(
-        spread_sum_kernel, shape(*pieces.shape), name="weight_sum", after=[pair_own_rows]
-    )(pieces)
-    pieces = lax.all_to_all(pieces, everyone, 0, 0, axis_index_groups=core_groups)
-
     left_found = call(
         left_add_kernel, [shape(size, rows * channels)] * inner, name="left_add"
     )(left_own, left_other)
+    pieces = call(
+        spread_sum_kernel,
+        shape(*pieces.shape),
+        name="weight_sum",
+        after=[pair_own, left_found[0], right_send],
+    )(pieces)
+    pieces = lax.all_to_all(pieces, everyone, 0, 0, axis_index_groups=core_groups)
+
     left_found = [
         lax.ppermute(part, "inner", inner_moves[slot]) if slot else part
         for slot, part in enumerate(left_found)
@@ -555,7 +620,7 @@
     )(*left_found)
 
     grad_right = call(
-        functools.partial(turn_right_kernel, blocks),
+        functools.partial(turn_right_kernel, 2),
         shape(depth, features),
         [
             pltpu.VMEM((channels * depth, sequences), F32),
@@ -563,9 +628,16 @@
             pltpu.VMEM((depth * features // LANES, LANES), F32),
         ],
         name="turn_right",
-    )(*right_found)
-
-    pair_update = pair(outer_own, [pair_peer], [], "pair_own")
+    )(right_keep, right_send)
+
+    pair_update = call(
+        merge_kernel,
+        pltpu.HBM(by_side.shape, F32),
+        [pltpu.SemaphoreType.DMA((2,))],
+        "merge",
+        out_specs=hbm,
+    )(pair_own, pair_found)
+    pair_update = pair_update.reshape(cotangent.shape)
 
     pieces, pair_update, grad_left, grad_right = lax.optimization_barrier(
         (pieces, pair_update, grad_left, grad_right)

time: 113 us -> 118 us (1.044)
  starting transfers between devices: 27.3 us -> 31.2 us
  waiting for transfers between devices: 34.6 us -> 36.7 us
  other arithmetic: 2.15 us -> 0.73 us
  local copies, waits for them, and re-layouts: 6.68 us -> 5.3 us
    ppermute x3, waiting for transfers between devices: 7.85 us -> 19.5 us  [local(): rights.append(lax.ppermute(right, 'blk', slot_moves[slot]))]
    ppermute x1, waiting for transfers between devices: 7.07 us -> 0.01 us  [local(): left_other = lax.ppermute(left_other, 'blk', partner)]
    ppermute x5 -> x4, waiting for transfers between devices: 11.5 us -> 5.53 us  [the longest x1 5.52 us: local(): right_send = lax.ppermute(right_send, 'blk', slot_moves[slot])]
    unnamed x6 -> x14, local copies, waits for them, and re-layouts: 0.01 us -> 5.3 us
    ppermute x1, waiting for transfers between devices: 0.04 us -> 5.21 us  [local(): left_peer = lax.ppermute(left, 'blk', partner)]
    reshape x2 -> x0, local copies, waits for them, and re-layouts: 3.59 us -> none  [the longest x1 2.27 us: local(): left = alignment_left.reshape(rows, sequences, channels).transpose(0, 2, 1)]
    all_to_all x2, waiting for transfers between devices: 3.57 us -> 0.01 us  [local(): lax.all_to_all(pieces, everyone, 0, 0, axis_index_groups=core_groups)]
    transpose x2 -> x0, local copies, waits for them, and re-layouts: 3.08 us -> none  [the longest x1 1.55 us: local(): alignment_right.reshape(depth, sequences, channels).transpose(2, 0, 1)]
  transfers between devices with their start and end apart: 17 -> 16, of which waited for: 7 -> 7; matrix products, arithmetic and copies ran while one was open for 6% -> 0% of each run, Pallas kernels for 27% -> 34%
where the time goes in v9:
time: 118 us; the launch traced here: 117 us
  Pallas kernels  42.3 us (36%)
  waiting for transfers between devices  36.7 us (31%)
  starting transfers between devices  31.2 us (26%)
  local copies, waits for them, and re-layouts  5.3 us (4%)
    pallas_call x14, Pallas kernels, run(): pl.pallas_call(lambda *refs: kernel(*refs[len(after):]), out_shape=out_sh...  42.3 us
    ppermute x3, waiting for transfers between devices, local(): rights.append(lax.ppermute(right, 'blk', slot_moves[slot]))  19.5 us
    all_to_all x2, starting transfers between devices, local(): lax.all_to_all(pieces, everyone, 0, 0, axis_index_groups=core_groups)  11.4 us
    ppermute x3, starting transfers between devices, local(): rights.append(lax.ppermute(right, 'blk', slot_moves[slot]))  7.12 us
    ppermute x1, waiting for transfers between devices, local(): right_send = lax.ppermute(right_send, 'blk', slot_moves[slot])  5.52 us
    unnamed x14, local copies, waits for them, and re-layouts  5.3 us
    ppermute x3, waiting for transfers between devices, local(): lax.ppermute(part, 'inner', inner_moves[slot])  5.3 us
    ppermute x1, waiting for transfers between devices, local(): left_peer = lax.ppermute(left, 'blk', partner)  5.21 us
  transfers between devices with their start and end apart: 16, of which 7 were waited for; matrix products, arithmetic and copies ran while one was open for 0% of the time, Pallas kernels for 34%

profile of v9, /device:TPU:0, one launch (start us, length us, event | category | flops | bytes accessed | tf_op | source)
XLA Modules:
  0.0 117.0 jit_solution(3942813941294018956)
XLA Ops:
  0.6 0.0 copy-start.1
  0.6 0.0 copy-start.5
  0.7 1.0 copy-done.5
  1.7 0.0 copy-start.6
  1.7 0.9 copy-done.6
  2.6 1.7 %prepare.1 = (f32[512,128]{1,0:T(8,128)S(1)}, f32[512,128]{1,0:T(8,128)S(1)}, f32[16,4,16,128]{3,2,1,0:T(8,128)S(1)}) custom-call(f32[16,4,2,16,128]{4,3,2,1,0:T(8,128)} %bitcast.4, f32[16,4096]{1,0:T(8,128)S(1)} %copy-done.5, f32[16,4096]{1,0:T(8,128)S(1)} %copy-done.6), custom_call_target="tpu_custom_call" | custom-call | flops 1 | bytes 1 | tf_op jit(solution)/shard_map/prepare/pallas_call | solution.py:456
  4.4 3.0 %collective-permute-start = (f32[16,4,16,128]{3,2,1,0:T(8,128)S(1)}, f32[16,4,16,128]{3,2,1,0:T(8,128)S(1)}, u32[]{:S(2)}, u32[]{:S(2)}) collective-permute-start(f32[16,4,16,128]{3,2,1,0:T(8,128)S(1)} %get-tuple-element.31), channel_id=1, source_target_pairs={{0,4},{4,0},{8,12},{12,8},{16,20},{20,16},{24,28},{28,24},{1,5},{5... | collective-permute-start | bytes 1572872 | tf_op jit(solution)/shard_map/ppermute | solution.py:514
  7.4 0.1 collective-permute-start.1
  7.5 4.0 %collective-permute-start.4 = (f32[512,128]{1,0:T(8,128)S(1)}, f32[512,128]{1,0:T(8,128)S(1)}, u32[]{:S(2)}, u32[]{:S(2)}) collective-permute-start(f32[512,128]{1,0:T(8,128)S(1)} %get-tuple-element.35.refs_5_.refs_3_), channel_id=1, source_target_pairs={{0,24},{4,28},{8,16},{12,20},{16,8},{20,12},{24,0},{28,4},{1,25},{... | collective-permute-start | bytes 786440 | tf_op jit(solution)/shard_map/ppermute | solution.py:513
  11.5 0.0 copy-start
  11.5 1.2 %copy-done = f32[16,8,16,128]{3,2,1,0:T(8,128)S(1)} copy-done((f32[16,8,16,128]{3,2,1,0:T(8,128)S(1)}, f32[16,8,16,128]{3,2,1,0:T(8,128)}, u32[]{:S(2)}) %copy-start) | copy-done | bytes 1048600
  12.7 0.0 copy-start.2
  12.7 1.0 copy-done.2
  13.8 5.9 %gradient_own.1 = (bf16[8,512,512]{2,1,0:T(8,128)(2,1)S(1)}, f32[8,128,256]{2,1,0:T(8,128)S(1)}) custom-call(f32[1024,128]{1,0:T(8,128)S(1)} %copy-done.2, f32[16,8,16,128]{3,2,1,0:T(8,128)S(1)} %copy-done, f32[512,128]{1,0:T(8,128)S(1)} %get-tuple-element.32.refs_2_.refs_1_), custom_call_target="tpu_custom_call" | custom-call | flops 1 | bytes 1 | tf_op jit(solution)/shard_map/gradient_own/pallas_call | solution.py:456
  19.7 5.2 %collective-permute-done.1.refs_2_ = f32[512,128]{1,0:T(8,128)S(1)} collective-permute-done((f32[512,128]{1,0:T(8,128)S(1)}, f32[512,128]{1,0:T(8,128)S(1)}, u32[]{:S(2)}, u32[]{:S(2)}) %collective-permute-start.1) | collective-permute-done | bytes 262176 | tf_op jit(solution)/shard_map/ppermute | solution.py:515
  24.9 0.0 collective-permute-done.refs_1_.refs_4_
  24.9 0.0 copy-start.3
  24.9 1.0 copy-done.3
  26.0 6.5 %right_parts.1 = (bf16[8,512,512]{2,1,0:T(8,128)(2,1)S(1)}, f32[2,512,128]{2,1,0:T(8,128)S(1)}, f32[2,512,128]{2,1,0:T(8,128)S(1)}) custom-call(f32[1024,128]{1,0:T(8,128)S(1)} %copy-done.3, f32[16,4,16,128]{3,2,1,0:T(8,128)S(1)} %collective-permute-done.refs_1_.refs_4_, f32[512,128]{1,0:T(8,128)S(1)} %collective-permute-done.1.refs_2_, ...), custom_call_target="tpu_custom_call" | custom-call | flops 1 | bytes 1 | tf_op jit(solution)/shard_map/right_parts/pallas_call | solution.py:456
  32.5 1.8 %collective-permute-start.5 = (f32[2,512,128]{2,1,0:T(8,128)S(1)}, f32[2,512,128]{2,1,0:T(8,128)S(1)}, u32[]{:S(2)}, u32[]{:S(2)}) collective-permute-start(f32[2,512,128]{2,1,0:T(8,128)S(1)} %get-tuple-element.40), channel_id=1, source_target_pairs={{0,8},{4,12},{8,0},{12,4},{16,24},{20,28},{24,16},{28,20},{1,9},{5... | collective-permute-start | bytes 1572872 | tf_op jit(solution)/shard_map/ppermute | solution.py:534
  34.3 2.6 %collective-permute-start.3 = (f32[512,128]{1,0:T(8,128)S(1)}, f32[512,128]{1,0:T(8,128)S(1)}, u32[]{:S(2)}, u32[]{:S(2)}) collective-permute-start(f32[512,128]{1,0:T(8,128)S(1)} %get-tuple-element.35.refs_5_.refs_3_), channel_id=1, source_target_pairs={{0,16},{4,20},{8,24},{12,28},{16,0},{20,4},{24,8},{28,12},{1,17},{... | collective-permute-start | bytes 786440 | tf_op jit(solution)/shard_map/ppermute | solution.py:513
  36.9 0.4 collective-permute-start.2
  37.4 0.0 collective-permute-done.4.refs_8_.refs_6_
  37.4 14.9 %collective-permute-done.3.refs_7_.refs_5_ = f32[512,128]{1,0:T(8,128)S(1)} collective-permute-done((f32[512,128]{1,0:T(8,128)S(1)}, f32[512,128]{1,0:T(8,128)S(1)}, u32[]{:S(2)}, u32[]{:S(2)}) %collective-permute-start.3) | collective-permute-done | bytes 262176 | tf_op jit(solution)/shard_map/ppermute | solution.py:513
  52.3 4.6 %collective-permute-done.2.refs_6_.refs_4_ = f32[512,128]{1,0:T(8,128)S(1)} collective-permute-done((f32[512,128]{1,0:T(8,128)S(1)}, f32[512,128]{1,0:T(8,128)S(1)}, u32[]{:S(2)}, u32[]{:S(2)}) %collective-permute-start.2) | collective-permute-done | bytes 262176 | tf_op jit(solution)/shard_map/ppermute | solution.py:513
  56.9 0.0 copy-done.1
  56.9 9.3 %weight.1 = (f32[512,128]{1,0:T(8,128)S(1)}, f32[512,128]{1,0:T(8,128)S(1)}, bf16[8,512,512]{2,1,0:T(8,128)(2,1)}, bf16[8,512,512]{2,1,0:T(8,128)(2,1)}) custom-call(f32[2,512,128]{2,1,0:T(8,128)S(1)} %get-tuple-element.34.refs_0_.refs_1_, f32[512,128]{1,0:T(8,128)S(1)} %get-tuple-element.32.refs_2_.refs_1_, f32[512,128]{1,0:T(8,128)S(1)} %collective-permute-done.1.refs_2_, ...), custom_call_target="tpu_custom_call" | custom-call | flops 1 | bytes 1 | tf_op jit(solution)/shard_map/weight/pallas_call | solution.py:456
  66.2 0.1 collective-permute-start.6
  66.3 0.0 copy-start.4
  66.3 3.1 %left_parts.1 = (f32[4,32,512]{2,1,0:T(8,128)S(1)}, f32[4,32,512]{2,1,0:T(8,128)S(1)}) custom-call(f32[512,128]{1,0:T(8,128)S(1)} %get-tuple-element.42.refs_0_, bf16[8,512,512]{2,1,0:T(8,128)(2,1)S(1)} %get-tuple-element.37.refs_1_, bf16[8,512,512]{2,1,0:T(8,128)(2,1)S(1)} %get-tuple-element.38.refs_2_, f32[512,128]{1,0:T(8,128)S(1)} %get-tuple-element.35.refs_5_.refs_3_, ...), custom_call_target="tpu_custom_call" | custom-call | flops 1 | bytes 1 | tf_op jit(solution)/shard_map/left_parts/pallas_call | solution.py:456
  69.4 0.0 collective-permute-done.5.refs_2_
  69.4 0.8 right_halve.1
  70.2 0.0 collective-permute-done.6
  70.2 0.7 add.3
  70.9 6.8 %all-to-all-start = ((f32[16,32,128]{2,1,0:T(8,128)}), f32[16,32,128]{2,1,0:T(8,128)S(1)}, u32[]{:S(2)}, u32[]{:S(2)}) async-start(f32[16,32,128]{2,1,0:T(8,128)} %bitcast.1.refs_0_), calls=%async_computation | async-start | bytes 524288 | tf_op jit(solution)/shard_map/all_to_all | solution.py:596
  77.7 1.9 %collective-permute-start.7 = (f32[4,32,512]{2,1,0:T(8,128)S(1)}, f32[4,32,512]{2,1,0:T(8,128)S(1)}, u32[]{:S(2)}, u32[]{:S(2)}) collective-permute-start(f32[4,32,512]{2,1,0:T(8,128)S(1)} %get-tuple-element.47), channel_id=1, source_target_pairs={{0,4},{4,0},{8,12},{12,8},{16,20},{20,16},{24,28},{28,24},{1,5},{5... | collective-permute-start | bytes 786440 | tf_op jit(solution)/shard_map/ppermute | solution.py:564
  79.7 2.3 %collective-permute-start.8 = (f32[1,512,128]{2,1,0:T(8,128)}, f32[1,512,128]{2,1,0:T(8,128)S(1)}, u32[]{:S(2)}, u32[]{:S(2)}) collective-permute-start(f32[1,512,128]{2,1,0:T(8,128)} %get-tuple-element.49), channel_id=1, source_target_pairs={{0,16},{4,20},{8,24},{12,28},{16,0},{20,4},{24,8},{28,12},{1,17},{... | collective-permute-start | bytes 786440 | tf_op jit(solution)/shard_map/ppermute | solution.py:571
  82.0 0.0 copy-done.4
  82.0 5.1 %pair_peer.1.refs_0_ = f32[16,4,16,128]{3,2,1,0:T(8,128)S(1)} custom-call(f32[16,32,128]{2,1,0:T(8,128)} %bitcast.1.refs_0_, bf16[8,512,512]{2,1,0:T(8,128)(2,1)} %get-tuple-element.44.refs_1_, f32[1024,128]{1,0:T(8,128)S(1)} %copy-done.4), custom_call_target="tpu_custom_call" | custom-call | flops 1 | bytes 1 | tf_op jit(solution)/shard_map/pair_peer/pallas_call | solution.py:456
  87.1 0.6 collective-permute-start.9
  87.7 5.1 %pair_own.1.refs_0_ = f32[16,4,16,128]{3,2,1,0:T(8,128)S(1)} custom-call(f32[16,4,16,128]{3,2,1,0:T(8,128)S(1)} %pair_peer.1.refs_0_, bf16[8,512,512]{2,1,0:T(8,128)(2,1)} %get-tuple-element.45.refs_1_, f32[1024,128]{1,0:T(8,128)S(1)} %copy-done.4), custom_call_target="tpu_custom_call" | custom-call | flops 1 | bytes 1 | tf_op jit(solution)/shard_map/pair_own/pallas_call | solution.py:456
  92.8 0.0 collective-permute-done.7.refs_1_
  92.8 5.5 %collective-permute-done.8.refs_2_.refs_1_ = f32[1,512,128]{2,1,0:T(8,128)S(1)} collective-permute-done((f32[1,512,128]{2,1,0:T(8,128)}, f32[1,512,128]{2,1,0:T(8,128)S(1)}, u32[]{:S(2)}, u32[]{:S(2)}) %collective-permute-start.8) | collective-permute-done | bytes 262176 | tf_op jit(solution)/shard_map/ppermute | solution.py:571
  98.4 0.0 all-to-all-done.refs_3_
  98.4 0.7 weight_sum.1
  99.1 4.6 %all-to-all-start.1 = ((f32[16,32,128]{2,1,0:T(8,128)}), f32[16,32,128]{2,1,0:T(8,128)S(1)}, u32[]{:S(2)}, u32[]{:S(2)}) async-start(f32[16,32,128]{2,1,0:T(8,128)} %weight_sum.1), calls=%async_computation.1 | async-start | bytes 524288 | tf_op jit(solution)/shard_map/all_to_all | solution.py:606
  103.8 0.1 collective-permute-start.10
  103.8 1.9 %collective-permute-start.11 = (f32[32,512]{1,0:T(8,128)S(1)}, f32[32,512]{1,0:T(8,128)S(1)}, u32[]{:S(2)}, u32[]{:S(2)}) collective-permute-start(f32[32,512]{1,0:T(8,128)S(1)} %get-tuple-element.51), channel_id=1, source_target_pairs={{0,2},{1,3},{2,0},{3,1},{4,6},{5,7},{6,4},{7,5},{8,10},{9,11},{10,... | collective-permute-start | bytes 196616 | tf_op jit(solution)/shard_map/ppermute | solution.py:609
  105.8 0.1 collective-permute-start.12
  105.8 0.0 collective-permute-done.10.refs_1_
  105.8 4.8 %collective-permute-done.11.refs_2_ = f32[32,512]{1,0:T(8,128)S(1)} collective-permute-done((f32[32,512]{1,0:T(8,128)S(1)}, f32[32,512]{1,0:T(8,128)S(1)}, u32[]{:S(2)}, u32[]{:S(2)}) %collective-permute-start.11) | collective-permute-done | bytes 65568 | tf_op jit(solution)/shard_map/ppermute | solution.py:609
  110.7 0.5 collective-permute-done.12.refs_3_
  111.1 0.8 turn_left.1
  111.9 1.2 turn_right.1
  113.1 0.0 collective-permute-done.9.refs_1_
  113.1 1.0 merge.1
  114.1 0.0 all-to-all-done.1
  114.1 0.7 collective-permute-start.13
  114.7 1.2 collective-permute-done.13.refs_1_
  115.9 1.1 place.1
  (1 shorter events, 0.0 us)
Async XLA Ops:
  0.6 56.2 %copy-start.1 = (f32[16,8,16,128]{3,2,1,0:T(8,128)S(1)}, f32[16,8,16,128]{3,2,1,0:T(8,128)}, u32[]{:S(2)}) copy-start(f32[16,8,16,128]{3,2,1,0:T(8,128)} %refs_3_.1) | copy-start | bytes 3145732
  0.6 1.0 copy-start.5
  1.7 0.9 copy-start.6
  4.4 20.6 %collective-permute-start = (f32[16,4,16,128]{3,2,1,0:T(8,128)S(1)}, f32[16,4,16,128]{3,2,1,0:T(8,128)S(1)}, u32[]{:S(2)}, u32[]{:S(2)}) collective-permute-start(f32[16,4,16,128]{3,2,1,0:T(8,128)S(1)} %get-tuple-element.31), channel_id=1, source_target_pairs={{0,4},{4,0},{8,12},{12,8},{16,20},{20,16},{24,28},{28,24},{1,5},{5... | collective-permute-start | bytes 1572872 | tf_op jit(solution)/shard_map/ppermute | solution.py:514
  7.4 17.5 %collective-permute-start.1 = (f32[512,128]{1,0:T(8,128)S(1)}, f32[512,128]{1,0:T(8,128)S(1)}, u32[]{:S(2)}, u32[]{:S(2)}) collective-permute-start(f32[512,128]{1,0:T(8,128)S(1)} %get-tuple-element.32.refs_2_.refs_1_), channel_id=1, source_target_pairs={{0,4},{4,0},{8,12},{12,8},{16,20},{20,16},{24,28},{28,24},{1,5},{5... | collective-permute-start | bytes 786440 | tf_op jit(solution)/shard_map/ppermute | solution.py:515
  7.5 29.9 %collective-permute-start.4 = (f32[512,128]{1,0:T(8,128)S(1)}, f32[512,128]{1,0:T(8,128)S(1)}, u32[]{:S(2)}, u32[]{:S(2)}) collective-permute-start(f32[512,128]{1,0:T(8,128)S(1)} %get-tuple-element.35.refs_5_.refs_3_), channel_id=1, source_target_pairs={{0,24},{4,28},{8,16},{12,20},{16,8},{20,12},{24,0},{28,4},{1,25},{... | collective-permute-start | bytes 786440 | tf_op jit(solution)/shard_map/ppermute | solution.py:513
  11.5 1.2 %copy-start = (f32[16,8,16,128]{3,2,1,0:T(8,128)S(1)}, f32[16,8,16,128]{3,2,1,0:T(8,128)}, u32[]{:S(2)}) copy-start(f32[16,8,16,128]{3,2,1,0:T(8,128)} %refs_3_.1) | copy-start | bytes 3145732
  12.7 1.0 copy-start.2
  24.9 1.0 copy-start.3
  32.5 37.0 %collective-permute-start.5 = (f32[2,512,128]{2,1,0:T(8,128)S(1)}, f32[2,512,128]{2,1,0:T(8,128)S(1)}, u32[]{:S(2)}, u32[]{:S(2)}) collective-permute-start(f32[2,512,128]{2,1,0:T(8,128)S(1)} %get-tuple-element.40), channel_id=1, source_target_pairs={{0,8},{4,12},{8,0},{12,4},{16,24},{20,28},{24,16},{28,20},{1,9},{5... | collective-permute-start | bytes 1572872 | tf_op jit(solution)/shard_map/ppermute | solution.py:534
  34.3 18.0 %collective-permute-start.3 = (f32[512,128]{1,0:T(8,128)S(1)}, f32[512,128]{1,0:T(8,128)S(1)}, u32[]{:S(2)}, u32[]{:S(2)}) collective-permute-start(f32[512,128]{1,0:T(8,128)S(1)} %get-tuple-element.35.refs_5_.refs_3_), channel_id=1, source_target_pairs={{0,16},{4,20},{8,24},{12,28},{16,0},{20,4},{24,8},{28,12},{1,17},{... | collective-permute-start | bytes 786440 | tf_op jit(solution)/shard_map/ppermute | solution.py:513
  36.9 19.9 %collective-permute-start.2 = (f32[512,128]{1,0:T(8,128)S(1)}, f32[512,128]{1,0:T(8,128)S(1)}, u32[]{:S(2)}, u32[]{:S(2)}) collective-permute-start(f32[512,128]{1,0:T(8,128)S(1)} %get-tuple-element.35.refs_5_.refs_3_), channel_id=1, source_target_pairs={{0,8},{4,12},{8,0},{12,4},{16,24},{20,28},{24,16},{28,20},{1,9},{5... | collective-permute-start | bytes 786440 | tf_op jit(solution)/shard_map/ppermute | solution.py:513
  66.2 4.0 %collective-permute-start.6 = (f32[512,128]{1,0:T(8,128)S(1)}, f32[512,128]{1,0:T(8,128)S(1)}, u32[]{:S(2)}, u32[]{:S(2)}) collective-permute-start(f32[512,128]{1,0:T(8,128)S(1)} %get-tuple-element.43), channel_id=1, source_target_pairs={{0,1},{1,0},{2,3},{3,2},{4,5},{5,4},{6,7},{7,6},{8,9},{9,8},{10,11... | collective-permute-start | bytes 786440 | tf_op jit(solution)/shard_map/ppermute | solution.py:551
  66.3 15.7 %copy-start.4 = (f32[1024,128]{1,0:T(8,128)S(1)}, f32[1024,128]{1,0:T(8,128)}, u32[]{:S(2)}) copy-start(f32[1024,128]{1,0:T(8,128)} %refs_2_.5) | copy-start | bytes 1572868
  70.9 27.5 %all-to-all-start = ((f32[16,32,128]{2,1,0:T(8,128)}), f32[16,32,128]{2,1,0:T(8,128)S(1)}, u32[]{:S(2)}, u32[]{:S(2)}) async-start(f32[16,32,128]{2,1,0:T(8,128)} %bitcast.1.refs_0_), calls=%async_computation | async-start | bytes 524288 | tf_op jit(solution)/shard_map/all_to_all | solution.py:596
  77.7 15.1 %collective-permute-start.7 = (f32[4,32,512]{2,1,0:T(8,128)S(1)}, f32[4,32,512]{2,1,0:T(8,128)S(1)}, u32[]{:S(2)}, u32[]{:S(2)}) collective-permute-start(f32[4,32,512]{2,1,0:T(8,128)S(1)} %get-tuple-element.47), channel_id=1, source_target_pairs={{0,4},{4,0},{8,12},{12,8},{16,20},{20,16},{24,28},{28,24},{1,5},{5... | collective-permute-start | bytes 786440 | tf_op jit(solution)/shard_map/ppermute | solution.py:564
  79.7 18.7 %collective-permute-start.8 = (f32[1,512,128]{2,1,0:T(8,128)}, f32[1,512,128]{2,1,0:T(8,128)S(1)}, u32[]{:S(2)}, u32[]{:S(2)}) collective-permute-start(f32[1,512,128]{2,1,0:T(8,128)} %get-tuple-element.49), channel_id=1, source_target_pairs={{0,16},{4,20},{8,24},{12,28},{16,0},{20,4},{24,8},{28,12},{1,17},{... | collective-permute-start | bytes 786440 | tf_op jit(solution)/shard_map/ppermute | solution.py:571
  87.1 26.0 %collective-permute-start.9 = (f32[16,4,16,128]{3,2,1,0:T(8,128)S(1)}, f32[16,4,16,128]{3,2,1,0:T(8,128)S(1)}, u32[]{:S(2)}, u32[]{:S(2)}) collective-permute-start(f32[16,4,16,128]{3,2,1,0:T(8,128)S(1)} %pair_peer.1.refs_0_), channel_id=1, source_target_pairs={{0,4},{4,0},{8,12},{12,8},{16,20},{20,16},{24,28},{28,24},{1,5},{5... | collective-permute-start | bytes 1572872 | tf_op jit(solution)/shard_map/ppermute | solution.py:593
  99.1 15.0 %all-to-all-start.1 = ((f32[16,32,128]{2,1,0:T(8,128)}), f32[16,32,128]{2,1,0:T(8,128)S(1)}, u32[]{:S(2)}, u32[]{:S(2)}) async-start(f32[16,32,128]{2,1,0:T(8,128)} %weight_sum.1), calls=%async_computation.1 | async-start | bytes 524288 | tf_op jit(solution)/shard_map/all_to_all | solution.py:606
  103.8 2.1 %collective-permute-start.10 = (f32[32,512]{1,0:T(8,128)S(1)}, f32[32,512]{1,0:T(8,128)S(1)}, u32[]{:S(2)}, u32[]{:S(2)}) collective-permute-start(f32[32,512]{1,0:T(8,128)S(1)} %get-tuple-element.50), channel_id=1, source_target_pairs={{0,1},{1,0},{2,3},{3,2},{4,5},{5,4},{6,7},{7,6},{8,9},{9,8},{10,11... | collective-permute-start | bytes 196616 | tf_op jit(solution)/shard_map/ppermute | solution.py:609
  103.8 6.8 %collective-permute-start.11 = (f32[32,512]{1,0:T(8,128)S(1)}, f32[32,512]{1,0:T(8,128)S(1)}, u32[]{:S(2)}, u32[]{:S(2)}) collective-permute-start(f32[32,512]{1,0:T(8,128)S(1)} %get-tuple-element.51), channel_id=1, source_target_pairs={{0,2},{1,3},{2,0},{3,1},{4,6},{5,7},{6,4},{7,5},{8,10},{9,11},{10,... | collective-permute-start | bytes 196616 | tf_op jit(solution)/shard_map/ppermute | solution.py:609
  105.8 5.4 %collective-permute-start.12 = (f32[32,512]{1,0:T(8,128)S(1)}, f32[32,512]{1,0:T(8,128)S(1)}, u32[]{:S(2)}, u32[]{:S(2)}) collective-permute-start(f32[32,512]{1,0:T(8,128)S(1)} %get-tuple-element.52), channel_id=1, source_target_pairs={{0,3},{1,2},{2,1},{3,0},{4,7},{5,6},{6,5},{7,4},{8,11},{9,10},{10,... | collective-permute-start | bytes 196616 | tf_op jit(solution)/shard_map/ppermute | solution.py:609
  114.1 1.8 %collective-permute-start.13 = (f32[512,128]{1,0:T(8,128)S(1)}, f32[512,128]{1,0:T(8,128)S(1)}, u32[]{:S(2)}, u32[]{:S(2)}) collective-permute-start(f32[512,128]{1,0:T(8,128)S(1)} %bitcast.5), channel_id=1, source_target_pairs={{0,1},{1,0},{2,3},{3,2},{4,5},{5,4},{6,7},{7,6},{8,9},{9,8},{10,11... | collective-permute-start | bytes 786440 | tf_op jit(solution)/shard_map/ppermute | solution.py:646

commit v10 on v9

--- a/solution.py
+++ b/solution.py
@@ -44,12 +44,7 @@
     )
 
 
-def own_slots(blocks):
-    here = lax.axis_index("blk")
-    return [lax.bitwise_xor(here, 2 * slot) for slot in range(blocks)]
-
-
-def peer_slots(blocks):
+def slots_of(blocks):
     here = lax.axis_index("blk") // 2
     return [lax.bitwise_xor(here, slot) for slot in range(blocks)]
 
@@ -94,14 +89,40 @@
 
 
 def prepare_kernel(
-    cotangent_hbm, right_ref, left_ref, right_out, left_out, send_ref, tiles, square, semaphore
+    cotangent_hbm,
+    right_hbm,
+    left_hbm,
+    weight_hbm,
+    right_out,
+    left_out,
+    send_out,
+    own_out,
+    weight_out,
+    inputs,
+    tiles,
+    square,
+    semaphores,
 ):
-    other = 1 - lax.rem(lax.axis_index("blk"), 2)
-    copy = pltpu.make_async_copy(cotangent_hbm.at[:, :, other], send_ref, semaphore)
-    copy.start()
-    turn_in(True, right_ref, right_out, tiles.at[0], square.at[0])
-    turn_in(False, left_ref, left_out, tiles.at[1], square.at[1])
-    copy.wait()
+    parity = lax.rem(lax.axis_index("blk"), 2)
+    moves = (
+        (right_hbm, inputs.at[0]),
+        (left_hbm, inputs.at[1]),
+        (cotangent_hbm.at[:, :, 1 - parity], send_out),
+        (cotangent_hbm.at[:, :, parity], own_out),
+        (weight_hbm, weight_out),
+    )
+    copies = [
+        pltpu.make_async_copy(source, target, semaphores.at[at])
+        for at, (source, target) in enumerate(moves)
+    ]
+    for copy in copies:
+        copy.start()
+    copies[0].wait()
+    turn_in(True, inputs.at[0], right_out, tiles.at[0], square.at[0])
+    copies[1].wait()
+    turn_in(False, inputs.at[1], left_out, tiles.at[1], square.at[1])
+    for copy in copies[2:]:
+        copy.wait()
 
 
 def turn_right_kernel(parts, *refs):
@@ -152,7 +173,10 @@
         )
 
 
-def gradient_phase(slots, fold, cotangent_ref, out_ref, weight_cat):
+def gradient_phase(blocks, cotangent_ref, out_ref, weight_cat):
+    fold = fold_of(blocks * cotangent_ref.shape[2])
+    slots = slots_of(blocks)
+
     def step_of(pair, carry):
         high, low = spread_of(cotangent_ref, pair, slots, fold)
         found = dot_rows(weight_cat[...], jnp.concatenate([high, high, low], 1))
@@ -162,10 +186,11 @@
     lax.fori_loop(0, out_ref.shape[0], step_of, 0)
 
 
-def gradient_kernel(blocks, weight_ref, cotangent_ref, left_ref, out_ref, partial_ref, weight_cat, left_flip):
-    fold = fold_of(blocks * cotangent_ref.shape[2])
-    prepare_weight(weight_ref, weight_cat, fold)
-    gradient_phase(own_slots(blocks), fold, cotangent_ref, out_ref, weight_cat)
+def gradient_kernel(
+    blocks, weight_ref, cotangent_ref, left_ref, out_ref, partial_ref, weight_cat, left_flip
+):
+    prepare_weight(weight_ref, weight_cat, fold_of(blocks * cotangent_ref.shape[2]))
+    gradient_phase(blocks, cotangent_ref, out_ref, weight_cat)
 
     def store(step, found):
         partial_ref[step] = found
@@ -215,13 +240,21 @@
     return jnp.concatenate([ref[...] for ref in left_refs], 0) * (1.0 / sequences)
 
 
-def right_kernel(blocks, weight_ref, cotangent_ref, left_ref, partial_ref, peer_ref, *refs):
-    keep_ref, send_ref, weight_cat, left_flip = refs
+def right_kernel(
+    blocks,
+    weight_cat,
+    cotangent_ref,
+    left_ref,
+    partial_ref,
+    peer_ref,
+    keep_ref,
+    send_ref,
+    left_flip,
+):
     depth = cotangent_ref.shape[2]
     fold = fold_of(blocks * depth)
     lanes = fold * blocks * depth
-    prepare_weight(weight_ref, weight_cat, fold)
-    gradient_phase(peer_slots(blocks), fold, cotangent_ref, peer_ref, weight_cat)
+    gradient_phase(blocks, cotangent_ref, peer_ref, weight_cat)
 
     def store(step, found):
         found = found + partial_ref[step]
@@ -297,11 +330,8 @@
 
     def weight_step(pair, carry):
         lefts, rights = [], []
-        for ref, cotangent_ref, slots in (
-            (own_ref, own_cotangent, own_slots(blocks)),
-            (peer_ref, peer_cotangent, peer_slots(blocks)),
-        ):
-            high, low = spread_of(cotangent_ref, pair, slots, fold)
+        for ref, cotangent_ref in ((own_ref, own_cotangent), (peer_ref, peer_cotangent)):
+            high, low = spread_of(cotangent_ref, pair, slots_of(blocks), fold)
             lefts += [ref[pair], ref[pair, :, : 2 * lanes]]
             rights += [high, high, low]
         total[...] += dot(jnp.concatenate(lefts, 1), jnp.concatenate(rights, 0))
@@ -364,7 +394,15 @@
 
 
 def pair_kernel(
-    blocks, outer_hbm, weight_ref, out_ref, outer_ref, weight_flip, weight_rows, semaphores
+    blocks,
+    outer_hbm,
+    weight_hbm,
+    out_ref,
+    outer_ref,
+    weight_ref,
+    weight_flip,
+    weight_rows,
+    semaphores,
 ):
     channels = ENTRY_CHANNELS
     depth, pairs = out_ref.shape[2:]
@@ -377,8 +415,11 @@
     def copy_of(pair):
         return pltpu.make_async_copy(outer_hbm.at[pair], outer_ref.at[pair], semaphores.at[pair])
 
+    weight_copy = pltpu.make_async_copy(weight_hbm, weight_ref, semaphores.at[count])
+    weight_copy.start()
     for pair in range(count):
         copy_of(pair).start()
+    weight_copy.wait()
     for step in range(channels // fold):
         weight_rows[step * channels : (step + 1) * channels, :] = folded_weight(
             weight_ref, step, fold
@@ -386,7 +427,7 @@
     flip_high, flip_low = halves(weight_rows[...].T)
     weight_flip[:wide, :] = flip_high
     weight_flip[wide:, :] = flip_low
-    slots = peer_slots(blocks)
+    slots = slots_of(blocks)
 
     def step_of(pair, carry):
         copy_of(pair).wait()
@@ -493,21 +534,25 @@
     large = functools.partial(call, limit=limit)
 
     by_side = cotangent.reshape(rows, blocks, 2, depth, pairs)
-    right, left, cotangent_send = call(
+    half_cotangent = shape(rows, blocks, depth, pairs)
+    right, left, cotangent_send, cotangent_own, weight = call(
         prepare_kernel,
         [
             shape(channels * depth, sequences),
             shape(rows * channels, sequences),
-            shape(rows, blocks, depth, pairs),
+            half_cotangent,
+            half_cotangent,
+            shape(outer, pairs),
         ],
         [
+            pltpu.VMEM((2, rows, features), F32),
             pltpu.VMEM((2, rows * features // LANES, LANES), F32),
             pltpu.VMEM((2, rows // PACK, LANES, LANES), F32),
-            pltpu.SemaphoreType.DMA,
+            pltpu.SemaphoreType.DMA((5,)),
         ],
         name="prepare",
-        far=[0],
-    )(by_side, alignment_right, alignment_left)
+        far=range(4),
+    )(by_side, alignment_right, alignment_left, projection_matrix)
     rights = [right]
     for slot in range(1, blocks):
         rights.append(lax.ppermute(right, "blk", slot_moves[slot]))
@@ -516,22 +561,21 @@
 
     factor = shape(row_pairs, tall, 4 * lanes, kind=BF16)
     factor_scratch = pltpu.VMEM(factor.shape, BF16)
-    weight_scratch = pltpu.VMEM((tall, 3 * fold * pairs), BF16)
+    weight_cat = shape(tall, 3 * fold * pairs, kind=BF16)
     flip_scratch = pltpu.VMEM((2 * sequences, rows * channels), BF16)
-    grad_own, partial = large(
+    grad_own, partial, weight_cat = large(
         functools.partial(gradient_kernel, blocks),
-        [factor, shape(steps // 2, sequences, 2 * lanes)],
-        [weight_scratch, flip_scratch],
+        [factor, shape(steps // 2, sequences, 2 * lanes), weight_cat],
+        [flip_scratch],
         "gradient_own",
-    )(projection_matrix, cotangent, left)
+    )(weight, cotangent_own, left)
     right_half = shape(blocks // 2, channels * depth, sequences)
     grad_peer, right_keep, right_send = large(
         functools.partial(right_kernel, blocks),
         [factor, right_half, right_half],
-        [weight_scratch, flip_scratch],
+        [flip_scratch],
         "right_parts",
-    )(projection_matrix, cotangent_peer, left_peer, partial)
-    right_send = lax.ppermute(right_send, "blk", slot_moves[1])
+    )(weight_cat, cotangent_peer, left_peer, partial)
 
     vmem = pl.BlockSpec(memory_space=pltpu.VMEM)
     hbm = pl.BlockSpec(memory_space=pltpu.HBM)
@@ -547,7 +591,7 @@
         "weight",
         after=[right_keep],
         out_specs=[vmem, vmem, hbm, hbm],
-    )(left, left_peer, cotangent, cotangent_peer, *rights)
+    )(left, left_peer, cotangent_own, cotangent_peer, *rights)
     sent = lax.ppermute(send, "inner", cores)
 
     size = sequences // inner
@@ -562,15 +606,16 @@
         after=[keep],
     )(grad_own, grad_peer, *rights)
     left_other = lax.ppermute(left_other, "blk", partner)
+    keep, left_own, right_send = lax.optimization_barrier((keep, left_own, right_send))
+    right_send = lax.ppermute(right_send, "blk", slot_moves[1])
     slot = 2
     while slot < blocks:
         part = shape(blocks // (2 * slot), channels * depth, sequences)
-        right_keep, right_send = call(
-            halve_kernel, [part, part], name="right_halve", after=[left_own]
-        )(right_keep, right_send)
+        right_keep, right_send = call(halve_kernel, [part, part], name="right_halve")(
+            right_keep, right_send
+        )
         right_send = lax.ppermute(right_send, "blk", slot_moves[slot])
         slot = 2 * slot
-    keep, left_own, right_keep = lax.optimization_barrier((keep, left_own, right_keep))
     members = count * inner // 2
     pieces = (keep + sent).reshape(members, outer // 2 // members, pairs)
 
@@ -580,29 +625,33 @@
             shape(rows, blocks, depth, pairs),
             [
                 factor_scratch,
+                pltpu.VMEM((outer, pairs), F32),
                 pltpu.VMEM((2 * fold * pairs, tall), BF16),
                 pltpu.VMEM((tall, fold * pairs), F32),
-                pltpu.SemaphoreType.DMA((row_pairs,)),
+                pltpu.SemaphoreType.DMA((row_pairs + 1,)),
             ],
             name,
-            far=[0],
+            far=[0, 1],
             after=after,
         )(values, projection_matrix)
 
     pair_other = pair(outer_peer, [pieces], "pair_peer")
     pair_found = lax.ppermute(pair_other, "blk", partner)
-    pair_own = pair(outer_own, [pair_other], "pair_own")
 
     pieces = lax.all_to_all(pieces, everyone, 0, 0, axis_index_groups=core_groups)
     left_found = call(
-        left_add_kernel, [shape(size, rows * channels)] * inner, name="left_add"
+        left_add_kernel,
+        [shape(size, rows * channels)] * inner,
+        name="left_add",
+        after=[pieces],
     )(left_own, left_other)
     pieces = call(
         spread_sum_kernel,
         shape(*pieces.shape),
         name="weight_sum",
-        after=[pair_own, left_found[0], right_send],
+        after=[pair_other, left_found[0], right_keep],
     )(pieces)
+    pair_own = pair(outer_own, [pieces], "pair_own")
     pieces = lax.all_to_all(pieces, everyone, 0, 0, axis_index_groups=core_groups)
 
     left_found = [

time: 118 us -> 95.7 us (0.81)
  waiting for transfers between devices: 36.7 us -> 25.3 us
  starting transfers between devices: 31.2 us -> 25.3 us
  local copies, waits for them, and re-layouts: 5.3 us -> 0 us
    ppermute x3, waiting for transfers between devices: 19.5 us -> 1.34 us  [local(): rights.append(lax.ppermute(right, 'blk', slot_moves[slot]))]
    unnamed x14 -> x0, local copies, waits for them, and re-layouts: 5.3 us -> none
    ppermute x3, waiting for transfers between devices: 5.3 us -> 0.01 us  [local(): lax.ppermute(part, 'inner', inner_moves[slot])]
    ppermute x1, waiting for transfers between devices: 5.52 us -> 9.31 us  [local(): right_send = lax.ppermute(right_send, 'blk', slot_moves[slot])]
    all_to_all x2, waiting for transfers between devices: 0.01 us -> 3.26 us  [local(): lax.all_to_all(pieces, everyone, 0, 0, axis_index_groups=core_groups)]
    ppermute x1, waiting for transfers between devices: 0.01 us -> 2.62 us  [local(): right_send = lax.ppermute(right_send, 'blk', slot_moves[1])]
    ppermute x3, starting transfers between devices: 7.12 us -> 4.6 us  [local(): rights.append(lax.ppermute(right, 'blk', slot_moves[slot]))]
    ppermute x1, waiting for transfers between devices: 5.21 us -> 6.92 us  [local(): left_peer = lax.ppermute(left, 'blk', partner)]
  transfers between devices with their start and end apart: 16 -> 16, of which waited for: 7 -> 7; matrix products, arithmetic and copies ran while one was open for 0% -> 1% of each run, Pallas kernels for 34% -> 32%
where the time goes in v10:
time: 95.7 us; the launch traced here: 95.3 us
  Pallas kernels  43.2 us (45%)
  starting transfers between devices  25.3 us (26%)
  waiting for transfers between devices  25.3 us (26%)
    pallas_call x14, Pallas kernels, run(): pl.pallas_call(lambda *refs: kernel(*refs[len(after):]), out_shape=out_sh...  43.2 us
    all_to_all x2, starting transfers between devices, local(): lax.all_to_all(pieces, everyone, 0, 0, axis_index_groups=core_groups)  10.2 us
    ppermute x1, waiting for transfers between devices, local(): right_send = lax.ppermute(right_send, 'blk', slot_moves[slot])  9.31 us
    ppermute x1, waiting for transfers between devices, local(): left_peer = lax.ppermute(left, 'blk', partner)  6.92 us
    ppermute x3, starting transfers between devices, local(): rights.append(lax.ppermute(right, 'blk', slot_moves[slot]))  4.6 us
    all_to_all x2, waiting for transfers between devices, local(): lax.all_to_all(pieces, everyone, 0, 0, axis_index_groups=core_groups)  3.26 us
    ppermute x1, starting transfers between devices, local(): cotangent_peer = lax.ppermute(cotangent_send, 'blk', partner)  3.03 us
    ppermute x1, starting transfers between devices, local(): right_send = lax.ppermute(right_send, 'blk', slot_moves[slot])  2.83 us
  transfers between devices with their start and end apart: 16, of which 7 were waited for; matrix products, arithmetic and copies ran while one was open for 1% of the time, Pallas kernels for 32%

profile of v10, /device:TPU:0, one launch (start us, length us, event | category | flops | bytes accessed | tf_op | source)
XLA Modules:
  0.0 95.3 jit_solution(13576731151647274210)
XLA Ops:
  0.6 2.0 %prepare.1 = (f32[512,128]{1,0:T(8,128)S(1)}, f32[512,128]{1,0:T(8,128)S(1)}, f32[16,4,16,128]{3,2,1,0:T(8,128)S(1)}, f32[16,4,16,128]{3,2,1,0:T(8,128)S(1)}, f32[1024,128]{1,0:T(8,128)S(1)}) custom-call(f32[16,4,2,16,128]{4,3,2,1,0:T(8,128)} %bitcast.6, f32[16,4096]{1,0:T(8,128)} %refs_1_.1, f32[16,4096]{1,0:T(8,128)} %refs_2_.3, f32[1024,128]{1,0:T(8,128)} %refs_2_.5), custom_call_target="tpu_custom_call" | custom-call | flops 1 | bytes 1 | tf_op jit(solution)/shard_map/prepare/pallas_call | solution.py:497
  2.6 3.0 %collective-permute-start = (f32[16,4,16,128]{3,2,1,0:T(8,128)S(1)}, f32[16,4,16,128]{3,2,1,0:T(8,128)S(1)}, u32[]{:S(2)}, u32[]{:S(2)}) collective-permute-start(f32[16,4,16,128]{3,2,1,0:T(8,128)S(1)} %get-tuple-element.38), channel_id=1, source_target_pairs={{0,4},{4,0},{8,12},{12,8},{16,20},{20,16},{24,28},{28,24},{1,5},{5... | collective-permute-start | bytes 1572872 | tf_op jit(solution)/shard_map/ppermute | solution.py:559
  5.6 0.1 collective-permute-start.1
  5.7 4.0 %collective-permute-start.4 = (f32[512,128]{1,0:T(8,128)S(1)}, f32[512,128]{1,0:T(8,128)S(1)}, u32[]{:S(2)}, u32[]{:S(2)}) collective-permute-start(f32[512,128]{1,0:T(8,128)S(1)} %get-tuple-element.41.refs_5_.refs_3_), channel_id=1, source_target_pairs={{0,24},{4,28},{8,16},{12,20},{16,8},{20,12},{24,0},{28,4},{1,25},{... | collective-permute-start | bytes 786440 | tf_op jit(solution)/shard_map/ppermute | solution.py:558
  9.7 0.0 collective-permute-start.3
  9.8 0.6 collective-permute-start.2
  10.3 5.9 %gradient_own.1 = (bf16[8,512,512]{2,1,0:T(8,128)(2,1)S(1)}, f32[8,128,256]{2,1,0:T(8,128)S(1)}, bf16[512,768]{1,0:T(8,128)(2,1)S(1)}) custom-call(f32[1024,128]{1,0:T(8,128)S(1)} %get-tuple-element.34.refs_0_, f32[16,4,16,128]{3,2,1,0:T(8,128)S(1)} %get-tuple-element.35.refs_1_.refs_3_, f32[512,128]{1,0:T(8,128)S(1)} %get-tuple-element.36.refs_2_.refs_1_), custom_call_target="tpu_custom_call" | custom-call | flops 1 | bytes 1 | tf_op jit(solution)/shard_map/gradient_own/pallas_call | solution.py:497
  16.3 6.9 %collective-permute-done.1.refs_2_ = f32[512,128]{1,0:T(8,128)S(1)} collective-permute-done((f32[512,128]{1,0:T(8,128)S(1)}, f32[512,128]{1,0:T(8,128)S(1)}, u32[]{:S(2)}, u32[]{:S(2)}) %collective-permute-start.1) | collective-permute-done | bytes 262176 | tf_op jit(solution)/shard_map/ppermute | solution.py:560
  23.2 0.0 collective-permute-done.refs_1_.refs_4_
  23.2 7.0 %right_parts.1 = (bf16[8,512,512]{2,1,0:T(8,128)(2,1)S(1)}, f32[2,512,128]{2,1,0:T(8,128)S(1)}, f32[2,512,128]{2,1,0:T(8,128)}) custom-call(bf16[512,768]{1,0:T(8,128)(2,1)S(1)} %get-tuple-element.37.refs_0_, f32[16,4,16,128]{3,2,1,0:T(8,128)S(1)} %collective-permute-done.refs_1_.refs_4_, f32[512,128]{1,0:T(8,128)S(1)} %collective-permute-done.1.refs_2_, ...), custom_call_target="tpu_custom_call" | custom-call | flops 1 | bytes 1 | tf_op jit(solution)/shard_map/right_parts/pallas_call | solution.py:497
  30.2 0.0 collective-permute-done.4.refs_8_.refs_6_
  30.2 1.3 %collective-permute-done.3.refs_7_.refs_5_ = f32[512,128]{1,0:T(8,128)S(1)} collective-permute-done((f32[512,128]{1,0:T(8,128)S(1)}, f32[512,128]{1,0:T(8,128)S(1)}, u32[]{:S(2)}, u32[]{:S(2)}) %collective-permute-start.3) | collective-permute-done | bytes 262176 | tf_op jit(solution)/shard_map/ppermute | solution.py:558
  31.5 0.0 collective-permute-done.2.refs_6_.refs_4_
  31.5 9.3 %weight.1 = (f32[512,128]{1,0:T(8,128)S(1)}, f32[512,128]{1,0:T(8,128)S(1)}, bf16[8,512,512]{2,1,0:T(8,128)(2,1)}, bf16[8,512,512]{2,1,0:T(8,128)(2,1)}) custom-call(f32[2,512,128]{2,1,0:T(8,128)S(1)} %get-tuple-element.40.refs_0_, f32[512,128]{1,0:T(8,128)S(1)} %get-tuple-element.36.refs_2_.refs_1_, f32[512,128]{1,0:T(8,128)S(1)} %collective-permute-done.1.refs_2_, ...), custom_call_target="tpu_custom_call" | custom-call | flops 1 | bytes 1 | tf_op jit(solution)/shard_map/weight/pallas_call | solution.py:497
  40.8 0.1 collective-permute-start.5
  40.9 3.8 %left_parts.1 = (f32[4,32,512]{2,1,0:T(8,128)S(1)}, f32[4,32,512]{2,1,0:T(8,128)}) custom-call(f32[512,128]{1,0:T(8,128)S(1)} %get-tuple-element.47.refs_0_, bf16[8,512,512]{2,1,0:T(8,128)(2,1)S(1)} %get-tuple-element.43.refs_1_, bf16[8,512,512]{2,1,0:T(8,128)(2,1)S(1)} %get-tuple-element.44.refs_2_, f32[512,128]{1,0:T(8,128)S(1)} %get-tuple-element.41.refs_5_.refs_3_, ...), custom_call_target="tpu_custom_call" | custom-call | flops 1 | bytes 1 | tf_op jit(solution)/shard_map/left_parts/pallas_call | solution.py:497
  44.7 0.5 collective-permute-start.7
  45.2 0.0 collective-permute-done.5
  45.2 0.7 add.3
  45.9 5.9 %all-to-all-start = ((f32[16,32,128]{2,1,0:T(8,128)}), f32[16,32,128]{2,1,0:T(8,128)S(1)}, u32[]{:S(2)}, u32[]{:S(2)}) async-start(f32[16,32,128]{2,1,0:T(8,128)} %bitcast.1.refs_0_), calls=%async_computation | async-start | bytes 524288 | tf_op jit(solution)/shard_map/all_to_all | solution.py:641
  51.8 1.9 %collective-permute-start.6 = (f32[4,32,512]{2,1,0:T(8,128)}, f32[4,32,512]{2,1,0:T(8,128)S(1)}, u32[]{:S(2)}, u32[]{:S(2)}) collective-permute-start(f32[4,32,512]{2,1,0:T(8,128)} %get-tuple-element.51), channel_id=1, source_target_pairs={{0,4},{4,0},{8,12},{12,8},{16,20},{20,16},{24,28},{28,24},{1,5},{5... | collective-permute-start | bytes 786440 | tf_op jit(solution)/shard_map/ppermute | solution.py:608
  53.7 5.2 %pair_peer.1.refs_0_ = f32[16,4,16,128]{3,2,1,0:T(8,128)S(1)} custom-call(f32[16,32,128]{2,1,0:T(8,128)} %bitcast.1.refs_0_, bf16[8,512,512]{2,1,0:T(8,128)(2,1)} %get-tuple-element.49.refs_1_, f32[1024,128]{1,0:T(8,128)} %refs_2_.5), custom_call_target="tpu_custom_call" | custom-call | flops 1 | bytes 1 | tf_op jit(solution)/shard_map/pair_peer/pallas_call | solution.py:497
  58.9 0.2 collective-permute-start.8
  59.1 2.6 %collective-permute-done.7.refs_1_ = f32[2,512,128]{2,1,0:T(8,128)S(1)} collective-permute-done((f32[2,512,128]{2,1,0:T(8,128)}, f32[2,512,128]{2,1,0:T(8,128)S(1)}, u32[]{:S(2)}, u32[]{:S(2)}) %collective-permute-start.7) | collective-permute-done | bytes 524320 | tf_op jit(solution)/shard_map/ppermute | solution.py:610
  61.8 0.1 right_halve.1
  61.8 0.3 collective-permute-done.6.refs_2_
  62.1 3.3 %all-to-all-done.refs_0_.refs_3_ = f32[16,32,128]{2,1,0:T(8,128)S(1)} async-done(((f32[16,32,128]{2,1,0:T(8,128)}), f32[16,32,128]{2,1,0:T(8,128)S(1)}, u32[]{:S(2)}, u32[]{:S(2)}) %all-to-all-start) | async-done | bytes 262176 | tf_op jit(solution)/shard_map/all_to_all | solution.py:641
  65.4 0.7 weight_sum.1.refs_0_
  66.1 4.4 %all-to-all-start.1 = ((f32[16,32,128]{2,1,0:T(8,128)}), f32[16,32,128]{2,1,0:T(8,128)S(1)}, u32[]{:S(2)}, u32[]{:S(2)}) async-start(f32[16,32,128]{2,1,0:T(8,128)} %weight_sum.1.refs_0_), calls=%async_computation.1 | async-start | bytes 524288 | tf_op jit(solution)/shard_map/all_to_all | solution.py:655
  70.5 2.8 %collective-permute-start.12 = (f32[1,512,128]{2,1,0:T(8,128)S(1)}, f32[1,512,128]{2,1,0:T(8,128)S(1)}, u32[]{:S(2)}, u32[]{:S(2)}) collective-permute-start(f32[1,512,128]{2,1,0:T(8,128)S(1)} %get-tuple-element.59), channel_id=1, source_target_pairs={{0,16},{4,20},{8,24},{12,28},{16,0},{20,4},{24,8},{28,12},{1,17},{... | collective-permute-start | bytes 786440 | tf_op jit(solution)/shard_map/ppermute | solution.py:617
  73.3 0.0 collective-permute-start.9
  73.3 1.5 %collective-permute-start.10 = (f32[32,512]{1,0:T(8,128)S(1)}, f32[32,512]{1,0:T(8,128)S(1)}, u32[]{:S(2)}, u32[]{:S(2)}) collective-permute-start(f32[32,512]{1,0:T(8,128)S(1)} %get-tuple-element.57), channel_id=1, source_target_pairs={{0,2},{1,3},{2,0},{3,1},{4,6},{5,7},{6,4},{7,5},{8,10},{9,11},{10,... | collective-permute-start | bytes 196616 | tf_op jit(solution)/shard_map/ppermute | solution.py:658
  74.8 0.4 collective-permute-start.11
  75.2 5.2 %pair_own.1.refs_0_ = f32[16,4,16,128]{3,2,1,0:T(8,128)S(1)} custom-call(f32[16,32,128]{2,1,0:T(8,128)} %weight_sum.1.refs_0_, bf16[8,512,512]{2,1,0:T(8,128)(2,1)} %get-tuple-element.55.refs_1_, f32[1024,128]{1,0:T(8,128)} %refs_2_.5), custom_call_target="tpu_custom_call" | custom-call | flops 1 | bytes 1 | tf_op jit(solution)/shard_map/pair_own/pallas_call | solution.py:497
  80.4 9.3 %collective-permute-done.12.refs_1_ = f32[1,512,128]{2,1,0:T(8,128)S(1)} collective-permute-done((f32[1,512,128]{2,1,0:T(8,128)S(1)}, f32[1,512,128]{2,1,0:T(8,128)S(1)}, u32[]{:S(2)}, u32[]{:S(2)}) %collective-permute-start.12) | collective-permute-done | bytes 262176 | tf_op jit(solution)/shard_map/ppermute | solution.py:617
  89.7 1.2 %turn_right.1 = f32[16,4096]{1,0:T(8,128)} custom-call(f32[1,512,128]{2,1,0:T(8,128)S(1)} %get-tuple-element.54.refs_2_.refs_0_, f32[1,512,128]{2,1,0:T(8,128)S(1)} %collective-permute-done.12.refs_1_), custom_call_target="tpu_custom_call" | custom-call | flops 1 | bytes 1 | tf_op jit(solution)/shard_map/turn_right/pallas_call | solution.py:497
  90.9 0.0 collective-permute-done.8.refs_1_
  90.9 1.0 %merge.1 = f32[16,4,2,16,128]{4,3,2,1,0:T(8,128)} custom-call(f32[16,4,16,128]{3,2,1,0:T(8,128)S(1)} %pair_own.1.refs_0_, f32[16,4,16,128]{3,2,1,0:T(8,128)S(1)} %collective-permute-done.8.refs_1_), custom_call_target="tpu_custom_call" | custom-call | flops 1 | bytes 1 | tf_op jit(solution)/shard_map/merge/pallas_call | solution.py:497
  91.9 0.0 collective-permute-done.9.refs_1_
  91.9 0.0 collective-permute-done.10.refs_2_
  91.9 0.0 collective-permute-done.11.refs_3_
  91.9 0.8 turn_left.1
  92.7 0.0 all-to-all-done.1
  92.7 0.0 collective-permute-start.13
  92.7 1.5 %collective-permute-done.13.refs_1_ = f32[512,128]{1,0:T(8,128)S(1)} collective-permute-done((f32[512,128]{1,0:T(8,128)S(1)}, f32[512,128]{1,0:T(8,128)S(1)}, u32[]{:S(2)}, u32[]{:S(2)}) %collective-permute-start.13) | collective-permute-done | bytes 262176 | tf_op jit(solution)/shard_map/ppermute | solution.py:695
  94.2 1.1 %place.1 = f32[1024,128]{1,0:T(8,128)} custom-call(f32[512,128]{1,0:T(8,128)S(1)} %bitcast.5, f32[512,128]{1,0:T(8,128)S(1)} %collective-permute-done.13.refs_1_), custom_call_target="tpu_custom_call" | custom-call | flops 1 | bytes 1 | tf_op jit(solution)/shard_map/place/pallas_call | solution.py:497
  (1 shorter events, 0.0 us)
Async XLA Ops:
  2.6 20.6 %collective-permute-start = (f32[16,4,16,128]{3,2,1,0:T(8,128)S(1)}, f32[16,4,16,128]{3,2,1,0:T(8,128)S(1)}, u32[]{:S(2)}, u32[]{:S(2)}) collective-permute-start(f32[16,4,16,128]{3,2,1,0:T(8,128)S(1)} %get-tuple-element.38), channel_id=1, source_target_pairs={{0,4},{4,0},{8,12},{12,8},{16,20},{20,16},{24,28},{28,24},{1,5},{5... | collective-permute-start | bytes 1572872 | tf_op jit(solution)/shard_map/ppermute | solution.py:559
  5.6 17.5 %collective-permute-start.1 = (f32[512,128]{1,0:T(8,128)S(1)}, f32[512,128]{1,0:T(8,128)S(1)}, u32[]{:S(2)}, u32[]{:S(2)}) collective-permute-start(f32[512,128]{1,0:T(8,128)S(1)} %get-tuple-element.36.refs_2_.refs_1_), channel_id=1, source_target_pairs={{0,4},{4,0},{8,12},{12,8},{16,20},{20,16},{24,28},{28,24},{1,5},{5... | collective-permute-start | bytes 786440 | tf_op jit(solution)/shard_map/ppermute | solution.py:560
  5.7 24.4 %collective-permute-start.4 = (f32[512,128]{1,0:T(8,128)S(1)}, f32[512,128]{1,0:T(8,128)S(1)}, u32[]{:S(2)}, u32[]{:S(2)}) collective-permute-start(f32[512,128]{1,0:T(8,128)S(1)} %get-tuple-element.41.refs_5_.refs_3_), channel_id=1, source_target_pairs={{0,24},{4,28},{8,16},{12,20},{16,8},{20,12},{24,0},{28,4},{1,25},{... | collective-permute-start | bytes 786440 | tf_op jit(solution)/shard_map/ppermute | solution.py:558
  9.7 21.7 %collective-permute-start.3 = (f32[512,128]{1,0:T(8,128)S(1)}, f32[512,128]{1,0:T(8,128)S(1)}, u32[]{:S(2)}, u32[]{:S(2)}) collective-permute-start(f32[512,128]{1,0:T(8,128)S(1)} %get-tuple-element.41.refs_5_.refs_3_), channel_id=1, source_target_pairs={{0,16},{4,20},{8,24},{12,28},{16,0},{20,4},{24,8},{28,12},{1,17},{... | collective-permute-start | bytes 786440 | tf_op jit(solution)/shard_map/ppermute | solution.py:558
  9.8 21.7 %collective-permute-start.2 = (f32[512,128]{1,0:T(8,128)S(1)}, f32[512,128]{1,0:T(8,128)S(1)}, u32[]{:S(2)}, u32[]{:S(2)}) collective-permute-start(f32[512,128]{1,0:T(8,128)S(1)} %get-tuple-element.41.refs_5_.refs_3_), channel_id=1, source_target_pairs={{0,8},{4,12},{8,0},{12,4},{16,24},{20,28},{24,16},{28,20},{1,9},{5... | collective-permute-start | bytes 786440 | tf_op jit(solution)/shard_map/ppermute | solution.py:558
  40.8 4.4 %collective-permute-start.5 = (f32[512,128]{1,0:T(8,128)S(1)}, f32[512,128]{1,0:T(8,128)S(1)}, u32[]{:S(2)}, u32[]{:S(2)}) collective-permute-start(f32[512,128]{1,0:T(8,128)S(1)} %get-tuple-element.48), channel_id=1, source_target_pairs={{0,1},{1,0},{2,3},{3,2},{4,5},{5,4},{6,7},{7,6},{8,9},{9,8},{10,11... | collective-permute-start | bytes 786440 | tf_op jit(solution)/shard_map/ppermute | solution.py:595
  44.7 17.0 %collective-permute-start.7 = (f32[2,512,128]{2,1,0:T(8,128)}, f32[2,512,128]{2,1,0:T(8,128)S(1)}, u32[]{:S(2)}, u32[]{:S(2)}) collective-permute-start(f32[2,512,128]{2,1,0:T(8,128)} %get-tuple-element.53), channel_id=1, source_target_pairs={{0,8},{4,12},{8,0},{12,4},{16,24},{20,28},{24,16},{28,20},{1,9},{5... | collective-permute-start | bytes 1572872 | tf_op jit(solution)/shard_map/ppermute | solution.py:610
  45.9 19.4 %all-to-all-start = ((f32[16,32,128]{2,1,0:T(8,128)}), f32[16,32,128]{2,1,0:T(8,128)S(1)}, u32[]{:S(2)}, u32[]{:S(2)}) async-start(f32[16,32,128]{2,1,0:T(8,128)} %bitcast.1.refs_0_), calls=%async_computation | async-start | bytes 524288 | tf_op jit(solution)/shard_map/all_to_all | solution.py:641
  51.8 10.3 %collective-permute-start.6 = (f32[4,32,512]{2,1,0:T(8,128)}, f32[4,32,512]{2,1,0:T(8,128)S(1)}, u32[]{:S(2)}, u32[]{:S(2)}) collective-permute-start(f32[4,32,512]{2,1,0:T(8,128)} %get-tuple-element.51), channel_id=1, source_target_pairs={{0,4},{4,0},{8,12},{12,8},{16,20},{20,16},{24,28},{28,24},{1,5},{5... | collective-permute-start | bytes 786440 | tf_op jit(solution)/shard_map/ppermute | solution.py:608
  58.9 32.0 %collective-permute-start.8 = (f32[16,4,16,128]{3,2,1,0:T(8,128)S(1)}, f32[16,4,16,128]{3,2,1,0:T(8,128)S(1)}, u32[]{:S(2)}, u32[]{:S(2)}) collective-permute-start(f32[16,4,16,128]{3,2,1,0:T(8,128)S(1)} %pair_peer.1.refs_0_), channel_id=1, source_target_pairs={{0,4},{4,0},{8,12},{12,8},{16,20},{20,16},{24,28},{28,24},{1,5},{5... | collective-permute-start | bytes 1572872 | tf_op jit(solution)/shard_map/ppermute | solution.py:639
  66.1 26.5 %all-to-all-start.1 = ((f32[16,32,128]{2,1,0:T(8,128)}), f32[16,32,128]{2,1,0:T(8,128)S(1)}, u32[]{:S(2)}, u32[]{:S(2)}) async-start(f32[16,32,128]{2,1,0:T(8,128)} %weight_sum.1.refs_0_), calls=%async_computation.1 | async-start | bytes 524288 | tf_op jit(solution)/shard_map/all_to_all | solution.py:655
  70.5 19.2 %collective-permute-start.12 = (f32[1,512,128]{2,1,0:T(8,128)S(1)}, f32[1,512,128]{2,1,0:T(8,128)S(1)}, u32[]{:S(2)}, u32[]{:S(2)}) collective-permute-start(f32[1,512,128]{2,1,0:T(8,128)S(1)} %get-tuple-element.59), channel_id=1, source_target_pairs={{0,16},{4,20},{8,24},{12,28},{16,0},{20,4},{24,8},{28,12},{1,17},{... | collective-permute-start | bytes 786440 | tf_op jit(solution)/shard_map/ppermute | solution.py:617
  73.3 18.5 %collective-permute-start.9 = (f32[32,512]{1,0:T(8,128)S(1)}, f32[32,512]{1,0:T(8,128)S(1)}, u32[]{:S(2)}, u32[]{:S(2)}) collective-permute-start(f32[32,512]{1,0:T(8,128)S(1)} %get-tuple-element.56), channel_id=1, source_target_pairs={{0,1},{1,0},{2,3},{3,2},{4,5},{5,4},{6,7},{7,6},{8,9},{9,8},{10,11... | collective-permute-start | bytes 196616 | tf_op jit(solution)/shard_map/ppermute | solution.py:658
  73.3 18.5 %collective-permute-start.10 = (f32[32,512]{1,0:T(8,128)S(1)}, f32[32,512]{1,0:T(8,128)S(1)}, u32[]{:S(2)}, u32[]{:S(2)}) collective-permute-start(f32[32,512]{1,0:T(8,128)S(1)} %get-tuple-element.57), channel_id=1, source_target_pairs={{0,2},{1,3},{2,0},{3,1},{4,6},{5,7},{6,4},{7,5},{8,10},{9,11},{10,... | collective-permute-start | bytes 196616 | tf_op jit(solution)/shard_map/ppermute | solution.py:658
  74.8 17.1 %collective-permute-start.11 = (f32[32,512]{1,0:T(8,128)S(1)}, f32[32,512]{1,0:T(8,128)S(1)}, u32[]{:S(2)}, u32[]{:S(2)}) collective-permute-start(f32[32,512]{1,0:T(8,128)S(1)} %get-tuple-element.58), channel_id=1, source_target_pairs={{0,3},{1,2},{2,1},{3,0},{4,7},{5,6},{6,5},{7,4},{8,11},{9,10},{10,... | collective-permute-start | bytes 196616 | tf_op jit(solution)/shard_map/ppermute | solution.py:658
  92.7 1.5 %collective-permute-start.13 = (f32[512,128]{1,0:T(8,128)S(1)}, f32[512,128]{1,0:T(8,128)S(1)}, u32[]{:S(2)}, u32[]{:S(2)}) collective-permute-start(f32[512,128]{1,0:T(8,128)S(1)} %bitcast.4), channel_id=1, source_target_pairs={{0,1},{1,0},{2,3},{3,2},{4,5},{5,4},{6,7},{7,6},{8,9},{9,8},{10,11... | collective-permute-start | bytes 786440 | tf_op jit(solution)/shard_map/ppermute | solution.py:695

commit v11 on v10

--- a/solution.py
+++ b/solution.py
@@ -125,16 +125,14 @@
         copy.wait()
 
 
-def turn_right_kernel(parts, *refs):
-    part_refs, (out_ref, total, square, tiles) = refs[:parts], refs[parts:]
+def turn_right_kernel(in_ref, out_ref, square, tiles):
     channels = ENTRY_CHANNELS
     rows, features = out_ref.shape
     count = features // LANES
-    total[...] = functools.reduce(jnp.add, [ref[0] for ref in part_refs])
     for group in range(rows // PACK):
-        stacked = [total[strided(group * PACK + k, channels, rows), :] for k in range(PACK)]
-        square[...] = jnp.concatenate(stacked, 0).T
-        pieces = [square[strided(part, count, PACK), :] for part in range(PACK)]
+        stacked = [in_ref[strided(group * PACK + k, channels, rows), :] for k in range(PACK)]
+        square[group] = jnp.concatenate(stacked, 0).T
+        pieces = [square[group, strided(part, count, PACK), :] for part in range(PACK)]
         for k in range(PACK):
             lanes = slice(k * channels, (k + 1) * channels)
             tiles[strided(group * PACK + k, count, rows), :] = jnp.concatenate(
@@ -173,29 +171,45 @@
         )
 
 
-def gradient_phase(blocks, cotangent_ref, out_ref, weight_cat):
+def gradient_phase(blocks, cotangent_ref, factor_ref, out_hbm, weight_cat, semaphores):
     fold = fold_of(blocks * cotangent_ref.shape[2])
     slots = slots_of(blocks)
+
+    def copy_of(pair):
+        return pltpu.make_async_copy(factor_ref.at[pair], out_hbm.at[pair], semaphores.at[pair])
 
     def step_of(pair, carry):
         high, low = spread_of(cotangent_ref, pair, slots, fold)
         found = dot_rows(weight_cat[...], jnp.concatenate([high, high, low], 1))
-        out_ref[pair] = jnp.concatenate(halves(found), 1)
+        factor_ref[pair] = jnp.concatenate(halves(found), 1)
+        copy_of(pair).start()
         return carry
 
-    lax.fori_loop(0, out_ref.shape[0], step_of, 0)
+    lax.fori_loop(0, factor_ref.shape[0], step_of, 0)
+    return [copy_of(pair) for pair in range(factor_ref.shape[0])]
 
 
 def gradient_kernel(
-    blocks, weight_ref, cotangent_ref, left_ref, out_ref, partial_ref, weight_cat, left_flip
+    blocks,
+    weight_ref,
+    cotangent_ref,
+    left_ref,
+    out_hbm,
+    partial_ref,
+    weight_cat,
+    factor_ref,
+    left_flip,
+    semaphores,
 ):
     prepare_weight(weight_ref, weight_cat, fold_of(blocks * cotangent_ref.shape[2]))
-    gradient_phase(blocks, cotangent_ref, out_ref, weight_cat)
+    copies = gradient_phase(blocks, cotangent_ref, factor_ref, out_hbm, weight_cat, semaphores)
 
     def store(step, found):
         partial_ref[step] = found
 
-    right_phase(left_ref, out_ref, left_flip, store)
+    right_phase(left_ref, factor_ref, left_flip, store)
+    for copy in copies:
+        copy.wait()
 
 
 def right_phase(left_ref, factor_ref, left_flip, store):
@@ -246,15 +260,17 @@
     cotangent_ref,
     left_ref,
     partial_ref,
-    peer_ref,
-    keep_ref,
-    send_ref,
+    out_hbm,
+    out_ref,
+    factor_ref,
     left_flip,
+    semaphores,
 ):
     depth = cotangent_ref.shape[2]
     fold = fold_of(blocks * depth)
     lanes = fold * blocks * depth
-    gradient_phase(blocks, cotangent_ref, peer_ref, weight_cat)
+    copies = gradient_phase(blocks, cotangent_ref, factor_ref, out_hbm, weight_cat, semaphores)
+    slots = slots_of(blocks)
 
     def store(step, found):
         found = found + partial_ref[step]
@@ -264,16 +280,11 @@
                 for slot in range(blocks):
                     start = (place * blocks + slot) * depth
                     row = pl.multiple_of(((2 * step + part) * fold + place) * depth, depth)
-                    out_ref = send_ref if slot % 2 else keep_ref
-                    out_ref[slot // 2, pl.ds(row, depth), :] = turned[start : start + depth]
-
-    right_phase(left_ref, peer_ref, left_flip, store)
-
-
-def halve_kernel(keep_ref, found_ref, keep_out, send_out):
-    for slot in range(keep_ref.shape[0]):
-        out_ref = send_out if slot % 2 else keep_out
-        out_ref[slot // 2] = keep_ref[slot] + found_ref[slot]
+                    out_ref[slots[slot], pl.ds(row, depth), :] = turned[start : start + depth]
+
+    right_phase(left_ref, factor_ref, left_flip, store)
+    for copy in copies:
+        copy.wait()
 
 
 def right_rows(right_refs, step, fold, depth):
@@ -358,15 +369,31 @@
     lax.fori_loop(0, channels // (2 * fold), finish, 0)
 
 
-def left_kernel(blocks, depth, own_ref, peer_ref, *refs):
-    right_refs, (own_out, peer_out, total, flipped) = refs[:blocks], refs[blocks:]
+def left_kernel(blocks, depth, own_hbm, peer_hbm, *refs):
+    right_refs, refs = refs[:blocks], refs[blocks:]
+    own_out, peer_out, own_ref, peer_ref, total, flipped, semaphores = refs
     lanes = own_ref.shape[2] // 4
     fold = lanes // (blocks * depth)
     sequences = right_refs[0].shape[1]
     group = 4
+    count = ENTRY_CHANNELS // (fold * group)
+
+    def copies(step):
+        size = group * ENTRY_CHANNELS
+        rows = pl.ds(pl.multiple_of(step * size, size), size)
+        return [
+            pltpu.make_async_copy(hbm.at[:, rows], ref.at[:, rows], semaphores.at[step, side])
+            for side, (hbm, ref) in enumerate(((own_hbm, own_ref), (peer_hbm, peer_ref)))
+        ]
+
+    for step in range(count):
+        for copy in copies(step):
+            copy.start()
     total[...] = jnp.zeros_like(total)
 
     def step_of(step, carry):
+        for copy in copies(step):
+            copy.wait()
         steps = [group * step + part for part in range(group)]
         right = [right_rows(right_refs, at, fold, depth) for at in steps]
         high, low = halves(jnp.concatenate(right, 0))
@@ -378,7 +405,7 @@
         total[...] += both[:, :sequences] + both[:, sequences:] + dot(grads[1], high)
         return carry
 
-    lax.fori_loop(0, ENTRY_CHANNELS // (fold * group), step_of, 0)
+    lax.fori_loop(0, count, step_of, 0)
     flipped[...] = total[...].T * (1.0 / sequences)
     inner, size, width = own_out.shape
     here = lax.axis_index("inner")
@@ -526,6 +553,7 @@
 
     partner = [(here, here ^ 1) for here in range(count)]
     slot_moves = [[(here, here ^ (2 * slot)) for here in range(count)] for slot in range(blocks)]
+    same_parity = [[2 * block + side for block in range(blocks)] for side in range(2)]
     inner_moves = [[(here, here ^ slot) for here in range(inner)] for slot in range(inner)]
     cores = [(here, here ^ 1) for here in range(inner)]
     core_groups = [list(range(core, count * inner, 2)) for core in range(2)]
@@ -559,29 +587,35 @@
     cotangent_peer = lax.ppermute(cotangent_send, "blk", partner)
     left_peer = lax.ppermute(left, "blk", partner)
 
+    vmem = pl.BlockSpec(memory_space=pltpu.VMEM)
+    hbm = pl.BlockSpec(memory_space=pltpu.HBM)
     factor = shape(row_pairs, tall, 4 * lanes, kind=BF16)
     factor_scratch = pltpu.VMEM(factor.shape, BF16)
     weight_cat = shape(tall, 3 * fold * pairs, kind=BF16)
     flip_scratch = pltpu.VMEM((2 * sequences, rows * channels), BF16)
+    factor_hbm = pltpu.HBM(factor.shape, BF16)
+    factor_copies = pltpu.SemaphoreType.DMA((row_pairs,))
     grad_own, partial, weight_cat = large(
         functools.partial(gradient_kernel, blocks),
-        [factor, shape(steps // 2, sequences, 2 * lanes), weight_cat],
-        [flip_scratch],
+        [factor_hbm, shape(steps // 2, sequences, 2 * lanes), weight_cat],
+        [factor_scratch, flip_scratch, factor_copies],
         "gradient_own",
+        out_specs=[hbm, vmem, vmem],
     )(weight, cotangent_own, left)
-    right_half = shape(blocks // 2, channels * depth, sequences)
-    grad_peer, right_keep, right_send = large(
+    grad_peer, right_parts = large(
         functools.partial(right_kernel, blocks),
-        [factor, right_half, right_half],
-        [flip_scratch],
+        [factor_hbm, shape(blocks, channels * depth, sequences)],
+        [factor_scratch, flip_scratch, factor_copies],
         "right_parts",
+        out_specs=[hbm, vmem],
     )(weight_cat, cotangent_peer, left_peer, partial)
-
-    vmem = pl.BlockSpec(memory_space=pltpu.VMEM)
-    hbm = pl.BlockSpec(memory_space=pltpu.HBM)
+    right_sum = lax.psum_scatter(
+        right_parts, "blk", scatter_dimension=0, axis_index_groups=same_parity
+    )
+
     keep, send, outer_own, outer_peer = large(
         functools.partial(weight_kernel, blocks),
-        [shape(outer // 2, pairs)] * 2 + [pltpu.HBM(factor.shape, BF16)] * 2,
+        [shape(outer // 2, pairs)] * 2 + [factor_hbm] * 2,
         [
             factor_scratch,
             factor_scratch,
@@ -589,7 +623,7 @@
             pltpu.SemaphoreType.DMA((steps // 2, 2)),
         ],
         "weight",
-        after=[right_keep],
+        after=[right_parts],
         out_specs=[vmem, vmem, hbm, hbm],
     )(left, left_peer, cotangent_own, cotangent_peer, *rights)
     sent = lax.ppermute(send, "inner", cores)
@@ -599,23 +633,18 @@
         functools.partial(left_kernel, blocks, depth),
         [shape(inner, size, rows * channels)] * 2,
         [
+            factor_scratch,
+            factor_scratch,
             pltpu.VMEM((2 * rows * channels, sequences), F32),
             pltpu.VMEM((sequences, 2 * rows * channels), F32),
+            pltpu.SemaphoreType.DMA((steps // 4, 2)),
         ],
         "left_parts",
+        far=[0, 1],
         after=[keep],
     )(grad_own, grad_peer, *rights)
     left_other = lax.ppermute(left_other, "blk", partner)
-    keep, left_own, right_send = lax.optimization_barrier((keep, left_own, right_send))
-    right_send = lax.ppermute(right_send, "blk", slot_moves[1])
-    slot = 2
-    while slot < blocks:
-        part = shape(blocks // (2 * slot), channels * depth, sequences)
-        right_keep, right_send = call(halve_kernel, [part, part], name="right_halve")(
-            right_keep, right_send
-        )
-        right_send = lax.ppermute(right_send, "blk", slot_moves[slot])
-        slot = 2 * slot
+    keep, left_own = lax.optimization_barrier((keep, left_own))
     members = count * inner // 2
     pieces = (keep + sent).reshape(members, outer // 2 // members, pairs)
 
@@ -649,7 +678,7 @@
         spread_sum_kernel,
         shape(*pieces.shape),
         name="weight_sum",
-        after=[pair_other, left_found[0], right_keep],
+        after=[pair_other],
     )(pieces)
     pair_own = pair(outer_own, [pieces], "pair_own")
     pieces = lax.all_to_all(pieces, everyone, 0, 0, axis_index_groups=core_groups)
@@ -669,15 +698,14 @@
     )(*left_found)
 
     grad_right = call(
-        functools.partial(turn_right_kernel, 2),
+        turn_right_kernel,
         shape(depth, features),
         [
-            pltpu.VMEM((channels * depth, sequences), F32),
-            pltpu.VMEM((LANES, LANES), F32),
+            pltpu.VMEM((depth // PACK, LANES, LANES), F32),
             pltpu.VMEM((depth * features // LANES, LANES), F32),
         ],
         name="turn_right",
-    )(right_keep, right_send)
+    )(right_sum)
 
     pair_update = call(
         merge_kernel,

time: 95.7 us -> 150 us (1.57)
  waiting for transfers between devices: 25.3 us -> 55.5 us
  between operations: 0.75 us -> 14.2 us
  starting transfers between devices: 25.3 us -> 33.6 us
    ppermute x3, waiting for transfers between devices: 1.34 us -> 27.5 us  [local(): rights.append(lax.ppermute(right, 'blk', slot_moves[slot]))]
    ppermute x2 -> x0, waiting for transfers between devices: 11.9 us -> none  [the longest x1 9.31 us: local(): right_send = lax.ppermute(right_send, 'blk', slot_moves[slot])]
    ppermute x1, waiting for transfers between devices: 0.27 us -> 11.6 us  [local(): left_other = lax.ppermute(left_other, 'blk', partner)]
    all_to_all x2, starting transfers between devices: 10.2 us -> 19.8 us  [local(): lax.all_to_all(pieces, everyone, 0, 0, axis_index_groups=core_groups)]
    ppermute x1, waiting for transfers between devices: 6.92 us -> 11.4 us  [local(): left_peer = lax.ppermute(left, 'blk', partner)]
    ppermute x2 -> x0, starting transfers between devices: 3.3 us -> none  [the longest x1 2.83 us: local(): right_send = lax.ppermute(right_send, 'blk', slot_moves[slot])]
    ppermute x1, starting transfers between devices: 0.23 us -> 1.99 us  [local(): pair_found = lax.ppermute(pair_other, 'blk', partner)]
    pallas_call x14 -> x13, Pallas kernels: 43.2 us -> 44.4 us  [run(): pl.pallas_call(lambda *refs: kernel(*refs[len(after):]), out_shape=out_sh...]
  transfers between devices with their start and end apart: 16 -> 15, of which waited for: 7 -> 7; matrix products, arithmetic and copies ran while one was open for 1% -> 0% of each run, Pallas kernels for 32% -> 23%
where the time goes in v11:
time: 150 us; the launch traced here: 149 us
  waiting for transfers between devices  55.5 us (37%)
  Pallas kernels  44.4 us (30%)
  starting transfers between devices  33.6 us (22%)
  between operations  14.2 us (9%)
    pallas_call x13, Pallas kernels, run(): pl.pallas_call(lambda *refs: kernel(*refs[len(after):]), out_shape=out_sh...  44.4 us
    ppermute x3, waiting for transfers between devices, local(): rights.append(lax.ppermute(right, 'blk', slot_moves[slot]))  27.5 us
    all_to_all x2, starting transfers between devices, local(): lax.all_to_all(pieces, everyone, 0, 0, axis_index_groups=core_groups)  19.8 us
    ppermute x1, waiting for transfers between devices, local(): left_other = lax.ppermute(left_other, 'blk', partner)  11.6 us
    ppermute x1, waiting for transfers between devices, local(): left_peer = lax.ppermute(left, 'blk', partner)  11.4 us
    ppermute x3, starting transfers between devices, local(): rights.append(lax.ppermute(right, 'blk', slot_moves[slot]))  4.46 us
    all_to_all x2, waiting for transfers between devices, local(): lax.all_to_all(pieces, everyone, 0, 0, axis_index_groups=core_groups)  3.47 us
    ppermute x1, starting transfers between devices, local(): cotangent_peer = lax.ppermute(cotangent_send, 'blk', partner)  3.03 us
  transfers between devices with their start and end apart: 15, of which 7 were waited for; matrix products, arithmetic and copies ran while one was open for 0% of the time, Pallas kernels for 23%

profile of v11, /device:TPU:0, one launch (start us, length us, event | category | flops | bytes accessed | tf_op | source)
XLA Modules:
  0.0 149.4 jit_solution(13992156424390079705)
XLA Ops:
  7.2 0.0 reduce-scatter.2.cloned.1.call-start
  7.2 2.0 %prepare.1 = (f32[512,128]{1,0:T(8,128)S(1)}, f32[512,128]{1,0:T(8,128)S(1)}, f32[16,4,16,128]{3,2,1,0:T(8,128)S(1)}, f32[16,4,16,128]{3,2,1,0:T(8,128)S(1)}, f32[1024,128]{1,0:T(8,128)S(1)}) custom-call(f32[16,4,2,16,128]{4,3,2,1,0:T(8,128)} %bitcast.8, f32[16,4096]{1,0:T(8,128)} %refs_1_.1, f32[16,4096]{1,0:T(8,128)} %refs_2_.3, f32[1024,128]{1,0:T(8,128)} %refs_2_.5), custom_call_target="tpu_custom_call" | custom-call | flops 1 | bytes 1 | tf_op jit(solution)/shard_map/prepare/pallas_call | solution.py:524
  9.2 3.0 %collective-permute-start = (f32[16,4,16,128]{3,2,1,0:T(8,128)S(1)}, f32[16,4,16,128]{3,2,1,0:T(8,128)S(1)}, u32[]{:S(2)}, u32[]{:S(2)}) collective-permute-start(f32[16,4,16,128]{3,2,1,0:T(8,128)S(1)} %get-tuple-element.34), channel_id=1, source_target_pairs={{0,4},{4,0},{8,12},{12,8},{16,20},{20,16},{24,28},{28,24},{1,5},{5... | collective-permute-start | bytes 1572872 | tf_op jit(solution)/shard_map/ppermute | solution.py:587
  12.2 0.1 collective-permute-start.1
  12.3 6.0 %gradient_own.1 = (bf16[8,512,512]{2,1,0:T(8,128)(2,1)}, f32[8,128,256]{2,1,0:T(8,128)S(1)}, bf16[512,768]{1,0:T(8,128)(2,1)S(1)}) custom-call(f32[1024,128]{1,0:T(8,128)S(1)} %get-tuple-element.30.refs_0_, f32[16,4,16,128]{3,2,1,0:T(8,128)S(1)} %get-tuple-element.31.refs_1_.refs_3_, f32[512,128]{1,0:T(8,128)S(1)} %get-tuple-element.32.refs_2_.refs_1_), custom_call_target="tpu_custom_call" | custom-call | flops 1 | bytes 1 | tf_op jit(solution)/shard_map/gradient_own/pallas_call | solution.py:524
  18.3 11.4 %collective-permute-done.1.refs_2_ = f32[512,128]{1,0:T(8,128)S(1)} collective-permute-done((f32[512,128]{1,0:T(8,128)S(1)}, f32[512,128]{1,0:T(8,128)S(1)}, u32[]{:S(2)}, u32[]{:S(2)}) %collective-permute-start.1) | collective-permute-done | bytes 262176 | tf_op jit(solution)/shard_map/ppermute | solution.py:588
  29.8 0.0 collective-permute-done.refs_1_.refs_4_
  29.8 7.3 %right_parts.1 = (bf16[8,512,512]{2,1,0:T(8,128)(2,1)}, f32[4,512,128]{2,1,0:T(8,128)}) custom-call(bf16[512,768]{1,0:T(8,128)(2,1)S(1)} %get-tuple-element.33.refs_0_, f32[16,4,16,128]{3,2,1,0:T(8,128)S(1)} %collective-permute-done.refs_1_.refs_4_, f32[512,128]{1,0:T(8,128)S(1)} %collective-permute-done.1.refs_2_, f32[8,128,256]{2,1,0:T(8,128)S(1)} %get-tuple-element.35.refs_3_), custom_call_target="tpu_custom_call" | custom-call | flops 1 | bytes 1 | tf_op jit(solution)/shard_map/right_parts/pallas_call | solution.py:524
  37.1 0.0 reduce-scatter.2.cloned.1.call-update
  37.1 1.9 %collective-permute-start.2 = (f32[512,128]{1,0:T(8,128)S(1)}, f32[512,128]{1,0:T(8,128)S(1)}, u32[]{:S(2)}, u32[]{:S(2)}) collective-permute-start(f32[512,128]{1,0:T(8,128)S(1)} %get-tuple-element.37.refs_5_.refs_3_), channel_id=1, source_target_pairs={{0,8},{4,12},{8,0},{12,4},{16,24},{20,28},{24,16},{28,20},{1,9},{5... | collective-permute-start | bytes 786440 | tf_op jit(solution)/shard_map/ppermute | solution.py:586
  39.0 2.6 %collective-permute-start.3 = (f32[512,128]{1,0:T(8,128)S(1)}, f32[512,128]{1,0:T(8,128)S(1)}, u32[]{:S(2)}, u32[]{:S(2)}) collective-permute-start(f32[512,128]{1,0:T(8,128)S(1)} %get-tuple-element.37.refs_5_.refs_3_), channel_id=1, source_target_pairs={{0,16},{4,20},{8,24},{12,28},{16,0},{20,4},{24,8},{28,12},{1,17},{... | collective-permute-start | bytes 786440 | tf_op jit(solution)/shard_map/ppermute | solution.py:586
  41.5 0.0 collective-permute-start.4
  41.5 12.5 %collective-permute-done.2.refs_6_.refs_4_ = f32[512,128]{1,0:T(8,128)S(1)} collective-permute-done((f32[512,128]{1,0:T(8,128)S(1)}, f32[512,128]{1,0:T(8,128)S(1)}, u32[]{:S(2)}, u32[]{:S(2)}) %collective-permute-start.2) | collective-permute-done | bytes 262176 | tf_op jit(solution)/shard_map/ppermute | solution.py:586
  54.1 14.7 %collective-permute-done.3.refs_7_.refs_5_ = f32[512,128]{1,0:T(8,128)S(1)} collective-permute-done((f32[512,128]{1,0:T(8,128)S(1)}, f32[512,128]{1,0:T(8,128)S(1)}, u32[]{:S(2)}, u32[]{:S(2)}) %collective-permute-start.3) | collective-permute-done | bytes 262176 | tf_op jit(solution)/shard_map/ppermute | solution.py:586
  68.8 0.3 collective-permute-done.4.refs_8_.refs_6_
  69.0 9.3 %weight.1 = (f32[512,128]{1,0:T(8,128)S(1)}, f32[512,128]{1,0:T(8,128)S(1)}, bf16[8,512,512]{2,1,0:T(8,128)(2,1)}, bf16[8,512,512]{2,1,0:T(8,128)(2,1)}) custom-call(f32[4,512,128]{2,1,0:T(8,128)} %get-tuple-element.36.refs_0_, f32[512,128]{1,0:T(8,128)S(1)} %get-tuple-element.32.refs_2_.refs_1_, f32[512,128]{1,0:T(8,128)S(1)} %collective-permute-done.1.refs_2_, ...), custom_call_target="tpu_custom_call" | custom-call | flops 1 | bytes 1 | tf_op jit(solution)/shard_map/weight/pallas_call | solution.py:524
  78.4 0.1 collective-permute-start.5
  78.4 4.7 %left_parts.1 = (f32[4,32,512]{2,1,0:T(8,128)S(1)}, f32[4,32,512]{2,1,0:T(8,128)S(1)}) custom-call(f32[512,128]{1,0:T(8,128)S(1)} %get-tuple-element.42.refs_0_, bf16[8,512,512]{2,1,0:T(8,128)(2,1)} %get-tuple-element.39.refs_1_, bf16[8,512,512]{2,1,0:T(8,128)(2,1)} %get-tuple-element.40.refs_2_, f32[512,128]{1,0:T(8,128)S(1)} %get-tuple-element.37.refs_5_.refs_3_, ...), custom_call_target="tpu_custom_call" | custom-call | flops 1 | bytes 1 | tf_op jit(solution)/shard_map/left_parts/pallas_call | solution.py:524
  83.2 0.0 collective-permute-done.5
  83.2 0.7 add.5
  83.9 16.3 %all-to-all-start = ((f32[16,32,128]{2,1,0:T(8,128)}), f32[16,32,128]{2,1,0:T(8,128)S(1)}, u32[]{:S(2)}, u32[]{:S(2)}) async-start(f32[16,32,128]{2,1,0:T(8,128)} %bitcast.1.refs_0_), calls=%async_computation | async-start | bytes 524288 | tf_op jit(solution)/shard_map/all_to_all | solution.py:670
  100.2 5.2 %pair_peer.1.refs_0_ = f32[16,4,16,128]{3,2,1,0:T(8,128)S(1)} custom-call(f32[16,32,128]{2,1,0:T(8,128)} %bitcast.1.refs_0_, bf16[8,512,512]{2,1,0:T(8,128)(2,1)} %get-tuple-element.44.refs_1_, f32[1024,128]{1,0:T(8,128)} %refs_2_.5), custom_call_target="tpu_custom_call" | custom-call | flops 1 | bytes 1 | tf_op jit(solution)/shard_map/pair_peer/pallas_call | solution.py:524
  105.4 2.0 %collective-permute-start.6 = (f32[16,4,16,128]{3,2,1,0:T(8,128)S(1)}, f32[16,4,16,128]{3,2,1,0:T(8,128)S(1)}, u32[]{:S(2)}, u32[]{:S(2)}) collective-permute-start(f32[16,4,16,128]{3,2,1,0:T(8,128)S(1)} %pair_peer.1.refs_0_), channel_id=1, source_target_pairs={{0,4},{4,0},{8,12},{12,8},{16,20},{20,16},{24,28},{28,24},{1,5},{5... | collective-permute-start | bytes 1572872 | tf_op jit(solution)/shard_map/ppermute | solution.py:668
  107.4 3.5 %all-to-all-done.refs_1_.refs_0_ = f32[16,32,128]{2,1,0:T(8,128)S(1)} async-done(((f32[16,32,128]{2,1,0:T(8,128)}), f32[16,32,128]{2,1,0:T(8,128)S(1)}, u32[]{:S(2)}, u32[]{:S(2)}) %all-to-all-start) | async-done | bytes 262176 | tf_op jit(solution)/shard_map/all_to_all | solution.py:670
  110.8 0.7 weight_sum.1.refs_0_
  111.6 3.5 %all-to-all-start.1 = ((f32[16,32,128]{2,1,0:T(8,128)}), f32[16,32,128]{2,1,0:T(8,128)S(1)}, u32[]{:S(2)}, u32[]{:S(2)}) async-start(f32[16,32,128]{2,1,0:T(8,128)} %weight_sum.1.refs_0_), calls=%async_computation.1 | async-start | bytes 524288 | tf_op jit(solution)/shard_map/all_to_all | solution.py:684
  115.1 1.9 %collective-permute-start.7 = (f32[4,32,512]{2,1,0:T(8,128)S(1)}, f32[4,32,512]{2,1,0:T(8,128)S(1)}, u32[]{:S(2)}, u32[]{:S(2)}) collective-permute-start(f32[4,32,512]{2,1,0:T(8,128)S(1)} %get-tuple-element.47), channel_id=1, source_target_pairs={{0,4},{4,0},{8,12},{12,8},{16,20},{20,16},{24,28},{28,24},{1,5},{5... | collective-permute-start | bytes 786440 | tf_op jit(solution)/shard_map/ppermute | solution.py:646
  117.1 11.6 %collective-permute-done.7.refs_2_ = f32[4,32,512]{2,1,0:T(8,128)S(1)} collective-permute-done((f32[4,32,512]{2,1,0:T(8,128)S(1)}, f32[4,32,512]{2,1,0:T(8,128)S(1)}, u32[]{:S(2)}, u32[]{:S(2)}) %collective-permute-start.7) | collective-permute-done | bytes 262176 | tf_op jit(solution)/shard_map/ppermute | solution.py:646
  128.6 0.6 collective-permute-start.10
  129.2 1.2 collective-permute-start.8
  130.4 0.5 collective-permute-start.9
  130.9 5.2 %pair_own.1.refs_0_ = f32[16,4,16,128]{3,2,1,0:T(8,128)S(1)} custom-call(f32[16,32,128]{2,1,0:T(8,128)} %weight_sum.1.refs_0_, bf16[8,512,512]{2,1,0:T(8,128)(2,1)} %get-tuple-element.45.refs_1_, f32[1024,128]{1,0:T(8,128)} %refs_2_.5), custom_call_target="tpu_custom_call" | custom-call | flops 1 | bytes 1 | tf_op jit(solution)/shard_map/pair_own/pallas_call | solution.py:524
  136.0 0.0 collective-permute-done.6.refs_1_
  136.0 1.0 merge.1
  137.0 0.0 collective-permute-done.10.refs_3_
  137.1 0.0 collective-permute-done.8.refs_1_
  137.1 0.0 collective-permute-done.9.refs_2_
  137.1 0.8 turn_left.1
  137.9 0.0 reduce-scatter.2.cloned.1.call-done
  137.9 0.0 copy-start
  137.9 0.9 copy-done
  138.8 1.1 turn_right.1
  140.0 0.0 all-to-all-done.1
  140.0 0.0 collective-permute-start.11
  140.0 1.5 %collective-permute-done.11.refs_1_ = f32[512,128]{1,0:T(8,128)S(1)} collective-permute-done((f32[512,128]{1,0:T(8,128)S(1)}, f32[512,128]{1,0:T(8,128)S(1)}, u32[]{:S(2)}, u32[]{:S(2)}) %collective-permute-start.11) | collective-permute-done | bytes 262176 | tf_op jit(solution)/shard_map/ppermute | solution.py:723
  141.5 1.1 place.1
  (1 shorter events, 0.0 us)
Async XLA Ops:
  7.2 130.7 %reduce-scatter.2.cloned.1.call-start = ((), (), s32[]{:S(2)}) async-start(), calls=%async_computation.3 | async-start | bytes 1310720 | tf_op jit(solution)/shard_map/reduce_scatter | solution.py:612
  9.2 20.6 %collective-permute-start = (f32[16,4,16,128]{3,2,1,0:T(8,128)S(1)}, f32[16,4,16,128]{3,2,1,0:T(8,128)S(1)}, u32[]{:S(2)}, u32[]{:S(2)}) collective-permute-start(f32[16,4,16,128]{3,2,1,0:T(8,128)S(1)} %get-tuple-element.34), channel_id=1, source_target_pairs={{0,4},{4,0},{8,12},{12,8},{16,20},{20,16},{24,28},{28,24},{1,5},{5... | collective-permute-start | bytes 1572872 | tf_op jit(solution)/shard_map/ppermute | solution.py:587
  12.2 17.5 %collective-permute-start.1 = (f32[512,128]{1,0:T(8,128)S(1)}, f32[512,128]{1,0:T(8,128)S(1)}, u32[]{:S(2)}, u32[]{:S(2)}) collective-permute-start(f32[512,128]{1,0:T(8,128)S(1)} %get-tuple-element.32.refs_2_.refs_1_), channel_id=1, source_target_pairs={{0,4},{4,0},{8,12},{12,8},{16,20},{20,16},{24,28},{28,24},{1,5},{5... | collective-permute-start | bytes 786440 | tf_op jit(solution)/shard_map/ppermute | solution.py:588
  37.1 17.0 %collective-permute-start.2 = (f32[512,128]{1,0:T(8,128)S(1)}, f32[512,128]{1,0:T(8,128)S(1)}, u32[]{:S(2)}, u32[]{:S(2)}) collective-permute-start(f32[512,128]{1,0:T(8,128)S(1)} %get-tuple-element.37.refs_5_.refs_3_), channel_id=1, source_target_pairs={{0,8},{4,12},{8,0},{12,4},{16,24},{20,28},{24,16},{28,20},{1,9},{5... | collective-permute-start | bytes 786440 | tf_op jit(solution)/shard_map/ppermute | solution.py:586
  39.0 29.8 %collective-permute-start.3 = (f32[512,128]{1,0:T(8,128)S(1)}, f32[512,128]{1,0:T(8,128)S(1)}, u32[]{:S(2)}, u32[]{:S(2)}) collective-permute-start(f32[512,128]{1,0:T(8,128)S(1)} %get-tuple-element.37.refs_5_.refs_3_), channel_id=1, source_target_pairs={{0,16},{4,20},{8,24},{12,28},{16,0},{20,4},{24,8},{28,12},{1,17},{... | collective-permute-start | bytes 786440 | tf_op jit(solution)/shard_map/ppermute | solution.py:586
  41.5 27.5 %collective-permute-start.4 = (f32[512,128]{1,0:T(8,128)S(1)}, f32[512,128]{1,0:T(8,128)S(1)}, u32[]{:S(2)}, u32[]{:S(2)}) collective-permute-start(f32[512,128]{1,0:T(8,128)S(1)} %get-tuple-element.37.refs_5_.refs_3_), channel_id=1, source_target_pairs={{0,24},{4,28},{8,16},{12,20},{16,8},{20,12},{24,0},{28,4},{1,25},{... | collective-permute-start | bytes 786440 | tf_op jit(solution)/shard_map/ppermute | solution.py:586
  78.4 4.8 %collective-permute-start.5 = (f32[512,128]{1,0:T(8,128)S(1)}, f32[512,128]{1,0:T(8,128)S(1)}, u32[]{:S(2)}, u32[]{:S(2)}) collective-permute-start(f32[512,128]{1,0:T(8,128)S(1)} %get-tuple-element.43), channel_id=1, source_target_pairs={{0,1},{1,0},{2,3},{3,2},{4,5},{5,4},{6,7},{7,6},{8,9},{9,8},{10,11... | collective-permute-start | bytes 786440 | tf_op jit(solution)/shard_map/ppermute | solution.py:629
  83.9 26.9 %all-to-all-start = ((f32[16,32,128]{2,1,0:T(8,128)}), f32[16,32,128]{2,1,0:T(8,128)S(1)}, u32[]{:S(2)}, u32[]{:S(2)}) async-start(f32[16,32,128]{2,1,0:T(8,128)} %bitcast.1.refs_0_), calls=%async_computation | async-start | bytes 524288 | tf_op jit(solution)/shard_map/all_to_all | solution.py:670
  105.4 30.7 %collective-permute-start.6 = (f32[16,4,16,128]{3,2,1,0:T(8,128)S(1)}, f32[16,4,16,128]{3,2,1,0:T(8,128)S(1)}, u32[]{:S(2)}, u32[]{:S(2)}) collective-permute-start(f32[16,4,16,128]{3,2,1,0:T(8,128)S(1)} %pair_peer.1.refs_0_), channel_id=1, source_target_pairs={{0,4},{4,0},{8,12},{12,8},{16,20},{20,16},{24,28},{28,24},{1,5},{5... | collective-permute-start | bytes 1572872 | tf_op jit(solution)/shard_map/ppermute | solution.py:668
  111.6 28.4 %all-to-all-start.1 = ((f32[16,32,128]{2,1,0:T(8,128)}), f32[16,32,128]{2,1,0:T(8,128)S(1)}, u32[]{:S(2)}, u32[]{:S(2)}) async-start(f32[16,32,128]{2,1,0:T(8,128)} %weight_sum.1.refs_0_), calls=%async_computation.1 | async-start | bytes 524288 | tf_op jit(solution)/shard_map/all_to_all | solution.py:684
  115.1 13.5 %collective-permute-start.7 = (f32[4,32,512]{2,1,0:T(8,128)S(1)}, f32[4,32,512]{2,1,0:T(8,128)S(1)}, u32[]{:S(2)}, u32[]{:S(2)}) collective-permute-start(f32[4,32,512]{2,1,0:T(8,128)S(1)} %get-tuple-element.47), channel_id=1, source_target_pairs={{0,4},{4,0},{8,12},{12,8},{16,20},{20,16},{24,28},{28,24},{1,5},{5... | collective-permute-start | bytes 786440 | tf_op jit(solution)/shard_map/ppermute | solution.py:646
  128.6 8.4 %collective-permute-start.10 = (f32[32,512]{1,0:T(8,128)S(1)}, f32[32,512]{1,0:T(8,128)S(1)}, u32[]{:S(2)}, u32[]{:S(2)}) collective-permute-start(f32[32,512]{1,0:T(8,128)S(1)} %get-tuple-element.51), channel_id=1, source_target_pairs={{0,3},{1,2},{2,1},{3,0},{4,7},{5,6},{6,5},{7,4},{8,11},{9,10},{10,... | collective-permute-start | bytes 196616 | tf_op jit(solution)/shard_map/ppermute | solution.py:687
  129.2 7.8 %collective-permute-start.8 = (f32[32,512]{1,0:T(8,128)S(1)}, f32[32,512]{1,0:T(8,128)S(1)}, u32[]{:S(2)}, u32[]{:S(2)}) collective-permute-start(f32[32,512]{1,0:T(8,128)S(1)} %get-tuple-element.49), channel_id=1, source_target_pairs={{0,1},{1,0},{2,3},{3,2},{4,5},{5,4},{6,7},{7,6},{8,9},{9,8},{10,11... | collective-permute-start | bytes 196616 | tf_op jit(solution)/shard_map/ppermute | solution.py:687
  130.4 6.7 %collective-permute-start.9 = (f32[32,512]{1,0:T(8,128)S(1)}, f32[32,512]{1,0:T(8,128)S(1)}, u32[]{:S(2)}, u32[]{:S(2)}) collective-permute-start(f32[32,512]{1,0:T(8,128)S(1)} %get-tuple-element.50), channel_id=1, source_target_pairs={{0,2},{1,3},{2,0},{3,1},{4,6},{5,7},{6,4},{7,5},{8,10},{9,11},{10,... | collective-permute-start | bytes 196616 | tf_op jit(solution)/shard_map/ppermute | solution.py:687
  137.9 1.0 copy-start
  140.0 1.5 %collective-permute-start.11 = (f32[512,128]{1,0:T(8,128)S(1)}, f32[512,128]{1,0:T(8,128)S(1)}, u32[]{:S(2)}, u32[]{:S(2)}) collective-permute-start(f32[512,128]{1,0:T(8,128)S(1)} %bitcast.5), channel_id=1, source_target_pairs={{0,1},{1,0},{2,3},{3,2},{4,5},{5,4},{6,7},{7,6},{8,9},{9,8},{10,11... | collective-permute-start | bytes 786440 | tf_op jit(solution)/shard_map/ppermute | solution.py:723
Sparse Core Ops, SparseCore 0:
  37.2 42.5 reduce-scatter.1

commit v12 on v11

--- a/solution.py
+++ b/solution.py
@@ -510,7 +510,17 @@
     return jax.ShapeDtypeStruct(sizes, kind)
 
 
-def call(kernel, out_shape, scratch=(), name=None, limit=16 * MIB, far=(), after=(), out_specs=None):
+def call(
+    kernel,
+    out_shape,
+    scratch=(),
+    name=None,
+    limit=16 * MIB,
+    far=(),
+    after=(),
+    out_specs=None,
+    flops=1,
+):
     def run(*operands):
         vmem = pl.BlockSpec(memory_space=pltpu.VMEM)
         hbm = pl.BlockSpec(memory_space=pltpu.HBM)
@@ -527,7 +537,7 @@
             in_specs=in_specs,
             scratch_shapes=list(scratch),
             compiler_params=pltpu.CompilerParams(vmem_limit_bytes=limit),
-            cost_estimate=pl.CostEstimate(flops=1, bytes_accessed=1, transcendentals=0),
+            cost_estimate=pl.CostEstimate(flops=flops, bytes_accessed=1, transcendentals=0),
             name=name,
             **extra,
         )(*after, *operands)
@@ -560,6 +570,7 @@
 
     limit = 20 * MIB * max(1, blocks * depth * fold // LANES * 2 // fold)
     large = functools.partial(call, limit=limit)
+    work = 4 * 2 * rows * 2 * blocks * depth * outer * pairs * 3
 
     by_side = cotangent.reshape(rows, blocks, 2, depth, pairs)
     half_cotangent = shape(rows, blocks, depth, pairs)
@@ -624,6 +635,7 @@
         ],
         "weight",
         after=[right_parts],
+        flops=2 * work,
         out_specs=[vmem, vmem, hbm, hbm],
     )(left, left_peer, cotangent_own, cotangent_peer, *rights)
     sent = lax.ppermute(send, "inner", cores)
@@ -642,6 +654,7 @@
         "left_parts",
         far=[0, 1],
         after=[keep],
+        flops=work,
     )(grad_own, grad_peer, *rights)
     left_other = lax.ppermute(left_other, "blk", partner)
     keep, left_own = lax.optimization_barrier((keep, left_own))
@@ -662,6 +675,7 @@
             name,
             far=[0, 1],
             after=after,
+            flops=work,
         )(values, projection_matrix)
 
     pair_other = pair(outer_peer, [pieces], "pair_peer")

time: 150 us -> 97.5 us (0.65)
  waiting for transfers between devices: 55.5 us -> 12.9 us
  starting transfers between devices: 33.6 us -> 23.8 us
    ppermute x3, waiting for transfers between devices: 27.5 us -> 0.01 us  [local(): rights.append(lax.ppermute(right, 'blk', slot_moves[slot]))]
    ppermute x1, waiting for transfers between devices: 11.6 us -> 0.01 us  [local(): left_other = lax.ppermute(left_other, 'blk', partner)]
    all_to_all x2, starting transfers between devices: 19.8 us -> 10 us  [local(): lax.all_to_all(pieces, everyone, 0, 0, axis_index_groups=core_groups)]
    ppermute x1, waiting for transfers between devices: 11.4 us -> 6.84 us  [local(): left_peer = lax.ppermute(left, 'blk', partner)]
  transfers between devices with their start and end apart: 15 -> 15, of which waited for: 7 -> 4; matrix products, arithmetic and copies ran while one was open for 0% -> 1% of each run, Pallas kernels for 23% -> 43%
where the time goes in v12:
time: 97.5 us; the launch traced here: 97.1 us
  Pallas kernels  44.4 us (46%)
  starting transfers between devices  23.8 us (24%)
  between operations  14.2 us (15%)
  waiting for transfers between devices  12.9 us (13%)
    pallas_call x13, Pallas kernels, run(): pl.pallas_call(lambda *refs: kernel(*refs[len(after):]), out_shape=out_sh...  44.4 us
    all_to_all x2, starting transfers between devices, local(): lax.all_to_all(pieces, everyone, 0, 0, axis_index_groups=core_groups)  10 us
    ppermute x1, waiting for transfers between devices, local(): left_peer = lax.ppermute(left, 'blk', partner)  6.84 us
    ppermute x3, starting transfers between devices, local(): rights.append(lax.ppermute(right, 'blk', slot_moves[slot]))  4.6 us
    all_to_all x2, waiting for transfers between devices, local(): lax.all_to_all(pieces, everyone, 0, 0, axis_index_groups=core_groups)  4.51 us
    ppermute x1, starting transfers between devices, local(): cotangent_peer = lax.ppermute(cotangent_send, 'blk', partner)  3.03 us
    ppermute x3, starting transfers between devices, local(): lax.ppermute(part, 'inner', inner_moves[slot])  2.21 us
    ppermute x1, starting transfers between devices, local(): pair_found = lax.ppermute(pair_other, 'blk', partner)  1.99 us
  transfers between devices with their start and end apart: 15, of which 4 were waited for; matrix products, arithmetic and copies ran while one was open for 1% of the time, Pallas kernels for 43%

profile of v12, /device:TPU:0, one launch (start us, length us, event | category | flops | bytes accessed | tf_op | source)
XLA Modules:
  0.0 97.1 jit_solution(1035583035365634339)
XLA Ops:
  7.2 0.0 reduce-scatter.2.cloned.1.call-start
  7.2 2.0 %prepare.1 = (f32[512,128]{1,0:T(8,128)S(1)}, f32[512,128]{1,0:T(8,128)S(1)}, f32[16,4,16,128]{3,2,1,0:T(8,128)S(1)}, f32[16,4,16,128]{3,2,1,0:T(8,128)S(1)}, f32[1024,128]{1,0:T(8,128)S(1)}) custom-call(f32[16,4,2,16,128]{4,3,2,1,0:T(8,128)} %bitcast.8, f32[16,4096]{1,0:T(8,128)} %refs_1_.1, f32[16,4096]{1,0:T(8,128)} %refs_2_.3, f32[1024,128]{1,0:T(8,128)} %refs_2_.5), custom_call_target="tpu_custom_call" | custom-call | flops 1 | bytes 1 | tf_op jit(solution)/shard_map/prepare/pallas_call | solution.py:534
  9.2 3.0 %collective-permute-start = (f32[16,4,16,128]{3,2,1,0:T(8,128)S(1)}, f32[16,4,16,128]{3,2,1,0:T(8,128)S(1)}, u32[]{:S(2)}, u32[]{:S(2)}) collective-permute-start(f32[16,4,16,128]{3,2,1,0:T(8,128)S(1)} %get-tuple-element.34), channel_id=1, source_target_pairs={{0,4},{4,0},{8,12},{12,8},{16,20},{20,16},{24,28},{28,24},{1,5},{5... | collective-permute-start | bytes 1572872 | tf_op jit(solution)/shard_map/ppermute | solution.py:598
  12.2 0.1 collective-permute-start.1
  12.3 2.0 %collective-permute-start.2 = (f32[512,128]{1,0:T(8,128)S(1)}, f32[512,128]{1,0:T(8,128)S(1)}, u32[]{:S(2)}, u32[]{:S(2)}) collective-permute-start(f32[512,128]{1,0:T(8,128)S(1)} %get-tuple-element.37.refs_5_.refs_3_), channel_id=1, source_target_pairs={{0,8},{4,12},{8,0},{12,4},{16,24},{20,28},{24,16},{28,20},{1,9},{5... | collective-permute-start | bytes 786440 | tf_op jit(solution)/shard_map/ppermute | solution.py:597
  14.3 2.6 %collective-permute-start.3 = (f32[512,128]{1,0:T(8,128)S(1)}, f32[512,128]{1,0:T(8,128)S(1)}, u32[]{:S(2)}, u32[]{:S(2)}) collective-permute-start(f32[512,128]{1,0:T(8,128)S(1)} %get-tuple-element.37.refs_5_.refs_3_), channel_id=1, source_target_pairs={{0,16},{4,20},{8,24},{12,28},{16,0},{20,4},{24,8},{28,12},{1,17},{... | collective-permute-start | bytes 786440 | tf_op jit(solution)/shard_map/ppermute | solution.py:597
  16.9 0.0 collective-permute-start.4
  16.9 6.0 %gradient_own.1 = (bf16[8,512,512]{2,1,0:T(8,128)(2,1)}, f32[8,128,256]{2,1,0:T(8,128)S(1)}, bf16[512,768]{1,0:T(8,128)(2,1)S(1)}) custom-call(f32[1024,128]{1,0:T(8,128)S(1)} %get-tuple-element.30.refs_0_, f32[16,4,16,128]{3,2,1,0:T(8,128)S(1)} %get-tuple-element.31.refs_1_.refs_3_, f32[512,128]{1,0:T(8,128)S(1)} %get-tuple-element.32.refs_2_.refs_1_), custom_call_target="tpu_custom_call" | custom-call | flops 1 | bytes 1 | tf_op jit(solution)/shard_map/gradient_own/pallas_call | solution.py:534
  22.9 6.8 %collective-permute-done.1.refs_2_ = f32[512,128]{1,0:T(8,128)S(1)} collective-permute-done((f32[512,128]{1,0:T(8,128)S(1)}, f32[512,128]{1,0:T(8,128)S(1)}, u32[]{:S(2)}, u32[]{:S(2)}) %collective-permute-start.1) | collective-permute-done | bytes 262176 | tf_op jit(solution)/shard_map/ppermute | solution.py:599
  29.8 0.0 collective-permute-done.refs_1_.refs_4_
  29.8 7.3 %right_parts.1 = (bf16[8,512,512]{2,1,0:T(8,128)(2,1)}, f32[4,512,128]{2,1,0:T(8,128)}) custom-call(bf16[512,768]{1,0:T(8,128)(2,1)S(1)} %get-tuple-element.33.refs_0_, f32[16,4,16,128]{3,2,1,0:T(8,128)S(1)} %collective-permute-done.refs_1_.refs_4_, f32[512,128]{1,0:T(8,128)S(1)} %collective-permute-done.1.refs_2_, f32[8,128,256]{2,1,0:T(8,128)S(1)} %get-tuple-element.35.refs_3_), custom_call_target="tpu_custom_call" | custom-call | flops 1 | bytes 1 | tf_op jit(solution)/shard_map/right_parts/pallas_call | solution.py:534
  37.1 0.0 reduce-scatter.2.cloned.1.call-update
  37.1 0.0 collective-permute-done.2.refs_6_.refs_4_
  37.1 0.0 collective-permute-done.3.refs_7_.refs_5_
  37.1 0.0 collective-permute-done.4.refs_8_.refs_6_
  37.1 9.3 %weight.1 = (f32[512,128]{1,0:T(8,128)S(1)}, f32[512,128]{1,0:T(8,128)S(1)}, bf16[8,512,512]{2,1,0:T(8,128)(2,1)}, bf16[8,512,512]{2,1,0:T(8,128)(2,1)}) custom-call(f32[4,512,128]{2,1,0:T(8,128)} %get-tuple-element.36.refs_0_, f32[512,128]{1,0:T(8,128)S(1)} %get-tuple-element.32.refs_2_.refs_1_, f32[512,128]{1,0:T(8,128)S(1)} %collective-permute-done.1.refs_2_, ...), custom_call_target="tpu_custom_call" | custom-call | flops 12884901888 | bytes 1 | tf_op jit(solution)/shard_map/weight/pallas_call | solution.py:534
  46.4 0.1 collective-permute-start.5
  46.5 4.7 %left_parts.1 = (f32[4,32,512]{2,1,0:T(8,128)S(1)}, f32[4,32,512]{2,1,0:T(8,128)S(1)}) custom-call(f32[512,128]{1,0:T(8,128)S(1)} %get-tuple-element.42.refs_0_, bf16[8,512,512]{2,1,0:T(8,128)(2,1)} %get-tuple-element.39.refs_1_, bf16[8,512,512]{2,1,0:T(8,128)(2,1)} %get-tuple-element.40.refs_2_, f32[512,128]{1,0:T(8,128)S(1)} %get-tuple-element.37.refs_5_.refs_3_, ...), custom_call_target="tpu_custom_call" | custom-call | flops 6442450944 | bytes 1 | tf_op jit(solution)/shard_map/left_parts/pallas_call | solution.py:534
  51.2 1.8 %collective-permute-start.7 = (f32[4,32,512]{2,1,0:T(8,128)S(1)}, f32[4,32,512]{2,1,0:T(8,128)S(1)}, u32[]{:S(2)}, u32[]{:S(2)}) collective-permute-start(f32[4,32,512]{2,1,0:T(8,128)S(1)} %get-tuple-element.47), channel_id=1, source_target_pairs={{0,4},{4,0},{8,12},{12,8},{16,20},{20,16},{24,28},{28,24},{1,5},{5... | collective-permute-start | bytes 786440 | tf_op jit(solution)/shard_map/ppermute | solution.py:659
  53.0 0.0 collective-permute-done.5
  53.0 0.7 add.5
  53.8 5.9 %all-to-all-start = ((f32[16,32,128]{2,1,0:T(8,128)}), f32[16,32,128]{2,1,0:T(8,128)S(1)}, u32[]{:S(2)}, u32[]{:S(2)}) async-start(f32[16,32,128]{2,1,0:T(8,128)} %bitcast.1.refs_0_), calls=%async_computation | async-start | bytes 524288 | tf_op jit(solution)/shard_map/all_to_all | solution.py:684
  59.7 5.2 %pair_peer.1.refs_0_ = f32[16,4,16,128]{3,2,1,0:T(8,128)S(1)} custom-call(f32[16,32,128]{2,1,0:T(8,128)} %bitcast.1.refs_0_, bf16[8,512,512]{2,1,0:T(8,128)(2,1)} %get-tuple-element.44.refs_1_, f32[1024,128]{1,0:T(8,128)} %refs_2_.5), custom_call_target="tpu_custom_call" | custom-call | flops 6442450944 | bytes 1 | tf_op jit(solution)/shard_map/pair_peer/pallas_call | solution.py:534
  64.9 2.0 %collective-permute-start.6 = (f32[16,4,16,128]{3,2,1,0:T(8,128)S(1)}, f32[16,4,16,128]{3,2,1,0:T(8,128)S(1)}, u32[]{:S(2)}, u32[]{:S(2)}) collective-permute-start(f32[16,4,16,128]{3,2,1,0:T(8,128)S(1)} %pair_peer.1.refs_0_), channel_id=1, source_target_pairs={{0,4},{4,0},{8,12},{12,8},{16,20},{20,16},{24,28},{28,24},{1,5},{5... | collective-permute-start | bytes 1572872 | tf_op jit(solution)/shard_map/ppermute | solution.py:682
  66.9 0.0 collective-permute-done.7.refs_2_
  66.9 3.9 %all-to-all-done.refs_1_.refs_0_ = f32[16,32,128]{2,1,0:T(8,128)S(1)} async-done(((f32[16,32,128]{2,1,0:T(8,128)}), f32[16,32,128]{2,1,0:T(8,128)S(1)}, u32[]{:S(2)}, u32[]{:S(2)}) %all-to-all-start) | async-done | bytes 262176 | tf_op jit(solution)/shard_map/all_to_all | solution.py:684
  70.8 0.5 collective-permute-start.10
  71.2 1.1 %collective-permute-start.8 = (f32[32,512]{1,0:T(8,128)S(1)}, f32[32,512]{1,0:T(8,128)S(1)}, u32[]{:S(2)}, u32[]{:S(2)}) collective-permute-start(f32[32,512]{1,0:T(8,128)S(1)} %get-tuple-element.49), channel_id=1, source_target_pairs={{0,1},{1,0},{2,3},{3,2},{4,5},{5,4},{6,7},{7,6},{8,9},{9,8},{10,11... | collective-permute-start | bytes 196616 | tf_op jit(solution)/shard_map/ppermute | solution.py:701
  72.3 0.7 collective-permute-start.9
  73.0 0.7 weight_sum.1.refs_0_
  73.7 4.1 %all-to-all-start.1 = ((f32[16,32,128]{2,1,0:T(8,128)}), f32[16,32,128]{2,1,0:T(8,128)S(1)}, u32[]{:S(2)}, u32[]{:S(2)}) async-start(f32[16,32,128]{2,1,0:T(8,128)} %weight_sum.1.refs_0_), calls=%async_computation.1 | async-start | bytes 524288 | tf_op jit(solution)/shard_map/all_to_all | solution.py:698
  77.8 5.2 %pair_own.1.refs_0_ = f32[16,4,16,128]{3,2,1,0:T(8,128)S(1)} custom-call(f32[16,32,128]{2,1,0:T(8,128)} %weight_sum.1.refs_0_, bf16[8,512,512]{2,1,0:T(8,128)(2,1)} %get-tuple-element.45.refs_1_, f32[1024,128]{1,0:T(8,128)} %refs_2_.5), custom_call_target="tpu_custom_call" | custom-call | flops 6442450944 | bytes 1 | tf_op jit(solution)/shard_map/pair_own/pallas_call | solution.py:534
  83.0 0.0 collective-permute-done.6.refs_1_
  83.0 1.0 %merge.1 = f32[16,4,2,16,128]{4,3,2,1,0:T(8,128)} custom-call(f32[16,4,16,128]{3,2,1,0:T(8,128)S(1)} %pair_own.1.refs_0_, f32[16,4,16,128]{3,2,1,0:T(8,128)S(1)} %collective-permute-done.6.refs_1_), custom_call_target="tpu_custom_call" | custom-call | flops 1 | bytes 1 | tf_op jit(solution)/shard_map/merge/pallas_call | solution.py:534
  84.0 0.0 collective-permute-done.10.refs_3_
  84.0 0.0 collective-permute-done.8.refs_1_
  84.0 0.0 collective-permute-done.9.refs_2_
  84.0 0.8 turn_left.1
  84.8 0.0 reduce-scatter.2.cloned.1.call-done
  84.8 0.0 copy-start
  84.8 0.9 copy-done
  85.8 1.1 %turn_right.1 = f32[16,4096]{1,0:T(8,128)} custom-call(f32[512,128]{1,0:T(8,128)S(1)} %bitcast.7), custom_call_target="tpu_custom_call" | custom-call | flops 1 | bytes 1 | tf_op jit(solution)/shard_map/turn_right/pallas_call | solution.py:534
  86.9 0.7 all-to-all-done.1
  87.6 0.0 collective-permute-start.11
  87.6 1.5 %collective-permute-done.11.refs_1_ = f32[512,128]{1,0:T(8,128)S(1)} collective-permute-done((f32[512,128]{1,0:T(8,128)S(1)}, f32[512,128]{1,0:T(8,128)S(1)}, u32[]{:S(2)}, u32[]{:S(2)}) %collective-permute-start.11) | collective-permute-done | bytes 262176 | tf_op jit(solution)/shard_map/ppermute | solution.py:737
  89.1 1.1 %place.1 = f32[1024,128]{1,0:T(8,128)} custom-call(f32[512,128]{1,0:T(8,128)S(1)} %bitcast.6, f32[512,128]{1,0:T(8,128)S(1)} %collective-permute-done.11.refs_1_), custom_call_target="tpu_custom_call" | custom-call | flops 1 | bytes 1 | tf_op jit(solution)/shard_map/place/pallas_call | solution.py:534
  (1 shorter events, 0.0 us)
Async XLA Ops:
  7.2 77.7 %reduce-scatter.2.cloned.1.call-start = ((), (), s32[]{:S(2)}) async-start(), calls=%async_computation.3 | async-start | bytes 1310720 | tf_op jit(solution)/shard_map/reduce_scatter | solution.py:623
  9.2 20.6 %collective-permute-start = (f32[16,4,16,128]{3,2,1,0:T(8,128)S(1)}, f32[16,4,16,128]{3,2,1,0:T(8,128)S(1)}, u32[]{:S(2)}, u32[]{:S(2)}) collective-permute-start(f32[16,4,16,128]{3,2,1,0:T(8,128)S(1)} %get-tuple-element.34), channel_id=1, source_target_pairs={{0,4},{4,0},{8,12},{12,8},{16,20},{20,16},{24,28},{28,24},{1,5},{5... | collective-permute-start | bytes 1572872 | tf_op jit(solution)/shard_map/ppermute | solution.py:598
  12.2 17.5 %collective-permute-start.1 = (f32[512,128]{1,0:T(8,128)S(1)}, f32[512,128]{1,0:T(8,128)S(1)}, u32[]{:S(2)}, u32[]{:S(2)}) collective-permute-start(f32[512,128]{1,0:T(8,128)S(1)} %get-tuple-element.32.refs_2_.refs_1_), channel_id=1, source_target_pairs={{0,4},{4,0},{8,12},{12,8},{16,20},{20,16},{24,28},{28,24},{1,5},{5... | collective-permute-start | bytes 786440 | tf_op jit(solution)/shard_map/ppermute | solution.py:599
  12.3 24.8 %collective-permute-start.2 = (f32[512,128]{1,0:T(8,128)S(1)}, f32[512,128]{1,0:T(8,128)S(1)}, u32[]{:S(2)}, u32[]{:S(2)}) collective-permute-start(f32[512,128]{1,0:T(8,128)S(1)} %get-tuple-element.37.refs_5_.refs_3_), channel_id=1, source_target_pairs={{0,8},{4,12},{8,0},{12,4},{16,24},{20,28},{24,16},{28,20},{1,9},{5... | collective-permute-start | bytes 786440 | tf_op jit(solution)/shard_map/ppermute | solution.py:597
  14.3 22.8 %collective-permute-start.3 = (f32[512,128]{1,0:T(8,128)S(1)}, f32[512,128]{1,0:T(8,128)S(1)}, u32[]{:S(2)}, u32[]{:S(2)}) collective-permute-start(f32[512,128]{1,0:T(8,128)S(1)} %get-tuple-element.37.refs_5_.refs_3_), channel_id=1, source_target_pairs={{0,16},{4,20},{8,24},{12,28},{16,0},{20,4},{24,8},{28,12},{1,17},{... | collective-permute-start | bytes 786440 | tf_op jit(solution)/shard_map/ppermute | solution.py:597
  16.9 20.2 %collective-permute-start.4 = (f32[512,128]{1,0:T(8,128)S(1)}, f32[512,128]{1,0:T(8,128)S(1)}, u32[]{:S(2)}, u32[]{:S(2)}) collective-permute-start(f32[512,128]{1,0:T(8,128)S(1)} %get-tuple-element.37.refs_5_.refs_3_), channel_id=1, source_target_pairs={{0,24},{4,28},{8,16},{12,20},{16,8},{20,12},{24,0},{28,4},{1,25},{... | collective-permute-start | bytes 786440 | tf_op jit(solution)/shard_map/ppermute | solution.py:597
  46.4 6.6 %collective-permute-start.5 = (f32[512,128]{1,0:T(8,128)S(1)}, f32[512,128]{1,0:T(8,128)S(1)}, u32[]{:S(2)}, u32[]{:S(2)}) collective-permute-start(f32[512,128]{1,0:T(8,128)S(1)} %get-tuple-element.43), channel_id=1, source_target_pairs={{0,1},{1,0},{2,3},{3,2},{4,5},{5,4},{6,7},{7,6},{8,9},{9,8},{10,11... | collective-permute-start | bytes 786440 | tf_op jit(solution)/shard_map/ppermute | solution.py:641
  51.2 15.6 %collective-permute-start.7 = (f32[4,32,512]{2,1,0:T(8,128)S(1)}, f32[4,32,512]{2,1,0:T(8,128)S(1)}, u32[]{:S(2)}, u32[]{:S(2)}) collective-permute-start(f32[4,32,512]{2,1,0:T(8,128)S(1)} %get-tuple-element.47), channel_id=1, source_target_pairs={{0,4},{4,0},{8,12},{12,8},{16,20},{20,16},{24,28},{28,24},{1,5},{5... | collective-permute-start | bytes 786440 | tf_op jit(solution)/shard_map/ppermute | solution.py:659
  53.8 17.0 %all-to-all-start = ((f32[16,32,128]{2,1,0:T(8,128)}), f32[16,32,128]{2,1,0:T(8,128)S(1)}, u32[]{:S(2)}, u32[]{:S(2)}) async-start(f32[16,32,128]{2,1,0:T(8,128)} %bitcast.1.refs_0_), calls=%async_computation | async-start | bytes 524288 | tf_op jit(solution)/shard_map/all_to_all | solution.py:684
  64.9 18.1 %collective-permute-start.6 = (f32[16,4,16,128]{3,2,1,0:T(8,128)S(1)}, f32[16,4,16,128]{3,2,1,0:T(8,128)S(1)}, u32[]{:S(2)}, u32[]{:S(2)}) collective-permute-start(f32[16,4,16,128]{3,2,1,0:T(8,128)S(1)} %pair_peer.1.refs_0_), channel_id=1, source_target_pairs={{0,4},{4,0},{8,12},{12,8},{16,20},{20,16},{24,28},{28,24},{1,5},{5... | collective-permute-start | bytes 1572872 | tf_op jit(solution)/shard_map/ppermute | solution.py:682
  70.8 13.2 %collective-permute-start.10 = (f32[32,512]{1,0:T(8,128)S(1)}, f32[32,512]{1,0:T(8,128)S(1)}, u32[]{:S(2)}, u32[]{:S(2)}) collective-permute-start(f32[32,512]{1,0:T(8,128)S(1)} %get-tuple-element.51), channel_id=1, source_target_pairs={{0,3},{1,2},{2,1},{3,0},{4,7},{5,6},{6,5},{7,4},{8,11},{9,10},{10,... | collective-permute-start | bytes 196616 | tf_op jit(solution)/shard_map/ppermute | solution.py:701
  71.2 12.8 %collective-permute-start.8 = (f32[32,512]{1,0:T(8,128)S(1)}, f32[32,512]{1,0:T(8,128)S(1)}, u32[]{:S(2)}, u32[]{:S(2)}) collective-permute-start(f32[32,512]{1,0:T(8,128)S(1)} %get-tuple-element.49), channel_id=1, source_target_pairs={{0,1},{1,0},{2,3},{3,2},{4,5},{5,4},{6,7},{7,6},{8,9},{9,8},{10,11... | collective-permute-start | bytes 196616 | tf_op jit(solution)/shard_map/ppermute | solution.py:701
  72.3 11.7 %collective-permute-start.9 = (f32[32,512]{1,0:T(8,128)S(1)}, f32[32,512]{1,0:T(8,128)S(1)}, u32[]{:S(2)}, u32[]{:S(2)}) collective-permute-start(f32[32,512]{1,0:T(8,128)S(1)} %get-tuple-element.50), channel_id=1, source_target_pairs={{0,2},{1,3},{2,0},{3,1},{4,6},{5,7},{6,4},{7,5},{8,10},{9,11},{10,... | collective-permute-start | bytes 196616 | tf_op jit(solution)/shard_map/ppermute | solution.py:701
  73.7 13.9 %all-to-all-start.1 = ((f32[16,32,128]{2,1,0:T(8,128)}), f32[16,32,128]{2,1,0:T(8,128)S(1)}, u32[]{:S(2)}, u32[]{:S(2)}) async-start(f32[16,32,128]{2,1,0:T(8,128)} %weight_sum.1.refs_0_), calls=%async_computation.1 | async-start | bytes 524288 | tf_op jit(solution)/shard_map/all_to_all | solution.py:698
  84.8 1.0 copy-start
  87.6 1.5 %collective-permute-start.11 = (f32[512,128]{1,0:T(8,128)S(1)}, f32[512,128]{1,0:T(8,128)S(1)}, u32[]{:S(2)}, u32[]{:S(2)}) collective-permute-start(f32[512,128]{1,0:T(8,128)S(1)} %bitcast.5), channel_id=1, source_target_pairs={{0,1},{1,0},{2,3},{3,2},{4,5},{5,4},{6,7},{7,6},{8,9},{9,8},{10,11... | collective-permute-start | bytes 786440 | tf_op jit(solution)/shard_map/ppermute | solution.py:737
Sparse Core Ops, SparseCore 0:
  37.2 28.9 reduce-scatter.1

commit v13 on v10

--- a/solution.py
+++ b/solution.py
@@ -264,16 +264,18 @@
                 for slot in range(blocks):
                     start = (place * blocks + slot) * depth
                     row = pl.multiple_of(((2 * step + part) * fold + place) * depth, depth)
-                    out_ref = send_ref if slot % 2 else keep_ref
-                    out_ref[slot // 2, pl.ds(row, depth), :] = turned[start : start + depth]
+                    out_ref = send_ref if slot >= blocks // 2 else keep_ref
+                    place_of = slot % (blocks // 2)
+                    out_ref[place_of, pl.ds(row, depth), :] = turned[start : start + depth]
 
     right_phase(left_ref, peer_ref, left_flip, store)
 
 
 def halve_kernel(keep_ref, found_ref, keep_out, send_out):
-    for slot in range(keep_ref.shape[0]):
-        out_ref = send_out if slot % 2 else keep_out
-        out_ref[slot // 2] = keep_ref[slot] + found_ref[slot]
+    half = keep_ref.shape[0] // 2
+    for slot in range(half):
+        keep_out[slot] = keep_ref[slot] + found_ref[slot]
+        send_out[slot] = keep_ref[half + slot] + found_ref[half + slot]
 
 
 def right_rows(right_refs, step, fold, depth):
@@ -483,7 +485,17 @@
     return jax.ShapeDtypeStruct(sizes, kind)
 
 
-def call(kernel, out_shape, scratch=(), name=None, limit=16 * MIB, far=(), after=(), out_specs=None):
+def call(
+    kernel,
+    out_shape,
+    scratch=(),
+    name=None,
+    limit=16 * MIB,
+    far=(),
+    after=(),
+    out_specs=None,
+    flops=1,
+):
     def run(*operands):
         vmem = pl.BlockSpec(memory_space=pltpu.VMEM)
         hbm = pl.BlockSpec(memory_space=pltpu.HBM)
@@ -500,7 +512,7 @@
             in_specs=in_specs,
             scratch_shapes=list(scratch),
             compiler_params=pltpu.CompilerParams(vmem_limit_bytes=limit),
-            cost_estimate=pl.CostEstimate(flops=1, bytes_accessed=1, transcendentals=0),
+            cost_estimate=pl.CostEstimate(flops=flops, bytes_accessed=1, transcendentals=0),
             name=name,
             **extra,
         )(*after, *operands)
@@ -532,6 +544,7 @@
 
     limit = 20 * MIB * max(1, blocks * depth * fold // LANES * 2 // fold)
     large = functools.partial(call, limit=limit)
+    work = 4 * 2 * rows * 2 * blocks * depth * outer * pairs * 3
 
     by_side = cotangent.reshape(rows, blocks, 2, depth, pairs)
     half_cotangent = shape(rows, blocks, depth, pairs)
@@ -576,6 +589,7 @@
         [flip_scratch],
         "right_parts",
     )(weight_cat, cotangent_peer, left_peer, partial)
+    right_send = lax.ppermute(right_send, "blk", slot_moves[blocks // 2])
 
     vmem = pl.BlockSpec(memory_space=pltpu.VMEM)
     hbm = pl.BlockSpec(memory_space=pltpu.HBM)
@@ -590,6 +604,7 @@
         ],
         "weight",
         after=[right_keep],
+        flops=2 * work,
         out_specs=[vmem, vmem, hbm, hbm],
     )(left, left_peer, cotangent_own, cotangent_peer, *rights)
     sent = lax.ppermute(send, "inner", cores)
@@ -604,18 +619,9 @@
         ],
         "left_parts",
         after=[keep],
+        flops=work,
     )(grad_own, grad_peer, *rights)
-    left_other = lax.ppermute(left_other, "blk", partner)
-    keep, left_own, right_send = lax.optimization_barrier((keep, left_own, right_send))
-    right_send = lax.ppermute(right_send, "blk", slot_moves[1])
-    slot = 2
-    while slot < blocks:
-        part = shape(blocks // (2 * slot), channels * depth, sequences)
-        right_keep, right_send = call(halve_kernel, [part, part], name="right_halve")(
-            right_keep, right_send
-        )
-        right_send = lax.ppermute(right_send, "blk", slot_moves[slot])
-        slot = 2 * slot
+    keep, left_own = lax.optimization_barrier((keep, left_own))
     members = count * inner // 2
     pieces = (keep + sent).reshape(members, outer // 2 // members, pairs)
 
@@ -633,25 +639,37 @@
             name,
             far=[0, 1],
             after=after,
+            flops=work,
         )(values, projection_matrix)
+
+    pieces, left_other = lax.optimization_barrier((pieces, left_other))
+    left_other = lax.ppermute(left_other, "blk", partner)
+    slot = blocks // 4
+    while slot:
+        part = shape(slot, channels * depth, sequences)
+        right_keep, right_send = call(
+            halve_kernel, [part, part], name="right_halve", after=[pieces]
+        )(right_keep, right_send)
+        right_send = lax.ppermute(right_send, "blk", slot_moves[slot])
+        slot = slot // 2
 
     pair_other = pair(outer_peer, [pieces], "pair_peer")
     pair_found = lax.ppermute(pair_other, "blk", partner)
 
     pieces = lax.all_to_all(pieces, everyone, 0, 0, axis_index_groups=core_groups)
+    pieces = call(
+        spread_sum_kernel,
+        shape(*pieces.shape),
+        name="weight_sum",
+        after=[pair_other, right_keep],
+    )(pieces)
+    pair_own = pair(outer_own, [pieces], "pair_own")
     left_found = call(
         left_add_kernel,
         [shape(size, rows * channels)] * inner,
         name="left_add",
         after=[pieces],
     )(left_own, left_other)
-    pieces = call(
-        spread_sum_kernel,
-        shape(*pieces.shape),
-        name="weight_sum",
-        after=[pair_other, left_found[0], right_keep],
-    )(pieces)
-    pair_own = pair(outer_own, [pieces], "pair_own")
     pieces = lax.all_to_all(pieces, everyone, 0, 0, axis_index_groups=core_groups)
 
     left_found = [

time: 95.7 us -> 82.1 us (0.86)
  waiting for transfers between devices: 25.3 us -> 9.87 us
  starting transfers between devices: 25.3 us -> 27.1 us
    ppermute x1, waiting for transfers between devices: 9.31 us -> 0.01 us  [local(): right_send = lax.ppermute(right_send, 'blk', slot_moves[slot])]
    ppermute x1, waiting for transfers between devices: 2.62 us -> 0.01 us  [local(): right_send = lax.ppermute(right_send, 'blk', slot_moves[blocks // 2])]
    ppermute x1, starting transfers between devices: 0.47 us -> 2.79 us  [local(): right_send = lax.ppermute(right_send, 'blk', slot_moves[blocks // 2])]
    all_to_all x2, waiting for transfers between devices: 3.26 us -> 1.54 us  [local(): lax.all_to_all(pieces, everyone, 0, 0, axis_index_groups=core_groups)]
    ppermute x3, waiting for transfers between devices: 1.34 us -> 0.01 us  [local(): rights.append(lax.ppermute(right, 'blk', slot_moves[slot]))]
    ppermute x1, starting transfers between devices: 2.83 us -> 1.86 us  [local(): right_send = lax.ppermute(right_send, 'blk', slot_moves[slot])]
  transfers between devices with their start and end apart: 16 -> 16, of which waited for: 7 -> 3; matrix products, arithmetic and copies ran while one was open for 1% -> 1% of each run, Pallas kernels for 32% -> 49%
where the time goes in v13:
time: 82.1 us; the launch traced here: 81.7 us
  Pallas kernels  43.2 us (53%)
  starting transfers between devices  27.1 us (33%)
  waiting for transfers between devices  9.87 us (12%)
    pallas_call x14, Pallas kernels, run(): pl.pallas_call(lambda *refs: kernel(*refs[len(after):]), out_shape=out_sh...  43.2 us
    all_to_all x2, starting transfers between devices, local(): lax.all_to_all(pieces, everyone, 0, 0, axis_index_groups=core_groups)  10.2 us
    ppermute x1, waiting for transfers between devices, local(): left_peer = lax.ppermute(left, 'blk', partner)  6.92 us
    ppermute x3, starting transfers between devices, local(): rights.append(lax.ppermute(right, 'blk', slot_moves[slot]))  4.6 us
    ppermute x1, starting transfers between devices, local(): cotangent_peer = lax.ppermute(cotangent_send, 'blk', partner)  3.03 us
    ppermute x1, starting transfers between devices, local(): right_send = lax.ppermute(right_send, 'blk', slot_moves[blocks // 2])  2.79 us
    ppermute x3, starting transfers between devices, local(): lax.ppermute(part, 'inner', inner_moves[slot])  2.13 us
    ppermute x1, starting transfers between devices, local(): left_other = lax.ppermute(left_other, 'blk', partner)  1.96 us
  transfers between devices with their start and end apart: 16, of which 3 were waited for; matrix products, arithmetic and copies ran while one was open for 1% of the time, Pallas kernels for 49%

profile of v13, /device:TPU:0, one launch (start us, length us, event | category | flops | bytes accessed | tf_op | source)
XLA Modules:
  0.0 81.7 jit_solution(8466598947241750953)
XLA Ops:
  0.6 2.0 %prepare.1 = (f32[512,128]{1,0:T(8,128)S(1)}, f32[512,128]{1,0:T(8,128)S(1)}, f32[16,4,16,128]{3,2,1,0:T(8,128)S(1)}, f32[16,4,16,128]{3,2,1,0:T(8,128)S(1)}, f32[1024,128]{1,0:T(8,128)S(1)}) custom-call(f32[16,4,2,16,128]{4,3,2,1,0:T(8,128)} %bitcast.6, f32[16,4096]{1,0:T(8,128)} %refs_1_.1, f32[16,4096]{1,0:T(8,128)} %refs_2_.3, f32[1024,128]{1,0:T(8,128)} %refs_2_.5), custom_call_target="tpu_custom_call" | custom-call | flops 1 | bytes 1 | tf_op jit(solution)/shard_map/prepare/pallas_call | solution.py:509
  2.6 3.0 %collective-permute-start = (f32[16,4,16,128]{3,2,1,0:T(8,128)S(1)}, f32[16,4,16,128]{3,2,1,0:T(8,128)S(1)}, u32[]{:S(2)}, u32[]{:S(2)}) collective-permute-start(f32[16,4,16,128]{3,2,1,0:T(8,128)S(1)} %get-tuple-element.39), channel_id=1, source_target_pairs={{0,4},{4,0},{8,12},{12,8},{16,20},{20,16},{24,28},{28,24},{1,5},{5... | collective-permute-start | bytes 1572872 | tf_op jit(solution)/shard_map/ppermute | solution.py:572
  5.6 0.1 collective-permute-start.1
  5.7 4.0 %collective-permute-start.4 = (f32[512,128]{1,0:T(8,128)S(1)}, f32[512,128]{1,0:T(8,128)S(1)}, u32[]{:S(2)}, u32[]{:S(2)}) collective-permute-start(f32[512,128]{1,0:T(8,128)S(1)} %get-tuple-element.42.refs_5_.refs_3_), channel_id=1, source_target_pairs={{0,24},{4,28},{8,16},{12,20},{16,8},{20,12},{24,0},{28,4},{1,25},{... | collective-permute-start | bytes 786440 | tf_op jit(solution)/shard_map/ppermute | solution.py:571
  9.7 0.0 collective-permute-start.3
  9.8 0.6 collective-permute-start.2
  10.3 5.9 %gradient_own.1 = (bf16[8,512,512]{2,1,0:T(8,128)(2,1)S(1)}, f32[8,128,256]{2,1,0:T(8,128)S(1)}, bf16[512,768]{1,0:T(8,128)(2,1)S(1)}) custom-call(f32[1024,128]{1,0:T(8,128)S(1)} %get-tuple-element.35.refs_0_, f32[16,4,16,128]{3,2,1,0:T(8,128)S(1)} %get-tuple-element.36.refs_1_.refs_3_, f32[512,128]{1,0:T(8,128)S(1)} %get-tuple-element.37.refs_2_.refs_1_), custom_call_target="tpu_custom_call" | custom-call | flops 1 | bytes 1 | tf_op jit(solution)/shard_map/gradient_own/pallas_call | solution.py:509
  16.3 6.9 %collective-permute-done.1.refs_2_ = f32[512,128]{1,0:T(8,128)S(1)} collective-permute-done((f32[512,128]{1,0:T(8,128)S(1)}, f32[512,128]{1,0:T(8,128)S(1)}, u32[]{:S(2)}, u32[]{:S(2)}) %collective-permute-start.1) | collective-permute-done | bytes 262176 | tf_op jit(solution)/shard_map/ppermute | solution.py:573
  23.2 0.0 collective-permute-done.refs_1_.refs_4_
  23.2 7.0 %right_parts.1 = (bf16[8,512,512]{2,1,0:T(8,128)(2,1)S(1)}, f32[2,512,128]{2,1,0:T(8,128)S(1)}, f32[2,512,128]{2,1,0:T(8,128)}) custom-call(bf16[512,768]{1,0:T(8,128)(2,1)S(1)} %get-tuple-element.38.refs_0_, f32[16,4,16,128]{3,2,1,0:T(8,128)S(1)} %collective-permute-done.refs_1_.refs_4_, f32[512,128]{1,0:T(8,128)S(1)} %collective-permute-done.1.refs_2_, ...), custom_call_target="tpu_custom_call" | custom-call | flops 1 | bytes 1 | tf_op jit(solution)/shard_map/right_parts/pallas_call | solution.py:509
  30.2 2.8 %collective-permute-start.6 = (f32[2,512,128]{2,1,0:T(8,128)}, f32[2,512,128]{2,1,0:T(8,128)S(1)}, u32[]{:S(2)}, u32[]{:S(2)}) collective-permute-start(f32[2,512,128]{2,1,0:T(8,128)} %get-tuple-element.52), channel_id=1, source_target_pairs={{0,16},{4,20},{8,24},{12,28},{16,0},{20,4},{24,8},{28,12},{1,17},{... | collective-permute-start | bytes 1572872 | tf_op jit(solution)/shard_map/ppermute | solution.py:592
  33.0 0.0 collective-permute-done.4.refs_8_.refs_6_
  33.0 0.0 collective-permute-done.3.refs_7_.refs_5_
  33.0 0.0 collective-permute-done.2.refs_6_.refs_4_
  33.0 9.3 %weight.1 = (f32[512,128]{1,0:T(8,128)S(1)}, f32[512,128]{1,0:T(8,128)S(1)}, bf16[8,512,512]{2,1,0:T(8,128)(2,1)}, bf16[8,512,512]{2,1,0:T(8,128)(2,1)}) custom-call(f32[2,512,128]{2,1,0:T(8,128)S(1)} %get-tuple-element.41.refs_0_.refs_1_, f32[512,128]{1,0:T(8,128)S(1)} %get-tuple-element.37.refs_2_.refs_1_, f32[512,128]{1,0:T(8,128)S(1)} %collective-permute-done.1.refs_2_, ...), custom_call_target="tpu_custom_call" | custom-call | flops 12884901888 | bytes 1 | tf_op jit(solution)/shard_map/weight/pallas_call | solution.py:509
  42.3 0.1 collective-permute-start.5
  42.4 3.1 %left_parts.1 = (f32[4,32,512]{2,1,0:T(8,128)S(1)}, f32[4,32,512]{2,1,0:T(8,128)S(1)}) custom-call(f32[512,128]{1,0:T(8,128)S(1)} %get-tuple-element.47.refs_0_, bf16[8,512,512]{2,1,0:T(8,128)(2,1)S(1)} %get-tuple-element.44.refs_1_, bf16[8,512,512]{2,1,0:T(8,128)(2,1)S(1)} %get-tuple-element.45.refs_2_, f32[512,128]{1,0:T(8,128)S(1)} %get-tuple-element.42.refs_5_.refs_3_, ...), custom_call_target="tpu_custom_call" | custom-call | flops 6442450944 | bytes 1 | tf_op jit(solution)/shard_map/left_parts/pallas_call | solution.py:509
  45.5 0.0 collective-permute-done.5
  45.5 0.7 add.3
  46.2 4.9 %all-to-all-start = ((f32[16,32,128]{2,1,0:T(8,128)}), f32[16,32,128]{2,1,0:T(8,128)S(1)}, u32[]{:S(2)}, u32[]{:S(2)}) async-start(f32[16,32,128]{2,1,0:T(8,128)} %bitcast.1.refs_0_), calls=%async_computation | async-start | bytes 524288 | tf_op jit(solution)/shard_map/all_to_all | solution.py:659
  51.1 2.0 %collective-permute-start.8 = (f32[4,32,512]{2,1,0:T(8,128)S(1)}, f32[4,32,512]{2,1,0:T(8,128)S(1)}, u32[]{:S(2)}, u32[]{:S(2)}) collective-permute-start(f32[4,32,512]{2,1,0:T(8,128)S(1)} %get-tuple-element.56), channel_id=1, source_target_pairs={{0,4},{4,0},{8,12},{12,8},{16,20},{20,16},{24,28},{28,24},{1,5},{5... | collective-permute-start | bytes 786440 | tf_op jit(solution)/shard_map/ppermute | solution.py:646
  53.1 5.2 %pair_peer.1.refs_0_ = f32[16,4,16,128]{3,2,1,0:T(8,128)S(1)} custom-call(f32[16,32,128]{2,1,0:T(8,128)} %bitcast.1.refs_0_, bf16[8,512,512]{2,1,0:T(8,128)(2,1)} %get-tuple-element.51.refs_1_, f32[1024,128]{1,0:T(8,128)} %refs_2_.5), custom_call_target="tpu_custom_call" | custom-call | flops 6442450944 | bytes 1 | tf_op jit(solution)/shard_map/pair_peer/pallas_call | solution.py:509
  58.2 0.2 collective-permute-start.7
  58.5 0.0 collective-permute-done.6.refs_2_
  58.5 0.8 right_halve.1
  59.2 1.9 %collective-permute-start.12 = (f32[1,512,128]{2,1,0:T(8,128)}, f32[1,512,128]{2,1,0:T(8,128)S(1)}, u32[]{:S(2)}, u32[]{:S(2)}) collective-permute-start(f32[1,512,128]{2,1,0:T(8,128)} %get-tuple-element.61), channel_id=1, source_target_pairs={{0,8},{4,12},{8,0},{12,4},{16,24},{20,28},{24,16},{28,20},{1,9},{5... | collective-permute-start | bytes 786440 | tf_op jit(solution)/shard_map/ppermute | solution.py:653
  61.1 1.5 %all-to-all-done.refs_2_ = f32[16,32,128]{2,1,0:T(8,128)S(1)} async-done(((f32[16,32,128]{2,1,0:T(8,128)}), f32[16,32,128]{2,1,0:T(8,128)S(1)}, u32[]{:S(2)}, u32[]{:S(2)}) %all-to-all-start) | async-done | bytes 262176 | tf_op jit(solution)/shard_map/all_to_all | solution.py:659
  62.6 0.8 weight_sum.1.refs_0_
  63.4 5.3 %all-to-all-start.1 = ((f32[16,32,128]{2,1,0:T(8,128)}), f32[16,32,128]{2,1,0:T(8,128)S(1)}, u32[]{:S(2)}, u32[]{:S(2)}) async-start(f32[16,32,128]{2,1,0:T(8,128)} %weight_sum.1.refs_0_), calls=%async_computation.1 | async-start | bytes 524288 | tf_op jit(solution)/shard_map/all_to_all | solution.py:673
  68.7 0.0 collective-permute-done.8.refs_2_
  68.8 0.1 collective-permute-start.9
  68.8 2.0 %collective-permute-start.10 = (f32[32,512]{1,0:T(8,128)S(1)}, f32[32,512]{1,0:T(8,128)S(1)}, u32[]{:S(2)}, u32[]{:S(2)}) collective-permute-start(f32[32,512]{1,0:T(8,128)S(1)} %get-tuple-element.59), channel_id=1, source_target_pairs={{0,2},{1,3},{2,0},{3,1},{4,6},{5,7},{6,4},{7,5},{8,10},{9,11},{10,... | collective-permute-start | bytes 196616 | tf_op jit(solution)/shard_map/ppermute | solution.py:676
  70.8 0.1 collective-permute-start.11
  70.9 5.2 %pair_own.1.refs_0_ = f32[16,4,16,128]{3,2,1,0:T(8,128)S(1)} custom-call(f32[16,32,128]{2,1,0:T(8,128)} %weight_sum.1.refs_0_, bf16[8,512,512]{2,1,0:T(8,128)(2,1)} %get-tuple-element.54.refs_1_, f32[1024,128]{1,0:T(8,128)} %refs_2_.5), custom_call_target="tpu_custom_call" | custom-call | flops 6442450944 | bytes 1 | tf_op jit(solution)/shard_map/pair_own/pallas_call | solution.py:509
  76.1 0.0 collective-permute-done.12.refs_1_
  76.1 1.2 %turn_right.1 = f32[16,4096]{1,0:T(8,128)} custom-call(f32[1,512,128]{2,1,0:T(8,128)S(1)} %get-tuple-element.53.refs_1_.refs_0_, f32[1,512,128]{2,1,0:T(8,128)S(1)} %collective-permute-done.12.refs_1_), custom_call_target="tpu_custom_call" | custom-call | flops 1 | bytes 1 | tf_op jit(solution)/shard_map/turn_right/pallas_call | solution.py:509
  77.3 0.0 collective-permute-done.7.refs_1_
  77.3 1.0 %merge.1 = f32[16,4,2,16,128]{4,3,2,1,0:T(8,128)} custom-call(f32[16,4,16,128]{3,2,1,0:T(8,128)S(1)} %pair_own.1.refs_0_, f32[16,4,16,128]{3,2,1,0:T(8,128)S(1)} %collective-permute-done.7.refs_1_), custom_call_target="tpu_custom_call" | custom-call | flops 1 | bytes 1 | tf_op jit(solution)/shard_map/merge/pallas_call | solution.py:509
  78.2 0.0 collective-permute-done.9.refs_1_
  78.3 0.0 collective-permute-done.10.refs_2_
  78.3 0.0 collective-permute-done.11.refs_3_
  78.3 0.8 turn_left.1
  79.1 0.0 all-to-all-done.1
  79.1 0.2 collective-permute-start.13
  79.2 1.4 %collective-permute-done.13.refs_1_ = f32[512,128]{1,0:T(8,128)S(1)} collective-permute-done((f32[512,128]{1,0:T(8,128)S(1)}, f32[512,128]{1,0:T(8,128)S(1)}, u32[]{:S(2)}, u32[]{:S(2)}) %collective-permute-start.13) | collective-permute-done | bytes 262176 | tf_op jit(solution)/shard_map/ppermute | solution.py:713
  80.6 1.1 %place.1 = f32[1024,128]{1,0:T(8,128)} custom-call(f32[512,128]{1,0:T(8,128)S(1)} %bitcast.5, f32[512,128]{1,0:T(8,128)S(1)} %collective-permute-done.13.refs_1_), custom_call_target="tpu_custom_call" | custom-call | flops 1 | bytes 1 | tf_op jit(solution)/shard_map/place/pallas_call | solution.py:509
  (1 shorter events, 0.0 us)
Async XLA Ops:
  2.6 20.6 %collective-permute-start = (f32[16,4,16,128]{3,2,1,0:T(8,128)S(1)}, f32[16,4,16,128]{3,2,1,0:T(8,128)S(1)}, u32[]{:S(2)}, u32[]{:S(2)}) collective-permute-start(f32[16,4,16,128]{3,2,1,0:T(8,128)S(1)} %get-tuple-element.39), channel_id=1, source_target_pairs={{0,4},{4,0},{8,12},{12,8},{16,20},{20,16},{24,28},{28,24},{1,5},{5... | collective-permute-start | bytes 1572872 | tf_op jit(solution)/shard_map/ppermute | solution.py:572
  5.6 17.5 %collective-permute-start.1 = (f32[512,128]{1,0:T(8,128)S(1)}, f32[512,128]{1,0:T(8,128)S(1)}, u32[]{:S(2)}, u32[]{:S(2)}) collective-permute-start(f32[512,128]{1,0:T(8,128)S(1)} %get-tuple-element.37.refs_2_.refs_1_), channel_id=1, source_target_pairs={{0,4},{4,0},{8,12},{12,8},{16,20},{20,16},{24,28},{28,24},{1,5},{5... | collective-permute-start | bytes 786440 | tf_op jit(solution)/shard_map/ppermute | solution.py:573
  5.7 27.2 %collective-permute-start.4 = (f32[512,128]{1,0:T(8,128)S(1)}, f32[512,128]{1,0:T(8,128)S(1)}, u32[]{:S(2)}, u32[]{:S(2)}) collective-permute-start(f32[512,128]{1,0:T(8,128)S(1)} %get-tuple-element.42.refs_5_.refs_3_), channel_id=1, source_target_pairs={{0,24},{4,28},{8,16},{12,20},{16,8},{20,12},{24,0},{28,4},{1,25},{... | collective-permute-start | bytes 786440 | tf_op jit(solution)/shard_map/ppermute | solution.py:571
  9.7 23.2 %collective-permute-start.3 = (f32[512,128]{1,0:T(8,128)S(1)}, f32[512,128]{1,0:T(8,128)S(1)}, u32[]{:S(2)}, u32[]{:S(2)}) collective-permute-start(f32[512,128]{1,0:T(8,128)S(1)} %get-tuple-element.42.refs_5_.refs_3_), channel_id=1, source_target_pairs={{0,16},{4,20},{8,24},{12,28},{16,0},{20,4},{24,8},{28,12},{1,17},{... | collective-permute-start | bytes 786440 | tf_op jit(solution)/shard_map/ppermute | solution.py:571
  9.8 23.2 %collective-permute-start.2 = (f32[512,128]{1,0:T(8,128)S(1)}, f32[512,128]{1,0:T(8,128)S(1)}, u32[]{:S(2)}, u32[]{:S(2)}) collective-permute-start(f32[512,128]{1,0:T(8,128)S(1)} %get-tuple-element.42.refs_5_.refs_3_), channel_id=1, source_target_pairs={{0,8},{4,12},{8,0},{12,4},{16,24},{20,28},{24,16},{28,20},{1,9},{5... | collective-permute-start | bytes 786440 | tf_op jit(solution)/shard_map/ppermute | solution.py:571
  30.2 28.3 %collective-permute-start.6 = (f32[2,512,128]{2,1,0:T(8,128)}, f32[2,512,128]{2,1,0:T(8,128)S(1)}, u32[]{:S(2)}, u32[]{:S(2)}) collective-permute-start(f32[2,512,128]{2,1,0:T(8,128)} %get-tuple-element.52), channel_id=1, source_target_pairs={{0,16},{4,20},{8,24},{12,28},{16,0},{20,4},{24,8},{28,12},{1,17},{... | collective-permute-start | bytes 1572872 | tf_op jit(solution)/shard_map/ppermute | solution.py:592
  42.3 3.2 %collective-permute-start.5 = (f32[512,128]{1,0:T(8,128)S(1)}, f32[512,128]{1,0:T(8,128)S(1)}, u32[]{:S(2)}, u32[]{:S(2)}) collective-permute-start(f32[512,128]{1,0:T(8,128)S(1)} %get-tuple-element.48), channel_id=1, source_target_pairs={{0,1},{1,0},{2,3},{3,2},{4,5},{5,4},{6,7},{7,6},{8,9},{9,8},{10,11... | collective-permute-start | bytes 786440 | tf_op jit(solution)/shard_map/ppermute | solution.py:610
  46.2 16.4 %all-to-all-start = ((f32[16,32,128]{2,1,0:T(8,128)}), f32[16,32,128]{2,1,0:T(8,128)S(1)}, u32[]{:S(2)}, u32[]{:S(2)}) async-start(f32[16,32,128]{2,1,0:T(8,128)} %bitcast.1.refs_0_), calls=%async_computation | async-start | bytes 524288 | tf_op jit(solution)/shard_map/all_to_all | solution.py:659
  51.1 17.6 %collective-permute-start.8 = (f32[4,32,512]{2,1,0:T(8,128)S(1)}, f32[4,32,512]{2,1,0:T(8,128)S(1)}, u32[]{:S(2)}, u32[]{:S(2)}) collective-permute-start(f32[4,32,512]{2,1,0:T(8,128)S(1)} %get-tuple-element.56), channel_id=1, source_target_pairs={{0,4},{4,0},{8,12},{12,8},{16,20},{20,16},{24,28},{28,24},{1,5},{5... | collective-permute-start | bytes 786440 | tf_op jit(solution)/shard_map/ppermute | solution.py:646
  58.2 19.0 %collective-permute-start.7 = (f32[16,4,16,128]{3,2,1,0:T(8,128)S(1)}, f32[16,4,16,128]{3,2,1,0:T(8,128)S(1)}, u32[]{:S(2)}, u32[]{:S(2)}) collective-permute-start(f32[16,4,16,128]{3,2,1,0:T(8,128)S(1)} %pair_peer.1.refs_0_), channel_id=1, source_target_pairs={{0,4},{4,0},{8,12},{12,8},{16,20},{20,16},{24,28},{28,24},{1,5},{5... | collective-permute-start | bytes 1572872 | tf_op jit(solution)/shard_map/ppermute | solution.py:657
  59.2 16.9 %collective-permute-start.12 = (f32[1,512,128]{2,1,0:T(8,128)}, f32[1,512,128]{2,1,0:T(8,128)S(1)}, u32[]{:S(2)}, u32[]{:S(2)}) collective-permute-start(f32[1,512,128]{2,1,0:T(8,128)} %get-tuple-element.61), channel_id=1, source_target_pairs={{0,8},{4,12},{8,0},{12,4},{16,24},{20,28},{24,16},{28,20},{1,9},{5... | collective-permute-start | bytes 786440 | tf_op jit(solution)/shard_map/ppermute | solution.py:653
  63.4 15.7 %all-to-all-start.1 = ((f32[16,32,128]{2,1,0:T(8,128)}), f32[16,32,128]{2,1,0:T(8,128)S(1)}, u32[]{:S(2)}, u32[]{:S(2)}) async-start(f32[16,32,128]{2,1,0:T(8,128)} %weight_sum.1.refs_0_), calls=%async_computation.1 | async-start | bytes 524288 | tf_op jit(solution)/shard_map/all_to_all | solution.py:673
  68.8 9.5 %collective-permute-start.9 = (f32[32,512]{1,0:T(8,128)S(1)}, f32[32,512]{1,0:T(8,128)S(1)}, u32[]{:S(2)}, u32[]{:S(2)}) collective-permute-start(f32[32,512]{1,0:T(8,128)S(1)} %get-tuple-element.58), channel_id=1, source_target_pairs={{0,1},{1,0},{2,3},{3,2},{4,5},{5,4},{6,7},{7,6},{8,9},{9,8},{10,11... | collective-permute-start | bytes 196616 | tf_op jit(solution)/shard_map/ppermute | solution.py:676
  68.8 9.4 %collective-permute-start.10 = (f32[32,512]{1,0:T(8,128)S(1)}, f32[32,512]{1,0:T(8,128)S(1)}, u32[]{:S(2)}, u32[]{:S(2)}) collective-permute-start(f32[32,512]{1,0:T(8,128)S(1)} %get-tuple-element.59), channel_id=1, source_target_pairs={{0,2},{1,3},{2,0},{3,1},{4,6},{5,7},{6,4},{7,5},{8,10},{9,11},{10,... | collective-permute-start | bytes 196616 | tf_op jit(solution)/shard_map/ppermute | solution.py:676
  70.8 7.4 %collective-permute-start.11 = (f32[32,512]{1,0:T(8,128)S(1)}, f32[32,512]{1,0:T(8,128)S(1)}, u32[]{:S(2)}, u32[]{:S(2)}) collective-permute-start(f32[32,512]{1,0:T(8,128)S(1)} %get-tuple-element.60), channel_id=1, source_target_pairs={{0,3},{1,2},{2,1},{3,0},{4,7},{5,6},{6,5},{7,4},{8,11},{9,10},{10,... | collective-permute-start | bytes 196616 | tf_op jit(solution)/shard_map/ppermute | solution.py:676
  79.1 1.5 %collective-permute-start.13 = (f32[512,128]{1,0:T(8,128)S(1)}, f32[512,128]{1,0:T(8,128)S(1)}, u32[]{:S(2)}, u32[]{:S(2)}) collective-permute-start(f32[512,128]{1,0:T(8,128)S(1)} %bitcast.4), channel_id=1, source_target_pairs={{0,1},{1,0},{2,3},{3,2},{4,5},{5,4},{6,7},{7,6},{8,9},{9,8},{10,11... | collective-permute-start | bytes 786440 | tf_op jit(solution)/shard_map/ppermute | solution.py:713

commit v14 on v13

--- a/solution.py
+++ b/solution.py
@@ -125,16 +125,15 @@
         copy.wait()
 
 
-def turn_right_kernel(parts, *refs):
-    part_refs, (out_ref, total, square, tiles) = refs[:parts], refs[parts:]
+def turn_right(part_refs, out_ref, total, square, tiles):
     channels = ENTRY_CHANNELS
     rows, features = out_ref.shape
     count = features // LANES
     total[...] = functools.reduce(jnp.add, [ref[0] for ref in part_refs])
     for group in range(rows // PACK):
         stacked = [total[strided(group * PACK + k, channels, rows), :] for k in range(PACK)]
-        square[...] = jnp.concatenate(stacked, 0).T
-        pieces = [square[strided(part, count, PACK), :] for part in range(PACK)]
+        square[group] = jnp.concatenate(stacked, 0).T
+        pieces = [square[group, strided(part, count, PACK), :] for part in range(PACK)]
         for k in range(PACK):
             lanes = slice(k * channels, (k + 1) * channels)
             tiles[strided(group * PACK + k, count, rows), :] = jnp.concatenate(
@@ -144,8 +143,7 @@
         out_ref[:, tile * LANES : (tile + 1) * LANES] = tiles[tile * rows : (tile + 1) * rows, :]
 
 
-def turn_left_kernel(parts, *refs):
-    part_refs, (out_ref, total, tiles) = refs[:parts], refs[parts:]
+def turn_left(part_refs, out_ref, total, tiles):
     channels = ENTRY_CHANNELS
     size, width = part_refs[0].shape
     rows, features = out_ref.shape
@@ -183,19 +181,47 @@
         out_ref[pair] = jnp.concatenate(halves(found), 1)
         return carry
 
-    lax.fori_loop(0, out_ref.shape[0], step_of, 0)
+    lax.fori_loop(0, out_ref.shape[0], step_of, 0, unroll=2)
 
 
 def gradient_kernel(
-    blocks, weight_ref, cotangent_ref, left_ref, out_ref, partial_ref, weight_cat, left_flip
+    blocks,
+    weight_ref,
+    cotangent_ref,
+    left_ref,
+    out_ref,
+    partial_ref,
+    weight_cat,
+    flip_hbm,
+    left_flip,
+    weight_rows,
+    weight_flip,
+    semaphore,
 ):
-    prepare_weight(weight_ref, weight_cat, fold_of(blocks * cotangent_ref.shape[2]))
+    fold = fold_of(blocks * cotangent_ref.shape[2])
+    prepare_weight(weight_ref, weight_cat, fold)
     gradient_phase(blocks, cotangent_ref, out_ref, weight_cat)
 
     def store(step, found):
         partial_ref[step] = found
 
     right_phase(left_ref, out_ref, left_flip, store)
+    channels = ENTRY_CHANNELS
+    wide = weight_rows.shape[1]
+    for step in range(channels // fold):
+        weight_rows[step * channels : (step + 1) * channels, :] = folded_weight(
+            weight_ref, step, fold
+        )
+    flip_high, flip_low = halves(weight_rows[...].T)
+    weight_flip[:wide, :] = flip_high
+    weight_flip[wide:, :] = flip_low
+    copy = pltpu.make_async_copy(weight_flip, flip_hbm, semaphore)
+    copy.start()
+    copy.wait()
+
+
+def peer_kernel(blocks, weight_cat, cotangent_ref, out_ref):
+    gradient_phase(blocks, cotangent_ref, out_ref, weight_cat)
 
 
 def right_phase(left_ref, factor_ref, left_flip, store):
@@ -217,7 +243,7 @@
         store(step, first[:sequences] + first[sequences:] + second)
         return carry
 
-    lax.fori_loop(0, factor_ref.shape[1] // (2 * ENTRY_CHANNELS), step_of, 0)
+    lax.fori_loop(0, factor_ref.shape[1] // (2 * ENTRY_CHANNELS), step_of, 0, unroll=2)
 
 
 def rows_of_step(refs, step, half, lanes):
@@ -241,20 +267,10 @@
 
 
 def right_kernel(
-    blocks,
-    weight_cat,
-    cotangent_ref,
-    left_ref,
-    partial_ref,
-    peer_ref,
-    keep_ref,
-    send_ref,
-    left_flip,
+    blocks, depth, peer_ref, left_ref, partial_ref, keep_ref, send_ref, left_flip
 ):
-    depth = cotangent_ref.shape[2]
     fold = fold_of(blocks * depth)
     lanes = fold * blocks * depth
-    gradient_phase(blocks, cotangent_ref, peer_ref, weight_cat)
 
     def store(step, found):
         found = found + partial_ref[step]
@@ -327,7 +343,7 @@
             copy.start()
         return carry
 
-    lax.fori_loop(0, channels // (2 * fold), outer_step, 0)
+    lax.fori_loop(0, channels // (2 * fold), outer_step, 0, unroll=2)
     total[...] = jnp.zeros_like(total)
 
     def weight_step(pair, carry):
@@ -339,7 +355,7 @@
         total[...] += dot(jnp.concatenate(lefts, 1), jnp.concatenate(rights, 0))
         return carry
 
-    lax.fori_loop(0, own_ref.shape[0], weight_step, 0)
+    lax.fori_loop(0, own_ref.shape[0], weight_step, 0, unroll=2)
     core = lax.rem(lax.axis_index("inner"), 2)
     steps = channels // (2 * fold)
     for out_ref, half in ((keep_ref, core), (send_ref, 1 - core)):
@@ -380,7 +396,7 @@
         total[...] += both[:, :sequences] + both[:, sequences:] + dot(grads[1], high)
         return carry
 
-    lax.fori_loop(0, ENTRY_CHANNELS // (fold * group), step_of, 0)
+    lax.fori_loop(0, ENTRY_CHANNELS // (fold * group), step_of, 0, unroll=2)
     flipped[...] = total[...].T * (1.0 / sequences)
     inner, size, width = own_out.shape
     here = lax.axis_index("inner")
@@ -395,18 +411,7 @@
         ref[...] = own_ref[slot] + other_ref[slot]
 
 
-def pair_kernel(
-    blocks,
-    outer_hbm,
-    weight_hbm,
-    out_ref,
-    outer_ref,
-    weight_ref,
-    weight_flip,
-    weight_rows,
-    semaphores,
-):
-    channels = ENTRY_CHANNELS
+def pair_kernel(blocks, outer_hbm, flip_hbm, out_ref, outer_ref, weight_flip, semaphores):
     depth, pairs = out_ref.shape[2:]
     count = outer_ref.shape[0]
     lanes = outer_ref.shape[2] // 4
@@ -417,18 +422,11 @@
     def copy_of(pair):
         return pltpu.make_async_copy(outer_hbm.at[pair], outer_ref.at[pair], semaphores.at[pair])
 
-    weight_copy = pltpu.make_async_copy(weight_hbm, weight_ref, semaphores.at[count])
-    weight_copy.start()
+    flip_copy = pltpu.make_async_copy(flip_hbm, weight_flip, semaphores.at[count])
+    flip_copy.start()
     for pair in range(count):
         copy_of(pair).start()
-    weight_copy.wait()
-    for step in range(channels // fold):
-        weight_rows[step * channels : (step + 1) * channels, :] = folded_weight(
-            weight_ref, step, fold
-        )
-    flip_high, flip_low = halves(weight_rows[...].T)
-    weight_flip[:wide, :] = flip_high
-    weight_flip[wide:, :] = flip_low
+    flip_copy.wait()
     slots = slots_of(blocks)
 
     def step_of(pair, carry):
@@ -448,17 +446,22 @@
                 out_ref[row, slots[slot]] = turned[slot * depth : (slot + 1) * depth]
         return carry
 
-    lax.fori_loop(0, count, step_of, 0)
-
-
-def merge_kernel(own_ref, other_ref, out_ref, semaphores):
+    lax.fori_loop(0, count, step_of, 0, unroll=2)
+
+
+def finish_kernel(own_ref, other_ref, keep_ref, found_ref, *refs):
+    left_refs, refs = refs[:-9], refs[-9:]
+    pair_hbm, left_out, right_out = refs[:3]
+    right_total, right_square, right_tiles, left_total, left_tiles, semaphores = refs[3:]
     parity = lax.rem(lax.axis_index("blk"), 2)
     copies = [
-        pltpu.make_async_copy(ref, out_ref.at[:, :, side], semaphores.at[at])
+        pltpu.make_async_copy(ref, pair_hbm.at[:, :, side], semaphores.at[at])
         for at, (ref, side) in enumerate(((own_ref, parity), (other_ref, 1 - parity)))
     ]
     for copy in copies:
         copy.start()
+    turn_right([keep_ref, found_ref], right_out, right_total, right_square, right_tiles)
+    turn_left(left_refs, left_out, left_total, left_tiles)
     for copy in copies:
         copy.wait()
 
@@ -572,27 +575,42 @@
     cotangent_peer = lax.ppermute(cotangent_send, "blk", partner)
     left_peer = lax.ppermute(left, "blk", partner)
 
+    vmem = pl.BlockSpec(memory_space=pltpu.VMEM)
+    hbm = pl.BlockSpec(memory_space=pltpu.HBM)
     factor = shape(row_pairs, tall, 4 * lanes, kind=BF16)
     factor_scratch = pltpu.VMEM(factor.shape, BF16)
     weight_cat = shape(tall, 3 * fold * pairs, kind=BF16)
     flip_scratch = pltpu.VMEM((2 * sequences, rows * channels), BF16)
-    grad_own, partial, weight_cat = large(
+    flip_sizes = (2 * fold * pairs, tall)
+    grad_own, partial, weight_cat, weight_flip = large(
         functools.partial(gradient_kernel, blocks),
-        [factor, shape(steps // 2, sequences, 2 * lanes), weight_cat],
-        [flip_scratch],
+        [
+            factor,
+            shape(steps // 2, sequences, 2 * lanes),
+            weight_cat,
+            pltpu.HBM(flip_sizes, BF16),
+        ],
+        [
+            flip_scratch,
+            pltpu.VMEM((tall, fold * pairs), F32),
+            pltpu.VMEM(flip_sizes, BF16),
+            pltpu.SemaphoreType.DMA,
+        ],
         "gradient_own",
+        out_specs=[vmem, vmem, vmem, hbm],
     )(weight, cotangent_own, left)
+    grad_peer = large(functools.partial(peer_kernel, blocks), factor, [], "gradient_peer")(
+        weight_cat, cotangent_peer
+    )
     right_half = shape(blocks // 2, channels * depth, sequences)
-    grad_peer, right_keep, right_send = large(
-        functools.partial(right_kernel, blocks),
-        [factor, right_half, right_half],
+    right_keep, right_send = large(
+        functools.partial(right_kernel, blocks, depth),
+        [right_half, right_half],
         [flip_scratch],
         "right_parts",
-    )(weight_cat, cotangent_peer, left_peer, partial)
+    )(grad_peer, left_peer, partial)
     right_send = lax.ppermute(right_send, "blk", slot_moves[blocks // 2])
 
-    vmem = pl.BlockSpec(memory_space=pltpu.VMEM)
-    hbm = pl.BlockSpec(memory_space=pltpu.HBM)
     keep, send, outer_own, outer_peer = large(
         functools.partial(weight_kernel, blocks),
         [shape(outer // 2, pairs)] * 2 + [pltpu.HBM(factor.shape, BF16)] * 2,
@@ -631,16 +649,14 @@
             shape(rows, blocks, depth, pairs),
             [
                 factor_scratch,
-                pltpu.VMEM((outer, pairs), F32),
-                pltpu.VMEM((2 * fold * pairs, tall), BF16),
-                pltpu.VMEM((tall, fold * pairs), F32),
+                pltpu.VMEM(flip_sizes, BF16),
                 pltpu.SemaphoreType.DMA((row_pairs + 1,)),
             ],
             name,
             far=[0, 1],
             after=after,
             flops=work,
-        )(values, projection_matrix)
+        )(values, weight_flip)
 
     pieces, left_other = lax.optimization_barrier((pieces, left_other))
     left_other = lax.ppermute(left_other, "blk", partner)
@@ -676,34 +692,24 @@
         lax.ppermute(part, "inner", inner_moves[slot]) if slot else part
         for slot, part in enumerate(left_found)
     ]
-    grad_left = call(
-        functools.partial(turn_left_kernel, inner),
-        shape(rows, features // inner),
-        [
+    pair_update, grad_left, grad_right = call(
+        finish_kernel,
+        [
+            pltpu.HBM(by_side.shape, F32),
+            shape(rows, features // inner),
+            shape(depth, features),
+        ],
+        [
+            pltpu.VMEM((channels * depth, sequences), F32),
+            pltpu.VMEM((depth // PACK, LANES, LANES), F32),
+            pltpu.VMEM((depth * features // LANES, LANES), F32),
             pltpu.VMEM((size * rows * channels // LANES, LANES), F32),
             pltpu.VMEM((rows * features // inner // LANES, LANES), F32),
-        ],
-        name="turn_left",
-    )(*left_found)
-
-    grad_right = call(
-        functools.partial(turn_right_kernel, 2),
-        shape(depth, features),
-        [
-            pltpu.VMEM((channels * depth, sequences), F32),
-            pltpu.VMEM((LANES, LANES), F32),
-            pltpu.VMEM((depth * features // LANES, LANES), F32),
-        ],
-        name="turn_right",
-    )(right_keep, right_send)
-
-    pair_update = call(
-        merge_kernel,
-        pltpu.HBM(by_side.shape, F32),
-        [pltpu.SemaphoreType.DMA((2,))],
-        "merge",
-        out_specs=hbm,
-    )(pair_own, pair_found)
+            pltpu.SemaphoreType.DMA((2,)),
+        ],
+        "finish",
+        out_specs=[hbm, vmem, vmem],
+    )(pair_own, pair_found, right_keep, right_send, *left_found)
     pair_update = pair_update.reshape(cotangent.shape)
 
     pieces, pair_update, grad_left, grad_right = lax.optimization_barrier(

time: 82.1 us -> 93.1 us (1.13)
  waiting for transfers between devices: 9.87 us -> 21.2 us
  Pallas kernels: 43.2 us -> 41.4 us
  starting transfers between devices: 27.1 us -> 28.6 us
    ppermute x3, waiting for transfers between devices: 0.01 us -> 14.9 us  [local(): rights.append(lax.ppermute(right, 'blk', slot_moves[slot]))]
    ppermute x1, waiting for transfers between devices: 6.92 us -> 2.34 us  [local(): left_peer = lax.ppermute(left, 'blk', partner)]
    ppermute x1, waiting for transfers between devices: 0.01 us -> 2.55 us  [local(): cotangent_peer = lax.ppermute(cotangent_send, 'blk', partner)]
    pallas_call x14 -> x13, Pallas kernels: 43.2 us -> 41.4 us  [run(): pl.pallas_call(lambda *refs: kernel(*refs[len(after):]), out_shape=out_sh...]
    all_to_all x2, waiting for transfers between devices: 1.54 us -> 0.01 us  [local(): lax.all_to_all(pieces, everyone, 0, 0, axis_index_groups=core_groups)]
    all_to_all x2, starting transfers between devices: 10.2 us -> 11.7 us  [local(): lax.all_to_all(pieces, everyone, 0, 0, axis_index_groups=core_groups)]
  transfers between devices with their start and end apart: 16 -> 16, of which waited for: 3 -> 4; matrix products, arithmetic and copies ran while one was open for 1% -> 1% of each run, Pallas kernels for 49% -> 41%
where the time goes in v14:
time: 93.1 us; the launch traced here: 92.8 us
  Pallas kernels  41.4 us (44%)
  starting transfers between devices  28.6 us (31%)
  waiting for transfers between devices  21.2 us (23%)
    pallas_call x13, Pallas kernels, run(): pl.pallas_call(lambda *refs: kernel(*refs[len(after):]), out_shape=out_sh...  41.4 us
    ppermute x3, waiting for transfers between devices, local(): rights.append(lax.ppermute(right, 'blk', slot_moves[slot]))  14.9 us
    all_to_all x2, starting transfers between devices, local(): lax.all_to_all(pieces, everyone, 0, 0, axis_index_groups=core_groups)  11.7 us
    ppermute x3, starting transfers between devices, local(): rights.append(lax.ppermute(right, 'blk', slot_moves[slot]))  4.6 us
    ppermute x1, starting transfers between devices, local(): cotangent_peer = lax.ppermute(cotangent_send, 'blk', partner)  3.03 us
    ppermute x1, starting transfers between devices, local(): right_send = lax.ppermute(right_send, 'blk', slot_moves[blocks // 2])  2.81 us
    ppermute x1, waiting for transfers between devices, local(): cotangent_peer = lax.ppermute(cotangent_send, 'blk', partner)  2.55 us
    ppermute x1, waiting for transfers between devices, local(): left_peer = lax.ppermute(left, 'blk', partner)  2.34 us
  transfers between devices with their start and end apart: 16, of which 4 were waited for; matrix products, arithmetic and copies ran while one was open for 1% of the time, Pallas kernels for 41%

profile of v14, /device:TPU:0, one launch (start us, length us, event | category | flops | bytes accessed | tf_op | source)
XLA Modules:
  0.0 92.8 jit_solution(14574262363000402621)
XLA Ops:
  0.6 2.0 %prepare.1 = (f32[512,128]{1,0:T(8,128)S(1)}, f32[512,128]{1,0:T(8,128)S(1)}, f32[16,4,16,128]{3,2,1,0:T(8,128)S(1)}, f32[16,4,16,128]{3,2,1,0:T(8,128)S(1)}, f32[1024,128]{1,0:T(8,128)S(1)}) custom-call(f32[16,4,2,16,128]{4,3,2,1,0:T(8,128)} %bitcast.6, f32[16,4096]{1,0:T(8,128)} %refs_1_.1, f32[16,4096]{1,0:T(8,128)} %refs_2_.1, f32[1024,128]{1,0:T(8,128)} %refs_3_.1), custom_call_target="tpu_custom_call" | custom-call | flops 1 | bytes 1 | tf_op jit(solution)/shard_map/prepare/pallas_call | solution.py:512
  2.6 3.0 %collective-permute-start = (f32[16,4,16,128]{3,2,1,0:T(8,128)S(1)}, f32[16,4,16,128]{3,2,1,0:T(8,128)S(1)}, u32[]{:S(2)}, u32[]{:S(2)}) collective-permute-start(f32[16,4,16,128]{3,2,1,0:T(8,128)S(1)} %get-tuple-element.42), channel_id=1, source_target_pairs={{0,4},{4,0},{8,12},{12,8},{16,20},{20,16},{24,28},{28,24},{1,5},{5... | collective-permute-start | bytes 1572872 | tf_op jit(solution)/shard_map/ppermute | solution.py:575
  5.6 0.1 collective-permute-start.1
  5.7 4.0 %collective-permute-start.4 = (f32[512,128]{1,0:T(8,128)S(1)}, f32[512,128]{1,0:T(8,128)S(1)}, u32[]{:S(2)}, u32[]{:S(2)}) collective-permute-start(f32[512,128]{1,0:T(8,128)S(1)} %get-tuple-element.45.refs_5_.refs_3_), channel_id=1, source_target_pairs={{0,24},{4,28},{8,16},{12,20},{16,8},{20,12},{24,0},{28,4},{1,25},{... | collective-permute-start | bytes 786440 | tf_op jit(solution)/shard_map/ppermute | solution.py:574
  9.8 0.0 collective-permute-start.3
  9.8 0.6 collective-permute-start.2
  10.3 5.5 %gradient_own.1 = (bf16[8,512,512]{2,1,0:T(8,128)(2,1)S(1)}, f32[8,128,256]{2,1,0:T(8,128)S(1)}, bf16[512,768]{1,0:T(8,128)(2,1)S(1)}, bf16[512,512]{1,0:T(8,128)(2,1)}) custom-call(f32[1024,128]{1,0:T(8,128)S(1)} %get-tuple-element.38.refs_0_, f32[16,4,16,128]{3,2,1,0:T(8,128)S(1)} %get-tuple-element.39.refs_1_.refs_3_, ...), custom_call_target="tpu_custom_call" | custom-call | flops 1 | bytes 1 | tf_op jit(solution)/shard_map/gradient_own/pallas_call | solution.py:512
  15.8 2.6 %collective-permute-done.refs_1_.refs_4_ = f32[16,4,16,128]{3,2,1,0:T(8,128)S(1)} collective-permute-done((f32[16,4,16,128]{3,2,1,0:T(8,128)S(1)}, f32[16,4,16,128]{3,2,1,0:T(8,128)S(1)}, u32[]{:S(2)}, u32[]{:S(2)}) %collective-permute-start) | collective-permute-done | bytes 524320 | tf_op jit(solution)/shard_map/ppermute | solution.py:575
  18.4 2.4 %gradient_peer.1.refs_0_.refs_2_ = bf16[8,512,512]{2,1,0:T(8,128)(2,1)S(1)} custom-call(bf16[512,768]{1,0:T(8,128)(2,1)S(1)} %get-tuple-element.41.refs_0_, f32[16,4,16,128]{3,2,1,0:T(8,128)S(1)} %collective-permute-done.refs_1_.refs_4_), custom_call_target="tpu_custom_call" | custom-call | flops 1 | bytes 1 | tf_op jit(solution)/shard_map/gradient_peer/pallas_call | solution.py:512
  20.8 2.3 %collective-permute-done.1.refs_1_.refs_2_ = f32[512,128]{1,0:T(8,128)S(1)} collective-permute-done((f32[512,128]{1,0:T(8,128)S(1)}, f32[512,128]{1,0:T(8,128)S(1)}, u32[]{:S(2)}, u32[]{:S(2)}) %collective-permute-start.1) | collective-permute-done | bytes 262176 | tf_op jit(solution)/shard_map/ppermute | solution.py:576
  23.2 2.8 %right_parts.1 = (f32[2,512,128]{2,1,0:T(8,128)S(1)}, f32[2,512,128]{2,1,0:T(8,128)}) custom-call(bf16[8,512,512]{2,1,0:T(8,128)(2,1)S(1)} %gradient_peer.1.refs_0_.refs_2_, f32[512,128]{1,0:T(8,128)S(1)} %collective-permute-done.1.refs_1_.refs_2_, f32[8,128,256]{2,1,0:T(8,128)S(1)} %get-tuple-element.43.refs_2_), custom_call_target="tpu_custom_call" | custom-call | flops 1 | bytes 1 | tf_op jit(solution)/shard_map/right_parts/pallas_call | solution.py:512
  26.0 2.8 %collective-permute-start.6 = (f32[2,512,128]{2,1,0:T(8,128)}, f32[2,512,128]{2,1,0:T(8,128)S(1)}, u32[]{:S(2)}, u32[]{:S(2)}) collective-permute-start(f32[2,512,128]{2,1,0:T(8,128)} %get-tuple-element.55), channel_id=1, source_target_pairs={{0,16},{4,20},{8,24},{12,28},{16,0},{20,4},{24,8},{28,12},{1,17},{... | collective-permute-start | bytes 1572872 | tf_op jit(solution)/shard_map/ppermute | solution.py:612
  28.8 0.0 collective-permute-done.4.refs_8_.refs_6_
  28.8 14.9 %collective-permute-done.3.refs_7_.refs_5_ = f32[512,128]{1,0:T(8,128)S(1)} collective-permute-done((f32[512,128]{1,0:T(8,128)S(1)}, f32[512,128]{1,0:T(8,128)S(1)}, u32[]{:S(2)}, u32[]{:S(2)}) %collective-permute-start.3) | collective-permute-done | bytes 262176 | tf_op jit(solution)/shard_map/ppermute | solution.py:574
  43.7 0.0 collective-permute-done.2.refs_6_.refs_4_
  43.7 8.3 %weight.1 = (f32[512,128]{1,0:T(8,128)S(1)}, f32[512,128]{1,0:T(8,128)S(1)}, bf16[8,512,512]{2,1,0:T(8,128)(2,1)}, bf16[8,512,512]{2,1,0:T(8,128)(2,1)}) custom-call(f32[2,512,128]{2,1,0:T(8,128)S(1)} %get-tuple-element.44.refs_0_.refs_1_, f32[512,128]{1,0:T(8,128)S(1)} %get-tuple-element.40.refs_2_.refs_1_, ...), custom_call_target="tpu_custom_call" | custom-call | flops 12884901888 | bytes 1 | tf_op jit(solution)/shard_map/weight/pallas_call | solution.py:512
  52.0 0.1 collective-permute-start.5
  52.1 2.8 %left_parts.1 = (f32[4,32,512]{2,1,0:T(8,128)S(1)}, f32[4,32,512]{2,1,0:T(8,128)S(1)}) custom-call(f32[512,128]{1,0:T(8,128)S(1)} %get-tuple-element.49.refs_0_, bf16[8,512,512]{2,1,0:T(8,128)(2,1)S(1)} %get-tuple-element.47.refs_1_, bf16[8,512,512]{2,1,0:T(8,128)(2,1)S(1)} %gradient_peer.1.refs_0_.refs_2_, ...), custom_call_target="tpu_custom_call" | custom-call | flops 6442450944 | bytes 1 | tf_op jit(solution)/shard_map/left_parts/pallas_call | solution.py:512
  54.9 0.0 collective-permute-done.5
  54.9 0.7 add.3
  55.6 6.1 %all-to-all-start = ((f32[16,32,128]{2,1,0:T(8,128)}), f32[16,32,128]{2,1,0:T(8,128)S(1)}, u32[]{:S(2)}, u32[]{:S(2)}) async-start(f32[16,32,128]{2,1,0:T(8,128)} %bitcast.1.refs_0_), calls=%async_computation | async-start | bytes 524288 | tf_op jit(solution)/shard_map/all_to_all | solution.py:675
  61.8 1.9 %collective-permute-start.9 = (f32[4,32,512]{2,1,0:T(8,128)S(1)}, f32[4,32,512]{2,1,0:T(8,128)S(1)}, u32[]{:S(2)}, u32[]{:S(2)}) collective-permute-start(f32[4,32,512]{2,1,0:T(8,128)S(1)} %get-tuple-element.60), channel_id=1, source_target_pairs={{0,4},{4,0},{8,12},{12,8},{16,20},{20,16},{24,28},{28,24},{1,5},{5... | collective-permute-start | bytes 786440 | tf_op jit(solution)/shard_map/ppermute | solution.py:662
  63.7 6.4 %pair_peer.1.refs_0_ = f32[16,4,16,128]{3,2,1,0:T(8,128)S(1)} custom-call(f32[16,32,128]{2,1,0:T(8,128)} %bitcast.1.refs_0_, bf16[8,512,512]{2,1,0:T(8,128)(2,1)} %get-tuple-element.53.refs_1_, bf16[512,512]{1,0:T(8,128)(2,1)} %get-tuple-element.54.refs_2_), custom_call_target="tpu_custom_call" | custom-call | flops 6442450944 | bytes 1 | tf_op jit(solution)/shard_map/pair_peer/pallas_call | solution.py:512
  70.1 0.2 collective-permute-start.7
  70.3 0.0 collective-permute-done.6.refs_2_
  70.3 0.8 right_halve.1
  71.1 1.9 %collective-permute-start.8 = (f32[1,512,128]{2,1,0:T(8,128)}, f32[1,512,128]{2,1,0:T(8,128)S(1)}, u32[]{:S(2)}, u32[]{:S(2)}) collective-permute-start(f32[1,512,128]{2,1,0:T(8,128)} %get-tuple-element.58), channel_id=1, source_target_pairs={{0,8},{4,12},{8,0},{12,4},{16,24},{20,28},{24,16},{28,20},{1,9},{5... | collective-permute-start | bytes 786440 | tf_op jit(solution)/shard_map/ppermute | solution.py:669
  72.9 0.0 all-to-all-done.refs_2_
  72.9 0.8 weight_sum.1.refs_0_
  73.7 5.5 %all-to-all-start.1 = ((f32[16,32,128]{2,1,0:T(8,128)}), f32[16,32,128]{2,1,0:T(8,128)S(1)}, u32[]{:S(2)}, u32[]{:S(2)}) async-start(f32[16,32,128]{2,1,0:T(8,128)} %weight_sum.1.refs_0_), calls=%async_computation.1 | async-start | bytes 524288 | tf_op jit(solution)/shard_map/all_to_all | solution.py:689
  79.3 0.0 collective-permute-done.9.refs_2_
  79.3 0.1 collective-permute-start.10
  79.4 2.0 %collective-permute-start.11 = (f32[32,512]{1,0:T(8,128)S(1)}, f32[32,512]{1,0:T(8,128)S(1)}, u32[]{:S(2)}, u32[]{:S(2)}) collective-permute-start(f32[32,512]{1,0:T(8,128)S(1)} %get-tuple-element.63), channel_id=1, source_target_pairs={{0,2},{1,3},{2,0},{3,1},{4,6},{5,7},{6,4},{7,5},{8,10},{9,11},{10,... | collective-permute-start | bytes 196616 | tf_op jit(solution)/shard_map/ppermute | solution.py:692
  81.4 0.1 collective-permute-start.12
  81.4 6.4 %pair_own.1.refs_0_ = f32[16,4,16,128]{3,2,1,0:T(8,128)S(1)} custom-call(f32[16,32,128]{2,1,0:T(8,128)} %weight_sum.1.refs_0_, bf16[8,512,512]{2,1,0:T(8,128)(2,1)} %get-tuple-element.57.refs_1_, bf16[512,512]{1,0:T(8,128)(2,1)} %get-tuple-element.54.refs_2_), custom_call_target="tpu_custom_call" | custom-call | flops 6442450944 | bytes 1 | tf_op jit(solution)/shard_map/pair_own/pallas_call | solution.py:512
  87.8 0.0 collective-permute-done.8.refs_3_
  87.8 0.0 collective-permute-done.7.refs_1_
  87.9 0.0 collective-permute-done.10.refs_5_
  87.9 0.0 collective-permute-done.11.refs_6_
  87.9 0.0 collective-permute-done.12.refs_7_
  87.9 2.2 %finish.1 = (f32[16,4,2,16,128]{4,3,2,1,0:T(8,128)}, f32[16,1024]{1,0:T(8,128)}, f32[16,4096]{1,0:T(8,128)}) custom-call(f32[16,4,16,128]{3,2,1,0:T(8,128)S(1)} %pair_own.1.refs_0_, f32[16,4,16,128]{3,2,1,0:T(8,128)S(1)} %collective-permute-done.7.refs_1_, f32[1,512,128]{2,1,0:T(8,128)S(1)} %get-tuple-element.56.refs_1_.refs_2_, ...), custom_call_target="tpu_custom_call" | custom-call | flops 1 | bytes 1 | tf_op jit(solution)/shard_map/finish/pallas_call | solution.py:512
  90.0 0.0 all-to-all-done.1
  90.1 0.2 collective-permute-start.13
  90.3 1.4 %collective-permute-done.13.refs_1_ = f32[512,128]{1,0:T(8,128)S(1)} collective-permute-done((f32[512,128]{1,0:T(8,128)S(1)}, f32[512,128]{1,0:T(8,128)S(1)}, u32[]{:S(2)}, u32[]{:S(2)}) %collective-permute-start.13) | collective-permute-done | bytes 262176 | tf_op jit(solution)/shard_map/ppermute | solution.py:719
  91.7 1.1 %place.1 = f32[1024,128]{1,0:T(8,128)} custom-call(f32[512,128]{1,0:T(8,128)S(1)} %bitcast.5, f32[512,128]{1,0:T(8,128)S(1)} %collective-permute-done.13.refs_1_), custom_call_target="tpu_custom_call" | custom-call | flops 1 | bytes 1 | tf_op jit(solution)/shard_map/place/pallas_call | solution.py:512
  (1 shorter events, 0.0 us)
Async XLA Ops:
  2.6 15.8 %collective-permute-start = (f32[16,4,16,128]{3,2,1,0:T(8,128)S(1)}, f32[16,4,16,128]{3,2,1,0:T(8,128)S(1)}, u32[]{:S(2)}, u32[]{:S(2)}) collective-permute-start(f32[16,4,16,128]{3,2,1,0:T(8,128)S(1)} %get-tuple-element.42), channel_id=1, source_target_pairs={{0,4},{4,0},{8,12},{12,8},{16,20},{20,16},{24,28},{28,24},{1,5},{5... | collective-permute-start | bytes 1572872 | tf_op jit(solution)/shard_map/ppermute | solution.py:575
  5.6 17.5 %collective-permute-start.1 = (f32[512,128]{1,0:T(8,128)S(1)}, f32[512,128]{1,0:T(8,128)S(1)}, u32[]{:S(2)}, u32[]{:S(2)}) collective-permute-start(f32[512,128]{1,0:T(8,128)S(1)} %get-tuple-element.40.refs_2_.refs_1_), channel_id=1, source_target_pairs={{0,4},{4,0},{8,12},{12,8},{16,20},{20,16},{24,28},{28,24},{1,5},{5... | collective-permute-start | bytes 786440 | tf_op jit(solution)/shard_map/ppermute | solution.py:576
  5.7 23.1 %collective-permute-start.4 = (f32[512,128]{1,0:T(8,128)S(1)}, f32[512,128]{1,0:T(8,128)S(1)}, u32[]{:S(2)}, u32[]{:S(2)}) collective-permute-start(f32[512,128]{1,0:T(8,128)S(1)} %get-tuple-element.45.refs_5_.refs_3_), channel_id=1, source_target_pairs={{0,24},{4,28},{8,16},{12,20},{16,8},{20,12},{24,0},{28,4},{1,25},{... | collective-permute-start | bytes 786440 | tf_op jit(solution)/shard_map/ppermute | solution.py:574
  9.8 34.0 %collective-permute-start.3 = (f32[512,128]{1,0:T(8,128)S(1)}, f32[512,128]{1,0:T(8,128)S(1)}, u32[]{:S(2)}, u32[]{:S(2)}) collective-permute-start(f32[512,128]{1,0:T(8,128)S(1)} %get-tuple-element.45.refs_5_.refs_3_), channel_id=1, source_target_pairs={{0,16},{4,20},{8,24},{12,28},{16,0},{20,4},{24,8},{28,12},{1,17},{... | collective-permute-start | bytes 786440 | tf_op jit(solution)/shard_map/ppermute | solution.py:574
  9.8 34.0 %collective-permute-start.2 = (f32[512,128]{1,0:T(8,128)S(1)}, f32[512,128]{1,0:T(8,128)S(1)}, u32[]{:S(2)}, u32[]{:S(2)}) collective-permute-start(f32[512,128]{1,0:T(8,128)S(1)} %get-tuple-element.45.refs_5_.refs_3_), channel_id=1, source_target_pairs={{0,8},{4,12},{8,0},{12,4},{16,24},{20,28},{24,16},{28,20},{1,9},{5... | collective-permute-start | bytes 786440 | tf_op jit(solution)/shard_map/ppermute | solution.py:574
  26.0 44.3 %collective-permute-start.6 = (f32[2,512,128]{2,1,0:T(8,128)}, f32[2,512,128]{2,1,0:T(8,128)S(1)}, u32[]{:S(2)}, u32[]{:S(2)}) collective-permute-start(f32[2,512,128]{2,1,0:T(8,128)} %get-tuple-element.55), channel_id=1, source_target_pairs={{0,16},{4,20},{8,24},{12,28},{16,0},{20,4},{24,8},{28,12},{1,17},{... | collective-permute-start | bytes 1572872 | tf_op jit(solution)/shard_map/ppermute | solution.py:612
  52.0 2.9 %collective-permute-start.5 = (f32[512,128]{1,0:T(8,128)S(1)}, f32[512,128]{1,0:T(8,128)S(1)}, u32[]{:S(2)}, u32[]{:S(2)}) collective-permute-start(f32[512,128]{1,0:T(8,128)S(1)} %get-tuple-element.50), channel_id=1, source_target_pairs={{0,1},{1,0},{2,3},{3,2},{4,5},{5,4},{6,7},{7,6},{8,9},{9,8},{10,11... | collective-permute-start | bytes 786440 | tf_op jit(solution)/shard_map/ppermute | solution.py:628
  55.6 17.3 %all-to-all-start = ((f32[16,32,128]{2,1,0:T(8,128)}), f32[16,32,128]{2,1,0:T(8,128)S(1)}, u32[]{:S(2)}, u32[]{:S(2)}) async-start(f32[16,32,128]{2,1,0:T(8,128)} %bitcast.1.refs_0_), calls=%async_computation | async-start | bytes 524288 | tf_op jit(solution)/shard_map/all_to_all | solution.py:675
  61.8 17.5 %collective-permute-start.9 = (f32[4,32,512]{2,1,0:T(8,128)S(1)}, f32[4,32,512]{2,1,0:T(8,128)S(1)}, u32[]{:S(2)}, u32[]{:S(2)}) collective-permute-start(f32[4,32,512]{2,1,0:T(8,128)S(1)} %get-tuple-element.60), channel_id=1, source_target_pairs={{0,4},{4,0},{8,12},{12,8},{16,20},{20,16},{24,28},{28,24},{1,5},{5... | collective-permute-start | bytes 786440 | tf_op jit(solution)/shard_map/ppermute | solution.py:662
  70.1 17.7 %collective-permute-start.7 = (f32[16,4,16,128]{3,2,1,0:T(8,128)S(1)}, f32[16,4,16,128]{3,2,1,0:T(8,128)S(1)}, u32[]{:S(2)}, u32[]{:S(2)}) collective-permute-start(f32[16,4,16,128]{3,2,1,0:T(8,128)S(1)} %pair_peer.1.refs_0_), channel_id=1, source_target_pairs={{0,4},{4,0},{8,12},{12,8},{16,20},{20,16},{24,28},{28,24},{1,5},{5... | collective-permute-start | bytes 1572872 | tf_op jit(solution)/shard_map/ppermute | solution.py:673
  71.1 16.8 %collective-permute-start.8 = (f32[1,512,128]{2,1,0:T(8,128)}, f32[1,512,128]{2,1,0:T(8,128)S(1)}, u32[]{:S(2)}, u32[]{:S(2)}) collective-permute-start(f32[1,512,128]{2,1,0:T(8,128)} %get-tuple-element.58), channel_id=1, source_target_pairs={{0,8},{4,12},{8,0},{12,4},{16,24},{20,28},{24,16},{28,20},{1,9},{5... | collective-permute-start | bytes 786440 | tf_op jit(solution)/shard_map/ppermute | solution.py:669
  73.7 16.4 %all-to-all-start.1 = ((f32[16,32,128]{2,1,0:T(8,128)}), f32[16,32,128]{2,1,0:T(8,128)S(1)}, u32[]{:S(2)}, u32[]{:S(2)}) async-start(f32[16,32,128]{2,1,0:T(8,128)} %weight_sum.1.refs_0_), calls=%async_computation.1 | async-start | bytes 524288 | tf_op jit(solution)/shard_map/all_to_all | solution.py:689
  79.3 8.6 %collective-permute-start.10 = (f32[32,512]{1,0:T(8,128)S(1)}, f32[32,512]{1,0:T(8,128)S(1)}, u32[]{:S(2)}, u32[]{:S(2)}) collective-permute-start(f32[32,512]{1,0:T(8,128)S(1)} %get-tuple-element.62), channel_id=1, source_target_pairs={{0,1},{1,0},{2,3},{3,2},{4,5},{5,4},{6,7},{7,6},{8,9},{9,8},{10,11... | collective-permute-start | bytes 196616 | tf_op jit(solution)/shard_map/ppermute | solution.py:692
  79.4 8.5 %collective-permute-start.11 = (f32[32,512]{1,0:T(8,128)S(1)}, f32[32,512]{1,0:T(8,128)S(1)}, u32[]{:S(2)}, u32[]{:S(2)}) collective-permute-start(f32[32,512]{1,0:T(8,128)S(1)} %get-tuple-element.63), channel_id=1, source_target_pairs={{0,2},{1,3},{2,0},{3,1},{4,6},{5,7},{6,4},{7,5},{8,10},{9,11},{10,... | collective-permute-start | bytes 196616 | tf_op jit(solution)/shard_map/ppermute | solution.py:692
  81.4 6.5 %collective-permute-start.12 = (f32[32,512]{1,0:T(8,128)S(1)}, f32[32,512]{1,0:T(8,128)S(1)}, u32[]{:S(2)}, u32[]{:S(2)}) collective-permute-start(f32[32,512]{1,0:T(8,128)S(1)} %get-tuple-element.64), channel_id=1, source_target_pairs={{0,3},{1,2},{2,1},{3,0},{4,7},{5,6},{6,5},{7,4},{8,11},{9,10},{10,... | collective-permute-start | bytes 196616 | tf_op jit(solution)/shard_map/ppermute | solution.py:692
  90.1 1.6 %collective-permute-start.13 = (f32[512,128]{1,0:T(8,128)S(1)}, f32[512,128]{1,0:T(8,128)S(1)}, u32[]{:S(2)}, u32[]{:S(2)}) collective-permute-start(f32[512,128]{1,0:T(8,128)S(1)} %bitcast.4), channel_id=1, source_target_pairs={{0,1},{1,0},{2,3},{3,2},{4,5},{5,4},{6,7},{7,6},{8,9},{9,8},{10,11... | collective-permute-start | bytes 786440 | tf_op jit(solution)/shard_map/ppermute | solution.py:719

commit v15 on v14

--- a/solution.py
+++ b/solution.py
@@ -171,12 +171,14 @@
         )
 
 
-def gradient_phase(blocks, cotangent_ref, out_ref, weight_cat):
+def gradient_phase(blocks, cotangent_ref, out_ref, spread_ref, weight_cat):
     fold = fold_of(blocks * cotangent_ref.shape[2])
     slots = slots_of(blocks)
 
     def step_of(pair, carry):
         high, low = spread_of(cotangent_ref, pair, slots, fold)
+        spread_ref[pair, 0] = high
+        spread_ref[pair, 1] = low
         found = dot_rows(weight_cat[...], jnp.concatenate([high, high, low], 1))
         out_ref[pair] = jnp.concatenate(halves(found), 1)
         return carry
@@ -190,6 +192,7 @@
     cotangent_ref,
     left_ref,
     out_ref,
+    spread_ref,
     partial_ref,
     weight_cat,
     flip_hbm,
@@ -200,7 +203,7 @@
 ):
     fold = fold_of(blocks * cotangent_ref.shape[2])
     prepare_weight(weight_ref, weight_cat, fold)
-    gradient_phase(blocks, cotangent_ref, out_ref, weight_cat)
+    gradient_phase(blocks, cotangent_ref, out_ref, spread_ref, weight_cat)
 
     def store(step, found):
         partial_ref[step] = found
@@ -220,8 +223,8 @@
     copy.wait()
 
 
-def peer_kernel(blocks, weight_cat, cotangent_ref, out_ref):
-    gradient_phase(blocks, cotangent_ref, out_ref, weight_cat)
+def peer_kernel(blocks, weight_cat, cotangent_ref, out_ref, spread_ref):
+    gradient_phase(blocks, cotangent_ref, out_ref, spread_ref, weight_cat)
 
 
 def right_phase(left_ref, factor_ref, left_flip, store):
@@ -280,18 +283,16 @@
                 for slot in range(blocks):
                     start = (place * blocks + slot) * depth
                     row = pl.multiple_of(((2 * step + part) * fold + place) * depth, depth)
-                    out_ref = send_ref if slot >= blocks // 2 else keep_ref
-                    place_of = slot % (blocks // 2)
-                    out_ref[place_of, pl.ds(row, depth), :] = turned[start : start + depth]
+                    out_ref = send_ref if slot % 2 else keep_ref
+                    out_ref[slot // 2, pl.ds(row, depth), :] = turned[start : start + depth]
 
     right_phase(left_ref, peer_ref, left_flip, store)
 
 
 def halve_kernel(keep_ref, found_ref, keep_out, send_out):
-    half = keep_ref.shape[0] // 2
-    for slot in range(half):
-        keep_out[slot] = keep_ref[slot] + found_ref[slot]
-        send_out[slot] = keep_ref[half + slot] + found_ref[half + slot]
+    for slot in range(keep_ref.shape[0]):
+        out_ref = send_out if slot % 2 else keep_out
+        out_ref[slot // 2] = keep_ref[slot] + found_ref[slot]
 
 
 def right_rows(right_refs, step, fold, depth):
@@ -305,13 +306,13 @@
     )
 
 
-def weight_kernel(blocks, own_left, peer_left, own_cotangent, peer_cotangent, *refs):
+def weight_kernel(blocks, depth, own_left, peer_left, own_spread, peer_spread, *refs):
     right_refs = refs[:blocks]
     keep_ref, send_ref, own_out, peer_out, own_ref, peer_ref, total, semaphores = refs[blocks:]
     channels = ENTRY_CHANNELS
-    depth, pairs = own_cotangent.shape[2:]
     fold = fold_of(blocks * depth)
     lanes = fold * blocks * depth
+    pairs = total.shape[1] // fold
     high, low = halves(both_left([own_left, peer_left]))
     left_cat = jnp.concatenate([high, low, high], 1)
 
@@ -348,10 +349,10 @@
 
     def weight_step(pair, carry):
         lefts, rights = [], []
-        for ref, cotangent_ref in ((own_ref, own_cotangent), (peer_ref, peer_cotangent)):
-            high, low = spread_of(cotangent_ref, pair, slots_of(blocks), fold)
+        for ref, spread_ref in ((own_ref, own_spread), (peer_ref, peer_spread)):
+            high = spread_ref[pair, 0]
             lefts += [ref[pair], ref[pair, :, : 2 * lanes]]
-            rights += [high, high, low]
+            rights += [high, high, spread_ref[pair, 1]]
         total[...] += dot(jnp.concatenate(lefts, 1), jnp.concatenate(rights, 0))
         return carry
 
@@ -446,7 +447,7 @@
                 out_ref[row, slots[slot]] = turned[slot * depth : (slot + 1) * depth]
         return carry
 
-    lax.fori_loop(0, count, step_of, 0, unroll=2)
+    lax.fori_loop(0, count, step_of, 0)
 
 
 def finish_kernel(own_ref, other_ref, keep_ref, found_ref, *refs):
@@ -582,10 +583,12 @@
     weight_cat = shape(tall, 3 * fold * pairs, kind=BF16)
     flip_scratch = pltpu.VMEM((2 * sequences, rows * channels), BF16)
     flip_sizes = (2 * fold * pairs, tall)
-    grad_own, partial, weight_cat, weight_flip = large(
+    spread = shape(row_pairs, 2, 2 * lanes, fold * pairs, kind=BF16)
+    grad_own, spread_own, partial, weight_cat, weight_flip = large(
         functools.partial(gradient_kernel, blocks),
         [
             factor,
+            spread,
             shape(steps // 2, sequences, 2 * lanes),
             weight_cat,
             pltpu.HBM(flip_sizes, BF16),
@@ -597,11 +600,11 @@
             pltpu.SemaphoreType.DMA,
         ],
         "gradient_own",
-        out_specs=[vmem, vmem, vmem, hbm],
+        out_specs=[vmem, vmem, vmem, vmem, hbm],
     )(weight, cotangent_own, left)
-    grad_peer = large(functools.partial(peer_kernel, blocks), factor, [], "gradient_peer")(
-        weight_cat, cotangent_peer
-    )
+    grad_peer, spread_peer = large(
+        functools.partial(peer_kernel, blocks), [factor, spread], [], "gradient_peer"
+    )(weight_cat, cotangent_peer)
     right_half = shape(blocks // 2, channels * depth, sequences)
     right_keep, right_send = large(
         functools.partial(right_kernel, blocks, depth),
@@ -609,10 +612,10 @@
         [flip_scratch],
         "right_parts",
     )(grad_peer, left_peer, partial)
-    right_send = lax.ppermute(right_send, "blk", slot_moves[blocks // 2])
+    right_send = lax.ppermute(right_send, "blk", slot_moves[1])
 
     keep, send, outer_own, outer_peer = large(
-        functools.partial(weight_kernel, blocks),
+        functools.partial(weight_kernel, blocks, depth),
         [shape(outer // 2, pairs)] * 2 + [pltpu.HBM(factor.shape, BF16)] * 2,
         [
             factor_scratch,
@@ -624,7 +627,7 @@
         after=[right_keep],
         flops=2 * work,
         out_specs=[vmem, vmem, hbm, hbm],
-    )(left, left_peer, cotangent_own, cotangent_peer, *rights)
+    )(left, left_peer, spread_own, spread_peer, *rights)
     sent = lax.ppermute(send, "inner", cores)
 
     size = sequences // inner
@@ -660,14 +663,14 @@
 
     pieces, left_other = lax.optimization_barrier((pieces, left_other))
     left_other = lax.ppermute(left_other, "blk", partner)
-    slot = blocks // 4
-    while slot:
-        part = shape(slot, channels * depth, sequences)
+    slot = 2
+    while slot < blocks:
+        part = shape(blocks // (2 * slot), channels * depth, sequences)
         right_keep, right_send = call(
             halve_kernel, [part, part], name="right_halve", after=[pieces]
         )(right_keep, right_send)
         right_send = lax.ppermute(right_send, "blk", slot_moves[slot])
-        slot = slot // 2
+        slot = 2 * slot
 
     pair_other = pair(outer_peer, [pieces], "pair_peer")
     pair_found = lax.ppermute(pair_other, "blk", partner)

time: 93.1 us -> 81.7 us (0.88)
  waiting for transfers between devices: 21.2 us -> 14.3 us
  Pallas kernels: 41.4 us -> 38.5 us
  starting transfers between devices: 28.6 us -> 27 us
    ppermute x3, waiting for transfers between devices: 14.9 us -> 3.78 us  [local(): rights.append(lax.ppermute(right, 'blk', slot_moves[slot]))]
    ppermute x1, waiting for transfers between devices: 0.01 us -> 3.28 us  [local(): right_send = lax.ppermute(right_send, 'blk', slot_moves[slot])]
    pallas_call x13, Pallas kernels: 41.4 us -> 38.5 us  [run(): pl.pallas_call(lambda *refs: kernel(*refs[len(after):]), out_shape=out_sh...]
    all_to_all x2, starting transfers between devices: 11.7 us -> 10.4 us  [local(): lax.all_to_all(pieces, everyone, 0, 0, axis_index_groups=core_groups)]
    ppermute x1, starting transfers between devices: 2.81 us -> 1.8 us  [local(): right_send = lax.ppermute(right_send, 'blk', slot_moves[1])]
  transfers between devices with their start and end apart: 16 -> 16, of which waited for: 4 -> 6; matrix products, arithmetic and copies ran while one was open for 1% -> 1% of each run, Pallas kernels for 41% -> 44%
where the time goes in v15:
time: 81.7 us; the launch traced here: 81.3 us
  Pallas kernels  38.5 us (47%)
  starting transfers between devices  27 us (33%)
  waiting for transfers between devices  14.3 us (18%)
    pallas_call x13, Pallas kernels, run(): pl.pallas_call(lambda *refs: kernel(*refs[len(after):]), out_shape=out_sh...  38.5 us
    all_to_all x2, starting transfers between devices, local(): lax.all_to_all(pieces, everyone, 0, 0, axis_index_groups=core_groups)  10.4 us
    ppermute x3, starting transfers between devices, local(): rights.append(lax.ppermute(right, 'blk', slot_moves[slot]))  4.6 us
    ppermute x3, waiting for transfers between devices, local(): rights.append(lax.ppermute(right, 'blk', slot_moves[slot]))  3.78 us
    ppermute x1, waiting for transfers between devices, local(): right_send = lax.ppermute(right_send, 'blk', slot_moves[slot])  3.28 us
    ppermute x1, starting transfers between devices, local(): cotangent_peer = lax.ppermute(cotangent_send, 'blk', partner)  3.03 us
    ppermute x1, starting transfers between devices, local(): right_send = lax.ppermute(right_send, 'blk', slot_moves[slot])  2.76 us
    ppermute x1, waiting for transfers between devices, local(): cotangent_peer = lax.ppermute(cotangent_send, 'blk', partner)  2.55 us
  transfers between devices with their start and end apart: 16, of which 6 were waited for; matrix products, arithmetic and copies ran while one was open for 1% of the time, Pallas kernels for 44%

profile of v15, /device:TPU:0, one launch (start us, length us, event | category | flops | bytes accessed | tf_op | source)
XLA Modules:
  0.0 81.3 jit_solution(16523810408279572980)
XLA Ops:
  0.6 2.0 %prepare.1 = (f32[512,128]{1,0:T(8,128)S(1)}, f32[512,128]{1,0:T(8,128)S(1)}, f32[16,4,16,128]{3,2,1,0:T(8,128)S(1)}, f32[16,4,16,128]{3,2,1,0:T(8,128)S(1)}, f32[1024,128]{1,0:T(8,128)S(1)}) custom-call(f32[16,4,2,16,128]{4,3,2,1,0:T(8,128)} %bitcast.6, f32[16,4096]{1,0:T(8,128)} %refs_1_.1, f32[16,4096]{1,0:T(8,128)} %refs_2_.1, f32[1024,128]{1,0:T(8,128)} %refs_3_.1), custom_call_target="tpu_custom_call" | custom-call | flops 1 | bytes 1 | tf_op jit(solution)/shard_map/prepare/pallas_call | solution.py:513
  2.6 3.0 %collective-permute-start = (f32[16,4,16,128]{3,2,1,0:T(8,128)S(1)}, f32[16,4,16,128]{3,2,1,0:T(8,128)S(1)}, u32[]{:S(2)}, u32[]{:S(2)}) collective-permute-start(f32[16,4,16,128]{3,2,1,0:T(8,128)S(1)} %get-tuple-element.45), channel_id=1, source_target_pairs={{0,4},{4,0},{8,12},{12,8},{16,20},{20,16},{24,28},{28,24},{1,5},{5... | collective-permute-start | bytes 1572872 | tf_op jit(solution)/shard_map/ppermute | solution.py:576
  5.6 0.1 collective-permute-start.1
  5.7 4.0 %collective-permute-start.4 = (f32[512,128]{1,0:T(8,128)S(1)}, f32[512,128]{1,0:T(8,128)S(1)}, u32[]{:S(2)}, u32[]{:S(2)}) collective-permute-start(f32[512,128]{1,0:T(8,128)S(1)} %get-tuple-element.51.refs_5_.refs_3_), channel_id=1, source_target_pairs={{0,24},{4,28},{8,16},{12,20},{16,8},{20,12},{24,0},{28,4},{1,25},{... | collective-permute-start | bytes 786440 | tf_op jit(solution)/shard_map/ppermute | solution.py:575
  9.8 0.0 collective-permute-start.3
  9.8 0.6 collective-permute-start.2
  10.3 5.5 %gradient_own.1 = (bf16[8,512,512]{2,1,0:T(8,128)(2,1)S(1)}, bf16[8,2,256,256]{3,2,1,0:T(8,128)(2,1)S(1)}, f32[8,128,256]{2,1,0:T(8,128)S(1)}, bf16[512,768]{1,0:T(8,128)(2,1)S(1)}, bf16[512,512]{1,0:T(8,128)(2,1)}) custom-call(f32[1024,128]{1,0:T(8,128)S(1)} %get-tuple-element.41.refs_0_, f32[16,4,16,128]{3,2,1,0:T(8,128)S(1)} %get-tuple-element.42.refs_1_, ...), custom_call_target="tpu_custom_call" | custom-call | flops 1 | bytes 1 | tf_op jit(solution)/shard_map/gradient_own/pallas_call | solution.py:513
  15.8 2.5 %collective-permute-done.refs_1_ = f32[16,4,16,128]{3,2,1,0:T(8,128)S(1)} collective-permute-done((f32[16,4,16,128]{3,2,1,0:T(8,128)S(1)}, f32[16,4,16,128]{3,2,1,0:T(8,128)S(1)}, u32[]{:S(2)}, u32[]{:S(2)}) %collective-permute-start) | collective-permute-done | bytes 524320 | tf_op jit(solution)/shard_map/ppermute | solution.py:576
  18.4 2.5 %gradient_peer.1 = (bf16[8,512,512]{2,1,0:T(8,128)(2,1)S(1)}, bf16[8,2,256,256]{3,2,1,0:T(8,128)(2,1)S(1)}) custom-call(bf16[512,768]{1,0:T(8,128)(2,1)S(1)} %get-tuple-element.44.refs_0_, f32[16,4,16,128]{3,2,1,0:T(8,128)S(1)} %collective-permute-done.refs_1_), custom_call_target="tpu_custom_call" | custom-call | flops 1 | bytes 1 | tf_op jit(solution)/shard_map/gradient_peer/pallas_call | solution.py:513
  20.9 2.3 %collective-permute-done.1.refs_1_.refs_2_ = f32[512,128]{1,0:T(8,128)S(1)} collective-permute-done((f32[512,128]{1,0:T(8,128)S(1)}, f32[512,128]{1,0:T(8,128)S(1)}, u32[]{:S(2)}, u32[]{:S(2)}) %collective-permute-start.1) | collective-permute-done | bytes 262176 | tf_op jit(solution)/shard_map/ppermute | solution.py:577
  23.2 2.8 %right_parts.1 = (f32[2,512,128]{2,1,0:T(8,128)S(1)}, f32[2,512,128]{2,1,0:T(8,128)}) custom-call(bf16[8,512,512]{2,1,0:T(8,128)(2,1)S(1)} %get-tuple-element.46.refs_0_.refs_2_, f32[512,128]{1,0:T(8,128)S(1)} %collective-permute-done.1.refs_1_.refs_2_, f32[8,128,256]{2,1,0:T(8,128)S(1)} %get-tuple-element.47.refs_2_), custom_call_target="tpu_custom_call" | custom-call | flops 1 | bytes 1 | tf_op jit(solution)/shard_map/right_parts/pallas_call | solution.py:513
  26.0 1.8 %collective-permute-start.6 = (f32[2,512,128]{2,1,0:T(8,128)}, f32[2,512,128]{2,1,0:T(8,128)S(1)}, u32[]{:S(2)}, u32[]{:S(2)}) collective-permute-start(f32[2,512,128]{2,1,0:T(8,128)} %get-tuple-element.61), channel_id=1, source_target_pairs={{0,8},{4,12},{8,0},{12,4},{16,24},{20,28},{24,16},{28,20},{1,9},{5... | collective-permute-start | bytes 1572872 | tf_op jit(solution)/shard_map/ppermute | solution.py:615
  27.8 0.0 collective-permute-done.4.refs_8_.refs_6_
  27.8 3.8 %collective-permute-done.3.refs_7_.refs_5_ = f32[512,128]{1,0:T(8,128)S(1)} collective-permute-done((f32[512,128]{1,0:T(8,128)S(1)}, f32[512,128]{1,0:T(8,128)S(1)}, u32[]{:S(2)}, u32[]{:S(2)}) %collective-permute-start.3) | collective-permute-done | bytes 262176 | tf_op jit(solution)/shard_map/ppermute | solution.py:575
  31.6 0.0 collective-permute-done.2.refs_6_.refs_4_
  31.6 8.2 %weight.1 = (f32[512,128]{1,0:T(8,128)S(1)}, f32[512,128]{1,0:T(8,128)S(1)}, bf16[8,512,512]{2,1,0:T(8,128)(2,1)}, bf16[8,512,512]{2,1,0:T(8,128)(2,1)}) custom-call(f32[2,512,128]{2,1,0:T(8,128)S(1)} %get-tuple-element.48.refs_0_.refs_1_, f32[512,128]{1,0:T(8,128)S(1)} %get-tuple-element.43.refs_2_.refs_1_, ...), custom_call_target="tpu_custom_call" | custom-call | flops 12884901888 | bytes 1 | tf_op jit(solution)/shard_map/weight/pallas_call | solution.py:513
  39.8 0.1 collective-permute-start.5
  39.9 2.8 %left_parts.1 = (f32[4,32,512]{2,1,0:T(8,128)S(1)}, f32[4,32,512]{2,1,0:T(8,128)S(1)}) custom-call(f32[512,128]{1,0:T(8,128)S(1)} %get-tuple-element.55.refs_0_, bf16[8,512,512]{2,1,0:T(8,128)(2,1)S(1)} %get-tuple-element.53.refs_1_, bf16[8,512,512]{2,1,0:T(8,128)(2,1)S(1)} %get-tuple-element.46.refs_0_.refs_2_, ...), custom_call_target="tpu_custom_call" | custom-call | flops 6442450944 | bytes 1 | tf_op jit(solution)/shard_map/left_parts/pallas_call | solution.py:513
  42.7 0.0 collective-permute-done.5
  42.7 0.7 add.3
  43.4 5.7 %all-to-all-start = ((f32[16,32,128]{2,1,0:T(8,128)}), f32[16,32,128]{2,1,0:T(8,128)S(1)}, u32[]{:S(2)}, u32[]{:S(2)}) async-start(f32[16,32,128]{2,1,0:T(8,128)} %bitcast.1.refs_0_), calls=%async_computation | async-start | bytes 524288 | tf_op jit(solution)/shard_map/all_to_all | solution.py:678
  49.2 2.0 %collective-permute-start.9 = (f32[4,32,512]{2,1,0:T(8,128)S(1)}, f32[4,32,512]{2,1,0:T(8,128)S(1)}, u32[]{:S(2)}, u32[]{:S(2)}) collective-permute-start(f32[4,32,512]{2,1,0:T(8,128)S(1)} %get-tuple-element.66), channel_id=1, source_target_pairs={{0,4},{4,0},{8,12},{12,8},{16,20},{20,16},{24,28},{28,24},{1,5},{5... | collective-permute-start | bytes 786440 | tf_op jit(solution)/shard_map/ppermute | solution.py:665
  51.1 5.0 %pair_peer.1.refs_0_ = f32[16,4,16,128]{3,2,1,0:T(8,128)S(1)} custom-call(f32[16,32,128]{2,1,0:T(8,128)} %bitcast.1.refs_0_, bf16[8,512,512]{2,1,0:T(8,128)(2,1)} %get-tuple-element.59.refs_1_, bf16[512,512]{1,0:T(8,128)(2,1)} %get-tuple-element.60.refs_2_), custom_call_target="tpu_custom_call" | custom-call | flops 6442450944 | bytes 1 | tf_op jit(solution)/shard_map/pair_peer/pallas_call | solution.py:513
  56.1 0.2 collective-permute-start.7
  56.3 0.0 collective-permute-done.6.refs_2_
  56.3 0.8 right_halve.1
  57.1 2.8 %collective-permute-start.8 = (f32[1,512,128]{2,1,0:T(8,128)}, f32[1,512,128]{2,1,0:T(8,128)S(1)}, u32[]{:S(2)}, u32[]{:S(2)}) collective-permute-start(f32[1,512,128]{2,1,0:T(8,128)} %get-tuple-element.64), channel_id=1, source_target_pairs={{0,16},{4,20},{8,24},{12,28},{16,0},{20,4},{24,8},{28,12},{1,17},{... | collective-permute-start | bytes 786440 | tf_op jit(solution)/shard_map/ppermute | solution.py:672
  59.8 0.0 all-to-all-done.refs_2_
  59.8 0.8 weight_sum.1.refs_0_
  60.6 4.6 %all-to-all-start.1 = ((f32[16,32,128]{2,1,0:T(8,128)}), f32[16,32,128]{2,1,0:T(8,128)S(1)}, u32[]{:S(2)}, u32[]{:S(2)}) async-start(f32[16,32,128]{2,1,0:T(8,128)} %weight_sum.1.refs_0_), calls=%async_computation.1 | async-start | bytes 524288 | tf_op jit(solution)/shard_map/all_to_all | solution.py:692
  65.2 0.0 collective-permute-done.9.refs_2_
  65.3 0.1 collective-permute-start.10
  65.4 2.0 %collective-permute-start.11 = (f32[32,512]{1,0:T(8,128)S(1)}, f32[32,512]{1,0:T(8,128)S(1)}, u32[]{:S(2)}, u32[]{:S(2)}) collective-permute-start(f32[32,512]{1,0:T(8,128)S(1)} %get-tuple-element.69), channel_id=1, source_target_pairs={{0,2},{1,3},{2,0},{3,1},{4,6},{5,7},{6,4},{7,5},{8,10},{9,11},{10,... | collective-permute-start | bytes 196616 | tf_op jit(solution)/shard_map/ppermute | solution.py:695
  67.3 0.1 collective-permute-start.12
  67.4 5.0 %pair_own.1.refs_0_ = f32[16,4,16,128]{3,2,1,0:T(8,128)S(1)} custom-call(f32[16,32,128]{2,1,0:T(8,128)} %weight_sum.1.refs_0_, bf16[8,512,512]{2,1,0:T(8,128)(2,1)} %get-tuple-element.63.refs_1_, bf16[512,512]{1,0:T(8,128)(2,1)} %get-tuple-element.60.refs_2_), custom_call_target="tpu_custom_call" | custom-call | flops 6442450944 | bytes 1 | tf_op jit(solution)/shard_map/pair_own/pallas_call | solution.py:513
  72.4 3.3 %collective-permute-done.8.refs_3_ = f32[1,512,128]{2,1,0:T(8,128)S(1)} collective-permute-done((f32[1,512,128]{2,1,0:T(8,128)}, f32[1,512,128]{2,1,0:T(8,128)S(1)}, u32[]{:S(2)}, u32[]{:S(2)}) %collective-permute-start.8) | collective-permute-done | bytes 262176 | tf_op jit(solution)/shard_map/ppermute | solution.py:672
  75.7 0.0 collective-permute-done.7.refs_1_
  75.7 0.0 collective-permute-done.10.refs_5_
  75.7 0.0 collective-permute-done.11.refs_6_
  75.7 0.0 collective-permute-done.12.refs_7_
  75.7 2.2 %finish.1 = (f32[16,4,2,16,128]{4,3,2,1,0:T(8,128)}, f32[16,1024]{1,0:T(8,128)}, f32[16,4096]{1,0:T(8,128)}) custom-call(f32[16,4,16,128]{3,2,1,0:T(8,128)S(1)} %pair_own.1.refs_0_, f32[16,4,16,128]{3,2,1,0:T(8,128)S(1)} %collective-permute-done.7.refs_1_, f32[1,512,128]{2,1,0:T(8,128)S(1)} %get-tuple-element.62.refs_1_.refs_2_, ...), custom_call_target="tpu_custom_call" | custom-call | flops 1 | bytes 1 | tf_op jit(solution)/shard_map/finish/pallas_call | solution.py:513
  77.8 0.9 %all-to-all-done.1 = f32[16,32,128]{2,1,0:T(8,128)S(1)} async-done(((f32[16,32,128]{2,1,0:T(8,128)}), f32[16,32,128]{2,1,0:T(8,128)S(1)}, u32[]{:S(2)}, u32[]{:S(2)}) %all-to-all-start.1) | async-done | bytes 262176 | tf_op jit(solution)/shard_map/all_to_all | solution.py:692
  78.7 0.0 collective-permute-start.13
  78.7 1.5 %collective-permute-done.13.refs_1_ = f32[512,128]{1,0:T(8,128)S(1)} collective-permute-done((f32[512,128]{1,0:T(8,128)S(1)}, f32[512,128]{1,0:T(8,128)S(1)}, u32[]{:S(2)}, u32[]{:S(2)}) %collective-permute-start.13) | collective-permute-done | bytes 262176 | tf_op jit(solution)/shard_map/ppermute | solution.py:722
  80.2 1.1 %place.1 = f32[1024,128]{1,0:T(8,128)} custom-call(f32[512,128]{1,0:T(8,128)S(1)} %bitcast.5, f32[512,128]{1,0:T(8,128)S(1)} %collective-permute-done.13.refs_1_), custom_call_target="tpu_custom_call" | custom-call | flops 1 | bytes 1 | tf_op jit(solution)/shard_map/place/pallas_call | solution.py:513
  (1 shorter events, 0.0 us)
Async XLA Ops:
  2.6 15.8 %collective-permute-start = (f32[16,4,16,128]{3,2,1,0:T(8,128)S(1)}, f32[16,4,16,128]{3,2,1,0:T(8,128)S(1)}, u32[]{:S(2)}, u32[]{:S(2)}) collective-permute-start(f32[16,4,16,128]{3,2,1,0:T(8,128)S(1)} %get-tuple-element.45), channel_id=1, source_target_pairs={{0,4},{4,0},{8,12},{12,8},{16,20},{20,16},{24,28},{28,24},{1,5},{5... | collective-permute-start | bytes 1572872 | tf_op jit(solution)/shard_map/ppermute | solution.py:576
  5.6 17.5 %collective-permute-start.1 = (f32[512,128]{1,0:T(8,128)S(1)}, f32[512,128]{1,0:T(8,128)S(1)}, u32[]{:S(2)}, u32[]{:S(2)}) collective-permute-start(f32[512,128]{1,0:T(8,128)S(1)} %get-tuple-element.43.refs_2_.refs_1_), channel_id=1, source_target_pairs={{0,4},{4,0},{8,12},{12,8},{16,20},{20,16},{24,28},{28,24},{1,5},{5... | collective-permute-start | bytes 786440 | tf_op jit(solution)/shard_map/ppermute | solution.py:577
  5.7 22.1 %collective-permute-start.4 = (f32[512,128]{1,0:T(8,128)S(1)}, f32[512,128]{1,0:T(8,128)S(1)}, u32[]{:S(2)}, u32[]{:S(2)}) collective-permute-start(f32[512,128]{1,0:T(8,128)S(1)} %get-tuple-element.51.refs_5_.refs_3_), channel_id=1, source_target_pairs={{0,24},{4,28},{8,16},{12,20},{16,8},{20,12},{24,0},{28,4},{1,25},{... | collective-permute-start | bytes 786440 | tf_op jit(solution)/shard_map/ppermute | solution.py:575
  9.8 21.9 %collective-permute-start.3 = (f32[512,128]{1,0:T(8,128)S(1)}, f32[512,128]{1,0:T(8,128)S(1)}, u32[]{:S(2)}, u32[]{:S(2)}) collective-permute-start(f32[512,128]{1,0:T(8,128)S(1)} %get-tuple-element.51.refs_5_.refs_3_), channel_id=1, source_target_pairs={{0,16},{4,20},{8,24},{12,28},{16,0},{20,4},{24,8},{28,12},{1,17},{... | collective-permute-start | bytes 786440 | tf_op jit(solution)/shard_map/ppermute | solution.py:575
  9.8 21.9 %collective-permute-start.2 = (f32[512,128]{1,0:T(8,128)S(1)}, f32[512,128]{1,0:T(8,128)S(1)}, u32[]{:S(2)}, u32[]{:S(2)}) collective-permute-start(f32[512,128]{1,0:T(8,128)S(1)} %get-tuple-element.51.refs_5_.refs_3_), channel_id=1, source_target_pairs={{0,8},{4,12},{8,0},{12,4},{16,24},{20,28},{24,16},{28,20},{1,9},{5... | collective-permute-start | bytes 786440 | tf_op jit(solution)/shard_map/ppermute | solution.py:575
  26.0 30.3 %collective-permute-start.6 = (f32[2,512,128]{2,1,0:T(8,128)}, f32[2,512,128]{2,1,0:T(8,128)S(1)}, u32[]{:S(2)}, u32[]{:S(2)}) collective-permute-start(f32[2,512,128]{2,1,0:T(8,128)} %get-tuple-element.61), channel_id=1, source_target_pairs={{0,8},{4,12},{8,0},{12,4},{16,24},{20,28},{24,16},{28,20},{1,9},{5... | collective-permute-start | bytes 1572872 | tf_op jit(solution)/shard_map/ppermute | solution.py:615
  39.8 2.9 %collective-permute-start.5 = (f32[512,128]{1,0:T(8,128)S(1)}, f32[512,128]{1,0:T(8,128)S(1)}, u32[]{:S(2)}, u32[]{:S(2)}) collective-permute-start(f32[512,128]{1,0:T(8,128)S(1)} %get-tuple-element.56), channel_id=1, source_target_pairs={{0,1},{1,0},{2,3},{3,2},{4,5},{5,4},{6,7},{7,6},{8,9},{9,8},{10,11... | collective-permute-start | bytes 786440 | tf_op jit(solution)/shard_map/ppermute | solution.py:631
  43.4 16.4 %all-to-all-start = ((f32[16,32,128]{2,1,0:T(8,128)}), f32[16,32,128]{2,1,0:T(8,128)S(1)}, u32[]{:S(2)}, u32[]{:S(2)}) async-start(f32[16,32,128]{2,1,0:T(8,128)} %bitcast.1.refs_0_), calls=%async_computation | async-start | bytes 524288 | tf_op jit(solution)/shard_map/all_to_all | solution.py:678
  49.2 16.1 %collective-permute-start.9 = (f32[4,32,512]{2,1,0:T(8,128)S(1)}, f32[4,32,512]{2,1,0:T(8,128)S(1)}, u32[]{:S(2)}, u32[]{:S(2)}) collective-permute-start(f32[4,32,512]{2,1,0:T(8,128)S(1)} %get-tuple-element.66), channel_id=1, source_target_pairs={{0,4},{4,0},{8,12},{12,8},{16,20},{20,16},{24,28},{28,24},{1,5},{5... | collective-permute-start | bytes 786440 | tf_op jit(solution)/shard_map/ppermute | solution.py:665
  56.1 19.6 %collective-permute-start.7 = (f32[16,4,16,128]{3,2,1,0:T(8,128)S(1)}, f32[16,4,16,128]{3,2,1,0:T(8,128)S(1)}, u32[]{:S(2)}, u32[]{:S(2)}) collective-permute-start(f32[16,4,16,128]{3,2,1,0:T(8,128)S(1)} %pair_peer.1.refs_0_), channel_id=1, source_target_pairs={{0,4},{4,0},{8,12},{12,8},{16,20},{20,16},{24,28},{28,24},{1,5},{5... | collective-permute-start | bytes 1572872 | tf_op jit(solution)/shard_map/ppermute | solution.py:676
  57.1 18.6 %collective-permute-start.8 = (f32[1,512,128]{2,1,0:T(8,128)}, f32[1,512,128]{2,1,0:T(8,128)S(1)}, u32[]{:S(2)}, u32[]{:S(2)}) collective-permute-start(f32[1,512,128]{2,1,0:T(8,128)} %get-tuple-element.64), channel_id=1, source_target_pairs={{0,16},{4,20},{8,24},{12,28},{16,0},{20,4},{24,8},{28,12},{1,17},{... | collective-permute-start | bytes 786440 | tf_op jit(solution)/shard_map/ppermute | solution.py:672
  60.6 18.1 %all-to-all-start.1 = ((f32[16,32,128]{2,1,0:T(8,128)}), f32[16,32,128]{2,1,0:T(8,128)S(1)}, u32[]{:S(2)}, u32[]{:S(2)}) async-start(f32[16,32,128]{2,1,0:T(8,128)} %weight_sum.1.refs_0_), calls=%async_computation.1 | async-start | bytes 524288 | tf_op jit(solution)/shard_map/all_to_all | solution.py:692
  65.3 10.4 %collective-permute-start.10 = (f32[32,512]{1,0:T(8,128)S(1)}, f32[32,512]{1,0:T(8,128)S(1)}, u32[]{:S(2)}, u32[]{:S(2)}) collective-permute-start(f32[32,512]{1,0:T(8,128)S(1)} %get-tuple-element.68), channel_id=1, source_target_pairs={{0,1},{1,0},{2,3},{3,2},{4,5},{5,4},{6,7},{7,6},{8,9},{9,8},{10,11... | collective-permute-start | bytes 196616 | tf_op jit(solution)/shard_map/ppermute | solution.py:695
  65.4 10.3 %collective-permute-start.11 = (f32[32,512]{1,0:T(8,128)S(1)}, f32[32,512]{1,0:T(8,128)S(1)}, u32[]{:S(2)}, u32[]{:S(2)}) collective-permute-start(f32[32,512]{1,0:T(8,128)S(1)} %get-tuple-element.69), channel_id=1, source_target_pairs={{0,2},{1,3},{2,0},{3,1},{4,6},{5,7},{6,4},{7,5},{8,10},{9,11},{10,... | collective-permute-start | bytes 196616 | tf_op jit(solution)/shard_map/ppermute | solution.py:695
  67.3 8.3 %collective-permute-start.12 = (f32[32,512]{1,0:T(8,128)S(1)}, f32[32,512]{1,0:T(8,128)S(1)}, u32[]{:S(2)}, u32[]{:S(2)}) collective-permute-start(f32[32,512]{1,0:T(8,128)S(1)} %get-tuple-element.70), channel_id=1, source_target_pairs={{0,3},{1,2},{2,1},{3,0},{4,7},{5,6},{6,5},{7,4},{8,11},{9,10},{10,... | collective-permute-start | bytes 196616 | tf_op jit(solution)/shard_map/ppermute | solution.py:695
  78.7 1.5 %collective-permute-start.13 = (f32[512,128]{1,0:T(8,128)S(1)}, f32[512,128]{1,0:T(8,128)S(1)}, u32[]{:S(2)}, u32[]{:S(2)}) collective-permute-start(f32[512,128]{1,0:T(8,128)S(1)} %bitcast.4), channel_id=1, source_target_pairs={{0,1},{1,0},{2,3},{3,2},{4,5},{5,4},{6,7},{7,6},{8,9},{9,8},{10,11... | collective-permute-start | bytes 786440 | tf_op jit(solution)/shard_map/ppermute | solution.py:722

commit v16 on v15

--- a/solution.py
+++ b/solution.py
@@ -570,9 +570,6 @@
         name="prepare",
         far=range(4),
     )(by_side, alignment_right, alignment_left, projection_matrix)
-    rights = [right]
-    for slot in range(1, blocks):
-        rights.append(lax.ppermute(right, "blk", slot_moves[slot]))
     cotangent_peer = lax.ppermute(cotangent_send, "blk", partner)
     left_peer = lax.ppermute(left, "blk", partner)
 
@@ -602,6 +599,16 @@
         "gradient_own",
         out_specs=[vmem, vmem, vmem, vmem, hbm],
     )(weight, cotangent_own, left)
+    rights = {0: right}
+    distance = blocks // 2
+    while distance:
+        for slot in list(rights):
+            sent = rights[slot]
+            if slot:
+                sent, _ = lax.optimization_barrier((sent, grad_own))
+            rights[slot + distance] = lax.ppermute(sent, "blk", slot_moves[distance])
+        distance = distance // 2
+    rights = [rights[slot] for slot in range(blocks)]
     grad_peer, spread_peer = large(
         functools.partial(peer_kernel, blocks), [factor, spread], [], "gradient_peer"
     )(weight_cat, cotangent_peer)
@@ -672,7 +679,7 @@
         right_send = lax.ppermute(right_send, "blk", slot_moves[slot])
         slot = 2 * slot
 
-    pair_other = pair(outer_peer, [pieces], "pair_peer")
+    pair_other = pair(outer_peer, [pieces, right_keep], "pair_peer")
     pair_found = lax.ppermute(pair_other, "blk", partner)
 
     pieces = lax.all_to_all(pieces, everyone, 0, 0, axis_index_groups=core_groups)

time: 81.7 us -> 80.6 us (0.987)
  starting transfers between devices: 27 us -> 29.5 us
  waiting for transfers between devices: 14.3 us -> 12.1 us
  Pallas kernels: 38.5 us -> 37 us
    all_to_all x2, waiting for transfers between devices: 0.86 us -> 6.5 us  [local(): lax.all_to_all(pieces, everyone, 0, 0, axis_index_groups=core_groups)]
    ppermute x1, waiting for transfers between devices: 3.28 us -> 0.01 us  [local(): right_send = lax.ppermute(right_send, 'blk', slot_moves[slot])]
    ppermute x1, waiting for transfers between devices: 2.55 us -> 0.01 us  [local(): cotangent_peer = lax.ppermute(cotangent_send, 'blk', partner)]
    ppermute x1, waiting for transfers between devices: 2.33 us -> 0.13 us  [local(): left_peer = lax.ppermute(left, 'blk', partner)]
    pallas_call x13, Pallas kernels: 38.5 us -> 37 us  [run(): pl.pallas_call(lambda *refs: kernel(*refs[len(after):]), out_shape=out_sh...]
    all_to_all x2, starting transfers between devices: 10.4 us -> 11.4 us  [local(): lax.all_to_all(pieces, everyone, 0, 0, axis_index_groups=core_groups)]
    ppermute x1, starting transfers between devices: 0.01 us -> 0.84 us  [local(): other = lax.ppermute(mine, 'inner', cores)]
  transfers between devices with their start and end apart: 16 -> 16, of which waited for: 6 -> 5; matrix products, arithmetic and copies ran while one was open for 1% -> 1% of each run, Pallas kernels for 44% -> 42%
where the time goes in v16:
time: 80.6 us; the launch traced here: 80.2 us
  Pallas kernels  37 us (46%)
  starting transfers between devices  29.5 us (37%)
  waiting for transfers between devices  12.1 us (15%)
  between operations  0.81 us (1%)
    pallas_call x13, Pallas kernels, run(): pl.pallas_call(lambda *refs: kernel(*refs[len(after):]), out_shape=out_sh...  37 us
    all_to_all x2, starting transfers between devices, local(): lax.all_to_all(pieces, everyone, 0, 0, axis_index_groups=core_groups)  11.4 us
    all_to_all x2, waiting for transfers between devices, local(): lax.all_to_all(pieces, everyone, 0, 0, axis_index_groups=core_groups)  6.5 us
    ppermute x3, starting transfers between devices, local(): rights[slot + distance] = lax.ppermute(sent, 'blk', slot_moves[distance])  4.73 us
    ppermute x3, waiting for transfers between devices, local(): rights[slot + distance] = lax.ppermute(sent, 'blk', slot_moves[distance])  4.22 us
    ppermute x1, starting transfers between devices, local(): cotangent_peer = lax.ppermute(cotangent_send, 'blk', partner)  3.03 us
    ppermute x1, starting transfers between devices, local(): right_send = lax.ppermute(right_send, 'blk', slot_moves[slot])  2.4 us
    ppermute x3, starting transfers between devices, local(): lax.ppermute(part, 'inner', inner_moves[slot])  2.13 us
  transfers between devices with their start and end apart: 16, of which 5 were waited for; matrix products, arithmetic and copies ran while one was open for 1% of the time, Pallas kernels for 42%

profile of v16, /device:TPU:0, one launch (start us, length us, event | category | flops | bytes accessed | tf_op | source)
XLA Modules:
  0.0 80.2 jit_solution(10503902349303059837)
XLA Ops:
  0.6 2.0 %prepare.1 = (f32[512,128]{1,0:T(8,128)S(1)}, f32[512,128]{1,0:T(8,128)S(1)}, f32[16,4,16,128]{3,2,1,0:T(8,128)S(1)}, f32[16,4,16,128]{3,2,1,0:T(8,128)S(1)}, f32[1024,128]{1,0:T(8,128)S(1)}) custom-call(f32[16,4,2,16,128]{4,3,2,1,0:T(8,128)} %bitcast.6, f32[16,4096]{1,0:T(8,128)} %refs_1_.1, f32[16,4096]{1,0:T(8,128)} %refs_2_.1, f32[1024,128]{1,0:T(8,128)} %refs_3_.1), custom_call_target="tpu_custom_call" | custom-call | flops 1 | bytes 1 | tf_op jit(solution)/shard_map/prepare/pallas_call | solution.py:513
  2.6 3.0 %collective-permute-start = (f32[16,4,16,128]{3,2,1,0:T(8,128)S(1)}, f32[16,4,16,128]{3,2,1,0:T(8,128)S(1)}, u32[]{:S(2)}, u32[]{:S(2)}) collective-permute-start(f32[16,4,16,128]{3,2,1,0:T(8,128)S(1)} %get-tuple-element.46), channel_id=1, source_target_pairs={{0,4},{4,0},{8,12},{12,8},{16,20},{20,16},{24,28},{28,24},{1,5},{5... | collective-permute-start | bytes 1572872 | tf_op jit(solution)/shard_map/ppermute | solution.py:573
  5.6 2.6 %collective-permute-start.3 = (f32[512,128]{1,0:T(8,128)S(1)}, f32[512,128]{1,0:T(8,128)S(1)}, u32[]{:S(2)}, u32[]{:S(2)}) collective-permute-start(f32[512,128]{1,0:T(8,128)S(1)} %get-tuple-element.52.refs_5_.refs_3_), channel_id=1, source_target_pairs={{0,16},{4,20},{8,24},{12,28},{16,0},{20,4},{24,8},{28,12},{1,17},{... | collective-permute-start | bytes 786440 | tf_op jit(solution)/shard_map/ppermute | solution.py:609
  8.2 1.6 %collective-permute-start.2 = (f32[512,128]{1,0:T(8,128)S(1)}, f32[512,128]{1,0:T(8,128)S(1)}, u32[]{:S(2)}, u32[]{:S(2)}) collective-permute-start(f32[512,128]{1,0:T(8,128)S(1)} %get-tuple-element.52.refs_5_.refs_3_), channel_id=1, source_target_pairs={{0,8},{4,12},{8,0},{12,4},{16,24},{20,28},{24,16},{28,20},{1,9},{5... | collective-permute-start | bytes 786440 | tf_op jit(solution)/shard_map/ppermute | solution.py:609
  9.8 0.5 collective-permute-start.1
  10.3 5.5 %gradient_own.1 = (bf16[8,512,512]{2,1,0:T(8,128)(2,1)S(1)}, bf16[8,2,256,256]{3,2,1,0:T(8,128)(2,1)S(1)}, f32[8,128,256]{2,1,0:T(8,128)S(1)}, bf16[512,768]{1,0:T(8,128)(2,1)S(1)}, bf16[512,512]{1,0:T(8,128)(2,1)}) custom-call(f32[1024,128]{1,0:T(8,128)S(1)} %get-tuple-element.42.refs_0_, f32[16,4,16,128]{3,2,1,0:T(8,128)S(1)} %get-tuple-element.43.refs_1_, ...), custom_call_target="tpu_custom_call" | custom-call | flops 1 | bytes 1 | tf_op jit(solution)/shard_map/gradient_own/pallas_call | solution.py:513
  15.8 4.2 %collective-permute-done.3.refs_7_.refs_5_ = f32[512,128]{1,0:T(8,128)S(1)} collective-permute-done((f32[512,128]{1,0:T(8,128)S(1)}, f32[512,128]{1,0:T(8,128)S(1)}, u32[]{:S(2)}, u32[]{:S(2)}) %collective-permute-start.3) | collective-permute-done | bytes 262176 | tf_op jit(solution)/shard_map/ppermute | solution.py:609
  20.0 0.6 collective-permute-start.4
  20.6 0.0 collective-permute-done.refs_1_
  20.6 2.4 %gradient_peer.1 = (bf16[8,512,512]{2,1,0:T(8,128)(2,1)S(1)}, bf16[8,2,256,256]{3,2,1,0:T(8,128)(2,1)S(1)}) custom-call(bf16[512,768]{1,0:T(8,128)(2,1)S(1)} %get-tuple-element.45.refs_0_, f32[16,4,16,128]{3,2,1,0:T(8,128)S(1)} %collective-permute-done.refs_1_), custom_call_target="tpu_custom_call" | custom-call | flops 1 | bytes 1 | tf_op jit(solution)/shard_map/gradient_peer/pallas_call | solution.py:513
  23.1 0.1 collective-permute-done.1.refs_1_.refs_2_
  23.2 2.0 %right_parts.1 = (f32[2,512,128]{2,1,0:T(8,128)S(1)}, f32[2,512,128]{2,1,0:T(8,128)S(1)}) custom-call(bf16[8,512,512]{2,1,0:T(8,128)(2,1)S(1)} %get-tuple-element.47.refs_0_.refs_2_, f32[512,128]{1,0:T(8,128)S(1)} %collective-permute-done.1.refs_1_.refs_2_, f32[8,128,256]{2,1,0:T(8,128)S(1)} %get-tuple-element.48.refs_2_), custom_call_target="tpu_custom_call" | custom-call | flops 1 | bytes 1 | tf_op jit(solution)/shard_map/right_parts/pallas_call | solution.py:513
  25.2 1.9 %collective-permute-start.6 = (f32[2,512,128]{2,1,0:T(8,128)S(1)}, f32[2,512,128]{2,1,0:T(8,128)S(1)}, u32[]{:S(2)}, u32[]{:S(2)}) collective-permute-start(f32[2,512,128]{2,1,0:T(8,128)S(1)} %get-tuple-element.61), channel_id=1, source_target_pairs={{0,8},{4,12},{8,0},{12,4},{16,24},{20,28},{24,16},{28,20},{1,9},{5... | collective-permute-start | bytes 1572872 | tf_op jit(solution)/shard_map/ppermute | solution.py:622
  27.1 0.0 collective-permute-done.2.refs_6_.refs_4_
  27.1 0.0 collective-permute-done.4.refs_8_.refs_6_
  27.1 8.2 %weight.1 = (f32[512,128]{1,0:T(8,128)S(1)}, f32[512,128]{1,0:T(8,128)S(1)}, bf16[8,512,512]{2,1,0:T(8,128)(2,1)}, bf16[8,512,512]{2,1,0:T(8,128)(2,1)}) custom-call(f32[2,512,128]{2,1,0:T(8,128)S(1)} %get-tuple-element.49.refs_0_.refs_1_, f32[512,128]{1,0:T(8,128)S(1)} %get-tuple-element.44.refs_2_.refs_1_, ...), custom_call_target="tpu_custom_call" | custom-call | flops 12884901888 | bytes 1 | tf_op jit(solution)/shard_map/weight/pallas_call | solution.py:513
  35.3 0.1 collective-permute-start.5
  35.4 2.8 %left_parts.1 = (f32[4,32,512]{2,1,0:T(8,128)S(1)}, f32[4,32,512]{2,1,0:T(8,128)S(1)}) custom-call(f32[512,128]{1,0:T(8,128)S(1)} %get-tuple-element.57.refs_0_, bf16[8,512,512]{2,1,0:T(8,128)(2,1)S(1)} %get-tuple-element.53.refs_1_, bf16[8,512,512]{2,1,0:T(8,128)(2,1)S(1)} %get-tuple-element.47.refs_0_.refs_2_, ...), custom_call_target="tpu_custom_call" | custom-call | flops 6442450944 | bytes 1 | tf_op jit(solution)/shard_map/left_parts/pallas_call | solution.py:513
  38.2 0.0 collective-permute-done.5
  38.2 0.7 add.3
  38.9 7.8 %all-to-all-start = ((f32[16,32,128]{2,1,0:T(8,128)}), f32[16,32,128]{2,1,0:T(8,128)S(1)}, u32[]{:S(2)}, u32[]{:S(2)}) async-start(f32[16,32,128]{2,1,0:T(8,128)} %bitcast.1.refs_0_), calls=%async_computation | async-start | bytes 524288 | tf_op jit(solution)/shard_map/all_to_all | solution.py:685
  46.7 2.0 %collective-permute-start.9 = (f32[4,32,512]{2,1,0:T(8,128)S(1)}, f32[4,32,512]{2,1,0:T(8,128)S(1)}, u32[]{:S(2)}, u32[]{:S(2)}) collective-permute-start(f32[4,32,512]{2,1,0:T(8,128)S(1)} %get-tuple-element.68), channel_id=1, source_target_pairs={{0,4},{4,0},{8,12},{12,8},{16,20},{20,16},{24,28},{28,24},{1,5},{5... | collective-permute-start | bytes 786440 | tf_op jit(solution)/shard_map/ppermute | solution.py:672
  48.7 0.0 collective-permute-done.6.refs_2_
  48.7 0.1 right_halve.1
  48.7 2.4 %collective-permute-start.8 = (f32[1,512,128]{2,1,0:T(8,128)S(1)}, f32[1,512,128]{2,1,0:T(8,128)S(1)}, u32[]{:S(2)}, u32[]{:S(2)}) collective-permute-start(f32[1,512,128]{2,1,0:T(8,128)S(1)} %get-tuple-element.66), channel_id=1, source_target_pairs={{0,16},{4,20},{8,24},{12,28},{16,0},{20,4},{24,8},{28,12},{1,17},{... | collective-permute-start | bytes 786440 | tf_op jit(solution)/shard_map/ppermute | solution.py:679
  51.1 5.0 %pair_peer.1.refs_0_ = f32[16,4,16,128]{3,2,1,0:T(8,128)S(1)} custom-call(f32[16,32,128]{2,1,0:T(8,128)} %bitcast.1.refs_0_, f32[1,512,128]{2,1,0:T(8,128)S(1)} %get-tuple-element.62.refs_1_.refs_2_, bf16[8,512,512]{2,1,0:T(8,128)(2,1)} %get-tuple-element.63.refs_2_, bf16[512,512]{1,0:T(8,128)(2,1)} %get-tuple-element.64.refs_3_.refs_2_), custom_call_target="tpu_custom_call" | custom-call | flops 6442450944 | bytes 1 | tf_op jit(solution)/shard_map/pair_peer/pallas_call | solution.py:513
  56.1 0.6 collective-permute-start.7
  56.7 6.5 %all-to-all-done.refs_2_ = f32[16,32,128]{2,1,0:T(8,128)S(1)} async-done(((f32[16,32,128]{2,1,0:T(8,128)}), f32[16,32,128]{2,1,0:T(8,128)S(1)}, u32[]{:S(2)}, u32[]{:S(2)}) %all-to-all-start) | async-done | bytes 262176 | tf_op jit(solution)/shard_map/all_to_all | solution.py:685
  63.2 0.8 weight_sum.1.refs_0_
  64.0 3.6 %all-to-all-start.1 = ((f32[16,32,128]{2,1,0:T(8,128)}), f32[16,32,128]{2,1,0:T(8,128)S(1)}, u32[]{:S(2)}, u32[]{:S(2)}) async-start(f32[16,32,128]{2,1,0:T(8,128)} %weight_sum.1.refs_0_), calls=%async_computation.1 | async-start | bytes 524288 | tf_op jit(solution)/shard_map/all_to_all | solution.py:699
  67.6 0.0 collective-permute-done.9.refs_2_
  67.6 0.1 collective-permute-start.10
  67.7 2.0 %collective-permute-start.11 = (f32[32,512]{1,0:T(8,128)S(1)}, f32[32,512]{1,0:T(8,128)S(1)}, u32[]{:S(2)}, u32[]{:S(2)}) collective-permute-start(f32[32,512]{1,0:T(8,128)S(1)} %get-tuple-element.71), channel_id=1, source_target_pairs={{0,2},{1,3},{2,0},{3,1},{4,6},{5,7},{6,4},{7,5},{8,10},{9,11},{10,... | collective-permute-start | bytes 196616 | tf_op jit(solution)/shard_map/ppermute | solution.py:702
  69.7 0.1 collective-permute-start.12
  69.8 5.0 %pair_own.1.refs_0_ = f32[16,4,16,128]{3,2,1,0:T(8,128)S(1)} custom-call(f32[16,32,128]{2,1,0:T(8,128)} %weight_sum.1.refs_0_, bf16[8,512,512]{2,1,0:T(8,128)(2,1)} %get-tuple-element.65.refs_1_, bf16[512,512]{1,0:T(8,128)(2,1)} %get-tuple-element.64.refs_3_.refs_2_), custom_call_target="tpu_custom_call" | custom-call | flops 6442450944 | bytes 1 | tf_op jit(solution)/shard_map/pair_own/pallas_call | solution.py:513
  74.7 0.0 collective-permute-done.8.refs_3_
  74.7 0.0 collective-permute-done.10.refs_5_
  74.7 0.0 collective-permute-done.11.refs_6_
  74.8 0.1 collective-permute-done.12.refs_7_
  74.9 0.0 collective-permute-done.7.refs_1_
  74.9 2.2 %finish.1 = (f32[16,4,2,16,128]{4,3,2,1,0:T(8,128)}, f32[16,1024]{1,0:T(8,128)}, f32[16,4096]{1,0:T(8,128)}) custom-call(f32[16,4,16,128]{3,2,1,0:T(8,128)S(1)} %pair_own.1.refs_0_, f32[16,4,16,128]{3,2,1,0:T(8,128)S(1)} %collective-permute-done.7.refs_1_, f32[1,512,128]{2,1,0:T(8,128)S(1)} %get-tuple-element.62.refs_1_.refs_2_, ...), custom_call_target="tpu_custom_call" | custom-call | flops 1 | bytes 1 | tf_op jit(solution)/shard_map/finish/pallas_call | solution.py:513
  77.0 0.0 all-to-all-done.1
  77.0 0.8 %collective-permute-start.13 = (f32[512,128]{1,0:T(8,128)S(1)}, f32[512,128]{1,0:T(8,128)S(1)}, u32[]{:S(2)}, u32[]{:S(2)}) collective-permute-start(f32[512,128]{1,0:T(8,128)S(1)} %bitcast.4), channel_id=1, source_target_pairs={{0,1},{1,0},{2,3},{3,2},{4,5},{5,4},{6,7},{7,6},{8,9},{9,8},{10,11... | collective-permute-start | bytes 786440 | tf_op jit(solution)/shard_map/ppermute | solution.py:729
  77.9 1.2 %collective-permute-done.13.refs_1_ = f32[512,128]{1,0:T(8,128)S(1)} collective-permute-done((f32[512,128]{1,0:T(8,128)S(1)}, f32[512,128]{1,0:T(8,128)S(1)}, u32[]{:S(2)}, u32[]{:S(2)}) %collective-permute-start.13) | collective-permute-done | bytes 262176 | tf_op jit(solution)/shard_map/ppermute | solution.py:729
  79.1 1.1 %place.1 = f32[1024,128]{1,0:T(8,128)} custom-call(f32[512,128]{1,0:T(8,128)S(1)} %bitcast.5, f32[512,128]{1,0:T(8,128)S(1)} %collective-permute-done.13.refs_1_), custom_call_target="tpu_custom_call" | custom-call | flops 1 | bytes 1 | tf_op jit(solution)/shard_map/place/pallas_call | solution.py:513
  (1 shorter events, 0.0 us)
Async XLA Ops:
  2.6 18.0 %collective-permute-start = (f32[16,4,16,128]{3,2,1,0:T(8,128)S(1)}, f32[16,4,16,128]{3,2,1,0:T(8,128)S(1)}, u32[]{:S(2)}, u32[]{:S(2)}) collective-permute-start(f32[16,4,16,128]{3,2,1,0:T(8,128)S(1)} %get-tuple-element.46), channel_id=1, source_target_pairs={{0,4},{4,0},{8,12},{12,8},{16,20},{20,16},{24,28},{28,24},{1,5},{5... | collective-permute-start | bytes 1572872 | tf_op jit(solution)/shard_map/ppermute | solution.py:573
  5.6 14.4 %collective-permute-start.3 = (f32[512,128]{1,0:T(8,128)S(1)}, f32[512,128]{1,0:T(8,128)S(1)}, u32[]{:S(2)}, u32[]{:S(2)}) collective-permute-start(f32[512,128]{1,0:T(8,128)S(1)} %get-tuple-element.52.refs_5_.refs_3_), channel_id=1, source_target_pairs={{0,16},{4,20},{8,24},{12,28},{16,0},{20,4},{24,8},{28,12},{1,17},{... | collective-permute-start | bytes 786440 | tf_op jit(solution)/shard_map/ppermute | solution.py:609
  8.2 18.9 %collective-permute-start.2 = (f32[512,128]{1,0:T(8,128)S(1)}, f32[512,128]{1,0:T(8,128)S(1)}, u32[]{:S(2)}, u32[]{:S(2)}) collective-permute-start(f32[512,128]{1,0:T(8,128)S(1)} %get-tuple-element.52.refs_5_.refs_3_), channel_id=1, source_target_pairs={{0,8},{4,12},{8,0},{12,4},{16,24},{20,28},{24,16},{28,20},{1,9},{5... | collective-permute-start | bytes 786440 | tf_op jit(solution)/shard_map/ppermute | solution.py:609
  9.8 13.4 %collective-permute-start.1 = (f32[512,128]{1,0:T(8,128)S(1)}, f32[512,128]{1,0:T(8,128)S(1)}, u32[]{:S(2)}, u32[]{:S(2)}) collective-permute-start(f32[512,128]{1,0:T(8,128)S(1)} %get-tuple-element.44.refs_2_.refs_1_), channel_id=1, source_target_pairs={{0,4},{4,0},{8,12},{12,8},{16,20},{20,16},{24,28},{28,24},{1,5},{5... | collective-permute-start | bytes 786440 | tf_op jit(solution)/shard_map/ppermute | solution.py:574
  20.0 7.1 %collective-permute-start.4 = (f32[512,128]{1,0:T(8,128)S(1)}, f32[512,128]{1,0:T(8,128)S(1)}, u32[]{:S(2)}, u32[]{:S(2)}) collective-permute-start(f32[512,128]{1,0:T(8,128)S(1)} %collective-permute-done.3.refs_7_.refs_5_), channel_id=1, source_target_pairs={{0,8},{4,12},{8,0},{12,4},{16,24},{20,28},{24,16},{28,20},{1,9},{5... | collective-permute-start | bytes 786440 | tf_op jit(solution)/shard_map/ppermute | solution.py:609
  25.2 23.4 %collective-permute-start.6 = (f32[2,512,128]{2,1,0:T(8,128)S(1)}, f32[2,512,128]{2,1,0:T(8,128)S(1)}, u32[]{:S(2)}, u32[]{:S(2)}) collective-permute-start(f32[2,512,128]{2,1,0:T(8,128)S(1)} %get-tuple-element.61), channel_id=1, source_target_pairs={{0,8},{4,12},{8,0},{12,4},{16,24},{20,28},{24,16},{28,20},{1,9},{5... | collective-permute-start | bytes 1572872 | tf_op jit(solution)/shard_map/ppermute | solution.py:622
  35.3 2.9 %collective-permute-start.5 = (f32[512,128]{1,0:T(8,128)S(1)}, f32[512,128]{1,0:T(8,128)S(1)}, u32[]{:S(2)}, u32[]{:S(2)}) collective-permute-start(f32[512,128]{1,0:T(8,128)S(1)} %get-tuple-element.58), channel_id=1, source_target_pairs={{0,1},{1,0},{2,3},{3,2},{4,5},{5,4},{6,7},{7,6},{8,9},{9,8},{10,11... | collective-permute-start | bytes 786440 | tf_op jit(solution)/shard_map/ppermute | solution.py:638
  38.9 24.3 %all-to-all-start = ((f32[16,32,128]{2,1,0:T(8,128)}), f32[16,32,128]{2,1,0:T(8,128)S(1)}, u32[]{:S(2)}, u32[]{:S(2)}) async-start(f32[16,32,128]{2,1,0:T(8,128)} %bitcast.1.refs_0_), calls=%async_computation | async-start | bytes 524288 | tf_op jit(solution)/shard_map/all_to_all | solution.py:685
  46.7 20.9 %collective-permute-start.9 = (f32[4,32,512]{2,1,0:T(8,128)S(1)}, f32[4,32,512]{2,1,0:T(8,128)S(1)}, u32[]{:S(2)}, u32[]{:S(2)}) collective-permute-start(f32[4,32,512]{2,1,0:T(8,128)S(1)} %get-tuple-element.68), channel_id=1, source_target_pairs={{0,4},{4,0},{8,12},{12,8},{16,20},{20,16},{24,28},{28,24},{1,5},{5... | collective-permute-start | bytes 786440 | tf_op jit(solution)/shard_map/ppermute | solution.py:672
  48.7 26.0 %collective-permute-start.8 = (f32[1,512,128]{2,1,0:T(8,128)S(1)}, f32[1,512,128]{2,1,0:T(8,128)S(1)}, u32[]{:S(2)}, u32[]{:S(2)}) collective-permute-start(f32[1,512,128]{2,1,0:T(8,128)S(1)} %get-tuple-element.66), channel_id=1, source_target_pairs={{0,16},{4,20},{8,24},{12,28},{16,0},{20,4},{24,8},{28,12},{1,17},{... | collective-permute-start | bytes 786440 | tf_op jit(solution)/shard_map/ppermute | solution.py:679
  56.1 18.8 %collective-permute-start.7 = (f32[16,4,16,128]{3,2,1,0:T(8,128)S(1)}, f32[16,4,16,128]{3,2,1,0:T(8,128)S(1)}, u32[]{:S(2)}, u32[]{:S(2)}) collective-permute-start(f32[16,4,16,128]{3,2,1,0:T(8,128)S(1)} %pair_peer.1.refs_0_), channel_id=1, source_target_pairs={{0,4},{4,0},{8,12},{12,8},{16,20},{20,16},{24,28},{28,24},{1,5},{5... | collective-permute-start | bytes 1572872 | tf_op jit(solution)/shard_map/ppermute | solution.py:683
  64.0 13.1 %all-to-all-start.1 = ((f32[16,32,128]{2,1,0:T(8,128)}), f32[16,32,128]{2,1,0:T(8,128)S(1)}, u32[]{:S(2)}, u32[]{:S(2)}) async-start(f32[16,32,128]{2,1,0:T(8,128)} %weight_sum.1.refs_0_), calls=%async_computation.1 | async-start | bytes 524288 | tf_op jit(solution)/shard_map/all_to_all | solution.py:699
  67.6 7.1 %collective-permute-start.10 = (f32[32,512]{1,0:T(8,128)S(1)}, f32[32,512]{1,0:T(8,128)S(1)}, u32[]{:S(2)}, u32[]{:S(2)}) collective-permute-start(f32[32,512]{1,0:T(8,128)S(1)} %get-tuple-element.70), channel_id=1, source_target_pairs={{0,1},{1,0},{2,3},{3,2},{4,5},{5,4},{6,7},{7,6},{8,9},{9,8},{10,11... | collective-permute-start | bytes 196616 | tf_op jit(solution)/shard_map/ppermute | solution.py:702
  67.7 7.0 %collective-permute-start.11 = (f32[32,512]{1,0:T(8,128)S(1)}, f32[32,512]{1,0:T(8,128)S(1)}, u32[]{:S(2)}, u32[]{:S(2)}) collective-permute-start(f32[32,512]{1,0:T(8,128)S(1)} %get-tuple-element.71), channel_id=1, source_target_pairs={{0,2},{1,3},{2,0},{3,1},{4,6},{5,7},{6,4},{7,5},{8,10},{9,11},{10,... | collective-permute-start | bytes 196616 | tf_op jit(solution)/shard_map/ppermute | solution.py:702
  69.7 5.2 %collective-permute-start.12 = (f32[32,512]{1,0:T(8,128)S(1)}, f32[32,512]{1,0:T(8,128)S(1)}, u32[]{:S(2)}, u32[]{:S(2)}) collective-permute-start(f32[32,512]{1,0:T(8,128)S(1)} %get-tuple-element.72), channel_id=1, source_target_pairs={{0,3},{1,2},{2,1},{3,0},{4,7},{5,6},{6,5},{7,4},{8,11},{9,10},{10,... | collective-permute-start | bytes 196616 | tf_op jit(solution)/shard_map/ppermute | solution.py:702
  77.0 2.0 %collective-permute-start.13 = (f32[512,128]{1,0:T(8,128)S(1)}, f32[512,128]{1,0:T(8,128)S(1)}, u32[]{:S(2)}, u32[]{:S(2)}) collective-permute-start(f32[512,128]{1,0:T(8,128)S(1)} %bitcast.4), channel_id=1, source_target_pairs={{0,1},{1,0},{2,3},{3,2},{4,5},{5,4},{6,7},{7,6},{8,9},{9,8},{10,11... | collective-permute-start | bytes 786440 | tf_op jit(solution)/shard_map/ppermute | solution.py:729

commit v17 on v16

--- a/solution.py
+++ b/solution.py
@@ -129,7 +129,7 @@
     channels = ENTRY_CHANNELS
     rows, features = out_ref.shape
     count = features // LANES
-    total[...] = functools.reduce(jnp.add, [ref[0] for ref in part_refs])
+    total[...] = functools.reduce(jnp.add, [ref[...] for ref in part_refs])
     for group in range(rows // PACK):
         stacked = [total[strided(group * PACK + k, channels, rows), :] for k in range(PACK)]
         square[group] = jnp.concatenate(stacked, 0).T
@@ -269,9 +269,8 @@
     return jnp.concatenate([ref[...] for ref in left_refs], 0) * (1.0 / sequences)
 
 
-def right_kernel(
-    blocks, depth, peer_ref, left_ref, partial_ref, keep_ref, send_ref, left_flip
-):
+def right_kernel(blocks, depth, peer_ref, left_ref, partial_ref, *refs):
+    out_refs, left_flip = refs[:blocks], refs[blocks]
     fold = fold_of(blocks * depth)
     lanes = fold * blocks * depth
 
@@ -283,16 +282,9 @@
                 for slot in range(blocks):
                     start = (place * blocks + slot) * depth
                     row = pl.multiple_of(((2 * step + part) * fold + place) * depth, depth)
-                    out_ref = send_ref if slot % 2 else keep_ref
-                    out_ref[slot // 2, pl.ds(row, depth), :] = turned[start : start + depth]
+                    out_refs[slot][pl.ds(row, depth), :] = turned[start : start + depth]
 
     right_phase(left_ref, peer_ref, left_flip, store)
-
-
-def halve_kernel(keep_ref, found_ref, keep_out, send_out):
-    for slot in range(keep_ref.shape[0]):
-        out_ref = send_out if slot % 2 else keep_out
-        out_ref[slot // 2] = keep_ref[slot] + found_ref[slot]
 
 
 def right_rows(right_refs, step, fold, depth):
@@ -450,8 +442,8 @@
     lax.fori_loop(0, count, step_of, 0)
 
 
-def finish_kernel(own_ref, other_ref, keep_ref, found_ref, *refs):
-    left_refs, refs = refs[:-9], refs[-9:]
+def finish_kernel(blocks, own_ref, other_ref, *refs):
+    right_refs, left_refs, refs = refs[:blocks], refs[blocks:-9], refs[-9:]
     pair_hbm, left_out, right_out = refs[:3]
     right_total, right_square, right_tiles, left_total, left_tiles, semaphores = refs[3:]
     parity = lax.rem(lax.axis_index("blk"), 2)
@@ -461,7 +453,7 @@
     ]
     for copy in copies:
         copy.start()
-    turn_right([keep_ref, found_ref], right_out, right_total, right_square, right_tiles)
+    turn_right(right_refs, right_out, right_total, right_square, right_tiles)
     turn_left(left_refs, left_out, left_total, left_tiles)
     for copy in copies:
         copy.wait()
@@ -612,14 +604,16 @@
     grad_peer, spread_peer = large(
         functools.partial(peer_kernel, blocks), [factor, spread], [], "gradient_peer"
     )(weight_cat, cotangent_peer)
-    right_half = shape(blocks // 2, channels * depth, sequences)
-    right_keep, right_send = large(
+    right_parts = large(
         functools.partial(right_kernel, blocks, depth),
-        [right_half, right_half],
+        [shape(channels * depth, sequences)] * blocks,
         [flip_scratch],
         "right_parts",
     )(grad_peer, left_peer, partial)
-    right_send = lax.ppermute(right_send, "blk", slot_moves[1])
+    right_found = [
+        lax.ppermute(part, "blk", slot_moves[slot]) if slot else part
+        for slot, part in enumerate(right_parts)
+    ]
 
     keep, send, outer_own, outer_peer = large(
         functools.partial(weight_kernel, blocks, depth),
@@ -631,7 +625,7 @@
             pltpu.SemaphoreType.DMA((steps // 2, 2)),
         ],
         "weight",
-        after=[right_keep],
+        after=[right_parts[0]],
         flops=2 * work,
         out_specs=[vmem, vmem, hbm, hbm],
     )(left, left_peer, spread_own, spread_peer, *rights)
@@ -670,16 +664,7 @@
 
     pieces, left_other = lax.optimization_barrier((pieces, left_other))
     left_other = lax.ppermute(left_other, "blk", partner)
-    slot = 2
-    while slot < blocks:
-        part = shape(blocks // (2 * slot), channels * depth, sequences)
-        right_keep, right_send = call(
-            halve_kernel, [part, part], name="right_halve", after=[pieces]
-        )(right_keep, right_send)
-        right_send = lax.ppermute(right_send, "blk", slot_moves[slot])
-        slot = 2 * slot
-
-    pair_other = pair(outer_peer, [pieces, right_keep], "pair_peer")
+    pair_other = pair(outer_peer, [pieces], "pair_peer")
     pair_found = lax.ppermute(pair_other, "blk", partner)
 
     pieces = lax.all_to_all(pieces, everyone, 0, 0, axis_index_groups=core_groups)
@@ -687,7 +672,7 @@
         spread_sum_kernel,
         shape(*pieces.shape),
         name="weight_sum",
-        after=[pair_other, right_keep],
+        after=[pair_other],
     )(pieces)
     pair_own = pair(outer_own, [pieces], "pair_own")
     left_found = call(
@@ -703,7 +688,7 @@
         for slot, part in enumerate(left_found)
     ]
     pair_update, grad_left, grad_right = call(
-        finish_kernel,
+        functools.partial(finish_kernel, blocks),
         [
             pltpu.HBM(by_side.shape, F32),
             shape(rows, features // inner),
@@ -719,7 +704,7 @@
         ],
         "finish",
         out_specs=[hbm, vmem, vmem],
-    )(pair_own, pair_found, right_keep, right_send, *left_found)
+    )(pair_own, pair_found, *right_found, *left_found)
     pair_update = pair_update.reshape(cotangent.shape)
 
     pieces, pair_update, grad_left, grad_right = lax.optimization_barrier(

time: 80.6 us -> 80.5 us (level)
  Pallas kernels: 37 us -> 38.4 us
    all_to_all x2, waiting for transfers between devices: 6.5 us -> 3.52 us  [local(): lax.all_to_all(pieces, everyone, 0, 0, axis_index_groups=core_groups)]
    ppermute x1, waiting for transfers between devices: 0.01 us -> 2.12 us  [local(): pair_found = lax.ppermute(pair_other, 'blk', partner)]
    pallas_call x13 -> x12, Pallas kernels: 37 us -> 38.4 us  [run(): pl.pallas_call(lambda *refs: kernel(*refs[len(after):]), out_shape=out_sh...]
    ppermute x2 -> x3, starting transfers between devices: 4.27 us -> 4.74 us  [local(): lax.ppermute(part, 'blk', slot_moves[slot])]
  transfers between devices with their start and end apart: 16 -> 17, of which waited for: 5 -> 5; matrix products, arithmetic and copies ran while one was open for 1% -> 1% of each run, Pallas kernels for 42% -> 44%
where the time goes in v17:
time: 80.5 us; the launch traced here: 80.1 us
  Pallas kernels  38.4 us (48%)
  starting transfers between devices  28.7 us (36%)
  waiting for transfers between devices  11.5 us (14%)
    pallas_call x12, Pallas kernels, run(): pl.pallas_call(lambda *refs: kernel(*refs[len(after):]), out_shape=out_sh...  38.4 us
    all_to_all x2, starting transfers between devices, local(): lax.all_to_all(pieces, everyone, 0, 0, axis_index_groups=core_groups)  11.2 us
    ppermute x3, starting transfers between devices, local(): lax.ppermute(part, 'blk', slot_moves[slot])  4.74 us
    ppermute x3, starting transfers between devices, local(): rights[slot + distance] = lax.ppermute(sent, 'blk', slot_moves[distance])  4.73 us
    ppermute x3, waiting for transfers between devices, local(): rights[slot + distance] = lax.ppermute(sent, 'blk', slot_moves[distance])  4.19 us
    all_to_all x2, waiting for transfers between devices, local(): lax.all_to_all(pieces, everyone, 0, 0, axis_index_groups=core_groups)  3.52 us
    ppermute x1, starting transfers between devices, local(): cotangent_peer = lax.ppermute(cotangent_send, 'blk', partner)  3.03 us
    ppermute x3, starting transfers between devices, local(): lax.ppermute(part, 'inner', inner_moves[slot])  2.16 us
  transfers between devices with their start and end apart: 17, of which 5 were waited for; matrix products, arithmetic and copies ran while one was open for 1% of the time, Pallas kernels for 44%

profile of v17, /device:TPU:0, one launch (start us, length us, event | category | flops | bytes accessed | tf_op | source)
XLA Modules:
  0.0 80.1 jit_solution(5036295072637761621)
XLA Ops:
  0.6 2.0 %prepare.1 = (f32[512,128]{1,0:T(8,128)S(1)}, f32[512,128]{1,0:T(8,128)S(1)}, f32[16,4,16,128]{3,2,1,0:T(8,128)S(1)}, f32[16,4,16,128]{3,2,1,0:T(8,128)S(1)}, f32[1024,128]{1,0:T(8,128)S(1)}) custom-call(f32[16,4,2,16,128]{4,3,2,1,0:T(8,128)} %bitcast.6, f32[16,4096]{1,0:T(8,128)} %refs_1_.1, f32[16,4096]{1,0:T(8,128)} %refs_2_.1, f32[1024,128]{1,0:T(8,128)} %refs_3_.1), custom_call_target="tpu_custom_call" | custom-call | flops 1 | bytes 1 | tf_op jit(solution)/shard_map/prepare/pallas_call | solution.py:505
  2.6 3.0 %collective-permute-start = (f32[16,4,16,128]{3,2,1,0:T(8,128)S(1)}, f32[16,4,16,128]{3,2,1,0:T(8,128)S(1)}, u32[]{:S(2)}, u32[]{:S(2)}) collective-permute-start(f32[16,4,16,128]{3,2,1,0:T(8,128)S(1)} %get-tuple-element.46), channel_id=1, source_target_pairs={{0,4},{4,0},{8,12},{12,8},{16,20},{20,16},{24,28},{28,24},{1,5},{5... | collective-permute-start | bytes 1572872 | tf_op jit(solution)/shard_map/ppermute | solution.py:565
  5.6 2.6 %collective-permute-start.3 = (f32[512,128]{1,0:T(8,128)S(1)}, f32[512,128]{1,0:T(8,128)S(1)}, u32[]{:S(2)}, u32[]{:S(2)}) collective-permute-start(f32[512,128]{1,0:T(8,128)S(1)} %get-tuple-element.52.refs_5_.refs_3_), channel_id=1, source_target_pairs={{0,16},{4,20},{8,24},{12,28},{16,0},{20,4},{24,8},{28,12},{1,17},{... | collective-permute-start | bytes 786440 | tf_op jit(solution)/shard_map/ppermute | solution.py:601
  8.2 0.5 collective-permute-start.1
  8.7 1.6 %collective-permute-start.2 = (f32[512,128]{1,0:T(8,128)S(1)}, f32[512,128]{1,0:T(8,128)S(1)}, u32[]{:S(2)}, u32[]{:S(2)}) collective-permute-start(f32[512,128]{1,0:T(8,128)S(1)} %get-tuple-element.52.refs_5_.refs_3_), channel_id=1, source_target_pairs={{0,8},{4,12},{8,0},{12,4},{16,24},{20,28},{24,16},{28,20},{1,9},{5... | collective-permute-start | bytes 786440 | tf_op jit(solution)/shard_map/ppermute | solution.py:601
  10.3 5.5 %gradient_own.1 = (bf16[8,512,512]{2,1,0:T(8,128)(2,1)S(1)}, bf16[8,2,256,256]{3,2,1,0:T(8,128)(2,1)S(1)}, f32[8,128,256]{2,1,0:T(8,128)S(1)}, bf16[512,768]{1,0:T(8,128)(2,1)S(1)}, bf16[512,512]{1,0:T(8,128)(2,1)}) custom-call(f32[1024,128]{1,0:T(8,128)S(1)} %get-tuple-element.42.refs_0_, f32[16,4,16,128]{3,2,1,0:T(8,128)S(1)} %get-tuple-element.43.refs_1_, ...), custom_call_target="tpu_custom_call" | custom-call | flops 1 | bytes 1 | tf_op jit(solution)/shard_map/gradient_own/pallas_call | solution.py:505
  15.8 4.2 %collective-permute-done.3.refs_7_.refs_5_ = f32[512,128]{1,0:T(8,128)S(1)} collective-permute-done((f32[512,128]{1,0:T(8,128)S(1)}, f32[512,128]{1,0:T(8,128)S(1)}, u32[]{:S(2)}, u32[]{:S(2)}) %collective-permute-start.3) | collective-permute-done | bytes 262176 | tf_op jit(solution)/shard_map/ppermute | solution.py:601
  20.0 0.6 collective-permute-start.4
  20.6 0.0 collective-permute-done.refs_1_
  20.6 2.5 %gradient_peer.1 = (bf16[8,512,512]{2,1,0:T(8,128)(2,1)S(1)}, bf16[8,2,256,256]{3,2,1,0:T(8,128)(2,1)S(1)}) custom-call(bf16[512,768]{1,0:T(8,128)(2,1)S(1)} %get-tuple-element.45.refs_0_, f32[16,4,16,128]{3,2,1,0:T(8,128)S(1)} %collective-permute-done.refs_1_), custom_call_target="tpu_custom_call" | custom-call | flops 1 | bytes 1 | tf_op jit(solution)/shard_map/gradient_peer/pallas_call | solution.py:505
  23.1 0.1 collective-permute-done.1.refs_1_.refs_2_
  23.2 2.7 %right_parts.1 = (f32[512,128]{1,0:T(8,128)S(1)}, f32[512,128]{1,0:T(8,128)}, f32[512,128]{1,0:T(8,128)S(1)}, f32[512,128]{1,0:T(8,128)S(1)}) custom-call(bf16[8,512,512]{2,1,0:T(8,128)(2,1)S(1)} %get-tuple-element.47.refs_0_.refs_2_, f32[512,128]{1,0:T(8,128)S(1)} %collective-permute-done.1.refs_1_.refs_2_, f32[8,128,256]{2,1,0:T(8,128)S(1)} %get-tuple-element.48.refs_2_), custom_call_target="tpu_custom_call" | custom-call | flops 1 | bytes 1 | tf_op jit(solution)/shard_map/right_parts/pallas_call | solution.py:505
  25.9 1.8 %collective-permute-start.7 = (f32[512,128]{1,0:T(8,128)}, f32[512,128]{1,0:T(8,128)S(1)}, u32[]{:S(2)}, u32[]{:S(2)}) collective-permute-start(f32[512,128]{1,0:T(8,128)} %get-tuple-element.64), channel_id=1, source_target_pairs={{0,8},{4,12},{8,0},{12,4},{16,24},{20,28},{24,16},{28,20},{1,9},{5... | collective-permute-start | bytes 786440 | tf_op jit(solution)/shard_map/ppermute | solution.py:614
  27.7 2.6 %collective-permute-start.8 = (f32[512,128]{1,0:T(8,128)S(1)}, f32[512,128]{1,0:T(8,128)S(1)}, u32[]{:S(2)}, u32[]{:S(2)}) collective-permute-start(f32[512,128]{1,0:T(8,128)S(1)} %get-tuple-element.65), channel_id=1, source_target_pairs={{0,16},{4,20},{8,24},{12,28},{16,0},{20,4},{24,8},{28,12},{1,17},{... | collective-permute-start | bytes 786440 | tf_op jit(solution)/shard_map/ppermute | solution.py:614
  30.3 0.4 collective-permute-start.9
  30.7 0.0 collective-permute-done.2.refs_6_.refs_4_
  30.7 0.0 collective-permute-done.4.refs_8_.refs_6_
  30.7 8.2 %weight.1 = (f32[512,128]{1,0:T(8,128)S(1)}, f32[512,128]{1,0:T(8,128)S(1)}, bf16[8,512,512]{2,1,0:T(8,128)(2,1)}, bf16[8,512,512]{2,1,0:T(8,128)(2,1)}) custom-call(f32[512,128]{1,0:T(8,128)S(1)} %get-tuple-element.49.refs_0_.refs_2_, f32[512,128]{1,0:T(8,128)S(1)} %get-tuple-element.44.refs_2_.refs_1_, ...), custom_call_target="tpu_custom_call" | custom-call | flops 12884901888 | bytes 1 | tf_op jit(solution)/shard_map/weight/pallas_call | solution.py:505
  38.9 0.1 collective-permute-start.5
  39.0 3.5 %left_parts.1 = (f32[4,32,512]{2,1,0:T(8,128)S(1)}, f32[4,32,512]{2,1,0:T(8,128)}) custom-call(f32[512,128]{1,0:T(8,128)S(1)} %get-tuple-element.57.refs_0_, bf16[8,512,512]{2,1,0:T(8,128)(2,1)S(1)} %get-tuple-element.53.refs_1_, bf16[8,512,512]{2,1,0:T(8,128)(2,1)S(1)} %get-tuple-element.47.refs_0_.refs_2_, ...), custom_call_target="tpu_custom_call" | custom-call | flops 6442450944 | bytes 1 | tf_op jit(solution)/shard_map/left_parts/pallas_call | solution.py:505
  42.5 0.0 collective-permute-done.5
  42.5 0.7 add.3
  43.2 6.7 %all-to-all-start = ((f32[16,32,128]{2,1,0:T(8,128)}), f32[16,32,128]{2,1,0:T(8,128)S(1)}, u32[]{:S(2)}, u32[]{:S(2)}) async-start(f32[16,32,128]{2,1,0:T(8,128)} %bitcast.1.refs_0_), calls=%async_computation | async-start | bytes 524288 | tf_op jit(solution)/shard_map/all_to_all | solution.py:670
  49.9 2.0 %collective-permute-start.10 = (f32[4,32,512]{2,1,0:T(8,128)}, f32[4,32,512]{2,1,0:T(8,128)S(1)}, u32[]{:S(2)}, u32[]{:S(2)}) collective-permute-start(f32[4,32,512]{2,1,0:T(8,128)} %get-tuple-element.68), channel_id=1, source_target_pairs={{0,4},{4,0},{8,12},{12,8},{16,20},{20,16},{24,28},{28,24},{1,5},{5... | collective-permute-start | bytes 786440 | tf_op jit(solution)/shard_map/ppermute | solution.py:666
  51.9 5.0 %pair_peer.1.refs_0_ = f32[16,4,16,128]{3,2,1,0:T(8,128)S(1)} custom-call(f32[16,32,128]{2,1,0:T(8,128)} %bitcast.1.refs_0_, bf16[8,512,512]{2,1,0:T(8,128)(2,1)} %get-tuple-element.61.refs_1_, bf16[512,512]{1,0:T(8,128)(2,1)} %get-tuple-element.62.refs_2_), custom_call_target="tpu_custom_call" | custom-call | flops 6442450944 | bytes 1 | tf_op jit(solution)/shard_map/pair_peer/pallas_call | solution.py:505
  56.9 0.2 collective-permute-start.6
  57.1 3.5 %all-to-all-done.refs_1_ = f32[16,32,128]{2,1,0:T(8,128)S(1)} async-done(((f32[16,32,128]{2,1,0:T(8,128)}), f32[16,32,128]{2,1,0:T(8,128)S(1)}, u32[]{:S(2)}, u32[]{:S(2)}) %all-to-all-start) | async-done | bytes 262176 | tf_op jit(solution)/shard_map/all_to_all | solution.py:670
  60.6 0.8 weight_sum.1.refs_0_
  61.3 4.5 %all-to-all-start.1 = ((f32[16,32,128]{2,1,0:T(8,128)}), f32[16,32,128]{2,1,0:T(8,128)S(1)}, u32[]{:S(2)}, u32[]{:S(2)}) async-start(f32[16,32,128]{2,1,0:T(8,128)} %weight_sum.1.refs_0_), calls=%async_computation.1 | async-start | bytes 524288 | tf_op jit(solution)/shard_map/all_to_all | solution.py:684
  65.8 0.0 collective-permute-done.10.refs_2_
  65.9 0.1 collective-permute-start.11
  66.0 0.0 collective-permute-done.7.refs_3_
  66.0 2.0 %collective-permute-start.12 = (f32[32,512]{1,0:T(8,128)S(1)}, f32[32,512]{1,0:T(8,128)S(1)}, u32[]{:S(2)}, u32[]{:S(2)}) collective-permute-start(f32[32,512]{1,0:T(8,128)S(1)} %get-tuple-element.71), channel_id=1, source_target_pairs={{0,2},{1,3},{2,0},{3,1},{4,6},{5,7},{6,4},{7,5},{8,10},{9,11},{10,... | collective-permute-start | bytes 196616 | tf_op jit(solution)/shard_map/ppermute | solution.py:687
  67.9 0.0 collective-permute-done.8.refs_4_
  68.0 0.1 collective-permute-start.13
  68.1 5.0 %pair_own.1.refs_0_ = f32[16,4,16,128]{3,2,1,0:T(8,128)S(1)} custom-call(f32[16,32,128]{2,1,0:T(8,128)} %weight_sum.1.refs_0_, bf16[8,512,512]{2,1,0:T(8,128)(2,1)} %get-tuple-element.63.refs_1_, bf16[512,512]{1,0:T(8,128)(2,1)} %get-tuple-element.62.refs_2_), custom_call_target="tpu_custom_call" | custom-call | flops 6442450944 | bytes 1 | tf_op jit(solution)/shard_map/pair_own/pallas_call | solution.py:505
  73.0 0.0 collective-permute-done.9.refs_5_
  73.0 2.1 %collective-permute-done.6.refs_1_ = f32[16,4,16,128]{3,2,1,0:T(8,128)S(1)} collective-permute-done((f32[16,4,16,128]{3,2,1,0:T(8,128)S(1)}, f32[16,4,16,128]{3,2,1,0:T(8,128)S(1)}, u32[]{:S(2)}, u32[]{:S(2)}) %collective-permute-start.6) | collective-permute-done | bytes 524320 | tf_op jit(solution)/shard_map/ppermute | solution.py:668
  75.2 0.0 collective-permute-done.11.refs_7_
  75.2 0.0 collective-permute-done.12.refs_8_
  75.2 0.0 collective-permute-done.13.refs_9_
  75.2 2.2 %finish.1 = (f32[16,4,2,16,128]{4,3,2,1,0:T(8,128)}, f32[16,1024]{1,0:T(8,128)}, f32[16,4096]{1,0:T(8,128)}) custom-call(f32[16,4,16,128]{3,2,1,0:T(8,128)S(1)} %pair_own.1.refs_0_, f32[16,4,16,128]{3,2,1,0:T(8,128)S(1)} %collective-permute-done.6.refs_1_, f32[512,128]{1,0:T(8,128)S(1)} %get-tuple-element.49.refs_0_.refs_2_, ...), custom_call_target="tpu_custom_call" | custom-call | flops 1 | bytes 1 | tf_op jit(solution)/shard_map/finish/pallas_call | solution.py:505
  77.4 0.0 all-to-all-done.1
  77.4 0.1 collective-permute-start.14
  77.4 1.5 %collective-permute-done.14.refs_1_ = f32[512,128]{1,0:T(8,128)S(1)} collective-permute-done((f32[512,128]{1,0:T(8,128)S(1)}, f32[512,128]{1,0:T(8,128)S(1)}, u32[]{:S(2)}, u32[]{:S(2)}) %collective-permute-start.14) | collective-permute-done | bytes 262176 | tf_op jit(solution)/shard_map/ppermute | solution.py:714
  79.0 1.1 %place.1 = f32[1024,128]{1,0:T(8,128)} custom-call(f32[512,128]{1,0:T(8,128)S(1)} %bitcast.5, f32[512,128]{1,0:T(8,128)S(1)} %collective-permute-done.14.refs_1_), custom_call_target="tpu_custom_call" | custom-call | flops 1 | bytes 1 | tf_op jit(solution)/shard_map/place/pallas_call | solution.py:505
  (1 shorter events, 0.0 us)
Async XLA Ops:
  2.6 18.0 %collective-permute-start = (f32[16,4,16,128]{3,2,1,0:T(8,128)S(1)}, f32[16,4,16,128]{3,2,1,0:T(8,128)S(1)}, u32[]{:S(2)}, u32[]{:S(2)}) collective-permute-start(f32[16,4,16,128]{3,2,1,0:T(8,128)S(1)} %get-tuple-element.46), channel_id=1, source_target_pairs={{0,4},{4,0},{8,12},{12,8},{16,20},{20,16},{24,28},{28,24},{1,5},{5... | collective-permute-start | bytes 1572872 | tf_op jit(solution)/shard_map/ppermute | solution.py:565
  5.6 14.4 %collective-permute-start.3 = (f32[512,128]{1,0:T(8,128)S(1)}, f32[512,128]{1,0:T(8,128)S(1)}, u32[]{:S(2)}, u32[]{:S(2)}) collective-permute-start(f32[512,128]{1,0:T(8,128)S(1)} %get-tuple-element.52.refs_5_.refs_3_), channel_id=1, source_target_pairs={{0,16},{4,20},{8,24},{12,28},{16,0},{20,4},{24,8},{28,12},{1,17},{... | collective-permute-start | bytes 786440 | tf_op jit(solution)/shard_map/ppermute | solution.py:601
  8.2 15.0 %collective-permute-start.1 = (f32[512,128]{1,0:T(8,128)S(1)}, f32[512,128]{1,0:T(8,128)S(1)}, u32[]{:S(2)}, u32[]{:S(2)}) collective-permute-start(f32[512,128]{1,0:T(8,128)S(1)} %get-tuple-element.44.refs_2_.refs_1_), channel_id=1, source_target_pairs={{0,4},{4,0},{8,12},{12,8},{16,20},{20,16},{24,28},{28,24},{1,5},{5... | collective-permute-start | bytes 786440 | tf_op jit(solution)/shard_map/ppermute | solution.py:566
  8.7 21.9 %collective-permute-start.2 = (f32[512,128]{1,0:T(8,128)S(1)}, f32[512,128]{1,0:T(8,128)S(1)}, u32[]{:S(2)}, u32[]{:S(2)}) collective-permute-start(f32[512,128]{1,0:T(8,128)S(1)} %get-tuple-element.52.refs_5_.refs_3_), channel_id=1, source_target_pairs={{0,8},{4,12},{8,0},{12,4},{16,24},{20,28},{24,16},{28,20},{1,9},{5... | collective-permute-start | bytes 786440 | tf_op jit(solution)/shard_map/ppermute | solution.py:601
  20.0 10.6 %collective-permute-start.4 = (f32[512,128]{1,0:T(8,128)S(1)}, f32[512,128]{1,0:T(8,128)S(1)}, u32[]{:S(2)}, u32[]{:S(2)}) collective-permute-start(f32[512,128]{1,0:T(8,128)S(1)} %collective-permute-done.3.refs_7_.refs_5_), channel_id=1, source_target_pairs={{0,8},{4,12},{8,0},{12,4},{16,24},{20,28},{24,16},{28,20},{1,9},{5... | collective-permute-start | bytes 786440 | tf_op jit(solution)/shard_map/ppermute | solution.py:601
  25.9 40.0 %collective-permute-start.7 = (f32[512,128]{1,0:T(8,128)}, f32[512,128]{1,0:T(8,128)S(1)}, u32[]{:S(2)}, u32[]{:S(2)}) collective-permute-start(f32[512,128]{1,0:T(8,128)} %get-tuple-element.64), channel_id=1, source_target_pairs={{0,8},{4,12},{8,0},{12,4},{16,24},{20,28},{24,16},{28,20},{1,9},{5... | collective-permute-start | bytes 786440 | tf_op jit(solution)/shard_map/ppermute | solution.py:614
  27.7 40.2 %collective-permute-start.8 = (f32[512,128]{1,0:T(8,128)S(1)}, f32[512,128]{1,0:T(8,128)S(1)}, u32[]{:S(2)}, u32[]{:S(2)}) collective-permute-start(f32[512,128]{1,0:T(8,128)S(1)} %get-tuple-element.65), channel_id=1, source_target_pairs={{0,16},{4,20},{8,24},{12,28},{16,0},{20,4},{24,8},{28,12},{1,17},{... | collective-permute-start | bytes 786440 | tf_op jit(solution)/shard_map/ppermute | solution.py:614
  30.3 42.7 %collective-permute-start.9 = (f32[512,128]{1,0:T(8,128)S(1)}, f32[512,128]{1,0:T(8,128)S(1)}, u32[]{:S(2)}, u32[]{:S(2)}) collective-permute-start(f32[512,128]{1,0:T(8,128)S(1)} %get-tuple-element.66), channel_id=1, source_target_pairs={{0,24},{4,28},{8,16},{12,20},{16,8},{20,12},{24,0},{28,4},{1,25},{... | collective-permute-start | bytes 786440 | tf_op jit(solution)/shard_map/ppermute | solution.py:614
  38.9 3.6 %collective-permute-start.5 = (f32[512,128]{1,0:T(8,128)S(1)}, f32[512,128]{1,0:T(8,128)S(1)}, u32[]{:S(2)}, u32[]{:S(2)}) collective-permute-start(f32[512,128]{1,0:T(8,128)S(1)} %get-tuple-element.58), channel_id=1, source_target_pairs={{0,1},{1,0},{2,3},{3,2},{4,5},{5,4},{6,7},{7,6},{8,9},{9,8},{10,11... | collective-permute-start | bytes 786440 | tf_op jit(solution)/shard_map/ppermute | solution.py:632
  43.2 17.4 %all-to-all-start = ((f32[16,32,128]{2,1,0:T(8,128)}), f32[16,32,128]{2,1,0:T(8,128)S(1)}, u32[]{:S(2)}, u32[]{:S(2)}) async-start(f32[16,32,128]{2,1,0:T(8,128)} %bitcast.1.refs_0_), calls=%async_computation | async-start | bytes 524288 | tf_op jit(solution)/shard_map/all_to_all | solution.py:670
  49.9 15.9 %collective-permute-start.10 = (f32[4,32,512]{2,1,0:T(8,128)}, f32[4,32,512]{2,1,0:T(8,128)S(1)}, u32[]{:S(2)}, u32[]{:S(2)}) collective-permute-start(f32[4,32,512]{2,1,0:T(8,128)} %get-tuple-element.68), channel_id=1, source_target_pairs={{0,4},{4,0},{8,12},{12,8},{16,20},{20,16},{24,28},{28,24},{1,5},{5... | collective-permute-start | bytes 786440 | tf_op jit(solution)/shard_map/ppermute | solution.py:666
  56.9 18.3 %collective-permute-start.6 = (f32[16,4,16,128]{3,2,1,0:T(8,128)S(1)}, f32[16,4,16,128]{3,2,1,0:T(8,128)S(1)}, u32[]{:S(2)}, u32[]{:S(2)}) collective-permute-start(f32[16,4,16,128]{3,2,1,0:T(8,128)S(1)} %pair_peer.1.refs_0_), channel_id=1, source_target_pairs={{0,4},{4,0},{8,12},{12,8},{16,20},{20,16},{24,28},{28,24},{1,5},{5... | collective-permute-start | bytes 1572872 | tf_op jit(solution)/shard_map/ppermute | solution.py:668
  61.3 16.0 %all-to-all-start.1 = ((f32[16,32,128]{2,1,0:T(8,128)}), f32[16,32,128]{2,1,0:T(8,128)S(1)}, u32[]{:S(2)}, u32[]{:S(2)}) async-start(f32[16,32,128]{2,1,0:T(8,128)} %weight_sum.1.refs_0_), calls=%async_computation.1 | async-start | bytes 524288 | tf_op jit(solution)/shard_map/all_to_all | solution.py:684
  65.9 9.3 %collective-permute-start.11 = (f32[32,512]{1,0:T(8,128)S(1)}, f32[32,512]{1,0:T(8,128)S(1)}, u32[]{:S(2)}, u32[]{:S(2)}) collective-permute-start(f32[32,512]{1,0:T(8,128)S(1)} %get-tuple-element.70), channel_id=1, source_target_pairs={{0,1},{1,0},{2,3},{3,2},{4,5},{5,4},{6,7},{7,6},{8,9},{9,8},{10,11... | collective-permute-start | bytes 196616 | tf_op jit(solution)/shard_map/ppermute | solution.py:687
  66.0 9.2 %collective-permute-start.12 = (f32[32,512]{1,0:T(8,128)S(1)}, f32[32,512]{1,0:T(8,128)S(1)}, u32[]{:S(2)}, u32[]{:S(2)}) collective-permute-start(f32[32,512]{1,0:T(8,128)S(1)} %get-tuple-element.71), channel_id=1, source_target_pairs={{0,2},{1,3},{2,0},{3,1},{4,6},{5,7},{6,4},{7,5},{8,10},{9,11},{10,... | collective-permute-start | bytes 196616 | tf_op jit(solution)/shard_map/ppermute | solution.py:687
  68.0 7.2 %collective-permute-start.13 = (f32[32,512]{1,0:T(8,128)S(1)}, f32[32,512]{1,0:T(8,128)S(1)}, u32[]{:S(2)}, u32[]{:S(2)}) collective-permute-start(f32[32,512]{1,0:T(8,128)S(1)} %get-tuple-element.72), channel_id=1, source_target_pairs={{0,3},{1,2},{2,1},{3,0},{4,7},{5,6},{6,5},{7,4},{8,11},{9,10},{10,... | collective-permute-start | bytes 196616 | tf_op jit(solution)/shard_map/ppermute | solution.py:687
  77.4 1.6 %collective-permute-start.14 = (f32[512,128]{1,0:T(8,128)S(1)}, f32[512,128]{1,0:T(8,128)S(1)}, u32[]{:S(2)}, u32[]{:S(2)}) collective-permute-start(f32[512,128]{1,0:T(8,128)S(1)} %bitcast.4), channel_id=1, source_target_pairs={{0,1},{1,0},{2,3},{3,2},{4,5},{5,4},{6,7},{7,6},{8,9},{9,8},{10,11... | collective-permute-start | bytes 786440 | tf_op jit(solution)/shard_map/ppermute | solution.py:714

commit v18 on v16

--- a/solution.py
+++ b/solution.py
@@ -283,16 +283,19 @@
                 for slot in range(blocks):
                     start = (place * blocks + slot) * depth
                     row = pl.multiple_of(((2 * step + part) * fold + place) * depth, depth)
-                    out_ref = send_ref if slot % 2 else keep_ref
-                    out_ref[slot // 2, pl.ds(row, depth), :] = turned[start : start + depth]
+                    out_ref = keep_ref if slot < blocks // 2 else send_ref
+                    out_ref[slot % (blocks // 2), pl.ds(row, depth), :] = turned[
+                        start : start + depth
+                    ]
 
     right_phase(left_ref, peer_ref, left_flip, store)
 
 
 def halve_kernel(keep_ref, found_ref, keep_out, send_out):
-    for slot in range(keep_ref.shape[0]):
-        out_ref = send_out if slot % 2 else keep_out
-        out_ref[slot // 2] = keep_ref[slot] + found_ref[slot]
+    half = keep_ref.shape[0] // 2
+    for slot in range(half):
+        keep_out[slot] = keep_ref[slot] + found_ref[slot]
+        send_out[slot] = keep_ref[half + slot] + found_ref[half + slot]
 
 
 def right_rows(right_refs, step, fold, depth):
@@ -378,7 +381,7 @@
 
 
 def left_kernel(blocks, depth, own_ref, peer_ref, *refs):
-    right_refs, (own_out, peer_out, total, flipped) = refs[:blocks], refs[blocks:]
+    right_refs, out_refs, (total, flipped) = refs[:blocks], refs[blocks:-2], refs[-2:]
     lanes = own_ref.shape[2] // 4
     fold = lanes // (blocks * depth)
     sequences = right_refs[0].shape[1]
@@ -399,17 +402,18 @@
 
     lax.fori_loop(0, ENTRY_CHANNELS // (fold * group), step_of, 0, unroll=2)
     flipped[...] = total[...].T * (1.0 / sequences)
-    inner, size, width = own_out.shape
     here = lax.axis_index("inner")
-    for slot in range(inner):
+    size, width = out_refs[0].shape[1:]
+    for slot, ref in enumerate(out_refs):
         start = pl.multiple_of(lax.bitwise_xor(here, slot) * size, size)
-        own_out[slot] = flipped[pl.ds(start, size), :width]
-        peer_out[slot] = flipped[pl.ds(start, size), width:]
-
-
-def left_add_kernel(own_ref, other_ref, *out_refs):
-    for slot, ref in enumerate(out_refs):
-        ref[...] = own_ref[slot] + other_ref[slot]
+        for side in range(2):
+            ref[side] = flipped[pl.ds(start, size), side * width : (side + 1) * width]
+
+
+def left_add_kernel(*refs):
+    parts, (own_out, send_out) = refs[:-2], refs[-2:]
+    for side, ref in enumerate((own_out, send_out)):
+        ref[...] = functools.reduce(jnp.add, [part[side] for part in parts])
 
 
 def pair_kernel(blocks, outer_hbm, flip_hbm, out_ref, outer_ref, weight_flip, semaphores):
@@ -619,7 +623,7 @@
         [flip_scratch],
         "right_parts",
     )(grad_peer, left_peer, partial)
-    right_send = lax.ppermute(right_send, "blk", slot_moves[1])
+    right_send = lax.ppermute(right_send, "blk", slot_moves[blocks // 2])
 
     keep, send, outer_own, outer_peer = large(
         functools.partial(weight_kernel, blocks, depth),
@@ -638,9 +642,9 @@
     sent = lax.ppermute(send, "inner", cores)
 
     size = sequences // inner
-    left_own, left_other = large(
+    left_parts = large(
         functools.partial(left_kernel, blocks, depth),
-        [shape(inner, size, rows * channels)] * 2,
+        [shape(2, size, rows * channels)] * inner,
         [
             pltpu.VMEM((2 * rows * channels, sequences), F32),
             pltpu.VMEM((sequences, 2 * rows * channels), F32),
@@ -649,7 +653,7 @@
         after=[keep],
         flops=work,
     )(grad_own, grad_peer, *rights)
-    keep, left_own = lax.optimization_barrier((keep, left_own))
+    keep, *left_parts = lax.optimization_barrier((keep, *left_parts))
     members = count * inner // 2
     pieces = (keep + sent).reshape(members, outer // 2 // members, pairs)
 
@@ -668,18 +672,21 @@
             flops=work,
         )(values, weight_flip)
 
-    pieces, left_other = lax.optimization_barrier((pieces, left_other))
-    left_other = lax.ppermute(left_other, "blk", partner)
-    slot = 2
-    while slot < blocks:
-        part = shape(blocks // (2 * slot), channels * depth, sequences)
+    pieces, *left_parts = lax.optimization_barrier((pieces, *left_parts))
+    left_parts = [
+        lax.ppermute(part, "inner", inner_moves[slot]) if slot else part
+        for slot, part in enumerate(left_parts)
+    ]
+    slot = blocks // 4
+    while slot:
+        part = shape(slot, channels * depth, sequences)
         right_keep, right_send = call(
             halve_kernel, [part, part], name="right_halve", after=[pieces]
         )(right_keep, right_send)
         right_send = lax.ppermute(right_send, "blk", slot_moves[slot])
-        slot = 2 * slot
-
-    pair_other = pair(outer_peer, [pieces, right_keep], "pair_peer")
+        slot = slot // 2
+
+    pair_other = pair(outer_peer, [pieces], "pair_peer")
     pair_found = lax.ppermute(pair_other, "blk", partner)
 
     pieces = lax.all_to_all(pieces, everyone, 0, 0, axis_index_groups=core_groups)
@@ -690,18 +697,12 @@
         after=[pair_other, right_keep],
     )(pieces)
     pair_own = pair(outer_own, [pieces], "pair_own")
-    left_found = call(
-        left_add_kernel,
-        [shape(size, rows * channels)] * inner,
-        name="left_add",
-        after=[pieces],
-    )(left_own, left_other)
+    left_own, left_send = call(
+        left_add_kernel, [shape(size, rows * channels)] * 2, name="left_add", after=[pieces]
+    )(*left_parts)
     pieces = lax.all_to_all(pieces, everyone, 0, 0, axis_index_groups=core_groups)
 
-    left_found = [
-        lax.ppermute(part, "inner", inner_moves[slot]) if slot else part
-        for slot, part in enumerate(left_found)
-    ]
+    left_found = [left_own, lax.ppermute(left_send, "blk", partner)]
     pair_update, grad_left, grad_right = call(
         finish_kernel,
         [

time: 80.6 us -> 77.1 us (0.957)
  waiting for transfers between devices: 12.1 us -> 7.77 us
  Pallas kernels: 37 us -> 38.5 us
    all_to_all x2, waiting for transfers between devices: 6.5 us -> 1.86 us  [local(): lax.all_to_all(pieces, everyone, 0, 0, axis_index_groups=core_groups)]
    pallas_call x13, Pallas kernels: 37 us -> 38.5 us  [run(): pl.pallas_call(lambda *refs: kernel(*refs[len(after):]), out_shape=out_sh...]
    ppermute x2, starting transfers between devices: 3.82 us -> 5.26 us  [the longest x1 3.27 us: local(): right_send = lax.ppermute(right_send, 'blk', slot_moves[blocks // 2])]
    all_to_all x2, starting transfers between devices: 11.4 us -> 9.95 us  [local(): lax.all_to_all(pieces, everyone, 0, 0, axis_index_groups=core_groups)]
    ppermute x1, starting transfers between devices: 0.63 us -> 1.78 us  [local(): pair_found = lax.ppermute(pair_other, 'blk', partner)]
    ppermute x1, starting transfers between devices: 2.4 us -> 1.47 us  [local(): right_send = lax.ppermute(right_send, 'blk', slot_moves[slot])]
    ppermute x1, starting transfers between devices: 0.84 us -> 0.03 us  [local(): other = lax.ppermute(mine, 'inner', cores)]
  transfers between devices with their start and end apart: 16 -> 16, of which waited for: 5 -> 6; matrix products, arithmetic and copies ran while one was open for 1% -> 1% of each run, Pallas kernels for 42% -> 46%
where the time goes in v18:
time: 77.1 us; the launch traced here: 76.7 us
  Pallas kernels  38.5 us (50%)
  starting transfers between devices  28.9 us (37%)
  waiting for transfers between devices  7.77 us (10%)
  between operations  0.79 us (1%)
    pallas_call x13, Pallas kernels, run(): pl.pallas_call(lambda *refs: kernel(*refs[len(after):]), out_shape=out_sh...  38.5 us
    all_to_all x2, starting transfers between devices, local(): lax.all_to_all(pieces, everyone, 0, 0, axis_index_groups=core_groups)  9.95 us
    ppermute x3, starting transfers between devices, local(): rights[slot + distance] = lax.ppermute(sent, 'blk', slot_moves[distance])  4.73 us
    ppermute x3, waiting for transfers between devices, local(): rights[slot + distance] = lax.ppermute(sent, 'blk', slot_moves[distance])  4.19 us
    ppermute x1, starting transfers between devices, local(): right_send = lax.ppermute(right_send, 'blk', slot_moves[blocks // 2])  3.27 us
    ppermute x1, starting transfers between devices, local(): cotangent_peer = lax.ppermute(cotangent_send, 'blk', partner)  3.03 us
    ppermute x3, starting transfers between devices, local(): lax.ppermute(part, 'inner', inner_moves[slot])  2.07 us
    ppermute x1, starting transfers between devices, local(): left_found = [left_own, lax.ppermute(left_send, 'blk', partner)]  1.99 us
  transfers between devices with their start and end apart: 16, of which 6 were waited for; matrix products, arithmetic and copies ran while one was open for 1% of the time, Pallas kernels for 46%

profile of v18, /device:TPU:0, one launch (start us, length us, event | category | flops | bytes accessed | tf_op | source)
XLA Modules:
  0.0 76.7 jit_solution(8126544429261130074)
XLA Ops:
  0.6 2.0 %prepare.1 = (f32[512,128]{1,0:T(8,128)S(1)}, f32[512,128]{1,0:T(8,128)S(1)}, f32[16,4,16,128]{3,2,1,0:T(8,128)S(1)}, f32[16,4,16,128]{3,2,1,0:T(8,128)S(1)}, f32[1024,128]{1,0:T(8,128)S(1)}) custom-call(f32[16,4,2,16,128]{4,3,2,1,0:T(8,128)} %bitcast.6, f32[16,4096]{1,0:T(8,128)} %refs_1_.1, f32[16,4096]{1,0:T(8,128)} %refs_2_.1, f32[1024,128]{1,0:T(8,128)} %refs_3_.1), custom_call_target="tpu_custom_call" | custom-call | flops 1 | bytes 1 | tf_op jit(solution)/shard_map/prepare/pallas_call | solution.py:517
  2.6 3.0 %collective-permute-start = (f32[16,4,16,128]{3,2,1,0:T(8,128)S(1)}, f32[16,4,16,128]{3,2,1,0:T(8,128)S(1)}, u32[]{:S(2)}, u32[]{:S(2)}) collective-permute-start(f32[16,4,16,128]{3,2,1,0:T(8,128)S(1)} %get-tuple-element.52), channel_id=1, source_target_pairs={{0,4},{4,0},{8,12},{12,8},{16,20},{20,16},{24,28},{28,24},{1,5},{5... | collective-permute-start | bytes 1572872 | tf_op jit(solution)/shard_map/ppermute | solution.py:577
  5.6 2.6 %collective-permute-start.3 = (f32[512,128]{1,0:T(8,128)S(1)}, f32[512,128]{1,0:T(8,128)S(1)}, u32[]{:S(2)}, u32[]{:S(2)}) collective-permute-start(f32[512,128]{1,0:T(8,128)S(1)} %get-tuple-element.58.refs_5_.refs_3_), channel_id=1, source_target_pairs={{0,16},{4,20},{8,24},{12,28},{16,0},{20,4},{24,8},{28,12},{1,17},{... | collective-permute-start | bytes 786440 | tf_op jit(solution)/shard_map/ppermute | solution.py:613
  8.2 1.6 %collective-permute-start.2 = (f32[512,128]{1,0:T(8,128)S(1)}, f32[512,128]{1,0:T(8,128)S(1)}, u32[]{:S(2)}, u32[]{:S(2)}) collective-permute-start(f32[512,128]{1,0:T(8,128)S(1)} %get-tuple-element.58.refs_5_.refs_3_), channel_id=1, source_target_pairs={{0,8},{4,12},{8,0},{12,4},{16,24},{20,28},{24,16},{28,20},{1,9},{5... | collective-permute-start | bytes 786440 | tf_op jit(solution)/shard_map/ppermute | solution.py:613
  9.8 0.5 collective-permute-start.1
  10.3 5.5 %gradient_own.1 = (bf16[8,512,512]{2,1,0:T(8,128)(2,1)S(1)}, bf16[8,2,256,256]{3,2,1,0:T(8,128)(2,1)S(1)}, f32[8,128,256]{2,1,0:T(8,128)S(1)}, bf16[512,768]{1,0:T(8,128)(2,1)S(1)}, bf16[512,512]{1,0:T(8,128)(2,1)}) custom-call(f32[1024,128]{1,0:T(8,128)S(1)} %get-tuple-element.48.refs_0_, f32[16,4,16,128]{3,2,1,0:T(8,128)S(1)} %get-tuple-element.49.refs_1_, ...), custom_call_target="tpu_custom_call" | custom-call | flops 1 | bytes 1 | tf_op jit(solution)/shard_map/gradient_own/pallas_call | solution.py:517
  15.8 4.2 %collective-permute-done.3.refs_7_.refs_5_ = f32[512,128]{1,0:T(8,128)S(1)} collective-permute-done((f32[512,128]{1,0:T(8,128)S(1)}, f32[512,128]{1,0:T(8,128)S(1)}, u32[]{:S(2)}, u32[]{:S(2)}) %collective-permute-start.3) | collective-permute-done | bytes 262176 | tf_op jit(solution)/shard_map/ppermute | solution.py:613
  20.0 0.6 collective-permute-start.4
  20.6 0.0 collective-permute-done.refs_1_
  20.6 2.5 %gradient_peer.1 = (bf16[8,512,512]{2,1,0:T(8,128)(2,1)S(1)}, bf16[8,2,256,256]{3,2,1,0:T(8,128)(2,1)S(1)}) custom-call(bf16[512,768]{1,0:T(8,128)(2,1)S(1)} %get-tuple-element.51.refs_0_, f32[16,4,16,128]{3,2,1,0:T(8,128)S(1)} %collective-permute-done.refs_1_), custom_call_target="tpu_custom_call" | custom-call | flops 1 | bytes 1 | tf_op jit(solution)/shard_map/gradient_peer/pallas_call | solution.py:517
  23.1 0.1 collective-permute-done.1.refs_1_.refs_2_
  23.2 2.8 %right_parts.1 = (f32[2,512,128]{2,1,0:T(8,128)S(1)}, f32[2,512,128]{2,1,0:T(8,128)}) custom-call(bf16[8,512,512]{2,1,0:T(8,128)(2,1)S(1)} %get-tuple-element.53.refs_0_.refs_2_, f32[512,128]{1,0:T(8,128)S(1)} %collective-permute-done.1.refs_1_.refs_2_, f32[8,128,256]{2,1,0:T(8,128)S(1)} %get-tuple-element.54.refs_2_), custom_call_target="tpu_custom_call" | custom-call | flops 1 | bytes 1 | tf_op jit(solution)/shard_map/right_parts/pallas_call | solution.py:517
  26.0 3.3 %collective-permute-start.6 = (f32[2,512,128]{2,1,0:T(8,128)}, f32[2,512,128]{2,1,0:T(8,128)S(1)}, u32[]{:S(2)}, u32[]{:S(2)}) collective-permute-start(f32[2,512,128]{2,1,0:T(8,128)} %get-tuple-element.75), channel_id=1, source_target_pairs={{0,16},{4,20},{8,24},{12,28},{16,0},{20,4},{24,8},{28,12},{1,17},{... | collective-permute-start | bytes 1572872 | tf_op jit(solution)/shard_map/ppermute | solution.py:626
  29.3 0.0 collective-permute-done.2.refs_6_.refs_4_
  29.3 0.0 collective-permute-done.4.refs_8_.refs_6_
  29.3 8.2 %weight.1 = (f32[512,128]{1,0:T(8,128)S(1)}, f32[512,128]{1,0:T(8,128)S(1)}, bf16[8,512,512]{2,1,0:T(8,128)(2,1)}, bf16[8,512,512]{2,1,0:T(8,128)(2,1)}) custom-call(f32[2,512,128]{2,1,0:T(8,128)S(1)} %get-tuple-element.55.refs_0_.refs_1_, f32[512,128]{1,0:T(8,128)S(1)} %get-tuple-element.50.refs_2_.refs_1_, ...), custom_call_target="tpu_custom_call" | custom-call | flops 12884901888 | bytes 1 | tf_op jit(solution)/shard_map/weight/pallas_call | solution.py:517
  37.5 0.1 collective-permute-start.5
  37.6 3.5 %left_parts.1 = (f32[2,32,512]{2,1,0:T(8,128)S(1)}, f32[2,32,512]{2,1,0:T(8,128)}, f32[2,32,512]{2,1,0:T(8,128)}, f32[2,32,512]{2,1,0:T(8,128)S(1)}) custom-call(f32[512,128]{1,0:T(8,128)S(1)} %get-tuple-element.66.refs_0_, bf16[8,512,512]{2,1,0:T(8,128)(2,1)S(1)} %get-tuple-element.59.refs_1_, bf16[8,512,512]{2,1,0:T(8,128)(2,1)S(1)} %get-tuple-element.53.refs_0_.refs_2_, ...), custom_call_target="tpu_custom_call" | custom-call | flops 6442450944 | bytes 1 | tf_op jit(solution)/shard_map/left_parts/pallas_call | solution.py:517
  41.1 0.0 collective-permute-done.5
  41.1 0.7 add.3
  41.8 4.6 %all-to-all-start = ((f32[16,32,128]{2,1,0:T(8,128)}), f32[16,32,128]{2,1,0:T(8,128)S(1)}, u32[]{:S(2)}, u32[]{:S(2)}) async-start(f32[16,32,128]{2,1,0:T(8,128)} %bitcast.1.refs_0_), calls=%async_computation | async-start | bytes 524288 | tf_op jit(solution)/shard_map/all_to_all | solution.py:692
  46.5 0.3 collective-permute-start.9
  46.7 1.7 %collective-permute-start.10 = (f32[2,32,512]{2,1,0:T(8,128)}, f32[2,32,512]{2,1,0:T(8,128)S(1)}, u32[]{:S(2)}, u32[]{:S(2)}) collective-permute-start(f32[2,32,512]{2,1,0:T(8,128)} %get-tuple-element.81), channel_id=1, source_target_pairs={{0,2},{1,3},{2,0},{3,1},{4,6},{5,7},{6,4},{7,5},{8,10},{9,11},{10,... | collective-permute-start | bytes 393224 | tf_op jit(solution)/shard_map/ppermute | solution.py:677
  48.5 0.1 collective-permute-start.11
  48.5 5.0 %pair_peer.1.refs_0_ = f32[16,4,16,128]{3,2,1,0:T(8,128)S(1)} custom-call(f32[16,32,128]{2,1,0:T(8,128)} %bitcast.1.refs_0_, bf16[8,512,512]{2,1,0:T(8,128)(2,1)} %get-tuple-element.73.refs_1_, bf16[512,512]{1,0:T(8,128)(2,1)} %get-tuple-element.74.refs_2_), custom_call_target="tpu_custom_call" | custom-call | flops 6442450944 | bytes 1 | tf_op jit(solution)/shard_map/pair_peer/pallas_call | solution.py:517
  53.5 1.8 %collective-permute-start.7 = (f32[16,4,16,128]{3,2,1,0:T(8,128)S(1)}, f32[16,4,16,128]{3,2,1,0:T(8,128)S(1)}, u32[]{:S(2)}, u32[]{:S(2)}) collective-permute-start(f32[16,4,16,128]{3,2,1,0:T(8,128)S(1)} %pair_peer.1.refs_0_), channel_id=1, source_target_pairs={{0,4},{4,0},{8,12},{12,8},{16,20},{20,16},{24,28},{28,24},{1,5},{5... | collective-permute-start | bytes 1572872 | tf_op jit(solution)/shard_map/ppermute | solution.py:690
  55.3 0.1 collective-permute-done.6.refs_2_
  55.3 0.1 right_halve.1
  55.4 1.5 %collective-permute-start.8 = (f32[1,512,128]{2,1,0:T(8,128)S(1)}, f32[1,512,128]{2,1,0:T(8,128)S(1)}, u32[]{:S(2)}, u32[]{:S(2)}) collective-permute-start(f32[1,512,128]{2,1,0:T(8,128)S(1)} %get-tuple-element.78), channel_id=1, source_target_pairs={{0,8},{4,12},{8,0},{12,4},{16,24},{20,28},{24,16},{28,20},{1,9},{5... | collective-permute-start | bytes 786440 | tf_op jit(solution)/shard_map/ppermute | solution.py:686
  56.9 1.8 %all-to-all-done.refs_2_ = f32[16,32,128]{2,1,0:T(8,128)S(1)} async-done(((f32[16,32,128]{2,1,0:T(8,128)}), f32[16,32,128]{2,1,0:T(8,128)S(1)}, u32[]{:S(2)}, u32[]{:S(2)}) %all-to-all-start) | async-done | bytes 262176 | tf_op jit(solution)/shard_map/all_to_all | solution.py:692
  58.7 0.8 weight_sum.1.refs_0_
  59.4 5.3 %all-to-all-start.1 = ((f32[16,32,128]{2,1,0:T(8,128)}), f32[16,32,128]{2,1,0:T(8,128)S(1)}, u32[]{:S(2)}, u32[]{:S(2)}) async-start(f32[16,32,128]{2,1,0:T(8,128)} %weight_sum.1.refs_0_), calls=%async_computation.1 | async-start | bytes 524288 | tf_op jit(solution)/shard_map/all_to_all | solution.py:703
  64.8 0.0 collective-permute-done.9.refs_2_
  64.8 0.0 collective-permute-done.10.refs_3_
  64.8 0.0 collective-permute-done.11.refs_4_
  64.8 2.0 %collective-permute-start.12 = (f32[32,512]{1,0:T(8,128)S(1)}, f32[32,512]{1,0:T(8,128)S(1)}, u32[]{:S(2)}, u32[]{:S(2)}) collective-permute-start(f32[32,512]{1,0:T(8,128)S(1)} %get-tuple-element.84), channel_id=1, source_target_pairs={{0,4},{4,0},{8,12},{12,8},{16,20},{20,16},{24,28},{28,24},{1,5},{5... | collective-permute-start | bytes 196616 | tf_op jit(solution)/shard_map/ppermute | solution.py:705
  66.8 5.0 %pair_own.1.refs_0_ = f32[16,4,16,128]{3,2,1,0:T(8,128)S(1)} custom-call(f32[16,32,128]{2,1,0:T(8,128)} %weight_sum.1.refs_0_, bf16[8,512,512]{2,1,0:T(8,128)(2,1)} %get-tuple-element.77.refs_1_, bf16[512,512]{1,0:T(8,128)(2,1)} %get-tuple-element.74.refs_2_), custom_call_target="tpu_custom_call" | custom-call | flops 6442450944 | bytes 1 | tf_op jit(solution)/shard_map/pair_own/pallas_call | solution.py:517
  71.8 0.0 collective-permute-done.8.refs_3_
  71.8 0.0 collective-permute-done.7.refs_1_
  71.8 0.0 collective-permute-done.12.refs_5_
  71.8 2.2 %finish.1 = (f32[16,4,2,16,128]{4,3,2,1,0:T(8,128)}, f32[16,1024]{1,0:T(8,128)}, f32[16,4096]{1,0:T(8,128)}) custom-call(f32[16,4,16,128]{3,2,1,0:T(8,128)S(1)} %pair_own.1.refs_0_, f32[16,4,16,128]{3,2,1,0:T(8,128)S(1)} %collective-permute-done.7.refs_1_, f32[1,512,128]{2,1,0:T(8,128)S(1)} %get-tuple-element.76.refs_1_.refs_2_, ...), custom_call_target="tpu_custom_call" | custom-call | flops 1 | bytes 1 | tf_op jit(solution)/shard_map/finish/pallas_call | solution.py:517
  74.0 0.1 all-to-all-done.1
  74.0 0.0 collective-permute-start.13
  74.1 1.5 %collective-permute-done.13.refs_1_ = f32[512,128]{1,0:T(8,128)S(1)} collective-permute-done((f32[512,128]{1,0:T(8,128)S(1)}, f32[512,128]{1,0:T(8,128)S(1)}, u32[]{:S(2)}, u32[]{:S(2)}) %collective-permute-start.13) | collective-permute-done | bytes 262176 | tf_op jit(solution)/shard_map/ppermute | solution.py:730
  75.6 1.1 %place.1 = f32[1024,128]{1,0:T(8,128)} custom-call(f32[512,128]{1,0:T(8,128)S(1)} %bitcast.5, f32[512,128]{1,0:T(8,128)S(1)} %collective-permute-done.13.refs_1_), custom_call_target="tpu_custom_call" | custom-call | flops 1 | bytes 1 | tf_op jit(solution)/shard_map/place/pallas_call | solution.py:517
  (1 shorter events, 0.0 us)
Async XLA Ops:
  2.6 18.0 %collective-permute-start = (f32[16,4,16,128]{3,2,1,0:T(8,128)S(1)}, f32[16,4,16,128]{3,2,1,0:T(8,128)S(1)}, u32[]{:S(2)}, u32[]{:S(2)}) collective-permute-start(f32[16,4,16,128]{3,2,1,0:T(8,128)S(1)} %get-tuple-element.52), channel_id=1, source_target_pairs={{0,4},{4,0},{8,12},{12,8},{16,20},{20,16},{24,28},{28,24},{1,5},{5... | collective-permute-start | bytes 1572872 | tf_op jit(solution)/shard_map/ppermute | solution.py:577
  5.6 14.4 %collective-permute-start.3 = (f32[512,128]{1,0:T(8,128)S(1)}, f32[512,128]{1,0:T(8,128)S(1)}, u32[]{:S(2)}, u32[]{:S(2)}) collective-permute-start(f32[512,128]{1,0:T(8,128)S(1)} %get-tuple-element.58.refs_5_.refs_3_), channel_id=1, source_target_pairs={{0,16},{4,20},{8,24},{12,28},{16,0},{20,4},{24,8},{28,12},{1,17},{... | collective-permute-start | bytes 786440 | tf_op jit(solution)/shard_map/ppermute | solution.py:613
  8.2 21.1 %collective-permute-start.2 = (f32[512,128]{1,0:T(8,128)S(1)}, f32[512,128]{1,0:T(8,128)S(1)}, u32[]{:S(2)}, u32[]{:S(2)}) collective-permute-start(f32[512,128]{1,0:T(8,128)S(1)} %get-tuple-element.58.refs_5_.refs_3_), channel_id=1, source_target_pairs={{0,8},{4,12},{8,0},{12,4},{16,24},{20,28},{24,16},{28,20},{1,9},{5... | collective-permute-start | bytes 786440 | tf_op jit(solution)/shard_map/ppermute | solution.py:613
  9.8 13.4 %collective-permute-start.1 = (f32[512,128]{1,0:T(8,128)S(1)}, f32[512,128]{1,0:T(8,128)S(1)}, u32[]{:S(2)}, u32[]{:S(2)}) collective-permute-start(f32[512,128]{1,0:T(8,128)S(1)} %get-tuple-element.50.refs_2_.refs_1_), channel_id=1, source_target_pairs={{0,4},{4,0},{8,12},{12,8},{16,20},{20,16},{24,28},{28,24},{1,5},{5... | collective-permute-start | bytes 786440 | tf_op jit(solution)/shard_map/ppermute | solution.py:578
  20.0 9.3 %collective-permute-start.4 = (f32[512,128]{1,0:T(8,128)S(1)}, f32[512,128]{1,0:T(8,128)S(1)}, u32[]{:S(2)}, u32[]{:S(2)}) collective-permute-start(f32[512,128]{1,0:T(8,128)S(1)} %collective-permute-done.3.refs_7_.refs_5_), channel_id=1, source_target_pairs={{0,8},{4,12},{8,0},{12,4},{16,24},{20,28},{24,16},{28,20},{1,9},{5... | collective-permute-start | bytes 786440 | tf_op jit(solution)/shard_map/ppermute | solution.py:613
  26.0 29.3 %collective-permute-start.6 = (f32[2,512,128]{2,1,0:T(8,128)}, f32[2,512,128]{2,1,0:T(8,128)S(1)}, u32[]{:S(2)}, u32[]{:S(2)}) collective-permute-start(f32[2,512,128]{2,1,0:T(8,128)} %get-tuple-element.75), channel_id=1, source_target_pairs={{0,16},{4,20},{8,24},{12,28},{16,0},{20,4},{24,8},{28,12},{1,17},{... | collective-permute-start | bytes 1572872 | tf_op jit(solution)/shard_map/ppermute | solution.py:626
  37.5 3.6 %collective-permute-start.5 = (f32[512,128]{1,0:T(8,128)S(1)}, f32[512,128]{1,0:T(8,128)S(1)}, u32[]{:S(2)}, u32[]{:S(2)}) collective-permute-start(f32[512,128]{1,0:T(8,128)S(1)} %get-tuple-element.67), channel_id=1, source_target_pairs={{0,1},{1,0},{2,3},{3,2},{4,5},{5,4},{6,7},{7,6},{8,9},{9,8},{10,11... | collective-permute-start | bytes 786440 | tf_op jit(solution)/shard_map/ppermute | solution.py:642
  41.8 16.9 %all-to-all-start = ((f32[16,32,128]{2,1,0:T(8,128)}), f32[16,32,128]{2,1,0:T(8,128)S(1)}, u32[]{:S(2)}, u32[]{:S(2)}) async-start(f32[16,32,128]{2,1,0:T(8,128)} %bitcast.1.refs_0_), calls=%async_computation | async-start | bytes 524288 | tf_op jit(solution)/shard_map/all_to_all | solution.py:692
  46.5 18.3 %collective-permute-start.9 = (f32[2,32,512]{2,1,0:T(8,128)}, f32[2,32,512]{2,1,0:T(8,128)S(1)}, u32[]{:S(2)}, u32[]{:S(2)}) collective-permute-start(f32[2,32,512]{2,1,0:T(8,128)} %get-tuple-element.80), channel_id=1, source_target_pairs={{0,1},{1,0},{2,3},{3,2},{4,5},{5,4},{6,7},{7,6},{8,9},{9,8},{10,11... | collective-permute-start | bytes 393224 | tf_op jit(solution)/shard_map/ppermute | solution.py:677
  46.7 18.0 %collective-permute-start.10 = (f32[2,32,512]{2,1,0:T(8,128)}, f32[2,32,512]{2,1,0:T(8,128)S(1)}, u32[]{:S(2)}, u32[]{:S(2)}) collective-permute-start(f32[2,32,512]{2,1,0:T(8,128)} %get-tuple-element.81), channel_id=1, source_target_pairs={{0,2},{1,3},{2,0},{3,1},{4,6},{5,7},{6,4},{7,5},{8,10},{9,11},{10,... | collective-permute-start | bytes 393224 | tf_op jit(solution)/shard_map/ppermute | solution.py:677
  48.5 16.3 %collective-permute-start.11 = (f32[2,32,512]{2,1,0:T(8,128)S(1)}, f32[2,32,512]{2,1,0:T(8,128)S(1)}, u32[]{:S(2)}, u32[]{:S(2)}) collective-permute-start(f32[2,32,512]{2,1,0:T(8,128)S(1)} %get-tuple-element.82), channel_id=1, source_target_pairs={{0,3},{1,2},{2,1},{3,0},{4,7},{5,6},{6,5},{7,4},{8,11},{9,10},{10,... | collective-permute-start | bytes 393224 | tf_op jit(solution)/shard_map/ppermute | solution.py:677
  53.5 18.3 %collective-permute-start.7 = (f32[16,4,16,128]{3,2,1,0:T(8,128)S(1)}, f32[16,4,16,128]{3,2,1,0:T(8,128)S(1)}, u32[]{:S(2)}, u32[]{:S(2)}) collective-permute-start(f32[16,4,16,128]{3,2,1,0:T(8,128)S(1)} %pair_peer.1.refs_0_), channel_id=1, source_target_pairs={{0,4},{4,0},{8,12},{12,8},{16,20},{20,16},{24,28},{28,24},{1,5},{5... | collective-permute-start | bytes 1572872 | tf_op jit(solution)/shard_map/ppermute | solution.py:690
  55.4 16.4 %collective-permute-start.8 = (f32[1,512,128]{2,1,0:T(8,128)S(1)}, f32[1,512,128]{2,1,0:T(8,128)S(1)}, u32[]{:S(2)}, u32[]{:S(2)}) collective-permute-start(f32[1,512,128]{2,1,0:T(8,128)S(1)} %get-tuple-element.78), channel_id=1, source_target_pairs={{0,8},{4,12},{8,0},{12,4},{16,24},{20,28},{24,16},{28,20},{1,9},{5... | collective-permute-start | bytes 786440 | tf_op jit(solution)/shard_map/ppermute | solution.py:686
  59.4 14.6 %all-to-all-start.1 = ((f32[16,32,128]{2,1,0:T(8,128)}), f32[16,32,128]{2,1,0:T(8,128)S(1)}, u32[]{:S(2)}, u32[]{:S(2)}) async-start(f32[16,32,128]{2,1,0:T(8,128)} %weight_sum.1.refs_0_), calls=%async_computation.1 | async-start | bytes 524288 | tf_op jit(solution)/shard_map/all_to_all | solution.py:703
  64.8 7.0 %collective-permute-start.12 = (f32[32,512]{1,0:T(8,128)S(1)}, f32[32,512]{1,0:T(8,128)S(1)}, u32[]{:S(2)}, u32[]{:S(2)}) collective-permute-start(f32[32,512]{1,0:T(8,128)S(1)} %get-tuple-element.84), channel_id=1, source_target_pairs={{0,4},{4,0},{8,12},{12,8},{16,20},{20,16},{24,28},{28,24},{1,5},{5... | collective-permute-start | bytes 196616 | tf_op jit(solution)/shard_map/ppermute | solution.py:705
  74.0 1.6 %collective-permute-start.13 = (f32[512,128]{1,0:T(8,128)S(1)}, f32[512,128]{1,0:T(8,128)S(1)}, u32[]{:S(2)}, u32[]{:S(2)}) collective-permute-start(f32[512,128]{1,0:T(8,128)S(1)} %bitcast.4), channel_id=1, source_target_pairs={{0,1},{1,0},{2,3},{3,2},{4,5},{5,4},{6,7},{7,6},{8,9},{9,8},{10,11... | collective-permute-start | bytes 786440 | tf_op jit(solution)/shard_map/ppermute | solution.py:730

commit v19 on v18

--- a/solution.py
+++ b/solution.py
@@ -183,7 +183,7 @@
         out_ref[pair] = jnp.concatenate(halves(found), 1)
         return carry
 
-    lax.fori_loop(0, out_ref.shape[0], step_of, 0, unroll=2)
+    lax.fori_loop(0, out_ref.shape[0], step_of, 0, unroll=4)
 
 
 def gradient_kernel(
@@ -246,7 +246,7 @@
         store(step, first[:sequences] + first[sequences:] + second)
         return carry
 
-    lax.fori_loop(0, factor_ref.shape[1] // (2 * ENTRY_CHANNELS), step_of, 0, unroll=2)
+    lax.fori_loop(0, factor_ref.shape[1] // (2 * ENTRY_CHANNELS), step_of, 0, unroll=4)
 
 
 def rows_of_step(refs, step, half, lanes):
@@ -347,7 +347,7 @@
             copy.start()
         return carry
 
-    lax.fori_loop(0, channels // (2 * fold), outer_step, 0, unroll=2)
+    lax.fori_loop(0, channels // (2 * fold), outer_step, 0, unroll=4)
     total[...] = jnp.zeros_like(total)
 
     def weight_step(pair, carry):
@@ -359,7 +359,7 @@
         total[...] += dot(jnp.concatenate(lefts, 1), jnp.concatenate(rights, 0))
         return carry
 
-    lax.fori_loop(0, own_ref.shape[0], weight_step, 0, unroll=2)
+    lax.fori_loop(0, own_ref.shape[0], weight_step, 0, unroll=4)
     core = lax.rem(lax.axis_index("inner"), 2)
     steps = channels // (2 * fold)
     for out_ref, half in ((keep_ref, core), (send_ref, 1 - core)):
@@ -400,7 +400,7 @@
         total[...] += both[:, :sequences] + both[:, sequences:] + dot(grads[1], high)
         return carry
 
-    lax.fori_loop(0, ENTRY_CHANNELS // (fold * group), step_of, 0, unroll=2)
+    lax.fori_loop(0, ENTRY_CHANNELS // (fold * group), step_of, 0, unroll=4)
     flipped[...] = total[...].T * (1.0 / sequences)
     here = lax.axis_index("inner")
     size, width = out_refs[0].shape[1:]
@@ -603,19 +603,19 @@
         "gradient_own",
         out_specs=[vmem, vmem, vmem, vmem, hbm],
     )(weight, cotangent_own, left)
+    grad_peer, spread_peer = large(
+        functools.partial(peer_kernel, blocks), [factor, spread], [], "gradient_peer"
+    )(weight_cat, cotangent_peer)
     rights = {0: right}
     distance = blocks // 2
     while distance:
         for slot in list(rights):
             sent = rights[slot]
             if slot:
-                sent, _ = lax.optimization_barrier((sent, grad_own))
+                sent, _ = lax.optimization_barrier((sent, grad_peer))
             rights[slot + distance] = lax.ppermute(sent, "blk", slot_moves[distance])
         distance = distance // 2
     rights = [rights[slot] for slot in range(blocks)]
-    grad_peer, spread_peer = large(
-        functools.partial(peer_kernel, blocks), [factor, spread], [], "gradient_peer"
-    )(weight_cat, cotangent_peer)
     right_half = shape(blocks // 2, channels * depth, sequences)
     right_keep, right_send = large(
         functools.partial(right_kernel, blocks, depth),

time: 77.1 us -> 81.6 us (1.058)
  waiting for transfers between devices: 7.77 us -> 14.7 us
  Pallas kernels: 38.5 us -> 34.3 us
  starting transfers between devices: 28.9 us -> 30.7 us
    ppermute x1, waiting for transfers between devices: 0.06 us -> 6.64 us  [local(): right_send = lax.ppermute(right_send, 'blk', slot_moves[blocks // 2])]
    pallas_call x13, Pallas kernels: 38.5 us -> 34.3 us  [run(): pl.pallas_call(lambda *refs: kernel(*refs[len(after):]), out_shape=out_sh...]
    ppermute x3, waiting for transfers between devices: 4.19 us -> 0.01 us  [local(): rights[slot + distance] = lax.ppermute(sent, 'blk', slot_moves[distance])]
    ppermute x1, waiting for transfers between devices: 0.01 us -> 3.28 us  [local(): cotangent_peer = lax.ppermute(cotangent_send, 'blk', partner)]
    all_to_all x2, starting transfers between devices: 9.95 us -> 12.4 us  [local(): lax.all_to_all(pieces, everyone, 0, 0, axis_index_groups=core_groups)]
    all_to_all x2, waiting for transfers between devices: 1.86 us -> 0.01 us  [local(): lax.all_to_all(pieces, everyone, 0, 0, axis_index_groups=core_groups)]
    ppermute x3, starting transfers between devices: 4.73 us -> 6.36 us  [local(): rights[slot + distance] = lax.ppermute(sent, 'blk', slot_moves[distance])]
    ppermute x1, waiting for transfers between devices: 0.01 us -> 1.4 us  [local(): left_found = [left_own, lax.ppermute(left_send, 'blk', partner)]]
  transfers between devices with their start and end apart: 16 -> 16, of which waited for: 6 -> 6; matrix products, arithmetic and copies ran while one was open for 1% -> 1% of each run, Pallas kernels for 46% -> 38%
where the time goes in v19:
time: 81.6 us; the launch traced here: 81.2 us
  Pallas kernels  34.3 us (42%)
  starting transfers between devices  30.7 us (38%)
  waiting for transfers between devices  14.7 us (18%)
  between operations  0.82 us (1%)
    pallas_call x13, Pallas kernels, run(): pl.pallas_call(lambda *refs: kernel(*refs[len(after):]), out_shape=out_sh...  34.3 us
    all_to_all x2, starting transfers between devices, local(): lax.all_to_all(pieces, everyone, 0, 0, axis_index_groups=core_groups)  12.4 us
    ppermute x1, waiting for transfers between devices, local(): right_send = lax.ppermute(right_send, 'blk', slot_moves[blocks // 2])  6.64 us
    ppermute x3, starting transfers between devices, local(): rights[slot + distance] = lax.ppermute(sent, 'blk', slot_moves[distance])  6.36 us
    ppermute x1, waiting for transfers between devices, local(): cotangent_peer = lax.ppermute(cotangent_send, 'blk', partner)  3.28 us
    ppermute x1, starting transfers between devices, local(): cotangent_peer = lax.ppermute(cotangent_send, 'blk', partner)  3.03 us
    ppermute x1, starting transfers between devices, local(): right_send = lax.ppermute(right_send, 'blk', slot_moves[blocks // 2])  2.87 us
    ppermute x3, starting transfers between devices, local(): lax.ppermute(part, 'inner', inner_moves[slot])  2.07 us
  transfers between devices with their start and end apart: 16, of which 6 were waited for; matrix products, arithmetic and copies ran while one was open for 1% of the time, Pallas kernels for 38%

profile of v19, /device:TPU:0, one launch (start us, length us, event | category | flops | bytes accessed | tf_op | source)
XLA Modules:
  0.0 81.2 jit_solution(11793020557858073156)
XLA Ops:
  0.6 2.0 %prepare.1 = (f32[512,128]{1,0:T(8,128)S(1)}, f32[512,128]{1,0:T(8,128)S(1)}, f32[16,4,16,128]{3,2,1,0:T(8,128)S(1)}, f32[16,4,16,128]{3,2,1,0:T(8,128)S(1)}, f32[1024,128]{1,0:T(8,128)S(1)}) custom-call(f32[16,4,2,16,128]{4,3,2,1,0:T(8,128)} %bitcast.6, f32[16,4096]{1,0:T(8,128)} %refs_1_.1, f32[16,4096]{1,0:T(8,128)} %refs_2_.1, f32[1024,128]{1,0:T(8,128)} %refs_3_.1), custom_call_target="tpu_custom_call" | custom-call | flops 1 | bytes 1 | tf_op jit(solution)/shard_map/prepare/pallas_call | solution.py:517
  2.6 3.0 %collective-permute-start = (f32[16,4,16,128]{3,2,1,0:T(8,128)S(1)}, f32[16,4,16,128]{3,2,1,0:T(8,128)S(1)}, u32[]{:S(2)}, u32[]{:S(2)}) collective-permute-start(f32[16,4,16,128]{3,2,1,0:T(8,128)S(1)} %get-tuple-element.52), channel_id=1, source_target_pairs={{0,4},{4,0},{8,12},{12,8},{16,20},{20,16},{24,28},{28,24},{1,5},{5... | collective-permute-start | bytes 1572872 | tf_op jit(solution)/shard_map/ppermute | solution.py:577
  5.6 2.6 %collective-permute-start.3 = (f32[512,128]{1,0:T(8,128)S(1)}, f32[512,128]{1,0:T(8,128)S(1)}, u32[]{:S(2)}, u32[]{:S(2)}) collective-permute-start(f32[512,128]{1,0:T(8,128)S(1)} %get-tuple-element.58.refs_5_.refs_3_), channel_id=1, source_target_pairs={{0,16},{4,20},{8,24},{12,28},{16,0},{20,4},{24,8},{28,12},{1,17},{... | collective-permute-start | bytes 786440 | tf_op jit(solution)/shard_map/ppermute | solution.py:616
  8.2 1.6 %collective-permute-start.2 = (f32[512,128]{1,0:T(8,128)S(1)}, f32[512,128]{1,0:T(8,128)S(1)}, u32[]{:S(2)}, u32[]{:S(2)}) collective-permute-start(f32[512,128]{1,0:T(8,128)S(1)} %get-tuple-element.58.refs_5_.refs_3_), channel_id=1, source_target_pairs={{0,8},{4,12},{8,0},{12,4},{16,24},{20,28},{24,16},{28,20},{1,9},{5... | collective-permute-start | bytes 786440 | tf_op jit(solution)/shard_map/ppermute | solution.py:616
  9.8 0.5 collective-permute-start.1
  10.3 4.8 %gradient_own.1 = (bf16[8,512,512]{2,1,0:T(8,128)(2,1)S(1)}, bf16[8,2,256,256]{3,2,1,0:T(8,128)(2,1)S(1)}, f32[8,128,256]{2,1,0:T(8,128)S(1)}, bf16[512,768]{1,0:T(8,128)(2,1)S(1)}, bf16[512,512]{1,0:T(8,128)(2,1)}) custom-call(f32[1024,128]{1,0:T(8,128)S(1)} %get-tuple-element.48.refs_0_, f32[16,4,16,128]{3,2,1,0:T(8,128)S(1)} %get-tuple-element.49.refs_1_, ...), custom_call_target="tpu_custom_call" | custom-call | flops 1 | bytes 1 | tf_op jit(solution)/shard_map/gradient_own/pallas_call | solution.py:517
  15.1 3.3 %collective-permute-done.refs_1_ = f32[16,4,16,128]{3,2,1,0:T(8,128)S(1)} collective-permute-done((f32[16,4,16,128]{3,2,1,0:T(8,128)S(1)}, f32[16,4,16,128]{3,2,1,0:T(8,128)S(1)}, u32[]{:S(2)}, u32[]{:S(2)}) %collective-permute-start) | collective-permute-done | bytes 524320 | tf_op jit(solution)/shard_map/ppermute | solution.py:577
  18.4 2.0 %gradient_peer.1 = (bf16[8,512,512]{2,1,0:T(8,128)(2,1)S(1)}, bf16[8,2,256,256]{3,2,1,0:T(8,128)(2,1)S(1)}) custom-call(bf16[512,768]{1,0:T(8,128)(2,1)S(1)} %get-tuple-element.51.refs_0_, f32[16,4,16,128]{3,2,1,0:T(8,128)S(1)} %collective-permute-done.refs_1_), custom_call_target="tpu_custom_call" | custom-call | flops 1 | bytes 1 | tf_op jit(solution)/shard_map/gradient_peer/pallas_call | solution.py:517
  20.4 0.0 collective-permute-done.3.refs_7_.refs_5_
  20.5 2.2 %collective-permute-start.4 = (f32[512,128]{1,0:T(8,128)S(1)}, f32[512,128]{1,0:T(8,128)S(1)}, u32[]{:S(2)}, u32[]{:S(2)}) collective-permute-start(f32[512,128]{1,0:T(8,128)S(1)} %collective-permute-done.3.refs_7_.refs_5_), channel_id=1, source_target_pairs={{0,8},{4,12},{8,0},{12,4},{16,24},{20,28},{24,16},{28,20},{1,9},{5... | collective-permute-start | bytes 786440 | tf_op jit(solution)/shard_map/ppermute | solution.py:616
  22.6 0.5 collective-permute-done.1.refs_1_.refs_2_
  23.2 1.5 %right_parts.1 = (f32[2,512,128]{2,1,0:T(8,128)S(1)}, f32[2,512,128]{2,1,0:T(8,128)S(1)}) custom-call(bf16[8,512,512]{2,1,0:T(8,128)(2,1)S(1)} %get-tuple-element.53.refs_0_.refs_2_, f32[512,128]{1,0:T(8,128)S(1)} %collective-permute-done.1.refs_1_.refs_2_, f32[8,128,256]{2,1,0:T(8,128)S(1)} %get-tuple-element.54.refs_2_), custom_call_target="tpu_custom_call" | custom-call | flops 1 | bytes 1 | tf_op jit(solution)/shard_map/right_parts/pallas_call | solution.py:517
  24.7 2.9 %collective-permute-start.6 = (f32[2,512,128]{2,1,0:T(8,128)S(1)}, f32[2,512,128]{2,1,0:T(8,128)S(1)}, u32[]{:S(2)}, u32[]{:S(2)}) collective-permute-start(f32[2,512,128]{2,1,0:T(8,128)S(1)} %get-tuple-element.75), channel_id=1, source_target_pairs={{0,16},{4,20},{8,24},{12,28},{16,0},{20,4},{24,8},{28,12},{1,17},{... | collective-permute-start | bytes 1572872 | tf_op jit(solution)/shard_map/ppermute | solution.py:626
  27.6 0.0 collective-permute-done.2.refs_6_.refs_4_
  27.6 0.0 collective-permute-done.4.refs_8_.refs_6_
  27.6 7.5 %weight.1 = (f32[512,128]{1,0:T(8,128)S(1)}, f32[512,128]{1,0:T(8,128)S(1)}, bf16[8,512,512]{2,1,0:T(8,128)(2,1)}, bf16[8,512,512]{2,1,0:T(8,128)(2,1)}) custom-call(f32[2,512,128]{2,1,0:T(8,128)S(1)} %get-tuple-element.55.refs_0_.refs_1_, f32[512,128]{1,0:T(8,128)S(1)} %get-tuple-element.50.refs_2_.refs_1_, ...), custom_call_target="tpu_custom_call" | custom-call | flops 12884901888 | bytes 1 | tf_op jit(solution)/shard_map/weight/pallas_call | solution.py:517
  35.1 0.1 collective-permute-start.5
  35.2 2.4 %left_parts.1 = (f32[2,32,512]{2,1,0:T(8,128)S(1)}, f32[2,32,512]{2,1,0:T(8,128)S(1)}, f32[2,32,512]{2,1,0:T(8,128)S(1)}, f32[2,32,512]{2,1,0:T(8,128)S(1)}) custom-call(f32[512,128]{1,0:T(8,128)S(1)} %get-tuple-element.66.refs_0_, bf16[8,512,512]{2,1,0:T(8,128)(2,1)S(1)} %get-tuple-element.61.refs_1_, ...), custom_call_target="tpu_custom_call" | custom-call | flops 6442450944 | bytes 1 | tf_op jit(solution)/shard_map/left_parts/pallas_call | solution.py:517
  37.6 0.0 collective-permute-done.5
  37.7 0.7 add.3
  38.4 6.7 %all-to-all-start = ((f32[16,32,128]{2,1,0:T(8,128)}), f32[16,32,128]{2,1,0:T(8,128)S(1)}, u32[]{:S(2)}, u32[]{:S(2)}) async-start(f32[16,32,128]{2,1,0:T(8,128)} %bitcast.1.refs_0_), calls=%async_computation | async-start | bytes 524288 | tf_op jit(solution)/shard_map/all_to_all | solution.py:692
  45.1 0.3 collective-permute-start.9
  45.4 1.7 %collective-permute-start.10 = (f32[2,32,512]{2,1,0:T(8,128)S(1)}, f32[2,32,512]{2,1,0:T(8,128)S(1)}, u32[]{:S(2)}, u32[]{:S(2)}) collective-permute-start(f32[2,32,512]{2,1,0:T(8,128)S(1)} %get-tuple-element.81), channel_id=1, source_target_pairs={{0,2},{1,3},{2,0},{3,1},{4,6},{5,7},{6,4},{7,5},{8,10},{9,11},{10,... | collective-permute-start | bytes 393224 | tf_op jit(solution)/shard_map/ppermute | solution.py:677
  47.1 0.1 collective-permute-start.11
  47.2 6.6 %collective-permute-done.6.refs_2_ = f32[2,512,128]{2,1,0:T(8,128)S(1)} collective-permute-done((f32[2,512,128]{2,1,0:T(8,128)S(1)}, f32[2,512,128]{2,1,0:T(8,128)S(1)}, u32[]{:S(2)}, u32[]{:S(2)}) %collective-permute-start.6) | collective-permute-done | bytes 524320 | tf_op jit(solution)/shard_map/ppermute | solution.py:626
  53.8 0.1 right_halve.1
  53.9 0.1 collective-permute-start.8
  54.0 5.0 %pair_peer.1.refs_0_ = f32[16,4,16,128]{3,2,1,0:T(8,128)S(1)} custom-call(f32[16,32,128]{2,1,0:T(8,128)} %bitcast.1.refs_0_, bf16[8,512,512]{2,1,0:T(8,128)(2,1)} %get-tuple-element.73.refs_1_, bf16[512,512]{1,0:T(8,128)(2,1)} %get-tuple-element.74.refs_2_), custom_call_target="tpu_custom_call" | custom-call | flops 6442450944 | bytes 1 | tf_op jit(solution)/shard_map/pair_peer/pallas_call | solution.py:517
  58.9 1.3 %collective-permute-start.7 = (f32[16,4,16,128]{3,2,1,0:T(8,128)S(1)}, f32[16,4,16,128]{3,2,1,0:T(8,128)S(1)}, u32[]{:S(2)}, u32[]{:S(2)}) collective-permute-start(f32[16,4,16,128]{3,2,1,0:T(8,128)S(1)} %pair_peer.1.refs_0_), channel_id=1, source_target_pairs={{0,4},{4,0},{8,12},{12,8},{16,20},{20,16},{24,28},{28,24},{1,5},{5... | collective-permute-start | bytes 1572872 | tf_op jit(solution)/shard_map/ppermute | solution.py:690
  60.2 0.0 all-to-all-done.refs_2_
  60.2 0.8 weight_sum.1.refs_0_
  61.0 5.6 %all-to-all-start.1 = ((f32[16,32,128]{2,1,0:T(8,128)}), f32[16,32,128]{2,1,0:T(8,128)S(1)}, u32[]{:S(2)}, u32[]{:S(2)}) async-start(f32[16,32,128]{2,1,0:T(8,128)} %weight_sum.1.refs_0_), calls=%async_computation.1 | async-start | bytes 524288 | tf_op jit(solution)/shard_map/all_to_all | solution.py:703
  66.6 0.0 collective-permute-done.9.refs_2_
  66.6 0.0 collective-permute-done.10.refs_3_
  66.6 0.0 collective-permute-done.11.refs_4_
  66.7 2.0 %collective-permute-start.12 = (f32[32,512]{1,0:T(8,128)S(1)}, f32[32,512]{1,0:T(8,128)S(1)}, u32[]{:S(2)}, u32[]{:S(2)}) collective-permute-start(f32[32,512]{1,0:T(8,128)S(1)} %get-tuple-element.84), channel_id=1, source_target_pairs={{0,4},{4,0},{8,12},{12,8},{16,20},{20,16},{24,28},{28,24},{1,5},{5... | collective-permute-start | bytes 196616 | tf_op jit(solution)/shard_map/ppermute | solution.py:705
  68.7 5.0 %pair_own.1.refs_0_ = f32[16,4,16,128]{3,2,1,0:T(8,128)S(1)} custom-call(f32[16,32,128]{2,1,0:T(8,128)} %weight_sum.1.refs_0_, bf16[8,512,512]{2,1,0:T(8,128)(2,1)} %get-tuple-element.77.refs_1_, bf16[512,512]{1,0:T(8,128)(2,1)} %get-tuple-element.74.refs_2_), custom_call_target="tpu_custom_call" | custom-call | flops 6442450944 | bytes 1 | tf_op jit(solution)/shard_map/pair_own/pallas_call | solution.py:517
  73.6 0.0 collective-permute-done.8.refs_3_
  73.6 1.3 %collective-permute-done.7.refs_1_ = f32[16,4,16,128]{3,2,1,0:T(8,128)S(1)} collective-permute-done((f32[16,4,16,128]{3,2,1,0:T(8,128)S(1)}, f32[16,4,16,128]{3,2,1,0:T(8,128)S(1)}, u32[]{:S(2)}, u32[]{:S(2)}) %collective-permute-start.7) | collective-permute-done | bytes 524320 | tf_op jit(solution)/shard_map/ppermute | solution.py:690
  74.9 1.4 %collective-permute-done.12.refs_5_ = f32[32,512]{1,0:T(8,128)S(1)} collective-permute-done((f32[32,512]{1,0:T(8,128)S(1)}, f32[32,512]{1,0:T(8,128)S(1)}, u32[]{:S(2)}, u32[]{:S(2)}) %collective-permute-start.12) | collective-permute-done | bytes 65568 | tf_op jit(solution)/shard_map/ppermute | solution.py:705
  76.3 2.2 %finish.1 = (f32[16,4,2,16,128]{4,3,2,1,0:T(8,128)}, f32[16,1024]{1,0:T(8,128)}, f32[16,4096]{1,0:T(8,128)}) custom-call(f32[16,4,16,128]{3,2,1,0:T(8,128)S(1)} %pair_own.1.refs_0_, f32[16,4,16,128]{3,2,1,0:T(8,128)S(1)} %collective-permute-done.7.refs_1_, f32[1,512,128]{2,1,0:T(8,128)S(1)} %get-tuple-element.76.refs_1_.refs_2_, ...), custom_call_target="tpu_custom_call" | custom-call | flops 1 | bytes 1 | tf_op jit(solution)/shard_map/finish/pallas_call | solution.py:517
  78.5 0.0 all-to-all-done.1
  78.5 0.1 collective-permute-start.13
  78.6 1.5 %collective-permute-done.13.refs_1_ = f32[512,128]{1,0:T(8,128)S(1)} collective-permute-done((f32[512,128]{1,0:T(8,128)S(1)}, f32[512,128]{1,0:T(8,128)S(1)}, u32[]{:S(2)}, u32[]{:S(2)}) %collective-permute-start.13) | collective-permute-done | bytes 262176 | tf_op jit(solution)/shard_map/ppermute | solution.py:730
  80.1 1.1 %place.1 = f32[1024,128]{1,0:T(8,128)} custom-call(f32[512,128]{1,0:T(8,128)S(1)} %bitcast.5, f32[512,128]{1,0:T(8,128)S(1)} %collective-permute-done.13.refs_1_), custom_call_target="tpu_custom_call" | custom-call | flops 1 | bytes 1 | tf_op jit(solution)/shard_map/place/pallas_call | solution.py:517
  (1 shorter events, 0.0 us)
Async XLA Ops:
  2.6 15.8 %collective-permute-start = (f32[16,4,16,128]{3,2,1,0:T(8,128)S(1)}, f32[16,4,16,128]{3,2,1,0:T(8,128)S(1)}, u32[]{:S(2)}, u32[]{:S(2)}) collective-permute-start(f32[16,4,16,128]{3,2,1,0:T(8,128)S(1)} %get-tuple-element.52), channel_id=1, source_target_pairs={{0,4},{4,0},{8,12},{12,8},{16,20},{20,16},{24,28},{28,24},{1,5},{5... | collective-permute-start | bytes 1572872 | tf_op jit(solution)/shard_map/ppermute | solution.py:577
  5.6 14.8 %collective-permute-start.3 = (f32[512,128]{1,0:T(8,128)S(1)}, f32[512,128]{1,0:T(8,128)S(1)}, u32[]{:S(2)}, u32[]{:S(2)}) collective-permute-start(f32[512,128]{1,0:T(8,128)S(1)} %get-tuple-element.58.refs_5_.refs_3_), channel_id=1, source_target_pairs={{0,16},{4,20},{8,24},{12,28},{16,0},{20,4},{24,8},{28,12},{1,17},{... | collective-permute-start | bytes 786440 | tf_op jit(solution)/shard_map/ppermute | solution.py:616
  8.2 19.3 %collective-permute-start.2 = (f32[512,128]{1,0:T(8,128)S(1)}, f32[512,128]{1,0:T(8,128)S(1)}, u32[]{:S(2)}, u32[]{:S(2)}) collective-permute-start(f32[512,128]{1,0:T(8,128)S(1)} %get-tuple-element.58.refs_5_.refs_3_), channel_id=1, source_target_pairs={{0,8},{4,12},{8,0},{12,4},{16,24},{20,28},{24,16},{28,20},{1,9},{5... | collective-permute-start | bytes 786440 | tf_op jit(solution)/shard_map/ppermute | solution.py:616
  9.8 13.4 %collective-permute-start.1 = (f32[512,128]{1,0:T(8,128)S(1)}, f32[512,128]{1,0:T(8,128)S(1)}, u32[]{:S(2)}, u32[]{:S(2)}) collective-permute-start(f32[512,128]{1,0:T(8,128)S(1)} %get-tuple-element.50.refs_2_.refs_1_), channel_id=1, source_target_pairs={{0,4},{4,0},{8,12},{12,8},{16,20},{20,16},{24,28},{28,24},{1,5},{5... | collective-permute-start | bytes 786440 | tf_op jit(solution)/shard_map/ppermute | solution.py:578
  20.5 7.1 %collective-permute-start.4 = (f32[512,128]{1,0:T(8,128)S(1)}, f32[512,128]{1,0:T(8,128)S(1)}, u32[]{:S(2)}, u32[]{:S(2)}) collective-permute-start(f32[512,128]{1,0:T(8,128)S(1)} %collective-permute-done.3.refs_7_.refs_5_), channel_id=1, source_target_pairs={{0,8},{4,12},{8,0},{12,4},{16,24},{20,28},{24,16},{28,20},{1,9},{5... | collective-permute-start | bytes 786440 | tf_op jit(solution)/shard_map/ppermute | solution.py:616
  24.7 29.1 %collective-permute-start.6 = (f32[2,512,128]{2,1,0:T(8,128)S(1)}, f32[2,512,128]{2,1,0:T(8,128)S(1)}, u32[]{:S(2)}, u32[]{:S(2)}) collective-permute-start(f32[2,512,128]{2,1,0:T(8,128)S(1)} %get-tuple-element.75), channel_id=1, source_target_pairs={{0,16},{4,20},{8,24},{12,28},{16,0},{20,4},{24,8},{28,12},{1,17},{... | collective-permute-start | bytes 1572872 | tf_op jit(solution)/shard_map/ppermute | solution.py:626
  35.1 2.5 %collective-permute-start.5 = (f32[512,128]{1,0:T(8,128)S(1)}, f32[512,128]{1,0:T(8,128)S(1)}, u32[]{:S(2)}, u32[]{:S(2)}) collective-permute-start(f32[512,128]{1,0:T(8,128)S(1)} %get-tuple-element.67), channel_id=1, source_target_pairs={{0,1},{1,0},{2,3},{3,2},{4,5},{5,4},{6,7},{7,6},{8,9},{9,8},{10,11... | collective-permute-start | bytes 786440 | tf_op jit(solution)/shard_map/ppermute | solution.py:642
  38.4 21.8 %all-to-all-start = ((f32[16,32,128]{2,1,0:T(8,128)}), f32[16,32,128]{2,1,0:T(8,128)S(1)}, u32[]{:S(2)}, u32[]{:S(2)}) async-start(f32[16,32,128]{2,1,0:T(8,128)} %bitcast.1.refs_0_), calls=%async_computation | async-start | bytes 524288 | tf_op jit(solution)/shard_map/all_to_all | solution.py:692
  45.1 21.5 %collective-permute-start.9 = (f32[2,32,512]{2,1,0:T(8,128)S(1)}, f32[2,32,512]{2,1,0:T(8,128)S(1)}, u32[]{:S(2)}, u32[]{:S(2)}) collective-permute-start(f32[2,32,512]{2,1,0:T(8,128)S(1)} %get-tuple-element.80), channel_id=1, source_target_pairs={{0,1},{1,0},{2,3},{3,2},{4,5},{5,4},{6,7},{7,6},{8,9},{9,8},{10,11... | collective-permute-start | bytes 393224 | tf_op jit(solution)/shard_map/ppermute | solution.py:677
  45.4 21.2 %collective-permute-start.10 = (f32[2,32,512]{2,1,0:T(8,128)S(1)}, f32[2,32,512]{2,1,0:T(8,128)S(1)}, u32[]{:S(2)}, u32[]{:S(2)}) collective-permute-start(f32[2,32,512]{2,1,0:T(8,128)S(1)} %get-tuple-element.81), channel_id=1, source_target_pairs={{0,2},{1,3},{2,0},{3,1},{4,6},{5,7},{6,4},{7,5},{8,10},{9,11},{10,... | collective-permute-start | bytes 393224 | tf_op jit(solution)/shard_map/ppermute | solution.py:677
  47.1 19.5 %collective-permute-start.11 = (f32[2,32,512]{2,1,0:T(8,128)S(1)}, f32[2,32,512]{2,1,0:T(8,128)S(1)}, u32[]{:S(2)}, u32[]{:S(2)}) collective-permute-start(f32[2,32,512]{2,1,0:T(8,128)S(1)} %get-tuple-element.82), channel_id=1, source_target_pairs={{0,3},{1,2},{2,1},{3,0},{4,7},{5,6},{6,5},{7,4},{8,11},{9,10},{10,... | collective-permute-start | bytes 393224 | tf_op jit(solution)/shard_map/ppermute | solution.py:677
  53.9 19.7 %collective-permute-start.8 = (f32[1,512,128]{2,1,0:T(8,128)S(1)}, f32[1,512,128]{2,1,0:T(8,128)S(1)}, u32[]{:S(2)}, u32[]{:S(2)}) collective-permute-start(f32[1,512,128]{2,1,0:T(8,128)S(1)} %get-tuple-element.78), channel_id=1, source_target_pairs={{0,8},{4,12},{8,0},{12,4},{16,24},{20,28},{24,16},{28,20},{1,9},{5... | collective-permute-start | bytes 786440 | tf_op jit(solution)/shard_map/ppermute | solution.py:686
  58.9 16.0 %collective-permute-start.7 = (f32[16,4,16,128]{3,2,1,0:T(8,128)S(1)}, f32[16,4,16,128]{3,2,1,0:T(8,128)S(1)}, u32[]{:S(2)}, u32[]{:S(2)}) collective-permute-start(f32[16,4,16,128]{3,2,1,0:T(8,128)S(1)} %pair_peer.1.refs_0_), channel_id=1, source_target_pairs={{0,4},{4,0},{8,12},{12,8},{16,20},{20,16},{24,28},{28,24},{1,5},{5... | collective-permute-start | bytes 1572872 | tf_op jit(solution)/shard_map/ppermute | solution.py:690
  61.0 17.5 %all-to-all-start.1 = ((f32[16,32,128]{2,1,0:T(8,128)}), f32[16,32,128]{2,1,0:T(8,128)S(1)}, u32[]{:S(2)}, u32[]{:S(2)}) async-start(f32[16,32,128]{2,1,0:T(8,128)} %weight_sum.1.refs_0_), calls=%async_computation.1 | async-start | bytes 524288 | tf_op jit(solution)/shard_map/all_to_all | solution.py:703
  66.7 9.7 %collective-permute-start.12 = (f32[32,512]{1,0:T(8,128)S(1)}, f32[32,512]{1,0:T(8,128)S(1)}, u32[]{:S(2)}, u32[]{:S(2)}) collective-permute-start(f32[32,512]{1,0:T(8,128)S(1)} %get-tuple-element.84), channel_id=1, source_target_pairs={{0,4},{4,0},{8,12},{12,8},{16,20},{20,16},{24,28},{28,24},{1,5},{5... | collective-permute-start | bytes 196616 | tf_op jit(solution)/shard_map/ppermute | solution.py:705
  78.5 1.6 %collective-permute-start.13 = (f32[512,128]{1,0:T(8,128)S(1)}, f32[512,128]{1,0:T(8,128)S(1)}, u32[]{:S(2)}, u32[]{:S(2)}) collective-permute-start(f32[512,128]{1,0:T(8,128)S(1)} %bitcast.4), channel_id=1, source_target_pairs={{0,1},{1,0},{2,3},{3,2},{4,5},{5,4},{6,7},{7,6},{8,9},{9,8},{10,11... | collective-permute-start | bytes 786440 | tf_op jit(solution)/shard_map/ppermute | solution.py:730

commit v20 on v19

--- a/solution.py
+++ b/solution.py
@@ -183,7 +183,7 @@
         out_ref[pair] = jnp.concatenate(halves(found), 1)
         return carry
 
-    lax.fori_loop(0, out_ref.shape[0], step_of, 0, unroll=4)
+    lax.fori_loop(0, out_ref.shape[0], step_of, 0, unroll=8)
 
 
 def gradient_kernel(
@@ -246,7 +246,7 @@
         store(step, first[:sequences] + first[sequences:] + second)
         return carry
 
-    lax.fori_loop(0, factor_ref.shape[1] // (2 * ENTRY_CHANNELS), step_of, 0, unroll=4)
+    lax.fori_loop(0, factor_ref.shape[1] // (2 * ENTRY_CHANNELS), step_of, 0, unroll=8)
 
 
 def rows_of_step(refs, step, half, lanes):
@@ -347,7 +347,7 @@
             copy.start()
         return carry
 
-    lax.fori_loop(0, channels // (2 * fold), outer_step, 0, unroll=4)
+    lax.fori_loop(0, channels // (2 * fold), outer_step, 0, unroll=8)
     total[...] = jnp.zeros_like(total)
 
     def weight_step(pair, carry):
@@ -359,7 +359,7 @@
         total[...] += dot(jnp.concatenate(lefts, 1), jnp.concatenate(rights, 0))
         return carry
 
-    lax.fori_loop(0, own_ref.shape[0], weight_step, 0, unroll=4)
+    lax.fori_loop(0, own_ref.shape[0], weight_step, 0, unroll=8)
     core = lax.rem(lax.axis_index("inner"), 2)
     steps = channels // (2 * fold)
     for out_ref, half in ((keep_ref, core), (send_ref, 1 - core)):
@@ -677,17 +677,16 @@
         lax.ppermute(part, "inner", inner_moves[slot]) if slot else part
         for slot, part in enumerate(left_parts)
     ]
+    pair_other = pair(outer_peer, [pieces], "pair_peer")
+    pair_found = lax.ppermute(pair_other, "blk", partner)
     slot = blocks // 4
     while slot:
         part = shape(slot, channels * depth, sequences)
         right_keep, right_send = call(
-            halve_kernel, [part, part], name="right_halve", after=[pieces]
+            halve_kernel, [part, part], name="right_halve", after=[pair_other]
         )(right_keep, right_send)
         right_send = lax.ppermute(right_send, "blk", slot_moves[slot])
         slot = slot // 2
-
-    pair_other = pair(outer_peer, [pieces], "pair_peer")
-    pair_found = lax.ppermute(pair_other, "blk", partner)
 
     pieces = lax.all_to_all(pieces, everyone, 0, 0, axis_index_groups=core_groups)
     pieces = call(

time: 81.6 us -> 79.6 us (0.975)
  waiting for transfers between devices: 14.7 us -> 9.61 us
  Pallas kernels: 34.3 us -> 37.3 us
    ppermute x1, waiting for transfers between devices: 6.64 us -> 0.01 us  [local(): right_send = lax.ppermute(right_send, 'blk', slot_moves[blocks // 2])]
    pallas_call x13, Pallas kernels: 34.3 us -> 37.3 us  [run(): pl.pallas_call(lambda *refs: kernel(*refs[len(after):]), out_shape=out_sh...]
    all_to_all x2, starting transfers between devices: 12.4 us -> 10.6 us  [local(): lax.all_to_all(pieces, everyone, 0, 0, axis_index_groups=core_groups)]
    ppermute x1, starting transfers between devices: 0.07 us -> 1.53 us  [local(): right_send = lax.ppermute(right_send, 'blk', slot_moves[slot])]
    ppermute x1, waiting for transfers between devices: 3.28 us -> 4.3 us  [local(): cotangent_peer = lax.ppermute(cotangent_send, 'blk', partner)]
  transfers between devices with their start and end apart: 16 -> 16, of which waited for: 6 -> 6; matrix products, arithmetic and copies ran while one was open for 1% -> 1% of each run, Pallas kernels for 38% -> 43%
where the time goes in v20:
time: 79.6 us; the launch traced here: 79.2 us
  Pallas kernels  37.3 us (47%)
  starting transfers between devices  30.8 us (39%)
  waiting for transfers between devices  9.61 us (12%)
    pallas_call x13, Pallas kernels, run(): pl.pallas_call(lambda *refs: kernel(*refs[len(after):]), out_shape=out_sh...  37.3 us
    all_to_all x2, starting transfers between devices, local(): lax.all_to_all(pieces, everyone, 0, 0, axis_index_groups=core_groups)  10.6 us
    ppermute x3, starting transfers between devices, local(): rights[slot + distance] = lax.ppermute(sent, 'blk', slot_moves[distance])  6.37 us
    ppermute x1, waiting for transfers between devices, local(): cotangent_peer = lax.ppermute(cotangent_send, 'blk', partner)  4.3 us
    ppermute x1, starting transfers between devices, local(): cotangent_peer = lax.ppermute(cotangent_send, 'blk', partner)  3.03 us
    ppermute x1, starting transfers between devices, local(): right_send = lax.ppermute(right_send, 'blk', slot_moves[blocks // 2])  2.81 us
    ppermute x3, starting transfers between devices, local(): lax.ppermute(part, 'inner', inner_moves[slot])  2.07 us
    ppermute x1, starting transfers between devices, local(): left_found = [left_own, lax.ppermute(left_send, 'blk', partner)]  1.99 us
  transfers between devices with their start and end apart: 16, of which 6 were waited for; matrix products, arithmetic and copies ran while one was open for 1% of the time, Pallas kernels for 43%

profile of v20, /device:TPU:0, one launch (start us, length us, event | category | flops | bytes accessed | tf_op | source)
XLA Modules:
  0.0 79.2 jit_solution(2023167694018895118)
XLA Ops:
  0.6 2.0 %prepare.1 = (f32[512,128]{1,0:T(8,128)S(1)}, f32[512,128]{1,0:T(8,128)S(1)}, f32[16,4,16,128]{3,2,1,0:T(8,128)S(1)}, f32[16,4,16,128]{3,2,1,0:T(8,128)S(1)}, f32[1024,128]{1,0:T(8,128)S(1)}) custom-call(f32[16,4,2,16,128]{4,3,2,1,0:T(8,128)} %bitcast.6, f32[16,4096]{1,0:T(8,128)} %refs_1_.1, f32[16,4096]{1,0:T(8,128)} %refs_2_.1, f32[1024,128]{1,0:T(8,128)} %refs_3_.1), custom_call_target="tpu_custom_call" | custom-call | flops 1 | bytes 1 | tf_op jit(solution)/shard_map/prepare/pallas_call | solution.py:517
  2.6 3.0 %collective-permute-start = (f32[16,4,16,128]{3,2,1,0:T(8,128)S(1)}, f32[16,4,16,128]{3,2,1,0:T(8,128)S(1)}, u32[]{:S(2)}, u32[]{:S(2)}) collective-permute-start(f32[16,4,16,128]{3,2,1,0:T(8,128)S(1)} %get-tuple-element.52), channel_id=1, source_target_pairs={{0,4},{4,0},{8,12},{12,8},{16,20},{20,16},{24,28},{28,24},{1,5},{5... | collective-permute-start | bytes 1572872 | tf_op jit(solution)/shard_map/ppermute | solution.py:577
  5.6 2.6 %collective-permute-start.3 = (f32[512,128]{1,0:T(8,128)S(1)}, f32[512,128]{1,0:T(8,128)S(1)}, u32[]{:S(2)}, u32[]{:S(2)}) collective-permute-start(f32[512,128]{1,0:T(8,128)S(1)} %get-tuple-element.58.refs_5_.refs_3_), channel_id=1, source_target_pairs={{0,16},{4,20},{8,24},{12,28},{16,0},{20,4},{24,8},{28,12},{1,17},{... | collective-permute-start | bytes 786440 | tf_op jit(solution)/shard_map/ppermute | solution.py:616
  8.2 1.6 %collective-permute-start.2 = (f32[512,128]{1,0:T(8,128)S(1)}, f32[512,128]{1,0:T(8,128)S(1)}, u32[]{:S(2)}, u32[]{:S(2)}) collective-permute-start(f32[512,128]{1,0:T(8,128)S(1)} %get-tuple-element.58.refs_5_.refs_3_), channel_id=1, source_target_pairs={{0,8},{4,12},{8,0},{12,4},{16,24},{20,28},{24,16},{28,20},{1,9},{5... | collective-permute-start | bytes 786440 | tf_op jit(solution)/shard_map/ppermute | solution.py:616
  9.8 0.5 collective-permute-start.1
  10.3 3.8 %gradient_own.1 = (bf16[8,512,512]{2,1,0:T(8,128)(2,1)S(1)}, bf16[8,2,256,256]{3,2,1,0:T(8,128)(2,1)S(1)}, f32[8,128,256]{2,1,0:T(8,128)S(1)}, bf16[512,768]{1,0:T(8,128)(2,1)S(1)}, bf16[512,512]{1,0:T(8,128)(2,1)}) custom-call(f32[1024,128]{1,0:T(8,128)S(1)} %get-tuple-element.48.refs_0_, f32[16,4,16,128]{3,2,1,0:T(8,128)S(1)} %get-tuple-element.49.refs_1_, ...), custom_call_target="tpu_custom_call" | custom-call | flops 1 | bytes 1 | tf_op jit(solution)/shard_map/gradient_own/pallas_call | solution.py:517
  14.1 4.3 %collective-permute-done.refs_1_ = f32[16,4,16,128]{3,2,1,0:T(8,128)S(1)} collective-permute-done((f32[16,4,16,128]{3,2,1,0:T(8,128)S(1)}, f32[16,4,16,128]{3,2,1,0:T(8,128)S(1)}, u32[]{:S(2)}, u32[]{:S(2)}) %collective-permute-start) | collective-permute-done | bytes 524320 | tf_op jit(solution)/shard_map/ppermute | solution.py:577
  18.4 1.8 %gradient_peer.1 = (bf16[8,512,512]{2,1,0:T(8,128)(2,1)S(1)}, bf16[8,2,256,256]{3,2,1,0:T(8,128)(2,1)S(1)}) custom-call(bf16[512,768]{1,0:T(8,128)(2,1)S(1)} %get-tuple-element.51.refs_0_, f32[16,4,16,128]{3,2,1,0:T(8,128)S(1)} %collective-permute-done.refs_1_), custom_call_target="tpu_custom_call" | custom-call | flops 1 | bytes 1 | tf_op jit(solution)/shard_map/gradient_peer/pallas_call | solution.py:517
  20.2 0.0 collective-permute-done.3.refs_7_.refs_5_
  20.2 2.2 %collective-permute-start.4 = (f32[512,128]{1,0:T(8,128)S(1)}, f32[512,128]{1,0:T(8,128)S(1)}, u32[]{:S(2)}, u32[]{:S(2)}) collective-permute-start(f32[512,128]{1,0:T(8,128)S(1)} %collective-permute-done.3.refs_7_.refs_5_), channel_id=1, source_target_pairs={{0,8},{4,12},{8,0},{12,4},{16,24},{20,28},{24,16},{28,20},{1,9},{5... | collective-permute-start | bytes 786440 | tf_op jit(solution)/shard_map/ppermute | solution.py:616
  22.4 0.7 collective-permute-done.1.refs_1_.refs_2_
  23.2 1.9 %right_parts.1 = (f32[2,512,128]{2,1,0:T(8,128)S(1)}, f32[2,512,128]{2,1,0:T(8,128)}) custom-call(bf16[8,512,512]{2,1,0:T(8,128)(2,1)S(1)} %get-tuple-element.53.refs_0_.refs_2_, f32[512,128]{1,0:T(8,128)S(1)} %collective-permute-done.1.refs_1_.refs_2_, f32[8,128,256]{2,1,0:T(8,128)S(1)} %get-tuple-element.54.refs_2_), custom_call_target="tpu_custom_call" | custom-call | flops 1 | bytes 1 | tf_op jit(solution)/shard_map/right_parts/pallas_call | solution.py:517
  25.1 2.8 %collective-permute-start.6 = (f32[2,512,128]{2,1,0:T(8,128)}, f32[2,512,128]{2,1,0:T(8,128)S(1)}, u32[]{:S(2)}, u32[]{:S(2)}) collective-permute-start(f32[2,512,128]{2,1,0:T(8,128)} %get-tuple-element.75), channel_id=1, source_target_pairs={{0,16},{4,20},{8,24},{12,28},{16,0},{20,4},{24,8},{28,12},{1,17},{... | collective-permute-start | bytes 1572872 | tf_op jit(solution)/shard_map/ppermute | solution.py:626
  27.9 0.0 collective-permute-done.2.refs_6_.refs_4_
  27.9 0.0 collective-permute-done.4.refs_8_.refs_6_
  27.9 10.6 %weight.1 = (f32[512,128]{1,0:T(8,128)S(1)}, f32[512,128]{1,0:T(8,128)S(1)}, bf16[8,512,512]{2,1,0:T(8,128)(2,1)}, bf16[8,512,512]{2,1,0:T(8,128)(2,1)}) custom-call(f32[2,512,128]{2,1,0:T(8,128)S(1)} %get-tuple-element.55.refs_0_.refs_1_, f32[512,128]{1,0:T(8,128)S(1)} %get-tuple-element.50.refs_2_.refs_1_, ...), custom_call_target="tpu_custom_call" | custom-call | flops 12884901888 | bytes 1 | tf_op jit(solution)/shard_map/weight/pallas_call | solution.py:517
  38.6 0.1 collective-permute-start.5
  38.6 3.2 %left_parts.1 = (f32[2,32,512]{2,1,0:T(8,128)S(1)}, f32[2,32,512]{2,1,0:T(8,128)}, f32[2,32,512]{2,1,0:T(8,128)}, f32[2,32,512]{2,1,0:T(8,128)S(1)}) custom-call(f32[512,128]{1,0:T(8,128)S(1)} %get-tuple-element.66.refs_0_, bf16[8,512,512]{2,1,0:T(8,128)(2,1)S(1)} %get-tuple-element.61.refs_1_, bf16[8,512,512]{2,1,0:T(8,128)(2,1)S(1)} %get-tuple-element.53.refs_0_.refs_2_, ...), custom_call_target="tpu_custom_call" | custom-call | flops 6442450944 | bytes 1 | tf_op jit(solution)/shard_map/left_parts/pallas_call | solution.py:517
  41.8 0.0 collective-permute-done.5
  41.8 0.7 add.3
  42.5 6.2 %all-to-all-start = ((f32[16,32,128]{2,1,0:T(8,128)}), f32[16,32,128]{2,1,0:T(8,128)S(1)}, u32[]{:S(2)}, u32[]{:S(2)}) async-start(f32[16,32,128]{2,1,0:T(8,128)} %bitcast.1.refs_0_), calls=%async_computation | async-start | bytes 524288 | tf_op jit(solution)/shard_map/all_to_all | solution.py:691
  48.7 0.3 collective-permute-start.9
  49.0 1.7 %collective-permute-start.10 = (f32[2,32,512]{2,1,0:T(8,128)}, f32[2,32,512]{2,1,0:T(8,128)S(1)}, u32[]{:S(2)}, u32[]{:S(2)}) collective-permute-start(f32[2,32,512]{2,1,0:T(8,128)} %get-tuple-element.81), channel_id=1, source_target_pairs={{0,2},{1,3},{2,0},{3,1},{4,6},{5,7},{6,4},{7,5},{8,10},{9,11},{10,... | collective-permute-start | bytes 393224 | tf_op jit(solution)/shard_map/ppermute | solution.py:677
  50.7 0.1 collective-permute-start.11
  50.8 5.0 %pair_peer.1.refs_0_ = f32[16,4,16,128]{3,2,1,0:T(8,128)S(1)} custom-call(f32[16,32,128]{2,1,0:T(8,128)} %bitcast.1.refs_0_, bf16[8,512,512]{2,1,0:T(8,128)(2,1)} %get-tuple-element.73.refs_1_, bf16[512,512]{1,0:T(8,128)(2,1)} %get-tuple-element.74.refs_2_), custom_call_target="tpu_custom_call" | custom-call | flops 6442450944 | bytes 1 | tf_op jit(solution)/shard_map/pair_peer/pallas_call | solution.py:517
  55.8 1.8 %collective-permute-start.7 = (f32[16,4,16,128]{3,2,1,0:T(8,128)S(1)}, f32[16,4,16,128]{3,2,1,0:T(8,128)S(1)}, u32[]{:S(2)}, u32[]{:S(2)}) collective-permute-start(f32[16,4,16,128]{3,2,1,0:T(8,128)S(1)} %pair_peer.1.refs_0_), channel_id=1, source_target_pairs={{0,4},{4,0},{8,12},{12,8},{16,20},{20,16},{24,28},{28,24},{1,5},{5... | collective-permute-start | bytes 1572872 | tf_op jit(solution)/shard_map/ppermute | solution.py:681
  57.5 0.0 collective-permute-done.6.refs_2_
  57.5 0.1 right_halve.1
  57.6 1.5 %collective-permute-start.8 = (f32[1,512,128]{2,1,0:T(8,128)S(1)}, f32[1,512,128]{2,1,0:T(8,128)S(1)}, u32[]{:S(2)}, u32[]{:S(2)}) collective-permute-start(f32[1,512,128]{2,1,0:T(8,128)S(1)} %get-tuple-element.78), channel_id=1, source_target_pairs={{0,8},{4,12},{8,0},{12,4},{16,24},{20,28},{24,16},{28,20},{1,9},{5... | collective-permute-start | bytes 786440 | tf_op jit(solution)/shard_map/ppermute | solution.py:688
  59.1 0.2 all-to-all-done.refs_2_
  59.4 0.8 weight_sum.1.refs_0_
  60.1 4.4 %all-to-all-start.1 = ((f32[16,32,128]{2,1,0:T(8,128)}), f32[16,32,128]{2,1,0:T(8,128)S(1)}, u32[]{:S(2)}, u32[]{:S(2)}) async-start(f32[16,32,128]{2,1,0:T(8,128)} %weight_sum.1.refs_0_), calls=%async_computation.1 | async-start | bytes 524288 | tf_op jit(solution)/shard_map/all_to_all | solution.py:702
  64.5 0.0 collective-permute-done.9.refs_2_
  64.6 0.0 collective-permute-done.10.refs_3_
  64.6 0.0 collective-permute-done.11.refs_4_
  64.6 2.0 %collective-permute-start.12 = (f32[32,512]{1,0:T(8,128)S(1)}, f32[32,512]{1,0:T(8,128)S(1)}, u32[]{:S(2)}, u32[]{:S(2)}) collective-permute-start(f32[32,512]{1,0:T(8,128)S(1)} %get-tuple-element.84), channel_id=1, source_target_pairs={{0,4},{4,0},{8,12},{12,8},{16,20},{20,16},{24,28},{28,24},{1,5},{5... | collective-permute-start | bytes 196616 | tf_op jit(solution)/shard_map/ppermute | solution.py:704
  66.6 5.0 %pair_own.1.refs_0_ = f32[16,4,16,128]{3,2,1,0:T(8,128)S(1)} custom-call(f32[16,32,128]{2,1,0:T(8,128)} %weight_sum.1.refs_0_, bf16[8,512,512]{2,1,0:T(8,128)(2,1)} %get-tuple-element.77.refs_1_, bf16[512,512]{1,0:T(8,128)(2,1)} %get-tuple-element.74.refs_2_), custom_call_target="tpu_custom_call" | custom-call | flops 6442450944 | bytes 1 | tf_op jit(solution)/shard_map/pair_own/pallas_call | solution.py:517
  71.6 0.0 collective-permute-done.8.refs_3_
  71.6 0.9 %collective-permute-done.7.refs_1_ = f32[16,4,16,128]{3,2,1,0:T(8,128)S(1)} collective-permute-done((f32[16,4,16,128]{3,2,1,0:T(8,128)S(1)}, f32[16,4,16,128]{3,2,1,0:T(8,128)S(1)}, u32[]{:S(2)}, u32[]{:S(2)}) %collective-permute-start.7) | collective-permute-done | bytes 524320 | tf_op jit(solution)/shard_map/ppermute | solution.py:681
  72.5 1.9 %collective-permute-done.12.refs_5_ = f32[32,512]{1,0:T(8,128)S(1)} collective-permute-done((f32[32,512]{1,0:T(8,128)S(1)}, f32[32,512]{1,0:T(8,128)S(1)}, u32[]{:S(2)}, u32[]{:S(2)}) %collective-permute-start.12) | collective-permute-done | bytes 65568 | tf_op jit(solution)/shard_map/ppermute | solution.py:704
  74.4 2.2 %finish.1 = (f32[16,4,2,16,128]{4,3,2,1,0:T(8,128)}, f32[16,1024]{1,0:T(8,128)}, f32[16,4096]{1,0:T(8,128)}) custom-call(f32[16,4,16,128]{3,2,1,0:T(8,128)S(1)} %pair_own.1.refs_0_, f32[16,4,16,128]{3,2,1,0:T(8,128)S(1)} %collective-permute-done.7.refs_1_, f32[1,512,128]{2,1,0:T(8,128)S(1)} %get-tuple-element.76.refs_1_.refs_2_, ...), custom_call_target="tpu_custom_call" | custom-call | flops 1 | bytes 1 | tf_op jit(solution)/shard_map/finish/pallas_call | solution.py:517
  76.5 0.0 all-to-all-done.1
  76.5 0.1 collective-permute-start.13
  76.6 1.5 %collective-permute-done.13.refs_1_ = f32[512,128]{1,0:T(8,128)S(1)} collective-permute-done((f32[512,128]{1,0:T(8,128)S(1)}, f32[512,128]{1,0:T(8,128)S(1)}, u32[]{:S(2)}, u32[]{:S(2)}) %collective-permute-start.13) | collective-permute-done | bytes 262176 | tf_op jit(solution)/shard_map/ppermute | solution.py:729
  78.1 1.1 %place.1 = f32[1024,128]{1,0:T(8,128)} custom-call(f32[512,128]{1,0:T(8,128)S(1)} %bitcast.5, f32[512,128]{1,0:T(8,128)S(1)} %collective-permute-done.13.refs_1_), custom_call_target="tpu_custom_call" | custom-call | flops 1 | bytes 1 | tf_op jit(solution)/shard_map/place/pallas_call | solution.py:517
  (1 shorter events, 0.0 us)
Async XLA Ops:
  2.6 15.8 %collective-permute-start = (f32[16,4,16,128]{3,2,1,0:T(8,128)S(1)}, f32[16,4,16,128]{3,2,1,0:T(8,128)S(1)}, u32[]{:S(2)}, u32[]{:S(2)}) collective-permute-start(f32[16,4,16,128]{3,2,1,0:T(8,128)S(1)} %get-tuple-element.52), channel_id=1, source_target_pairs={{0,4},{4,0},{8,12},{12,8},{16,20},{20,16},{24,28},{28,24},{1,5},{5... | collective-permute-start | bytes 1572872 | tf_op jit(solution)/shard_map/ppermute | solution.py:577
  5.6 14.6 %collective-permute-start.3 = (f32[512,128]{1,0:T(8,128)S(1)}, f32[512,128]{1,0:T(8,128)S(1)}, u32[]{:S(2)}, u32[]{:S(2)}) collective-permute-start(f32[512,128]{1,0:T(8,128)S(1)} %get-tuple-element.58.refs_5_.refs_3_), channel_id=1, source_target_pairs={{0,16},{4,20},{8,24},{12,28},{16,0},{20,4},{24,8},{28,12},{1,17},{... | collective-permute-start | bytes 786440 | tf_op jit(solution)/shard_map/ppermute | solution.py:616
  8.2 19.7 %collective-permute-start.2 = (f32[512,128]{1,0:T(8,128)S(1)}, f32[512,128]{1,0:T(8,128)S(1)}, u32[]{:S(2)}, u32[]{:S(2)}) collective-permute-start(f32[512,128]{1,0:T(8,128)S(1)} %get-tuple-element.58.refs_5_.refs_3_), channel_id=1, source_target_pairs={{0,8},{4,12},{8,0},{12,4},{16,24},{20,28},{24,16},{28,20},{1,9},{5... | collective-permute-start | bytes 786440 | tf_op jit(solution)/shard_map/ppermute | solution.py:616
  9.8 13.4 %collective-permute-start.1 = (f32[512,128]{1,0:T(8,128)S(1)}, f32[512,128]{1,0:T(8,128)S(1)}, u32[]{:S(2)}, u32[]{:S(2)}) collective-permute-start(f32[512,128]{1,0:T(8,128)S(1)} %get-tuple-element.50.refs_2_.refs_1_), channel_id=1, source_target_pairs={{0,4},{4,0},{8,12},{12,8},{16,20},{20,16},{24,28},{28,24},{1,5},{5... | collective-permute-start | bytes 786440 | tf_op jit(solution)/shard_map/ppermute | solution.py:578
  20.2 7.7 %collective-permute-start.4 = (f32[512,128]{1,0:T(8,128)S(1)}, f32[512,128]{1,0:T(8,128)S(1)}, u32[]{:S(2)}, u32[]{:S(2)}) collective-permute-start(f32[512,128]{1,0:T(8,128)S(1)} %collective-permute-done.3.refs_7_.refs_5_), channel_id=1, source_target_pairs={{0,8},{4,12},{8,0},{12,4},{16,24},{20,28},{24,16},{28,20},{1,9},{5... | collective-permute-start | bytes 786440 | tf_op jit(solution)/shard_map/ppermute | solution.py:616
  25.1 32.4 %collective-permute-start.6 = (f32[2,512,128]{2,1,0:T(8,128)}, f32[2,512,128]{2,1,0:T(8,128)S(1)}, u32[]{:S(2)}, u32[]{:S(2)}) collective-permute-start(f32[2,512,128]{2,1,0:T(8,128)} %get-tuple-element.75), channel_id=1, source_target_pairs={{0,16},{4,20},{8,24},{12,28},{16,0},{20,4},{24,8},{28,12},{1,17},{... | collective-permute-start | bytes 1572872 | tf_op jit(solution)/shard_map/ppermute | solution.py:626
  38.6 3.2 %collective-permute-start.5 = (f32[512,128]{1,0:T(8,128)S(1)}, f32[512,128]{1,0:T(8,128)S(1)}, u32[]{:S(2)}, u32[]{:S(2)}) collective-permute-start(f32[512,128]{1,0:T(8,128)S(1)} %get-tuple-element.67), channel_id=1, source_target_pairs={{0,1},{1,0},{2,3},{3,2},{4,5},{5,4},{6,7},{7,6},{8,9},{9,8},{10,11... | collective-permute-start | bytes 786440 | tf_op jit(solution)/shard_map/ppermute | solution.py:642
  42.5 16.8 %all-to-all-start = ((f32[16,32,128]{2,1,0:T(8,128)}), f32[16,32,128]{2,1,0:T(8,128)S(1)}, u32[]{:S(2)}, u32[]{:S(2)}) async-start(f32[16,32,128]{2,1,0:T(8,128)} %bitcast.1.refs_0_), calls=%async_computation | async-start | bytes 524288 | tf_op jit(solution)/shard_map/all_to_all | solution.py:691
  48.7 15.8 %collective-permute-start.9 = (f32[2,32,512]{2,1,0:T(8,128)}, f32[2,32,512]{2,1,0:T(8,128)S(1)}, u32[]{:S(2)}, u32[]{:S(2)}) collective-permute-start(f32[2,32,512]{2,1,0:T(8,128)} %get-tuple-element.80), channel_id=1, source_target_pairs={{0,1},{1,0},{2,3},{3,2},{4,5},{5,4},{6,7},{7,6},{8,9},{9,8},{10,11... | collective-permute-start | bytes 393224 | tf_op jit(solution)/shard_map/ppermute | solution.py:677
  49.0 15.6 %collective-permute-start.10 = (f32[2,32,512]{2,1,0:T(8,128)}, f32[2,32,512]{2,1,0:T(8,128)S(1)}, u32[]{:S(2)}, u32[]{:S(2)}) collective-permute-start(f32[2,32,512]{2,1,0:T(8,128)} %get-tuple-element.81), channel_id=1, source_target_pairs={{0,2},{1,3},{2,0},{3,1},{4,6},{5,7},{6,4},{7,5},{8,10},{9,11},{10,... | collective-permute-start | bytes 393224 | tf_op jit(solution)/shard_map/ppermute | solution.py:677
  50.7 13.9 %collective-permute-start.11 = (f32[2,32,512]{2,1,0:T(8,128)S(1)}, f32[2,32,512]{2,1,0:T(8,128)S(1)}, u32[]{:S(2)}, u32[]{:S(2)}) collective-permute-start(f32[2,32,512]{2,1,0:T(8,128)S(1)} %get-tuple-element.82), channel_id=1, source_target_pairs={{0,3},{1,2},{2,1},{3,0},{4,7},{5,6},{6,5},{7,4},{8,11},{9,10},{10,... | collective-permute-start | bytes 393224 | tf_op jit(solution)/shard_map/ppermute | solution.py:677
  55.8 16.7 %collective-permute-start.7 = (f32[16,4,16,128]{3,2,1,0:T(8,128)S(1)}, f32[16,4,16,128]{3,2,1,0:T(8,128)S(1)}, u32[]{:S(2)}, u32[]{:S(2)}) collective-permute-start(f32[16,4,16,128]{3,2,1,0:T(8,128)S(1)} %pair_peer.1.refs_0_), channel_id=1, source_target_pairs={{0,4},{4,0},{8,12},{12,8},{16,20},{20,16},{24,28},{28,24},{1,5},{5... | collective-permute-start | bytes 1572872 | tf_op jit(solution)/shard_map/ppermute | solution.py:681
  57.6 14.0 %collective-permute-start.8 = (f32[1,512,128]{2,1,0:T(8,128)S(1)}, f32[1,512,128]{2,1,0:T(8,128)S(1)}, u32[]{:S(2)}, u32[]{:S(2)}) collective-permute-start(f32[1,512,128]{2,1,0:T(8,128)S(1)} %get-tuple-element.78), channel_id=1, source_target_pairs={{0,8},{4,12},{8,0},{12,4},{16,24},{20,28},{24,16},{28,20},{1,9},{5... | collective-permute-start | bytes 786440 | tf_op jit(solution)/shard_map/ppermute | solution.py:688
  60.1 16.4 %all-to-all-start.1 = ((f32[16,32,128]{2,1,0:T(8,128)}), f32[16,32,128]{2,1,0:T(8,128)S(1)}, u32[]{:S(2)}, u32[]{:S(2)}) async-start(f32[16,32,128]{2,1,0:T(8,128)} %weight_sum.1.refs_0_), calls=%async_computation.1 | async-start | bytes 524288 | tf_op jit(solution)/shard_map/all_to_all | solution.py:702
  64.6 9.8 %collective-permute-start.12 = (f32[32,512]{1,0:T(8,128)S(1)}, f32[32,512]{1,0:T(8,128)S(1)}, u32[]{:S(2)}, u32[]{:S(2)}) collective-permute-start(f32[32,512]{1,0:T(8,128)S(1)} %get-tuple-element.84), channel_id=1, source_target_pairs={{0,4},{4,0},{8,12},{12,8},{16,20},{20,16},{24,28},{28,24},{1,5},{5... | collective-permute-start | bytes 196616 | tf_op jit(solution)/shard_map/ppermute | solution.py:704
  76.5 1.6 %collective-permute-start.13 = (f32[512,128]{1,0:T(8,128)S(1)}, f32[512,128]{1,0:T(8,128)S(1)}, u32[]{:S(2)}, u32[]{:S(2)}) collective-permute-start(f32[512,128]{1,0:T(8,128)S(1)} %bitcast.4), channel_id=1, source_target_pairs={{0,1},{1,0},{2,3},{3,2},{4,5},{5,4},{6,7},{7,6},{8,9},{9,8},{10,11... | collective-permute-start | bytes 786440 | tf_op jit(solution)/shard_map/ppermute | solution.py:729

commit v21 on v20

--- a/solution.py
+++ b/solution.py
@@ -208,7 +208,7 @@
     def store(step, found):
         partial_ref[step] = found
 
-    right_phase(left_ref, out_ref, left_flip, store)
+    right_phase(left_ref, out_ref, left_flip, store, 8)
     channels = ENTRY_CHANNELS
     wide = weight_rows.shape[1]
     for step in range(channels // fold):
@@ -227,7 +227,7 @@
     gradient_phase(blocks, cotangent_ref, out_ref, spread_ref, weight_cat)
 
 
-def right_phase(left_ref, factor_ref, left_flip, store):
+def right_phase(left_ref, factor_ref, left_flip, store, unroll):
     sequences = left_ref.shape[1]
     lanes = factor_ref.shape[2] // 4
     flip_high, flip_low = halves((left_ref[...] * (1.0 / sequences)).T)
@@ -246,7 +246,8 @@
         store(step, first[:sequences] + first[sequences:] + second)
         return carry
 
-    lax.fori_loop(0, factor_ref.shape[1] // (2 * ENTRY_CHANNELS), step_of, 0, unroll=8)
+    count = factor_ref.shape[1] // (2 * ENTRY_CHANNELS)
+    lax.fori_loop(0, count, step_of, 0, unroll=unroll)
 
 
 def rows_of_step(refs, step, half, lanes):
@@ -288,7 +289,7 @@
                         start : start + depth
                     ]
 
-    right_phase(left_ref, peer_ref, left_flip, store)
+    right_phase(left_ref, peer_ref, left_flip, store, 4)
 
 
 def halve_kernel(keep_ref, found_ref, keep_out, send_out):
@@ -347,7 +348,7 @@
             copy.start()
         return carry
 
-    lax.fori_loop(0, channels // (2 * fold), outer_step, 0, unroll=8)
+    lax.fori_loop(0, channels // (2 * fold), outer_step, 0, unroll=4)
     total[...] = jnp.zeros_like(total)
 
     def weight_step(pair, carry):
@@ -359,7 +360,7 @@
         total[...] += dot(jnp.concatenate(lefts, 1), jnp.concatenate(rights, 0))
         return carry
 
-    lax.fori_loop(0, own_ref.shape[0], weight_step, 0, unroll=8)
+    lax.fori_loop(0, own_ref.shape[0], weight_step, 0, unroll=4)
     core = lax.rem(lax.axis_index("inner"), 2)
     steps = channels // (2 * fold)
     for out_ref, half in ((keep_ref, core), (send_ref, 1 - core)):
@@ -672,13 +673,13 @@
             flops=work,
         )(values, weight_flip)
 
-    pieces, *left_parts = lax.optimization_barrier((pieces, *left_parts))
+    pair_other = pair(outer_peer, [pieces], "pair_peer")
+    pair_found = lax.ppermute(pair_other, "blk", partner)
+    _, *left_parts = lax.optimization_barrier((pair_other, *left_parts))
     left_parts = [
         lax.ppermute(part, "inner", inner_moves[slot]) if slot else part
         for slot, part in enumerate(left_parts)
     ]
-    pair_other = pair(outer_peer, [pieces], "pair_peer")
-    pair_found = lax.ppermute(pair_other, "blk", partner)
     slot = blocks // 4
     while slot:
         part = shape(slot, channels * depth, sequences)

time: 79.6 us -> 77 us (0.967)
  Pallas kernels: 37.3 us -> 34.6 us
    pallas_call x13, Pallas kernels: 37.3 us -> 34.6 us  [run(): pl.pallas_call(lambda *refs: kernel(*refs[len(after):]), out_shape=out_sh...]
    all_to_all x2, waiting for transfers between devices: 0.24 us -> 2.55 us  [local(): lax.all_to_all(pieces, everyone, 0, 0, axis_index_groups=core_groups)]
    ppermute x1, waiting for transfers between devices: 1.86 us -> 0.01 us  [local(): left_found = [left_own, lax.ppermute(left_send, 'blk', partner)]]
    ppermute x1, waiting for transfers between devices: 0.92 us -> 0.01 us  [local(): pair_found = lax.ppermute(pair_other, 'blk', partner)]
  transfers between devices with their start and end apart: 16 -> 16, of which waited for: 6 -> 6; matrix products, arithmetic and copies ran while one was open for 1% -> 1% of each run, Pallas kernels for 43% -> 41%
where the time goes in v21:
time: 77 us; the launch traced here: 76.6 us
  Pallas kernels  34.6 us (45%)
  starting transfers between devices  30.6 us (40%)
  waiting for transfers between devices  9.85 us (13%)
  between operations  0.79 us (1%)
    pallas_call x13, Pallas kernels, run(): pl.pallas_call(lambda *refs: kernel(*refs[len(after):]), out_shape=out_sh...  34.6 us
    all_to_all x2, starting transfers between devices, local(): lax.all_to_all(pieces, everyone, 0, 0, axis_index_groups=core_groups)  11.2 us
    ppermute x3, starting transfers between devices, local(): rights[slot + distance] = lax.ppermute(sent, 'blk', slot_moves[distance])  6.35 us
    ppermute x1, waiting for transfers between devices, local(): cotangent_peer = lax.ppermute(cotangent_send, 'blk', partner)  4.3 us
    ppermute x1, starting transfers between devices, local(): cotangent_peer = lax.ppermute(cotangent_send, 'blk', partner)  3.03 us
    ppermute x1, starting transfers between devices, local(): right_send = lax.ppermute(right_send, 'blk', slot_moves[blocks // 2])  2.8 us
    all_to_all x2, waiting for transfers between devices, local(): lax.all_to_all(pieces, everyone, 0, 0, axis_index_groups=core_groups)  2.55 us
    ppermute x3, starting transfers between devices, local(): lax.ppermute(part, 'inner', inner_moves[slot])  2.13 us
  transfers between devices with their start and end apart: 16, of which 6 were waited for; matrix products, arithmetic and copies ran while one was open for 1% of the time, Pallas kernels for 41%

profile of v21, /device:TPU:0, one launch (start us, length us, event | category | flops | bytes accessed | tf_op | source)
XLA Modules:
  0.0 76.6 jit_solution(3503716726527527339)
XLA Ops:
  0.6 2.0 %prepare.1 = (f32[512,128]{1,0:T(8,128)S(1)}, f32[512,128]{1,0:T(8,128)S(1)}, f32[16,4,16,128]{3,2,1,0:T(8,128)S(1)}, f32[16,4,16,128]{3,2,1,0:T(8,128)S(1)}, f32[1024,128]{1,0:T(8,128)S(1)}) custom-call(f32[16,4,2,16,128]{4,3,2,1,0:T(8,128)} %bitcast.6, f32[16,4096]{1,0:T(8,128)} %refs_1_.1, f32[16,4096]{1,0:T(8,128)} %refs_2_.1, f32[1024,128]{1,0:T(8,128)} %refs_3_.1), custom_call_target="tpu_custom_call" | custom-call | flops 1 | bytes 1 | tf_op jit(solution)/shard_map/prepare/pallas_call | solution.py:518
  2.6 3.0 %collective-permute-start = (f32[16,4,16,128]{3,2,1,0:T(8,128)S(1)}, f32[16,4,16,128]{3,2,1,0:T(8,128)S(1)}, u32[]{:S(2)}, u32[]{:S(2)}) collective-permute-start(f32[16,4,16,128]{3,2,1,0:T(8,128)S(1)} %get-tuple-element.51), channel_id=1, source_target_pairs={{0,4},{4,0},{8,12},{12,8},{16,20},{20,16},{24,28},{28,24},{1,5},{5... | collective-permute-start | bytes 1572872 | tf_op jit(solution)/shard_map/ppermute | solution.py:578
  5.6 2.6 %collective-permute-start.3 = (f32[512,128]{1,0:T(8,128)S(1)}, f32[512,128]{1,0:T(8,128)S(1)}, u32[]{:S(2)}, u32[]{:S(2)}) collective-permute-start(f32[512,128]{1,0:T(8,128)S(1)} %get-tuple-element.57.refs_5_.refs_3_), channel_id=1, source_target_pairs={{0,16},{4,20},{8,24},{12,28},{16,0},{20,4},{24,8},{28,12},{1,17},{... | collective-permute-start | bytes 786440 | tf_op jit(solution)/shard_map/ppermute | solution.py:617
  8.2 1.6 %collective-permute-start.2 = (f32[512,128]{1,0:T(8,128)S(1)}, f32[512,128]{1,0:T(8,128)S(1)}, u32[]{:S(2)}, u32[]{:S(2)}) collective-permute-start(f32[512,128]{1,0:T(8,128)S(1)} %get-tuple-element.57.refs_5_.refs_3_), channel_id=1, source_target_pairs={{0,8},{4,12},{8,0},{12,4},{16,24},{20,28},{24,16},{28,20},{1,9},{5... | collective-permute-start | bytes 786440 | tf_op jit(solution)/shard_map/ppermute | solution.py:617
  9.8 0.5 collective-permute-start.1
  10.3 3.8 %gradient_own.1 = (bf16[8,512,512]{2,1,0:T(8,128)(2,1)S(1)}, bf16[8,2,256,256]{3,2,1,0:T(8,128)(2,1)S(1)}, f32[8,128,256]{2,1,0:T(8,128)S(1)}, bf16[512,768]{1,0:T(8,128)(2,1)S(1)}, bf16[512,512]{1,0:T(8,128)(2,1)}) custom-call(f32[1024,128]{1,0:T(8,128)S(1)} %get-tuple-element.47.refs_0_, f32[16,4,16,128]{3,2,1,0:T(8,128)S(1)} %get-tuple-element.48.refs_1_, ...), custom_call_target="tpu_custom_call" | custom-call | flops 1 | bytes 1 | tf_op jit(solution)/shard_map/gradient_own/pallas_call | solution.py:518
  14.1 4.3 %collective-permute-done.refs_1_ = f32[16,4,16,128]{3,2,1,0:T(8,128)S(1)} collective-permute-done((f32[16,4,16,128]{3,2,1,0:T(8,128)S(1)}, f32[16,4,16,128]{3,2,1,0:T(8,128)S(1)}, u32[]{:S(2)}, u32[]{:S(2)}) %collective-permute-start) | collective-permute-done | bytes 524320 | tf_op jit(solution)/shard_map/ppermute | solution.py:578
  18.4 1.8 %gradient_peer.1 = (bf16[8,512,512]{2,1,0:T(8,128)(2,1)S(1)}, bf16[8,2,256,256]{3,2,1,0:T(8,128)(2,1)S(1)}) custom-call(bf16[512,768]{1,0:T(8,128)(2,1)S(1)} %get-tuple-element.50.refs_0_, f32[16,4,16,128]{3,2,1,0:T(8,128)S(1)} %collective-permute-done.refs_1_), custom_call_target="tpu_custom_call" | custom-call | flops 1 | bytes 1 | tf_op jit(solution)/shard_map/gradient_peer/pallas_call | solution.py:518
  20.2 0.0 collective-permute-done.3.refs_7_.refs_5_
  20.3 2.2 %collective-permute-start.4 = (f32[512,128]{1,0:T(8,128)S(1)}, f32[512,128]{1,0:T(8,128)S(1)}, u32[]{:S(2)}, u32[]{:S(2)}) collective-permute-start(f32[512,128]{1,0:T(8,128)S(1)} %collective-permute-done.3.refs_7_.refs_5_), channel_id=1, source_target_pairs={{0,8},{4,12},{8,0},{12,4},{16,24},{20,28},{24,16},{28,20},{1,9},{5... | collective-permute-start | bytes 786440 | tf_op jit(solution)/shard_map/ppermute | solution.py:617
  22.4 0.7 collective-permute-done.1.refs_1_.refs_2_
  23.2 2.3 %right_parts.1 = (f32[2,512,128]{2,1,0:T(8,128)S(1)}, f32[2,512,128]{2,1,0:T(8,128)}) custom-call(bf16[8,512,512]{2,1,0:T(8,128)(2,1)S(1)} %get-tuple-element.52.refs_0_.refs_2_, f32[512,128]{1,0:T(8,128)S(1)} %collective-permute-done.1.refs_1_.refs_2_, f32[8,128,256]{2,1,0:T(8,128)S(1)} %get-tuple-element.53.refs_2_), custom_call_target="tpu_custom_call" | custom-call | flops 1 | bytes 1 | tf_op jit(solution)/shard_map/right_parts/pallas_call | solution.py:518
  25.5 2.8 %collective-permute-start.6 = (f32[2,512,128]{2,1,0:T(8,128)}, f32[2,512,128]{2,1,0:T(8,128)S(1)}, u32[]{:S(2)}, u32[]{:S(2)}) collective-permute-start(f32[2,512,128]{2,1,0:T(8,128)} %get-tuple-element.69), channel_id=1, source_target_pairs={{0,16},{4,20},{8,24},{12,28},{16,0},{20,4},{24,8},{28,12},{1,17},{... | collective-permute-start | bytes 1572872 | tf_op jit(solution)/shard_map/ppermute | solution.py:627
  28.3 0.0 collective-permute-done.2.refs_6_.refs_4_
  28.3 0.0 collective-permute-done.4.refs_8_.refs_6_
  28.3 7.5 %weight.1 = (f32[512,128]{1,0:T(8,128)S(1)}, f32[512,128]{1,0:T(8,128)S(1)}, bf16[8,512,512]{2,1,0:T(8,128)(2,1)}, bf16[8,512,512]{2,1,0:T(8,128)(2,1)}) custom-call(f32[2,512,128]{2,1,0:T(8,128)S(1)} %get-tuple-element.54.refs_0_.refs_1_, f32[512,128]{1,0:T(8,128)S(1)} %get-tuple-element.49.refs_2_.refs_1_, ...), custom_call_target="tpu_custom_call" | custom-call | flops 12884901888 | bytes 1 | tf_op jit(solution)/shard_map/weight/pallas_call | solution.py:518
  35.8 0.1 collective-permute-start.5
  35.9 3.2 %left_parts.1 = (f32[2,32,512]{2,1,0:T(8,128)S(1)}, f32[2,32,512]{2,1,0:T(8,128)}, f32[2,32,512]{2,1,0:T(8,128)}, f32[2,32,512]{2,1,0:T(8,128)S(1)}) custom-call(f32[512,128]{1,0:T(8,128)S(1)} %get-tuple-element.65.refs_0_, bf16[8,512,512]{2,1,0:T(8,128)(2,1)S(1)} %get-tuple-element.60.refs_1_, bf16[8,512,512]{2,1,0:T(8,128)(2,1)S(1)} %get-tuple-element.52.refs_0_.refs_2_, ...), custom_call_target="tpu_custom_call" | custom-call | flops 6442450944 | bytes 1 | tf_op jit(solution)/shard_map/left_parts/pallas_call | solution.py:518
  39.1 0.0 collective-permute-done.5
  39.1 0.7 add.3
  39.8 5.8 %all-to-all-start = ((f32[16,32,128]{2,1,0:T(8,128)}), f32[16,32,128]{2,1,0:T(8,128)S(1)}, u32[]{:S(2)}, u32[]{:S(2)}) async-start(f32[16,32,128]{2,1,0:T(8,128)} %bitcast.1.refs_0_), calls=%async_computation | async-start | bytes 524288 | tf_op jit(solution)/shard_map/all_to_all | solution.py:692
  45.6 5.0 %pair_peer.1.refs_0_ = f32[16,4,16,128]{3,2,1,0:T(8,128)S(1)} custom-call(f32[16,32,128]{2,1,0:T(8,128)} %bitcast.1.refs_0_, bf16[8,512,512]{2,1,0:T(8,128)(2,1)} %get-tuple-element.67.refs_1_, bf16[512,512]{1,0:T(8,128)(2,1)} %get-tuple-element.68.refs_2_), custom_call_target="tpu_custom_call" | custom-call | flops 6442450944 | bytes 1 | tf_op jit(solution)/shard_map/pair_peer/pallas_call | solution.py:518
  50.6 0.3 collective-permute-start.9
  50.9 1.8 %collective-permute-start.10 = (f32[2,32,512]{2,1,0:T(8,128)}, f32[2,32,512]{2,1,0:T(8,128)S(1)}, u32[]{:S(2)}, u32[]{:S(2)}) collective-permute-start(f32[2,32,512]{2,1,0:T(8,128)} %get-tuple-element.79), channel_id=1, source_target_pairs={{0,2},{1,3},{2,0},{3,1},{4,6},{5,7},{6,4},{7,5},{8,10},{9,11},{10,... | collective-permute-start | bytes 393224 | tf_op jit(solution)/shard_map/ppermute | solution.py:680
  52.7 0.1 collective-permute-start.11
  52.7 1.7 %collective-permute-start.7 = (f32[16,4,16,128]{3,2,1,0:T(8,128)S(1)}, f32[16,4,16,128]{3,2,1,0:T(8,128)S(1)}, u32[]{:S(2)}, u32[]{:S(2)}) collective-permute-start(f32[16,4,16,128]{3,2,1,0:T(8,128)S(1)} %pair_peer.1.refs_0_), channel_id=1, source_target_pairs={{0,4},{4,0},{8,12},{12,8},{16,20},{20,16},{24,28},{28,24},{1,5},{5... | collective-permute-start | bytes 1572872 | tf_op jit(solution)/shard_map/ppermute | solution.py:677
  54.5 0.7 collective-permute-done.6.refs_2_
  55.2 0.1 right_halve.1
  55.2 0.8 %collective-permute-start.8 = (f32[1,512,128]{2,1,0:T(8,128)S(1)}, f32[1,512,128]{2,1,0:T(8,128)S(1)}, u32[]{:S(2)}, u32[]{:S(2)}) collective-permute-start(f32[1,512,128]{2,1,0:T(8,128)S(1)} %get-tuple-element.72), channel_id=1, source_target_pairs={{0,8},{4,12},{8,0},{12,4},{16,24},{20,28},{24,16},{28,20},{1,9},{5... | collective-permute-start | bytes 786440 | tf_op jit(solution)/shard_map/ppermute | solution.py:689
  56.1 1.9 %all-to-all-done.refs_2_ = f32[16,32,128]{2,1,0:T(8,128)S(1)} async-done(((f32[16,32,128]{2,1,0:T(8,128)}), f32[16,32,128]{2,1,0:T(8,128)S(1)}, u32[]{:S(2)}, u32[]{:S(2)}) %all-to-all-start) | async-done | bytes 262176 | tf_op jit(solution)/shard_map/all_to_all | solution.py:692
  58.0 0.8 weight_sum.1.refs_0_
  58.7 5.4 %all-to-all-start.1 = ((f32[16,32,128]{2,1,0:T(8,128)}), f32[16,32,128]{2,1,0:T(8,128)S(1)}, u32[]{:S(2)}, u32[]{:S(2)}) async-start(f32[16,32,128]{2,1,0:T(8,128)} %weight_sum.1.refs_0_), calls=%async_computation.1 | async-start | bytes 524288 | tf_op jit(solution)/shard_map/all_to_all | solution.py:703
  64.1 0.0 collective-permute-done.9.refs_2_
  64.1 0.0 collective-permute-done.10.refs_3_
  64.1 0.0 collective-permute-done.11.refs_4_
  64.2 2.0 %collective-permute-start.12 = (f32[32,512]{1,0:T(8,128)S(1)}, f32[32,512]{1,0:T(8,128)S(1)}, u32[]{:S(2)}, u32[]{:S(2)}) collective-permute-start(f32[32,512]{1,0:T(8,128)S(1)} %get-tuple-element.82), channel_id=1, source_target_pairs={{0,4},{4,0},{8,12},{12,8},{16,20},{20,16},{24,28},{28,24},{1,5},{5... | collective-permute-start | bytes 196616 | tf_op jit(solution)/shard_map/ppermute | solution.py:705
  66.2 5.0 %pair_own.1.refs_0_ = f32[16,4,16,128]{3,2,1,0:T(8,128)S(1)} custom-call(f32[16,32,128]{2,1,0:T(8,128)} %weight_sum.1.refs_0_, bf16[8,512,512]{2,1,0:T(8,128)(2,1)} %get-tuple-element.71.refs_1_, bf16[512,512]{1,0:T(8,128)(2,1)} %get-tuple-element.68.refs_2_), custom_call_target="tpu_custom_call" | custom-call | flops 6442450944 | bytes 1 | tf_op jit(solution)/shard_map/pair_own/pallas_call | solution.py:518
  71.1 0.0 collective-permute-done.8.refs_3_
  71.2 0.0 collective-permute-done.7.refs_1_
  71.2 0.0 collective-permute-done.12.refs_5_
  71.2 2.2 %finish.1 = (f32[16,4,2,16,128]{4,3,2,1,0:T(8,128)}, f32[16,1024]{1,0:T(8,128)}, f32[16,4096]{1,0:T(8,128)}) custom-call(f32[16,4,16,128]{3,2,1,0:T(8,128)S(1)} %pair_own.1.refs_0_, f32[16,4,16,128]{3,2,1,0:T(8,128)S(1)} %collective-permute-done.7.refs_1_, f32[1,512,128]{2,1,0:T(8,128)S(1)} %get-tuple-element.70.refs_1_.refs_2_, ...), custom_call_target="tpu_custom_call" | custom-call | flops 1 | bytes 1 | tf_op jit(solution)/shard_map/finish/pallas_call | solution.py:518
  73.3 0.6 all-to-all-done.1
  74.0 0.0 collective-permute-start.13
  74.0 1.5 %collective-permute-done.13.refs_1_ = f32[512,128]{1,0:T(8,128)S(1)} collective-permute-done((f32[512,128]{1,0:T(8,128)S(1)}, f32[512,128]{1,0:T(8,128)S(1)}, u32[]{:S(2)}, u32[]{:S(2)}) %collective-permute-start.13) | collective-permute-done | bytes 262176 | tf_op jit(solution)/shard_map/ppermute | solution.py:730
  75.5 1.1 %place.1 = f32[1024,128]{1,0:T(8,128)} custom-call(f32[512,128]{1,0:T(8,128)S(1)} %bitcast.5, f32[512,128]{1,0:T(8,128)S(1)} %collective-permute-done.13.refs_1_), custom_call_target="tpu_custom_call" | custom-call | flops 1 | bytes 1 | tf_op jit(solution)/shard_map/place/pallas_call | solution.py:518
  (1 shorter events, 0.0 us)
Async XLA Ops:
  2.6 15.8 %collective-permute-start = (f32[16,4,16,128]{3,2,1,0:T(8,128)S(1)}, f32[16,4,16,128]{3,2,1,0:T(8,128)S(1)}, u32[]{:S(2)}, u32[]{:S(2)}) collective-permute-start(f32[16,4,16,128]{3,2,1,0:T(8,128)S(1)} %get-tuple-element.51), channel_id=1, source_target_pairs={{0,4},{4,0},{8,12},{12,8},{16,20},{20,16},{24,28},{28,24},{1,5},{5... | collective-permute-start | bytes 1572872 | tf_op jit(solution)/shard_map/ppermute | solution.py:578
  5.6 14.6 %collective-permute-start.3 = (f32[512,128]{1,0:T(8,128)S(1)}, f32[512,128]{1,0:T(8,128)S(1)}, u32[]{:S(2)}, u32[]{:S(2)}) collective-permute-start(f32[512,128]{1,0:T(8,128)S(1)} %get-tuple-element.57.refs_5_.refs_3_), channel_id=1, source_target_pairs={{0,16},{4,20},{8,24},{12,28},{16,0},{20,4},{24,8},{28,12},{1,17},{... | collective-permute-start | bytes 786440 | tf_op jit(solution)/shard_map/ppermute | solution.py:617
  8.2 20.1 %collective-permute-start.2 = (f32[512,128]{1,0:T(8,128)S(1)}, f32[512,128]{1,0:T(8,128)S(1)}, u32[]{:S(2)}, u32[]{:S(2)}) collective-permute-start(f32[512,128]{1,0:T(8,128)S(1)} %get-tuple-element.57.refs_5_.refs_3_), channel_id=1, source_target_pairs={{0,8},{4,12},{8,0},{12,4},{16,24},{20,28},{24,16},{28,20},{1,9},{5... | collective-permute-start | bytes 786440 | tf_op jit(solution)/shard_map/ppermute | solution.py:617
  9.8 13.4 %collective-permute-start.1 = (f32[512,128]{1,0:T(8,128)S(1)}, f32[512,128]{1,0:T(8,128)S(1)}, u32[]{:S(2)}, u32[]{:S(2)}) collective-permute-start(f32[512,128]{1,0:T(8,128)S(1)} %get-tuple-element.49.refs_2_.refs_1_), channel_id=1, source_target_pairs={{0,4},{4,0},{8,12},{12,8},{16,20},{20,16},{24,28},{28,24},{1,5},{5... | collective-permute-start | bytes 786440 | tf_op jit(solution)/shard_map/ppermute | solution.py:579
  20.3 8.0 %collective-permute-start.4 = (f32[512,128]{1,0:T(8,128)S(1)}, f32[512,128]{1,0:T(8,128)S(1)}, u32[]{:S(2)}, u32[]{:S(2)}) collective-permute-start(f32[512,128]{1,0:T(8,128)S(1)} %collective-permute-done.3.refs_7_.refs_5_), channel_id=1, source_target_pairs={{0,8},{4,12},{8,0},{12,4},{16,24},{20,28},{24,16},{28,20},{1,9},{5... | collective-permute-start | bytes 786440 | tf_op jit(solution)/shard_map/ppermute | solution.py:617
  25.5 29.7 %collective-permute-start.6 = (f32[2,512,128]{2,1,0:T(8,128)}, f32[2,512,128]{2,1,0:T(8,128)S(1)}, u32[]{:S(2)}, u32[]{:S(2)}) collective-permute-start(f32[2,512,128]{2,1,0:T(8,128)} %get-tuple-element.69), channel_id=1, source_target_pairs={{0,16},{4,20},{8,24},{12,28},{16,0},{20,4},{24,8},{28,12},{1,17},{... | collective-permute-start | bytes 1572872 | tf_op jit(solution)/shard_map/ppermute | solution.py:627
  35.8 3.2 %collective-permute-start.5 = (f32[512,128]{1,0:T(8,128)S(1)}, f32[512,128]{1,0:T(8,128)S(1)}, u32[]{:S(2)}, u32[]{:S(2)}) collective-permute-start(f32[512,128]{1,0:T(8,128)S(1)} %get-tuple-element.66), channel_id=1, source_target_pairs={{0,1},{1,0},{2,3},{3,2},{4,5},{5,4},{6,7},{7,6},{8,9},{9,8},{10,11... | collective-permute-start | bytes 786440 | tf_op jit(solution)/shard_map/ppermute | solution.py:643
  39.8 18.2 %all-to-all-start = ((f32[16,32,128]{2,1,0:T(8,128)}), f32[16,32,128]{2,1,0:T(8,128)S(1)}, u32[]{:S(2)}, u32[]{:S(2)}) async-start(f32[16,32,128]{2,1,0:T(8,128)} %bitcast.1.refs_0_), calls=%async_computation | async-start | bytes 524288 | tf_op jit(solution)/shard_map/all_to_all | solution.py:692
  50.6 13.5 %collective-permute-start.9 = (f32[2,32,512]{2,1,0:T(8,128)}, f32[2,32,512]{2,1,0:T(8,128)S(1)}, u32[]{:S(2)}, u32[]{:S(2)}) collective-permute-start(f32[2,32,512]{2,1,0:T(8,128)} %get-tuple-element.78), channel_id=1, source_target_pairs={{0,1},{1,0},{2,3},{3,2},{4,5},{5,4},{6,7},{7,6},{8,9},{9,8},{10,11... | collective-permute-start | bytes 393224 | tf_op jit(solution)/shard_map/ppermute | solution.py:680
  50.9 13.2 %collective-permute-start.10 = (f32[2,32,512]{2,1,0:T(8,128)}, f32[2,32,512]{2,1,0:T(8,128)S(1)}, u32[]{:S(2)}, u32[]{:S(2)}) collective-permute-start(f32[2,32,512]{2,1,0:T(8,128)} %get-tuple-element.79), channel_id=1, source_target_pairs={{0,2},{1,3},{2,0},{3,1},{4,6},{5,7},{6,4},{7,5},{8,10},{9,11},{10,... | collective-permute-start | bytes 393224 | tf_op jit(solution)/shard_map/ppermute | solution.py:680
  52.7 11.5 %collective-permute-start.11 = (f32[2,32,512]{2,1,0:T(8,128)S(1)}, f32[2,32,512]{2,1,0:T(8,128)S(1)}, u32[]{:S(2)}, u32[]{:S(2)}) collective-permute-start(f32[2,32,512]{2,1,0:T(8,128)S(1)} %get-tuple-element.80), channel_id=1, source_target_pairs={{0,3},{1,2},{2,1},{3,0},{4,7},{5,6},{6,5},{7,4},{8,11},{9,10},{10,... | collective-permute-start | bytes 393224 | tf_op jit(solution)/shard_map/ppermute | solution.py:680
  52.7 18.4 %collective-permute-start.7 = (f32[16,4,16,128]{3,2,1,0:T(8,128)S(1)}, f32[16,4,16,128]{3,2,1,0:T(8,128)S(1)}, u32[]{:S(2)}, u32[]{:S(2)}) collective-permute-start(f32[16,4,16,128]{3,2,1,0:T(8,128)S(1)} %pair_peer.1.refs_0_), channel_id=1, source_target_pairs={{0,4},{4,0},{8,12},{12,8},{16,20},{20,16},{24,28},{28,24},{1,5},{5... | collective-permute-start | bytes 1572872 | tf_op jit(solution)/shard_map/ppermute | solution.py:677
  55.2 15.9 %collective-permute-start.8 = (f32[1,512,128]{2,1,0:T(8,128)S(1)}, f32[1,512,128]{2,1,0:T(8,128)S(1)}, u32[]{:S(2)}, u32[]{:S(2)}) collective-permute-start(f32[1,512,128]{2,1,0:T(8,128)S(1)} %get-tuple-element.72), channel_id=1, source_target_pairs={{0,8},{4,12},{8,0},{12,4},{16,24},{20,28},{24,16},{28,20},{1,9},{5... | collective-permute-start | bytes 786440 | tf_op jit(solution)/shard_map/ppermute | solution.py:689
  58.7 15.2 %all-to-all-start.1 = ((f32[16,32,128]{2,1,0:T(8,128)}), f32[16,32,128]{2,1,0:T(8,128)S(1)}, u32[]{:S(2)}, u32[]{:S(2)}) async-start(f32[16,32,128]{2,1,0:T(8,128)} %weight_sum.1.refs_0_), calls=%async_computation.1 | async-start | bytes 524288 | tf_op jit(solution)/shard_map/all_to_all | solution.py:703
  64.2 7.0 %collective-permute-start.12 = (f32[32,512]{1,0:T(8,128)S(1)}, f32[32,512]{1,0:T(8,128)S(1)}, u32[]{:S(2)}, u32[]{:S(2)}) collective-permute-start(f32[32,512]{1,0:T(8,128)S(1)} %get-tuple-element.82), channel_id=1, source_target_pairs={{0,4},{4,0},{8,12},{12,8},{16,20},{20,16},{24,28},{28,24},{1,5},{5... | collective-permute-start | bytes 196616 | tf_op jit(solution)/shard_map/ppermute | solution.py:705
  74.0 1.5 %collective-permute-start.13 = (f32[512,128]{1,0:T(8,128)S(1)}, f32[512,128]{1,0:T(8,128)S(1)}, u32[]{:S(2)}, u32[]{:S(2)}) collective-permute-start(f32[512,128]{1,0:T(8,128)S(1)} %bitcast.4), channel_id=1, source_target_pairs={{0,1},{1,0},{2,3},{3,2},{4,5},{5,4},{6,7},{7,6},{8,9},{9,8},{10,11... | collective-permute-start | bytes 786440 | tf_op jit(solution)/shard_map/ppermute | solution.py:730

commit v22 on v21

--- a/solution.py
+++ b/solution.py
@@ -284,19 +284,16 @@
                 for slot in range(blocks):
                     start = (place * blocks + slot) * depth
                     row = pl.multiple_of(((2 * step + part) * fold + place) * depth, depth)
-                    out_ref = keep_ref if slot < blocks // 2 else send_ref
-                    out_ref[slot % (blocks // 2), pl.ds(row, depth), :] = turned[
-                        start : start + depth
-                    ]
+                    out_ref = send_ref if slot % 2 else keep_ref
+                    out_ref[slot // 2, pl.ds(row, depth), :] = turned[start : start + depth]
 
     right_phase(left_ref, peer_ref, left_flip, store, 4)
 
 
 def halve_kernel(keep_ref, found_ref, keep_out, send_out):
-    half = keep_ref.shape[0] // 2
-    for slot in range(half):
-        keep_out[slot] = keep_ref[slot] + found_ref[slot]
-        send_out[slot] = keep_ref[half + slot] + found_ref[half + slot]
+    for slot in range(keep_ref.shape[0]):
+        out_ref = send_out if slot % 2 else keep_out
+        out_ref[slot // 2] = keep_ref[slot] + found_ref[slot]
 
 
 def right_rows(right_refs, step, fold, depth):
@@ -624,7 +621,7 @@
         [flip_scratch],
         "right_parts",
     )(grad_peer, left_peer, partial)
-    right_send = lax.ppermute(right_send, "blk", slot_moves[blocks // 2])
+    right_send = lax.ppermute(right_send, "blk", slot_moves[1])
 
     keep, send, outer_own, outer_peer = large(
         functools.partial(weight_kernel, blocks, depth),
@@ -654,7 +651,15 @@
         after=[keep],
         flops=work,
     )(grad_own, grad_peer, *rights)
-    keep, *left_parts = lax.optimization_barrier((keep, *left_parts))
+    slot = 2
+    while slot < blocks:
+        part = shape(blocks // (2 * slot), channels * depth, sequences)
+        right_keep, right_send = call(
+            halve_kernel, [part, part], name="right_halve", after=[left_parts[0]]
+        )(right_keep, right_send)
+        right_send = lax.ppermute(right_send, "blk", slot_moves[slot])
+        slot = 2 * slot
+    keep, right_keep, *left_parts = lax.optimization_barrier((keep, right_keep, *left_parts))
     members = count * inner // 2
     pieces = (keep + sent).reshape(members, outer // 2 // members, pairs)
 
@@ -680,21 +685,12 @@
         lax.ppermute(part, "inner", inner_moves[slot]) if slot else part
         for slot, part in enumerate(left_parts)
     ]
-    slot = blocks // 4
-    while slot:
-        part = shape(slot, channels * depth, sequences)
-        right_keep, right_send = call(
-            halve_kernel, [part, part], name="right_halve", after=[pair_other]
-        )(right_keep, right_send)
-        right_send = lax.ppermute(right_send, "blk", slot_moves[slot])
-        slot = slot // 2
-
     pieces = lax.all_to_all(pieces, everyone, 0, 0, axis_index_groups=core_groups)
     pieces = call(
         spread_sum_kernel,
         shape(*pieces.shape),
         name="weight_sum",
-        after=[pair_other, right_keep],
+        after=[pair_other],
     )(pieces)
     pair_own = pair(outer_own, [pieces], "pair_own")
     left_own, left_send = call(

time: 77 us -> 79 us (1.026)
  waiting for transfers between devices: 9.85 us -> 13.1 us
  Pallas kernels: 34.6 us -> 33.1 us
    ppermute x1, waiting for transfers between devices: 0.01 us -> 4.58 us  [local(): right_send = lax.ppermute(right_send, 'blk', slot_moves[slot])]
    all_to_all x2, waiting for transfers between devices: 2.55 us -> 0.18 us  [local(): lax.all_to_all(pieces, everyone, 0, 0, axis_index_groups=core_groups)]
    ppermute x1, starting transfers between devices: 0.82 us -> 2.37 us  [local(): right_send = lax.ppermute(right_send, 'blk', slot_moves[slot])]
    pallas_call x13, Pallas kernels: 34.6 us -> 33.1 us  [run(): pl.pallas_call(lambda *refs: kernel(*refs[len(after):]), out_shape=out_sh...]
    ppermute x3, waiting for transfers between devices: 0.01 us -> 1 us  [local(): rights[slot + distance] = lax.ppermute(sent, 'blk', slot_moves[distance])]
    ppermute x1, starting transfers between devices: 2.8 us -> 1.86 us  [local(): right_send = lax.ppermute(right_send, 'blk', slot_moves[1])]
  transfers between devices with their start and end apart: 16 -> 16, of which waited for: 6 -> 7; matrix products, arithmetic and copies ran while one was open for 1% -> 0% of each run, Pallas kernels for 41% -> 38%
where the time goes in v22:
time: 79 us; the launch traced here: 78.6 us
  Pallas kernels  33.1 us (42%)
  starting transfers between devices  30.9 us (39%)
  waiting for transfers between devices  13.1 us (17%)
  between operations  0.79 us (1%)
    pallas_call x13, Pallas kernels, run(): pl.pallas_call(lambda *refs: kernel(*refs[len(after):]), out_shape=out_sh...  33.1 us
    all_to_all x2, starting transfers between devices, local(): lax.all_to_all(pieces, everyone, 0, 0, axis_index_groups=core_groups)  10.9 us
    ppermute x3, starting transfers between devices, local(): rights[slot + distance] = lax.ppermute(sent, 'blk', slot_moves[distance])  6.36 us
    ppermute x1, waiting for transfers between devices, local(): right_send = lax.ppermute(right_send, 'blk', slot_moves[slot])  4.58 us
    ppermute x1, waiting for transfers between devices, local(): cotangent_peer = lax.ppermute(cotangent_send, 'blk', partner)  4.3 us
    ppermute x1, starting transfers between devices, local(): cotangent_peer = lax.ppermute(cotangent_send, 'blk', partner)  3.03 us
    ppermute x1, starting transfers between devices, local(): right_send = lax.ppermute(right_send, 'blk', slot_moves[slot])  2.37 us
    ppermute x3, starting transfers between devices, local(): lax.ppermute(part, 'inner', inner_moves[slot])  2.13 us
  transfers between devices with their start and end apart: 16, of which 7 were waited for; matrix products, arithmetic and copies ran while one was open for 0% of the time, Pallas kernels for 38%

profile of v22, /device:TPU:0, one launch (start us, length us, event | category | flops | bytes accessed | tf_op | source)
XLA Modules:
  0.0 78.6 jit_solution(6218403994005830615)
XLA Ops:
  0.6 2.0 %prepare.1 = (f32[512,128]{1,0:T(8,128)S(1)}, f32[512,128]{1,0:T(8,128)S(1)}, f32[16,4,16,128]{3,2,1,0:T(8,128)S(1)}, f32[16,4,16,128]{3,2,1,0:T(8,128)S(1)}, f32[1024,128]{1,0:T(8,128)S(1)}) custom-call(f32[16,4,2,16,128]{4,3,2,1,0:T(8,128)} %bitcast.6, f32[16,4096]{1,0:T(8,128)} %refs_1_.1, f32[16,4096]{1,0:T(8,128)} %refs_2_.1, f32[1024,128]{1,0:T(8,128)} %refs_3_.1), custom_call_target="tpu_custom_call" | custom-call | flops 1 | bytes 1 | tf_op jit(solution)/shard_map/prepare/pallas_call | solution.py:515
  2.6 3.0 %collective-permute-start = (f32[16,4,16,128]{3,2,1,0:T(8,128)S(1)}, f32[16,4,16,128]{3,2,1,0:T(8,128)S(1)}, u32[]{:S(2)}, u32[]{:S(2)}) collective-permute-start(f32[16,4,16,128]{3,2,1,0:T(8,128)S(1)} %get-tuple-element.52), channel_id=1, source_target_pairs={{0,4},{4,0},{8,12},{12,8},{16,20},{20,16},{24,28},{28,24},{1,5},{5... | collective-permute-start | bytes 1572872 | tf_op jit(solution)/shard_map/ppermute | solution.py:575
  5.6 2.6 %collective-permute-start.3 = (f32[512,128]{1,0:T(8,128)S(1)}, f32[512,128]{1,0:T(8,128)S(1)}, u32[]{:S(2)}, u32[]{:S(2)}) collective-permute-start(f32[512,128]{1,0:T(8,128)S(1)} %get-tuple-element.58.refs_5_.refs_3_), channel_id=1, source_target_pairs={{0,16},{4,20},{8,24},{12,28},{16,0},{20,4},{24,8},{28,12},{1,17},{... | collective-permute-start | bytes 786440 | tf_op jit(solution)/shard_map/ppermute | solution.py:614
  8.2 1.6 %collective-permute-start.2 = (f32[512,128]{1,0:T(8,128)S(1)}, f32[512,128]{1,0:T(8,128)S(1)}, u32[]{:S(2)}, u32[]{:S(2)}) collective-permute-start(f32[512,128]{1,0:T(8,128)S(1)} %get-tuple-element.58.refs_5_.refs_3_), channel_id=1, source_target_pairs={{0,8},{4,12},{8,0},{12,4},{16,24},{20,28},{24,16},{28,20},{1,9},{5... | collective-permute-start | bytes 786440 | tf_op jit(solution)/shard_map/ppermute | solution.py:614
  9.8 0.5 collective-permute-start.1
  10.3 3.8 %gradient_own.1 = (bf16[8,512,512]{2,1,0:T(8,128)(2,1)S(1)}, bf16[8,2,256,256]{3,2,1,0:T(8,128)(2,1)S(1)}, f32[8,128,256]{2,1,0:T(8,128)S(1)}, bf16[512,768]{1,0:T(8,128)(2,1)S(1)}, bf16[512,512]{1,0:T(8,128)(2,1)}) custom-call(f32[1024,128]{1,0:T(8,128)S(1)} %get-tuple-element.48.refs_0_, f32[16,4,16,128]{3,2,1,0:T(8,128)S(1)} %get-tuple-element.49.refs_1_, ...), custom_call_target="tpu_custom_call" | custom-call | flops 1 | bytes 1 | tf_op jit(solution)/shard_map/gradient_own/pallas_call | solution.py:515
  14.1 4.3 %collective-permute-done.refs_1_ = f32[16,4,16,128]{3,2,1,0:T(8,128)S(1)} collective-permute-done((f32[16,4,16,128]{3,2,1,0:T(8,128)S(1)}, f32[16,4,16,128]{3,2,1,0:T(8,128)S(1)}, u32[]{:S(2)}, u32[]{:S(2)}) %collective-permute-start) | collective-permute-done | bytes 524320 | tf_op jit(solution)/shard_map/ppermute | solution.py:575
  18.4 1.8 %gradient_peer.1 = (bf16[8,512,512]{2,1,0:T(8,128)(2,1)S(1)}, bf16[8,2,256,256]{3,2,1,0:T(8,128)(2,1)S(1)}) custom-call(bf16[512,768]{1,0:T(8,128)(2,1)S(1)} %get-tuple-element.51.refs_0_, f32[16,4,16,128]{3,2,1,0:T(8,128)S(1)} %collective-permute-done.refs_1_), custom_call_target="tpu_custom_call" | custom-call | flops 1 | bytes 1 | tf_op jit(solution)/shard_map/gradient_peer/pallas_call | solution.py:515
  20.2 0.0 collective-permute-done.3.refs_7_.refs_5_
  20.3 2.2 %collective-permute-start.4 = (f32[512,128]{1,0:T(8,128)S(1)}, f32[512,128]{1,0:T(8,128)S(1)}, u32[]{:S(2)}, u32[]{:S(2)}) collective-permute-start(f32[512,128]{1,0:T(8,128)S(1)} %collective-permute-done.3.refs_7_.refs_5_), channel_id=1, source_target_pairs={{0,8},{4,12},{8,0},{12,4},{16,24},{20,28},{24,16},{28,20},{1,9},{5... | collective-permute-start | bytes 786440 | tf_op jit(solution)/shard_map/ppermute | solution.py:614
  22.4 0.7 collective-permute-done.1.refs_1_.refs_2_
  23.2 1.5 %right_parts.1 = (f32[2,512,128]{2,1,0:T(8,128)S(1)}, f32[2,512,128]{2,1,0:T(8,128)S(1)}) custom-call(bf16[8,512,512]{2,1,0:T(8,128)(2,1)S(1)} %get-tuple-element.53.refs_0_.refs_2_, f32[512,128]{1,0:T(8,128)S(1)} %collective-permute-done.1.refs_1_.refs_2_, f32[8,128,256]{2,1,0:T(8,128)S(1)} %get-tuple-element.54.refs_2_), custom_call_target="tpu_custom_call" | custom-call | flops 1 | bytes 1 | tf_op jit(solution)/shard_map/right_parts/pallas_call | solution.py:515
  24.7 1.9 %collective-permute-start.5 = (f32[2,512,128]{2,1,0:T(8,128)S(1)}, f32[2,512,128]{2,1,0:T(8,128)S(1)}, u32[]{:S(2)}, u32[]{:S(2)}) collective-permute-start(f32[2,512,128]{2,1,0:T(8,128)S(1)} %get-tuple-element.63), channel_id=1, source_target_pairs={{0,8},{4,12},{8,0},{12,4},{16,24},{20,28},{24,16},{28,20},{1,9},{5... | collective-permute-start | bytes 1572872 | tf_op jit(solution)/shard_map/ppermute | solution.py:624
  26.6 0.0 collective-permute-done.2.refs_6_.refs_4_
  26.6 1.0 %collective-permute-done.4.refs_8_.refs_6_ = f32[512,128]{1,0:T(8,128)S(1)} collective-permute-done((f32[512,128]{1,0:T(8,128)S(1)}, f32[512,128]{1,0:T(8,128)S(1)}, u32[]{:S(2)}, u32[]{:S(2)}) %collective-permute-start.4) | collective-permute-done | bytes 262176 | tf_op jit(solution)/shard_map/ppermute | solution.py:614
  27.5 7.5 %weight.1 = (f32[512,128]{1,0:T(8,128)S(1)}, f32[512,128]{1,0:T(8,128)S(1)}, bf16[8,512,512]{2,1,0:T(8,128)(2,1)}, bf16[8,512,512]{2,1,0:T(8,128)(2,1)}) custom-call(f32[2,512,128]{2,1,0:T(8,128)S(1)} %get-tuple-element.55.refs_0_.refs_1_, f32[512,128]{1,0:T(8,128)S(1)} %get-tuple-element.50.refs_2_.refs_1_, ...), custom_call_target="tpu_custom_call" | custom-call | flops 12884901888 | bytes 1 | tf_op jit(solution)/shard_map/weight/pallas_call | solution.py:515
  35.1 0.1 collective-permute-start.6
  35.2 2.4 %left_parts.1 = (f32[2,32,512]{2,1,0:T(8,128)S(1)}, f32[2,32,512]{2,1,0:T(8,128)S(1)}, f32[2,32,512]{2,1,0:T(8,128)S(1)}, f32[2,32,512]{2,1,0:T(8,128)S(1)}) custom-call(f32[512,128]{1,0:T(8,128)S(1)} %get-tuple-element.68.refs_0_, bf16[8,512,512]{2,1,0:T(8,128)(2,1)S(1)} %get-tuple-element.61.refs_1_, ...), custom_call_target="tpu_custom_call" | custom-call | flops 6442450944 | bytes 1 | tf_op jit(solution)/shard_map/left_parts/pallas_call | solution.py:515
  37.6 0.7 collective-permute-done.5.refs_2_
  38.4 0.1 right_halve.1
  38.4 0.0 collective-permute-done.6
  38.4 0.7 add.3
  39.2 7.1 %all-to-all-start = ((f32[16,32,128]{2,1,0:T(8,128)}), f32[16,32,128]{2,1,0:T(8,128)S(1)}, u32[]{:S(2)}, u32[]{:S(2)}) async-start(f32[16,32,128]{2,1,0:T(8,128)} %bitcast.1.refs_0_), calls=%async_computation | async-start | bytes 524288 | tf_op jit(solution)/shard_map/all_to_all | solution.py:688
  46.3 5.0 %pair_peer.1.refs_0_ = f32[16,4,16,128]{3,2,1,0:T(8,128)S(1)} custom-call(f32[16,32,128]{2,1,0:T(8,128)} %bitcast.1.refs_0_, bf16[8,512,512]{2,1,0:T(8,128)(2,1)} %get-tuple-element.70.refs_1_, bf16[512,512]{1,0:T(8,128)(2,1)} %get-tuple-element.71.refs_2_), custom_call_target="tpu_custom_call" | custom-call | flops 6442450944 | bytes 1 | tf_op jit(solution)/shard_map/pair_peer/pallas_call | solution.py:515
  51.3 0.3 collective-permute-start.9
  51.5 1.8 %collective-permute-start.10 = (f32[2,32,512]{2,1,0:T(8,128)S(1)}, f32[2,32,512]{2,1,0:T(8,128)S(1)}, u32[]{:S(2)}, u32[]{:S(2)}) collective-permute-start(f32[2,32,512]{2,1,0:T(8,128)S(1)} %get-tuple-element.81), channel_id=1, source_target_pairs={{0,2},{1,3},{2,0},{3,1},{4,6},{5,7},{6,4},{7,5},{8,10},{9,11},{10,... | collective-permute-start | bytes 393224 | tf_op jit(solution)/shard_map/ppermute | solution.py:685
  53.3 0.1 collective-permute-start.11
  53.4 1.7 %collective-permute-start.7 = (f32[16,4,16,128]{3,2,1,0:T(8,128)S(1)}, f32[16,4,16,128]{3,2,1,0:T(8,128)S(1)}, u32[]{:S(2)}, u32[]{:S(2)}) collective-permute-start(f32[16,4,16,128]{3,2,1,0:T(8,128)S(1)} %pair_peer.1.refs_0_), channel_id=1, source_target_pairs={{0,4},{4,0},{8,12},{12,8},{16,20},{20,16},{24,28},{28,24},{1,5},{5... | collective-permute-start | bytes 1572872 | tf_op jit(solution)/shard_map/ppermute | solution.py:682
  55.1 2.4 %collective-permute-start.8 = (f32[1,512,128]{2,1,0:T(8,128)S(1)}, f32[1,512,128]{2,1,0:T(8,128)S(1)}, u32[]{:S(2)}, u32[]{:S(2)}) collective-permute-start(f32[1,512,128]{2,1,0:T(8,128)S(1)} %get-tuple-element.74), channel_id=1, source_target_pairs={{0,16},{4,20},{8,24},{12,28},{16,0},{20,4},{24,8},{28,12},{1,17},{... | collective-permute-start | bytes 786440 | tf_op jit(solution)/shard_map/ppermute | solution.py:660
  57.5 0.0 all-to-all-done.refs_1_
  57.5 0.8 weight_sum.1.refs_0_
  58.2 3.7 %all-to-all-start.1 = ((f32[16,32,128]{2,1,0:T(8,128)}), f32[16,32,128]{2,1,0:T(8,128)S(1)}, u32[]{:S(2)}, u32[]{:S(2)}) async-start(f32[16,32,128]{2,1,0:T(8,128)} %weight_sum.1.refs_0_), calls=%async_computation.1 | async-start | bytes 524288 | tf_op jit(solution)/shard_map/all_to_all | solution.py:699
  62.0 0.0 collective-permute-done.9.refs_2_
  62.0 0.0 collective-permute-done.10.refs_3_
  62.0 0.0 collective-permute-done.11.refs_4_
  62.1 2.0 %collective-permute-start.12 = (f32[32,512]{1,0:T(8,128)S(1)}, f32[32,512]{1,0:T(8,128)S(1)}, u32[]{:S(2)}, u32[]{:S(2)}) collective-permute-start(f32[32,512]{1,0:T(8,128)S(1)} %get-tuple-element.84), channel_id=1, source_target_pairs={{0,4},{4,0},{8,12},{12,8},{16,20},{20,16},{24,28},{28,24},{1,5},{5... | collective-permute-start | bytes 196616 | tf_op jit(solution)/shard_map/ppermute | solution.py:701
  64.1 5.0 %pair_own.1.refs_0_ = f32[16,4,16,128]{3,2,1,0:T(8,128)S(1)} custom-call(f32[16,32,128]{2,1,0:T(8,128)} %weight_sum.1.refs_0_, bf16[8,512,512]{2,1,0:T(8,128)(2,1)} %get-tuple-element.72.refs_1_, bf16[512,512]{1,0:T(8,128)(2,1)} %get-tuple-element.71.refs_2_), custom_call_target="tpu_custom_call" | custom-call | flops 6442450944 | bytes 1 | tf_op jit(solution)/shard_map/pair_own/pallas_call | solution.py:515
  69.0 4.6 %collective-permute-done.8.refs_3_ = f32[1,512,128]{2,1,0:T(8,128)S(1)} collective-permute-done((f32[1,512,128]{2,1,0:T(8,128)S(1)}, f32[1,512,128]{2,1,0:T(8,128)S(1)}, u32[]{:S(2)}, u32[]{:S(2)}) %collective-permute-start.8) | collective-permute-done | bytes 262176 | tf_op jit(solution)/shard_map/ppermute | solution.py:660
  73.6 0.0 collective-permute-done.7.refs_1_
  73.6 0.0 collective-permute-done.12.refs_5_
  73.6 2.2 %finish.1 = (f32[16,4,2,16,128]{4,3,2,1,0:T(8,128)}, f32[16,1024]{1,0:T(8,128)}, f32[16,4096]{1,0:T(8,128)}) custom-call(f32[16,4,16,128]{3,2,1,0:T(8,128)S(1)} %pair_own.1.refs_0_, f32[16,4,16,128]{3,2,1,0:T(8,128)S(1)} %collective-permute-done.7.refs_1_, f32[1,512,128]{2,1,0:T(8,128)S(1)} %get-tuple-element.73.refs_2_, ...), custom_call_target="tpu_custom_call" | custom-call | flops 1 | bytes 1 | tf_op jit(solution)/shard_map/finish/pallas_call | solution.py:515
  75.8 0.2 all-to-all-done.1
  75.9 0.0 collective-permute-start.13
  76.0 1.5 %collective-permute-done.13.refs_1_ = f32[512,128]{1,0:T(8,128)S(1)} collective-permute-done((f32[512,128]{1,0:T(8,128)S(1)}, f32[512,128]{1,0:T(8,128)S(1)}, u32[]{:S(2)}, u32[]{:S(2)}) %collective-permute-start.13) | collective-permute-done | bytes 262176 | tf_op jit(solution)/shard_map/ppermute | solution.py:726
  77.5 1.1 %place.1 = f32[1024,128]{1,0:T(8,128)} custom-call(f32[512,128]{1,0:T(8,128)S(1)} %bitcast.5, f32[512,128]{1,0:T(8,128)S(1)} %collective-permute-done.13.refs_1_), custom_call_target="tpu_custom_call" | custom-call | flops 1 | bytes 1 | tf_op jit(solution)/shard_map/place/pallas_call | solution.py:515
  (1 shorter events, 0.0 us)
Async XLA Ops:
  2.6 15.8 %collective-permute-start = (f32[16,4,16,128]{3,2,1,0:T(8,128)S(1)}, f32[16,4,16,128]{3,2,1,0:T(8,128)S(1)}, u32[]{:S(2)}, u32[]{:S(2)}) collective-permute-start(f32[16,4,16,128]{3,2,1,0:T(8,128)S(1)} %get-tuple-element.52), channel_id=1, source_target_pairs={{0,4},{4,0},{8,12},{12,8},{16,20},{20,16},{24,28},{28,24},{1,5},{5... | collective-permute-start | bytes 1572872 | tf_op jit(solution)/shard_map/ppermute | solution.py:575
  5.6 14.6 %collective-permute-start.3 = (f32[512,128]{1,0:T(8,128)S(1)}, f32[512,128]{1,0:T(8,128)S(1)}, u32[]{:S(2)}, u32[]{:S(2)}) collective-permute-start(f32[512,128]{1,0:T(8,128)S(1)} %get-tuple-element.58.refs_5_.refs_3_), channel_id=1, source_target_pairs={{0,16},{4,20},{8,24},{12,28},{16,0},{20,4},{24,8},{28,12},{1,17},{... | collective-permute-start | bytes 786440 | tf_op jit(solution)/shard_map/ppermute | solution.py:614
  8.2 18.3 %collective-permute-start.2 = (f32[512,128]{1,0:T(8,128)S(1)}, f32[512,128]{1,0:T(8,128)S(1)}, u32[]{:S(2)}, u32[]{:S(2)}) collective-permute-start(f32[512,128]{1,0:T(8,128)S(1)} %get-tuple-element.58.refs_5_.refs_3_), channel_id=1, source_target_pairs={{0,8},{4,12},{8,0},{12,4},{16,24},{20,28},{24,16},{28,20},{1,9},{5... | collective-permute-start | bytes 786440 | tf_op jit(solution)/shard_map/ppermute | solution.py:614
  9.8 13.4 %collective-permute-start.1 = (f32[512,128]{1,0:T(8,128)S(1)}, f32[512,128]{1,0:T(8,128)S(1)}, u32[]{:S(2)}, u32[]{:S(2)}) collective-permute-start(f32[512,128]{1,0:T(8,128)S(1)} %get-tuple-element.50.refs_2_.refs_1_), channel_id=1, source_target_pairs={{0,4},{4,0},{8,12},{12,8},{16,20},{20,16},{24,28},{28,24},{1,5},{5... | collective-permute-start | bytes 786440 | tf_op jit(solution)/shard_map/ppermute | solution.py:576
  20.3 7.3 %collective-permute-start.4 = (f32[512,128]{1,0:T(8,128)S(1)}, f32[512,128]{1,0:T(8,128)S(1)}, u32[]{:S(2)}, u32[]{:S(2)}) collective-permute-start(f32[512,128]{1,0:T(8,128)S(1)} %collective-permute-done.3.refs_7_.refs_5_), channel_id=1, source_target_pairs={{0,8},{4,12},{8,0},{12,4},{16,24},{20,28},{24,16},{28,20},{1,9},{5... | collective-permute-start | bytes 786440 | tf_op jit(solution)/shard_map/ppermute | solution.py:614
  24.7 13.7 %collective-permute-start.5 = (f32[2,512,128]{2,1,0:T(8,128)S(1)}, f32[2,512,128]{2,1,0:T(8,128)S(1)}, u32[]{:S(2)}, u32[]{:S(2)}) collective-permute-start(f32[2,512,128]{2,1,0:T(8,128)S(1)} %get-tuple-element.63), channel_id=1, source_target_pairs={{0,8},{4,12},{8,0},{12,4},{16,24},{20,28},{24,16},{28,20},{1,9},{5... | collective-permute-start | bytes 1572872 | tf_op jit(solution)/shard_map/ppermute | solution.py:624
  35.1 3.3 %collective-permute-start.6 = (f32[512,128]{1,0:T(8,128)S(1)}, f32[512,128]{1,0:T(8,128)S(1)}, u32[]{:S(2)}, u32[]{:S(2)}) collective-permute-start(f32[512,128]{1,0:T(8,128)S(1)} %get-tuple-element.69), channel_id=1, source_target_pairs={{0,1},{1,0},{2,3},{3,2},{4,5},{5,4},{6,7},{7,6},{8,9},{9,8},{10,11... | collective-permute-start | bytes 786440 | tf_op jit(solution)/shard_map/ppermute | solution.py:640
  39.2 18.3 %all-to-all-start = ((f32[16,32,128]{2,1,0:T(8,128)}), f32[16,32,128]{2,1,0:T(8,128)S(1)}, u32[]{:S(2)}, u32[]{:S(2)}) async-start(f32[16,32,128]{2,1,0:T(8,128)} %bitcast.1.refs_0_), calls=%async_computation | async-start | bytes 524288 | tf_op jit(solution)/shard_map/all_to_all | solution.py:688
  51.3 10.7 %collective-permute-start.9 = (f32[2,32,512]{2,1,0:T(8,128)S(1)}, f32[2,32,512]{2,1,0:T(8,128)S(1)}, u32[]{:S(2)}, u32[]{:S(2)}) collective-permute-start(f32[2,32,512]{2,1,0:T(8,128)S(1)} %get-tuple-element.80), channel_id=1, source_target_pairs={{0,1},{1,0},{2,3},{3,2},{4,5},{5,4},{6,7},{7,6},{8,9},{9,8},{10,11... | collective-permute-start | bytes 393224 | tf_op jit(solution)/shard_map/ppermute | solution.py:685
  51.5 10.5 %collective-permute-start.10 = (f32[2,32,512]{2,1,0:T(8,128)S(1)}, f32[2,32,512]{2,1,0:T(8,128)S(1)}, u32[]{:S(2)}, u32[]{:S(2)}) collective-permute-start(f32[2,32,512]{2,1,0:T(8,128)S(1)} %get-tuple-element.81), channel_id=1, source_target_pairs={{0,2},{1,3},{2,0},{3,1},{4,6},{5,7},{6,4},{7,5},{8,10},{9,11},{10,... | collective-permute-start | bytes 393224 | tf_op jit(solution)/shard_map/ppermute | solution.py:685
  53.3 8.7 %collective-permute-start.11 = (f32[2,32,512]{2,1,0:T(8,128)S(1)}, f32[2,32,512]{2,1,0:T(8,128)S(1)}, u32[]{:S(2)}, u32[]{:S(2)}) collective-permute-start(f32[2,32,512]{2,1,0:T(8,128)S(1)} %get-tuple-element.82), channel_id=1, source_target_pairs={{0,3},{1,2},{2,1},{3,0},{4,7},{5,6},{6,5},{7,4},{8,11},{9,10},{10,... | collective-permute-start | bytes 393224 | tf_op jit(solution)/shard_map/ppermute | solution.py:685
  53.4 20.2 %collective-permute-start.7 = (f32[16,4,16,128]{3,2,1,0:T(8,128)S(1)}, f32[16,4,16,128]{3,2,1,0:T(8,128)S(1)}, u32[]{:S(2)}, u32[]{:S(2)}) collective-permute-start(f32[16,4,16,128]{3,2,1,0:T(8,128)S(1)} %pair_peer.1.refs_0_), channel_id=1, source_target_pairs={{0,4},{4,0},{8,12},{12,8},{16,20},{20,16},{24,28},{28,24},{1,5},{5... | collective-permute-start | bytes 1572872 | tf_op jit(solution)/shard_map/ppermute | solution.py:682
  55.1 18.5 %collective-permute-start.8 = (f32[1,512,128]{2,1,0:T(8,128)S(1)}, f32[1,512,128]{2,1,0:T(8,128)S(1)}, u32[]{:S(2)}, u32[]{:S(2)}) collective-permute-start(f32[1,512,128]{2,1,0:T(8,128)S(1)} %get-tuple-element.74), channel_id=1, source_target_pairs={{0,16},{4,20},{8,24},{12,28},{16,0},{20,4},{24,8},{28,12},{1,17},{... | collective-permute-start | bytes 786440 | tf_op jit(solution)/shard_map/ppermute | solution.py:660
  58.2 17.7 %all-to-all-start.1 = ((f32[16,32,128]{2,1,0:T(8,128)}), f32[16,32,128]{2,1,0:T(8,128)S(1)}, u32[]{:S(2)}, u32[]{:S(2)}) async-start(f32[16,32,128]{2,1,0:T(8,128)} %weight_sum.1.refs_0_), calls=%async_computation.1 | async-start | bytes 524288 | tf_op jit(solution)/shard_map/all_to_all | solution.py:699
  62.1 11.5 %collective-permute-start.12 = (f32[32,512]{1,0:T(8,128)S(1)}, f32[32,512]{1,0:T(8,128)S(1)}, u32[]{:S(2)}, u32[]{:S(2)}) collective-permute-start(f32[32,512]{1,0:T(8,128)S(1)} %get-tuple-element.84), channel_id=1, source_target_pairs={{0,4},{4,0},{8,12},{12,8},{16,20},{20,16},{24,28},{28,24},{1,5},{5... | collective-permute-start | bytes 196616 | tf_op jit(solution)/shard_map/ppermute | solution.py:701
  75.9 1.5 %collective-permute-start.13 = (f32[512,128]{1,0:T(8,128)S(1)}, f32[512,128]{1,0:T(8,128)S(1)}, u32[]{:S(2)}, u32[]{:S(2)}) collective-permute-start(f32[512,128]{1,0:T(8,128)S(1)} %bitcast.4), channel_id=1, source_target_pairs={{0,1},{1,0},{2,3},{3,2},{4,5},{5,4},{6,7},{7,6},{8,9},{9,8},{10,11... | collective-permute-start | bytes 786440 | tf_op jit(solution)/shard_map/ppermute | solution.py:726

commit v23 on v22

--- a/solution.py
+++ b/solution.py
@@ -129,7 +129,9 @@
     channels = ENTRY_CHANNELS
     rows, features = out_ref.shape
     count = features // LANES
-    total[...] = functools.reduce(jnp.add, [ref[0] for ref in part_refs])
+    size = part_refs[0].shape[1]
+    total[:size, :] = part_refs[0][0] + part_refs[1][0]
+    total[size:, :] = part_refs[2][0] + part_refs[3][0]
     for group in range(rows // PACK):
         stacked = [total[strided(group * PACK + k, channels, rows), :] for k in range(PACK)]
         square[group] = jnp.concatenate(stacked, 0).T
@@ -208,7 +210,7 @@
     def store(step, found):
         partial_ref[step] = found
 
-    right_phase(left_ref, out_ref, left_flip, store, 8)
+    right_phase(left_ref, out_ref, left_flip, [store])
     channels = ENTRY_CHANNELS
     wide = weight_rows.shape[1]
     for step in range(channels // fold):
@@ -227,14 +229,14 @@
     gradient_phase(blocks, cotangent_ref, out_ref, spread_ref, weight_cat)
 
 
-def right_phase(left_ref, factor_ref, left_flip, store, unroll):
+def right_phase(left_ref, factor_ref, left_flip, stores):
     sequences = left_ref.shape[1]
     lanes = factor_ref.shape[2] // 4
     flip_high, flip_low = halves((left_ref[...] * (1.0 / sequences)).T)
     left_flip[:sequences, :] = flip_high
     left_flip[sequences:, :] = flip_low
 
-    def step_of(step, carry):
+    def compute(step, store):
         high, low = (
             jnp.concatenate(
                 [rows_of_step([factor_ref], 2 * step + part, half, lanes) for part in range(2)], 1
@@ -244,10 +246,16 @@
         first = dot(left_flip[...], high)
         second = dot(left_flip[:sequences, :], low)
         store(step, first[:sequences] + first[sequences:] + second)
-        return carry
 
     count = factor_ref.shape[1] // (2 * ENTRY_CHANNELS)
-    lax.fori_loop(0, count, step_of, 0, unroll=unroll)
+    size = count // len(stores)
+    for at, store in enumerate(stores):
+
+        def step_of(step, carry):
+            compute(step, store)
+            return carry
+
+        lax.fori_loop(at * size, (at + 1) * size, step_of, 0, unroll=min(size, 8))
 
 
 def rows_of_step(refs, step, half, lanes):
@@ -271,29 +279,58 @@
 
 
 def right_kernel(
-    blocks, depth, peer_ref, left_ref, partial_ref, keep_ref, send_ref, left_flip
+    blocks,
+    depth,
+    peer_ref,
+    left_ref,
+    partial_ref,
+    near_keep,
+    near_send,
+    far_keep,
+    far_send,
+    left_flip,
 ):
     fold = fold_of(blocks * depth)
     lanes = fold * blocks * depth
-
-    def store(step, found):
-        found = found + partial_ref[step]
-        for part in range(2):
-            turned = found[:, part * lanes : (part + 1) * lanes].T
-            for place in range(fold):
-                for slot in range(blocks):
-                    start = (place * blocks + slot) * depth
-                    row = pl.multiple_of(((2 * step + part) * fold + place) * depth, depth)
-                    out_ref = send_ref if slot % 2 else keep_ref
-                    out_ref[slot // 2, pl.ds(row, depth), :] = turned[start : start + depth]
-
-    right_phase(left_ref, peer_ref, left_flip, store, 4)
-
-
-def halve_kernel(keep_ref, found_ref, keep_out, send_out):
-    for slot in range(keep_ref.shape[0]):
-        out_ref = send_out if slot % 2 else keep_out
-        out_ref[slot // 2] = keep_ref[slot] + found_ref[slot]
+    size = near_keep.shape[1]
+
+    def store_to(outs, first_row):
+        def store(step, found):
+            found = found + partial_ref[step]
+            for part in range(2):
+                turned = found[:, part * lanes : (part + 1) * lanes].T
+                for place in range(fold):
+                    for slot in range(blocks):
+                        start = (place * blocks + slot) * depth
+                        row = ((2 * step + part) * fold + place) * depth - first_row
+                        row = pl.multiple_of(row, depth)
+                        ref, at = outs[slot]
+                        ref[at, pl.ds(row, depth), :] = turned[start : start + depth]
+
+        return store
+
+    half = blocks // 2
+    near = [(near_send if slot % 2 else near_keep, slot // 2) for slot in range(blocks)]
+    far = [(far_send if slot >= half else far_keep, slot % half) for slot in range(blocks)]
+    right_phase(left_ref, peer_ref, left_flip, [store_to(near, 0), store_to(far, size)])
+
+
+def halve_kernel(
+    near_keep,
+    near_found,
+    far_keep,
+    far_found,
+    near_keep_out,
+    near_send_out,
+    far_keep_out,
+    far_send_out,
+):
+    half = near_keep.shape[0] // 2
+    for slot in range(2 * half):
+        out_ref = near_send_out if slot % 2 else near_keep_out
+        out_ref[slot // 2] = near_keep[slot] + near_found[slot]
+        out_ref = far_send_out if slot >= half else far_keep_out
+        out_ref[slot % half] = far_keep[slot] + far_found[slot]
 
 
 def right_rows(right_refs, step, fold, depth):
@@ -452,8 +489,8 @@
     lax.fori_loop(0, count, step_of, 0)
 
 
-def finish_kernel(own_ref, other_ref, keep_ref, found_ref, *refs):
-    left_refs, refs = refs[:-9], refs[-9:]
+def finish_kernel(own_ref, other_ref, *refs):
+    right_refs, left_refs, refs = refs[:4], refs[4:-9], refs[-9:]
     pair_hbm, left_out, right_out = refs[:3]
     right_total, right_square, right_tiles, left_total, left_tiles, semaphores = refs[3:]
     parity = lax.rem(lax.axis_index("blk"), 2)
@@ -463,7 +500,7 @@
     ]
     for copy in copies:
         copy.start()
-    turn_right([keep_ref, found_ref], right_out, right_total, right_square, right_tiles)
+    turn_right(right_refs, right_out, right_total, right_square, right_tiles)
     turn_left(left_refs, left_out, left_total, left_tiles)
     for copy in copies:
         copy.wait()
@@ -614,14 +651,15 @@
             rights[slot + distance] = lax.ppermute(sent, "blk", slot_moves[distance])
         distance = distance // 2
     rights = [rights[slot] for slot in range(blocks)]
-    right_half = shape(blocks // 2, channels * depth, sequences)
-    right_keep, right_send = large(
+    right_half = shape(blocks // 2, channels * depth // 2, sequences)
+    near_keep, near_send, far_keep, far_send = large(
         functools.partial(right_kernel, blocks, depth),
-        [right_half, right_half],
+        [right_half] * 4,
         [flip_scratch],
         "right_parts",
     )(grad_peer, left_peer, partial)
-    right_send = lax.ppermute(right_send, "blk", slot_moves[1])
+    near_send = lax.ppermute(near_send, "blk", slot_moves[1])
+    far_send = lax.ppermute(far_send, "blk", slot_moves[blocks // 2])
 
     keep, send, outer_own, outer_peer = large(
         functools.partial(weight_kernel, blocks, depth),
@@ -633,7 +671,7 @@
             pltpu.SemaphoreType.DMA((steps // 2, 2)),
         ],
         "weight",
-        after=[right_keep],
+        after=[near_keep],
         flops=2 * work,
         out_specs=[vmem, vmem, hbm, hbm],
     )(left, left_peer, spread_own, spread_peer, *rights)
@@ -651,15 +689,7 @@
         after=[keep],
         flops=work,
     )(grad_own, grad_peer, *rights)
-    slot = 2
-    while slot < blocks:
-        part = shape(blocks // (2 * slot), channels * depth, sequences)
-        right_keep, right_send = call(
-            halve_kernel, [part, part], name="right_halve", after=[left_parts[0]]
-        )(right_keep, right_send)
-        right_send = lax.ppermute(right_send, "blk", slot_moves[slot])
-        slot = 2 * slot
-    keep, right_keep, *left_parts = lax.optimization_barrier((keep, right_keep, *left_parts))
+    keep, *left_parts = lax.optimization_barrier((keep, *left_parts))
     members = count * inner // 2
     pieces = (keep + sent).reshape(members, outer // 2 // members, pairs)
 
@@ -685,12 +715,22 @@
         lax.ppermute(part, "inner", inner_moves[slot]) if slot else part
         for slot, part in enumerate(left_parts)
     ]
+    slot = 2
+    while slot < blocks:
+        part = shape(blocks // (2 * slot), channels * depth // 2, sequences)
+        near_keep, near_send, far_keep, far_send = call(
+            halve_kernel, [part] * 4, name="right_halve", after=[pair_other]
+        )(near_keep, near_send, far_keep, far_send)
+        near_send = lax.ppermute(near_send, "blk", slot_moves[slot])
+        far_send = lax.ppermute(far_send, "blk", slot_moves[blocks // (2 * slot)])
+        slot = 2 * slot
+
     pieces = lax.all_to_all(pieces, everyone, 0, 0, axis_index_groups=core_groups)
     pieces = call(
         spread_sum_kernel,
         shape(*pieces.shape),
         name="weight_sum",
-        after=[pair_other],
+        after=[pair_other, near_keep],
     )(pieces)
     pair_own = pair(outer_own, [pieces], "pair_own")
     left_own, left_send = call(
@@ -716,7 +756,7 @@
         ],
         "finish",
         out_specs=[hbm, vmem, vmem],
-    )(pair_own, pair_found, right_keep, right_send, *left_found)
+    )(pair_own, pair_found, near_keep, near_send, far_keep, far_send, *left_found)
     pair_update = pair_update.reshape(cotangent.shape)
 
     pieces, pair_update, grad_left, grad_right = lax.optimization_barrier(

time: 79 us -> 84 us (1.063)
  starting transfers between devices: 30.9 us -> 40.5 us
  waiting for transfers between devices: 13.1 us -> 7.59 us
  Pallas kernels: 33.1 us -> 34 us
    all_to_all x2, starting transfers between devices: 10.9 us -> 16.2 us  [local(): lax.all_to_all(pieces, everyone, 0, 0, axis_index_groups=core_groups)]
    ppermute x2 -> x4, starting transfers between devices: 4.23 us -> 8.8 us  [the longest x1 2.59 us: local(): far_send = lax.ppermute(far_send, 'blk', slot_moves[blocks // 2])]
    ppermute x2 -> x4, waiting for transfers between devices: 5.32 us -> 1 us  [the longest x1 0.99 us: local(): far_send = lax.ppermute(far_send, 'blk', slot_moves[blocks // (2 * slot)])]
    ppermute x3, waiting for transfers between devices: 1 us -> 0.01 us  [local(): rights[slot + distance] = lax.ppermute(sent, 'blk', slot_moves[distance])]
    pallas_call x13, Pallas kernels: 33.1 us -> 34 us  [run(): pl.pallas_call(lambda *refs: kernel(*refs[len(after):]), out_shape=out_sh...]
  transfers between devices with their start and end apart: 16 -> 18, of which waited for: 7 -> 4; matrix products, arithmetic and copies ran while one was open for 0% -> 1% of each run, Pallas kernels for 38% -> 37%
where the time goes in v23:
time: 84 us; the launch traced here: 83.6 us
  starting transfers between devices  40.5 us (48%)
  Pallas kernels  34 us (40%)
  waiting for transfers between devices  7.59 us (9%)
    pallas_call x13, Pallas kernels, run(): pl.pallas_call(lambda *refs: kernel(*refs[len(after):]), out_shape=out_sh...  34 us
    all_to_all x2, starting transfers between devices, local(): lax.all_to_all(pieces, everyone, 0, 0, axis_index_groups=core_groups)  16.2 us
    ppermute x3, starting transfers between devices, local(): rights[slot + distance] = lax.ppermute(sent, 'blk', slot_moves[distance])  6.36 us
    ppermute x1, waiting for transfers between devices, local(): cotangent_peer = lax.ppermute(cotangent_send, 'blk', partner)  4.3 us
    ppermute x1, starting transfers between devices, local(): cotangent_peer = lax.ppermute(cotangent_send, 'blk', partner)  3.03 us
    ppermute x1, starting transfers between devices, local(): far_send = lax.ppermute(far_send, 'blk', slot_moves[blocks // 2])  2.59 us
    ppermute x1, starting transfers between devices, local(): near_send = lax.ppermute(near_send, 'blk', slot_moves[slot])  2.37 us
    ppermute x3, starting transfers between devices, local(): lax.ppermute(part, 'inner', inner_moves[slot])  2.13 us
  transfers between devices with their start and end apart: 18, of which 4 were waited for; matrix products, arithmetic and copies ran while one was open for 1% of the time, Pallas kernels for 37%

profile of v23, /device:TPU:0, one launch (start us, length us, event | category | flops | bytes accessed | tf_op | source)
XLA Modules:
  0.0 83.6 jit_solution(13726026970512474638)
XLA Ops:
  0.6 2.0 %prepare.1 = (f32[512,128]{1,0:T(8,128)S(1)}, f32[512,128]{1,0:T(8,128)S(1)}, f32[16,4,16,128]{3,2,1,0:T(8,128)S(1)}, f32[16,4,16,128]{3,2,1,0:T(8,128)S(1)}, f32[1024,128]{1,0:T(8,128)S(1)}) custom-call(f32[16,4,2,16,128]{4,3,2,1,0:T(8,128)} %bitcast.6, f32[16,4096]{1,0:T(8,128)} %refs_1_.1, f32[16,4096]{1,0:T(8,128)} %refs_2_.1, f32[1024,128]{1,0:T(8,128)} %refs_3_.1), custom_call_target="tpu_custom_call" | custom-call | flops 1 | bytes 1 | tf_op jit(solution)/shard_map/prepare/pallas_call | solution.py:552
  2.6 3.0 %collective-permute-start = (f32[16,4,16,128]{3,2,1,0:T(8,128)S(1)}, f32[16,4,16,128]{3,2,1,0:T(8,128)S(1)}, u32[]{:S(2)}, u32[]{:S(2)}) collective-permute-start(f32[16,4,16,128]{3,2,1,0:T(8,128)S(1)} %get-tuple-element.55), channel_id=1, source_target_pairs={{0,4},{4,0},{8,12},{12,8},{16,20},{20,16},{24,28},{28,24},{1,5},{5... | collective-permute-start | bytes 1572872 | tf_op jit(solution)/shard_map/ppermute | solution.py:612
  5.6 2.6 %collective-permute-start.3 = (f32[512,128]{1,0:T(8,128)S(1)}, f32[512,128]{1,0:T(8,128)S(1)}, u32[]{:S(2)}, u32[]{:S(2)}) collective-permute-start(f32[512,128]{1,0:T(8,128)S(1)} %get-tuple-element.61.refs_5_.refs_3_), channel_id=1, source_target_pairs={{0,16},{4,20},{8,24},{12,28},{16,0},{20,4},{24,8},{28,12},{1,17},{... | collective-permute-start | bytes 786440 | tf_op jit(solution)/shard_map/ppermute | solution.py:651
  8.2 1.6 %collective-permute-start.2 = (f32[512,128]{1,0:T(8,128)S(1)}, f32[512,128]{1,0:T(8,128)S(1)}, u32[]{:S(2)}, u32[]{:S(2)}) collective-permute-start(f32[512,128]{1,0:T(8,128)S(1)} %get-tuple-element.61.refs_5_.refs_3_), channel_id=1, source_target_pairs={{0,8},{4,12},{8,0},{12,4},{16,24},{20,28},{24,16},{28,20},{1,9},{5... | collective-permute-start | bytes 786440 | tf_op jit(solution)/shard_map/ppermute | solution.py:651
  9.8 0.5 collective-permute-start.1
  10.3 3.8 %gradient_own.1 = (bf16[8,512,512]{2,1,0:T(8,128)(2,1)S(1)}, bf16[8,2,256,256]{3,2,1,0:T(8,128)(2,1)S(1)}, f32[8,128,256]{2,1,0:T(8,128)S(1)}, bf16[512,768]{1,0:T(8,128)(2,1)S(1)}, bf16[512,512]{1,0:T(8,128)(2,1)}) custom-call(f32[1024,128]{1,0:T(8,128)S(1)} %get-tuple-element.51.refs_0_, f32[16,4,16,128]{3,2,1,0:T(8,128)S(1)} %get-tuple-element.52.refs_1_, ...), custom_call_target="tpu_custom_call" | custom-call | flops 1 | bytes 1 | tf_op jit(solution)/shard_map/gradient_own/pallas_call | solution.py:552
  14.1 4.3 %collective-permute-done.refs_1_ = f32[16,4,16,128]{3,2,1,0:T(8,128)S(1)} collective-permute-done((f32[16,4,16,128]{3,2,1,0:T(8,128)S(1)}, f32[16,4,16,128]{3,2,1,0:T(8,128)S(1)}, u32[]{:S(2)}, u32[]{:S(2)}) %collective-permute-start) | collective-permute-done | bytes 524320 | tf_op jit(solution)/shard_map/ppermute | solution.py:612
  18.4 1.8 %gradient_peer.1 = (bf16[8,512,512]{2,1,0:T(8,128)(2,1)S(1)}, bf16[8,2,256,256]{3,2,1,0:T(8,128)(2,1)S(1)}) custom-call(bf16[512,768]{1,0:T(8,128)(2,1)S(1)} %get-tuple-element.54.refs_0_, f32[16,4,16,128]{3,2,1,0:T(8,128)S(1)} %collective-permute-done.refs_1_), custom_call_target="tpu_custom_call" | custom-call | flops 1 | bytes 1 | tf_op jit(solution)/shard_map/gradient_peer/pallas_call | solution.py:552
  20.2 0.0 collective-permute-done.3.refs_7_.refs_5_
  20.2 2.2 %collective-permute-start.4 = (f32[512,128]{1,0:T(8,128)S(1)}, f32[512,128]{1,0:T(8,128)S(1)}, u32[]{:S(2)}, u32[]{:S(2)}) collective-permute-start(f32[512,128]{1,0:T(8,128)S(1)} %collective-permute-done.3.refs_7_.refs_5_), channel_id=1, source_target_pairs={{0,8},{4,12},{8,0},{12,4},{16,24},{20,28},{24,16},{28,20},{1,9},{5... | collective-permute-start | bytes 786440 | tf_op jit(solution)/shard_map/ppermute | solution.py:651
  22.4 0.7 collective-permute-done.1.refs_1_.refs_2_
  23.2 1.1 %right_parts.1 = (f32[2,256,128]{2,1,0:T(8,128)S(1)}, f32[2,256,128]{2,1,0:T(8,128)S(1)}, f32[2,256,128]{2,1,0:T(8,128)S(1)}, f32[2,256,128]{2,1,0:T(8,128)S(1)}) custom-call(bf16[8,512,512]{2,1,0:T(8,128)(2,1)S(1)} %get-tuple-element.56.refs_0_.refs_2_, f32[512,128]{1,0:T(8,128)S(1)} %collective-permute-done.1.refs_1_.refs_2_, ...), custom_call_target="tpu_custom_call" | custom-call | flops 1 | bytes 1 | tf_op jit(solution)/shard_map/right_parts/pallas_call | solution.py:552
  24.3 1.9 %collective-permute-start.6 = (f32[2,256,128]{2,1,0:T(8,128)S(1)}, f32[2,256,128]{2,1,0:T(8,128)S(1)}, u32[]{:S(2)}, u32[]{:S(2)}) collective-permute-start(f32[2,256,128]{2,1,0:T(8,128)S(1)} %get-tuple-element.73), channel_id=1, source_target_pairs={{0,8},{4,12},{8,0},{12,4},{16,24},{20,28},{24,16},{28,20},{1,9},{5... | collective-permute-start | bytes 786440 | tf_op jit(solution)/shard_map/ppermute | solution.py:661
  26.2 2.6 %collective-permute-start.7 = (f32[2,256,128]{2,1,0:T(8,128)S(1)}, f32[2,256,128]{2,1,0:T(8,128)S(1)}, u32[]{:S(2)}, u32[]{:S(2)}) collective-permute-start(f32[2,256,128]{2,1,0:T(8,128)S(1)} %get-tuple-element.75), channel_id=1, source_target_pairs={{0,16},{4,20},{8,24},{12,28},{16,0},{20,4},{24,8},{28,12},{1,17},{... | collective-permute-start | bytes 786440 | tf_op jit(solution)/shard_map/ppermute | solution.py:662
  28.8 0.0 collective-permute-done.2.refs_6_.refs_4_
  28.8 0.0 collective-permute-done.4.refs_8_.refs_6_
  28.8 7.5 %weight.1 = (f32[512,128]{1,0:T(8,128)S(1)}, f32[512,128]{1,0:T(8,128)S(1)}, bf16[8,512,512]{2,1,0:T(8,128)(2,1)}, bf16[8,512,512]{2,1,0:T(8,128)(2,1)}) custom-call(f32[2,256,128]{2,1,0:T(8,128)S(1)} %get-tuple-element.58.refs_0_.refs_1_, f32[512,128]{1,0:T(8,128)S(1)} %get-tuple-element.53.refs_2_.refs_1_, ...), custom_call_target="tpu_custom_call" | custom-call | flops 12884901888 | bytes 1 | tf_op jit(solution)/shard_map/weight/pallas_call | solution.py:552
  36.3 0.1 collective-permute-start.5
  36.4 3.1 %left_parts.1 = (f32[2,32,512]{2,1,0:T(8,128)S(1)}, f32[2,32,512]{2,1,0:T(8,128)}, f32[2,32,512]{2,1,0:T(8,128)S(1)}, f32[2,32,512]{2,1,0:T(8,128)S(1)}) custom-call(f32[512,128]{1,0:T(8,128)S(1)} %get-tuple-element.69.refs_0_, bf16[8,512,512]{2,1,0:T(8,128)(2,1)S(1)} %get-tuple-element.64.refs_1_, ...), custom_call_target="tpu_custom_call" | custom-call | flops 6442450944 | bytes 1 | tf_op jit(solution)/shard_map/left_parts/pallas_call | solution.py:552
  39.5 0.0 collective-permute-done.5
  39.5 0.7 add.3
  40.2 12.5 %all-to-all-start = ((f32[16,32,128]{2,1,0:T(8,128)}), f32[16,32,128]{2,1,0:T(8,128)S(1)}, u32[]{:S(2)}, u32[]{:S(2)}) async-start(f32[16,32,128]{2,1,0:T(8,128)} %bitcast.1.refs_0_), calls=%async_computation | async-start | bytes 524288 | tf_op jit(solution)/shard_map/all_to_all | solution.py:728
  52.7 5.0 %pair_peer.1.refs_0_ = f32[16,4,16,128]{3,2,1,0:T(8,128)S(1)} custom-call(f32[16,32,128]{2,1,0:T(8,128)} %bitcast.1.refs_0_, bf16[8,512,512]{2,1,0:T(8,128)(2,1)} %get-tuple-element.71.refs_1_, bf16[512,512]{1,0:T(8,128)(2,1)} %get-tuple-element.72.refs_2_), custom_call_target="tpu_custom_call" | custom-call | flops 6442450944 | bytes 1 | tf_op jit(solution)/shard_map/pair_peer/pallas_call | solution.py:552
  57.7 0.3 collective-permute-start.11
  58.0 1.8 %collective-permute-start.12 = (f32[2,32,512]{2,1,0:T(8,128)S(1)}, f32[2,32,512]{2,1,0:T(8,128)S(1)}, u32[]{:S(2)}, u32[]{:S(2)}) collective-permute-start(f32[2,32,512]{2,1,0:T(8,128)S(1)} %get-tuple-element.87), channel_id=1, source_target_pairs={{0,2},{1,3},{2,0},{3,1},{4,6},{5,7},{6,4},{7,5},{8,10},{9,11},{10,... | collective-permute-start | bytes 393224 | tf_op jit(solution)/shard_map/ppermute | solution.py:715
  59.8 0.1 collective-permute-start.13
  59.8 0.0 collective-permute-done.6.refs_2_
  59.8 1.7 %collective-permute-start.8 = (f32[16,4,16,128]{3,2,1,0:T(8,128)S(1)}, f32[16,4,16,128]{3,2,1,0:T(8,128)S(1)}, u32[]{:S(2)}, u32[]{:S(2)}) collective-permute-start(f32[16,4,16,128]{3,2,1,0:T(8,128)S(1)} %pair_peer.1.refs_0_), channel_id=1, source_target_pairs={{0,4},{4,0},{8,12},{12,8},{16,20},{20,16},{24,28},{28,24},{1,5},{5... | collective-permute-start | bytes 1572872 | tf_op jit(solution)/shard_map/ppermute | solution.py:712
  61.6 0.0 collective-permute-done.7.refs_4_
  61.6 0.7 right_halve.1
  62.3 2.4 %collective-permute-start.9 = (f32[1,256,128]{2,1,0:T(8,128)}, f32[1,256,128]{2,1,0:T(8,128)S(1)}, u32[]{:S(2)}, u32[]{:S(2)}) collective-permute-start(f32[1,256,128]{2,1,0:T(8,128)} %get-tuple-element.78), channel_id=1, source_target_pairs={{0,16},{4,20},{8,24},{12,28},{16,0},{20,4},{24,8},{28,12},{1,17},{... | collective-permute-start | bytes 393224 | tf_op jit(solution)/shard_map/ppermute | solution.py:724
  64.6 0.0 all-to-all-done.refs_2_
  64.7 0.7 weight_sum.1.refs_0_
  65.4 3.7 %all-to-all-start.1 = ((f32[16,32,128]{2,1,0:T(8,128)}), f32[16,32,128]{2,1,0:T(8,128)S(1)}, u32[]{:S(2)}, u32[]{:S(2)}) async-start(f32[16,32,128]{2,1,0:T(8,128)} %weight_sum.1.refs_0_), calls=%async_computation.1 | async-start | bytes 524288 | tf_op jit(solution)/shard_map/all_to_all | solution.py:739
  69.2 0.0 collective-permute-done.11.refs_2_
  69.2 2.0 %collective-permute-start.10 = (f32[1,256,128]{2,1,0:T(8,128)S(1)}, f32[1,256,128]{2,1,0:T(8,128)S(1)}, u32[]{:S(2)}, u32[]{:S(2)}) collective-permute-start(f32[1,256,128]{2,1,0:T(8,128)S(1)} %get-tuple-element.80), channel_id=1, source_target_pairs={{0,8},{4,12},{8,0},{12,4},{16,24},{20,28},{24,16},{28,20},{1,9},{5... | collective-permute-start | bytes 393224 | tf_op jit(solution)/shard_map/ppermute | solution.py:725
  71.2 0.0 collective-permute-done.12.refs_3_
  71.2 0.0 collective-permute-done.13.refs_4_
  71.2 1.5 %collective-permute-start.14 = (f32[32,512]{1,0:T(8,128)S(1)}, f32[32,512]{1,0:T(8,128)S(1)}, u32[]{:S(2)}, u32[]{:S(2)}) collective-permute-start(f32[32,512]{1,0:T(8,128)S(1)} %get-tuple-element.90), channel_id=1, source_target_pairs={{0,4},{4,0},{8,12},{12,8},{16,20},{20,16},{24,28},{28,24},{1,5},{5... | collective-permute-start | bytes 196616 | tf_op jit(solution)/shard_map/ppermute | solution.py:741
  72.7 5.0 %pair_own.1.refs_0_ = f32[16,4,16,128]{3,2,1,0:T(8,128)S(1)} custom-call(f32[16,32,128]{2,1,0:T(8,128)} %weight_sum.1.refs_0_, bf16[8,512,512]{2,1,0:T(8,128)(2,1)} %get-tuple-element.77.refs_1_, bf16[512,512]{1,0:T(8,128)(2,1)} %get-tuple-element.72.refs_2_), custom_call_target="tpu_custom_call" | custom-call | flops 6442450944 | bytes 1 | tf_op jit(solution)/shard_map/pair_own/pallas_call | solution.py:552
  77.7 0.0 collective-permute-done.9.refs_3_
  77.7 1.0 %collective-permute-done.10.refs_5_ = f32[1,256,128]{2,1,0:T(8,128)S(1)} collective-permute-done((f32[1,256,128]{2,1,0:T(8,128)S(1)}, f32[1,256,128]{2,1,0:T(8,128)S(1)}, u32[]{:S(2)}, u32[]{:S(2)}) %collective-permute-start.10) | collective-permute-done | bytes 131104 | tf_op jit(solution)/shard_map/ppermute | solution.py:725
  78.7 0.0 collective-permute-done.8.refs_1_
  78.7 0.0 collective-permute-done.14.refs_7_
  78.7 2.2 %finish.1 = (f32[16,4,2,16,128]{4,3,2,1,0:T(8,128)}, f32[16,1024]{1,0:T(8,128)}, f32[16,4096]{1,0:T(8,128)}) custom-call(f32[16,4,16,128]{3,2,1,0:T(8,128)S(1)} %pair_own.1.refs_0_, f32[16,4,16,128]{3,2,1,0:T(8,128)S(1)} %collective-permute-done.8.refs_1_, f32[1,256,128]{2,1,0:T(8,128)S(1)} %get-tuple-element.76.refs_1_.refs_2_, ...), custom_call_target="tpu_custom_call" | custom-call | flops 1 | bytes 1 | tf_op jit(solution)/shard_map/finish/pallas_call | solution.py:552
  80.9 0.0 all-to-all-done.1
  80.9 0.1 collective-permute-start.15
  80.9 1.5 %collective-permute-done.15.refs_1_ = f32[512,128]{1,0:T(8,128)S(1)} collective-permute-done((f32[512,128]{1,0:T(8,128)S(1)}, f32[512,128]{1,0:T(8,128)S(1)}, u32[]{:S(2)}, u32[]{:S(2)}) %collective-permute-start.15) | collective-permute-done | bytes 262176 | tf_op jit(solution)/shard_map/ppermute | solution.py:766
  82.5 1.1 %place.1 = f32[1024,128]{1,0:T(8,128)} custom-call(f32[512,128]{1,0:T(8,128)S(1)} %bitcast.5, f32[512,128]{1,0:T(8,128)S(1)} %collective-permute-done.15.refs_1_), custom_call_target="tpu_custom_call" | custom-call | flops 1 | bytes 1 | tf_op jit(solution)/shard_map/place/pallas_call | solution.py:552
  (1 shorter events, 0.0 us)
Async XLA Ops:
  2.6 15.8 %collective-permute-start = (f32[16,4,16,128]{3,2,1,0:T(8,128)S(1)}, f32[16,4,16,128]{3,2,1,0:T(8,128)S(1)}, u32[]{:S(2)}, u32[]{:S(2)}) collective-permute-start(f32[16,4,16,128]{3,2,1,0:T(8,128)S(1)} %get-tuple-element.55), channel_id=1, source_target_pairs={{0,4},{4,0},{8,12},{12,8},{16,20},{20,16},{24,28},{28,24},{1,5},{5... | collective-permute-start | bytes 1572872 | tf_op jit(solution)/shard_map/ppermute | solution.py:612
  5.6 14.6 %collective-permute-start.3 = (f32[512,128]{1,0:T(8,128)S(1)}, f32[512,128]{1,0:T(8,128)S(1)}, u32[]{:S(2)}, u32[]{:S(2)}) collective-permute-start(f32[512,128]{1,0:T(8,128)S(1)} %get-tuple-element.61.refs_5_.refs_3_), channel_id=1, source_target_pairs={{0,16},{4,20},{8,24},{12,28},{16,0},{20,4},{24,8},{28,12},{1,17},{... | collective-permute-start | bytes 786440 | tf_op jit(solution)/shard_map/ppermute | solution.py:651
  8.2 20.5 %collective-permute-start.2 = (f32[512,128]{1,0:T(8,128)S(1)}, f32[512,128]{1,0:T(8,128)S(1)}, u32[]{:S(2)}, u32[]{:S(2)}) collective-permute-start(f32[512,128]{1,0:T(8,128)S(1)} %get-tuple-element.61.refs_5_.refs_3_), channel_id=1, source_target_pairs={{0,8},{4,12},{8,0},{12,4},{16,24},{20,28},{24,16},{28,20},{1,9},{5... | collective-permute-start | bytes 786440 | tf_op jit(solution)/shard_map/ppermute | solution.py:651
  9.8 13.4 %collective-permute-start.1 = (f32[512,128]{1,0:T(8,128)S(1)}, f32[512,128]{1,0:T(8,128)S(1)}, u32[]{:S(2)}, u32[]{:S(2)}) collective-permute-start(f32[512,128]{1,0:T(8,128)S(1)} %get-tuple-element.53.refs_2_.refs_1_), channel_id=1, source_target_pairs={{0,4},{4,0},{8,12},{12,8},{16,20},{20,16},{24,28},{28,24},{1,5},{5... | collective-permute-start | bytes 786440 | tf_op jit(solution)/shard_map/ppermute | solution.py:613
  20.2 8.5 %collective-permute-start.4 = (f32[512,128]{1,0:T(8,128)S(1)}, f32[512,128]{1,0:T(8,128)S(1)}, u32[]{:S(2)}, u32[]{:S(2)}) collective-permute-start(f32[512,128]{1,0:T(8,128)S(1)} %collective-permute-done.3.refs_7_.refs_5_), channel_id=1, source_target_pairs={{0,8},{4,12},{8,0},{12,4},{16,24},{20,28},{24,16},{28,20},{1,9},{5... | collective-permute-start | bytes 786440 | tf_op jit(solution)/shard_map/ppermute | solution.py:651
  24.3 35.5 %collective-permute-start.6 = (f32[2,256,128]{2,1,0:T(8,128)S(1)}, f32[2,256,128]{2,1,0:T(8,128)S(1)}, u32[]{:S(2)}, u32[]{:S(2)}) collective-permute-start(f32[2,256,128]{2,1,0:T(8,128)S(1)} %get-tuple-element.73), channel_id=1, source_target_pairs={{0,8},{4,12},{8,0},{12,4},{16,24},{20,28},{24,16},{28,20},{1,9},{5... | collective-permute-start | bytes 786440 | tf_op jit(solution)/shard_map/ppermute | solution.py:661
  26.2 35.4 %collective-permute-start.7 = (f32[2,256,128]{2,1,0:T(8,128)S(1)}, f32[2,256,128]{2,1,0:T(8,128)S(1)}, u32[]{:S(2)}, u32[]{:S(2)}) collective-permute-start(f32[2,256,128]{2,1,0:T(8,128)S(1)} %get-tuple-element.75), channel_id=1, source_target_pairs={{0,16},{4,20},{8,24},{12,28},{16,0},{20,4},{24,8},{28,12},{1,17},{... | collective-permute-start | bytes 786440 | tf_op jit(solution)/shard_map/ppermute | solution.py:662
  36.3 3.2 %collective-permute-start.5 = (f32[512,128]{1,0:T(8,128)S(1)}, f32[512,128]{1,0:T(8,128)S(1)}, u32[]{:S(2)}, u32[]{:S(2)}) collective-permute-start(f32[512,128]{1,0:T(8,128)S(1)} %get-tuple-element.70), channel_id=1, source_target_pairs={{0,1},{1,0},{2,3},{3,2},{4,5},{5,4},{6,7},{7,6},{8,9},{9,8},{10,11... | collective-permute-start | bytes 786440 | tf_op jit(solution)/shard_map/ppermute | solution.py:678
  40.2 24.4 %all-to-all-start = ((f32[16,32,128]{2,1,0:T(8,128)}), f32[16,32,128]{2,1,0:T(8,128)S(1)}, u32[]{:S(2)}, u32[]{:S(2)}) async-start(f32[16,32,128]{2,1,0:T(8,128)} %bitcast.1.refs_0_), calls=%async_computation | async-start | bytes 524288 | tf_op jit(solution)/shard_map/all_to_all | solution.py:728
  57.7 11.4 %collective-permute-start.11 = (f32[2,32,512]{2,1,0:T(8,128)}, f32[2,32,512]{2,1,0:T(8,128)S(1)}, u32[]{:S(2)}, u32[]{:S(2)}) collective-permute-start(f32[2,32,512]{2,1,0:T(8,128)} %get-tuple-element.86), channel_id=1, source_target_pairs={{0,1},{1,0},{2,3},{3,2},{4,5},{5,4},{6,7},{7,6},{8,9},{9,8},{10,11... | collective-permute-start | bytes 393224 | tf_op jit(solution)/shard_map/ppermute | solution.py:715
  58.0 13.2 %collective-permute-start.12 = (f32[2,32,512]{2,1,0:T(8,128)S(1)}, f32[2,32,512]{2,1,0:T(8,128)S(1)}, u32[]{:S(2)}, u32[]{:S(2)}) collective-permute-start(f32[2,32,512]{2,1,0:T(8,128)S(1)} %get-tuple-element.87), channel_id=1, source_target_pairs={{0,2},{1,3},{2,0},{3,1},{4,6},{5,7},{6,4},{7,5},{8,10},{9,11},{10,... | collective-permute-start | bytes 393224 | tf_op jit(solution)/shard_map/ppermute | solution.py:715
  59.8 11.4 %collective-permute-start.13 = (f32[2,32,512]{2,1,0:T(8,128)S(1)}, f32[2,32,512]{2,1,0:T(8,128)S(1)}, u32[]{:S(2)}, u32[]{:S(2)}) collective-permute-start(f32[2,32,512]{2,1,0:T(8,128)S(1)} %get-tuple-element.88), channel_id=1, source_target_pairs={{0,3},{1,2},{2,1},{3,0},{4,7},{5,6},{6,5},{7,4},{8,11},{9,10},{10,... | collective-permute-start | bytes 393224 | tf_op jit(solution)/shard_map/ppermute | solution.py:715
  59.8 18.9 %collective-permute-start.8 = (f32[16,4,16,128]{3,2,1,0:T(8,128)S(1)}, f32[16,4,16,128]{3,2,1,0:T(8,128)S(1)}, u32[]{:S(2)}, u32[]{:S(2)}) collective-permute-start(f32[16,4,16,128]{3,2,1,0:T(8,128)S(1)} %pair_peer.1.refs_0_), channel_id=1, source_target_pairs={{0,4},{4,0},{8,12},{12,8},{16,20},{20,16},{24,28},{28,24},{1,5},{5... | collective-permute-start | bytes 1572872 | tf_op jit(solution)/shard_map/ppermute | solution.py:712
  62.3 15.4 %collective-permute-start.9 = (f32[1,256,128]{2,1,0:T(8,128)}, f32[1,256,128]{2,1,0:T(8,128)S(1)}, u32[]{:S(2)}, u32[]{:S(2)}) collective-permute-start(f32[1,256,128]{2,1,0:T(8,128)} %get-tuple-element.78), channel_id=1, source_target_pairs={{0,16},{4,20},{8,24},{12,28},{16,0},{20,4},{24,8},{28,12},{1,17},{... | collective-permute-start | bytes 393224 | tf_op jit(solution)/shard_map/ppermute | solution.py:724
  65.4 15.5 %all-to-all-start.1 = ((f32[16,32,128]{2,1,0:T(8,128)}), f32[16,32,128]{2,1,0:T(8,128)S(1)}, u32[]{:S(2)}, u32[]{:S(2)}) async-start(f32[16,32,128]{2,1,0:T(8,128)} %weight_sum.1.refs_0_), calls=%async_computation.1 | async-start | bytes 524288 | tf_op jit(solution)/shard_map/all_to_all | solution.py:739
  69.2 9.5 %collective-permute-start.10 = (f32[1,256,128]{2,1,0:T(8,128)S(1)}, f32[1,256,128]{2,1,0:T(8,128)S(1)}, u32[]{:S(2)}, u32[]{:S(2)}) collective-permute-start(f32[1,256,128]{2,1,0:T(8,128)S(1)} %get-tuple-element.80), channel_id=1, source_target_pairs={{0,8},{4,12},{8,0},{12,4},{16,24},{20,28},{24,16},{28,20},{1,9},{5... | collective-permute-start | bytes 393224 | tf_op jit(solution)/shard_map/ppermute | solution.py:725
  71.2 7.5 %collective-permute-start.14 = (f32[32,512]{1,0:T(8,128)S(1)}, f32[32,512]{1,0:T(8,128)S(1)}, u32[]{:S(2)}, u32[]{:S(2)}) collective-permute-start(f32[32,512]{1,0:T(8,128)S(1)} %get-tuple-element.90), channel_id=1, source_target_pairs={{0,4},{4,0},{8,12},{12,8},{16,20},{20,16},{24,28},{28,24},{1,5},{5... | collective-permute-start | bytes 196616 | tf_op jit(solution)/shard_map/ppermute | solution.py:741
  80.9 1.6 %collective-permute-start.15 = (f32[512,128]{1,0:T(8,128)S(1)}, f32[512,128]{1,0:T(8,128)S(1)}, u32[]{:S(2)}, u32[]{:S(2)}) collective-permute-start(f32[512,128]{1,0:T(8,128)S(1)} %bitcast.4), channel_id=1, source_target_pairs={{0,1},{1,0},{2,3},{3,2},{4,5},{5,4},{6,7},{7,6},{8,9},{9,8},{10,11... | collective-permute-start | bytes 786440 | tf_op jit(solution)/shard_map/ppermute | solution.py:766

commit v24 on v21

--- a/solution.py
+++ b/solution.py
@@ -208,7 +208,7 @@
     def store(step, found):
         partial_ref[step] = found
 
-    right_phase(left_ref, out_ref, left_flip, store, 8)
+    right_phase(left_ref, out_ref, left_flip, store, 1)
     channels = ENTRY_CHANNELS
     wide = weight_rows.shape[1]
     for step in range(channels // fold):
@@ -227,7 +227,7 @@
     gradient_phase(blocks, cotangent_ref, out_ref, spread_ref, weight_cat)
 
 
-def right_phase(left_ref, factor_ref, left_flip, store, unroll):
+def right_phase(left_ref, factor_ref, left_flip, store, loops):
     sequences = left_ref.shape[1]
     lanes = factor_ref.shape[2] // 4
     flip_high, flip_low = halves((left_ref[...] * (1.0 / sequences)).T)
@@ -247,7 +247,9 @@
         return carry
 
     count = factor_ref.shape[1] // (2 * ENTRY_CHANNELS)
-    lax.fori_loop(0, count, step_of, 0, unroll=unroll)
+    size = count // loops
+    for at in range(loops):
+        lax.fori_loop(at * size, (at + 1) * size, step_of, 0, unroll=min(size, 8))
 
 
 def rows_of_step(refs, step, half, lanes):
@@ -289,7 +291,7 @@
                         start : start + depth
                     ]
 
-    right_phase(left_ref, peer_ref, left_flip, store, 4)
+    right_phase(left_ref, peer_ref, left_flip, store, 2)
 
 
 def halve_kernel(keep_ref, found_ref, keep_out, send_out):
@@ -675,11 +677,6 @@
 
     pair_other = pair(outer_peer, [pieces], "pair_peer")
     pair_found = lax.ppermute(pair_other, "blk", partner)
-    _, *left_parts = lax.optimization_barrier((pair_other, *left_parts))
-    left_parts = [
-        lax.ppermute(part, "inner", inner_moves[slot]) if slot else part
-        for slot, part in enumerate(left_parts)
-    ]
     slot = blocks // 4
     while slot:
         part = shape(slot, channels * depth, sequences)
@@ -689,6 +686,11 @@
         right_send = lax.ppermute(right_send, "blk", slot_moves[slot])
         slot = slot // 2
 
+    _, *left_parts = lax.optimization_barrier((right_keep, *left_parts))
+    left_parts = [
+        lax.ppermute(part, "inner", inner_moves[slot]) if slot else part
+        for slot, part in enumerate(left_parts)
+    ]
     pieces = lax.all_to_all(pieces, everyone, 0, 0, axis_index_groups=core_groups)
     pieces = call(
         spread_sum_kernel,

time: 77 us -> 76.9 us (level); the launches traced: 76.6 us -> 75.6 us
  starting transfers between devices: 30.6 us -> 34.1 us
  waiting for transfers between devices: 9.85 us -> 7.21 us
  Pallas kernels: 34.6 us -> 32.7 us
    all_to_all x2, waiting for transfers between devices: 2.55 us -> 0.42 us  [local(): lax.all_to_all(pieces, everyone, 0, 0, axis_index_groups=core_groups)]
    pallas_call x13, Pallas kernels: 34.6 us -> 32.7 us  [run(): pl.pallas_call(lambda *refs: kernel(*refs[len(after):]), out_shape=out_sh...]
    all_to_all x2, starting transfers between devices: 11.2 us -> 13 us  [local(): lax.all_to_all(pieces, everyone, 0, 0, axis_index_groups=core_groups)]
    ppermute x1, starting transfers between devices: 0.82 us -> 2.42 us  [local(): right_send = lax.ppermute(right_send, 'blk', slot_moves[slot])]
  transfers between devices with their start and end apart: 16 -> 16, of which waited for: 6 -> 5; matrix products, arithmetic and copies ran while one was open for 1% -> 1% of each run, Pallas kernels for 41% -> 39%
where the time goes in v24:
time: 76.9 us; the launch traced here: 75.6 us
  starting transfers between devices  34.1 us (44%)
  Pallas kernels  32.7 us (43%)
  waiting for transfers between devices  7.21 us (9%)
  between operations  0.82 us (1%)
    pallas_call x13, Pallas kernels, run(): pl.pallas_call(lambda *refs: kernel(*refs[len(after):]), out_shape=out_sh...  32.7 us
    all_to_all x2, starting transfers between devices, local(): lax.all_to_all(pieces, everyone, 0, 0, axis_index_groups=core_groups)  13 us
    ppermute x3, starting transfers between devices, local(): rights[slot + distance] = lax.ppermute(sent, 'blk', slot_moves[distance])  6.36 us
    ppermute x1, waiting for transfers between devices, local(): cotangent_peer = lax.ppermute(cotangent_send, 'blk', partner)  4.3 us
    ppermute x1, starting transfers between devices, local(): cotangent_peer = lax.ppermute(cotangent_send, 'blk', partner)  3.03 us
    ppermute x1, starting transfers between devices, local(): right_send = lax.ppermute(right_send, 'blk', slot_moves[blocks // 2])  2.87 us
    ppermute x1, starting transfers between devices, local(): right_send = lax.ppermute(right_send, 'blk', slot_moves[slot])  2.42 us
    ppermute x3, starting transfers between devices, local(): lax.ppermute(part, 'inner', inner_moves[slot])  2.13 us
  transfers between devices with their start and end apart: 16, of which 5 were waited for; matrix products, arithmetic and copies ran while one was open for 1% of the time, Pallas kernels for 39%

profile of v24, /device:TPU:0, one launch (start us, length us, event | category | flops | bytes accessed | tf_op | source)
XLA Modules:
  0.0 75.6 jit_solution(3892493411812444930)
XLA Ops:
  0.6 2.0 %prepare.1 = (f32[512,128]{1,0:T(8,128)S(1)}, f32[512,128]{1,0:T(8,128)S(1)}, f32[16,4,16,128]{3,2,1,0:T(8,128)S(1)}, f32[16,4,16,128]{3,2,1,0:T(8,128)S(1)}, f32[1024,128]{1,0:T(8,128)S(1)}) custom-call(f32[16,4,2,16,128]{4,3,2,1,0:T(8,128)} %bitcast.6, f32[16,4096]{1,0:T(8,128)} %refs_1_.1, f32[16,4096]{1,0:T(8,128)} %refs_2_.1, f32[1024,128]{1,0:T(8,128)} %refs_3_.1), custom_call_target="tpu_custom_call" | custom-call | flops 1 | bytes 1 | tf_op jit(solution)/shard_map/prepare/pallas_call | solution.py:520
  2.6 3.0 %collective-permute-start = (f32[16,4,16,128]{3,2,1,0:T(8,128)S(1)}, f32[16,4,16,128]{3,2,1,0:T(8,128)S(1)}, u32[]{:S(2)}, u32[]{:S(2)}) collective-permute-start(f32[16,4,16,128]{3,2,1,0:T(8,128)S(1)} %get-tuple-element.51), channel_id=1, source_target_pairs={{0,4},{4,0},{8,12},{12,8},{16,20},{20,16},{24,28},{28,24},{1,5},{5... | collective-permute-start | bytes 1572872 | tf_op jit(solution)/shard_map/ppermute | solution.py:580
  5.6 2.6 %collective-permute-start.3 = (f32[512,128]{1,0:T(8,128)S(1)}, f32[512,128]{1,0:T(8,128)S(1)}, u32[]{:S(2)}, u32[]{:S(2)}) collective-permute-start(f32[512,128]{1,0:T(8,128)S(1)} %get-tuple-element.57.refs_5_.refs_3_), channel_id=1, source_target_pairs={{0,16},{4,20},{8,24},{12,28},{16,0},{20,4},{24,8},{28,12},{1,17},{... | collective-permute-start | bytes 786440 | tf_op jit(solution)/shard_map/ppermute | solution.py:619
  8.2 1.6 %collective-permute-start.2 = (f32[512,128]{1,0:T(8,128)S(1)}, f32[512,128]{1,0:T(8,128)S(1)}, u32[]{:S(2)}, u32[]{:S(2)}) collective-permute-start(f32[512,128]{1,0:T(8,128)S(1)} %get-tuple-element.57.refs_5_.refs_3_), channel_id=1, source_target_pairs={{0,8},{4,12},{8,0},{12,4},{16,24},{20,28},{24,16},{28,20},{1,9},{5... | collective-permute-start | bytes 786440 | tf_op jit(solution)/shard_map/ppermute | solution.py:619
  9.8 0.5 collective-permute-start.1
  10.3 3.8 %gradient_own.1 = (bf16[8,512,512]{2,1,0:T(8,128)(2,1)S(1)}, bf16[8,2,256,256]{3,2,1,0:T(8,128)(2,1)S(1)}, f32[8,128,256]{2,1,0:T(8,128)S(1)}, bf16[512,768]{1,0:T(8,128)(2,1)S(1)}, bf16[512,512]{1,0:T(8,128)(2,1)}) custom-call(f32[1024,128]{1,0:T(8,128)S(1)} %get-tuple-element.47.refs_0_, f32[16,4,16,128]{3,2,1,0:T(8,128)S(1)} %get-tuple-element.48.refs_1_, ...), custom_call_target="tpu_custom_call" | custom-call | flops 1 | bytes 1 | tf_op jit(solution)/shard_map/gradient_own/pallas_call | solution.py:520
  14.1 4.3 %collective-permute-done.refs_1_ = f32[16,4,16,128]{3,2,1,0:T(8,128)S(1)} collective-permute-done((f32[16,4,16,128]{3,2,1,0:T(8,128)S(1)}, f32[16,4,16,128]{3,2,1,0:T(8,128)S(1)}, u32[]{:S(2)}, u32[]{:S(2)}) %collective-permute-start) | collective-permute-done | bytes 524320 | tf_op jit(solution)/shard_map/ppermute | solution.py:580
  18.4 1.8 %gradient_peer.1 = (bf16[8,512,512]{2,1,0:T(8,128)(2,1)S(1)}, bf16[8,2,256,256]{3,2,1,0:T(8,128)(2,1)S(1)}) custom-call(bf16[512,768]{1,0:T(8,128)(2,1)S(1)} %get-tuple-element.50.refs_0_, f32[16,4,16,128]{3,2,1,0:T(8,128)S(1)} %collective-permute-done.refs_1_), custom_call_target="tpu_custom_call" | custom-call | flops 1 | bytes 1 | tf_op jit(solution)/shard_map/gradient_peer/pallas_call | solution.py:520
  20.2 0.0 collective-permute-done.3.refs_7_.refs_5_
  20.2 2.2 %collective-permute-start.4 = (f32[512,128]{1,0:T(8,128)S(1)}, f32[512,128]{1,0:T(8,128)S(1)}, u32[]{:S(2)}, u32[]{:S(2)}) collective-permute-start(f32[512,128]{1,0:T(8,128)S(1)} %collective-permute-done.3.refs_7_.refs_5_), channel_id=1, source_target_pairs={{0,8},{4,12},{8,0},{12,4},{16,24},{20,28},{24,16},{28,20},{1,9},{5... | collective-permute-start | bytes 786440 | tf_op jit(solution)/shard_map/ppermute | solution.py:619
  22.4 0.7 collective-permute-done.1.refs_1_.refs_2_
  23.2 1.1 %right_parts.1 = (f32[2,512,128]{2,1,0:T(8,128)S(1)}, f32[2,512,128]{2,1,0:T(8,128)S(1)}) custom-call(bf16[8,512,512]{2,1,0:T(8,128)(2,1)S(1)} %get-tuple-element.52.refs_0_.refs_2_, f32[512,128]{1,0:T(8,128)S(1)} %collective-permute-done.1.refs_1_.refs_2_, f32[8,128,256]{2,1,0:T(8,128)S(1)} %get-tuple-element.53.refs_2_), custom_call_target="tpu_custom_call" | custom-call | flops 1 | bytes 1 | tf_op jit(solution)/shard_map/right_parts/pallas_call | solution.py:520
  24.3 2.9 %collective-permute-start.6 = (f32[2,512,128]{2,1,0:T(8,128)S(1)}, f32[2,512,128]{2,1,0:T(8,128)S(1)}, u32[]{:S(2)}, u32[]{:S(2)}) collective-permute-start(f32[2,512,128]{2,1,0:T(8,128)S(1)} %get-tuple-element.69), channel_id=1, source_target_pairs={{0,16},{4,20},{8,24},{12,28},{16,0},{20,4},{24,8},{28,12},{1,17},{... | collective-permute-start | bytes 1572872 | tf_op jit(solution)/shard_map/ppermute | solution.py:629
  27.2 0.0 collective-permute-done.2.refs_6_.refs_4_
  27.2 0.0 collective-permute-done.4.refs_8_.refs_6_
  27.2 7.5 %weight.1 = (f32[512,128]{1,0:T(8,128)S(1)}, f32[512,128]{1,0:T(8,128)S(1)}, bf16[8,512,512]{2,1,0:T(8,128)(2,1)}, bf16[8,512,512]{2,1,0:T(8,128)(2,1)}) custom-call(f32[2,512,128]{2,1,0:T(8,128)S(1)} %get-tuple-element.54.refs_0_.refs_1_, f32[512,128]{1,0:T(8,128)S(1)} %get-tuple-element.49.refs_2_.refs_1_, ...), custom_call_target="tpu_custom_call" | custom-call | flops 12884901888 | bytes 1 | tf_op jit(solution)/shard_map/weight/pallas_call | solution.py:520
  34.7 0.1 collective-permute-start.5
  34.8 2.4 %left_parts.1 = (f32[2,32,512]{2,1,0:T(8,128)S(1)}, f32[2,32,512]{2,1,0:T(8,128)S(1)}, f32[2,32,512]{2,1,0:T(8,128)S(1)}, f32[2,32,512]{2,1,0:T(8,128)S(1)}) custom-call(f32[512,128]{1,0:T(8,128)S(1)} %get-tuple-element.65.refs_0_, bf16[8,512,512]{2,1,0:T(8,128)(2,1)S(1)} %get-tuple-element.60.refs_1_, ...), custom_call_target="tpu_custom_call" | custom-call | flops 6442450944 | bytes 1 | tf_op jit(solution)/shard_map/left_parts/pallas_call | solution.py:520
  37.3 0.0 collective-permute-done.5
  37.3 0.7 add.3
  38.0 7.3 %all-to-all-start = ((f32[16,32,128]{2,1,0:T(8,128)}), f32[16,32,128]{2,1,0:T(8,128)S(1)}, u32[]{:S(2)}, u32[]{:S(2)}) async-start(f32[16,32,128]{2,1,0:T(8,128)} %bitcast.1.refs_0_), calls=%async_computation | async-start | bytes 524288 | tf_op jit(solution)/shard_map/all_to_all | solution.py:694
  45.4 5.0 %pair_peer.1.refs_0_ = f32[16,4,16,128]{3,2,1,0:T(8,128)S(1)} custom-call(f32[16,32,128]{2,1,0:T(8,128)} %bitcast.1.refs_0_, bf16[8,512,512]{2,1,0:T(8,128)(2,1)} %get-tuple-element.67.refs_1_, bf16[512,512]{1,0:T(8,128)(2,1)} %get-tuple-element.68.refs_2_), custom_call_target="tpu_custom_call" | custom-call | flops 6442450944 | bytes 1 | tf_op jit(solution)/shard_map/pair_peer/pallas_call | solution.py:520
  50.3 0.0 collective-permute-done.6.refs_2_
  50.3 0.1 right_halve.1
  50.4 0.3 collective-permute-start.9
  50.7 1.8 %collective-permute-start.10 = (f32[2,32,512]{2,1,0:T(8,128)S(1)}, f32[2,32,512]{2,1,0:T(8,128)S(1)}, u32[]{:S(2)}, u32[]{:S(2)}) collective-permute-start(f32[2,32,512]{2,1,0:T(8,128)S(1)} %get-tuple-element.79), channel_id=1, source_target_pairs={{0,2},{1,3},{2,0},{3,1},{4,6},{5,7},{6,4},{7,5},{8,10},{9,11},{10,... | collective-permute-start | bytes 393224 | tf_op jit(solution)/shard_map/ppermute | solution.py:691
  52.5 0.1 collective-permute-start.11
  52.5 1.7 %collective-permute-start.7 = (f32[16,4,16,128]{3,2,1,0:T(8,128)S(1)}, f32[16,4,16,128]{3,2,1,0:T(8,128)S(1)}, u32[]{:S(2)}, u32[]{:S(2)}) collective-permute-start(f32[16,4,16,128]{3,2,1,0:T(8,128)S(1)} %pair_peer.1.refs_0_), channel_id=1, source_target_pairs={{0,4},{4,0},{8,12},{12,8},{16,20},{20,16},{24,28},{28,24},{1,5},{5... | collective-permute-start | bytes 1572872 | tf_op jit(solution)/shard_map/ppermute | solution.py:679
  54.3 2.4 %collective-permute-start.8 = (f32[1,512,128]{2,1,0:T(8,128)S(1)}, f32[1,512,128]{2,1,0:T(8,128)S(1)}, u32[]{:S(2)}, u32[]{:S(2)}) collective-permute-start(f32[1,512,128]{2,1,0:T(8,128)S(1)} %get-tuple-element.72), channel_id=1, source_target_pairs={{0,8},{4,12},{8,0},{12,4},{16,24},{20,28},{24,16},{28,20},{1,9},{5... | collective-permute-start | bytes 786440 | tf_op jit(solution)/shard_map/ppermute | solution.py:686
  56.7 0.0 all-to-all-done.refs_2_
  56.7 0.8 weight_sum.1.refs_0_
  57.4 5.7 %all-to-all-start.1 = ((f32[16,32,128]{2,1,0:T(8,128)}), f32[16,32,128]{2,1,0:T(8,128)S(1)}, u32[]{:S(2)}, u32[]{:S(2)}) async-start(f32[16,32,128]{2,1,0:T(8,128)} %weight_sum.1.refs_0_), calls=%async_computation.1 | async-start | bytes 524288 | tf_op jit(solution)/shard_map/all_to_all | solution.py:705
  63.1 0.0 collective-permute-done.9.refs_2_
  63.1 0.0 collective-permute-done.10.refs_3_
  63.2 0.0 collective-permute-done.11.refs_4_
  63.2 2.0 %collective-permute-start.12 = (f32[32,512]{1,0:T(8,128)S(1)}, f32[32,512]{1,0:T(8,128)S(1)}, u32[]{:S(2)}, u32[]{:S(2)}) collective-permute-start(f32[32,512]{1,0:T(8,128)S(1)} %get-tuple-element.82), channel_id=1, source_target_pairs={{0,4},{4,0},{8,12},{12,8},{16,20},{20,16},{24,28},{28,24},{1,5},{5... | collective-permute-start | bytes 196616 | tf_op jit(solution)/shard_map/ppermute | solution.py:707
  65.2 5.0 %pair_own.1.refs_0_ = f32[16,4,16,128]{3,2,1,0:T(8,128)S(1)} custom-call(f32[16,32,128]{2,1,0:T(8,128)} %weight_sum.1.refs_0_, bf16[8,512,512]{2,1,0:T(8,128)(2,1)} %get-tuple-element.71.refs_1_, bf16[512,512]{1,0:T(8,128)(2,1)} %get-tuple-element.68.refs_2_), custom_call_target="tpu_custom_call" | custom-call | flops 6442450944 | bytes 1 | tf_op jit(solution)/shard_map/pair_own/pallas_call | solution.py:520
  70.2 0.0 collective-permute-done.8.refs_3_
  70.2 0.0 collective-permute-done.7.refs_1_
  70.2 0.2 collective-permute-done.12.refs_5_
  70.4 2.2 %finish.1 = (f32[16,4,2,16,128]{4,3,2,1,0:T(8,128)}, f32[16,1024]{1,0:T(8,128)}, f32[16,4096]{1,0:T(8,128)}) custom-call(f32[16,4,16,128]{3,2,1,0:T(8,128)S(1)} %pair_own.1.refs_0_, f32[16,4,16,128]{3,2,1,0:T(8,128)S(1)} %collective-permute-done.7.refs_1_, f32[1,512,128]{2,1,0:T(8,128)S(1)} %get-tuple-element.70.refs_1_.refs_2_, ...), custom_call_target="tpu_custom_call" | custom-call | flops 1 | bytes 1 | tf_op jit(solution)/shard_map/finish/pallas_call | solution.py:520
  72.5 0.4 all-to-all-done.1
  73.0 0.0 collective-permute-start.13
  73.0 1.5 %collective-permute-done.13.refs_1_ = f32[512,128]{1,0:T(8,128)S(1)} collective-permute-done((f32[512,128]{1,0:T(8,128)S(1)}, f32[512,128]{1,0:T(8,128)S(1)}, u32[]{:S(2)}, u32[]{:S(2)}) %collective-permute-start.13) | collective-permute-done | bytes 262176 | tf_op jit(solution)/shard_map/ppermute | solution.py:732
  74.5 1.1 %place.1 = f32[1024,128]{1,0:T(8,128)} custom-call(f32[512,128]{1,0:T(8,128)S(1)} %bitcast.5, f32[512,128]{1,0:T(8,128)S(1)} %collective-permute-done.13.refs_1_), custom_call_target="tpu_custom_call" | custom-call | flops 1 | bytes 1 | tf_op jit(solution)/shard_map/place/pallas_call | solution.py:520
  (1 shorter events, 0.0 us)
Async XLA Ops:
  2.6 15.8 %collective-permute-start = (f32[16,4,16,128]{3,2,1,0:T(8,128)S(1)}, f32[16,4,16,128]{3,2,1,0:T(8,128)S(1)}, u32[]{:S(2)}, u32[]{:S(2)}) collective-permute-start(f32[16,4,16,128]{3,2,1,0:T(8,128)S(1)} %get-tuple-element.51), channel_id=1, source_target_pairs={{0,4},{4,0},{8,12},{12,8},{16,20},{20,16},{24,28},{28,24},{1,5},{5... | collective-permute-start | bytes 1572872 | tf_op jit(solution)/shard_map/ppermute | solution.py:580
  5.6 14.6 %collective-permute-start.3 = (f32[512,128]{1,0:T(8,128)S(1)}, f32[512,128]{1,0:T(8,128)S(1)}, u32[]{:S(2)}, u32[]{:S(2)}) collective-permute-start(f32[512,128]{1,0:T(8,128)S(1)} %get-tuple-element.57.refs_5_.refs_3_), channel_id=1, source_target_pairs={{0,16},{4,20},{8,24},{12,28},{16,0},{20,4},{24,8},{28,12},{1,17},{... | collective-permute-start | bytes 786440 | tf_op jit(solution)/shard_map/ppermute | solution.py:619
  8.2 19.0 %collective-permute-start.2 = (f32[512,128]{1,0:T(8,128)S(1)}, f32[512,128]{1,0:T(8,128)S(1)}, u32[]{:S(2)}, u32[]{:S(2)}) collective-permute-start(f32[512,128]{1,0:T(8,128)S(1)} %get-tuple-element.57.refs_5_.refs_3_), channel_id=1, source_target_pairs={{0,8},{4,12},{8,0},{12,4},{16,24},{20,28},{24,16},{28,20},{1,9},{5... | collective-permute-start | bytes 786440 | tf_op jit(solution)/shard_map/ppermute | solution.py:619
  9.8 13.4 %collective-permute-start.1 = (f32[512,128]{1,0:T(8,128)S(1)}, f32[512,128]{1,0:T(8,128)S(1)}, u32[]{:S(2)}, u32[]{:S(2)}) collective-permute-start(f32[512,128]{1,0:T(8,128)S(1)} %get-tuple-element.49.refs_2_.refs_1_), channel_id=1, source_target_pairs={{0,4},{4,0},{8,12},{12,8},{16,20},{20,16},{24,28},{28,24},{1,5},{5... | collective-permute-start | bytes 786440 | tf_op jit(solution)/shard_map/ppermute | solution.py:581
  20.2 6.9 %collective-permute-start.4 = (f32[512,128]{1,0:T(8,128)S(1)}, f32[512,128]{1,0:T(8,128)S(1)}, u32[]{:S(2)}, u32[]{:S(2)}) collective-permute-start(f32[512,128]{1,0:T(8,128)S(1)} %collective-permute-done.3.refs_7_.refs_5_), channel_id=1, source_target_pairs={{0,8},{4,12},{8,0},{12,4},{16,24},{20,28},{24,16},{28,20},{1,9},{5... | collective-permute-start | bytes 786440 | tf_op jit(solution)/shard_map/ppermute | solution.py:619
  24.3 26.0 %collective-permute-start.6 = (f32[2,512,128]{2,1,0:T(8,128)S(1)}, f32[2,512,128]{2,1,0:T(8,128)S(1)}, u32[]{:S(2)}, u32[]{:S(2)}) collective-permute-start(f32[2,512,128]{2,1,0:T(8,128)S(1)} %get-tuple-element.69), channel_id=1, source_target_pairs={{0,16},{4,20},{8,24},{12,28},{16,0},{20,4},{24,8},{28,12},{1,17},{... | collective-permute-start | bytes 1572872 | tf_op jit(solution)/shard_map/ppermute | solution.py:629
  34.7 2.5 %collective-permute-start.5 = (f32[512,128]{1,0:T(8,128)S(1)}, f32[512,128]{1,0:T(8,128)S(1)}, u32[]{:S(2)}, u32[]{:S(2)}) collective-permute-start(f32[512,128]{1,0:T(8,128)S(1)} %get-tuple-element.66), channel_id=1, source_target_pairs={{0,1},{1,0},{2,3},{3,2},{4,5},{5,4},{6,7},{7,6},{8,9},{9,8},{10,11... | collective-permute-start | bytes 786440 | tf_op jit(solution)/shard_map/ppermute | solution.py:645
  38.0 18.7 %all-to-all-start = ((f32[16,32,128]{2,1,0:T(8,128)}), f32[16,32,128]{2,1,0:T(8,128)S(1)}, u32[]{:S(2)}, u32[]{:S(2)}) async-start(f32[16,32,128]{2,1,0:T(8,128)} %bitcast.1.refs_0_), calls=%async_computation | async-start | bytes 524288 | tf_op jit(solution)/shard_map/all_to_all | solution.py:694
  50.4 12.7 %collective-permute-start.9 = (f32[2,32,512]{2,1,0:T(8,128)S(1)}, f32[2,32,512]{2,1,0:T(8,128)S(1)}, u32[]{:S(2)}, u32[]{:S(2)}) collective-permute-start(f32[2,32,512]{2,1,0:T(8,128)S(1)} %get-tuple-element.78), channel_id=1, source_target_pairs={{0,1},{1,0},{2,3},{3,2},{4,5},{5,4},{6,7},{7,6},{8,9},{9,8},{10,11... | collective-permute-start | bytes 393224 | tf_op jit(solution)/shard_map/ppermute | solution.py:691
  50.7 12.5 %collective-permute-start.10 = (f32[2,32,512]{2,1,0:T(8,128)S(1)}, f32[2,32,512]{2,1,0:T(8,128)S(1)}, u32[]{:S(2)}, u32[]{:S(2)}) collective-permute-start(f32[2,32,512]{2,1,0:T(8,128)S(1)} %get-tuple-element.79), channel_id=1, source_target_pairs={{0,2},{1,3},{2,0},{3,1},{4,6},{5,7},{6,4},{7,5},{8,10},{9,11},{10,... | collective-permute-start | bytes 393224 | tf_op jit(solution)/shard_map/ppermute | solution.py:691
  52.5 10.7 %collective-permute-start.11 = (f32[2,32,512]{2,1,0:T(8,128)S(1)}, f32[2,32,512]{2,1,0:T(8,128)S(1)}, u32[]{:S(2)}, u32[]{:S(2)}) collective-permute-start(f32[2,32,512]{2,1,0:T(8,128)S(1)} %get-tuple-element.80), channel_id=1, source_target_pairs={{0,3},{1,2},{2,1},{3,0},{4,7},{5,6},{6,5},{7,4},{8,11},{9,10},{10,... | collective-permute-start | bytes 393224 | tf_op jit(solution)/shard_map/ppermute | solution.py:691
  52.5 17.6 %collective-permute-start.7 = (f32[16,4,16,128]{3,2,1,0:T(8,128)S(1)}, f32[16,4,16,128]{3,2,1,0:T(8,128)S(1)}, u32[]{:S(2)}, u32[]{:S(2)}) collective-permute-start(f32[16,4,16,128]{3,2,1,0:T(8,128)S(1)} %pair_peer.1.refs_0_), channel_id=1, source_target_pairs={{0,4},{4,0},{8,12},{12,8},{16,20},{20,16},{24,28},{28,24},{1,5},{5... | collective-permute-start | bytes 1572872 | tf_op jit(solution)/shard_map/ppermute | solution.py:679
  54.3 15.9 %collective-permute-start.8 = (f32[1,512,128]{2,1,0:T(8,128)S(1)}, f32[1,512,128]{2,1,0:T(8,128)S(1)}, u32[]{:S(2)}, u32[]{:S(2)}) collective-permute-start(f32[1,512,128]{2,1,0:T(8,128)S(1)} %get-tuple-element.72), channel_id=1, source_target_pairs={{0,8},{4,12},{8,0},{12,4},{16,24},{20,28},{24,16},{28,20},{1,9},{5... | collective-permute-start | bytes 786440 | tf_op jit(solution)/shard_map/ppermute | solution.py:686
  57.4 15.5 %all-to-all-start.1 = ((f32[16,32,128]{2,1,0:T(8,128)}), f32[16,32,128]{2,1,0:T(8,128)S(1)}, u32[]{:S(2)}, u32[]{:S(2)}) async-start(f32[16,32,128]{2,1,0:T(8,128)} %weight_sum.1.refs_0_), calls=%async_computation.1 | async-start | bytes 524288 | tf_op jit(solution)/shard_map/all_to_all | solution.py:705
  63.2 7.2 %collective-permute-start.12 = (f32[32,512]{1,0:T(8,128)S(1)}, f32[32,512]{1,0:T(8,128)S(1)}, u32[]{:S(2)}, u32[]{:S(2)}) collective-permute-start(f32[32,512]{1,0:T(8,128)S(1)} %get-tuple-element.82), channel_id=1, source_target_pairs={{0,4},{4,0},{8,12},{12,8},{16,20},{20,16},{24,28},{28,24},{1,5},{5... | collective-permute-start | bytes 196616 | tf_op jit(solution)/shard_map/ppermute | solution.py:707
  73.0 1.5 %collective-permute-start.13 = (f32[512,128]{1,0:T(8,128)S(1)}, f32[512,128]{1,0:T(8,128)S(1)}, u32[]{:S(2)}, u32[]{:S(2)}) collective-permute-start(f32[512,128]{1,0:T(8,128)S(1)} %bitcast.4), channel_id=1, source_target_pairs={{0,1},{1,0},{2,3},{3,2},{4,5},{5,4},{6,7},{7,6},{8,9},{9,8},{10,11... | collective-permute-start | bytes 786440 | tf_op jit(solution)/shard_map/ppermute | solution.py:732

commit v25 on v24

--- a/solution.py
+++ b/solution.py
@@ -615,7 +615,7 @@
         for slot in list(rights):
             sent = rights[slot]
             if slot:
-                sent, _ = lax.optimization_barrier((sent, grad_peer))
+                sent, _ = lax.optimization_barrier((sent, grad_own))
             rights[slot + distance] = lax.ppermute(sent, "blk", slot_moves[distance])
         distance = distance // 2
     rights = [rights[slot] for slot in range(blocks)]

time: 76.9 us -> 78.7 us (1.023); the launches traced: 75.6 us -> 78.3 us
  waiting for transfers between devices: 7.21 us -> 13.7 us
  starting transfers between devices: 34.1 us -> 30.4 us
    ppermute x3, waiting for transfers between devices: 0.01 us -> 5.94 us  [local(): rights[slot + distance] = lax.ppermute(sent, 'blk', slot_moves[distance])]
    ppermute x1, waiting for transfers between devices: 4.3 us -> 0.01 us  [local(): cotangent_peer = lax.ppermute(cotangent_send, 'blk', partner)]
    ppermute x1, waiting for transfers between devices: 0.01 us -> 2.78 us  [local(): right_send = lax.ppermute(right_send, 'blk', slot_moves[blocks // 2])]
    ppermute x1, starting transfers between devices: 1.73 us -> 0.01 us  [local(): pair_found = lax.ppermute(pair_other, 'blk', partner)]
    ppermute x3, starting transfers between devices: 6.36 us -> 4.73 us  [local(): rights[slot + distance] = lax.ppermute(sent, 'blk', slot_moves[distance])]
    ppermute x1, waiting for transfers between devices: 0.19 us -> 1.64 us  [local(): left_found = [left_own, lax.ppermute(left_send, 'blk', partner)]]
    ppermute x1, waiting for transfers between devices: 0.01 us -> 1.08 us  [local(): pair_found = lax.ppermute(pair_other, 'blk', partner)]
    ppermute x1, starting transfers between devices: 2.42 us -> 1.46 us  [local(): right_send = lax.ppermute(right_send, 'blk', slot_moves[slot])]
  transfers between devices with their start and end apart: 16 -> 16, of which waited for: 5 -> 6; matrix products, arithmetic and copies ran while one was open for 1% -> 1% of each run, Pallas kernels for 39% -> 38%
where the time goes in v25:
time: 78.7 us; the launch traced here: 78.3 us
  Pallas kernels  32.7 us (42%)
  starting transfers between devices  30.4 us (39%)
  waiting for transfers between devices  13.7 us (17%)
  between operations  0.81 us (1%)
    pallas_call x13, Pallas kernels, run(): pl.pallas_call(lambda *refs: kernel(*refs[len(after):]), out_shape=out_sh...  32.7 us
    all_to_all x2, starting transfers between devices, local(): lax.all_to_all(pieces, everyone, 0, 0, axis_index_groups=core_groups)  13.7 us
    ppermute x3, waiting for transfers between devices, local(): rights[slot + distance] = lax.ppermute(sent, 'blk', slot_moves[distance])  5.94 us
    ppermute x3, starting transfers between devices, local(): rights[slot + distance] = lax.ppermute(sent, 'blk', slot_moves[distance])  4.73 us
    ppermute x1, starting transfers between devices, local(): cotangent_peer = lax.ppermute(cotangent_send, 'blk', partner)  3.03 us
    ppermute x1, starting transfers between devices, local(): right_send = lax.ppermute(right_send, 'blk', slot_moves[blocks // 2])  2.87 us
    ppermute x1, waiting for transfers between devices, local(): right_send = lax.ppermute(right_send, 'blk', slot_moves[blocks // 2])  2.78 us
    ppermute x1, starting transfers between devices, local(): left_found = [left_own, lax.ppermute(left_send, 'blk', partner)]  1.99 us
  transfers between devices with their start and end apart: 16, of which 6 were waited for; matrix products, arithmetic and copies ran while one was open for 1% of the time, Pallas kernels for 38%

profile of v25, /device:TPU:0, one launch (start us, length us, event | category | flops | bytes accessed | tf_op | source)
XLA Modules:
  0.0 78.3 jit_solution(1722115697088097179)
XLA Ops:
  0.6 2.0 %prepare.1 = (f32[512,128]{1,0:T(8,128)S(1)}, f32[512,128]{1,0:T(8,128)S(1)}, f32[16,4,16,128]{3,2,1,0:T(8,128)S(1)}, f32[16,4,16,128]{3,2,1,0:T(8,128)S(1)}, f32[1024,128]{1,0:T(8,128)S(1)}) custom-call(f32[16,4,2,16,128]{4,3,2,1,0:T(8,128)} %bitcast.6, f32[16,4096]{1,0:T(8,128)} %refs_1_.1, f32[16,4096]{1,0:T(8,128)} %refs_2_.1, f32[1024,128]{1,0:T(8,128)} %refs_3_.1), custom_call_target="tpu_custom_call" | custom-call | flops 1 | bytes 1 | tf_op jit(solution)/shard_map/prepare/pallas_call | solution.py:520
  2.6 3.0 %collective-permute-start = (f32[16,4,16,128]{3,2,1,0:T(8,128)S(1)}, f32[16,4,16,128]{3,2,1,0:T(8,128)S(1)}, u32[]{:S(2)}, u32[]{:S(2)}) collective-permute-start(f32[16,4,16,128]{3,2,1,0:T(8,128)S(1)} %get-tuple-element.51), channel_id=1, source_target_pairs={{0,4},{4,0},{8,12},{12,8},{16,20},{20,16},{24,28},{28,24},{1,5},{5... | collective-permute-start | bytes 1572872 | tf_op jit(solution)/shard_map/ppermute | solution.py:580
  5.6 2.6 %collective-permute-start.3 = (f32[512,128]{1,0:T(8,128)S(1)}, f32[512,128]{1,0:T(8,128)S(1)}, u32[]{:S(2)}, u32[]{:S(2)}) collective-permute-start(f32[512,128]{1,0:T(8,128)S(1)} %get-tuple-element.57.refs_5_.refs_3_), channel_id=1, source_target_pairs={{0,16},{4,20},{8,24},{12,28},{16,0},{20,4},{24,8},{28,12},{1,17},{... | collective-permute-start | bytes 786440 | tf_op jit(solution)/shard_map/ppermute | solution.py:619
  8.2 1.6 %collective-permute-start.2 = (f32[512,128]{1,0:T(8,128)S(1)}, f32[512,128]{1,0:T(8,128)S(1)}, u32[]{:S(2)}, u32[]{:S(2)}) collective-permute-start(f32[512,128]{1,0:T(8,128)S(1)} %get-tuple-element.57.refs_5_.refs_3_), channel_id=1, source_target_pairs={{0,8},{4,12},{8,0},{12,4},{16,24},{20,28},{24,16},{28,20},{1,9},{5... | collective-permute-start | bytes 786440 | tf_op jit(solution)/shard_map/ppermute | solution.py:619
  9.8 0.5 collective-permute-start.1
  10.3 3.8 %gradient_own.1 = (bf16[8,512,512]{2,1,0:T(8,128)(2,1)S(1)}, bf16[8,2,256,256]{3,2,1,0:T(8,128)(2,1)S(1)}, f32[8,128,256]{2,1,0:T(8,128)S(1)}, bf16[512,768]{1,0:T(8,128)(2,1)S(1)}, bf16[512,512]{1,0:T(8,128)(2,1)}) custom-call(f32[1024,128]{1,0:T(8,128)S(1)} %get-tuple-element.47.refs_0_, f32[16,4,16,128]{3,2,1,0:T(8,128)S(1)} %get-tuple-element.48.refs_1_, ...), custom_call_target="tpu_custom_call" | custom-call | flops 1 | bytes 1 | tf_op jit(solution)/shard_map/gradient_own/pallas_call | solution.py:520
  14.1 5.9 %collective-permute-done.3.refs_7_.refs_5_ = f32[512,128]{1,0:T(8,128)S(1)} collective-permute-done((f32[512,128]{1,0:T(8,128)S(1)}, f32[512,128]{1,0:T(8,128)S(1)}, u32[]{:S(2)}, u32[]{:S(2)}) %collective-permute-start.3) | collective-permute-done | bytes 262176 | tf_op jit(solution)/shard_map/ppermute | solution.py:619
  20.0 0.6 collective-permute-start.4
  20.6 0.0 collective-permute-done.refs_1_
  20.6 1.8 %gradient_peer.1 = (bf16[8,512,512]{2,1,0:T(8,128)(2,1)S(1)}, bf16[8,2,256,256]{3,2,1,0:T(8,128)(2,1)S(1)}) custom-call(bf16[512,768]{1,0:T(8,128)(2,1)S(1)} %get-tuple-element.50.refs_0_, f32[16,4,16,128]{3,2,1,0:T(8,128)S(1)} %collective-permute-done.refs_1_), custom_call_target="tpu_custom_call" | custom-call | flops 1 | bytes 1 | tf_op jit(solution)/shard_map/gradient_peer/pallas_call | solution.py:520
  22.4 0.7 collective-permute-done.1.refs_1_.refs_2_
  23.2 1.1 %right_parts.1 = (f32[2,512,128]{2,1,0:T(8,128)S(1)}, f32[2,512,128]{2,1,0:T(8,128)S(1)}) custom-call(bf16[8,512,512]{2,1,0:T(8,128)(2,1)S(1)} %get-tuple-element.52.refs_0_.refs_2_, f32[512,128]{1,0:T(8,128)S(1)} %collective-permute-done.1.refs_1_.refs_2_, f32[8,128,256]{2,1,0:T(8,128)S(1)} %get-tuple-element.53.refs_2_), custom_call_target="tpu_custom_call" | custom-call | flops 1 | bytes 1 | tf_op jit(solution)/shard_map/right_parts/pallas_call | solution.py:520
  24.3 2.9 %collective-permute-start.6 = (f32[2,512,128]{2,1,0:T(8,128)S(1)}, f32[2,512,128]{2,1,0:T(8,128)S(1)}, u32[]{:S(2)}, u32[]{:S(2)}) collective-permute-start(f32[2,512,128]{2,1,0:T(8,128)S(1)} %get-tuple-element.69), channel_id=1, source_target_pairs={{0,16},{4,20},{8,24},{12,28},{16,0},{20,4},{24,8},{28,12},{1,17},{... | collective-permute-start | bytes 1572872 | tf_op jit(solution)/shard_map/ppermute | solution.py:629
  27.2 0.0 collective-permute-done.2.refs_6_.refs_4_
  27.2 0.0 collective-permute-done.4.refs_8_.refs_6_
  27.2 7.5 %weight.1 = (f32[512,128]{1,0:T(8,128)S(1)}, f32[512,128]{1,0:T(8,128)S(1)}, bf16[8,512,512]{2,1,0:T(8,128)(2,1)}, bf16[8,512,512]{2,1,0:T(8,128)(2,1)}) custom-call(f32[2,512,128]{2,1,0:T(8,128)S(1)} %get-tuple-element.54.refs_0_.refs_1_, f32[512,128]{1,0:T(8,128)S(1)} %get-tuple-element.49.refs_2_.refs_1_, ...), custom_call_target="tpu_custom_call" | custom-call | flops 12884901888 | bytes 1 | tf_op jit(solution)/shard_map/weight/pallas_call | solution.py:520
  34.7 0.1 collective-permute-start.5
  34.8 2.4 %left_parts.1 = (f32[2,32,512]{2,1,0:T(8,128)S(1)}, f32[2,32,512]{2,1,0:T(8,128)S(1)}, f32[2,32,512]{2,1,0:T(8,128)S(1)}, f32[2,32,512]{2,1,0:T(8,128)S(1)}) custom-call(f32[512,128]{1,0:T(8,128)S(1)} %get-tuple-element.65.refs_0_, bf16[8,512,512]{2,1,0:T(8,128)(2,1)S(1)} %get-tuple-element.58.refs_1_, ...), custom_call_target="tpu_custom_call" | custom-call | flops 6442450944 | bytes 1 | tf_op jit(solution)/shard_map/left_parts/pallas_call | solution.py:520
  37.3 0.0 collective-permute-done.5
  37.3 0.7 add.3
  38.0 7.4 %all-to-all-start = ((f32[16,32,128]{2,1,0:T(8,128)}), f32[16,32,128]{2,1,0:T(8,128)S(1)}, u32[]{:S(2)}, u32[]{:S(2)}) async-start(f32[16,32,128]{2,1,0:T(8,128)} %bitcast.1.refs_0_), calls=%async_computation | async-start | bytes 524288 | tf_op jit(solution)/shard_map/all_to_all | solution.py:694
  45.4 5.0 %pair_peer.1.refs_0_ = f32[16,4,16,128]{3,2,1,0:T(8,128)S(1)} custom-call(f32[16,32,128]{2,1,0:T(8,128)} %bitcast.1.refs_0_, bf16[8,512,512]{2,1,0:T(8,128)(2,1)} %get-tuple-element.67.refs_1_, bf16[512,512]{1,0:T(8,128)(2,1)} %get-tuple-element.68.refs_2_), custom_call_target="tpu_custom_call" | custom-call | flops 6442450944 | bytes 1 | tf_op jit(solution)/shard_map/pair_peer/pallas_call | solution.py:520
  50.4 2.8 %collective-permute-done.6.refs_2_ = f32[2,512,128]{2,1,0:T(8,128)S(1)} collective-permute-done((f32[2,512,128]{2,1,0:T(8,128)S(1)}, f32[2,512,128]{2,1,0:T(8,128)S(1)}, u32[]{:S(2)}, u32[]{:S(2)}) %collective-permute-start.6) | collective-permute-done | bytes 524320 | tf_op jit(solution)/shard_map/ppermute | solution.py:629
  53.1 0.1 right_halve.1
  53.2 0.1 collective-permute-start.9
  53.3 1.6 %collective-permute-start.10 = (f32[2,32,512]{2,1,0:T(8,128)S(1)}, f32[2,32,512]{2,1,0:T(8,128)S(1)}, u32[]{:S(2)}, u32[]{:S(2)}) collective-permute-start(f32[2,32,512]{2,1,0:T(8,128)S(1)} %get-tuple-element.79), channel_id=1, source_target_pairs={{0,2},{1,3},{2,0},{3,1},{4,6},{5,7},{6,4},{7,5},{8,10},{9,11},{10,... | collective-permute-start | bytes 393224 | tf_op jit(solution)/shard_map/ppermute | solution.py:691
  54.9 0.2 collective-permute-start.11
  55.1 0.0 collective-permute-start.7
  55.2 1.5 %collective-permute-start.8 = (f32[1,512,128]{2,1,0:T(8,128)S(1)}, f32[1,512,128]{2,1,0:T(8,128)S(1)}, u32[]{:S(2)}, u32[]{:S(2)}) collective-permute-start(f32[1,512,128]{2,1,0:T(8,128)S(1)} %get-tuple-element.72), channel_id=1, source_target_pairs={{0,8},{4,12},{8,0},{12,4},{16,24},{20,28},{24,16},{28,20},{1,9},{5... | collective-permute-start | bytes 786440 | tf_op jit(solution)/shard_map/ppermute | solution.py:686
  56.6 0.0 all-to-all-done.refs_2_
  56.6 0.8 weight_sum.1.refs_0_
  57.4 6.3 %all-to-all-start.1 = ((f32[16,32,128]{2,1,0:T(8,128)}), f32[16,32,128]{2,1,0:T(8,128)S(1)}, u32[]{:S(2)}, u32[]{:S(2)}) async-start(f32[16,32,128]{2,1,0:T(8,128)} %weight_sum.1.refs_0_), calls=%async_computation.1 | async-start | bytes 524288 | tf_op jit(solution)/shard_map/all_to_all | solution.py:705
  63.7 0.0 collective-permute-done.9.refs_2_
  63.7 0.0 collective-permute-done.10.refs_3_
  63.7 0.0 collective-permute-done.11.refs_4_
  63.8 2.0 %collective-permute-start.12 = (f32[32,512]{1,0:T(8,128)S(1)}, f32[32,512]{1,0:T(8,128)S(1)}, u32[]{:S(2)}, u32[]{:S(2)}) collective-permute-start(f32[32,512]{1,0:T(8,128)S(1)} %get-tuple-element.82), channel_id=1, source_target_pairs={{0,4},{4,0},{8,12},{12,8},{16,20},{20,16},{24,28},{28,24},{1,5},{5... | collective-permute-start | bytes 196616 | tf_op jit(solution)/shard_map/ppermute | solution.py:707
  65.8 5.0 %pair_own.1.refs_0_ = f32[16,4,16,128]{3,2,1,0:T(8,128)S(1)} custom-call(f32[16,32,128]{2,1,0:T(8,128)} %weight_sum.1.refs_0_, bf16[8,512,512]{2,1,0:T(8,128)(2,1)} %get-tuple-element.71.refs_1_, bf16[512,512]{1,0:T(8,128)(2,1)} %get-tuple-element.68.refs_2_), custom_call_target="tpu_custom_call" | custom-call | flops 6442450944 | bytes 1 | tf_op jit(solution)/shard_map/pair_own/pallas_call | solution.py:520
  70.7 0.0 collective-permute-done.8.refs_3_
  70.7 1.1 %collective-permute-done.7.refs_1_ = f32[16,4,16,128]{3,2,1,0:T(8,128)S(1)} collective-permute-done((f32[16,4,16,128]{3,2,1,0:T(8,128)S(1)}, f32[16,4,16,128]{3,2,1,0:T(8,128)S(1)}, u32[]{:S(2)}, u32[]{:S(2)}) %collective-permute-start.7) | collective-permute-done | bytes 524320 | tf_op jit(solution)/shard_map/ppermute | solution.py:679
  71.8 1.6 %collective-permute-done.12.refs_5_ = f32[32,512]{1,0:T(8,128)S(1)} collective-permute-done((f32[32,512]{1,0:T(8,128)S(1)}, f32[32,512]{1,0:T(8,128)S(1)}, u32[]{:S(2)}, u32[]{:S(2)}) %collective-permute-start.12) | collective-permute-done | bytes 65568 | tf_op jit(solution)/shard_map/ppermute | solution.py:707
  73.5 2.2 %finish.1 = (f32[16,4,2,16,128]{4,3,2,1,0:T(8,128)}, f32[16,1024]{1,0:T(8,128)}, f32[16,4096]{1,0:T(8,128)}) custom-call(f32[16,4,16,128]{3,2,1,0:T(8,128)S(1)} %pair_own.1.refs_0_, f32[16,4,16,128]{3,2,1,0:T(8,128)S(1)} %collective-permute-done.7.refs_1_, f32[1,512,128]{2,1,0:T(8,128)S(1)} %get-tuple-element.70.refs_1_.refs_2_, ...), custom_call_target="tpu_custom_call" | custom-call | flops 1 | bytes 1 | tf_op jit(solution)/shard_map/finish/pallas_call | solution.py:520
  75.6 0.0 all-to-all-done.1
  75.6 0.1 collective-permute-start.13
  75.7 1.5 %collective-permute-done.13.refs_1_ = f32[512,128]{1,0:T(8,128)S(1)} collective-permute-done((f32[512,128]{1,0:T(8,128)S(1)}, f32[512,128]{1,0:T(8,128)S(1)}, u32[]{:S(2)}, u32[]{:S(2)}) %collective-permute-start.13) | collective-permute-done | bytes 262176 | tf_op jit(solution)/shard_map/ppermute | solution.py:732
  77.2 1.1 %place.1 = f32[1024,128]{1,0:T(8,128)} custom-call(f32[512,128]{1,0:T(8,128)S(1)} %bitcast.5, f32[512,128]{1,0:T(8,128)S(1)} %collective-permute-done.13.refs_1_), custom_call_target="tpu_custom_call" | custom-call | flops 1 | bytes 1 | tf_op jit(solution)/shard_map/place/pallas_call | solution.py:520
  (1 shorter events, 0.0 us)
Async XLA Ops:
  2.6 18.0 %collective-permute-start = (f32[16,4,16,128]{3,2,1,0:T(8,128)S(1)}, f32[16,4,16,128]{3,2,1,0:T(8,128)S(1)}, u32[]{:S(2)}, u32[]{:S(2)}) collective-permute-start(f32[16,4,16,128]{3,2,1,0:T(8,128)S(1)} %get-tuple-element.51), channel_id=1, source_target_pairs={{0,4},{4,0},{8,12},{12,8},{16,20},{20,16},{24,28},{28,24},{1,5},{5... | collective-permute-start | bytes 1572872 | tf_op jit(solution)/shard_map/ppermute | solution.py:580
  5.6 14.4 %collective-permute-start.3 = (f32[512,128]{1,0:T(8,128)S(1)}, f32[512,128]{1,0:T(8,128)S(1)}, u32[]{:S(2)}, u32[]{:S(2)}) collective-permute-start(f32[512,128]{1,0:T(8,128)S(1)} %get-tuple-element.57.refs_5_.refs_3_), channel_id=1, source_target_pairs={{0,16},{4,20},{8,24},{12,28},{16,0},{20,4},{24,8},{28,12},{1,17},{... | collective-permute-start | bytes 786440 | tf_op jit(solution)/shard_map/ppermute | solution.py:619
  8.2 19.0 %collective-permute-start.2 = (f32[512,128]{1,0:T(8,128)S(1)}, f32[512,128]{1,0:T(8,128)S(1)}, u32[]{:S(2)}, u32[]{:S(2)}) collective-permute-start(f32[512,128]{1,0:T(8,128)S(1)} %get-tuple-element.57.refs_5_.refs_3_), channel_id=1, source_target_pairs={{0,8},{4,12},{8,0},{12,4},{16,24},{20,28},{24,16},{28,20},{1,9},{5... | collective-permute-start | bytes 786440 | tf_op jit(solution)/shard_map/ppermute | solution.py:619
  9.8 13.4 %collective-permute-start.1 = (f32[512,128]{1,0:T(8,128)S(1)}, f32[512,128]{1,0:T(8,128)S(1)}, u32[]{:S(2)}, u32[]{:S(2)}) collective-permute-start(f32[512,128]{1,0:T(8,128)S(1)} %get-tuple-element.49.refs_2_.refs_1_), channel_id=1, source_target_pairs={{0,4},{4,0},{8,12},{12,8},{16,20},{20,16},{24,28},{28,24},{1,5},{5... | collective-permute-start | bytes 786440 | tf_op jit(solution)/shard_map/ppermute | solution.py:581
  20.0 7.2 %collective-permute-start.4 = (f32[512,128]{1,0:T(8,128)S(1)}, f32[512,128]{1,0:T(8,128)S(1)}, u32[]{:S(2)}, u32[]{:S(2)}) collective-permute-start(f32[512,128]{1,0:T(8,128)S(1)} %collective-permute-done.3.refs_7_.refs_5_), channel_id=1, source_target_pairs={{0,8},{4,12},{8,0},{12,4},{16,24},{20,28},{24,16},{28,20},{1,9},{5... | collective-permute-start | bytes 786440 | tf_op jit(solution)/shard_map/ppermute | solution.py:619
  24.3 28.8 %collective-permute-start.6 = (f32[2,512,128]{2,1,0:T(8,128)S(1)}, f32[2,512,128]{2,1,0:T(8,128)S(1)}, u32[]{:S(2)}, u32[]{:S(2)}) collective-permute-start(f32[2,512,128]{2,1,0:T(8,128)S(1)} %get-tuple-element.69), channel_id=1, source_target_pairs={{0,16},{4,20},{8,24},{12,28},{16,0},{20,4},{24,8},{28,12},{1,17},{... | collective-permute-start | bytes 1572872 | tf_op jit(solution)/shard_map/ppermute | solution.py:629
  34.7 2.5 %collective-permute-start.5 = (f32[512,128]{1,0:T(8,128)S(1)}, f32[512,128]{1,0:T(8,128)S(1)}, u32[]{:S(2)}, u32[]{:S(2)}) collective-permute-start(f32[512,128]{1,0:T(8,128)S(1)} %get-tuple-element.66), channel_id=1, source_target_pairs={{0,1},{1,0},{2,3},{3,2},{4,5},{5,4},{6,7},{7,6},{8,9},{9,8},{10,11... | collective-permute-start | bytes 786440 | tf_op jit(solution)/shard_map/ppermute | solution.py:645
  38.0 18.6 %all-to-all-start = ((f32[16,32,128]{2,1,0:T(8,128)}), f32[16,32,128]{2,1,0:T(8,128)S(1)}, u32[]{:S(2)}, u32[]{:S(2)}) async-start(f32[16,32,128]{2,1,0:T(8,128)} %bitcast.1.refs_0_), calls=%async_computation | async-start | bytes 524288 | tf_op jit(solution)/shard_map/all_to_all | solution.py:694
  53.2 10.5 %collective-permute-start.9 = (f32[2,32,512]{2,1,0:T(8,128)S(1)}, f32[2,32,512]{2,1,0:T(8,128)S(1)}, u32[]{:S(2)}, u32[]{:S(2)}) collective-permute-start(f32[2,32,512]{2,1,0:T(8,128)S(1)} %get-tuple-element.78), channel_id=1, source_target_pairs={{0,1},{1,0},{2,3},{3,2},{4,5},{5,4},{6,7},{7,6},{8,9},{9,8},{10,11... | collective-permute-start | bytes 393224 | tf_op jit(solution)/shard_map/ppermute | solution.py:691
  53.3 10.4 %collective-permute-start.10 = (f32[2,32,512]{2,1,0:T(8,128)S(1)}, f32[2,32,512]{2,1,0:T(8,128)S(1)}, u32[]{:S(2)}, u32[]{:S(2)}) collective-permute-start(f32[2,32,512]{2,1,0:T(8,128)S(1)} %get-tuple-element.79), channel_id=1, source_target_pairs={{0,2},{1,3},{2,0},{3,1},{4,6},{5,7},{6,4},{7,5},{8,10},{9,11},{10,... | collective-permute-start | bytes 393224 | tf_op jit(solution)/shard_map/ppermute | solution.py:691
  54.9 8.8 %collective-permute-start.11 = (f32[2,32,512]{2,1,0:T(8,128)S(1)}, f32[2,32,512]{2,1,0:T(8,128)S(1)}, u32[]{:S(2)}, u32[]{:S(2)}) collective-permute-start(f32[2,32,512]{2,1,0:T(8,128)S(1)} %get-tuple-element.80), channel_id=1, source_target_pairs={{0,3},{1,2},{2,1},{3,0},{4,7},{5,6},{6,5},{7,4},{8,11},{9,10},{10,... | collective-permute-start | bytes 393224 | tf_op jit(solution)/shard_map/ppermute | solution.py:691
  55.1 16.7 %collective-permute-start.7 = (f32[16,4,16,128]{3,2,1,0:T(8,128)S(1)}, f32[16,4,16,128]{3,2,1,0:T(8,128)S(1)}, u32[]{:S(2)}, u32[]{:S(2)}) collective-permute-start(f32[16,4,16,128]{3,2,1,0:T(8,128)S(1)} %pair_peer.1.refs_0_), channel_id=1, source_target_pairs={{0,4},{4,0},{8,12},{12,8},{16,20},{20,16},{24,28},{28,24},{1,5},{5... | collective-permute-start | bytes 1572872 | tf_op jit(solution)/shard_map/ppermute | solution.py:679
  55.2 15.6 %collective-permute-start.8 = (f32[1,512,128]{2,1,0:T(8,128)S(1)}, f32[1,512,128]{2,1,0:T(8,128)S(1)}, u32[]{:S(2)}, u32[]{:S(2)}) collective-permute-start(f32[1,512,128]{2,1,0:T(8,128)S(1)} %get-tuple-element.72), channel_id=1, source_target_pairs={{0,8},{4,12},{8,0},{12,4},{16,24},{20,28},{24,16},{28,20},{1,9},{5... | collective-permute-start | bytes 786440 | tf_op jit(solution)/shard_map/ppermute | solution.py:686
  57.4 18.2 %all-to-all-start.1 = ((f32[16,32,128]{2,1,0:T(8,128)}), f32[16,32,128]{2,1,0:T(8,128)S(1)}, u32[]{:S(2)}, u32[]{:S(2)}) async-start(f32[16,32,128]{2,1,0:T(8,128)} %weight_sum.1.refs_0_), calls=%async_computation.1 | async-start | bytes 524288 | tf_op jit(solution)/shard_map/all_to_all | solution.py:705
  63.8 9.7 %collective-permute-start.12 = (f32[32,512]{1,0:T(8,128)S(1)}, f32[32,512]{1,0:T(8,128)S(1)}, u32[]{:S(2)}, u32[]{:S(2)}) collective-permute-start(f32[32,512]{1,0:T(8,128)S(1)} %get-tuple-element.82), channel_id=1, source_target_pairs={{0,4},{4,0},{8,12},{12,8},{16,20},{20,16},{24,28},{28,24},{1,5},{5... | collective-permute-start | bytes 196616 | tf_op jit(solution)/shard_map/ppermute | solution.py:707
  75.6 1.6 %collective-permute-start.13 = (f32[512,128]{1,0:T(8,128)S(1)}, f32[512,128]{1,0:T(8,128)S(1)}, u32[]{:S(2)}, u32[]{:S(2)}) collective-permute-start(f32[512,128]{1,0:T(8,128)S(1)} %bitcast.4), channel_id=1, source_target_pairs={{0,1},{1,0},{2,3},{3,2},{4,5},{5,4},{6,7},{7,6},{8,9},{9,8},{10,11... | collective-permute-start | bytes 786440 | tf_op jit(solution)/shard_map/ppermute | solution.py:732
